TPU v7x, 32 devices: a whole 2x2x4 slice. The times are simulated.
32 devices in a mesh: ha: 8 (over z, core), ba: 4 (over y, x).
Axes of the slice: x: 2, y: 2, z: 4, core: 2. Of those that a mesh axis runs over, the one named last changes fastest.
Arguments:
- canvas: float32 [4, 64, 64, 512], P('ba', 'ha'), may hold values from -6 to 6
- image_id: int32 [4, 64, 64], P('ba'), may hold values from -1 to 35, as said below
- keep_first: int32 [4, 36], P('ba'), may hold values 0 or 1
- keep_second: int32 [4, 36], P('ba'), may hold values 0 or 1
- first_gain: float32 [512], replicated, may hold values from 0.1 to 1.9
- weight_in: float32 [512, 1024], replicated, may hold values from -0.25 to 0.25
- depth_kernel: float32 [49, 960], replicated, may hold values from -2.5 to 2.5
- gate_first: float32 [64, 128], replicated, may hold values from -0.75 to 0.75
- gate_second: float32 [128, 256], replicated, may hold values from -0.5 to 0.5
- gate_third: float32 [256, 512], replicated, may hold values from -0.375 to 0.375
- weight_out: float32 [512, 512], replicated, may hold values from -0.25 to 0.25
- scale_first: float32 [512], replicated, may hold values from 0.5 to 1.5
- second_gain: float32 [512], replicated, may hold values from 0.1 to 1.9
- weight_up: float32 [512, 2048], replicated, may hold values from -0.25 to 0.25
- weight_down: float32 [2048, 512], replicated, may hold values from -0.125 to 0.125
- scale_second: float32 [512], replicated, may hold values from 0.5 to 1.5
- cotangent: float32 [4, 64, 64, 512], P('ba', 'ha'), may hold values from -6 to 6
Outputs:
- output: float32 [4, 64, 64, 512], P('ba', 'ha')
- grad_canvas: float32 [4, 64, 64, 512], P('ba', 'ha')
- grad_first_gain: float32 [512], replicated
- grad_weight_in: float32 [512, 1024], P('ba', 'ha')
- grad_depth_kernel: float32 [49, 960], replicated
- grad_gate_first: float32 [64, 128], replicated
- grad_gate_second: float32 [128, 256], replicated
- grad_gate_third: float32 [256, 512], replicated
- grad_weight_out: float32 [512, 512], P('ba', 'ha')
- grad_scale_first: float32 [512], replicated
- grad_second_gain: float32 [512], replicated
- grad_weight_up: float32 [512, 2048], P('ba', 'ha')
- grad_weight_down: float32 [2048, 512], P('ba', 'ha')
- grad_scale_second: float32 [512], replicated
Inputs may be any that keep to these rules, and one draw needn't show every extreme that they name: `image_id`: each canvas holds either one image on all its cells (number 0) or 36 images of 10 x 10 cells in a 6 x 6 arrangement, numbered 0 to 35 in row order, at a row and column offset of 0 to 4 cells, with -1 on the cells that no image covers. Canvas 0 holds one image, canvas 1 holds 36.
All inputs are finite; a program needn't handle non-finite values. No bound on the sum of `keep_first` or of `keep_second` on one device may be relied on, other than what follows from the above.
Results may differ from a plain program's by a relative error of at most 0.0003.
Values sent between devices are 32-bit elements; how exact they have to be, the bound alone decides.
No kernel may reach another device: no remote copies, remote signals or barrier semaphores. Data moves between devices by JAX's collectives and lax.ppermute only.
A program may use at most 320 MiB of HBM per device.

v0:
```python
import jax
import jax.numpy as jnp
from jax import lax
from jax.sharding import PartitionSpec as P

KERN = 7


KEEP_RATE = 0.8
SPREAD = 1.0 / 3.0
EPSILON = 1e-06


def padded_2(cells, sides, width):
    for axis, dim in sides:
        count = lax.axis_size(axis)
        ends = count - 1
        head = lax.slice_in_dim(cells, 0, width, axis=dim)
        tail = lax.slice_in_dim(cells, cells.shape[dim] - width, cells.shape[dim], axis=dim)
        cells = jnp.concatenate(
            [
                lax.ppermute(tail, axis, [(i, (i + 1) % count) for i in range(ends)]),
                cells,
                lax.ppermute(head, axis, [((i + 1) % count, i) for i in range(ends)]),
            ],
            axis=dim,
        )
    return cells


def matmul(left, right):
    return jnp.dot(left, right, precision=lax.Precision.HIGHEST, preferred_element_type=jnp.float32)


def layer_norm(values, gain):
    centered = values - jnp.mean(values, axis=-1, keepdims=True)
    variance = jnp.mean(centered * centered, axis=-1, keepdims=True)
    return centered * lax.rsqrt(variance + EPSILON) * gain


def masked_depthwise(padded, padded_ids, own_ids, kernel, row_count, col_count):
    total = jnp.zeros(own_ids.shape + (padded.shape[-1],), jnp.float32)
    for tap_row in range(KERN):
        for tap_col in range(KERN):
            window = padded[..., tap_row : tap_row + row_count, tap_col : tap_col + col_count, :]
            same = (
                padded_ids[..., tap_row : tap_row + row_count, tap_col : tap_col + col_count]
                == own_ids
            )
            total = (
                total
                + kernel[tap_row * KERN + tap_col] * window * same.astype(jnp.float32)[..., None]
            )
    return total * SPREAD


def keep_lookup(ids, table):
    slots = jnp.arange(table.shape[-1], dtype=jnp.int32)
    hits = (ids[..., None] == slots).astype(jnp.float32)
    return jnp.sum(hits * table, axis=-1) / KEEP_RATE


def recursive_gates(gate_base, conv, gates, weight_out):
    width = gate_base.shape[-1]
    mixed = gate_base * conv[..., :width]
    start = width
    for level in range(len(gates)):
        width = gates[level].shape[1]
        mixed = matmul(mixed, gates[level]) * conv[..., start : start + width]
        start = start + width
    return matmul(mixed, weight_out)


def residual_tail(
    masked,
    branch,
    keep_one,
    keep_two,
    scale_first,
    second_gain,
    weight_up,
    weight_down,
    scale_second,
):
    middle = masked + keep_one[..., None] * scale_first * branch
    hidden = jax.nn.gelu(matmul(layer_norm(middle, second_gain), weight_up), approximate=False)
    return middle + keep_two[..., None] * scale_second * matmul(hidden, weight_down)


def head_map(values, gain, weight):
    return matmul(layer_norm(values, gain), weight)


def edge_rows(grad_ext, reach_rows):
    return jnp.concatenate([grad_ext[:, :reach_rows], grad_ext[:, -reach_rows:]], axis=1)


def fold_back(grad_ext, returned, row_count, reach_rows):
    own = grad_ext[:, reach_rows : reach_rows + row_count]
    rest = row_count - reach_rows
    lower_part = jnp.pad(returned[:, :reach_rows], ((0, 0), (0, rest), (0, 0), (0, 0)))
    upper_part = jnp.pad(returned[:, -reach_rows:], ((0, 0), (rest, 0), (0, 0), (0, 0)))
    return own + lower_part + upper_part


def shards(
    canvas,
    image_id,
    keep_first,
    keep_second,
    first_gain,
    weight_in,
    depth_kernel,
    gate_first,
    gate_second,
    gate_third,
    weight_out,
    scale_first,
    second_gain,
    weight_up,
    weight_down,
    scale_second,
    cotangent,
):
    row_count = canvas.shape[1]
    col_count = canvas.shape[2]
    reach_rows = KERN // 2
    split = weight_in.shape[1] - depth_kernel.shape[1]
    first_row = lax.axis_index("ha") * row_count
    padded_ids_all = jnp.pad(
        image_id, ((0, 0), (reach_rows, reach_rows), (reach_rows, reach_rows)), constant_values=-1
    )
    window_ids = lax.dynamic_slice_in_dim(padded_ids_all, first_row, row_count + 2 * reach_rows, 1)
    own_ids = lax.dynamic_slice_in_dim(image_id, first_row, row_count, 1)
    valid = (own_ids >= 0).astype(jnp.float32)[..., None]
    masked = canvas * valid
    keep_one = keep_lookup(own_ids, keep_first.astype(jnp.float32)[:, None, None, :])
    keep_two = keep_lookup(own_ids, keep_second.astype(jnp.float32)[:, None, None, :])
    joined, head_pull = jax.vjp(head_map, masked, first_gain, weight_in)
    gate_base = joined[..., :split]
    mixed_ext = padded_2(joined[..., split:], (("ha", 1),), reach_rows)
    padded = jnp.pad(mixed_ext, ((0, 0), (0, 0), (reach_rows, reach_rows), (0, 0)))

    def conv_of(padded_v, kernel_v):
        return masked_depthwise(padded_v, window_ids, own_ids, kernel_v, row_count, col_count)

    conv_fn = jax.checkpoint(conv_of)

    def tail_map(
        masked_v,
        base_v,
        padded_v,
        kernel_v,
        first_v,
        second_v,
        third_v,
        out_v,
        scale_one,
        gain_two,
        up_v,
        down_v,
        scale_two,
    ):
        conv = conv_fn(padded_v, kernel_v)
        branch = recursive_gates(base_v, conv, (first_v, second_v, third_v), out_v)
        return residual_tail(
            masked_v, branch, keep_one, keep_two, scale_one, gain_two, up_v, down_v, scale_two
        )

    output, tail_pull = jax.vjp(
        tail_map,
        masked,
        gate_base,
        padded,
        depth_kernel,
        gate_first,
        gate_second,
        gate_third,
        weight_out,
        scale_first,
        second_gain,
        weight_up,
        weight_down,
        scale_second,
    )
    grads = tail_pull(cotangent)
    grad_mixed_ext = grads[2][:, :, reach_rows : reach_rows + col_count, :]
    returned = padded_2(edge_rows(grad_mixed_ext, reach_rows), (("ha", 1),), reach_rows)
    grad_mixed = fold_back(grad_mixed_ext, returned, row_count, reach_rows)
    grad_head, grad_gain_one, grad_in = head_pull(jnp.concatenate([grads[1], grad_mixed], axis=-1))
    grad_canvas = (grad_head + grads[0]) * valid
    partial_large = (
        lax.psum_scatter(grad_in, "ha", scatter_dimension=1, tiled=True),
        lax.psum_scatter(grads[7], "ha", scatter_dimension=1, tiled=True),
        lax.psum_scatter(grads[10], "ha", scatter_dimension=1, tiled=True),
        lax.psum_scatter(grads[11], "ha", scatter_dimension=1, tiled=True),
    )
    large = (
        lax.psum_scatter(partial_large[0], "ba", scatter_dimension=0, tiled=True),
        lax.psum_scatter(partial_large[1], "ba", scatter_dimension=0, tiled=True),
        lax.psum_scatter(partial_large[2], "ba", scatter_dimension=0, tiled=True),
        lax.psum_scatter(partial_large[3], "ba", scatter_dimension=0, tiled=True),
    )
    small = lax.psum(
        (grad_gain_one, grads[3], grads[4], grads[5], grads[6], grads[8], grads[9], grads[12]),
        ("ha", "ba"),
    )
    return (
        output,
        grad_canvas,
        small[0],
        large[0],
        small[1],
        small[2],
        small[3],
        small[4],
        large[1],
        small[5],
        small[6],
        large[2],
        large[3],
        small[7],
    )


def solution(mesh):
    in_specs = (
        P("ba", "ha", None, None),
        P("ba", None, None),
        P("ba", None),
        P("ba", None),
        P(),
        P(),
        P(),
        P(),
        P(),
        P(),
        P(),
        P(),
        P(),
        P(),
        P(),
        P(),
        P("ba", "ha", None, None),
    )
    out_specs = (
        P("ba", "ha", None, None),
        P("ba", "ha", None, None),
        P(),
        P("ba", "ha"),
        P(),
        P(),
        P(),
        P(),
        P("ba", "ha"),
        P(),
        P(),
        P("ba", "ha"),
        P("ba", "ha"),
        P(),
    )
    return jax.shard_map(shards, mesh=mesh, in_specs=in_specs, out_specs=out_specs, check_vma=False)
```

profile of v0, /device:TPU:0, one launch (start us, length us, event | category | flops | bytes accessed | tf_op | source)
XLA Modules:
  0.0 501.8 jit_solution(17865568540849495878)
XLA Ops:
  11.4 1.6 multiply_reduce_fusion.50
  13.1 3.7 fusion.129
  18.1 1.6 fusion.267
  19.7 3.3 collective-permute-start
  24.3 2.2 slice.1238
  28.8 2.1 select_maximum_fusion
  31.0 20.4 %fusion.31 = f32[1,8,64,960]{3,2,1,0:T(8,128)S(1)} fusion(f32[1,8,64,960]{3,2,1,0:T(8,128)S(1)} %slice.1238, f32[1,3,64,960]{3,2,1,0:T(8,128)} %collective-permute-done.1, f32[1,14,70,960]{3,2,1,0:T(8,128)S(1)} %select_maximum_fusion, f32[1,3,64,960]{3,2,1,0:T(8,128)} %collective-permute-done, f32[8,64]{1,0:T(8,128)S(1)} %get-tuple-element.254, ...), kind=kLoop, calls=%fused_computation.61 | loop fusion | flops 75202560 | bytes 88270592 | tf_op jit(solution)/shard_map/jvp()/mul | solution.py:54
  54.8 2.1 fusion.265
  57.2 19.7 %fusion.158 = (u8[64,2048]{1,0:T(8,128)(4,1)S(1)}, u8[64,2048]{1,0:T(8,128)(4,1)S(1)}, u8[64,2048]{1,0:T(8,128)(4,1)S(1)}, f32[8,64,2048]{2,1,0:T(8,128)S(1)}) fusion(f32[512,2048]{1,0:T(8,128)S(1)} %copy-done.23, f32[1,8,64,512]{3,2,1,0:T(8,128)S(1)} %get-tuple-element.93, f32[512]{0:T(512)S(1)} %copy-done.72, f32[8,64]{1,0:T(8,128)S(1)} %fusion.260, ...), kind=kOutput, calls=%fused_computation.356 | convolution fusion | flops 6463815680 | bytes 9836544 | tf_op jit(solution)/shard_map/jvp()/dot_general | solution.py:32
  76.9 9.0 %fusion = f32[8,64,2048]{2,1,0:T(8,128)S(1)} fusion(f32[8,64,2048]{2,1,0:T(8,128)S(1)} %get-tuple-element.352, u8[64,2048]{1,0:T(8,128)(4,1)S(1)} %get-tuple-element.74, u8[64,2048]{1,0:T(8,128)(4,1)S(1)} %get-tuple-element.75, u8[64,2048]{1,0:T(8,128)(4,1)S(1)} %get-tuple-element.73), kind=kLoop, calls=%fused_computation.3 | loop fusion | flops 72351744 | bytes 8781824 | tf_op jit(solution)/shard_map/jvp()/erfc | solution.py:86
  86.0 8.3 %multiply_add_fusion = f32[8,64,2048]{2,1,0:T(8,128)S(1)} fusion(f32[8,64,2048]{2,1,0:T(8,128)S(1)} %fusion, f32[8,64,2048]{2,1,0:T(8,128)S(1)} %get-tuple-element.352, f32[2048,512]{1,0:T(8,128)S(1)} %copy-done.27, f32[1,8,64,512]{3,2,1,0:T(8,128)S(1)} %copy-done.28, f32[512]{0:T(512)S(1)} %copy-done.127, f32[8,64]{1,0:T(8,128)S(1)} %broadcast_multiply_fusion.2), kind=kOutput, calls=%fused_computation.19 | convolution fusion | flops 6456606720 | bytes 17829888 | tf_op jit(solution)/shard_map/transpose(jvp())/dot_general | solution.py:32
  94.3 7.5 %fusion.145 = (f32[8,64]{1,0:T(8,128)S(1)}, f32[8,64,512]{2,1,0:T(8,128)S(1)}) fusion(f32[1,8,64,512]{3,2,1,0:T(8,128)S(1)} %get-tuple-element.93, f32[512]{0:T(512)S(1)} %copy-done.72, f32[8,64]{1,0:T(8,128)S(1)} %broadcast_multiply_fusion, f32[8,64,2048]{2,1,0:T(8,128)S(1)} %multiply_add_fusion, f32[512,2048]{1,0:T(8,128)S(1)} %copy-done.23), kind=kOutput, calls=%fused_computation.333 | convolution fusion | flops 6443499008 | bytes 10491904 | tf_op jit(solution)/shard_map/transpose(jvp())/dot_general | solution.py:32
  103.0 9.0 %fusion.133 = (f32[512]{0:T(512)}, f32[1,8,64,512]{3,2,1,0:T(8,128)}, f32[512]{0:T(512)}, f32[1,8,64,512]{3,2,1,0:T(8,128)S(1)}) fusion(f32[1,8,64,512]{3,2,1,0:T(8,128)S(1)} %copy-done.29, f32[8,64]{1,0:T(8,128)S(1)} %broadcast_multiply_fusion.2, f32[1,8,64,512]{3,2,1,0:T(8,128)S(1)} %get-tuple-element.93, f32[512]{0:T(512)S(1)} %copy-done.127, ...), kind=kOutput, calls=%fused_computation.315 | convolution fusion | flops 6449003520 | bytes 18894848 | tf_op jit(solution)/shard_map/jvp()/dot_general | solution.py:32
  112.0 1.9 fusion.143
  118.7 3.4 convolution_bitcast_fusion.3
  123.2 2.5 slice_multiply_fusion.42
  125.7 2.1 pad_add_fusion.1
  132.2 6.5 %multiply_multiply_fusion.50 = (f32[1,8,64,960]{3,2,1,0:T(8,128)}, f32[1,8,64,960]{3,2,1,0:T(8,128)}, f32[1,8,64,960]{3,2,1,0:T(8,128)}, f32[1,8,64,960]{3,2,1,0...) fusion(f32[1,8,64,960]{3,2,1,0:T(8,128)} %pad_add_fusion.1, f32[8,64]{1,0:T(8,128)S(1)} %get-tuple-element.348, ...), kind=kLoop, calls=%fused_computation.299 | loop fusion | flops 5898240 | bytes 13797888 | tf_op jit(solution)/shard_map/transpose(jvp(jvp()))/checkpoint/mul | solution.py:52
  139.0 5.0 multiply_reduce_fusion.43
  144.2 7.5 %multiply_multiply_fusion.54 = (f32[1,8,64,960]{3,2,1,0:T(8,128)}, f32[1,8,64,960]{3,2,1,0:T(8,128)}, f32[1,8,64,960]{3,2,1,0:T(8,128)}, f32[1,8,64,960]{3,2,1,0...) fusion(f32[1,8,64,960]{3,2,1,0:T(8,128)S(1)} %copy-done.4, ...), kind=kLoop, calls=%fused_computation.303 | loop fusion | flops 8847360 | bytes 19713792 | tf_op jit(solution)/shard_map/transpose(jvp(jvp()))/checkpoint/mul | solution.py:52
  151.8 7.4 %multiply_multiply_fusion.53 = (f32[1,8,64,960]{3,2,1,0:T(8,128)}, f32[1,8,64,960]{3,2,1,0:T(8,128)}, f32[1,8,64,960]{3,2,1,0:T(8,128)}, f32[1,8,64,960]{3,2,1,0...) fusion(f32[1,8,64,960]{3,2,1,0:T(8,128)S(1)} %copy-done.4, ...), kind=kLoop, calls=%fused_computation.302 | loop fusion | flops 8847360 | bytes 19713792 | tf_op jit(solution)/shard_map/transpose(jvp(jvp()))/checkpoint/mul | solution.py:52
  159.6 7.4 %multiply_multiply_fusion.52 = (f32[1,8,64,960]{3,2,1,0:T(8,128)}, f32[1,8,64,960]{3,2,1,0:T(8,128)}, f32[1,8,64,960]{3,2,1,0:T(8,128)}, f32[1,8,64,960]{3,2,1,0...) fusion(f32[1,8,64,960]{3,2,1,0:T(8,128)S(1)} %copy-done.4, ...), kind=kLoop, calls=%fused_computation.301 | loop fusion | flops 8847360 | bytes 19713792 | tf_op jit(solution)/shard_map/transpose(jvp(jvp()))/checkpoint/mul | solution.py:52
  167.1 7.4 %multiply_multiply_fusion.51 = (f32[1,8,64,960]{3,2,1,0:T(8,128)}, f32[1,8,64,960]{3,2,1,0:T(8,128)}, f32[1,8,64,960]{3,2,1,0:T(8,128)}, f32[1,8,64,960]{3,2,1,0...) fusion(f32[1,8,64,960]{3,2,1,0:T(8,128)S(1)} %copy-done.4, ...), kind=kLoop, calls=%fused_computation.300 | loop fusion | flops 8847360 | bytes 19713792 | tf_op jit(solution)/shard_map/transpose(jvp(jvp()))/checkpoint/mul | solution.py:52
  174.5 31.6 %pad_add_fusion = f32[1,14,70,960]{3,2,1,0:T(8,128)S(1)} fusion(f32[1,8,64,960]{3,2,1,0:T(8,128)} %get-tuple-element.102, f32[1,8,64,960]{3,2,1,0:T(8,128)} %get-tuple-element.103, f32[1,8,64,960]{3,2,1,0:T(8,128)} %get-tuple-element.104, f32[1,8,64,960]{3,2,1,0:T(8,128)} %get-tuple-element.106, f32[1,8,64,960]{3,2,1,0:T(8,128)} %get-tuple-element.107, ...), kind=kLoop, calls=%fused_computation.34 | loop fusion | flops 45158400 | bytes 100101120 | tf_op jit(solution)/shard_map/transpose(jvp(jvp()))/checkpoint/add_any | solution.py:45
  206.4 11.5 %collective-permute-start.2 = (f32[1,3,64,960]{3,2,1,0:T(8,128)S(1)}, f32[1,3,64,960]{3,2,1,0:T(8,128)S(1)}, u32[]{:S(2)}, u32[]{:S(2)}) collective-permute-start(f32[1,3,64,960]{3,2,1,0:T(8,128)S(1)} %get-tuple-element.96), channel_id=1, source_target_pairs={{0,4},{4,8},{8,12},{12,16},{16,20},{20,24},{24,28},{1,5},{5,9},{9,... | collective-permute-start | bytes 2211848 | tf_op jit(solution)/shard_map/ppermute | solution.py:22
  217.9 1.8 collective-permute-start.3
  219.8 2.5 collective-permute-done.3
  224.1 5.6 %convolution_bitcast_fusion.2 = f32[512,1024]{1,0:T(8,128)} fusion(f32[1,8,64,960]{3,2,1,0:T(8,128)S(1)} %fusion.75, f32[1,8,64,64]{3,2,1,0:T(8,128)S(1)} %copy-done.33, f32[512]{0:T(512)S(1)} %copy-done.69, f32[8,64]{1,0:T(8,128)S(1)} %fusion.259, f32[1,8,64,512]{3,2,1,0:T(8,128)S(1)} %copy-done.6, f32[8,64]{1,0:T(8,128)S(1)} %broadcast_multiply_fusion.1, ...), kind=kOutput, calls=%fused_computation.305 | convolution fusion | flops 3222798336 | bytes 5251072 | tf_op jit(solution)/shard_map/transpose(jvp())/dot_general | solution.py:32
  229.8 10.4 %convolution_bitcast_fusion.1 = f32[512,2048]{1,0:T(8,128)} fusion(f32[8,64,2048]{2,1,0:T(8,128)} %copy-done.24, f32[1,8,64,512]{3,2,1,0:T(8,128)} %copy-done.11, f32[512]{0:T(512)} %param.29, f32[8,64]{1,0:T(8,128)S(1)} %fusion.260, f32[8,64]{1,0:T(8,128)S(1)} %broadcast_multiply_fusion), kind=kOutput, calls=%fused_computation.42 | convolution fusion | flops 6443237376 | bytes 9443328 | tf_op jit(solution)/shard_map/transpose(jvp())/dot_general | solution.py:32
  240.9 11.3 %convolution_bitcast_fusion = f32[2048,512]{0,1:T(8,128)} fusion(f32[8,64,2048]{2,1,0:T(8,128)} %copy-done.10, f32[8,64,2048]{2,1,0:T(8,128)} %copy-done.9, f32[1,8,64,512]{3,2,1,0:T(8,128)} %param.33, f32[512]{0:T(512)S(1)} %copy-done.128, f32[8,64]{1,0:T(8,128)S(1)} %broadcast_multiply_fusion.2), kind=kOutput, calls=%fused_computation.41 | convolution fusion | flops 6445072384 | bytes 13635584 | tf_op jit(solution)/shard_map/transpose(jvp())/dot_general | solution.py:32
  252.9 13.5 %multiply_reduce_fusion.45 = (f32[960]{0:T(1024)S(1)}, f32[960]{0:T(1024)S(1)}, f32[960]{0:T(1024)S(1)}, f32[960]{0:T(1024)S(1)}, f32[960]{0:T(1024)S(1)}, /*ind...) fusion(f32[1,14,70,960]{3,2,1,0:T(8,128)} %copy-done.1, ...), kind=kLoop, calls=%fused_computation.250 | loop fusion | flops 13262400 | bytes 19713792 | tf_op jit(solution)/shard_map/transpose(jvp(jvp()))/checkpoint/reduce_sum | solution.py:52
  266.5 4.4 multiply_reduce_fusion.44
  271.0 4.4 multiply_reduce_fusion.48
  275.4 4.6 multiply_reduce_fusion.47
  280.0 4.5 multiply_reduce_fusion.46
  287.3 2.4 convolution_bitcast_fusion.4
  290.9 36.9 %reduce-scatter.17.cloned.1.call-done = f32[512,256]{1,0:T(8,128)} async-done(((f32[512,2048]{1,0:T(8,128)}), f32[512,256]{1,0:T(8,128)}) %reduce-scatter.17.cloned.1.call-update) | async-done | bytes 524304 | tf_op jit(solution)/shard_map/reduce_scatter | solution.py:195
  328.0 2.0 convolution_bitcast_fusion.7
  330.0 49.2 %reduce-scatter.21.cloned.1.call-done = f32[2048,64]{0,1:T(8,128)} async-done(((f32[2048,512]{0,1:T(8,128)}), f32[2048,64]{0,1:T(8,128)}) %reduce-scatter.21.cloned.1.call-update) | async-done | bytes 524304 | tf_op jit(solution)/shard_map/reduce_scatter | solution.py:196
  379.3 5.3 %fusion.138 = (f32[8,64]{1,0:T(8,128)S(1)}, f32[8,64,512]{2,1,0:T(8,128)S(1)}) fusion(f32[512]{0:T(512)S(1)} %copy-done.70, f32[8,64]{1,0:T(8,128)S(1)} %broadcast_multiply_fusion.1, f32[1,8,64,512]{3,2,1,0:T(8,128)S(1)} %copy-done.6, f32[8,64]{1,0:T(8,128)S(1)} %get-tuple-element.350, f32[512,1024]{1,0:T(8,128)S(1)} %copy-done, ...), kind=kOutput, calls=%fused_computation.324 | convolution fusion | flops 3223059968 | bytes 6299648 | tf_op jit(solution)/shard_map/transpose(jvp())/dot_general | solution.py:32
  386.3 38.8 %all-reduce.106 = (f32[512]{0:T(512)}, f32[64,128]{1,0:T(8,128)}, f32[512]{0:T(512)}, f32[512]{0:T(512)}, f32[512]{0:T(512)}) all-reduce(f32[512]{0:T(512)S(1)} %get-tuple-element.76, f32[64,128]{1,0:T(8,128)S(1)} %convolution_bitcast_fusion.7, f32[512]{0:T(512)S(1)} %copy-done.126, ...), channel_id=1, replica_groups=mesh['ha'=8,'ba'=4] {'ha','ba'}, use_global_device_ids=true, to_apply=%region_11.12 | all-reduce | flops 10240 | bytes 81920 | tf_op jit(solution)/shard_map/psum | solution.py:204
  425.1 2.9 add_multiply_fusion
  428.0 25.8 %all-reduce.110.cloned.1.call-done = (f32[49,960]{1,0:T(8,128)}, f32[128,256]{1,0:T(8,128)}, f32[256,512]{1,0:T(8,128)}) async-done(((f32[49,960]{1,0:T(8,128)}, f32[128,256]{1,0:T(8,128)}, f32[256,512]{1,0:T(8,128)}), (f32[49,960]{1,0:T(8,128)}, f32[128,256]{1,0:T(8,128)}, f32[256,512]{1,0:T(8,128)})) %all-reduce.110.cloned.1.call-update) | async-done | bytes 843536 | tf_op jit(solution)/shard_map/psum | solution.py:204
  453.8 6.9 %reduce-scatter.19.cloned.1.call-done = f32[128,256]{1,0:T(8,128)} async-done(((f32[512,256]{1,0:T(8,128)}), f32[128,256]{1,0:T(8,128)}) %reduce-scatter.19.cloned.1.call-update) | async-done | bytes 131088 | tf_op jit(solution)/shard_map/reduce_scatter | solution.py:201
  460.6 28.4 %reduce-scatter.23.cloned.1.call-done = f32[512,64]{0,1:T(8,128)} async-done(((f32[2048,64]{0,1:T(8,128)}), f32[512,64]{0,1:T(8,128)}) %reduce-scatter.23.cloned.1.call-update) | async-done | bytes 131088 | tf_op jit(solution)/shard_map/reduce_scatter | solution.py:202
  489.1 1.6 copy.37
  490.7 1.6 copy.38
  492.3 1.9 copy.39
  (333 shorter events, 32.6 us)
Async XLA Ops:
  8.1 281.7 %reduce-scatter.13.cloned.1.call-start = ((), (), s32[]{:S(2)}) async-start(), calls=%async_computation.10 | async-start | bytes 1179648 | tf_op jit(solution)/shard_map/reduce_scatter | solution.py:194
  19.7 8.1 %collective-permute-start = (f32[1,3,64,960]{3,2,1,0:T(8,128)}, f32[1,3,64,960]{3,2,1,0:T(8,128)}, u32[]{:S(2)}, u32[]{:S(2)}) collective-permute-start(f32[1,3,64,960]{3,2,1,0:T(8,128)} %get-tuple-element.147), channel_id=1, source_target_pairs={{0,4},{4,8},{8,12},{12,16},{16,20},{20,24},{24,28},{1,5},{5,9},{9,... | collective-permute-start | bytes 2211848 | tf_op jit(solution)/shard_map/ppermute | solution.py:22
  23.0 5.8 %collective-permute-start.1 = (f32[1,3,64,960]{3,2,1,0:T(8,128)}, f32[1,3,64,960]{3,2,1,0:T(8,128)}, u32[]{:S(2)}, u32[]{:S(2)}) collective-permute-start(f32[1,3,64,960]{3,2,1,0:T(8,128)} %get-tuple-element.148), channel_id=1, source_target_pairs={{4,0},{8,4},{12,8},{16,12},{20,16},{24,20},{28,24},{5,1},{9,5},{13... | collective-permute-start | bytes 2211848 | tf_op jit(solution)/shard_map/ppermute | solution.py:24
  30.9 20.4 %copy-start.1 = (f32[1,14,70,960]{3,2,1,0:T(8,128)}, f32[1,14,70,960]{3,2,1,0:T(8,128)S(1)}, u32[]{:S(2)}) copy-start(f32[1,14,70,960]{3,2,1,0:T(8,128)S(1)} %select_maximum_fusion) | copy-start | bytes 11289604
  30.9 20.4 %copy-start.37 = (f32[64,128]{1,0:T(8,128)S(1)}, f32[64,128]{1,0:T(8,128)}, u32[]{:S(2)}) copy-start(f32[64,128]{1,0:T(8,128)} %param.24) | copy-start | bytes 98308
  31.0 22.0 %copy-start.36 = (f32[128,256]{1,0:T(8,128)S(1)}, f32[128,256]{1,0:T(8,128)}, u32[]{:S(2)}) copy-start(f32[128,256]{1,0:T(8,128)} %param.25) | copy-start | bytes 393220
  51.4 67.3 %copy-start.7 = (f32[1,8,64,960]{3,2,1,0:T(8,128)}, f32[1,8,64,960]{3,2,1,0:T(8,128)S(1)}, u32[]{:S(2)}) copy-start(f32[1,8,64,960]{3,2,1,0:T(8,128)S(1)} %fusion.31) | copy-start | bytes 5898244
  53.6 62.9 %copy-start.17 = (f32[8,64,256]{2,1,0:T(8,128)}, f32[8,64,256]{2,1,0:T(8,128)S(1)}, u32[]{:S(2)}) copy-start(f32[8,64,256]{2,1,0:T(8,128)S(1)} %fusion.199) | copy-start | bytes 1572868
  56.9 46.0 %copy-start.11 = (f32[1,8,64,512]{3,2,1,0:T(8,128)}, f32[1,8,64,512]{3,2,1,0:T(8,128)S(1)}, u32[]{:S(2)}) copy-start(f32[1,8,64,512]{3,2,1,0:T(8,128)S(1)} %get-tuple-element.93) | copy-start | bytes 3145732
  76.9 26.0 %copy-start.9 = (f32[8,64,2048]{2,1,0:T(8,128)}, f32[8,64,2048]{2,1,0:T(8,128)S(1)}, u32[]{:S(2)}) copy-start(f32[8,64,2048]{2,1,0:T(8,128)S(1)} %get-tuple-element.352) | copy-start | bytes 12582916
  76.9 9.0 %copy-start.27 = (f32[2048,512]{1,0:T(8,128)S(1)}, f32[2048,512]{1,0:T(8,128)}, u32[]{:S(2)}) copy-start(f32[2048,512]{1,0:T(8,128)} %param.31) | copy-start | bytes 12582916
  76.9 9.0 %copy-start.28 = (f32[1,8,64,512]{3,2,1,0:T(8,128)S(1)}, f32[1,8,64,512]{3,2,1,0:T(8,128)}, u32[]{:S(2)}) copy-start(f32[1,8,64,512]{3,2,1,0:T(8,128)} %param.33) | copy-start | bytes 3145732
  76.9 9.0 %copy-start.127 = (f32[512]{0:T(512)S(1)}, f32[512]{0:T(512)}, u32[]{:S(2)}) copy-start(f32[512]{0:T(512)} %param.32) | copy-start | bytes 6148
  86.0 17.0 %copy-start.10 = (f32[8,64,2048]{2,1,0:T(8,128)}, f32[8,64,2048]{2,1,0:T(8,128)S(1)}, u32[]{:S(2)}) copy-start(f32[8,64,2048]{2,1,0:T(8,128)S(1)} %fusion) | copy-start | bytes 12582916
  131.9 158.4 %reduce-scatter.9.cloned.1.call-start = ((), (), s32[]{:S(2)}) async-start(), calls=%async_computation.8 | async-start | bytes 2359296 | tf_op jit(solution)/shard_map/reduce_scatter | solution.py:193
  144.1 7.6 %copy-start.99 = (f32[1,960]{1,0:T(1,128)S(1)}, f32[1,960]{1,0:T(1,128)}, u32[]{:S(2)}) copy-start(f32[1,960]{1,0:T(1,128)} %get-tuple-element.174) | copy-start | bytes 11524
  144.1 7.5 %copy-start.100 = (f32[1,960]{1,0:T(1,128)S(1)}, f32[1,960]{1,0:T(1,128)}, u32[]{:S(2)}) copy-start(f32[1,960]{1,0:T(1,128)} %get-tuple-element.175) | copy-start | bytes 11524
  144.1 7.5 %copy-start.105 = (f32[1,960]{1,0:T(1,128)S(1)}, f32[1,960]{1,0:T(1,128)}, u32[]{:S(2)}) copy-start(f32[1,960]{1,0:T(1,128)} %get-tuple-element.167) | copy-start | bytes 11524
  144.1 7.5 %copy-start.106 = (f32[1,960]{1,0:T(1,128)S(1)}, f32[1,960]{1,0:T(1,128)}, u32[]{:S(2)}) copy-start(f32[1,960]{1,0:T(1,128)} %get-tuple-element.168) | copy-start | bytes 11524
  144.1 7.5 %copy-start.107 = (f32[1,960]{1,0:T(1,128)S(1)}, f32[1,960]{1,0:T(1,128)}, u32[]{:S(2)}) copy-start(f32[1,960]{1,0:T(1,128)} %get-tuple-element.169) | copy-start | bytes 11524
  144.1 7.5 %copy-start.108 = (f32[1,960]{1,0:T(1,128)S(1)}, f32[1,960]{1,0:T(1,128)}, u32[]{:S(2)}) copy-start(f32[1,960]{1,0:T(1,128)} %get-tuple-element.170) | copy-start | bytes 11524
  151.7 7.6 %copy-start.55 = (f32[8,64]{1,0:T(8,128)S(1)}, f32[8,64]{1,0:T(8,128)}, u32[]{:S(2)}) copy-start(f32[8,64]{1,0:T(8,128)} %get-tuple-element.327) | copy-start | bytes 6148
  151.7 7.6 %copy-start.57 = (f32[8,64]{1,0:T(8,128)S(1)}, f32[8,64]{1,0:T(8,128)}, u32[]{:S(2)}) copy-start(f32[8,64]{1,0:T(8,128)} %get-tuple-element.328) | copy-start | bytes 6148
  151.7 7.6 %copy-start.59 = (f32[8,64]{1,0:T(8,128)S(1)}, f32[8,64]{1,0:T(8,128)}, u32[]{:S(2)}) copy-start(f32[8,64]{1,0:T(8,128)} %get-tuple-element.329) | copy-start | bytes 6148
  151.7 7.6 %copy-start.90 = (f32[1,960]{1,0:T(1,128)S(1)}, f32[1,960]{1,0:T(1,128)}, u32[]{:S(2)}) copy-start(f32[1,960]{1,0:T(1,128)} %get-tuple-element.193) | copy-start | bytes 11524
  151.8 7.6 %copy-start.91 = (f32[1,960]{1,0:T(1,128)S(1)}, f32[1,960]{1,0:T(1,128)}, u32[]{:S(2)}) copy-start(f32[1,960]{1,0:T(1,128)} %get-tuple-element.176) | copy-start | bytes 11524
  151.8 7.6 %copy-start.92 = (f32[1,960]{1,0:T(1,128)S(1)}, f32[1,960]{1,0:T(1,128)}, u32[]{:S(2)}) copy-start(f32[1,960]{1,0:T(1,128)} %get-tuple-element.177) | copy-start | bytes 11524
  151.8 7.6 %copy-start.93 = (f32[1,960]{1,0:T(1,128)S(1)}, f32[1,960]{1,0:T(1,128)}, u32[]{:S(2)}) copy-start(f32[1,960]{1,0:T(1,128)} %get-tuple-element.178) | copy-start | bytes 11524
  151.8 7.6 %copy-start.94 = (f32[1,960]{1,0:T(1,128)S(1)}, f32[1,960]{1,0:T(1,128)}, u32[]{:S(2)}) copy-start(f32[1,960]{1,0:T(1,128)} %get-tuple-element.179) | copy-start | bytes 11524
  151.8 7.6 %copy-start.95 = (f32[1,960]{1,0:T(1,128)S(1)}, f32[1,960]{1,0:T(1,128)}, u32[]{:S(2)}) copy-start(f32[1,960]{1,0:T(1,128)} %get-tuple-element.180) | copy-start | bytes 11524
  151.8 7.6 %copy-start.96 = (f32[1,960]{1,0:T(1,128)S(1)}, f32[1,960]{1,0:T(1,128)}, u32[]{:S(2)}) copy-start(f32[1,960]{1,0:T(1,128)} %get-tuple-element.181) | copy-start | bytes 11524
  151.8 7.6 %copy-start.97 = (f32[1,960]{1,0:T(1,128)S(1)}, f32[1,960]{1,0:T(1,128)}, u32[]{:S(2)}) copy-start(f32[1,960]{1,0:T(1,128)} %get-tuple-element.182) | copy-start | bytes 11524
  151.8 7.6 %copy-start.98 = (f32[1,960]{1,0:T(1,128)S(1)}, f32[1,960]{1,0:T(1,128)}, u32[]{:S(2)}) copy-start(f32[1,960]{1,0:T(1,128)} %get-tuple-element.183) | copy-start | bytes 11524
  206.4 13.3 %collective-permute-start.2 = (f32[1,3,64,960]{3,2,1,0:T(8,128)S(1)}, f32[1,3,64,960]{3,2,1,0:T(8,128)S(1)}, u32[]{:S(2)}, u32[]{:S(2)}) collective-permute-start(f32[1,3,64,960]{3,2,1,0:T(8,128)S(1)} %get-tuple-element.96), channel_id=1, source_target_pairs={{0,4},{4,8},{8,12},{12,16},{16,20},{20,24},{24,28},{1,5},{5,9},{9,... | collective-permute-start | bytes 2211848 | tf_op jit(solution)/shard_map/ppermute | solution.py:22
  217.9 4.3 collective-permute-start.3
  229.8 98.0 %reduce-scatter.17.cloned.1.call-start = ((), (), s32[]{:S(2)}) async-start(), calls=%async_computation.12 | async-start | bytes 4718592 | tf_op jit(solution)/shard_map/reduce_scatter | solution.py:195
  240.3 138.9 %reduce-scatter.21.cloned.1.call-start = ((), (), s32[]{:S(2)}) async-start(), calls=%async_computation.14 | async-start | bytes 4718592 | tf_op jit(solution)/shard_map/reduce_scatter | solution.py:196
  252.3 201.5 %all-reduce.110.cloned.1.call-start = ((), (), s32[]{:S(2)}) async-start(), calls=%async_computation.16 | async-start | bytes 1769472 | tf_op jit(solution)/shard_map/psum | solution.py:204
  252.9 13.5 %copy-start.3 = (f32[1,14,70,960]{3,2,1,0:T(8,128)S(1)}, f32[1,14,70,960]{3,2,1,0:T(8,128)}, u32[]{:S(2)}) copy-start(f32[1,14,70,960]{3,2,1,0:T(8,128)} %copy-done.1) | copy-start | bytes 11289604
  252.9 13.5 %copy-start.5 = (f32[1,8,64,960]{3,2,1,0:T(8,128)S(1)}, f32[1,8,64,960]{3,2,1,0:T(8,128)}, u32[]{:S(2)}) copy-start(f32[1,8,64,960]{3,2,1,0:T(8,128)} %pad_add_fusion.1) | copy-start | bytes 5898244
  252.9 13.5 %copy-start.52 = (f32[8,64]{1,0:T(8,128)S(1)}, f32[8,64]{1,0:T(8,128)}, u32[]{:S(2)}) copy-start(f32[8,64]{1,0:T(8,128)} %get-tuple-element.335) | copy-start | bytes 6148
  252.9 13.5 %copy-start.54 = (f32[8,64]{1,0:T(8,128)S(1)}, f32[8,64]{1,0:T(8,128)}, u32[]{:S(2)}) copy-start(f32[8,64]{1,0:T(8,128)} %get-tuple-element.336) | copy-start | bytes 6148
  287.3 40.8 %copy-start.26 = (f32[8,64,128]{2,1,0:T(8,128)S(1)}, f32[8,64,128]{2,1,0:T(8,128)}, u32[]{:S(2)}) copy-start(f32[8,64,128]{2,1,0:T(8,128)} %fusion.171) | copy-start | bytes 786436
  289.6 89.6 %copy-start.70 = (f32[512]{0:T(512)S(1)}, f32[512]{0:T(512)}, u32[]{:S(2)}) copy-start(f32[512]{0:T(512)} %param.21) | copy-start | bytes 6148
  289.7 164.1 %reduce-scatter.15.cloned.1.call-start = ((), (), s32[]{:S(2)}) async-start(), calls=%async_computation.11 | async-start | bytes 163840 | tf_op jit(solution)/shard_map/reduce_scatter | solution.py:200
  290.2 163.5 %reduce-scatter.11.cloned.1.call-start = ((), (), s32[]{:S(2)}) async-start(), calls=%async_computation.9 | async-start | bytes 327680 | tf_op jit(solution)/shard_map/reduce_scatter | solution.py:199
  290.8 169.8 %reduce-scatter.19.cloned.1.call-start = ((), (), s32[]{:S(2)}) async-start(), calls=%async_computation.13 | async-start | bytes 655360 | tf_op jit(solution)/shard_map/reduce_scatter | solution.py:201
  327.8 161.3 %reduce-scatter.23.cloned.1.call-start = ((), (), s32[]{:S(2)}) async-start(), calls=%async_computation.15 | async-start | bytes 655360 | tf_op jit(solution)/shard_map/reduce_scatter | solution.py:202
  (96 other events, 481.8 us)
Sparse Core Ops, SparseCore 0:
  132.1 41.8 reduce-scatter.12
  229.9 44.7 reduce-scatter.8
  277.0 50.7 reduce-scatter.16
  329.9 49.2 reduce-scatter.20
  382.4 22.3 reduce-scatter.14
  408.2 24.1 reduce-scatter.10
  435.8 24.7 reduce-scatter.18
  464.3 24.7 reduce-scatter.22
Sparse Core Ops, SparseCore 1:
  289.7 164.0 all-reduce.109
where the time goes:
time: 504 us; the launch traced here: 502 us
  other arithmetic  156 us (31%)
  waiting for transfers between devices  152 us (30%)
  matrix products  102 us (20%)
  blocking collectives  38.8 us (8%)
  starting transfers between devices  18.6 us (4%)
  between operations  17.9 us (4%)
  local copies, waits for them, and re-layouts  16.7 us (3%)
    dot_general x21, matrix products, matmul(): jnp.dot(left, right, precision=lax.Precision.HIGHEST, preferred_element_t...  102 us
    reduce_scatter x1, waiting for transfers between devices, shards(): lax.psum_scatter(grads[11], 'ha', scatter_dimension=1, tiled=True)  49.2 us
    mul x15, other arithmetic, masked_depthwise(): kernel[tap_row * KERN + tap_col] * window  40.9 us
    psum x1, blocking collectives, shards(): lax.psum((grad_gain_one, grads[3], grads[4], grads[5], grads[6], grads[8]...  38.8 us
    reduce_scatter x1, waiting for transfers between devices, shards(): lax.psum_scatter(grads[10], 'ha', scatter_dimension=1, tiled=True)  36.9 us
    reduce_sum x6, other arithmetic, masked_depthwise(): kernel[tap_row * KERN + tap_col] * window  36.3 us
    add_any x1, other arithmetic, masked_depthwise(): padded[..., tap_row:tap_row + row_count, tap_col:tap_col + col_count, :]  31.6 us
    reduce_scatter x1, waiting for transfers between devices, shards(): lax.psum_scatter(partial_large[3], 'ba', scatter_dimension=0, tiled=True)  28.4 us
  transfers between devices with their start and end apart: 13, of which 7 were waited for; matrix products, arithmetic and copies ran while one was open for 30% of the time, Pallas kernels for 0%

commit v1 on v0

v1 whole, which is shorter than its diff:
```python
import functools

import jax
import jax.numpy as jnp
from jax import lax
from jax.experimental import pallas as pl
from jax.experimental.pallas import tpu as pltpu
from jax.sharding import PartitionSpec as P

KERN = 7
REACH = KERN // 2
KEEP_RATE = 0.8
SPREAD = 1.0 / 3.0
EPSILON = 1e-06
LANES = 128
EDGE = 8
VMEM_BYTES = 56 << 20
F32 = jnp.float32
BF16 = jnp.bfloat16
INV_SQRT_2 = 0.7071067811865476
INV_SQRT_2PI = 0.3989422804014327
NN = (((1,), (0,)), ((), ()))
NT = (((1,), (1,)), ((), ()))
TN = (((0,), (0,)), ((), ()))


def halves(x):
    high = x.astype(BF16)
    return high, (x - high.astype(F32)).astype(BF16)


def dot_once(left, right, dims):
    return lax.dot_general(left, right, dims, preferred_element_type=F32)


def dot_pairs(left, right, dims=NN):
    return dot_once(left[0], right[0], dims) + (
        dot_once(left[0], right[1], dims) + dot_once(left[1], right[0], dims)
    )


def dot(left, right, dims=NN):
    return dot_pairs(halves(left), halves(right), dims)


def normalized(values):
    centered = values - jnp.mean(values, axis=-1, keepdims=True)
    scale = lax.rsqrt(jnp.mean(centered * centered, axis=-1, keepdims=True) + EPSILON)
    return centered * scale, scale


def norm_backward(grad_hat, hat, scale):
    return scale * (
        grad_hat
        - jnp.mean(grad_hat, axis=-1, keepdims=True)
        - hat * jnp.mean(grad_hat * hat, axis=-1, keepdims=True)
    )


def params():
    return pltpu.CompilerParams(vmem_limit_bytes=VMEM_BYTES)


def lasting(microseconds):
    return pl.CostEstimate(flops=int(microseconds * 1.1e9), bytes_accessed=0, transcendentals=0)


def whole(shape):
    return pl.BlockSpec(shape, lambda *_: (0,) * len(shape))


def shape_of(*shape):
    return jax.ShapeDtypeStruct(shape, F32)


def masks_kernel(
    first_row, keep_one, keep_two, ids_ref, middle_ref, valid_ref, one_ref, two_ref, row_ref, col_ref, *, rows, height
):
    cols = ids_ref.shape[1]
    slots = keep_one.shape[1]
    start = first_row[0]
    ids = ids_ref[pl.ds(start, rows + 2 * REACH), :]
    turned = jnp.concatenate([ids, jnp.full((-ids.shape[0] % 8, cols), -1, jnp.int32)], axis=0).T
    own = turned[:, REACH : REACH + rows]
    one = jnp.zeros(own.shape, F32)
    two = jnp.zeros(own.shape, F32)
    for slot in range(slots):
        hit = own == slot
        one = jnp.where(hit, keep_one[0, slot].astype(F32) / KEEP_RATE, one)
        two = jnp.where(hit, keep_two[0, slot].astype(F32) / KEEP_RATE, two)
    valid = (turned >= 0).astype(F32)
    for r in range(rows + 2 * REACH):
        valid_ref[r] = jnp.broadcast_to(valid[:, r : r + 1], (cols, LANES))
    for r in range(rows):
        one_ref[r] = jnp.broadcast_to(one[:, r : r + 1], (cols, LANES))
        two_ref[r] = jnp.broadcast_to(two[:, r : r + 1], (cols, LANES))
    tall = middle_ref[...]
    wide_ids = jnp.broadcast_to(tall, (cols, LANES))
    column = lax.broadcasted_iota(jnp.int32, (cols, LANES), 0)
    for b in range(KERN):
        shift = b - REACH
        moved = pltpu.roll(wide_ids, (-shift) % cols, 0)
        inside = (column + shift >= 0) & (column + shift < cols)
        same = (moved == wide_ids) & inside
        col_ref[b] = same.astype(F32).reshape(cols // 8, 8, LANES)
    across = ids_ref[pl.ds(start, rows + 2 * REACH), cols // 2 : cols // 2 + 1]
    place = start - REACH + lax.broadcasted_iota(jnp.int32, across.shape, 0)
    across = jnp.where((place >= 0) & (place < height), across, -2)
    lane = lax.broadcasted_iota(jnp.int32, (rows, LANES), 1)
    mask = jnp.zeros((rows, LANES), F32)
    for a in range(KERN):
        same = (across[a : a + rows] == across[REACH : REACH + rows]).astype(F32)
        mask = jnp.where(lane == a + 1, same, mask)
    row_ref[...] = mask


def masks(first_row, keep_one, keep_two, ids, rows):
    cols = ids.shape[1]
    padded = jnp.pad(ids, ((REACH, 16 - REACH), (0, 0)), constant_values=-1)
    middle = ids[ids.shape[0] // 2][:, None]
    smem = pl.BlockSpec(memory_space=pltpu.SMEM)
    return pl.pallas_call(
        functools.partial(masks_kernel, rows=rows, height=ids.shape[0]),
        in_specs=[smem, smem, smem, whole(padded.shape), whole(middle.shape)],
        out_shape=[
            shape_of(rows + 2 * REACH, cols, LANES),
            shape_of(rows, cols, LANES),
            shape_of(rows, cols, LANES),
            shape_of(rows, LANES),
            shape_of(KERN, cols // 8, 8, LANES),
        ],
        compiler_params=params(),
        cost_estimate=lasting(2),
    )(first_row, keep_one, keep_two, padded, middle)


def head_kernel(canvas_ref, valid_ref, gain_ref, weight_ref, out_ref, high, low):
    @pl.when(pl.program_id(0) == 0)
    def _():
        hat, _ = normalized(canvas_ref[...] * valid_ref[:, :1])
        high[...], low[...] = halves(hat * gain_ref[...])

    joined = dot_pairs((high[...], low[...]), halves(weight_ref[...]))
    for k in range(out_ref.shape[0]):
        out_ref[k] = joined[:, k * LANES : (k + 1) * LANES]


def head_forward(canvas, valid, gain, weight):
    cells, dim = canvas.shape
    blocks = weight.shape[1] // LANES
    return pl.pallas_call(
        head_kernel,
        grid=(blocks // 2,),
        in_specs=[
            whole((cells, dim)),
            whole((cells, LANES)),
            whole((1, dim)),
            pl.BlockSpec((dim, 2 * LANES), lambda i: (0, i)),
        ],
        out_specs=pl.BlockSpec((2, cells, LANES), lambda i: (i, 0, 0)),
        out_shape=shape_of(blocks, cells, LANES),
        scratch_shapes=[pltpu.VMEM((cells, dim), BF16), pltpu.VMEM((cells, dim), BF16)],
        compiler_params=params(),
        cost_estimate=lasting(4),
    )(canvas, valid, gain, weight)


def fill_shifted(above_ref, own_ref, below_ref, col_ref, flat, shifted, rows_ext, cols):
    groups = cols // 8
    reach = above_ref.shape[1]
    cells = own_ref.shape[1]
    flat[:EDGE] = jnp.zeros((EDGE, LANES), F32)
    flat[EDGE : EDGE + reach] = above_ref[0]
    flat[EDGE + reach : EDGE + reach + cells] = own_ref[0]
    flat[EDGE + reach + cells : EDGE + 2 * reach + cells] = below_ref[0]
    flat[EDGE + 2 * reach + cells :] = jnp.zeros((EDGE, LANES), F32)
    for b in range(KERN):
        mask = col_ref[b]

        def some(h, _, b=b, mask=mask):
            for k in range(2):
                r = 2 * h + k
                start = pl.multiple_of(r * cols, cols) + (EDGE + b - REACH)
                x = flat[pl.ds(start, cols), :].reshape(groups, 8, LANES)
                shifted[b, r] = x if b == REACH else x * mask
            return 0

        lax.fori_loop(0, rows_ext // 2, some, 0)


def conv_kernel(
    row_mask, above_ref, own_ref, below_ref, kern_ref, col_ref, out_ref, flat, shifted, wide, *, rows, cols
):
    groups = cols // 8
    fill_shifted(above_ref, own_ref, below_ref, col_ref, flat, shifted, rows + 2 * REACH, cols)
    for t in range(KERN):
        wide[t] = jnp.zeros((8, LANES), F32)
        wide[KERN * (KERN + 1) + t] = jnp.zeros((8, LANES), F32)
    for t in range(KERN * KERN):
        wide[KERN + t] = jnp.broadcast_to(kern_ref[t : t + 1, :] * SPREAD, (8, LANES))

    def pair(h, _):
        r = 2 * h

        def step(i, totals):
            first, second = totals
            mask_first = row_mask[r, i + 1]
            mask_second = row_mask[r + 1, i]
            for b in range(KERN):
                x = shifted[b, r + i]
                first = first + (wide[(i + 1) * KERN + b] * mask_first)[None] * x
                second = second + (wide[i * KERN + b] * mask_second)[None] * x
            return first, second

        zero = jnp.zeros((groups, 8, LANES), F32)
        first, second = lax.fori_loop(0, KERN + 1, step, (zero, zero))
        out_ref[pl.ds(pl.multiple_of(r * cols, cols), cols), :] = first.reshape(cols, LANES)
        out_ref[pl.ds(pl.multiple_of((r + 1) * cols, cols), cols), :] = second.reshape(cols, LANES)
        return 0

    lax.fori_loop(0, rows // 2, pair, 0)


def conv_specs(reach, cells):
    return [
        pl.BlockSpec(memory_space=pltpu.SMEM),
        pl.BlockSpec((1, reach, LANES), lambda i: (i, 0, 0)),
        pl.BlockSpec((1, cells, LANES), lambda i: (i, 0, 0)),
        pl.BlockSpec((1, reach, LANES), lambda i: (i, 0, 0)),
    ]


def conv_scratch(rows, cols):
    cells_ext = (rows + 2 * REACH) * cols
    return [
        pltpu.VMEM((cells_ext + 2 * EDGE, LANES), F32),
        pltpu.VMEM((KERN, rows + 2 * REACH, cols // 8, 8, LANES), F32),
    ]


def conv_forward(row_mask, above, own, below, kern, col_mask, rows, cols):
    blocks = own.shape[0]
    taps = KERN * KERN
    return pl.pallas_call(
        functools.partial(conv_kernel, rows=rows, cols=cols),
        grid=(blocks,),
        in_specs=conv_specs(REACH * cols, rows * cols)
        + [pl.BlockSpec((taps, LANES), lambda i: (0, i)), whole((KERN, cols // 8, 8, LANES))],
        out_specs=pl.BlockSpec((rows * cols, LANES), lambda i: (0, i)),
        out_shape=shape_of(rows * cols, blocks * LANES),
        scratch_shapes=conv_scratch(rows, cols) + [pltpu.VMEM((KERN * (KERN + 2), 8, LANES), F32)],
        compiler_params=params(),
        cost_estimate=lasting(16),
    )(row_mask, above, own, below, kern, col_mask)


def conv_grad_kernel(
    row_mask, above_ref, own_ref, below_ref, mix_ref, kern_ref, col_ref, out_ref, dk_ref, flat, shifted, wide, dk,
    *, rows, cols,
):
    groups = cols // 8
    taps = KERN * KERN
    fill_shifted(above_ref, own_ref, below_ref, col_ref, flat, shifted, rows + 2 * REACH, cols)
    for t in range(taps):
        wide[t] = jnp.broadcast_to(kern_ref[taps - 1 - t : taps - t, :] * SPREAD, (8, LANES))
        dk[t] = jnp.zeros((8, LANES), F32)

    def one(r, _):
        mix = mix_ref[0, pl.ds(pl.multiple_of(r * cols, cols), cols), :].reshape(groups, 8, LANES)

        def step(i, total):
            mask = row_mask[r, i + 1]
            for b in range(KERN):
                x = shifted[b, r + i]
                total = total + (wide[i * KERN + b] * mask)[None] * x
                dk[i * KERN + b] += jnp.sum(mix * x, axis=0) * mask
            return total

        total = lax.fori_loop(0, KERN, step, jnp.zeros((groups, 8, LANES), F32))
        out_ref[pl.ds(pl.multiple_of(r * cols, cols), cols), :] = total.reshape(cols, LANES)
        return 0

    lax.fori_loop(0, rows, one, 0)
    for t in range(taps):
        dk_ref[0, taps - 1 - t : taps - t, :] = jnp.sum(dk[t], axis=0, keepdims=True) * SPREAD
    dk_ref[0, taps:, :] = jnp.zeros((dk_ref.shape[1] - taps, LANES), F32)


def conv_backward(row_mask, above, own, below, mix, kern, col_mask, rows, cols):
    blocks = own.shape[0]
    taps = KERN * KERN
    tall = -(-taps // 8) * 8
    return pl.pallas_call(
        functools.partial(conv_grad_kernel, rows=rows, cols=cols),
        grid=(blocks,),
        in_specs=conv_specs(REACH * cols, rows * cols)
        + [
            pl.BlockSpec((1, rows * cols, LANES), lambda i: (i, 0, 0)),
            pl.BlockSpec((taps, LANES), lambda i: (0, i)),
            whole((KERN, cols // 8, 8, LANES)),
        ],
        out_specs=[
            pl.BlockSpec((rows * cols, LANES), lambda i: (0, i)),
            pl.BlockSpec((1, tall, LANES), lambda i: (i, 0, 0)),
        ],
        out_shape=[shape_of(rows * cols, blocks * LANES), shape_of(blocks, tall, LANES)],
        scratch_shapes=conv_scratch(rows, cols)
        + [pltpu.VMEM((taps, 8, LANES), F32), pltpu.VMEM((taps, 8, LANES), F32)],
        compiler_params=params(),
        cost_estimate=lasting(24),
    )(row_mask, above, own, below, mix, kern, col_mask)


def gates_kernel(
    conv_ref, canvas_ref, valid_ref, keep_ref, scale_ref, one_ref, two_ref, three_ref, out_ref,
    middle_ref, mixed_ref, mapped_ref,
):
    split = one_ref.shape[0]
    mixed = conv_ref[:, :split] * conv_ref[:, split : 2 * split]
    mixed_ref[:, :split] = mixed
    mixed_ref[:, split : 2 * split] = jnp.zeros_like(mixed)
    start = 2 * split
    for ref in (one_ref, two_ref, three_ref):
        width = ref.shape[1]
        mapped = dot(mixed, ref[...])
        mapped_ref[:, start - 2 * split : start - 2 * split + width] = mapped
        mixed = mapped * conv_ref[:, start : start + width]
        mixed_ref[:, start : start + width] = mixed
        start += width
    branch = dot(mixed, out_ref[...])
    middle_ref[...] = canvas_ref[...] * valid_ref[:, :1] + keep_ref[:, :1] * scale_ref[...] * branch


def row_blocks(cells, width, tile):
    return pl.BlockSpec((tile, width), lambda i: (i, 0))


def gates_forward(conv, canvas, valid, keep, scale, gates, weight_out, tile=256):
    cells, dim = canvas.shape
    wide = conv.shape[1]
    narrow = wide - 2 * gates[0].shape[0]
    return pl.pallas_call(
        gates_kernel,
        grid=(cells // tile,),
        in_specs=[
            row_blocks(cells, wide, tile),
            row_blocks(cells, dim, tile),
            row_blocks(cells, LANES, tile),
            row_blocks(cells, LANES, tile),
            whole(scale.shape),
        ]
        + [whole(g.shape) for g in gates]
        + [whole(weight_out.shape)],
        out_specs=[row_blocks(cells, dim, tile), row_blocks(cells, wide, tile), row_blocks(cells, narrow, tile)],
        out_shape=[shape_of(cells, dim), shape_of(cells, wide), shape_of(cells, narrow)],
        compiler_params=params(),
        cost_estimate=lasting(6),
    )(conv, canvas, valid, keep, scale, *gates, weight_out)


def gates_grad_kernel(
    grad_ref, conv_ref, mapped_ref, keep_ref, scale_ref, one_ref, two_ref, three_ref, out_ref, dconv_ref, dmapped_ref
):
    split = one_ref.shape[0]
    grad = dot(keep_ref[:, :1] * grad_ref[...] * scale_ref[...], out_ref[...], NT)
    start = conv_ref.shape[1]
    for ref in (three_ref, two_ref, one_ref):
        width = ref.shape[1]
        start -= width
        dconv = grad * mapped_ref[:, start - 2 * split : start - 2 * split + width]
        for k in range(width // LANES):
            dconv_ref[start // LANES + k] = dconv[:, k * LANES : (k + 1) * LANES]
        grad_mapped = grad * conv_ref[:, start : start + width]
        dmapped_ref[:, start - 2 * split : start - 2 * split + width] = grad_mapped
        grad = dot(grad_mapped, ref[...], NT)
    dconv_ref[0, :, split : 2 * split] = grad * conv_ref[:, :split]
    dconv_ref[0, :, :split] = grad * conv_ref[:, split : 2 * split]


def gates_backward(grad, conv, mapped, keep, scale, gates, weight_out, tile=256):
    cells, dim = grad.shape
    wide = conv.shape[1]
    narrow = mapped.shape[1]
    return pl.pallas_call(
        gates_grad_kernel,
        grid=(cells // tile,),
        in_specs=[
            row_blocks(cells, dim, tile),
            row_blocks(cells, wide, tile),
            row_blocks(cells, narrow, tile),
            row_blocks(cells, LANES, tile),
            whole(scale.shape),
        ]
        + [whole(g.shape) for g in gates]
        + [whole(weight_out.shape)],
        out_specs=[
            pl.BlockSpec((wide // LANES, tile, LANES), lambda i: (0, i, 0)),
            row_blocks(cells, narrow, tile),
        ],
        out_shape=[shape_of(wide // LANES, cells, LANES), shape_of(cells, narrow)],
        compiler_params=params(),
        cost_estimate=lasting(5),
    )(grad, conv, mapped, keep, scale, *gates, weight_out)


def share(core, first, second, kept_ref, sent_ref, place):
    mine = core == 0
    kept_ref[place] = jnp.where(mine, first, second)
    sent_ref[place] = jnp.where(mine, second, first)


def gates_weight_kernel(
    core_ref, grad_ref, keep_ref, scale_ref, out_ref, mixed_ref, dmapped_ref, dgain_ref, dscale_ref,
    kept_ref, sent_ref, packed_ref, *, widths,
):
    split = widths[0]
    kept = keep_ref[:, :1] * grad_ref[...]
    start = 2 * split
    source = 0
    row = 0
    for level in range(len(widths) - 1):
        tall, width = widths[level], widths[level + 1]
        part = dot(
            mixed_ref[:, source : source + tall], dmapped_ref[:, start - 2 * split : start - 2 * split + width], TN
        )
        for k in range(width // LANES):
            packed_ref[row : row + tall] = part[:, k * LANES : (k + 1) * LANES]
            row += tall
        source = start
        start += width
    crossed = dot(mixed_ref[:, source:], kept, TN)
    dscale = jnp.sum(crossed * out_ref[...], axis=0, keepdims=True)
    packed_ref[row:] = jnp.zeros((packed_ref.shape[0] - row, LANES), F32)
    for vector in (dscale, dgain_ref[...], dscale_ref[...]):
        for k in range(vector.shape[1] // LANES):
            packed_ref[row : row + 1] = vector[:, k * LANES : (k + 1) * LANES]
            row += 1
    turned = (crossed * scale_ref[...]).T
    groups, parts, tall, width = kept_ref.shape
    for z in range(groups):
        for p in range(parts):
            base = 2 * z * tall
            columns = slice(p * width, (p + 1) * width)
            share(
                core_ref[0],
                turned[base : base + tall, columns],
                turned[base + tall : base + 2 * tall, columns],
                kept_ref,
                sent_ref,
                (z, p),
            )


def gates_weights(core, grad, keep, scale, weight_out, mixed, dmapped, dgain, dscale, widths, count_ha, count_ba):
    dim, width = weight_out.shape
    chunks = shape_of(count_ha // 2, count_ba, width // count_ha, dim // count_ba)
    rows = sum(a * b for a, b in zip(widths[:-1], widths[1:])) // LANES + 3 * width // LANES
    rows = -(-rows // 16) * 16
    return pl.pallas_call(
        functools.partial(gates_weight_kernel, widths=widths),
        in_specs=[pl.BlockSpec(memory_space=pltpu.SMEM)] + [pl.BlockSpec(memory_space=pltpu.VMEM)] * 8,
        out_shape=[chunks, chunks, shape_of(rows, LANES)],
        compiler_params=params(),
        cost_estimate=lasting(5),
    )(core, grad, keep, scale, weight_out, mixed, dmapped, dgain, dscale)


def share_columns(core, grad, kept_ref, sent_ref):
    groups, parts, tall, width = kept_ref.shape
    for z in range(groups):
        first = grad[:, 2 * z * width : (2 * z + 1) * width].reshape(parts, tall, width)
        second = grad[:, (2 * z + 1) * width : (2 * z + 2) * width].reshape(parts, tall, width)
        share(core, first, second, kept_ref, sent_ref, z)


def ffn_kernel(
    core_ref, middle_ref, cot_ref, keep_ref, gain_ref, scale_ref, up_ref, down_ref,
    out_ref, dmiddle_ref, up_kept_ref, up_sent_ref, down_kept_ref, down_sent_ref, dgain_ref, dscale_ref,
    n_high, n_low, nt_high, nt_low, y_high, y_low, yt_high, yt_low, result, dnorm,
):
    step = pl.program_id(0)

    @pl.when(step == 0)
    def _():
        hat, _ = normalized(middle_ref[...])
        normed = hat * gain_ref[...]
        n_high[...], n_low[...] = halves(normed)
        nt_high[...], nt_low[...] = halves(normed.T)
        grad = keep_ref[:, :1] * scale_ref[...] * cot_ref[...]
        y_high[...], y_low[...] = halves(grad)
        yt_high[...], yt_low[...] = halves(grad.T)
        result[...] = jnp.zeros_like(result)
        dnorm[...] = jnp.zeros_like(dnorm)

    up = halves(up_ref[...])
    down = halves(down_ref[...])
    pre = dot_pairs((n_high[...], n_low[...]), up)
    cdf = 0.5 + 0.5 * lax.erf(pre * INV_SQRT_2)
    slope = cdf + pre * (INV_SQRT_2PI * jnp.exp(-0.5 * pre * pre))
    hidden = halves(pre * cdf)
    result[...] += dot_pairs(hidden, down)
    grad_pre = halves(dot_pairs((y_high[...], y_low[...]), down, NT) * slope)
    ddown = dot_pairs((yt_high[...], yt_low[...]), hidden)
    groups, parts, tall, width = down_kept_ref.shape
    for z in range(groups):
        for p in range(parts):
            base = 2 * z * tall
            columns = slice(p * width, (p + 1) * width)
            share(
                core_ref[0],
                ddown[base : base + tall, columns],
                ddown[base + tall : base + 2 * tall, columns],
                down_kept_ref,
                down_sent_ref,
                (z, p),
            )
    share_columns(
        core_ref[0], dot_pairs((nt_high[...], nt_low[...]), grad_pre), up_kept_ref, up_sent_ref
    )
    dnorm[...] += dot_pairs(grad_pre, up, NT)

    @pl.when(step == pl.num_programs(0) - 1)
    def _():
        hat, scale = normalized(middle_ref[...])
        kept = keep_ref[:, :1] * result[...]
        out_ref[...] = middle_ref[...] + scale_ref[...] * kept
        dscale_ref[...] = jnp.sum(cot_ref[...] * kept, axis=0, keepdims=True)
        dgain_ref[...] = jnp.sum(dnorm[...] * hat, axis=0, keepdims=True)
        dmiddle_ref[...] = cot_ref[...] + norm_backward(dnorm[...] * gain_ref[...], hat, scale)


def ffn(core, middle, cot, keep, gain, scale, weight_up, weight_down, count_ha, count_ba, chunk=512):
    cells, dim = middle.shape
    hidden = weight_up.shape[1]
    pair = [pltpu.VMEM((cells, dim), BF16)] * 2
    pair_turned = [pltpu.VMEM((dim, cells), BF16)] * 2
    up_wide, down_wide = hidden // count_ha, hidden // count_ba
    up = pl.BlockSpec((chunk // (2 * up_wide), count_ba, dim // count_ba, up_wide), lambda i: (i, 0, 0, 0))
    down = pl.BlockSpec((count_ha // 2, chunk // down_wide, dim // count_ha, down_wide), lambda i: (0, i, 0, 0))
    up_shape = shape_of(count_ha // 2, count_ba, dim // count_ba, up_wide)
    down_shape = shape_of(count_ha // 2, count_ba, dim // count_ha, down_wide)
    return pl.pallas_call(
        ffn_kernel,
        grid=(hidden // chunk,),
        in_specs=[
            pl.BlockSpec(memory_space=pltpu.SMEM),
            whole((cells, dim)),
            whole((cells, dim)),
            whole((cells, LANES)),
            whole((1, dim)),
            whole((1, dim)),
            pl.BlockSpec((dim, chunk), lambda i: (0, i)),
            pl.BlockSpec((chunk, dim), lambda i: (i, 0)),
        ],
        out_specs=[whole((cells, dim)), whole((cells, dim)), up, up, down, down, whole((1, dim)), whole((1, dim))],
        out_shape=[
            shape_of(cells, dim),
            shape_of(cells, dim),
            up_shape,
            up_shape,
            down_shape,
            down_shape,
            shape_of(1, dim),
            shape_of(1, dim),
        ],
        scratch_shapes=pair
        + pair_turned
        + pair
        + pair_turned
        + [pltpu.VMEM((cells, dim), F32), pltpu.VMEM((cells, dim), F32)],
        compiler_params=params(),
        cost_estimate=lasting(30),
    )(core, middle, cot, keep, gain, scale, weight_up, weight_down)


def head_grad_kernel(
    core_ref, canvas_ref, valid_ref, gain_ref, dmiddle_ref, djoined_ref, weight_ref,
    dcanvas_ref, kept_ref, sent_ref, dgain_ref, nt_high, nt_low, dnorm,
):
    step = pl.program_id(0)

    @pl.when(step == 0)
    def _():
        hat, _ = normalized(canvas_ref[...] * valid_ref[:, :1])
        nt_high[...], nt_low[...] = halves((hat * gain_ref[...]).T)
        dnorm[...] = jnp.zeros_like(dnorm)

    grad = halves(djoined_ref[...])
    share_columns(core_ref[0], dot_pairs((nt_high[...], nt_low[...]), grad), kept_ref, sent_ref)
    dnorm[...] += dot_pairs(grad, halves(weight_ref[...]), NT)

    @pl.when(step == pl.num_programs(0) - 1)
    def _():
        hat, scale = normalized(canvas_ref[...] * valid_ref[:, :1])
        dgain = jnp.sum(dnorm[...] * hat, axis=0, keepdims=True)
        dgain_ref[...] = jnp.zeros_like(dgain_ref)
        for k in range(dgain.shape[1] // LANES):
            dgain_ref[k : k + 1] = dgain[:, k * LANES : (k + 1) * LANES]
        inner = dmiddle_ref[...] + norm_backward(dnorm[...] * gain_ref[...], hat, scale)
        dcanvas_ref[...] = inner * valid_ref[:, :1]


def head_backward(core, canvas, valid, gain, dmiddle, djoined, weight, count_ha, count_ba, chunk=256):
    cells, dim = canvas.shape
    width = weight.shape[1]
    own = width // count_ha
    chunks = shape_of(count_ha // 2, count_ba, dim // count_ba, own)
    chunk_spec = pl.BlockSpec((chunk // (2 * own), count_ba, dim // count_ba, own), lambda i: (i, 0, 0, 0))
    return pl.pallas_call(
        head_grad_kernel,
        grid=(width // chunk,),
        in_specs=[
            pl.BlockSpec(memory_space=pltpu.SMEM),
            whole((cells, dim)),
            whole((cells, LANES)),
            whole((1, dim)),
            whole((cells, dim)),
            pl.BlockSpec((cells, chunk), lambda i: (0, i)),
            pl.BlockSpec((dim, chunk), lambda i: (0, i)),
        ],
        out_specs=[whole((cells, dim)), chunk_spec, chunk_spec, whole((16, LANES))],
        out_shape=[shape_of(cells, dim), chunks, chunks, shape_of(16, LANES)],
        scratch_shapes=[
            pltpu.VMEM((dim, cells), BF16),
            pltpu.VMEM((dim, cells), BF16),
            pltpu.VMEM((cells, dim), F32),
        ],
        compiler_params=params(),
        cost_estimate=lasting(9),
    )(core, canvas, valid, gain, dmiddle, djoined, weight)


def exchange(values, axis, bit):
    return lax.ppermute(values, axis, [(i, i ^ bit) for i in range(lax.axis_size(axis))])


def picked(parts, index, axis):
    return [lax.dynamic_index_in_dim(part, index, axis, keepdims=False) for part in parts]


def total(parts):
    result = parts[0]
    for part in parts[1:]:
        result = result + part
    return result


def reduce_chunks(parts, order):
    bits = len(order)
    z = lax.axis_index("ha") // 2
    ba = lax.axis_index("ba")
    parts = [part.reshape(part.shape[:1] + (2,) * bits + part.shape[2:]) for part in parts]
    left = list(reversed(range(bits)))
    for bit in order:
        axis = 1 + left.index(bit)
        left.remove(bit)
        mine = (ba >> bit) & 1
        got = exchange(total(picked(parts, 1 - mine, axis)), "ba", 1 << bit)
        parts = picked(parts, mine, axis) + [got]
    got = [
        exchange(total(picked(parts, z ^ step, 0)), "ha", 2 * step) for step in range(1, lax.axis_size("ha") // 2)
    ]
    return total(picked(parts, z, 0) + got)


def reduce_whole(rows):
    half = rows.shape[0] // 2
    core = lax.axis_index("ha") % 2
    halves_of = rows.reshape(2, half, rows.shape[1])
    mine = total(picked([halves_of], core, 0) + [exchange(picked([halves_of], 1 - core, 0)[0], "ha", 1)])
    for axis, first in (("ba", 1), ("ha", 2)):
        bit = first
        while bit < lax.axis_size(axis):
            mine = mine + exchange(mine, axis, bit)
            bit *= 2
    other = exchange(mine, "ha", 1)
    low = jnp.where(core == 0, mine, other)
    high = jnp.where(core == 0, other, mine)
    return jnp.concatenate([low, high], axis=0)


def from_blocks(rows, tall):
    return jnp.concatenate([rows[i : i + tall] for i in range(0, rows.shape[0], tall)], axis=1)


def neighbour_rows(rows, width, dim):
    count = lax.axis_size("ha")
    up = [(i, i + 1) for i in range(count - 1)]
    down = [(i + 1, i) for i in range(count - 1)]
    tail = lax.slice_in_dim(rows, rows.shape[dim] - width, rows.shape[dim], axis=dim)
    head = lax.slice_in_dim(rows, 0, width, axis=dim)
    return lax.ppermute(tail, "ha", up), lax.ppermute(head, "ha", down)


def shards(
    canvas,
    image_id,
    keep_first,
    keep_second,
    first_gain,
    weight_in,
    depth_kernel,
    gate_first,
    gate_second,
    gate_third,
    weight_out,
    scale_first,
    second_gain,
    weight_up,
    weight_down,
    scale_second,
    cotangent,
):
    _, rows, cols, dim = canvas.shape
    cells = rows * cols
    taps = KERN * KERN
    reach = REACH * cols
    split = weight_in.shape[1] - depth_kernel.shape[1]
    count_ha, count_ba = lax.axis_size("ha"), lax.axis_size("ba")
    core = (lax.axis_index("ha") % 2)[None]
    first_row = (lax.axis_index("ha") * rows)[None]
    own = canvas.reshape(cells, dim)
    above, below = neighbour_rows(own, reach, 0)
    valid_ext, keep_one, keep_two, row_mask, col_mask = masks(first_row, keep_first, keep_second, image_id[0], rows)
    valid_ext = valid_ext.reshape(-1, LANES)
    valid = valid_ext[reach : reach + cells]
    keep_one = keep_one.reshape(cells, LANES)
    keep_two = keep_two.reshape(cells, LANES)
    middle_tap = (jnp.arange(taps) == taps // 2).astype(F32) / SPREAD
    kern = jnp.concatenate([jnp.broadcast_to(middle_tap[:, None], (taps, split)), depth_kernel], axis=1)
    gates = (gate_first, gate_second, gate_third)
    widths = (split,) + tuple(gate.shape[1] for gate in gates)

    joined = head_forward(own, valid, first_gain[None], weight_in)
    joined_above = head_forward(above, valid_ext[:reach], first_gain[None], weight_in)
    joined_below = head_forward(below, valid_ext[reach + cells :], first_gain[None], weight_in)
    conv = conv_forward(row_mask, joined_above, joined, joined_below, kern, col_mask, rows, cols)
    middle, mixed, mapped = gates_forward(conv, own, valid, keep_one, scale_first[None], gates, weight_out)
    output, dmiddle, up_kept, up_sent, down_kept, down_sent, dgain_two, dscale_two = ffn(
        core, middle, cotangent.reshape(cells, dim), keep_two, second_gain[None], scale_second[None],
        weight_up, weight_down, count_ha, count_ba,
    )
    order = list(range(count_ba.bit_length() - 1))
    turned = order[len(order) // 2 :] + order[: len(order) // 2]
    dup = reduce_chunks([up_kept, exchange(up_sent, "ha", 1)], order)
    ddown = reduce_chunks([down_kept, exchange(down_sent, "ha", 1)], turned)
    dconv, dmapped = gates_backward(dmiddle, conv, mapped, keep_one, scale_first[None], gates, weight_out)
    above, below = neighbour_rows(dconv, reach, 1)
    out_kept, out_sent, packed = gates_weights(
        core, dmiddle, keep_one, scale_first[None], weight_out, mixed, dmapped, dgain_two, dscale_two,
        widths, count_ha, count_ba,
    )
    dout = reduce_chunks([out_kept, exchange(out_sent, "ha", 1)], order)
    packed = reduce_whole(packed)
    djoined, dkern = conv_backward(row_mask, above, dconv, below, joined, kern, col_mask, rows, cols)
    dkern = reduce_whole(dkern.reshape(-1, LANES)).reshape(dkern.shape)
    dcanvas, in_kept, in_sent, dgain_one = head_backward(
        core, own, valid, first_gain[None], dmiddle, djoined, weight_in, count_ha, count_ba
    )
    in_parts = [in_kept, exchange(in_sent, "ha", 1)]
    middle_row = in_kept.shape[2] // 2
    din = jnp.concatenate(
        [
            reduce_chunks([part[:, :, :middle_row] for part in in_parts], order),
            reduce_chunks([part[:, :, middle_row:] for part in in_parts], turned),
        ],
        axis=0,
    )
    dgain_one = reduce_whole(dgain_one)

    small = []
    row = 0
    for tall, width in zip(widths[:-1], widths[1:]):
        size = tall * width // LANES
        small.append(from_blocks(packed[row : row + size], tall))
        row += size
    for _ in range(3):
        small.append(packed[row : row + dim // LANES].reshape(dim))
        row += dim // LANES
    dkern = jnp.concatenate([dkern[k, :taps] for k in range(dkern.shape[0])], axis=1)[:, split:]
    return (
        output.reshape(canvas.shape),
        dcanvas.reshape(canvas.shape),
        dgain_one[: dim // LANES].reshape(dim),
        din,
        dkern,
        small[0],
        small[1],
        small[2],
        dout.T,
        small[3],
        small[4],
        dup,
        ddown.T,
        small[5],
    )


def solution(mesh):
    in_specs = (
        P("ba", "ha", None, None),
        P("ba", None, None),
        P("ba", None),
        P("ba", None),
    ) + (P(),) * 12 + (P("ba", "ha", None, None),)
    tiled = P("ba", "ha")
    out_specs = (
        P("ba", "ha", None, None),
        P("ba", "ha", None, None),
        P(),
        tiled,
        P(),
        P(),
        P(),
        P(),
        tiled,
        P(),
        P(),
        tiled,
        tiled,
        P(),
    )
    return jax.shard_map(shards, mesh=mesh, in_specs=in_specs, out_specs=out_specs, check_vma=False)
```

time: 504 us -> 292 us (0.58)
  other arithmetic: 156 us -> 8.32 us
  Pallas kernels: 0 us -> 116 us
  matrix products: 102 us -> 0 us
  waiting for transfers between devices: 152 us -> 78.3 us
  starting transfers between devices: 18.6 us -> 71.8 us
  blocking collectives: 38.8 us -> 0 us
  between operations: 17.9 us -> 1.12 us
    reduce_scatter x8 -> x0, waiting for transfers between devices: 121 us -> none  [the longest x1 49.2 us: shards(): lax.psum_scatter(grads[11], 'ha', scatter_dimension=1, tiled=True)]
    pallas_call x0 -> x11, Pallas kernels: none -> 116 us  [the longest x1 28.1 us: ffn(): pl.pallas_call(ffn_kernel, grid=(hidden // chunk,), in_specs=[pl.BlockSpe...]
    dot_general x21 -> x0, matrix products: 102 us -> none  [matmul(): jnp.dot(left, right, precision=lax.Precision.HIGHEST, preferred_element_t...]
    ppermute x4 -> x51, waiting for transfers between devices: 3.42 us -> 78.3 us  [the longest x47 78.3 us: exchange(): lax.ppermute(values, axis, [(i, i ^ bit) for i in range(lax.axis_size(axi...]
    mul x21 -> x0, other arithmetic: 67.5 us -> none  [the longest x15 40.9 us: masked_depthwise(): kernel[tap_row * KERN + tap_col] * window]
    ppermute x4 -> x51, starting transfers between devices: 17.8 us -> 71.8 us  [the longest x47 60.6 us: exchange(): lax.ppermute(values, axis, [(i, i ^ bit) for i in range(lax.axis_size(axi...]
    reduce_sum x12 -> x0, other arithmetic: 41.5 us -> none  [the longest x6 36.3 us: masked_depthwise(): kernel[tap_row * KERN + tap_col] * window]
    psum x1 -> x0, blocking collectives: 38.8 us -> none  [shards(): lax.psum((grad_gain_one, grads[3], grads[4], grads[5], grads[6], grads[8]...]
  transfers between devices with their start and end apart: 13 -> 51, of which waited for: 7 -> 15; matrix products, arithmetic and copies ran while one was open for 30% -> 6% of each run, Pallas kernels for 0% -> 18%
where the time goes in v1:
time: 292 us; the launch traced here: 291 us
  Pallas kernels  116 us (40%)
  waiting for transfers between devices  78.3 us (27%)
  starting transfers between devices  71.8 us (25%)
  local copies, waits for them, and re-layouts  15.8 us (5%)
  other arithmetic  8.32 us (3%)
    ppermute x47, waiting for transfers between devices, exchange(): lax.ppermute(values, axis, [(i, i ^ bit) for i in range(lax.axis_size(axi...  78.3 us
    ppermute x47, starting transfers between devices, exchange(): lax.ppermute(values, axis, [(i, i ^ bit) for i in range(lax.axis_size(axi...  60.6 us
    pallas_call x1, Pallas kernels, ffn(): pl.pallas_call(ffn_kernel, grid=(hidden // chunk,), in_specs=[pl.BlockSpe...  28.1 us
    pallas_call x1, Pallas kernels, conv_backward(): pl.pallas_call(functools.partial(conv_grad_kernel, rows=rows, cols=cols),...  24.9 us
    pallas_call x1, Pallas kernels, conv_forward(): pl.pallas_call(functools.partial(conv_kernel, rows=rows, cols=cols), grid...  16.6 us
    pallas_call x3, Pallas kernels, head_forward(): pl.pallas_call(head_kernel, grid=(blocks // 2,), in_specs=[whole((cells,...  15 us
    ppermute x4, starting transfers between devices, neighbour_rows(): return (lax.ppermute(tail, 'ha', up), lax.ppermute(head, 'ha', down))  11.2 us
    pallas_call x1, Pallas kernels, head_backward(): pl.pallas_call(head_grad_kernel, grid=(width // chunk,), in_specs=[pl.Blo...  9.25 us
  transfers between devices with their start and end apart: 51, of which 15 were waited for; matrix products, arithmetic and copies ran while one was open for 6% of the time, Pallas kernels for 18%

profile of v1, /device:TPU:0, one launch (start us, length us, event | category | flops | bytes accessed | tf_op | source)
XLA Modules:
  0.0 291.1 jit_solution(6589510908945378797)
XLA Ops:
  1.8 2.4 collective-permute-start
  8.3 2.3 shard_map.272
  10.6 1.7 slice.128
  12.2 1.6 fusion.35
  14.8 5.8 %shard_map.274.own_ref.mix_ref = f32[8,512,128]{2,1,0:T(8,128)} custom-call(f32[512,512]{1,0:T(8,128)} %bitcast.358, f32[512,128]{1,0:T(8,128)} %bitcast.371, f32[1,512]{1,0:T(1,128)} %bitcast.387, f32[512,1024]{1,0:T(8,128)} %weight_ref.7), custom_call_target="tpu_custom_call" | custom-call | flops 4400000000 | tf_op jit(solution)/shard_map/pallas_call | solution.py:151
  21.3 4.6 %shard_map.273.above_ref = f32[8,192,128]{2,1,0:T(8,128)} custom-call(f32[192,512]{1,0:T(8,128)} %copy-done.10, f32[192,128]{1,0:T(8,128)} %bitcast.377, f32[1,512]{1,0:T(1,128)} %bitcast.388, f32[512,1024]{1,0:T(8,128)} %weight_ref.7), custom_call_target="tpu_custom_call" | custom-call | flops 4400000000 | tf_op jit(solution)/shard_map/pallas_call | solution.py:151
  26.6 4.6 %shard_map.275.below_ref = f32[8,192,128]{2,1,0:T(8,128)} custom-call(f32[192,512]{1,0:T(8,128)} %copy-done.9, f32[192,128]{1,0:T(8,128)} %bitcast.376, f32[1,512]{1,0:T(1,128)} %bitcast.389, f32[512,1024]{1,0:T(8,128)} %weight_ref.7), custom_call_target="tpu_custom_call" | custom-call | flops 4400000000 | tf_op jit(solution)/shard_map/pallas_call | solution.py:151
  31.2 16.6 %shard_map.276.conv_ref = f32[512,1024]{1,0:T(8,128)} custom-call(f32[8,128]{1,0:T(8,128)} %get-tuple-element.41.row_mask, f32[8,192,128]{2,1,0:T(8,128)} %shard_map.273.above_ref, f32[8,512,128]{2,1,0:T(8,128)} %shard_map.274.own_ref.mix_ref, f32[8,192,128]{2,1,0:T(8,128)} %shard_map.275.below_ref, f32[49,1024]{1,0:T(8,128)} %pad_maximum_fusion.1.kern_ref, ...), custom_call_target="tpu_custom_call" | custom-call | flops 17600000000 | tf_op jit(solution)/shard_map/pallas_call | solution.py:244
  47.8 6.6 %shard_map.277 = (f32[512,512]{1,0:T(8,128)}, f32[512,1024]{1,0:T(8,128)}, f32[512,896]{1,0:T(8,128)}) custom-call(f32[512,1024]{1,0:T(8,128)} %shard_map.276.conv_ref, f32[512,512]{1,0:T(8,128)} %bitcast.359, f32[512,128]{1,0:T(8,128)} %bitcast.372, f32[512,128]{1,0:T(8,128)} %bitcast.393, f32[1,512]{1,0:T(1,128)} %bitcast.384, f32[64,128]{1,0:T(8,128)} %one_ref.3, ...), custom_call_target="tpu_custom_call" | custom-call | flops 6600000000 | tf_op jit(solution)/shard_map/pallas_call | solution.py:342
  54.4 28.1 %shard_map.278 = (f32[512,512]{1,0:T(8,128)}, f32[512,512]{1,0:T(8,128)}, f32[4,4,128,256]{3,2,1,0:T(8,128)}, f32[4,4,128,256]{3,2,1,0:T(8,128)}, f32[4,4,64,512...) custom-call(s32[1]{0:T(128)} %bitcast.core_ref, ...), custom_call_target="tpu_custom_call" | custom-call | flops 32999999488 | tf_op jit(solution)/shard_map/pallas_call | solution.py:542
  82.4 7.2 %shard_map.279 = (f32[8,512,128]{2,1,0:T(8,128)}, f32[512,896]{1,0:T(8,128)}) custom-call(f32[512,512]{1,0:T(8,128)} %get-tuple-element.48.grad_ref.dmiddle_ref, f32[512,1024]{1,0:T(8,128)} %shard_map.276.conv_ref, f32[512,896]{1,0:T(8,128)} %get-tuple-element.49.mapped_ref, f32[512,128]{1,0:T(8,128)} %bitcast.394, f32[1,512]{1,0:T(1,128)} %bitcast.385, ...), custom_call_target="tpu_custom_call" | custom-call | flops 5500000256 | tf_op jit(solution)/shard_map/pallas_call | solution.py:384
  91.2 6.1 %collective-permute-start.2 = (f32[8,192,128]{2,1,0:T(8,128)S(1)}, f32[8,192,128]{2,1,0:T(8,128)}, u32[]{:S(2)}, u32[]{:S(2)}) collective-permute-start(f32[8,192,128]{2,1,0:T(8,128)S(1)} %get-tuple-element.75), channel_id=1, source_target_pairs={{0,4},{4,8},{8,12},{12,16},{16,20},{20,24},{24,28},{1,5},{5,9},{9,... | collective-permute-start | bytes 2359304 | tf_op jit(solution)/shard_map/ppermute | solution.py:692
  98.7 5.9 %shard_map.282 = (f32[4,4,64,128]{3,2,1,0:T(8,128)}, f32[4,4,64,128]{3,2,1,0:T(8,128)}, f32[1360,128]{1,0:T(8,128)}) custom-call(s32[1]{0:T(128)} %bitcast.core_ref, f32[512,512]{1,0:T(8,128)} %get-tuple-element.48.grad_ref.dmiddle_ref, f32[512,128]{1,0:T(8,128)} %bitcast.395, f32[1,512]{1,0:T(1,128)} %bitcast.386, f32[512,512]{1,0:T(8,128)} %out_ref.5, ...), custom_call_target="tpu_custom_call" | custom-call | flops 5500000256 | tf_op jit(solution)/shard_map/pallas_call | solution.py:459
  105.6 1.6 collective-permute-start.27
  109.5 1.6 collective-permute-start.28
  111.1 24.9 %shard_map.280 = (f32[512,1024]{1,0:T(8,128)}, f32[8,56,128]{2,1,0:T(8,128)}) custom-call(f32[8,128]{1,0:T(8,128)} %get-tuple-element.41.row_mask, f32[8,192,128]{2,1,0:T(8,128)} %collective-permute-done.2.above_ref, f32[8,512,128]{2,1,0:T(8,128)} %get-tuple-element.50.own_ref, f32[8,192,128]{2,1,0:T(8,128)} %collective-permute-done.3.below_ref, ...), custom_call_target="tpu_custom_call" | custom-call | flops 26400000000 | tf_op jit(solution)/shard_map/pallas_call | solution.py:293
  136.0 9.2 %shard_map.281 = (f32[512,512]{1,0:T(8,128)}, f32[4,4,128,128]{3,2,1,0:T(8,128)}, f32[4,4,128,128]{3,2,1,0:T(8,128)}, f32[16,128]{1,0:T(8,128)}) custom-call(s32[1]{0:T(128)} %bitcast.core_ref, f32[512,512]{1,0:T(8,128)} %bitcast.360, f32[512,128]{1,0:T(8,128)} %bitcast.373, f32[1,512]{1,0:T(1,128)} %bitcast.390, ...), custom_call_target="tpu_custom_call" | custom-call | flops 9900000256 | tf_op jit(solution)/shard_map/pallas_call | solution.py:609
  146.5 1.6 collective-permute-start.34
  149.5 5.5 %collective-permute-done.5 = f32[8,128]{1,0:T(8,128)S(1)} collective-permute-done((f32[8,128]{1,0:T(8,128)S(1)}, f32[8,128]{1,0:T(8,128)S(1)}, u32[]{:S(2)}, u32[]{:S(2)}) %collective-permute-start.5) | collective-permute-done | bytes 4128 | tf_op jit(solution)/shard_map/ppermute | solution.py:634
  158.6 2.0 collective-permute-start.7
  162.2 3.0 %collective-permute-start.8 = (f32[8,128]{1,0:T(8,128)S(1)}, f32[8,128]{1,0:T(8,128)S(1)}, u32[]{:S(2)}, u32[]{:S(2)}) collective-permute-start(f32[8,128]{1,0:T(8,128)S(1)} %add.973), channel_id=1, source_target_pairs={{0,16},{4,20},{8,24},{12,28},{16,0},{20,4},{24,8},{28,12},{1,17},{... | collective-permute-start | bytes 12296 | tf_op jit(solution)/shard_map/ppermute | solution.py:634
  165.2 1.6 collective-permute-start.35
  168.3 4.2 %collective-permute-done.22 = f32[224,128]{1,0:T(8,128)S(1)} collective-permute-done((f32[224,128]{1,0:T(8,128)S(1)}, f32[224,128]{1,0:T(8,128)S(1)}, u32[]{:S(2)}, u32[]{:S(2)}) %collective-permute-start.22) | collective-permute-done | bytes 114720 | tf_op jit(solution)/shard_map/ppermute | solution.py:634
  172.5 1.6 collective-permute-start.23
  174.1 3.3 %collective-permute-done.23 = f32[224,128]{1,0:T(8,128)S(1)} collective-permute-done((f32[224,128]{1,0:T(8,128)S(1)}, f32[224,128]{1,0:T(8,128)S(1)}, u32[]{:S(2)}, u32[]{:S(2)}) %collective-permute-start.23) | collective-permute-done | bytes 114720 | tf_op jit(solution)/shard_map/ppermute | solution.py:634
  177.4 1.9 collective-permute-start.24
  179.6 2.9 collective-permute-start.37
  184.1 2.9 collective-permute-start.25
  187.6 5.7 %collective-permute-done.25 = f32[224,128]{1,0:T(8,128)S(1)} collective-permute-done((f32[224,128]{1,0:T(8,128)S(1)}, f32[224,128]{1,0:T(8,128)S(1)}, u32[]{:S(2)}, u32[]{:S(2)}) %collective-permute-start.25) | collective-permute-done | bytes 114720 | tf_op jit(solution)/shard_map/ppermute | solution.py:634
  195.1 3.4 %collective-permute-start.31 = (f32[680,128]{1,0:T(8,128)S(1)}, f32[680,128]{1,0:T(8,128)S(1)}, u32[]{:S(2)}, u32[]{:S(2)}) collective-permute-start(f32[680,128]{1,0:T(8,128)S(1)} %add.1039), channel_id=1, source_target_pairs={{0,16},{4,20},{8,24},{12,28},{16,0},{20,4},{24,8},{28,12},{1,17},{... | collective-permute-start | bytes 1044488 | tf_op jit(solution)/shard_map/ppermute | solution.py:634
  198.5 3.6 %collective-permute-done.26 = f32[224,128]{1,0:T(8,128)S(1)} collective-permute-done((f32[224,128]{1,0:T(8,128)S(1)}, f32[224,128]{1,0:T(8,128)S(1)}, u32[]{:S(2)}, u32[]{:S(2)}) %collective-permute-start.26) | collective-permute-done | bytes 114720 | tf_op jit(solution)/shard_map/ppermute | solution.py:634
  203.0 11.3 %collective-permute-done.31 = f32[680,128]{1,0:T(8,128)S(1)} collective-permute-done((f32[680,128]{1,0:T(8,128)S(1)}, f32[680,128]{1,0:T(8,128)S(1)}, u32[]{:S(2)}, u32[]{:S(2)}) %collective-permute-start.31) | collective-permute-done | bytes 348192 | tf_op jit(solution)/shard_map/ppermute | solution.py:634
  215.8 1.7 collective-permute-start.16
  221.7 2.1 collective-permute-done.11
  223.9 1.6 collective-permute-start.12
  228.0 21.6 %collective-permute-done.12 = f32[4,64,128]{2,1,0:T(8,128)S(1)} collective-permute-done((f32[4,64,128]{2,1,0:T(8,128)S(1)}, f32[4,64,128]{2,1,0:T(8,128)S(1)}, u32[]{:S(2)}, u32[]{:S(2)}) %collective-permute-start.12) | collective-permute-done | bytes 131104 | tf_op jit(solution)/shard_map/ppermute | solution.py:634
  249.7 2.7 collective-permute-start.14
  252.4 1.7 collective-permute-start.15
  255.5 2.8 collective-permute-start.19
  258.4 1.6 collective-permute-start.20
  261.6 2.5 collective-permute-done.20
  264.1 2.7 collective-permute-done.47
  267.0 1.8 collective-permute-start.48
  269.7 1.7 collective-permute-start.50
  273.1 1.9 collective-permute-start.43
  274.9 3.1 %collective-permute-start.44 = (f32[128,256]{1,0:T(8,128)S(1)}, f32[128,256]{1,0:T(8,128)S(1)}, u32[]{:S(2)}, u32[]{:S(2)}) collective-permute-start(f32[128,256]{1,0:T(8,128)S(1)} %get-tuple-element.72), channel_id=1, source_target_pairs={{0,24},{4,28},{8,16},{12,20},{16,8},{20,12},{24,0},{28,4},{1,25},{... | collective-permute-start | bytes 393224 | tf_op jit(solution)/shard_map/ppermute | solution.py:634
  278.1 3.6 %collective-permute-done.49 = f32[64,512]{1,0:T(8,128)S(1)} collective-permute-done((f32[64,512]{1,0:T(8,128)S(1)}, f32[64,512]{1,0:T(8,128)S(1)}, u32[]{:S(2)}, u32[]{:S(2)}) %collective-permute-start.49) | collective-permute-done | bytes 131104 | tf_op jit(solution)/shard_map/ppermute | solution.py:634
  282.4 7.9 %collective-permute-done.43 = f32[128,256]{1,0:T(8,128)S(1)} collective-permute-done((f32[128,256]{1,0:T(8,128)S(1)}, f32[128,256]{1,0:T(8,128)S(1)}, u32[]{:S(2)}, u32[]{:S(2)}) %collective-permute-start.43) | collective-permute-done | bytes 131104 | tf_op jit(solution)/shard_map/ppermute | solution.py:634
  (159 shorter events, 44.0 us)
Async XLA Ops:
  1.8 18.7 %collective-permute-start = (f32[192,512]{1,0:T(8,128)S(1)}, f32[192,512]{1,0:T(8,128)S(1)}, u32[]{:S(2)}, u32[]{:S(2)}) collective-permute-start(f32[192,512]{1,0:T(8,128)S(1)} %bitcast.370), channel_id=1, source_target_pairs={{0,4},{4,8},{8,12},{12,16},{16,20},{20,24},{24,28},{1,5},{5,9},{9,... | collective-permute-start | bytes 1179656 | tf_op jit(solution)/shard_map/ppermute | solution.py:692
  4.2 21.7 %collective-permute-start.1 = (f32[192,512]{1,0:T(8,128)S(1)}, f32[192,512]{1,0:T(8,128)S(1)}, u32[]{:S(2)}, u32[]{:S(2)}) collective-permute-start(f32[192,512]{1,0:T(8,128)S(1)} %bitcast.369), channel_id=1, source_target_pairs={{4,0},{8,4},{12,8},{16,12},{20,16},{24,20},{28,24},{5,1},{9,5},{13... | collective-permute-start | bytes 1179656 | tf_op jit(solution)/shard_map/ppermute | solution.py:692
  91.2 19.9 %collective-permute-start.2 = (f32[8,192,128]{2,1,0:T(8,128)S(1)}, f32[8,192,128]{2,1,0:T(8,128)}, u32[]{:S(2)}, u32[]{:S(2)}) collective-permute-start(f32[8,192,128]{2,1,0:T(8,128)S(1)} %get-tuple-element.75), channel_id=1, source_target_pairs={{0,4},{4,8},{8,12},{12,16},{16,20},{20,24},{24,28},{1,5},{5,9},{9,... | collective-permute-start | bytes 2359304 | tf_op jit(solution)/shard_map/ppermute | solution.py:692
  97.3 13.8 %collective-permute-start.3 = (f32[8,192,128]{2,1,0:T(8,128)S(1)}, f32[8,192,128]{2,1,0:T(8,128)}, u32[]{:S(2)}, u32[]{:S(2)}) collective-permute-start(f32[8,192,128]{2,1,0:T(8,128)S(1)} %get-tuple-element.74), channel_id=1, source_target_pairs={{4,0},{8,4},{12,8},{16,12},{20,16},{24,20},{28,24},{5,1},{9,5},{13... | collective-permute-start | bytes 2359304 | tf_op jit(solution)/shard_map/ppermute | solution.py:692
  107.2 39.3 %collective-permute-start.33 = (f32[4,4,64,128]{3,2,1,0:T(8,128)}, f32[4,4,64,128]{3,2,1,0:T(8,128)S(1)}, u32[]{:S(2)}, u32[]{:S(2)}) collective-permute-start(f32[4,4,64,128]{3,2,1,0:T(8,128)} %get-tuple-element.63), channel_id=1, source_target_pairs={{0,4},{4,0},{8,12},{12,8},{16,20},{20,16},{24,28},{28,24},{1,5},{5... | collective-permute-start | bytes 1572872 | tf_op jit(solution)/shard_map/ppermute | solution.py:634
  109.5 47.0 %collective-permute-start.28 = (f32[680,128]{1,0:T(8,128)S(1)}, f32[680,128]{1,0:T(8,128)S(1)}, u32[]{:S(2)}, u32[]{:S(2)}) collective-permute-start(f32[680,128]{1,0:T(8,128)S(1)} %bitcast_add_fusion.2), channel_id=1, source_target_pairs={{0,1},{1,0},{2,3},{3,2},{4,5},{5,4},{6,7},{7,6},{8,9},{9,8},{10,11... | collective-permute-start | bytes 1044488 | tf_op jit(solution)/shard_map/ppermute | solution.py:634
  146.5 18.7 %collective-permute-start.34 = (f32[4,2,64,128]{3,2,1,0:T(8,128)S(1)}, f32[4,2,64,128]{3,2,1,0:T(8,128)S(1)}, u32[]{:S(2)}, u32[]{:S(2)}) collective-permute-start(f32[4,2,64,128]{3,2,1,0:T(8,128)S(1)} %add_bitcast_fusion.2), channel_id=1, source_target_pairs={{0,1},{1,0},{2,3},{3,2},{4,5},{5,4},{6,7},{7,6},{8,9},{9,8},{10,11... | collective-permute-start | bytes 786440 | tf_op jit(solution)/shard_map/ppermute | solution.py:634
  148.8 6.2 %collective-permute-start.5 = (f32[8,128]{1,0:T(8,128)S(1)}, f32[8,128]{1,0:T(8,128)S(1)}, u32[]{:S(2)}, u32[]{:S(2)}) collective-permute-start(f32[8,128]{1,0:T(8,128)S(1)} %fusion.29), channel_id=1, source_target_pairs={{0,1},{1,0},{2,3},{3,2},{4,5},{5,4},{6,7},{7,6},{8,9},{9,8},{10,11... | collective-permute-start | bytes 12296 | tf_op jit(solution)/shard_map/ppermute | solution.py:634
  155.0 3.6 %collective-permute-start.6 = (f32[8,128]{1,0:T(8,128)S(1)}, f32[8,128]{1,0:T(8,128)S(1)}, u32[]{:S(2)}, u32[]{:S(2)}) collective-permute-start(f32[8,128]{1,0:T(8,128)S(1)} %add.971), channel_id=1, source_target_pairs={{0,2},{1,3},{2,0},{3,1},{4,6},{5,7},{6,4},{7,5},{8,10},{9,11},{10,... | collective-permute-start | bytes 12296 | tf_op jit(solution)/shard_map/ppermute | solution.py:634
  156.5 27.2 %collective-permute-start.29 = (f32[680,128]{1,0:T(8,128)S(1)}, f32[680,128]{1,0:T(8,128)S(1)}, u32[]{:S(2)}, u32[]{:S(2)}) collective-permute-start(f32[680,128]{1,0:T(8,128)S(1)} %add.1037), channel_id=1, source_target_pairs={{0,2},{1,3},{2,0},{3,1},{4,6},{5,7},{6,4},{7,5},{8,10},{9,11},{10,... | collective-permute-start | bytes 1044488 | tf_op jit(solution)/shard_map/ppermute | solution.py:634
  158.6 3.6 %collective-permute-start.7 = (f32[8,128]{1,0:T(8,128)S(1)}, f32[8,128]{1,0:T(8,128)S(1)}, u32[]{:S(2)}, u32[]{:S(2)}) collective-permute-start(f32[8,128]{1,0:T(8,128)S(1)} %add.972), channel_id=1, source_target_pairs={{0,8},{4,12},{8,0},{12,4},{16,24},{20,28},{24,16},{28,20},{1,9},{5... | collective-permute-start | bytes 12296 | tf_op jit(solution)/shard_map/ppermute | solution.py:634
  160.6 6.3 %collective-permute-start.21 = (f32[224,128]{1,0:T(8,128)S(1)}, f32[224,128]{1,0:T(8,128)S(1)}, u32[]{:S(2)}, u32[]{:S(2)}) collective-permute-start(f32[224,128]{1,0:T(8,128)S(1)} %dynamic-slice_bitcast_fusion.1), channel_id=1, source_target_pairs={{0,4},{4,0},{8,12},{12,8},{16,20},{20,16},{24,28},{28,24},{1,5},{5... | collective-permute-start | bytes 344072 | tf_op jit(solution)/shard_map/ppermute | solution.py:634
  162.2 4.6 %collective-permute-start.8 = (f32[8,128]{1,0:T(8,128)S(1)}, f32[8,128]{1,0:T(8,128)S(1)}, u32[]{:S(2)}, u32[]{:S(2)}) collective-permute-start(f32[8,128]{1,0:T(8,128)S(1)} %add.973), channel_id=1, source_target_pairs={{0,16},{4,20},{8,24},{12,28},{16,0},{20,4},{24,8},{28,12},{1,17},{... | collective-permute-start | bytes 12296 | tf_op jit(solution)/shard_map/ppermute | solution.py:634
  165.2 14.1 %collective-permute-start.35 = (f32[4,64,128]{2,1,0:T(8,128)S(1)}, f32[4,64,128]{2,1,0:T(8,128)S(1)}, u32[]{:S(2)}, u32[]{:S(2)}) collective-permute-start(f32[4,64,128]{2,1,0:T(8,128)S(1)} %bitcast_add_fusion.19), channel_id=1, source_target_pairs={{0,2},{1,3},{2,0},{3,1},{4,6},{5,7},{6,4},{7,5},{8,10},{9,11},{10,... | collective-permute-start | bytes 393224 | tf_op jit(solution)/shard_map/ppermute | solution.py:634
  166.8 7.2 %collective-permute-start.9 = (f32[8,128]{1,0:T(8,128)S(1)}, f32[8,128]{1,0:T(8,128)S(1)}, u32[]{:S(2)}, u32[]{:S(2)}) collective-permute-start(f32[8,128]{1,0:T(8,128)S(1)} %add.974), channel_id=1, source_target_pairs={{0,4},{4,0},{8,12},{12,8},{16,20},{20,16},{24,28},{28,24},{1,5},{5... | collective-permute-start | bytes 12296 | tf_op jit(solution)/shard_map/ppermute | solution.py:634
  166.9 5.6 %collective-permute-start.22 = (f32[224,128]{1,0:T(8,128)S(1)}, f32[224,128]{1,0:T(8,128)S(1)}, u32[]{:S(2)}, u32[]{:S(2)}) collective-permute-start(f32[224,128]{1,0:T(8,128)S(1)} %bitcast_add_fusion.22), channel_id=1, source_target_pairs={{0,1},{1,0},{2,3},{3,2},{4,5},{5,4},{6,7},{7,6},{8,9},{9,8},{10,11... | collective-permute-start | bytes 344072 | tf_op jit(solution)/shard_map/ppermute | solution.py:634
  172.5 4.9 %collective-permute-start.23 = (f32[224,128]{1,0:T(8,128)S(1)}, f32[224,128]{1,0:T(8,128)S(1)}, u32[]{:S(2)}, u32[]{:S(2)}) collective-permute-start(f32[224,128]{1,0:T(8,128)S(1)} %add.1032), channel_id=1, source_target_pairs={{0,2},{1,3},{2,0},{3,1},{4,6},{5,7},{6,4},{7,5},{8,10},{9,11},{10,... | collective-permute-start | bytes 344072 | tf_op jit(solution)/shard_map/ppermute | solution.py:634
  177.4 6.7 %collective-permute-start.24 = (f32[224,128]{1,0:T(8,128)S(1)}, f32[224,128]{1,0:T(8,128)S(1)}, u32[]{:S(2)}, u32[]{:S(2)}) collective-permute-start(f32[224,128]{1,0:T(8,128)S(1)} %add.1033), channel_id=1, source_target_pairs={{0,8},{4,12},{8,0},{12,4},{16,24},{20,28},{24,16},{28,20},{1,9},{5... | collective-permute-start | bytes 344072 | tf_op jit(solution)/shard_map/ppermute | solution.py:634
  179.3 14.0 %collective-permute-start.36 = (f32[64,128]{1,0:T(8,128)S(1)}, f32[64,128]{1,0:T(8,128)S(1)}, u32[]{:S(2)}, u32[]{:S(2)}) collective-permute-start(f32[64,128]{1,0:T(8,128)S(1)} %get-tuple-element.76), channel_id=1, source_target_pairs={{0,8},{4,12},{8,0},{12,4},{16,24},{20,28},{24,16},{28,20},{1,9},{5... | collective-permute-start | bytes 98312 | tf_op jit(solution)/shard_map/ppermute | solution.py:634
  179.6 14.3 %collective-permute-start.37 = (f32[64,128]{1,0:T(8,128)S(1)}, f32[64,128]{1,0:T(8,128)S(1)}, u32[]{:S(2)}, u32[]{:S(2)}) collective-permute-start(f32[64,128]{1,0:T(8,128)S(1)} %get-tuple-element.78), channel_id=1, source_target_pairs={{0,16},{4,20},{8,24},{12,28},{16,0},{20,4},{24,8},{28,12},{1,17},{... | collective-permute-start | bytes 98312 | tf_op jit(solution)/shard_map/ppermute | solution.py:634
  182.4 11.6 %collective-permute-start.38 = (f32[64,128]{1,0:T(8,128)S(1)}, f32[64,128]{1,0:T(8,128)S(1)}, u32[]{:S(2)}, u32[]{:S(2)}) collective-permute-start(f32[64,128]{1,0:T(8,128)S(1)} %get-tuple-element.77), channel_id=1, source_target_pairs={{0,24},{4,28},{8,16},{12,20},{16,8},{20,12},{24,0},{28,4},{1,25},{... | collective-permute-start | bytes 98312 | tf_op jit(solution)/shard_map/ppermute | solution.py:634
  183.8 11.2 %collective-permute-start.30 = (f32[680,128]{1,0:T(8,128)S(1)}, f32[680,128]{1,0:T(8,128)S(1)}, u32[]{:S(2)}, u32[]{:S(2)}) collective-permute-start(f32[680,128]{1,0:T(8,128)S(1)} %add.1038), channel_id=1, source_target_pairs={{0,8},{4,12},{8,0},{12,4},{16,24},{20,28},{24,16},{28,20},{1,9},{5... | collective-permute-start | bytes 1044488 | tf_op jit(solution)/shard_map/ppermute | solution.py:634
  184.1 9.1 %collective-permute-start.25 = (f32[224,128]{1,0:T(8,128)S(1)}, f32[224,128]{1,0:T(8,128)S(1)}, u32[]{:S(2)}, u32[]{:S(2)}) collective-permute-start(f32[224,128]{1,0:T(8,128)S(1)} %add.1034), channel_id=1, source_target_pairs={{0,16},{4,20},{8,24},{12,28},{16,0},{20,4},{24,8},{28,12},{1,17},{... | collective-permute-start | bytes 344072 | tf_op jit(solution)/shard_map/ppermute | solution.py:634
  193.3 24.4 %collective-permute-start.45 = (f32[4,4,64,512]{3,2,1,0:T(8,128)S(1)}, f32[4,4,64,512]{3,2,1,0:T(8,128)S(1)}, u32[]{:S(2)}, u32[]{:S(2)}) collective-permute-start(f32[4,4,64,512]{3,2,1,0:T(8,128)S(1)} %copy-done.7), channel_id=1, source_target_pairs={{0,4},{4,0},{8,12},{12,8},{16,20},{20,16},{24,28},{28,24},{1,5},{5... | collective-permute-start | bytes 6291464 | tf_op jit(solution)/shard_map/ppermute | solution.py:634
  193.3 25.0 %collective-permute-start.39 = (f32[4,4,128,256]{3,2,1,0:T(8,128)S(1)}, f32[4,4,128,256]{3,2,1,0:T(8,128)S(1)}, u32[]{:S(2)}, u32[]{:S(2)}) collective-permute-start(f32[4,4,128,256]{3,2,1,0:T(8,128)S(1)} %copy-done.6), channel_id=1, source_target_pairs={{0,4},{4,0},{8,12},{12,8},{16,20},{20,16},{24,28},{28,24},{1,5},{5... | collective-permute-start | bytes 6291464 | tf_op jit(solution)/shard_map/ppermute | solution.py:634
  193.9 20.6 %collective-permute-start.10 = (f32[4,4,128,128]{3,2,1,0:T(8,128)S(1)}, f32[4,4,128,128]{3,2,1,0:T(8,128)S(1)}, u32[]{:S(2)}, u32[]{:S(2)}) collective-permute-start(f32[4,4,128,128]{3,2,1,0:T(8,128)S(1)} %copy-done.8), channel_id=1, source_target_pairs={{0,4},{4,0},{8,12},{12,8},{16,20},{20,16},{24,28},{28,24},{1,5},{5... | collective-permute-start | bytes 3145736 | tf_op jit(solution)/shard_map/ppermute | solution.py:634
  194.0 8.1 %collective-permute-start.26 = (f32[224,128]{1,0:T(8,128)S(1)}, f32[224,128]{1,0:T(8,128)S(1)}, u32[]{:S(2)}, u32[]{:S(2)}) collective-permute-start(f32[224,128]{1,0:T(8,128)S(1)} %add.1035), channel_id=1, source_target_pairs={{0,4},{4,0},{8,12},{12,8},{16,20},{20,16},{24,28},{28,24},{1,5},{5... | collective-permute-start | bytes 344072 | tf_op jit(solution)/shard_map/ppermute | solution.py:634
  195.1 19.3 %collective-permute-start.31 = (f32[680,128]{1,0:T(8,128)S(1)}, f32[680,128]{1,0:T(8,128)S(1)}, u32[]{:S(2)}, u32[]{:S(2)}) collective-permute-start(f32[680,128]{1,0:T(8,128)S(1)} %add.1039), channel_id=1, source_target_pairs={{0,16},{4,20},{8,24},{12,28},{16,0},{20,4},{24,8},{28,12},{1,17},{... | collective-permute-start | bytes 1044488 | tf_op jit(solution)/shard_map/ppermute | solution.py:634
  214.7 9.2 %collective-permute-start.11 = (f32[4,2,64,128]{3,2,1,0:T(8,128)S(1)}, f32[4,2,64,128]{3,2,1,0:T(8,128)S(1)}, u32[]{:S(2)}, u32[]{:S(2)}) collective-permute-start(f32[4,2,64,128]{3,2,1,0:T(8,128)S(1)} %add_bitcast_fusion.4), channel_id=1, source_target_pairs={{0,1},{1,0},{2,3},{3,2},{4,5},{5,4},{6,7},{7,6},{8,9},{9,8},{10,11... | collective-permute-start | bytes 786440 | tf_op jit(solution)/shard_map/ppermute | solution.py:634
  215.8 9.7 %collective-permute-start.16 = (f32[4,2,64,128]{3,2,1,0:T(8,128)S(1)}, f32[4,2,64,128]{3,2,1,0:T(8,128)S(1)}, u32[]{:S(2)}, u32[]{:S(2)}) collective-permute-start(f32[4,2,64,128]{3,2,1,0:T(8,128)S(1)} %add_bitcast_fusion.3), channel_id=1, source_target_pairs={{0,2},{1,3},{2,0},{3,1},{4,6},{5,7},{6,4},{7,5},{8,10},{9,11},{10,... | collective-permute-start | bytes 786440 | tf_op jit(solution)/shard_map/ppermute | solution.py:634
  217.9 36.2 %collective-permute-start.46 = (f32[4,2,64,512]{3,2,1,0:T(8,128)S(1)}, f32[4,2,64,512]{3,2,1,0:T(8,128)S(1)}, u32[]{:S(2)}, u32[]{:S(2)}) collective-permute-start(f32[4,2,64,512]{3,2,1,0:T(8,128)S(1)} %add_bitcast_fusion), channel_id=1, source_target_pairs={{0,2},{1,3},{2,0},{3,1},{4,6},{5,7},{6,4},{7,5},{8,10},{9,11},{10,... | collective-permute-start | bytes 3145736 | tf_op jit(solution)/shard_map/ppermute | solution.py:634
  219.3 35.1 %collective-permute-start.40 = (f32[4,2,128,256]{3,2,1,0:T(8,128)S(1)}, f32[4,2,128,256]{3,2,1,0:T(8,128)S(1)}, u32[]{:S(2)}, u32[]{:S(2)}) collective-permute-start(f32[4,2,128,256]{3,2,1,0:T(8,128)S(1)} %add_bitcast_fusion.1), channel_id=1, source_target_pairs={{0,1},{1,0},{2,3},{3,2},{4,5},{5,4},{6,7},{7,6},{8,9},{9,8},{10,11... | collective-permute-start | bytes 3145736 | tf_op jit(solution)/shard_map/ppermute | solution.py:634
  223.9 25.7 %collective-permute-start.12 = (f32[4,64,128]{2,1,0:T(8,128)S(1)}, f32[4,64,128]{2,1,0:T(8,128)S(1)}, u32[]{:S(2)}, u32[]{:S(2)}) collective-permute-start(f32[4,64,128]{2,1,0:T(8,128)S(1)} %bitcast_add_fusion.21), channel_id=1, source_target_pairs={{0,2},{1,3},{2,0},{3,1},{4,6},{5,7},{6,4},{7,5},{8,10},{9,11},{10,... | collective-permute-start | bytes 393224 | tf_op jit(solution)/shard_map/ppermute | solution.py:634
  225.5 26.8 %collective-permute-start.17 = (f32[4,64,128]{2,1,0:T(8,128)S(1)}, f32[4,64,128]{2,1,0:T(8,128)S(1)}, u32[]{:S(2)}, u32[]{:S(2)}) collective-permute-start(f32[4,64,128]{2,1,0:T(8,128)S(1)} %bitcast_add_fusion.20), channel_id=1, source_target_pairs={{0,1},{1,0},{2,3},{3,2},{4,5},{5,4},{6,7},{7,6},{8,9},{9,8},{10,11... | collective-permute-start | bytes 393224 | tf_op jit(solution)/shard_map/ppermute | solution.py:634
  249.6 5.9 %collective-permute-start.13 = (f32[64,128]{1,0:T(8,128)S(1)}, f32[64,128]{1,0:T(8,128)S(1)}, u32[]{:S(2)}, u32[]{:S(2)}) collective-permute-start(f32[64,128]{1,0:T(8,128)S(1)} %get-tuple-element.79), channel_id=1, source_target_pairs={{0,8},{4,12},{8,0},{12,4},{16,24},{20,28},{24,16},{28,20},{1,9},{5... | collective-permute-start | bytes 98312 | tf_op jit(solution)/shard_map/ppermute | solution.py:634
  249.7 8.7 %collective-permute-start.14 = (f32[64,128]{1,0:T(8,128)S(1)}, f32[64,128]{1,0:T(8,128)S(1)}, u32[]{:S(2)}, u32[]{:S(2)}) collective-permute-start(f32[64,128]{1,0:T(8,128)S(1)} %get-tuple-element.81), channel_id=1, source_target_pairs={{0,16},{4,20},{8,24},{12,28},{16,0},{20,4},{24,8},{28,12},{1,17},{... | collective-permute-start | bytes 98312 | tf_op jit(solution)/shard_map/ppermute | solution.py:634
  252.4 7.6 %collective-permute-start.15 = (f32[64,128]{1,0:T(8,128)S(1)}, f32[64,128]{1,0:T(8,128)S(1)}, u32[]{:S(2)}, u32[]{:S(2)}) collective-permute-start(f32[64,128]{1,0:T(8,128)S(1)} %get-tuple-element.80), channel_id=1, source_target_pairs={{0,24},{4,28},{8,16},{12,20},{16,8},{20,12},{24,0},{28,4},{1,25},{... | collective-permute-start | bytes 98312 | tf_op jit(solution)/shard_map/ppermute | solution.py:634
  254.1 7.4 %collective-permute-start.18 = (f32[64,128]{1,0:T(8,128)S(1)}, f32[64,128]{1,0:T(8,128)S(1)}, u32[]{:S(2)}, u32[]{:S(2)}) collective-permute-start(f32[64,128]{1,0:T(8,128)S(1)} %get-tuple-element.82), channel_id=1, source_target_pairs={{0,8},{4,12},{8,0},{12,4},{16,24},{20,28},{24,16},{28,20},{1,9},{5... | collective-permute-start | bytes 98312 | tf_op jit(solution)/shard_map/ppermute | solution.py:634
  254.4 12.4 %collective-permute-start.47 = (f32[4,64,512]{2,1,0:T(8,128)S(1)}, f32[4,64,512]{2,1,0:T(8,128)S(1)}, u32[]{:S(2)}, u32[]{:S(2)}) collective-permute-start(f32[4,64,512]{2,1,0:T(8,128)S(1)} %bitcast_add_fusion), channel_id=1, source_target_pairs={{0,1},{1,0},{2,3},{3,2},{4,5},{5,4},{6,7},{7,6},{8,9},{9,8},{10,11... | collective-permute-start | bytes 1572872 | tf_op jit(solution)/shard_map/ppermute | solution.py:634
  255.5 6.0 %collective-permute-start.19 = (f32[64,128]{1,0:T(8,128)S(1)}, f32[64,128]{1,0:T(8,128)S(1)}, u32[]{:S(2)}, u32[]{:S(2)}) collective-permute-start(f32[64,128]{1,0:T(8,128)S(1)} %get-tuple-element.84), channel_id=1, source_target_pairs={{0,16},{4,20},{8,24},{12,28},{16,0},{20,4},{24,8},{28,12},{1,17},{... | collective-permute-start | bytes 98312 | tf_op jit(solution)/shard_map/ppermute | solution.py:634
  258.4 5.7 %collective-permute-start.20 = (f32[64,128]{1,0:T(8,128)S(1)}, f32[64,128]{1,0:T(8,128)S(1)}, u32[]{:S(2)}, u32[]{:S(2)}) collective-permute-start(f32[64,128]{1,0:T(8,128)S(1)} %get-tuple-element.83), channel_id=1, source_target_pairs={{0,24},{4,28},{8,16},{12,20},{16,8},{20,12},{24,0},{28,4},{1,25},{... | collective-permute-start | bytes 98312 | tf_op jit(solution)/shard_map/ppermute | solution.py:634
  260.0 12.1 %collective-permute-start.41 = (f32[4,128,256]{2,1,0:T(8,128)S(1)}, f32[4,128,256]{2,1,0:T(8,128)S(1)}, u32[]{:S(2)}, u32[]{:S(2)}) collective-permute-start(f32[4,128,256]{2,1,0:T(8,128)S(1)} %bitcast_add_fusion.1), channel_id=1, source_target_pairs={{0,2},{1,3},{2,0},{3,1},{4,6},{5,7},{6,4},{7,5},{8,10},{9,11},{10,... | collective-permute-start | bytes 1572872 | tf_op jit(solution)/shard_map/ppermute | solution.py:634
  267.0 8.0 %collective-permute-start.48 = (f32[64,512]{1,0:T(8,128)S(1)}, f32[64,512]{1,0:T(8,128)S(1)}, u32[]{:S(2)}, u32[]{:S(2)}) collective-permute-start(f32[64,512]{1,0:T(8,128)S(1)} %get-tuple-element.68), channel_id=1, source_target_pairs={{0,8},{4,12},{8,0},{12,4},{16,24},{20,28},{24,16},{28,20},{1,9},{5... | collective-permute-start | bytes 393224 | tf_op jit(solution)/shard_map/ppermute | solution.py:634
  268.7 13.0 %collective-permute-start.49 = (f32[64,512]{1,0:T(8,128)S(1)}, f32[64,512]{1,0:T(8,128)S(1)}, u32[]{:S(2)}, u32[]{:S(2)}) collective-permute-start(f32[64,512]{1,0:T(8,128)S(1)} %get-tuple-element.70), channel_id=1, source_target_pairs={{0,16},{4,20},{8,24},{12,28},{16,0},{20,4},{24,8},{28,12},{1,17},{... | collective-permute-start | bytes 393224 | tf_op jit(solution)/shard_map/ppermute | solution.py:634
  269.7 12.0 %collective-permute-start.50 = (f32[64,512]{1,0:T(8,128)S(1)}, f32[64,512]{1,0:T(8,128)S(1)}, u32[]{:S(2)}, u32[]{:S(2)}) collective-permute-start(f32[64,512]{1,0:T(8,128)S(1)} %get-tuple-element.69), channel_id=1, source_target_pairs={{0,24},{4,28},{8,16},{12,20},{16,8},{20,12},{24,0},{28,4},{1,25},{... | collective-permute-start | bytes 393224 | tf_op jit(solution)/shard_map/ppermute | solution.py:634
  272.2 10.3 %collective-permute-start.42 = (f32[128,256]{1,0:T(8,128)S(1)}, f32[128,256]{1,0:T(8,128)S(1)}, u32[]{:S(2)}, u32[]{:S(2)}) collective-permute-start(f32[128,256]{1,0:T(8,128)S(1)} %get-tuple-element.71), channel_id=1, source_target_pairs={{0,8},{4,12},{8,0},{12,4},{16,24},{20,28},{24,16},{28,20},{1,9},{5... | collective-permute-start | bytes 393224 | tf_op jit(solution)/shard_map/ppermute | solution.py:634
  273.1 17.3 %collective-permute-start.43 = (f32[128,256]{1,0:T(8,128)S(1)}, f32[128,256]{1,0:T(8,128)S(1)}, u32[]{:S(2)}, u32[]{:S(2)}) collective-permute-start(f32[128,256]{1,0:T(8,128)S(1)} %get-tuple-element.73), channel_id=1, source_target_pairs={{0,16},{4,20},{8,24},{12,28},{16,0},{20,4},{24,8},{28,12},{1,17},{... | collective-permute-start | bytes 393224 | tf_op jit(solution)/shard_map/ppermute | solution.py:634
  274.9 15.4 %collective-permute-start.44 = (f32[128,256]{1,0:T(8,128)S(1)}, f32[128,256]{1,0:T(8,128)S(1)}, u32[]{:S(2)}, u32[]{:S(2)}) collective-permute-start(f32[128,256]{1,0:T(8,128)S(1)} %get-tuple-element.72), channel_id=1, source_target_pairs={{0,24},{4,28},{8,16},{12,20},{16,8},{20,12},{24,0},{28,4},{1,25},{... | collective-permute-start | bytes 393224 | tf_op jit(solution)/shard_map/ppermute | solution.py:634
  (14 other events, 156.4 us)

commit v2 on v0

v2 whole, which is shorter than its diff:
```python
import functools

import jax
import jax.numpy as jnp
from jax import lax
from jax.experimental import pallas as pl
from jax.experimental.pallas import tpu as pltpu
from jax.sharding import PartitionSpec as P

KERN = 7
TAPS = KERN * KERN
REACH = KERN // 2
KEEP_RATE = 0.8
SPREAD = 1.0 / 3.0
EPSILON = 1e-06
LANES = 128
EDGE = 8
F32 = jnp.float32
INV_SQRT_2 = 0.7071067811865476
INV_SQRT_2PI = 0.3989422804014327
NN = (((1,), (0,)), ((), ()))
NT = (((1,), (1,)), ((), ()))
TN = (((0,), (0,)), ((), ()))


def dot(left, right, dims=NN):
    return lax.dot_general(left, right, dims, precision=lax.Precision.HIGH, preferred_element_type=F32)


def normalized(values):
    centered = values - jnp.mean(values, axis=-1, keepdims=True)
    scale = lax.rsqrt(jnp.mean(centered * centered, axis=-1, keepdims=True) + EPSILON)
    return centered * scale, scale


def norm_backward(grad_hat, hat, scale):
    return scale * (
        grad_hat
        - jnp.mean(grad_hat, axis=-1, keepdims=True)
        - hat * jnp.mean(grad_hat * hat, axis=-1, keepdims=True)
    )


def params(mebibytes):
    return pltpu.CompilerParams(vmem_limit_bytes=mebibytes << 20)


def lasting(microseconds):
    return pl.CostEstimate(flops=int(microseconds * 1.1e9), bytes_accessed=0, transcendentals=0)


def whole(shape):
    return pl.BlockSpec(tuple(shape), lambda *_: (0,) * len(shape), pipeline_mode=pl.Buffered(1))


def in_smem():
    return pl.BlockSpec(memory_space=pltpu.SMEM)


def anywhere():
    return pl.BlockSpec(memory_space=pl.ANY)


def shape_of(*shape):
    return jax.ShapeDtypeStruct(shape, F32)


def lane_blocks(width):
    return -(-width // LANES)


def masks_kernel(
    place_ref, keep_one, keep_two, ids_ref, valid_ref, one_ref, two_ref, row_ref, col_ref, padded, *, rows
):
    height, cols = ids_ref.shape
    slots = keep_one.shape[1]
    rows_ext = rows + 2 * REACH
    padded[...] = jnp.full(padded.shape, -1, jnp.int32)
    padded[EDGE : EDGE + height, :] = ids_ref[...]
    first = place_ref[0] * rows
    ids = padded[pl.ds(first + (EDGE - REACH), rows_ext), :]
    turned = jnp.concatenate([ids, jnp.full((-rows_ext % 8, cols), -1, jnp.int32)], axis=0).T
    own = turned[:, REACH : REACH + rows]
    one = jnp.zeros(own.shape, F32)
    two = jnp.zeros(own.shape, F32)
    for slot in range(slots):
        hit = own == slot
        one = jnp.where(hit, keep_one[0, slot].astype(F32) / KEEP_RATE, one)
        two = jnp.where(hit, keep_two[0, slot].astype(F32) / KEEP_RATE, two)
    valid = (turned >= 0).astype(F32)
    for r in range(rows_ext):
        valid_ref[r * cols : (r + 1) * cols, :] = jnp.broadcast_to(valid[:, r : r + 1], (cols, LANES))
    for r in range(rows):
        one_ref[r * cols : (r + 1) * cols, :] = jnp.broadcast_to(one[:, r : r + 1], (cols, LANES))
        two_ref[r * cols : (r + 1) * cols, :] = jnp.broadcast_to(two[:, r : r + 1], (cols, LANES))
    wide_ids = jnp.broadcast_to(ids_ref[...].T[:, height // 2 : height // 2 + 1], (cols, LANES))
    column = lax.broadcasted_iota(jnp.int32, (cols, LANES), 0)
    for b in range(KERN):
        shift = b - REACH
        moved = pltpu.roll(wide_ids, (-shift) % cols, 0)
        inside = (column + shift >= 0) & (column + shift < cols)
        same = (moved == wide_ids) & inside
        col_ref[b] = same.astype(F32).reshape(cols // 8, 8, LANES)
    across = ids[:, cols // 2 : cols // 2 + 1]
    place = first - REACH + lax.broadcasted_iota(jnp.int32, across.shape, 0)
    across = jnp.where((place >= 0) & (place < height), across, -2)
    lane = lax.broadcasted_iota(jnp.int32, (rows, LANES), 1)
    mask = jnp.zeros((rows, LANES), F32)
    for a in range(KERN):
        same = (across[a : a + rows] == across[REACH : REACH + rows]).astype(F32)
        mask = jnp.where(lane == a + 1, same, mask)
    row_ref[...] = mask


def masks(place, keep_one, keep_two, ids, rows):
    height, cols = ids.shape
    return pl.pallas_call(
        functools.partial(masks_kernel, rows=rows),
        in_specs=[in_smem(), in_smem(), in_smem(), pl.BlockSpec(memory_space=pltpu.VMEM)],
        out_shape=[
            shape_of((rows + 2 * REACH) * cols, LANES),
            shape_of(rows * cols, LANES),
            shape_of(rows * cols, LANES),
            shape_of(rows, LANES),
            shape_of(KERN, cols // 8, 8, LANES),
        ],
        scratch_shapes=[pltpu.VMEM((height + 2 * EDGE, cols), jnp.int32)],
        compiler_params=params(16),
        cost_estimate=lasting(3),
    )(place, keep_one, keep_two, ids)


def lay_kernel(kern_ref, laid, split):
    tap = lax.broadcasted_iota(jnp.int32, (TAPS, split), 0)
    own = jnp.where(tap == TAPS // 2, 1.0 / SPREAD, 0.0).astype(F32)
    for k in range(laid.shape[0]):
        start = k * LANES - split
        left = own if k == 0 else kern_ref[:, start : start + split]
        laid[k] = jnp.concatenate([left, kern_ref[:, start + split : start + LANES]], axis=1) * SPREAD


def fill_shifted(flat, col_ref, shifted, rows_ext, cols):
    groups = cols // 8
    for b in range(KERN):
        mask = col_ref[b]

        def some(h, _, b=b, mask=mask):
            for k in range(2):
                r = 2 * h + k
                start = pl.multiple_of(r * cols, cols) + (EDGE + b - REACH)
                x = flat[pl.ds(start, cols), :].reshape(groups, 8, LANES)
                shifted[b, r] = x if b == REACH else x * mask
            return 0

        lax.fori_loop(0, rows_ext // 2, some, 0)


def conv_block(row_mask, kern, shifted, wide, out_ref, rows, cols):
    groups = cols // 8
    for t in range(KERN):
        wide[t] = jnp.zeros((8, LANES), F32)
        wide[KERN * (KERN + 1) + t] = jnp.zeros((8, LANES), F32)
    for t in range(TAPS):
        wide[KERN + t] = jnp.broadcast_to(kern[t : t + 1, :], (8, LANES))

    def pair(h, _):
        r = 2 * h

        def step(i, totals):
            first, second = totals
            mask_first = row_mask[r, i + 1]
            mask_second = row_mask[r + 1, i]
            for b in range(KERN):
                x = shifted[b, r + i]
                first = first + (wide[(i + 1) * KERN + b] * mask_first)[None] * x
                second = second + (wide[i * KERN + b] * mask_second)[None] * x
            return first, second

        zero = jnp.zeros((groups, 8, LANES), F32)
        first, second = lax.fori_loop(0, KERN + 1, step, (zero, zero))
        out_ref[pl.ds(pl.multiple_of(r * cols, cols), cols), :] = first.reshape(cols, LANES)
        out_ref[pl.ds(pl.multiple_of((r + 1) * cols, cols), cols), :] = second.reshape(cols, LANES)
        return 0

    lax.fori_loop(0, rows // 2, pair, 0)


def conv_grad_block(row_mask, kern, shifted, wide, dk, mix_ref, out_ref, dk_ref, rows, cols):
    groups = cols // 8
    for t in range(TAPS):
        wide[t] = jnp.broadcast_to(kern[TAPS - 1 - t : TAPS - t, :], (8, LANES))
        dk[t] = jnp.zeros((8, LANES), F32)

    def one(r, _):
        start = pl.ds(pl.multiple_of(r * cols, cols), cols)
        mix = mix_ref[start, :].reshape(groups, 8, LANES)

        def step(i, total):
            mask = row_mask[r, i + 1]
            for b in range(KERN):
                x = shifted[b, r + i]
                total = total + (wide[i * KERN + b] * mask)[None] * x
                dk[i * KERN + b] += jnp.sum(mix * x, axis=0) * mask
            return total

        total = lax.fori_loop(0, KERN, step, jnp.zeros((groups, 8, LANES), F32))
        out_ref[start, :] = total.reshape(cols, LANES)
        return 0

    lax.fori_loop(0, rows, one, 0)
    for t in range(TAPS):
        dk_ref[TAPS - 1 - t : TAPS - t, :] = jnp.sum(dk[t], axis=0, keepdims=True) * SPREAD
    dk_ref[TAPS:, :] = jnp.zeros((dk_ref.shape[0] - TAPS, LANES), F32)


def share(core, first, second, kept_ref, sent_ref, z, p):
    mine = core == 0
    tall, width = first.shape
    for ref, chunk in (
        (kept_ref, jnp.where(mine, first, second)),
        (sent_ref, jnp.where(mine, second, first)),
    ):
        for k in range(lane_blocks(width)):
            part = chunk[:, k * LANES : (k + 1) * LANES]
            if part.shape[1] < LANES:
                part = jnp.concatenate([part, jnp.zeros((tall, LANES - part.shape[1]), F32)], axis=1)
            ref[z, p, k * tall : (k + 1) * tall, :] = part


def share_columns(core, grad, kept_ref, sent_ref, width):
    groups, parts = kept_ref.shape[:2]
    tall = grad.shape[0] // parts
    for z in range(groups):
        for p in range(parts):
            rows = slice(p * tall, (p + 1) * tall)
            first = grad[rows, 2 * z * width : (2 * z + 1) * width]
            second = grad[rows, (2 * z + 1) * width : (2 * z + 2) * width]
            share(core, first, second, kept_ref, sent_ref, z, p)


def share_rows(core, grad, kept_ref, sent_ref, tall):
    groups, parts = kept_ref.shape[:2]
    width = grad.shape[1] // parts
    for z in range(groups):
        for p in range(parts):
            columns = slice(p * width, (p + 1) * width)
            first = grad[2 * z * tall : (2 * z + 1) * tall, columns]
            second = grad[(2 * z + 1) * tall : (2 * z + 2) * tall, columns]
            share(core, first, second, kept_ref, sent_ref, z, p)


def forward_kernel(
    place_ref, row_mask, above_ref, own_ref, below_ref, valid_ref, one_keep_ref, two_keep_ref, cot_ref,
    first_gain_ref, first_scale_ref, second_gain_ref, second_scale_ref,
    in_ref, kern_ref, col_ref, one_ref, two_ref, three_ref, out_ref, up_ref, down_ref,
    joined_ref, output_ref, dmiddle_ref, dconv_ref,
    up_kept_ref, up_sent_ref, down_kept_ref, down_sent_ref, out_kept_ref, out_sent_ref, packed_ref,
    normed, flat, shifted, laid, wide, conv, mixed_ref, mapped_ref, middle_ref, result, dnorm,
    *, rows, cols, count_ha, count_ba,
):
    step = pl.program_id(0)
    blocks = flat.shape[0]
    cells = rows * cols
    reach = REACH * cols
    cells_ext = cells + 2 * reach
    core = place_ref[0] % 2
    split = one_ref.shape[0]
    dim = own_ref.shape[1]
    head_steps = blocks // 2
    ffn_first = head_steps + blocks
    gate_refs = (one_ref, two_ref, three_ref)

    @pl.when(step == 0)
    def _():
        lay_kernel(kern_ref, laid, split)
        start = 0
        for ref in (above_ref, own_ref, below_ref):
            size = ref.shape[0]
            hat, _ = normalized(ref[...] * valid_ref[start : start + size, :1])
            normed[start : start + size] = hat * first_gain_ref[...]
            start += size

    @pl.when(step < head_steps)
    def _():
        joined = dot(normed[...], in_ref[...])
        for k in range(2):
            part = joined[:, k * LANES : (k + 1) * LANES]
            block = 2 * step + k
            flat[block, :EDGE] = jnp.zeros((EDGE, LANES), F32)
            flat[block, EDGE : EDGE + cells_ext] = part
            flat[block, EDGE + cells_ext :] = jnp.zeros((EDGE, LANES), F32)
            joined_ref[k] = part[reach : reach + cells]

    @pl.when((step >= head_steps) & (step < ffn_first))
    def _():
        block = step - head_steps
        fill_shifted(flat.at[block], col_ref, shifted, rows + 2 * REACH, cols)
        conv_block(row_mask, laid[block], shifted, wide, conv.at[block], rows, cols)

    def conv_part(start, width):
        return jnp.concatenate([conv[start // LANES + k] for k in range(width // LANES)], axis=1)

    @pl.when(step == ffn_first)
    def _():
        mixed = conv[0, :, :split] * conv[0, :, split:]
        mixed_ref[:, :split] = mixed
        start = 2 * split
        for ref in gate_refs:
            width = ref.shape[1]
            mapped = dot(mixed, ref[...])
            mapped_ref[:, start - 2 * split : start - 2 * split + width] = mapped
            mixed = mapped * conv_part(start, width)
            mixed_ref[:, start : start + width] = mixed
            start += width
        branch = dot(mixed, out_ref[...])
        masked = own_ref[...] * valid_ref[reach : reach + cells, :1]
        middle = masked + one_keep_ref[:, :1] * first_scale_ref[...] * branch
        middle_ref[...] = middle
        hat, _ = normalized(middle)
        normed[:cells] = hat * second_gain_ref[...]
        normed[cells : cells + reach] = jnp.zeros((reach, dim), F32)
        result[...] = jnp.zeros_like(result)
        dnorm[...] = jnp.zeros_like(dnorm)

    @pl.when(step >= ffn_first)
    def _():
        grad_result = two_keep_ref[:, :1] * second_scale_ref[...] * cot_ref[...]
        pre = dot(normed[:cells], up_ref[...])
        cdf = 0.5 + 0.5 * lax.erf(pre * INV_SQRT_2)
        slope = cdf + pre * (INV_SQRT_2PI * jnp.exp(-0.5 * pre * pre))
        hidden = pre * cdf
        result[...] += dot(hidden, down_ref[...])
        grad_pre = dot(grad_result, down_ref[...], NT) * slope
        share_rows(core, dot(grad_result, hidden, TN), down_kept_ref, down_sent_ref, dim // count_ha)
        width = down_ref.shape[0] // (2 * up_kept_ref.shape[0])
        share_columns(core, dot(normed[:cells], grad_pre, TN), up_kept_ref, up_sent_ref, width)
        dnorm[...] += dot(grad_pre, up_ref[...], NT)

    @pl.when(step == pl.num_programs(0) - 1)
    def _():
        hat, scale = normalized(middle_ref[...])
        kept = two_keep_ref[:, :1] * result[...]
        output_ref[...] = middle_ref[...] + second_scale_ref[...] * kept
        dscale_two = jnp.sum(cot_ref[...] * kept, axis=0, keepdims=True)
        dgain_two = jnp.sum(dnorm[...] * hat, axis=0, keepdims=True)
        dmiddle = cot_ref[...] + norm_backward(dnorm[...] * second_gain_ref[...], hat, scale)
        dmiddle_ref[...] = dmiddle
        kept = one_keep_ref[:, :1] * dmiddle
        start = mixed_ref.shape[1] - out_ref.shape[0]
        crossed = dot(mixed_ref[:, start:], kept, TN)
        dscale_one = jnp.sum(crossed * out_ref[...], axis=0, keepdims=True)
        share_rows(core, (crossed * first_scale_ref[...]).T, out_kept_ref, out_sent_ref, dim // count_ha)
        grad = dot(kept * first_scale_ref[...], out_ref[...], NT)
        row = packed_ref.shape[0]
        start = blocks * LANES
        for ref in reversed(gate_refs):
            tall, width = ref.shape
            start -= width
            source = start - tall if tall > split else 0
            columns = slice(start - 2 * split, start - 2 * split + width)
            dconv = grad * mapped_ref[:, columns]
            for k in range(width // LANES):
                dconv_ref[start // LANES + k] = dconv[:, k * LANES : (k + 1) * LANES]
            grad_mapped = grad * conv_part(start, width)
            part = dot(mixed_ref[:, source : source + tall], grad_mapped, TN)
            row -= tall * width // LANES
            for k in range(width // LANES):
                packed_ref[row + k * tall : row + (k + 1) * tall] = part[:, k * LANES : (k + 1) * LANES]
            grad = dot(grad_mapped, ref[...], NT)
        dconv_ref[0] = jnp.concatenate([grad * conv[0, :, split:], grad * conv[0, :, :split]], axis=1)
        packed_ref[:row] = jnp.zeros((row, LANES), F32)
        row = 0
        for vector in (dscale_one, dgain_two, dscale_two):
            for k in range(dim // LANES):
                packed_ref[row : row + 1] = vector[:, k * LANES : (k + 1) * LANES]
                row += 1


def packed_rows(gates, dim):
    rows = sum(gate.size for gate in gates) // LANES + 3 * dim // LANES
    return -(-rows // 16) * 16


def forward(
    place, row_mask, above, own, below, valid, one_keep, two_keep, cot, vectors, weight_in, kern, col_mask, gates,
    weight_out, weight_up, weight_down, rows, cols, count_ha, count_ba, chunk=512,
):
    cells, dim = own.shape
    reach = above.shape[0]
    blocks = weight_in.shape[1] // LANES
    hidden = weight_up.shape[1]
    split = gates[0].shape[0]
    wide = blocks * LANES
    head_steps = blocks // 2
    ffn_first = head_steps + blocks
    ffn_steps = hidden // chunk

    def ffn_step(i):
        return jnp.clip(i - ffn_first, 0, ffn_steps - 1)

    up_wide, down_wide = hidden // count_ha, hidden // count_ba
    up_rows = dim // count_ba * lane_blocks(up_wide)
    down_rows = dim // count_ha * lane_blocks(down_wide)
    out_rows = dim // count_ha * lane_blocks(dim // count_ba)
    half = count_ha // 2
    up_spec = pl.BlockSpec((chunk // (2 * up_wide), count_ba, up_rows, LANES), lambda i: (ffn_step(i), 0, 0, 0))
    down_spec = pl.BlockSpec((half, chunk // down_wide, down_rows, LANES), lambda i: (0, ffn_step(i), 0, 0))
    out_shape = (half, count_ba, out_rows, LANES)
    packed_shape = (packed_rows(gates, dim), LANES)
    cells_ext = cells + 2 * reach
    return pl.pallas_call(
        functools.partial(forward_kernel, rows=rows, cols=cols, count_ha=count_ha, count_ba=count_ba),
        grid=(ffn_first + ffn_steps,),
        in_specs=[in_smem(), in_smem()]
        + [whole(x.shape) for x in (above, own, below, valid, one_keep, two_keep, cot)]
        + [whole((1, dim))] * 4
        + [
            pl.BlockSpec((dim, 2 * LANES), lambda i: (0, jnp.minimum(i, head_steps - 1))),
            whole(kern.shape),
            whole(col_mask.shape),
        ]
        + [whole(gate.shape) for gate in gates]
        + [
            whole(weight_out.shape),
            pl.BlockSpec((dim, chunk), lambda i: (0, ffn_step(i))),
            pl.BlockSpec((chunk, dim), lambda i: (ffn_step(i), 0)),
        ],
        out_specs=[
            pl.BlockSpec((2, cells, LANES), lambda i: (jnp.minimum(i, head_steps - 1), 0, 0)),
            whole((cells, dim)),
            whole((cells, dim)),
            whole((blocks, cells, LANES)),
            up_spec,
            up_spec,
            down_spec,
            down_spec,
            whole(out_shape),
            whole(out_shape),
            whole(packed_shape),
        ],
        out_shape=[
            shape_of(blocks, cells, LANES),
            shape_of(cells, dim),
            shape_of(cells, dim),
            shape_of(blocks, cells, LANES),
            shape_of(half, count_ba, up_rows, LANES),
            shape_of(half, count_ba, up_rows, LANES),
            shape_of(half, count_ba, down_rows, LANES),
            shape_of(half, count_ba, down_rows, LANES),
            shape_of(*out_shape),
            shape_of(*out_shape),
            shape_of(*packed_shape),
        ],
        scratch_shapes=[
            pltpu.VMEM((cells_ext, dim), F32),
            pltpu.VMEM((blocks, cells_ext + 2 * EDGE, LANES), F32),
            pltpu.VMEM((KERN, rows + 2 * REACH, cols // 8, 8, LANES), F32),
            pltpu.VMEM((blocks, TAPS, LANES), F32),
            pltpu.VMEM((KERN * (KERN + 2), 8, LANES), F32),
            pltpu.VMEM((blocks, cells, LANES), F32),
            pltpu.VMEM((cells, wide), F32),
            pltpu.VMEM((cells, wide - 2 * split), F32),
            pltpu.VMEM((cells, dim), F32),
            pltpu.VMEM((cells, dim), F32),
            pltpu.VMEM((cells, dim), F32),
        ],
        compiler_params=params(60),
        cost_estimate=lasting(70),
    )(
        place, row_mask, above, own, below, valid, one_keep, two_keep, cot, *vectors,
        weight_in, kern, col_mask, *gates, weight_out, weight_up, weight_down,
    )


def backward_kernel(
    place_ref, row_mask, above_ref, own_ref, below_ref, mix_ref, kern_ref, col_ref, canvas_ref, valid_ref, gain_ref,
    dmiddle_ref, before_ref, in_ref, *rest, rows, cols, first_block, last, count_ties,
):
    rest = rest[count_ties:]
    if last:
        dcanvas_ref, kept_ref, sent_ref, dk_ref, dgain_ref = rest[:5]
    else:
        dnorm_ref, kept_ref, sent_ref, dk_ref = rest[:4]
    flat, shifted, laid, wide, dk, djoined, normed, dnorm = rest[-8:]
    step = pl.program_id(0)
    block = first_block + step
    cells = rows * cols
    reach = REACH * cols
    core = place_ref[0] % 2
    split = laid.shape[0] * LANES - kern_ref.shape[1]
    width = in_ref.shape[1] // (2 * kept_ref.shape[0])

    @pl.when(step == 0)
    def _():
        lay_kernel(kern_ref, laid, split)
        hat, _ = normalized(canvas_ref[...] * valid_ref[reach : reach + cells, :1])
        normed[...] = hat * gain_ref[...]
        dnorm[...] = before_ref[...] if first_block else jnp.zeros_like(dnorm)

    flat[:EDGE] = jnp.zeros((EDGE, LANES), F32)
    flat[EDGE : EDGE + reach] = above_ref[0]
    flat[EDGE + reach : EDGE + reach + cells] = own_ref[0]
    flat[EDGE + reach + cells : EDGE + 2 * reach + cells] = below_ref[0]
    flat[EDGE + 2 * reach + cells :] = jnp.zeros((EDGE, LANES), F32)
    fill_shifted(flat, col_ref, shifted, rows + 2 * REACH, cols)
    conv_grad_block(
        row_mask, laid[block], shifted, wide, dk, mix_ref.at[0], djoined.at[step % 2], dk_ref.at[0], rows, cols
    )

    @pl.when(step % 2 == 1)
    def _():
        grad = jnp.concatenate([djoined[0], djoined[1]], axis=1)
        share_columns(core, dot(normed[...], grad, TN), kept_ref, sent_ref, width)
        dnorm[...] += dot(grad, in_ref[...], NT)

    @pl.when(step == pl.num_programs(0) - 1)
    def _():
        if last:
            hat, scale = normalized(canvas_ref[...] * valid_ref[reach : reach + cells, :1])
            dgain = jnp.sum(dnorm[...] * hat, axis=0, keepdims=True)
            dgain_ref[...] = jnp.zeros_like(dgain_ref)
            for k in range(dgain.shape[1] // LANES):
                dgain_ref[k : k + 1] = dgain[:, k * LANES : (k + 1) * LANES]
            inner = dmiddle_ref[...] + norm_backward(dnorm[...] * gain_ref[...], hat, scale)
            dcanvas_ref[...] = inner * valid_ref[reach : reach + cells, :1]
        else:
            dnorm_ref[...] = dnorm[...]


def backward(
    place, row_mask, above, own, below, mix, kern, col_mask, canvas, valid, gain, dmiddle, before, weight_in,
    first_block, end_block, ties, rows, cols, count_ha, count_ba,
):
    cells, dim = canvas.shape
    blocks = own.shape[0]
    reach = above.shape[1]
    last = end_block == blocks
    steps = end_block - first_block
    own_wide = weight_in.shape[1] // count_ha
    chunk_rows = dim // count_ba * lane_blocks(own_wide)
    groups = 2 * LANES // (2 * own_wide)
    tall = -(-TAPS // 8) * 8

    def block_of(size):
        return pl.BlockSpec((1, size, LANES), lambda i: (first_block + i, 0, 0))

    chunk_spec = pl.BlockSpec((groups, count_ba, chunk_rows, LANES), lambda i: (i // 2, 0, 0, 0))
    chunks = shape_of(groups * steps // 2, count_ba, chunk_rows, LANES)
    dk_spec = pl.BlockSpec((1, tall, LANES), lambda i: (i, 0, 0))
    dk_shape = shape_of(steps, tall, LANES)
    gain_shape = (-(-dim // LANES // 16) * 16, LANES)
    return pl.pallas_call(
        functools.partial(
            backward_kernel, rows=rows, cols=cols, first_block=first_block, last=last, count_ties=len(ties)
        ),
        grid=(steps,),
        in_specs=[in_smem(), in_smem(), block_of(reach), block_of(cells), block_of(reach), block_of(cells)]
        + [whole(x.shape) for x in (kern, col_mask, canvas, valid)]
        + [whole((1, dim)), whole((cells, dim)), whole((cells, dim))]
        + [pl.BlockSpec((dim, 2 * LANES), lambda i: (0, first_block // 2 + i // 2))]
        + [anywhere()] * len(ties),
        out_specs=[whole((cells, dim)), chunk_spec, chunk_spec, dk_spec] + [whole(gain_shape)] * last,
        out_shape=[shape_of(cells, dim), chunks, chunks, dk_shape] + [shape_of(*gain_shape)] * last,
        scratch_shapes=[
            pltpu.VMEM((cells + 2 * reach + 2 * EDGE, LANES), F32),
            pltpu.VMEM((KERN, rows + 2 * REACH, cols // 8, 8, LANES), F32),
            pltpu.VMEM((blocks, TAPS, LANES), F32),
            pltpu.VMEM((TAPS, 8, LANES), F32),
            pltpu.VMEM((TAPS, 8, LANES), F32),
            pltpu.VMEM((2, cells, LANES), F32),
            pltpu.VMEM((cells, dim), F32),
            pltpu.VMEM((cells, dim), F32),
        ],
        compiler_params=params(32),
        cost_estimate=lasting(4 * steps),
    )(
        place, row_mask, above, own, below, mix, kern, col_mask, canvas, valid, gain, dmiddle, before, weight_in, *ties
    )


def unpack_kernel(packed_ref, dkern_ref, dgain_ref, *outs, dim):
    row = 0
    for ref in outs[:3]:
        for k in range(dim // LANES):
            ref[:, k * LANES : (k + 1) * LANES] = packed_ref[row : row + 1]
            row += 1
    row = packed_ref.shape[0]
    for ref in reversed(outs[3:6]):
        tall, width = ref.shape
        row -= tall * width // LANES
        for k in range(width // LANES):
            ref[:, k * LANES : (k + 1) * LANES] = packed_ref[row + k * tall : row + (k + 1) * tall]
    dk_ref, gain_ref = outs[6:]
    joined = jnp.concatenate([dkern_ref[k, :TAPS] for k in range(dkern_ref.shape[0])], axis=1)
    dk_ref[...] = joined[:, joined.shape[1] - dk_ref.shape[1] :]
    for k in range(dim // LANES):
        gain_ref[:, k * LANES : (k + 1) * LANES] = dgain_ref[k : k + 1]


def unpack(packed, dkern, dgain, gates, kern, dim):
    return pl.pallas_call(
        functools.partial(unpack_kernel, dim=dim),
        out_shape=[shape_of(1, dim)] * 3
        + [shape_of(*gate.shape) for gate in gates]
        + [shape_of(*kern.shape), shape_of(1, dim)],
        compiler_params=params(16),
        cost_estimate=lasting(2),
    )(packed, dkern, dgain)


def exchange(values, axis, bit):
    return lax.ppermute(values, axis, [(i, i ^ bit) for i in range(lax.axis_size(axis))])


def picked(parts, index, axis):
    return [lax.dynamic_index_in_dim(part, index, axis, keepdims=False) for part in parts]


def total(parts):
    result = parts[0]
    for part in parts[1:]:
        result = result + part
    return result


class Chunks:
    def __init__(self, parts, order):
        bits = len(order)
        self.parts = [part.reshape(part.shape[:1] + (2,) * bits + part.shape[2:]) for part in parts]
        self.order = list(order)
        self.left = list(reversed(range(bits)))

    def outgoing(self):
        bit = self.order[0]
        self.axis = 1 + self.left.index(bit)
        self.mine = (lax.axis_index("ba") >> bit) & 1
        self.leaving = total(picked(self.parts, 1 - self.mine, self.axis))
        return self.leaving

    def halve(self):
        bit = self.order.pop(0)
        self.left.remove(bit)
        got = exchange(self.leaving, "ba", 1 << bit)
        self.parts = picked(self.parts, self.mine, self.axis) + [got]

    def halve_rest(self):
        while self.order:
            self.outgoing()
            self.halve()


def finish(sums):
    z = lax.axis_index("ha") // 2
    stages = range(1, lax.axis_size("ha") // 2)
    got = []
    for step in stages:
        leaving = [total(picked(one.parts, z ^ step, 0)) for one in sums]
        got.append(exchange(jnp.concatenate(leaving, axis=0), "ha", 2 * step))
    results = []
    row = 0
    for one in sums:
        rows = one.parts[0].shape[1]
        results.append(total(picked(one.parts, z, 0) + [part[row : row + rows] for part in got]))
        row += rows
    return results


def reduce_whole(rows):
    half = rows.shape[0] // 2
    core = lax.axis_index("ha") % 2
    halves_of = rows.reshape(2, half, rows.shape[1])
    mine = total(picked([halves_of], core, 0) + [exchange(picked([halves_of], 1 - core, 0)[0], "ha", 1)])
    for axis, first in (("ba", 1), ("ha", 2)):
        bit = first
        while bit < lax.axis_size(axis):
            mine = mine + exchange(mine, axis, bit)
            bit *= 2
    other = exchange(mine, "ha", 1)
    low = jnp.where(core == 0, mine, other)
    high = jnp.where(core == 0, other, mine)
    return jnp.concatenate([low, high], axis=0)


def beside(rows, tall, width):
    parts = [rows[k * tall : (k + 1) * tall] for k in range(lane_blocks(width))]
    return jnp.concatenate(parts, axis=1)[:, :width]


def neighbour_rows(rows, width, dim):
    count = lax.axis_size("ha")
    up = [(i, i + 1) for i in range(count - 1)]
    down = [(i + 1, i) for i in range(count - 1)]
    tail = lax.slice_in_dim(rows, rows.shape[dim] - width, rows.shape[dim], axis=dim)
    head = lax.slice_in_dim(rows, 0, width, axis=dim)
    return lax.ppermute(tail, "ha", up), lax.ppermute(head, "ha", down)


def shards(
    canvas,
    image_id,
    keep_first,
    keep_second,
    first_gain,
    weight_in,
    depth_kernel,
    gate_first,
    gate_second,
    gate_third,
    weight_out,
    scale_first,
    second_gain,
    weight_up,
    weight_down,
    scale_second,
    cotangent,
):
    _, rows, cols, dim = canvas.shape
    cells = rows * cols
    reach = REACH * cols
    count_ha, count_ba = lax.axis_size("ha"), lax.axis_size("ba")
    hidden = weight_up.shape[1]
    blocks = weight_in.shape[1] // LANES
    place = lax.axis_index("ha")[None]
    own = canvas.reshape(cells, dim)
    gates = (gate_first, gate_second, gate_third)
    gain = first_gain[None]
    vectors = (gain, scale_first[None], second_gain[None], scale_second[None])
    order = list(range(count_ba.bit_length() - 1))
    turned = order[len(order) // 2 :] + order[: len(order) // 2]

    above, below = neighbour_rows(own, reach, 0)
    valid, one_keep, two_keep, row_mask, col_mask = masks(place, keep_first, keep_second, image_id[0], rows)
    (
        joined, output, dmiddle, dconv, up_kept, up_sent, down_kept, down_sent, out_kept, out_sent, packed
    ) = forward(
        place, row_mask, above, own, below, valid, one_keep, two_keep, cotangent.reshape(cells, dim), vectors,
        weight_in, depth_kernel, col_mask, gates, weight_out, weight_up, weight_down, rows, cols, count_ha, count_ba,
    )
    above, below = neighbour_rows(dconv, reach, 1)
    up = Chunks([up_kept, exchange(up_sent, "ha", 1)], order)
    down = Chunks([down_kept, exchange(down_sent, "ha", 1)], turned)
    out = Chunks([out_kept, exchange(out_sent, "ha", 1)], turned)
    packed = reduce_whole(packed)

    def back(first_block, end_block, before, ties):
        return backward(
            place, row_mask, above, dconv, below, joined, depth_kernel, col_mask, own, valid, gain, dmiddle, before,
            weight_in, first_block, end_block, ties, rows, cols, count_ha, count_ba,
        )

    ties = [up.outgoing(), down.outgoing()]
    up.halve()
    down.halve()
    cut = blocks * 3 // 4
    dnorm, first_kept, first_sent, first_dk = back(0, cut, dmiddle, ties)
    ties = [up.outgoing(), down.outgoing()]
    up.halve_rest()
    down.halve_rest()
    out.halve_rest()
    dcanvas, second_kept, second_sent, second_dk, dgain_one = back(cut, blocks, dnorm, ties)
    dkern = jnp.concatenate([first_dk, second_dk], axis=0)
    dkern = reduce_whole(dkern.reshape(-1, LANES)).reshape(dkern.shape)
    kept = jnp.concatenate([first_kept, second_kept], axis=0)
    sent = jnp.concatenate([first_sent, second_sent], axis=0)
    parts = [kept, exchange(sent, "ha", 1)]
    middle_row = kept.shape[2] // 2
    in_first = Chunks([part[:, :, :middle_row] for part in parts], order)
    in_second = Chunks([part[:, :, middle_row:] for part in parts], turned)
    in_first.halve_rest()
    in_second.halve_rest()
    dgain_one = reduce_whole(dgain_one)
    dup, ddown, dout = finish([up, down, out])
    din = jnp.concatenate(finish([in_first, in_second]), axis=0)
    dscale_one, dgain_two, dscale_two, dfirst, dsecond, dthird, dkern, dgain_one = unpack(
        packed, dkern, dgain_one, gates, depth_kernel, dim
    )
    return (
        output.reshape(canvas.shape),
        dcanvas.reshape(canvas.shape),
        dgain_one[0],
        beside(din, dim // count_ba, weight_in.shape[1] // count_ha),
        dkern,
        dfirst,
        dsecond,
        dthird,
        beside(dout, dim // count_ha, dim // count_ba).T,
        dscale_one[0],
        dgain_two[0],
        beside(dup, dim // count_ba, hidden // count_ha),
        beside(ddown, dim // count_ha, hidden // count_ba).T,
        dscale_two[0],
    )


def solution(mesh):
    in_specs = (
        P("ba", "ha", None, None),
        P("ba", None, None),
        P("ba", None),
        P("ba", None),
    ) + (P(),) * 12 + (P("ba", "ha", None, None),)
    tiled = P("ba", "ha")
    out_specs = (
        P("ba", "ha", None, None),
        P("ba", "ha", None, None),
        P(),
        tiled,
        P(),
        P(),
        P(),
        P(),
        tiled,
        P(),
        P(),
        tiled,
        tiled,
        P(),
    )
    return jax.shard_map(shards, mesh=mesh, in_specs=in_specs, out_specs=out_specs, check_vma=False)
```

time: 504 us -> 271 us (0.54)
  other arithmetic: 156 us -> 17.1 us
  matrix products: 102 us -> 0 us
  Pallas kernels: 0 us -> 91 us
  waiting for transfers between devices: 152 us -> 96.2 us
  blocking collectives: 38.8 us -> 0 us
  starting transfers between devices: 18.6 us -> 53.9 us
  between operations: 17.9 us -> 1.34 us
  local copies, waits for them, and re-layouts: 16.7 us -> 10.9 us
    reduce_scatter x8 -> x0, waiting for transfers between devices: 121 us -> none  [the longest x1 49.2 us: shards(): lax.psum_scatter(grads[11], 'ha', scatter_dimension=1, tiled=True)]
    dot_general x21 -> x0, matrix products: 102 us -> none  [matmul(): jnp.dot(left, right, precision=lax.Precision.HIGHEST, preferred_element_t...]
    ppermute x4 -> x42, waiting for transfers between devices: 3.42 us -> 96.2 us  [the longest x38 96.2 us: exchange(): lax.ppermute(values, axis, [(i, i ^ bit) for i in range(lax.axis_size(axi...]
    pallas_call x0 -> x5, Pallas kernels: none -> 91 us  [the longest x1 57.3 us: forward(): pl.pallas_call(functools.partial(forward_kernel, rows=rows, cols=cols, co...]
    mul x21 -> x0, other arithmetic: 67.5 us -> none  [the longest x15 40.9 us: masked_depthwise(): kernel[tap_row * KERN + tap_col] * window]
    reduce_sum x12 -> x0, other arithmetic: 41.5 us -> none  [the longest x6 36.3 us: masked_depthwise(): kernel[tap_row * KERN + tap_col] * window]
    psum x1 -> x0, blocking collectives: 38.8 us -> none  [shards(): lax.psum((grad_gain_one, grads[3], grads[4], grads[5], grads[6], grads[8]...]
    ppermute x4 -> x42, starting transfers between devices: 17.8 us -> 53.9 us  [the longest x38 46.2 us: exchange(): lax.ppermute(values, axis, [(i, i ^ bit) for i in range(lax.axis_size(axi...]
  transfers between devices with their start and end apart: 13 -> 42, of which waited for: 7 -> 21; matrix products, arithmetic and copies ran while one was open for 30% -> 6% of each run, Pallas kernels for 0% -> 9%
where the time goes in v2:
time: 271 us; the launch traced here: 270 us
  waiting for transfers between devices  96.2 us (35%)
  Pallas kernels  91 us (34%)
  starting transfers between devices  53.9 us (20%)
  other arithmetic  17.1 us (6%)
  local copies, waits for them, and re-layouts  10.9 us (4%)
    ppermute x38, waiting for transfers between devices, exchange(): lax.ppermute(values, axis, [(i, i ^ bit) for i in range(lax.axis_size(axi...  96.2 us
    pallas_call x1, Pallas kernels, forward(): pl.pallas_call(functools.partial(forward_kernel, rows=rows, cols=cols, co...  57.3 us
    ppermute x38, starting transfers between devices, exchange(): lax.ppermute(values, axis, [(i, i ^ bit) for i in range(lax.axis_size(axi...  46.2 us
    pallas_call x2, Pallas kernels, backward(): pl.pallas_call(functools.partial(backward_kernel, rows=rows, cols=cols, f...  31.6 us
    add x20, other arithmetic, total(): result = result + part  12.2 us
    ppermute x4, starting transfers between devices, neighbour_rows(): return (lax.ppermute(tail, 'ha', up), lax.ppermute(head, 'ha', down))  7.66 us
    unnamed x47, local copies, waits for them, and re-layouts  6.57 us
  transfers between devices with their start and end apart: 42, of which 21 were waited for; matrix products, arithmetic and copies ran while one was open for 6% of the time, Pallas kernels for 9%

profile of v2, /device:TPU:0, one launch (start us, length us, event | category | flops | bytes accessed | tf_op | source)
XLA Modules:
  0.0 270.4 jit_solution(4892104164569584684)
XLA Ops:
  1.8 2.4 collective-permute-start
  4.2 1.3 collective-permute-start.1
  13.2 57.3 %shard_map.273 = (f32[8,512,128]{2,1,0:T(8,128)}, f32[512,512]{1,0:T(8,128)}, f32[512,512]{1,0:T(8,128)}, f32[8,512,128]{2,1,0:T(8,128)}, f32[4,4,256,128]{3,2,1...) custom-call(s32[1]{0:T(128)} %bitcast.place_ref, ...), custom_call_target="tpu_custom_call" | custom-call | flops 76999999488 | tf_op jit(solution)/shard_map/pallas_call | solution.py:411
  71.6 3.6 %collective-permute-start.8 = (f32[680,128]{1,0:T(8,128)S(1)}, f32[680,128]{1,0:T(8,128)S(1)}, u32[]{:S(2)}, u32[]{:S(2)}) collective-permute-start(f32[680,128]{1,0:T(8,128)S(1)} %dynamic-slice_bitcast_fusion), channel_id=1, source_target_pairs={{0,4},{4,0},{8,12},{12,8},{16,20},{20,16},{24,28},{28,24},{1,5},{5... | collective-permute-start | bytes 1044488 | tf_op jit(solution)/shard_map/ppermute | solution.py:612
  75.2 1.3 collective-permute-done.8
  77.5 1.6 collective-permute-start.9
  79.6 8.4 %collective-permute-done.9 = f32[680,128]{1,0:T(8,128)S(1)} collective-permute-done((f32[680,128]{1,0:T(8,128)S(1)}, f32[680,128]{1,0:T(8,128)S(1)}, u32[]{:S(2)}, u32[]{:S(2)}) %collective-permute-start.9) | collective-permute-done | bytes 348192 | tf_op jit(solution)/shard_map/ppermute | solution.py:612
  88.1 1.6 collective-permute-start.10
  89.6 8.1 %collective-permute-done.10 = f32[680,128]{1,0:T(8,128)S(1)} collective-permute-done((f32[680,128]{1,0:T(8,128)S(1)}, f32[680,128]{1,0:T(8,128)S(1)}, u32[]{:S(2)}, u32[]{:S(2)}) %collective-permute-start.10) | collective-permute-done | bytes 348192 | tf_op jit(solution)/shard_map/ppermute | solution.py:612
  97.8 1.5 collective-permute-start.11
  99.3 1.7 add_bitcast_fusion.2
  101.0 1.6 collective-permute-start.35
  102.5 4.1 %collective-permute-done.11 = f32[680,128]{1,0:T(8,128)} collective-permute-done((f32[680,128]{1,0:T(8,128)S(1)}, f32[680,128]{1,0:T(8,128)}, u32[]{:S(2)}, u32[]{:S(2)}) %collective-permute-start.11) | collective-permute-done | bytes 348192 | tf_op jit(solution)/shard_map/ppermute | solution.py:612
  107.7 2.4 collective-permute-start.12
  111.0 1.6 collective-permute-start.36
  112.6 11.2 %collective-permute-done.12 = f32[680,128]{1,0:T(8,128)S(1)} collective-permute-done((f32[680,128]{1,0:T(8,128)S(1)}, f32[680,128]{1,0:T(8,128)S(1)}, u32[]{:S(2)}, u32[]{:S(2)}) %collective-permute-start.12) | collective-permute-done | bytes 348192 | tf_op jit(solution)/shard_map/ppermute | solution.py:612
  124.1 2.7 collective-permute-start.2
  126.9 1.3 collective-permute-start.3
  129.2 1.5 add_bitcast_fusion.1.rest_0_
  130.8 1.5 collective-permute-start.6
  132.3 1.3 add_bitcast_fusion.rest_1_
  133.7 1.6 collective-permute-start.7
  135.4 21.7 %shard_map.274 = (f32[512,512]{1,0:T(8,128)S(1)}, f32[3,4,128,128]{3,2,1,0:T(8,128)S(1)}, f32[3,4,128,128]{3,2,1,0:T(8,128)S(1)}, f32[6,56,128]{2,1,0:T(8,128)S(1)}) custom-call(s32[1]{0:T(128)} %bitcast.place_ref, f32[8,128]{1,0:T(8,128)S(1)} %copy-done.17, f32[8,192,128]{2,1,0:T(8,128)S(1)} %collective-permute-done.2.above_ref, ...), custom_call_target="tpu_custom_call" | custom-call | flops 26400000000 | tf_op jit(solution)/shard_map/pallas_call | solution.py:552
  157.0 1.7 copy.31
  160.1 9.9 %shard_map.275 = (f32[512,512]{1,0:T(8,128)}, f32[1,4,128,128]{3,2,1,0:T(8,128)S(1)}, f32[1,4,128,128]{3,2,1,0:T(8,128)S(1)}, f32[2,56,128]{2,1,0:T(8,128)S(1)}, f32[16,128]{1,0:T(8,128)S(1)}) custom-call(s32[1]{0:T(128)} %bitcast.place_ref, f32[8,128]{1,0:T(8,128)S(1)} %copy-done.17, f32[8,192,128]{2,1,0:T(8,128)S(1)} %collective-permute-done.2.above_ref, ...), custom_call_target="tpu_custom_call" | custom-call | flops 8800000000 | tf_op jit(solution)/shard_map/pallas_call | solution.py:552
  170.0 5.1 %collective-permute-start.20 = (f32[8,128]{1,0:T(8,128)S(1)}, f32[8,128]{1,0:T(8,128)S(1)}, u32[]{:S(2)}, u32[]{:S(2)}) collective-permute-start(f32[8,128]{1,0:T(8,128)S(1)} %fusion.3), channel_id=1, source_target_pairs={{0,4},{4,0},{8,12},{12,8},{16,20},{20,16},{24,28},{28,24},{1,5},{5... | collective-permute-start | bytes 12296 | tf_op jit(solution)/shard_map/ppermute | solution.py:612
  175.2 1.6 collective-permute-start.37
  176.8 1.5 collective-permute-start.38
  178.8 11.6 %collective-permute-done.21 = f32[8,128]{1,0:T(8,128)S(1)} collective-permute-done((f32[8,128]{1,0:T(8,128)S(1)}, f32[8,128]{1,0:T(8,128)S(1)}, u32[]{:S(2)}, u32[]{:S(2)}) %collective-permute-start.21) | collective-permute-done | bytes 4128 | tf_op jit(solution)/shard_map/ppermute | solution.py:612
  191.0 3.0 %collective-permute-done.22 = f32[8,128]{1,0:T(8,128)S(1)} collective-permute-done((f32[8,128]{1,0:T(8,128)S(1)}, f32[8,128]{1,0:T(8,128)S(1)}, u32[]{:S(2)}, u32[]{:S(2)}) %collective-permute-start.22) | collective-permute-done | bytes 4128 | tf_op jit(solution)/shard_map/ppermute | solution.py:612
  194.0 3.6 %collective-permute-done.23 = f32[8,128]{1,0:T(8,128)S(1)} collective-permute-done((f32[8,128]{1,0:T(8,128)S(1)}, f32[8,128]{1,0:T(8,128)S(1)}, u32[]{:S(2)}, u32[]{:S(2)}) %collective-permute-start.23) | collective-permute-done | bytes 4128 | tf_op jit(solution)/shard_map/ppermute | solution.py:612
  197.6 2.9 %collective-permute-start.24 = (f32[8,128]{1,0:T(8,128)S(1)}, f32[8,128]{1,0:T(8,128)S(1)}, u32[]{:S(2)}, u32[]{:S(2)}) collective-permute-start(f32[8,128]{1,0:T(8,128)S(1)} %add.1000), channel_id=1, source_target_pairs={{0,16},{4,20},{8,24},{12,28},{16,0},{20,4},{24,8},{28,12},{1,17},{... | collective-permute-start | bytes 12296 | tf_op jit(solution)/shard_map/ppermute | solution.py:612
  200.6 1.6 collective-permute-start.15
  202.3 3.1 %collective-permute-done.15 = f32[224,128]{1,0:T(8,128)S(1)} collective-permute-done((f32[224,128]{1,0:T(8,128)S(1)}, f32[224,128]{1,0:T(8,128)S(1)}, u32[]{:S(2)}, u32[]{:S(2)}) %collective-permute-start.15) | collective-permute-done | bytes 114720 | tf_op jit(solution)/shard_map/ppermute | solution.py:612
  206.2 4.1 %collective-permute-done.16 = f32[224,128]{1,0:T(8,128)S(1)} collective-permute-done((f32[224,128]{1,0:T(8,128)S(1)}, f32[224,128]{1,0:T(8,128)S(1)}, u32[]{:S(2)}, u32[]{:S(2)}) %collective-permute-start.16) | collective-permute-done | bytes 114720 | tf_op jit(solution)/shard_map/ppermute | solution.py:612
  210.4 5.2 %collective-permute-done.17 = f32[224,128]{1,0:T(8,128)S(1)} collective-permute-done((f32[224,128]{1,0:T(8,128)S(1)}, f32[224,128]{1,0:T(8,128)S(1)}, u32[]{:S(2)}, u32[]{:S(2)}) %collective-permute-start.17) | collective-permute-done | bytes 114720 | tf_op jit(solution)/shard_map/ppermute | solution.py:612
  218.8 2.4 collective-permute-start.40
  221.2 4.3 %collective-permute-done.18 = f32[224,128]{1,0:T(8,128)S(1)} collective-permute-done((f32[224,128]{1,0:T(8,128)S(1)}, f32[224,128]{1,0:T(8,128)S(1)}, u32[]{:S(2)}, u32[]{:S(2)}) %collective-permute-start.18) | collective-permute-done | bytes 114720 | tf_op jit(solution)/shard_map/ppermute | solution.py:612
  227.9 2.2 collective-permute-done.39
  230.2 12.2 %collective-permute-done.40 = f32[576,128]{1,0:T(8,128)S(1)} collective-permute-done((f32[576,128]{1,0:T(8,128)S(1)}, f32[576,128]{1,0:T(8,128)S(1)}, u32[]{:S(2)}, u32[]{:S(2)}) %collective-permute-start.40) | collective-permute-done | bytes 294944 | tf_op jit(solution)/shard_map/ppermute | solution.py:612
  243.6 1.6 collective-permute-start.27
  245.6 1.4 fusion
  247.0 3.0 %collective-permute-done.27 = f32[4,2,64,128]{3,2,1,0:T(8,128)S(1)} collective-permute-done((f32[4,2,64,128]{3,2,1,0:T(8,128)S(1)}, f32[4,2,64,128]{3,2,1,0:T(8,128)S(1)}, u32[]{:S(2)}, u32[]{:S(2)}) %collective-permute-start.27) | collective-permute-done | bytes 262176 | tf_op jit(solution)/shard_map/ppermute | solution.py:612
  250.5 2.3 collective-permute-done.29
  255.1 2.8 %collective-permute-done.30 = f32[4,64,128]{2,1,0:T(8,128)S(1)} collective-permute-done((f32[4,64,128]{2,1,0:T(8,128)S(1)}, f32[4,64,128]{2,1,0:T(8,128)S(1)}, u32[]{:S(2)}, u32[]{:S(2)}) %collective-permute-start.30) | collective-permute-done | bytes 131104 | tf_op jit(solution)/shard_map/ppermute | solution.py:612
  257.9 5.2 %collective-permute-start.31 = (f32[128,128]{1,0:T(8,128)S(1)}, f32[128,128]{1,0:T(8,128)S(1)}, u32[]{:S(2)}, u32[]{:S(2)}) collective-permute-start(f32[128,128]{1,0:T(8,128)S(1)} %pad_maximum_fusion.8), channel_id=1, source_target_pairs={{0,8},{4,12},{8,0},{12,4},{16,24},{20,28},{24,16},{28,20},{1,9},{5... | collective-permute-start | bytes 196616 | tf_op jit(solution)/shard_map/ppermute | solution.py:612
  263.6 2.0 collective-permute-start.33
  266.3 2.3 collective-permute-done.32
  (149 shorter events, 31.1 us)
Async XLA Ops:
  1.8 10.4 %collective-permute-start = (f32[192,512]{1,0:T(8,128)S(1)}, f32[192,512]{1,0:T(8,128)S(1)}, u32[]{:S(2)}, u32[]{:S(2)}) collective-permute-start(f32[192,512]{1,0:T(8,128)S(1)} %bitcast.302), channel_id=1, source_target_pairs={{0,4},{4,8},{8,12},{12,16},{16,20},{20,24},{24,28},{1,5},{5,9},{9,... | collective-permute-start | bytes 1179656 | tf_op jit(solution)/shard_map/ppermute | solution.py:695
  4.2 8.0 %collective-permute-start.1 = (f32[192,512]{1,0:T(8,128)S(1)}, f32[192,512]{1,0:T(8,128)S(1)}, u32[]{:S(2)}, u32[]{:S(2)}) collective-permute-start(f32[192,512]{1,0:T(8,128)S(1)} %bitcast.301), channel_id=1, source_target_pairs={{4,0},{8,4},{12,8},{16,12},{20,16},{24,20},{28,24},{5,1},{9,5},{13... | collective-permute-start | bytes 1179656 | tf_op jit(solution)/shard_map/ppermute | solution.py:695
  70.5 28.8 %copy-start.20 = (f32[4,4,64,128]{3,2,1,0:T(8,128)S(1)}, f32[4,4,64,128]{3,2,1,0:T(8,128)}, u32[]{:S(2)}) copy-start(f32[4,4,64,128]{3,2,1,0:T(8,128)} %get-tuple-element.75) | copy-start | bytes 1572868
  71.6 4.9 %collective-permute-start.8 = (f32[680,128]{1,0:T(8,128)S(1)}, f32[680,128]{1,0:T(8,128)S(1)}, u32[]{:S(2)}, u32[]{:S(2)}) collective-permute-start(f32[680,128]{1,0:T(8,128)S(1)} %dynamic-slice_bitcast_fusion), channel_id=1, source_target_pairs={{0,4},{4,0},{8,12},{12,8},{16,20},{20,16},{24,28},{28,24},{1,5},{5... | collective-permute-start | bytes 1044488 | tf_op jit(solution)/shard_map/ppermute | solution.py:612
  77.5 10.5 %collective-permute-start.9 = (f32[680,128]{1,0:T(8,128)S(1)}, f32[680,128]{1,0:T(8,128)S(1)}, u32[]{:S(2)}, u32[]{:S(2)}) collective-permute-start(f32[680,128]{1,0:T(8,128)S(1)} %bitcast_add_fusion.3), channel_id=1, source_target_pairs={{0,1},{1,0},{2,3},{3,2},{4,5},{5,4},{6,7},{7,6},{8,9},{9,8},{10,11... | collective-permute-start | bytes 1044488 | tf_op jit(solution)/shard_map/ppermute | solution.py:612
  79.1 50.1 %collective-permute-start.4 = (f32[4,4,256,128]{3,2,1,0:T(8,128)}, f32[4,4,256,128]{3,2,1,0:T(8,128)}, u32[]{:S(2)}, u32[]{:S(2)}) collective-permute-start(f32[4,4,256,128]{3,2,1,0:T(8,128)} %get-tuple-element.57), channel_id=1, source_target_pairs={{0,4},{4,0},{8,12},{12,8},{16,20},{20,16},{24,28},{28,24},{1,5},{5... | collective-permute-start | bytes 6291464 | tf_op jit(solution)/shard_map/ppermute | solution.py:612
  79.1 53.2 %collective-permute-start.5 = (f32[4,4,256,128]{3,2,1,0:T(8,128)}, f32[4,4,256,128]{3,2,1,0:T(8,128)}, u32[]{:S(2)}, u32[]{:S(2)}) collective-permute-start(f32[4,4,256,128]{3,2,1,0:T(8,128)} %get-tuple-element.59), channel_id=1, source_target_pairs={{0,4},{4,0},{8,12},{12,8},{16,20},{20,16},{24,28},{28,24},{1,5},{5... | collective-permute-start | bytes 6291464 | tf_op jit(solution)/shard_map/ppermute | solution.py:612
  88.1 9.7 %collective-permute-start.10 = (f32[680,128]{1,0:T(8,128)S(1)}, f32[680,128]{1,0:T(8,128)S(1)}, u32[]{:S(2)}, u32[]{:S(2)}) collective-permute-start(f32[680,128]{1,0:T(8,128)S(1)} %add.988), channel_id=1, source_target_pairs={{0,2},{1,3},{2,0},{3,1},{4,6},{5,7},{6,4},{7,5},{8,10},{9,11},{10,... | collective-permute-start | bytes 1044488 | tf_op jit(solution)/shard_map/ppermute | solution.py:612
  89.6 34.4 %copy-start = (f32[8,512,128]{2,1,0:T(8,128)S(1)}, f32[8,512,128]{2,1,0:T(8,128)}, u32[]{:S(2)}) copy-start(f32[8,512,128]{2,1,0:T(8,128)} %get-tuple-element.53.own_ref) | copy-start | bytes 6291460
  89.6 9.6 %collective-permute-start.34 = (f32[4,4,64,128]{3,2,1,0:T(8,128)}, f32[4,4,64,128]{3,2,1,0:T(8,128)}, u32[]{:S(2)}, u32[]{:S(2)}) collective-permute-start(f32[4,4,64,128]{3,2,1,0:T(8,128)} %get-tuple-element.76), channel_id=1, source_target_pairs={{0,4},{4,0},{8,12},{12,8},{16,20},{20,16},{24,28},{28,24},{1,5},{5... | collective-permute-start | bytes 1572872 | tf_op jit(solution)/shard_map/ppermute | solution.py:612
  97.8 8.9 %collective-permute-start.11 = (f32[680,128]{1,0:T(8,128)S(1)}, f32[680,128]{1,0:T(8,128)}, u32[]{:S(2)}, u32[]{:S(2)}) collective-permute-start(f32[680,128]{1,0:T(8,128)S(1)} %add.989), channel_id=1, source_target_pairs={{0,8},{4,12},{8,0},{12,4},{16,24},{20,28},{24,16},{28,20},{1,9},{5... | collective-permute-start | bytes 1044488 | tf_op jit(solution)/shard_map/ppermute | solution.py:612
  101.0 9.1 %collective-permute-start.35 = (f32[4,2,64,128]{3,2,1,0:T(8,128)}, f32[4,2,64,128]{3,2,1,0:T(8,128)}, u32[]{:S(2)}, u32[]{:S(2)}) collective-permute-start(f32[4,2,64,128]{3,2,1,0:T(8,128)} %add_bitcast_fusion.2), channel_id=1, source_target_pairs={{0,2},{1,3},{2,0},{3,1},{4,6},{5,7},{6,4},{7,5},{8,10},{9,11},{10,... | collective-permute-start | bytes 786440 | tf_op jit(solution)/shard_map/ppermute | solution.py:612
  107.7 16.2 %collective-permute-start.12 = (f32[680,128]{1,0:T(8,128)S(1)}, f32[680,128]{1,0:T(8,128)S(1)}, u32[]{:S(2)}, u32[]{:S(2)}) collective-permute-start(f32[680,128]{1,0:T(8,128)S(1)} %add.990), channel_id=1, source_target_pairs={{0,16},{4,20},{8,24},{12,28},{16,0},{20,4},{24,8},{28,12},{1,17},{... | collective-permute-start | bytes 1044488 | tf_op jit(solution)/shard_map/ppermute | solution.py:612
  111.0 15.8 %collective-permute-start.36 = (f32[4,64,128]{2,1,0:T(8,128)S(1)}, f32[4,64,128]{2,1,0:T(8,128)S(1)}, u32[]{:S(2)}, u32[]{:S(2)}) collective-permute-start(f32[4,64,128]{2,1,0:T(8,128)S(1)} %bitcast_add_fusion.21), channel_id=1, source_target_pairs={{0,1},{1,0},{2,3},{3,2},{4,5},{5,4},{6,7},{7,6},{8,9},{9,8},{10,11... | collective-permute-start | bytes 393224 | tf_op jit(solution)/shard_map/ppermute | solution.py:612
  123.9 5.1 %collective-permute-start.13 = (f32[680,128]{1,0:T(8,128)S(1)}, f32[680,128]{1,0:T(8,128)S(1)}, u32[]{:S(2)}, u32[]{:S(2)}) collective-permute-start(f32[680,128]{1,0:T(8,128)S(1)} %add.991), channel_id=1, source_target_pairs={{0,4},{4,0},{8,12},{12,8},{16,20},{20,16},{24,28},{28,24},{1,5},{5... | collective-permute-start | bytes 1044488 | tf_op jit(solution)/shard_map/ppermute | solution.py:612
  124.0 8.3 %copy-start.19 = (f32[4,4,256,128]{3,2,1,0:T(8,128)S(1)}, f32[4,4,256,128]{3,2,1,0:T(8,128)}, u32[]{:S(2)}) copy-start(f32[4,4,256,128]{3,2,1,0:T(8,128)} %get-tuple-element.58) | copy-start | bytes 6291460
  124.1 11.1 %collective-permute-start.2 = (f32[8,192,128]{2,1,0:T(8,128)S(1)}, f32[8,192,128]{2,1,0:T(8,128)S(1)}, u32[]{:S(2)}, u32[]{:S(2)}) collective-permute-start(f32[8,192,128]{2,1,0:T(8,128)S(1)} %get-tuple-element.87), channel_id=1, source_target_pairs={{0,4},{4,8},{8,12},{12,16},{16,20},{20,24},{24,28},{1,5},{5,9},{9,... | collective-permute-start | bytes 2359304 | tf_op jit(solution)/shard_map/ppermute | solution.py:695
  126.9 8.4 %collective-permute-start.3 = (f32[8,192,128]{2,1,0:T(8,128)S(1)}, f32[8,192,128]{2,1,0:T(8,128)S(1)}, u32[]{:S(2)}, u32[]{:S(2)}) collective-permute-start(f32[8,192,128]{2,1,0:T(8,128)S(1)} %get-tuple-element.86), channel_id=1, source_target_pairs={{4,0},{8,4},{12,8},{16,12},{20,16},{24,20},{28,24},{5,1},{9,5},{13... | collective-permute-start | bytes 2359304 | tf_op jit(solution)/shard_map/ppermute | solution.py:695
  129.1 6.2 %copy-start.11 = (f32[512,512]{1,0:T(8,128)S(1)}, f32[512,512]{1,0:T(8,128)}, u32[]{:S(2)}) copy-start(f32[512,512]{1,0:T(8,128)} %get-tuple-element.55.dmiddle_ref.before_ref) | copy-start | bytes 3145732
  129.2 6.1 %copy-start.3 = (f32[49,960]{1,0:T(8,128)S(1)}, f32[49,960]{1,0:T(8,128)}, u32[]{:S(2)}) copy-start(f32[49,960]{1,0:T(8,128)} %kern_ref.5) | copy-start | bytes 564484
  129.2 6.1 %copy-start.8 = (f32[8,512,128]{2,1,0:T(8,128)S(1)}, f32[8,512,128]{2,1,0:T(8,128)}, u32[]{:S(2)}) copy-start(f32[8,512,128]{2,1,0:T(8,128)} %get-tuple-element.54.mix_ref) | copy-start | bytes 6291460
  130.8 28.0 %collective-permute-start.6 = (f32[4,2,256,128]{3,2,1,0:T(8,128)S(1)}, f32[4,2,256,128]{3,2,1,0:T(8,128)S(1)}, u32[]{:S(2)}, u32[]{:S(2)}) collective-permute-start(f32[4,2,256,128]{3,2,1,0:T(8,128)S(1)} %add_bitcast_fusion.1.rest_0_), channel_id=1, source_target_pairs={{0,1},{1,0},{2,3},{3,2},{4,5},{5,4},{6,7},{7,6},{8,9},{9,8},{10,11... | collective-permute-start | bytes 3145736 | tf_op jit(solution)/shard_map/ppermute | solution.py:612
  133.7 26.3 %collective-permute-start.7 = (f32[4,2,256,128]{3,2,1,0:T(8,128)S(1)}, f32[4,2,256,128]{3,2,1,0:T(8,128)S(1)}, u32[]{:S(2)}, u32[]{:S(2)}) collective-permute-start(f32[4,2,256,128]{3,2,1,0:T(8,128)S(1)} %add_bitcast_fusion.rest_1_), channel_id=1, source_target_pairs={{0,2},{1,3},{2,0},{3,1},{4,6},{5,7},{6,4},{7,5},{8,10},{9,11},{10,... | collective-permute-start | bytes 3145736 | tf_op jit(solution)/shard_map/ppermute | solution.py:612
  170.0 8.3 %collective-permute-start.20 = (f32[8,128]{1,0:T(8,128)S(1)}, f32[8,128]{1,0:T(8,128)S(1)}, u32[]{:S(2)}, u32[]{:S(2)}) collective-permute-start(f32[8,128]{1,0:T(8,128)S(1)} %fusion.3), channel_id=1, source_target_pairs={{0,4},{4,0},{8,12},{12,8},{16,20},{20,16},{24,28},{28,24},{1,5},{5... | collective-permute-start | bytes 12296 | tf_op jit(solution)/shard_map/ppermute | solution.py:612
  175.2 41.2 %collective-permute-start.37 = (f32[4,256,128]{2,1,0:T(8,128)S(1)}, f32[4,256,128]{2,1,0:T(8,128)S(1)}, u32[]{:S(2)}, u32[]{:S(2)}) collective-permute-start(f32[4,256,128]{2,1,0:T(8,128)S(1)} %bitcast_add_fusion.2.rest_0_), channel_id=1, source_target_pairs={{0,2},{1,3},{2,0},{3,1},{4,6},{5,7},{6,4},{7,5},{8,10},{9,11},{10,... | collective-permute-start | bytes 1572872 | tf_op jit(solution)/shard_map/ppermute | solution.py:612
  176.8 40.7 %collective-permute-start.38 = (f32[4,256,128]{2,1,0:T(8,128)S(1)}, f32[4,256,128]{2,1,0:T(8,128)S(1)}, u32[]{:S(2)}, u32[]{:S(2)}) collective-permute-start(f32[4,256,128]{2,1,0:T(8,128)S(1)} %bitcast_add_fusion.rest_1_), channel_id=1, source_target_pairs={{0,1},{1,0},{2,3},{3,2},{4,5},{5,4},{6,7},{7,6},{8,9},{9,8},{10,11... | collective-permute-start | bytes 1572872 | tf_op jit(solution)/shard_map/ppermute | solution.py:612
  178.3 12.1 %collective-permute-start.21 = (f32[8,128]{1,0:T(8,128)S(1)}, f32[8,128]{1,0:T(8,128)S(1)}, u32[]{:S(2)}, u32[]{:S(2)}) collective-permute-start(f32[8,128]{1,0:T(8,128)S(1)} %fusion.2), channel_id=1, source_target_pairs={{0,1},{1,0},{2,3},{3,2},{4,5},{5,4},{6,7},{7,6},{8,9},{9,8},{10,11... | collective-permute-start | bytes 12296 | tf_op jit(solution)/shard_map/ppermute | solution.py:612
  190.4 3.6 %collective-permute-start.22 = (f32[8,128]{1,0:T(8,128)S(1)}, f32[8,128]{1,0:T(8,128)S(1)}, u32[]{:S(2)}, u32[]{:S(2)}) collective-permute-start(f32[8,128]{1,0:T(8,128)S(1)} %add.998), channel_id=1, source_target_pairs={{0,2},{1,3},{2,0},{3,1},{4,6},{5,7},{6,4},{7,5},{8,10},{9,11},{10,... | collective-permute-start | bytes 12296 | tf_op jit(solution)/shard_map/ppermute | solution.py:612
  190.9 9.6 %collective-permute-start.14 = (f32[224,128]{1,0:T(8,128)S(1)}, f32[224,128]{1,0:T(8,128)S(1)}, u32[]{:S(2)}, u32[]{:S(2)}) collective-permute-start(f32[224,128]{1,0:T(8,128)S(1)} %dynamic-slice_bitcast_fusion.1), channel_id=1, source_target_pairs={{0,4},{4,0},{8,12},{12,8},{16,20},{20,16},{24,28},{28,24},{1,5},{5... | collective-permute-start | bytes 344072 | tf_op jit(solution)/shard_map/ppermute | solution.py:612
  194.0 3.6 %collective-permute-start.23 = (f32[8,128]{1,0:T(8,128)S(1)}, f32[8,128]{1,0:T(8,128)S(1)}, u32[]{:S(2)}, u32[]{:S(2)}) collective-permute-start(f32[8,128]{1,0:T(8,128)S(1)} %add.999), channel_id=1, source_target_pairs={{0,8},{4,12},{8,0},{12,4},{16,24},{20,28},{24,16},{28,20},{1,9},{5... | collective-permute-start | bytes 12296 | tf_op jit(solution)/shard_map/ppermute | solution.py:612
  197.6 4.6 %collective-permute-start.24 = (f32[8,128]{1,0:T(8,128)S(1)}, f32[8,128]{1,0:T(8,128)S(1)}, u32[]{:S(2)}, u32[]{:S(2)}) collective-permute-start(f32[8,128]{1,0:T(8,128)S(1)} %add.1000), channel_id=1, source_target_pairs={{0,16},{4,20},{8,24},{12,28},{16,0},{20,4},{24,8},{28,12},{1,17},{... | collective-permute-start | bytes 12296 | tf_op jit(solution)/shard_map/ppermute | solution.py:612
  200.6 4.9 %collective-permute-start.15 = (f32[224,128]{1,0:T(8,128)S(1)}, f32[224,128]{1,0:T(8,128)S(1)}, u32[]{:S(2)}, u32[]{:S(2)}) collective-permute-start(f32[224,128]{1,0:T(8,128)S(1)} %bitcast_add_fusion.24), channel_id=1, source_target_pairs={{0,1},{1,0},{2,3},{3,2},{4,5},{5,4},{6,7},{7,6},{8,9},{9,8},{10,11... | collective-permute-start | bytes 344072 | tf_op jit(solution)/shard_map/ppermute | solution.py:612
  202.3 8.1 %collective-permute-start.25 = (f32[8,128]{1,0:T(8,128)S(1)}, f32[8,128]{1,0:T(8,128)S(1)}, u32[]{:S(2)}, u32[]{:S(2)}) collective-permute-start(f32[8,128]{1,0:T(8,128)S(1)} %add.1001), channel_id=1, source_target_pairs={{0,4},{4,0},{8,12},{12,8},{16,20},{20,16},{24,28},{28,24},{1,5},{5... | collective-permute-start | bytes 12296 | tf_op jit(solution)/shard_map/ppermute | solution.py:612
  205.5 4.9 %collective-permute-start.16 = (f32[224,128]{1,0:T(8,128)S(1)}, f32[224,128]{1,0:T(8,128)S(1)}, u32[]{:S(2)}, u32[]{:S(2)}) collective-permute-start(f32[224,128]{1,0:T(8,128)S(1)} %add.993), channel_id=1, source_target_pairs={{0,2},{1,3},{2,0},{3,1},{4,6},{5,7},{6,4},{7,5},{8,10},{9,11},{10,... | collective-permute-start | bytes 344072 | tf_op jit(solution)/shard_map/ppermute | solution.py:612
  206.1 37.3 %collective-permute-start.26 = (f32[4,4,128,128]{3,2,1,0:T(8,128)S(1)}, f32[4,4,128,128]{3,2,1,0:T(8,128)S(1)}, u32[]{:S(2)}, u32[]{:S(2)}) collective-permute-start(f32[4,4,128,128]{3,2,1,0:T(8,128)S(1)} %pad_maximum_fusion), channel_id=1, source_target_pairs={{0,4},{4,0},{8,12},{12,8},{16,20},{20,16},{24,28},{28,24},{1,5},{5... | collective-permute-start | bytes 3145736 | tf_op jit(solution)/shard_map/ppermute | solution.py:612
  210.3 5.4 %collective-permute-start.17 = (f32[224,128]{1,0:T(8,128)S(1)}, f32[224,128]{1,0:T(8,128)S(1)}, u32[]{:S(2)}, u32[]{:S(2)}) collective-permute-start(f32[224,128]{1,0:T(8,128)S(1)} %add.994), channel_id=1, source_target_pairs={{0,8},{4,12},{8,0},{12,4},{16,24},{20,28},{24,16},{28,20},{1,9},{5... | collective-permute-start | bytes 344072 | tf_op jit(solution)/shard_map/ppermute | solution.py:612
  215.7 9.8 %collective-permute-start.18 = (f32[224,128]{1,0:T(8,128)S(1)}, f32[224,128]{1,0:T(8,128)S(1)}, u32[]{:S(2)}, u32[]{:S(2)}) collective-permute-start(f32[224,128]{1,0:T(8,128)S(1)} %add.995), channel_id=1, source_target_pairs={{0,16},{4,20},{8,24},{12,28},{16,0},{20,4},{24,8},{28,12},{1,17},{... | collective-permute-start | bytes 344072 | tf_op jit(solution)/shard_map/ppermute | solution.py:612
  218.7 11.5 %collective-permute-start.39 = (f32[576,128]{1,0:T(8,128)S(1)}, f32[576,128]{1,0:T(8,128)S(1)}, u32[]{:S(2)}, u32[]{:S(2)}) collective-permute-start(f32[576,128]{1,0:T(8,128)S(1)} %pad_maximum_fusion.2), channel_id=1, source_target_pairs={{0,8},{4,12},{8,0},{12,4},{16,24},{20,28},{24,16},{28,20},{1,9},{5... | collective-permute-start | bytes 884744 | tf_op jit(solution)/shard_map/ppermute | solution.py:612
  218.8 23.6 %collective-permute-start.40 = (f32[576,128]{1,0:T(8,128)S(1)}, f32[576,128]{1,0:T(8,128)S(1)}, u32[]{:S(2)}, u32[]{:S(2)}) collective-permute-start(f32[576,128]{1,0:T(8,128)S(1)} %pad_maximum_fusion.3), channel_id=1, source_target_pairs={{0,16},{4,20},{8,24},{12,28},{16,0},{20,4},{24,8},{28,12},{1,17},{... | collective-permute-start | bytes 884744 | tf_op jit(solution)/shard_map/ppermute | solution.py:612
  225.5 1.4 collective-permute-start.19
  225.6 16.8 %collective-permute-start.41 = (f32[576,128]{1,0:T(8,128)S(1)}, f32[576,128]{1,0:T(8,128)S(1)}, u32[]{:S(2)}, u32[]{:S(2)}) collective-permute-start(f32[576,128]{1,0:T(8,128)S(1)} %pad_maximum_fusion.4), channel_id=1, source_target_pairs={{0,24},{4,28},{8,16},{12,20},{16,8},{20,12},{24,0},{28,4},{1,25},{... | collective-permute-start | bytes 884744 | tf_op jit(solution)/shard_map/ppermute | solution.py:612
  243.6 6.4 %collective-permute-start.27 = (f32[4,2,64,128]{3,2,1,0:T(8,128)S(1)}, f32[4,2,64,128]{3,2,1,0:T(8,128)S(1)}, u32[]{:S(2)}, u32[]{:S(2)}) collective-permute-start(f32[4,2,64,128]{3,2,1,0:T(8,128)S(1)} %add_bitcast_fusion.4), channel_id=1, source_target_pairs={{0,1},{1,0},{2,3},{3,2},{4,5},{5,4},{6,7},{7,6},{8,9},{9,8},{10,11... | collective-permute-start | bytes 786440 | tf_op jit(solution)/shard_map/ppermute | solution.py:612
  245.2 7.6 %collective-permute-start.29 = (f32[4,2,64,128]{3,2,1,0:T(8,128)S(1)}, f32[4,2,64,128]{3,2,1,0:T(8,128)S(1)}, u32[]{:S(2)}, u32[]{:S(2)}) collective-permute-start(f32[4,2,64,128]{3,2,1,0:T(8,128)S(1)} %add_bitcast_fusion.3), channel_id=1, source_target_pairs={{0,2},{1,3},{2,0},{3,1},{4,6},{5,7},{6,4},{7,5},{8,10},{9,11},{10,... | collective-permute-start | bytes 786440 | tf_op jit(solution)/shard_map/ppermute | solution.py:612
  250.1 5.0 %collective-permute-start.28 = (f32[4,64,128]{2,1,0:T(8,128)S(1)}, f32[4,64,128]{2,1,0:T(8,128)S(1)}, u32[]{:S(2)}, u32[]{:S(2)}) collective-permute-start(f32[4,64,128]{2,1,0:T(8,128)S(1)} %bitcast_add_fusion.23), channel_id=1, source_target_pairs={{0,2},{1,3},{2,0},{3,1},{4,6},{5,7},{6,4},{7,5},{8,10},{9,11},{10,... | collective-permute-start | bytes 393224 | tf_op jit(solution)/shard_map/ppermute | solution.py:612
  252.9 5.0 %collective-permute-start.30 = (f32[4,64,128]{2,1,0:T(8,128)S(1)}, f32[4,64,128]{2,1,0:T(8,128)S(1)}, u32[]{:S(2)}, u32[]{:S(2)}) collective-permute-start(f32[4,64,128]{2,1,0:T(8,128)S(1)} %bitcast_add_fusion.22), channel_id=1, source_target_pairs={{0,1},{1,0},{2,3},{3,2},{4,5},{5,4},{6,7},{7,6},{8,9},{9,8},{10,11... | collective-permute-start | bytes 393224 | tf_op jit(solution)/shard_map/ppermute | solution.py:612
  257.9 8.4 %collective-permute-start.31 = (f32[128,128]{1,0:T(8,128)S(1)}, f32[128,128]{1,0:T(8,128)S(1)}, u32[]{:S(2)}, u32[]{:S(2)}) collective-permute-start(f32[128,128]{1,0:T(8,128)S(1)} %pad_maximum_fusion.8), channel_id=1, source_target_pairs={{0,8},{4,12},{8,0},{12,4},{16,24},{20,28},{24,16},{28,20},{1,9},{5... | collective-permute-start | bytes 196616 | tf_op jit(solution)/shard_map/ppermute | solution.py:612
  263.2 5.4 %collective-permute-start.32 = (f32[128,128]{1,0:T(8,128)S(1)}, f32[128,128]{1,0:T(8,128)S(1)}, u32[]{:S(2)}, u32[]{:S(2)}) collective-permute-start(f32[128,128]{1,0:T(8,128)S(1)} %pad_maximum_fusion.9), channel_id=1, source_target_pairs={{0,16},{4,20},{8,24},{12,28},{16,0},{20,4},{24,8},{28,12},{1,17},{... | collective-permute-start | bytes 196616 | tf_op jit(solution)/shard_map/ppermute | solution.py:612
  263.6 6.2 %collective-permute-start.33 = (f32[128,128]{1,0:T(8,128)S(1)}, f32[128,128]{1,0:T(8,128)S(1)}, u32[]{:S(2)}, u32[]{:S(2)}) collective-permute-start(f32[128,128]{1,0:T(8,128)S(1)} %pad_maximum_fusion.10), channel_id=1, source_target_pairs={{0,24},{4,28},{8,16},{12,20},{16,8},{20,12},{24,0},{28,4},{1,25},{... | collective-permute-start | bytes 196616 | tf_op jit(solution)/shard_map/ppermute | solution.py:612
  (17 other events, 42.7 us)

commit v3 on v2

v3 whole, which is shorter than its diff:
```python
import functools

import jax
import jax.numpy as jnp
from jax import lax
from jax.experimental import pallas as pl
from jax.experimental.pallas import tpu as pltpu
from jax.sharding import PartitionSpec as P

KERN = 7
TAPS = KERN * KERN
REACH = KERN // 2
KEEP_RATE = 0.8
SPREAD = 1.0 / 3.0
EPSILON = 1e-06
LANES = 128
EDGE = 8
VMEM_BYTES = 62 << 20
F32 = jnp.float32
INV_SQRT_2 = 0.7071067811865476
INV_SQRT_2PI = 0.3989422804014327
NN = (((1,), (0,)), ((), ()))
NT = (((1,), (1,)), ((), ()))
TN = (((0,), (0,)), ((), ()))


def dot(left, right, dims=NN):
    return lax.dot_general(left, right, dims, precision=lax.Precision.HIGH, preferred_element_type=F32)


def normalized(values):
    centered = values - jnp.mean(values, axis=-1, keepdims=True)
    scale = lax.rsqrt(jnp.mean(centered * centered, axis=-1, keepdims=True) + EPSILON)
    return centered * scale, scale


def norm_backward(grad_hat, hat, scale):
    return scale * (
        grad_hat
        - jnp.mean(grad_hat, axis=-1, keepdims=True)
        - hat * jnp.mean(grad_hat * hat, axis=-1, keepdims=True)
    )


def params():
    return pltpu.CompilerParams(vmem_limit_bytes=VMEM_BYTES)


def lasting(microseconds):
    return pl.CostEstimate(flops=int(microseconds * 1.1e9), bytes_accessed=0, transcendentals=0)


def whole(shape):
    return pl.BlockSpec(tuple(shape), lambda *_: (0,) * len(shape), pipeline_mode=pl.Buffered(1))


def in_smem():
    return pl.BlockSpec(memory_space=pltpu.SMEM)


def anywhere():
    return pl.BlockSpec(memory_space=pl.ANY)


def shape_of(*shape):
    return jax.ShapeDtypeStruct(shape, F32)


def lane_blocks(width):
    return -(-width // LANES)


def image_ids(ids_ref, padded, place, rows):
    height, cols = ids_ref.shape
    padded[...] = jnp.full(padded.shape, -1, jnp.int32)
    padded[EDGE : EDGE + height, :] = ids_ref[...]
    ids = padded[pl.ds(place * rows + (EDGE - REACH), rows + 2 * REACH), :]
    return jnp.concatenate([ids, jnp.full((-ids.shape[0] % 8, cols), -1, jnp.int32)], axis=0).T


def spread_cells(factors, out_ref, first, rows):
    cols = factors.shape[0]
    for r in range(rows):
        column = factors[:, first + r : first + r + 1]
        out_ref[r * cols : (r + 1) * cols, :] = jnp.broadcast_to(column, (cols, LANES))


def keep_factors(turned, table_ref):
    result = jnp.zeros(turned.shape, F32)
    for slot in range(table_ref.shape[1]):
        result = jnp.where(turned == slot, table_ref[0, slot].astype(F32) / KEEP_RATE, result)
    return result


def conv_masks(ids_scalar, ids_ref, place, row_taps, col_mask, rows):
    height, cols = ids_ref.shape
    wide_ids = jnp.broadcast_to(ids_ref[...].T[:, height // 2 : height // 2 + 1], (cols, LANES))
    column = lax.broadcasted_iota(jnp.int32, (cols, LANES), 0)
    for b in range(KERN):
        shift = b - REACH
        moved = pltpu.roll(wide_ids, (-shift) % cols, 0)
        inside = (column + shift >= 0) & (column + shift < cols)
        same = (moved == wide_ids) & inside
        col_mask[b] = same.astype(F32).reshape(cols // 8, 8, LANES)

    def one(r, _):
        own = ids_scalar[place * rows + r, cols // 2]
        row_taps[r, 0] = KERN
        row_taps[r, KERN + 1] = KERN
        for a in range(KERN):
            other = place * rows + r + a - REACH
            inside = (other >= 0) & (other < height)
            same = ids_scalar[jnp.clip(other, 0, height - 1), cols // 2] == own
            row_taps[r, a + 1] = jnp.where(inside & same, a, KERN)
        return 0

    lax.fori_loop(0, rows, one, 0)


def lay_kernel(kern_ref, laid, split):
    tap = lax.broadcasted_iota(jnp.int32, (TAPS, split), 0)
    own = jnp.where(tap == TAPS // 2, 1.0 / SPREAD, 0.0).astype(F32)
    for k in range(laid.shape[0]):
        start = k * LANES - split
        left = own if k == 0 else kern_ref[:, start : start + split]
        laid[k] = jnp.concatenate([left, kern_ref[:, start + split : start + LANES]], axis=1) * SPREAD


def fill_shifted(flat, col_ref, shifted, rows_ext, cols):
    for b in range(KERN):
        for g in range(cols // 8):
            mask = None if b == REACH else col_ref[b, g]
            for r in range(rows_ext):
                x = flat[pl.ds(EDGE + r * cols + 8 * g + b - REACH, 8), :]
                shifted[b, r, g] = x if b == REACH else x * mask


def spread_taps(kern, wide, turned):
    for t in range(TAPS):
        source = TAPS - 1 - t if turned else t
        wide[t] = jnp.broadcast_to(kern[source : source + 1, :], (8, LANES))
    for t in range(KERN):
        wide[TAPS + t] = jnp.zeros((8, LANES), F32)


def conv_block(row_taps, kern, shifted, wide, out_ref, rows, cols):
    groups = cols // 8
    spread_taps(kern, wide, False)

    def pair(h, _):
        r = 2 * h

        def step(i, totals):
            first, second = totals
            taps_first = row_taps[r, i + 1] * KERN
            taps_second = row_taps[r + 1, i] * KERN
            for b in range(KERN):
                x = shifted[b, r + i]
                first = first + wide[taps_first + b][None] * x
                second = second + wide[taps_second + b][None] * x
            return first, second

        zero = jnp.zeros((groups, 8, LANES), F32)
        first, second = lax.fori_loop(0, KERN + 1, step, (zero, zero), unroll=4)
        out_ref[pl.ds(pl.multiple_of(r * cols, cols), cols), :] = first.reshape(cols, LANES)
        out_ref[pl.ds(pl.multiple_of((r + 1) * cols, cols), cols), :] = second.reshape(cols, LANES)
        return 0

    lax.fori_loop(0, rows // 2, pair, 0)


def conv_grad_block(row_taps, kern, shifted, wide, dk, mix_ref, out_ref, dk_ref, rows, cols):
    groups = cols // 8
    spread_taps(kern, wide, True)
    for t in range(TAPS):
        dk[t] = jnp.zeros((8, LANES), F32)

    def one(r, _):
        start = pl.ds(pl.multiple_of(r * cols, cols), cols)
        mix = mix_ref[start, :].reshape(groups, 8, LANES)
        total = jnp.zeros((groups, 8, LANES), F32)
        for i in range(KERN):
            row = row_taps[r, i + 1]
            same = jnp.where(row < KERN, 1.0, 0.0).astype(F32)
            for b in range(KERN):
                x = shifted[b, r + i]
                total = total + wide[row * KERN + b][None] * x
                dk[i * KERN + b] += jnp.sum(mix * x, axis=0) * same
        out_ref[start, :] = total.reshape(cols, LANES)
        return 0

    lax.fori_loop(0, rows, one, 0)
    for t in range(TAPS):
        dk_ref[TAPS - 1 - t : TAPS - t, :] = jnp.sum(dk[t], axis=0, keepdims=True) * SPREAD
    dk_ref[TAPS:, :] = jnp.zeros((dk_ref.shape[0] - TAPS, LANES), F32)


def share(core, first, second, kept_ref, sent_ref, z, p):
    mine = core == 0
    tall, width = first.shape
    for ref, chunk in (
        (kept_ref, jnp.where(mine, first, second)),
        (sent_ref, jnp.where(mine, second, first)),
    ):
        for k in range(lane_blocks(width)):
            part = chunk[:, k * LANES : (k + 1) * LANES]
            if part.shape[1] < LANES:
                part = jnp.concatenate([part, jnp.zeros((tall, LANES - part.shape[1]), F32)], axis=1)
            ref[z, p, k * tall : (k + 1) * tall, :] = part


def share_columns(core, grad, kept_ref, sent_ref, width):
    groups, parts = kept_ref.shape[:2]
    tall = grad.shape[0] // parts
    for z in range(groups):
        for p in range(parts):
            rows = slice(p * tall, (p + 1) * tall)
            first = grad[rows, 2 * z * width : (2 * z + 1) * width]
            second = grad[rows, (2 * z + 1) * width : (2 * z + 2) * width]
            share(core, first, second, kept_ref, sent_ref, z, p)


def share_rows(core, grad, kept_ref, sent_ref, tall):
    groups, parts = kept_ref.shape[:2]
    width = grad.shape[1] // parts
    for z in range(groups):
        for p in range(parts):
            columns = slice(p * width, (p + 1) * width)
            first = grad[2 * z * tall : (2 * z + 1) * tall, columns]
            second = grad[(2 * z + 1) * tall : (2 * z + 2) * tall, columns]
            share(core, first, second, kept_ref, sent_ref, z, p)


def forward_kernel(
    place_ref, ids_scalar, one_table, two_table, ids_ref, above_ref, own_ref, below_ref, cot_ref,
    first_gain_ref, first_scale_ref, second_gain_ref, second_scale_ref,
    in_ref, kern_ref, one_ref, two_ref, three_ref, out_ref, up_ref, down_ref,
    joined_ref, output_ref, dmiddle_ref, dconv_ref, dconv_top_ref, dconv_bottom_ref,
    up_kept_ref, up_sent_ref, down_kept_ref, down_sent_ref, out_kept_ref, out_sent_ref,
    packed_kept_ref, packed_sent_ref,
    row_taps, padded, valid_ref, one_keep_ref, two_keep_ref, col_ref, packed_ref, normed, flat, shifted, laid, wide, conv, mixed_ref, mapped_ref, middle_ref, result, dnorm,
    *, rows, cols, count_ha, count_ba,
):
    step = pl.program_id(0)
    blocks = flat.shape[0]
    cells = rows * cols
    reach = REACH * cols
    cells_ext = cells + 2 * reach
    core = place_ref[0] % 2
    split = one_ref.shape[0]
    dim = own_ref.shape[1]
    head_steps = blocks // 2
    ffn_first = head_steps + blocks
    gate_refs = (one_ref, two_ref, three_ref)

    @pl.when(step == 0)
    def _():
        lay_kernel(kern_ref, laid, split)
        turned = image_ids(ids_ref, padded, place_ref[0], rows)
        spread_cells((turned >= 0).astype(F32), valid_ref, 0, rows + 2 * REACH)
        spread_cells(keep_factors(turned, one_table), one_keep_ref, REACH, rows)
        spread_cells(keep_factors(turned, two_table), two_keep_ref, REACH, rows)
        conv_masks(ids_scalar, ids_ref, place_ref[0], row_taps, col_ref, rows)
        start = 0
        for ref in (above_ref, own_ref, below_ref):
            size = ref.shape[0]
            hat, _ = normalized(ref[...] * valid_ref[start : start + size, :1])
            normed[start : start + size] = hat * first_gain_ref[...]
            start += size

    @pl.when(step < head_steps)
    def _():
        joined = dot(normed[...], in_ref[...])
        for k in range(2):
            part = joined[:, k * LANES : (k + 1) * LANES]
            block = 2 * step + k
            flat[block, :EDGE] = jnp.zeros((EDGE, LANES), F32)
            flat[block, EDGE : EDGE + cells_ext] = part
            flat[block, EDGE + cells_ext :] = jnp.zeros((EDGE, LANES), F32)
            joined_ref[k] = part[reach : reach + cells]

    @pl.when((step >= head_steps) & (step < ffn_first))
    def _():
        block = step - head_steps
        fill_shifted(flat.at[block], col_ref, shifted, rows + 2 * REACH, cols)
        conv_block(row_taps, laid[block], shifted, wide, conv.at[block], rows, cols)

    def conv_part(start, width):
        return jnp.concatenate([conv[start // LANES + k] for k in range(width // LANES)], axis=1)

    @pl.when(step == ffn_first)
    def _():
        mixed = conv[0, :, :split] * conv[0, :, split:]
        mixed_ref[:, :split] = mixed
        start = 2 * split
        for ref in gate_refs:
            width = ref.shape[1]
            mapped = dot(mixed, ref[...])
            mapped_ref[:, start - 2 * split : start - 2 * split + width] = mapped
            mixed = mapped * conv_part(start, width)
            mixed_ref[:, start : start + width] = mixed
            start += width
        branch = dot(mixed, out_ref[...])
        masked = own_ref[...] * valid_ref[reach : reach + cells, :1]
        middle = masked + one_keep_ref[:, :1] * first_scale_ref[...] * branch
        middle_ref[...] = middle
        hat, _ = normalized(middle)
        normed[:cells] = hat * second_gain_ref[...]
        normed[cells : cells + reach] = jnp.zeros((reach, dim), F32)
        result[...] = jnp.zeros_like(result)
        dnorm[...] = jnp.zeros_like(dnorm)

    @pl.when(step >= ffn_first)
    def _():
        grad_result = two_keep_ref[:, :1] * second_scale_ref[...] * cot_ref[...]
        pre = dot(normed[:cells], up_ref[...])
        cdf = 0.5 + 0.5 * lax.erf(pre * INV_SQRT_2)
        slope = cdf + pre * (INV_SQRT_2PI * jnp.exp(-0.5 * pre * pre))
        hidden = pre * cdf
        result[...] += dot(hidden, down_ref[...])
        grad_pre = dot(grad_result, down_ref[...], NT) * slope
        share_rows(core, dot(grad_result, hidden, TN), down_kept_ref, down_sent_ref, dim // count_ha)
        width = down_ref.shape[0] // (2 * up_kept_ref.shape[0])
        share_columns(core, dot(normed[:cells], grad_pre, TN), up_kept_ref, up_sent_ref, width)
        dnorm[...] += dot(grad_pre, up_ref[...], NT)

    @pl.when(step == pl.num_programs(0) - 1)
    def _():
        hat, scale = normalized(middle_ref[...])
        kept = two_keep_ref[:, :1] * result[...]
        output_ref[...] = middle_ref[...] + second_scale_ref[...] * kept
        dscale_two = jnp.sum(cot_ref[...] * kept, axis=0, keepdims=True)
        dgain_two = jnp.sum(dnorm[...] * hat, axis=0, keepdims=True)
        dmiddle = cot_ref[...] + norm_backward(dnorm[...] * second_gain_ref[...], hat, scale)
        dmiddle_ref[...] = dmiddle
        kept = one_keep_ref[:, :1] * dmiddle
        start = mixed_ref.shape[1] - out_ref.shape[0]
        crossed = dot(mixed_ref[:, start:], kept, TN)
        dscale_one = jnp.sum(crossed * out_ref[...], axis=0, keepdims=True)
        share_rows(core, (crossed * first_scale_ref[...]).T, out_kept_ref, out_sent_ref, dim // count_ha)
        grad = dot(kept * first_scale_ref[...], out_ref[...], NT)
        row = packed_ref.shape[0]
        start = blocks * LANES
        for ref in reversed(gate_refs):
            tall, width = ref.shape
            start -= width
            source = start - tall if tall > split else 0
            columns = slice(start - 2 * split, start - 2 * split + width)
            dconv = grad * mapped_ref[:, columns]
            for k in range(width // LANES):
                dconv_ref[start // LANES + k] = dconv[:, k * LANES : (k + 1) * LANES]
            grad_mapped = grad * conv_part(start, width)
            part = dot(mixed_ref[:, source : source + tall], grad_mapped, TN)
            row -= tall * width // LANES
            for k in range(width // LANES):
                packed_ref[row + k * tall : row + (k + 1) * tall] = part[:, k * LANES : (k + 1) * LANES]
            grad = dot(grad_mapped, ref[...], NT)
        dconv_ref[0] = jnp.concatenate([grad * conv[0, :, split:], grad * conv[0, :, :split]], axis=1)
        packed_ref[:row] = jnp.zeros((row, LANES), F32)
        row = 0
        for vector in (dscale_one, dgain_two, dscale_two):
            for k in range(dim // LANES):
                packed_ref[row : row + 1] = vector[:, k * LANES : (k + 1) * LANES]
                row += 1
        half = packed_kept_ref.shape[0]
        packed_kept_ref[...] = packed_ref[pl.ds(pl.multiple_of(core * half, 8), half), :]
        packed_sent_ref[...] = packed_ref[pl.ds(pl.multiple_of((1 - core) * half, 8), half), :]
        dconv_top_ref[...] = dconv_ref[:, :reach, :]
        dconv_bottom_ref[...] = dconv_ref[:, cells - reach :, :]


def mask_scratch(ids, rows):
    height, cols = ids.shape
    return [
        pltpu.SMEM((rows, KERN + 2), jnp.int32),
        pltpu.VMEM((height + 2 * EDGE, cols), jnp.int32),
        pltpu.VMEM(((rows + 2 * REACH) * cols, LANES), F32),
    ]


def packed_rows(gates, dim):
    rows = sum(gate.size for gate in gates) // LANES + 3 * dim // LANES
    return -(-rows // 16) * 16


def forward(
    place, ids, keep_one, keep_two, above, own, below, cot, vectors, weight_in, kern, gates,
    weight_out, weight_up, weight_down, rows, cols, count_ha, count_ba, chunk=512,
):
    cells, dim = own.shape
    reach = above.shape[0]
    blocks = weight_in.shape[1] // LANES
    hidden = weight_up.shape[1]
    split = gates[0].shape[0]
    wide = blocks * LANES
    head_steps = blocks // 2
    ffn_first = head_steps + blocks
    ffn_steps = hidden // chunk

    def ffn_step(i):
        return jnp.clip(i - ffn_first, 0, ffn_steps - 1)

    up_wide, down_wide = hidden // count_ha, hidden // count_ba
    up_rows = dim // count_ba * lane_blocks(up_wide)
    down_rows = dim // count_ha * lane_blocks(down_wide)
    out_rows = dim // count_ha * lane_blocks(dim // count_ba)
    half = count_ha // 2
    up_spec = pl.BlockSpec((chunk // (2 * up_wide), count_ba, up_rows, LANES), lambda i: (ffn_step(i), 0, 0, 0))
    down_spec = pl.BlockSpec((half, chunk // down_wide, down_rows, LANES), lambda i: (0, ffn_step(i), 0, 0))
    out_shape = (half, count_ba, out_rows, LANES)
    packed_shape = (packed_rows(gates, dim), LANES)
    half_packed = (packed_shape[0] // 2, LANES)
    cells_ext = cells + 2 * reach
    return pl.pallas_call(
        functools.partial(forward_kernel, rows=rows, cols=cols, count_ha=count_ha, count_ba=count_ba),
        grid=(ffn_first + ffn_steps,),
        in_specs=[in_smem()] * 4
        + [whole(x.shape) for x in (ids, above, own, below, cot)]
        + [whole((1, dim))] * 4
        + [
            pl.BlockSpec((dim, 2 * LANES), lambda i: (0, jnp.minimum(i, head_steps - 1))),
            whole(kern.shape),
        ]
        + [whole(gate.shape) for gate in gates]
        + [
            whole(weight_out.shape),
            pl.BlockSpec((dim, chunk), lambda i: (0, ffn_step(i))),
            pl.BlockSpec((chunk, dim), lambda i: (ffn_step(i), 0)),
        ],
        out_specs=[
            pl.BlockSpec((2, cells, LANES), lambda i: (jnp.minimum(i, head_steps - 1), 0, 0)),
            whole((cells, dim)),
            whole((cells, dim)),
            whole((blocks, cells, LANES)),
            whole((blocks, reach, LANES)),
            whole((blocks, reach, LANES)),
            up_spec,
            up_spec,
            down_spec,
            down_spec,
            whole(out_shape),
            whole(out_shape),
            whole(half_packed),
            whole(half_packed),
        ],
        out_shape=[
            shape_of(blocks, cells, LANES),
            shape_of(cells, dim),
            shape_of(cells, dim),
            shape_of(blocks, cells, LANES),
            shape_of(blocks, reach, LANES),
            shape_of(blocks, reach, LANES),
            shape_of(half, count_ba, up_rows, LANES),
            shape_of(half, count_ba, up_rows, LANES),
            shape_of(half, count_ba, down_rows, LANES),
            shape_of(half, count_ba, down_rows, LANES),
            shape_of(*out_shape),
            shape_of(*out_shape),
            shape_of(*half_packed),
            shape_of(*half_packed),
        ],
        scratch_shapes=mask_scratch(ids, rows)
        + [
            pltpu.VMEM((cells, LANES), F32),
            pltpu.VMEM((cells, LANES), F32),
            pltpu.VMEM((KERN, cols // 8, 8, LANES), F32),
            pltpu.VMEM(packed_shape, F32),
            pltpu.VMEM((cells_ext, dim), F32),
            pltpu.VMEM((blocks, cells_ext + 2 * EDGE, LANES), F32),
            pltpu.VMEM((KERN, rows + 2 * REACH, cols // 8, 8, LANES), F32),
            pltpu.VMEM((blocks, TAPS, LANES), F32),
            pltpu.VMEM((TAPS + KERN, 8, LANES), F32),
            pltpu.VMEM((blocks, cells, LANES), F32),
            pltpu.VMEM((cells, wide), F32),
            pltpu.VMEM((cells, wide - 2 * split), F32),
            pltpu.VMEM((cells, dim), F32),
            pltpu.VMEM((cells, dim), F32),
            pltpu.VMEM((cells, dim), F32),
        ],
        compiler_params=params(),
        cost_estimate=lasting(55),
    )(
        place, ids, keep_one, keep_two, ids, above, own, below, cot, *vectors,
        weight_in, kern, *gates, weight_out, weight_up, weight_down,
    )


def backward_kernel(
    place_ref, ids_scalar, ids_ref, above_ref, own_ref, below_ref, mix_ref, kern_ref, canvas_ref, gain_ref,
    dmiddle_ref, before_ref, in_ref, *rest, rows, cols, first_block, last,
):
    total_ref, kept_ref, sent_ref, dk_ref = rest[-16:-12]
    row_taps, padded, valid_ref, col_ref, flat, shifted, laid, wide, dk, djoined, normed, dnorm = rest[-12:]
    step = pl.program_id(0)
    block = first_block + step
    cells = rows * cols
    reach = REACH * cols
    core = place_ref[0] % 2
    split = laid.shape[0] * LANES - kern_ref.shape[1]
    width = in_ref.shape[1] // (2 * kept_ref.shape[0])

    @pl.when(step == 0)
    def _():
        lay_kernel(kern_ref, laid, split)
        turned = image_ids(ids_ref, padded, place_ref[0], rows)
        spread_cells((turned >= 0).astype(F32), valid_ref, 0, rows + 2 * REACH)
        conv_masks(ids_scalar, ids_ref, place_ref[0], row_taps, col_ref, rows)
        hat, _ = normalized(canvas_ref[...] * valid_ref[reach : reach + cells, :1])
        normed[...] = hat * gain_ref[...]
        dnorm[...] = before_ref[...] if first_block else jnp.zeros_like(dnorm)

    flat[:EDGE] = jnp.zeros((EDGE, LANES), F32)
    flat[EDGE : EDGE + reach] = above_ref[0]
    flat[EDGE + reach : EDGE + reach + cells] = own_ref[0]
    flat[EDGE + reach + cells : EDGE + 2 * reach + cells] = below_ref[0]
    flat[EDGE + 2 * reach + cells :] = jnp.zeros((EDGE, LANES), F32)
    fill_shifted(flat, col_ref, shifted, rows + 2 * REACH, cols)
    conv_grad_block(
        row_taps, laid[block], shifted, wide, dk, mix_ref.at[0], djoined.at[step % 2], dk_ref.at[0], rows, cols
    )

    @pl.when(step % 2 == 1)
    def _():
        grad = jnp.concatenate([djoined[0], djoined[1]], axis=1)
        share_columns(core, dot(normed[...], grad, TN), kept_ref, sent_ref, width)
        dnorm[...] += dot(grad, in_ref[...], NT)

    @pl.when(step == pl.num_programs(0) - 1)
    def _():
        if not last:
            total_ref[...] = dnorm[...]
            return
        hat, scale = normalized(canvas_ref[...] * valid_ref[reach : reach + cells, :1])
        dgain = jnp.sum(dnorm[...] * hat, axis=0, keepdims=True)
        for k in range(dgain.shape[1] // LANES):
            dk_ref[0, TAPS + k : TAPS + k + 1] = dgain[:, k * LANES : (k + 1) * LANES]
        inner = dmiddle_ref[...] + norm_backward(dnorm[...] * gain_ref[...], hat, scale)
        total_ref[...] = inner * valid_ref[reach : reach + cells, :1]


def backward(
    place, ids, above, own, below, mix, kern, canvas, gain, dmiddle, before, weight_in,
    first_block, end_block, written, ties, rows, cols, count_ha, count_ba,
):
    cells, dim = canvas.shape
    blocks = own.shape[0]
    reach = above.shape[1]
    steps = end_block - first_block
    own_wide = weight_in.shape[1] // count_ha
    chunk_rows = dim // count_ba * lane_blocks(own_wide)
    groups = 2 * LANES // (2 * own_wide)
    tall = -(-(TAPS + dim // LANES) // 8) * 8

    def block_of(size):
        return pl.BlockSpec((1, size, LANES), lambda i: (first_block + i, 0, 0))

    chunk_spec = pl.BlockSpec((groups, count_ba, chunk_rows, LANES), lambda i: (first_block // 2 + i // 2, 0, 0, 0))
    chunks = shape_of(count_ha // 2, count_ba, chunk_rows, LANES)
    fixed = 13
    return pl.pallas_call(
        functools.partial(
            backward_kernel, rows=rows, cols=cols, first_block=first_block, last=end_block == blocks
        ),
        grid=(steps,),
        in_specs=[in_smem(), in_smem(), whole(ids.shape)]
        + [block_of(size) for size in (reach, cells, reach, cells)]
        + [whole(kern.shape), whole(canvas.shape)]
        + [whole((1, dim)), whole((cells, dim)), whole((cells, dim))]
        + [pl.BlockSpec((dim, 2 * LANES), lambda i: (0, first_block // 2 + i // 2))]
        + [anywhere()] * (len(written) + len(ties)),
        out_specs=[whole((cells, dim)), chunk_spec, chunk_spec, block_of(tall)],
        out_shape=[shape_of(cells, dim), chunks, chunks, shape_of(blocks, tall, LANES)],
        input_output_aliases={fixed + k: 1 + k for k in range(len(written))},
        scratch_shapes=mask_scratch(ids, rows)
        + [
            pltpu.VMEM((KERN, cols // 8, 8, LANES), F32),
            pltpu.VMEM((cells + 2 * reach + 2 * EDGE, LANES), F32),
            pltpu.VMEM((KERN, rows + 2 * REACH, cols // 8, 8, LANES), F32),
            pltpu.VMEM((blocks, TAPS, LANES), F32),
            pltpu.VMEM((TAPS + KERN, 8, LANES), F32),
            pltpu.VMEM((TAPS, 8, LANES), F32),
            pltpu.VMEM((2, cells, LANES), F32),
            pltpu.VMEM((cells, dim), F32),
            pltpu.VMEM((cells, dim), F32),
        ],
        compiler_params=params(),
        cost_estimate=lasting(4 * steps),
    )(
        place, ids, ids, above, own, below, mix, kern, canvas, gain, dmiddle, before, weight_in,
        *written, *ties,
    )


def unpack_kernel(packed_ref, dkern_ref, *outs, dim):
    row = 0
    for ref in outs[:3]:
        for k in range(dim // LANES):
            ref[:, k * LANES : (k + 1) * LANES] = packed_ref[row : row + 1]
            row += 1
    row = packed_ref.shape[0]
    for ref in reversed(outs[3:6]):
        tall, width = ref.shape
        row -= tall * width // LANES
        for k in range(width // LANES):
            ref[:, k * LANES : (k + 1) * LANES] = packed_ref[row + k * tall : row + (k + 1) * tall]
    dk_ref, gain_ref = outs[6:]
    joined = jnp.concatenate([dkern_ref[k, :TAPS] for k in range(dkern_ref.shape[0])], axis=1)
    dk_ref[...] = joined[:, joined.shape[1] - dk_ref.shape[1] :]
    for k in range(dim // LANES):
        gain_ref[:, k * LANES : (k + 1) * LANES] = dkern_ref[dkern_ref.shape[0] - 1, TAPS + k : TAPS + k + 1]


def unpack(packed, dkern, gates, kern, dim):
    return pl.pallas_call(
        functools.partial(unpack_kernel, dim=dim),
        out_shape=[shape_of(1, dim)] * 3
        + [shape_of(*gate.shape) for gate in gates]
        + [shape_of(*kern.shape), shape_of(1, dim)],
        compiler_params=params(),
        cost_estimate=lasting(2),
    )(packed, dkern)


def exchange(values, axis, bit):
    return lax.ppermute(values, axis, [(i, i ^ bit) for i in range(lax.axis_size(axis))])


def picked(parts, index, axis):
    return [lax.dynamic_index_in_dim(part, index, axis, keepdims=False) for part in parts]


def total(parts):
    result = parts[0]
    for part in parts[1:]:
        result = result + part
    return result


def along(way):
    return lax.axis_index("ha") // 2 if way == "z" else (lax.axis_index("ba") >> way) & 1


class Sum:
    def __init__(self, parts):
        bits = lax.axis_size("ba").bit_length() - 1
        self.parts = [part.reshape(part.shape[:1] + (2,) * bits + part.shape[2:]) for part in parts]
        self.ways = ["z"] + list(reversed(range(bits)))

    def leaving(self, way, step):
        return total(picked(self.parts, along(way) ^ step, self.ways.index(way)))

    def keep(self, way, got):
        self.parts = picked(self.parts, along(way), self.ways.index(way)) + got
        self.ways.remove(way)

    def result(self):
        return total(self.parts)


class Stage:
    def __init__(self, sums, way, riders=()):
        self.sums, self.way, self.riders = sums, way, list(riders)
        self.steps = range(1, lax.axis_size("ha") // 2) if way == "z" else [1]
        self.shapes, self.leaving = [], []
        for step in self.steps:
            leaving = [one.leaving(way, step) for one in sums]
            self.shapes = [part.shape for part in leaving]
            flat = [part.reshape(-1, LANES) for part in leaving] + self.riders
            self.leaving.append(flat[0] if len(flat) == 1 else jnp.concatenate(flat, axis=0))

    def go(self):
        axis, unit = ("ha", 2) if self.way == "z" else ("ba", 1 << self.way)
        arrived = [exchange(part, axis, unit * step) for step, part in zip(self.steps, self.leaving)]
        row = 0
        for one, shape in zip(self.sums, self.shapes):
            rows = 1
            for size in shape[:-1]:
                rows *= size
            one.keep(self.way, [part[row : row + rows].reshape(shape) for part in arrived])
            row += rows
        for k, rider in enumerate(self.riders):
            self.riders[k] = total([rider] + [part[row : row + rider.shape[0]] for part in arrived])
            row += rider.shape[0]
        return self.riders


def half_of(rows):
    core = lax.axis_index("ha") % 2
    both = rows.reshape(2, rows.shape[0] // 2, rows.shape[1])
    return total(picked([both], core, 0) + [exchange(picked([both], 1 - core, 0)[0], "ha", 1)])


def with_other_half(mine):
    core = lax.axis_index("ha") % 2
    other = exchange(mine, "ha", 1)
    return jnp.concatenate([jnp.where(core == 0, mine, other), jnp.where(core == 0, other, mine)], axis=0)


def beside(rows, tall, width):
    parts = [rows[k * tall : (k + 1) * tall] for k in range(lane_blocks(width))]
    return jnp.concatenate(parts, axis=1)[:, :width]


def neighbour_rows(top, bottom):
    count = lax.axis_size("ha")
    up = [(i, i + 1) for i in range(count - 1)]
    down = [(i + 1, i) for i in range(count - 1)]
    return lax.ppermute(bottom, "ha", up), lax.ppermute(top, "ha", down)


def after(values, token):
    return values + 0.0 * token[0, 0]


def shards(
    canvas,
    image_id,
    keep_first,
    keep_second,
    first_gain,
    weight_in,
    depth_kernel,
    gate_first,
    gate_second,
    gate_third,
    weight_out,
    scale_first,
    second_gain,
    weight_up,
    weight_down,
    scale_second,
    cotangent,
):
    _, rows, cols, dim = canvas.shape
    cells = rows * cols
    reach = REACH * cols
    count_ha, count_ba = lax.axis_size("ha"), lax.axis_size("ba")
    hidden = weight_up.shape[1]
    blocks = weight_in.shape[1] // LANES
    place = lax.axis_index("ha")[None]
    own = canvas.reshape(cells, dim)
    gates = (gate_first, gate_second, gate_third)
    gain = first_gain[None]
    vectors = (gain, scale_first[None], second_gain[None], scale_second[None])
    order = list(range(count_ba.bit_length() - 1))
    turned = order[len(order) // 2 :] + order[: len(order) // 2]

    ids = image_id[0]
    above, below = neighbour_rows(own[:reach], own[cells - reach :])
    (
        joined, output, dmiddle, dconv, dconv_top, dconv_bottom, up_kept, up_sent, down_kept, down_sent,
        out_kept, out_sent, packed_kept, packed_sent,
    ) = forward(
        place, ids, keep_first, keep_second, above, own, below, cotangent.reshape(cells, dim), vectors,
        weight_in, depth_kernel, gates, weight_out, weight_up, weight_down, rows, cols, count_ha, count_ba,
    )
    above, below = neighbour_rows(dconv_top, dconv_bottom)

    def back(first_block, end_block, before, written, ties):
        return backward(
            place, ids, above, dconv, below, joined, depth_kernel, own, gain, dmiddle, before,
            weight_in, first_block, end_block, written, ties, rows, cols, count_ha, count_ba,
        )

    up = Sum([up_kept, exchange(up_sent, "ha", 1)])
    down = Sum([down_kept, exchange(down_sent, "ha", 1)])
    out = Sum([out_kept, exchange(out_sent, "ha", 1)])
    packed = packed_kept + exchange(packed_sent, "ha", 1)
    stages = [Stage([up], order[0]), Stage([down, out], turned[0])]
    cut = blocks * 3 // 4
    dnorm, *written = back(0, cut, dmiddle, [], stages[0].leaving + stages[1].leaving)
    for stage in stages:
        stage.go()
    z_steps = [2 << k for k in range((count_ha // 2).bit_length() - 1)]
    packed = after(packed + exchange(packed, "ha", z_steps[0]), dnorm)
    stages = [Stage([up], order[1]), Stage([down, out], turned[1])]
    dcanvas, in_kept, in_sent, dkern = back(
        cut, blocks, dnorm, written, stages[0].leaving + stages[1].leaving + [packed]
    )
    for stage in stages:
        stage.go()
    for step in z_steps[1:]:
        packed = after(packed + exchange(packed, "ha", step), dcanvas)
    for first, second in zip(order[2:], turned[2:]):
        Stage([up], first).go()
        Stage([down, out], second).go()
    Stage([up, down, out], "z").go()
    parts = [in_kept, exchange(in_sent, "ha", 1)]
    middle_row = in_kept.shape[2] // 2
    in_first = Sum([part[:, :, :middle_row] for part in parts])
    in_second = Sum([part[:, :, middle_row:] for part in parts])
    small = half_of(dkern.reshape(-1, LANES))
    for first, second in zip(order, turned):
        (small,) = Stage([in_first], first, [small]).go()
        (packed,) = Stage([in_second], second, [packed]).go()
    sums = [after(one.result(), small) for one in (up, down, out)]
    (small,) = Stage([in_first, in_second], "z", [small]).go()
    din = jnp.concatenate([in_first.result(), in_second.result()], axis=0)
    dup, ddown, dout = sums
    dscale_one, dgain_two, dscale_two, dfirst, dsecond, dthird, dkern, dgain_one = unpack(
        with_other_half(packed), with_other_half(small).reshape(dkern.shape), gates, depth_kernel, dim
    )
    return (
        output.reshape(canvas.shape),
        dcanvas.reshape(canvas.shape),
        dgain_one[0],
        beside(din, dim // count_ba, weight_in.shape[1] // count_ha),
        dkern,
        dfirst,
        dsecond,
        dthird,
        beside(dout, dim // count_ha, dim // count_ba).T,
        dscale_one[0],
        dgain_two[0],
        beside(dup, dim // count_ba, hidden // count_ha),
        beside(ddown, dim // count_ha, hidden // count_ba).T,
        dscale_two[0],
    )


def solution(mesh):
    in_specs = (
        P("ba", "ha", None, None),
        P("ba", None, None),
        P("ba", None),
        P("ba", None),
    ) + (P(),) * 12 + (P("ba", "ha", None, None),)
    tiled = P("ba", "ha")
    out_specs = (
        P("ba", "ha", None, None),
        P("ba", "ha", None, None),
        P(),
        tiled,
        P(),
        P(),
        P(),
        P(),
        tiled,
        P(),
        P(),
        tiled,
        tiled,
        P(),
    )
    return jax.shard_map(shards, mesh=mesh, in_specs=in_specs, out_specs=out_specs, check_vma=False)
```

time: 271 us -> 213 us (0.79)
  waiting for transfers between devices: 96.2 us -> 38.4 us
  starting transfers between devices: 53.9 us -> 41.1 us
  other arithmetic: 17.1 us -> 25.1 us
    ppermute x38 -> x24, waiting for transfers between devices: 96.2 us -> 33.9 us  [exchange(): lax.ppermute(values, axis, [(i, i ^ bit) for i in range(lax.axis_size(axi...]
    ppermute x38 -> x24, starting transfers between devices: 46.2 us -> 32.9 us  [exchange(): lax.ppermute(values, axis, [(i, i ^ bit) for i in range(lax.axis_size(axi...]
    slice x4 -> x14, local copies, waits for them, and re-layouts: 1.48 us -> 9.75 us  [the longest x8 4.31 us: go(): part[row:row + rows].reshape(shape)]
    unnamed x47 -> x16, local copies, waits for them, and re-layouts: 6.57 us -> 0.79 us
    ppermute x4, waiting for transfers between devices: 0.01 us -> 4.47 us  [neighbour_rows(): return (lax.ppermute(bottom, 'ha', up), lax.ppermute(top, 'ha', down))]
    concatenate x12 -> x13, other arithmetic: 0.87 us -> 4.51 us  [the longest x10 2.25 us: __init__(): jnp.concatenate(flat, axis=0)]
    add x12 -> x4, other arithmetic: 1.24 us -> 4.36 us  [the longest x3 3.33 us: after(): return values + 0.0 * token[0, 0]]
    add x20 -> x27, other arithmetic: 12.2 us -> 13.3 us  [total(): result = result + part]
  transfers between devices with their start and end apart: 42 -> 28, of which waited for: 21 -> 10; matrix products, arithmetic and copies ran while one was open for 6% -> 16% of each run, Pallas kernels for 9% -> 16%
where the time goes in v3:
time: 213 us; the launch traced here: 212 us
  Pallas kernels  92.5 us (43%)
  starting transfers between devices  41.1 us (19%)
  waiting for transfers between devices  38.4 us (18%)
  other arithmetic  25.1 us (12%)
  local copies, waits for them, and re-layouts  11.8 us (6%)
  between operations  3.09 us (1%)
    pallas_call x1, Pallas kernels, forward(): pl.pallas_call(functools.partial(forward_kernel, rows=rows, cols=cols, co...  56.1 us
    pallas_call x2, Pallas kernels, backward(): pl.pallas_call(functools.partial(backward_kernel, rows=rows, cols=cols, f...  34.3 us
    ppermute x24, waiting for transfers between devices, exchange(): lax.ppermute(values, axis, [(i, i ^ bit) for i in range(lax.axis_size(axi...  33.9 us
    ppermute x24, starting transfers between devices, exchange(): lax.ppermute(values, axis, [(i, i ^ bit) for i in range(lax.axis_size(axi...  32.9 us
    add x27, other arithmetic, total(): result = result + part  13.3 us
    ppermute x4, starting transfers between devices, neighbour_rows(): return (lax.ppermute(bottom, 'ha', up), lax.ppermute(top, 'ha', down))  8.18 us
    ppermute x4, waiting for transfers between devices, neighbour_rows(): return (lax.ppermute(bottom, 'ha', up), lax.ppermute(top, 'ha', down))  4.47 us
    slice x8, local copies, waits for them, and re-layouts, go(): part[row:row + rows].reshape(shape)  4.31 us
  transfers between devices with their start and end apart: 28, of which 10 were waited for; matrix products, arithmetic and copies ran while one was open for 16% of the time, Pallas kernels for 16%

profile of v3, /device:TPU:0, one launch (start us, length us, event | category | flops | bytes accessed | tf_op | source)
XLA Modules:
  0.0 211.9 jit_solution(13330916468144873108)
XLA Ops:
  0.6 1.2 fusion.6
  1.8 2.4 %collective-permute-start = (f32[192,512]{1,0:T(8,128)S(1)}, f32[192,512]{1,0:T(8,128)S(1)}, u32[]{:S(2)}, u32[]{:S(2)}) collective-permute-start(f32[192,512]{1,0:T(8,128)S(1)} %bitcast.310), channel_id=1, source_target_pairs={{0,4},{4,8},{8,12},{12,16},{16,20},{20,24},{24,28},{1,5},{5,9},{9,... | collective-permute-start | bytes 1179656 | tf_op jit(solution)/shard_map/ppermute | solution.py:708
  4.2 1.3 collective-permute-start.1
  5.5 4.5 %collective-permute-done.1.below_ref = f32[192,512]{1,0:T(8,128)S(1)} collective-permute-done((f32[192,512]{1,0:T(8,128)S(1)}, f32[192,512]{1,0:T(8,128)S(1)}, u32[]{:S(2)}, u32[]{:S(2)}) %collective-permute-start.1) | collective-permute-done | bytes 393248 | tf_op jit(solution)/shard_map/ppermute | solution.py:708
  10.8 56.1 %shard_map.272 = (f32[8,512,128]{2,1,0:T(8,128)}, f32[512,512]{1,0:T(8,128)}, f32[512,512]{1,0:T(8,128)}, f32[8,512,128]{2,1,0:T(8,128)}, f32[8,192,128]{2,1,0:T...) custom-call(s32[1]{0:T(128)} %bitcast.place_ref, ...), custom_call_target="tpu_custom_call" | custom-call | flops 60500000768 | tf_op jit(solution)/shard_map/pallas_call | solution.py:414
  66.9 6.1 %collective-permute-start.4 = (f32[4,4,256,128]{3,2,1,0:T(8,128)}, f32[4,4,256,128]{3,2,1,0:T(8,128)}, u32[]{:S(2)}, u32[]{:S(2)}) collective-permute-start(f32[4,4,256,128]{3,2,1,0:T(8,128)} %get-tuple-element.51), channel_id=1, source_target_pairs={{0,4},{4,0},{8,12},{12,8},{16,20},{20,16},{24,28},{28,24},{1,5},{5... | collective-permute-start | bytes 6291464 | tf_op jit(solution)/shard_map/ppermute | solution.py:625
  73.5 3.2 %collective-permute-start.2 = (f32[8,192,128]{2,1,0:T(8,128)}, f32[8,192,128]{2,1,0:T(8,128)}, u32[]{:S(2)}, u32[]{:S(2)}) collective-permute-start(f32[8,192,128]{2,1,0:T(8,128)} %get-tuple-element.45), channel_id=1, source_target_pairs={{0,4},{4,8},{8,12},{12,16},{16,20},{20,24},{24,28},{1,5},{5,9},{9,... | collective-permute-start | bytes 2359304 | tf_op jit(solution)/shard_map/ppermute | solution.py:708
  76.8 2.7 %collective-permute-done.9 = f32[680,128]{1,0:T(8,128)S(1)} collective-permute-done((f32[680,128]{1,0:T(8,128)}, f32[680,128]{1,0:T(8,128)S(1)}, u32[]{:S(2)}, u32[]{:S(2)}) %collective-permute-start.9) | collective-permute-done | bytes 348192 | tf_op jit(solution)/shard_map/ppermute | solution.py:625
  79.4 1.3 collective-permute-start.3
  80.7 1.0 add.1004
  81.8 2.7 %collective-permute-start.10 = (f32[680,128]{1,0:T(8,128)S(1)}, f32[680,128]{1,0:T(8,128)}, u32[]{:S(2)}, u32[]{:S(2)}) collective-permute-start(f32[680,128]{1,0:T(8,128)S(1)} %add.1004), channel_id=1, source_target_pairs={{0,8},{4,12},{8,0},{12,4},{16,24},{20,28},{24,16},{28,20},{1,9},{5... | collective-permute-start | bytes 1044488 | tf_op jit(solution)/shard_map/ppermute | solution.py:625
  84.5 1.1 dynamic-slice_add_fusion.9
  85.5 1.0 dynamic-slice_add_fusion.6
  86.6 2.3 %dynamic-slice_add_fusion.1 = f32[4,2,1,256,128]{4,3,2,1,0:T(8,128)} fusion(f32[4,2,2,256,128]{4,3,2,1,0:T(8,128)} %bitcast.12, s32[]{:T(128)S(6)} %select_n.235, f32[4,2,2,256,128]{4,3,2,1,0:T(8,128)S(1)} %bitcast.257), kind=kLoop, calls=%fused_computation.2 | loop fusion | flops 262144 | bytes 3145732 | tf_op jit(solution)/shard_map/add | solution.py:635
  88.9 1.5 collective-permute-start.7
  90.4 1.3 dynamic-slice_add_fusion
  91.7 1.1 pad_maximum_fusion.rest_1_
  92.8 1.5 collective-permute-start.8
  94.4 22.7 %shard_map.273 = (f32[512,512]{1,0:T(8,128)}, f32[4,4,128,128]{3,2,1,0:T(8,128)}, f32[4,4,128,128]{3,2,1,0:T(8,128)}, f32[8,56,128]{2,1,0:T(8,128)}) custom-call(s32[1]{0:T(128)} %bitcast.place_ref, s32[64,64]{1,0:T(8,128)} %bitcast.317, s32[64,64]{1,0:T(8,128)} %bitcast.318, f32[8,192,128]{2,1,0:T(8,128)} %collective-permute-done.2.above_ref, ...), custom_call_target="tpu_custom_call" | custom-call | flops 26400000000 | tf_op jit(solution)/shard_map/pallas_call | solution.py:560
  117.1 1.2 slice.149
  119.0 1.0 add_add_fusion.1.rest_5_
  120.0 2.6 %collective-permute-start.11 = (f32[680,128]{1,0:T(8,128)S(1)}, f32[680,128]{1,0:T(8,128)}, u32[]{:S(2)}, u32[]{:S(2)}) collective-permute-start(f32[680,128]{1,0:T(8,128)S(1)} %add_add_fusion.1.rest_5_), channel_id=1, source_target_pairs={{0,16},{4,20},{8,24},{12,28},{16,0},{20,4},{24,8},{28,12},{1,17},{... | collective-permute-start | bytes 1044488 | tf_op jit(solution)/shard_map/ppermute | solution.py:625
  122.6 1.3 dynamic-slice_add_fusion.2
  123.9 1.3 dynamic-slice_add_fusion.3
  125.2 1.1 constant_dynamic-slice_fusion.4
  128.6 1.3 slice.190
  131.5 11.5 %shard_map.274 = (f32[512,512]{1,0:T(8,128)}, f32[4,4,128,128]{3,2,1,0:T(8,128)}, f32[4,4,128,128]{3,2,1,0:T(8,128)}, f32[8,56,128]{2,1,0:T(8,128)}) custom-call(s32[1]{0:T(128)} %bitcast.place_ref, s32[64,64]{1,0:T(8,128)} %bitcast.319, s32[64,64]{1,0:T(8,128)} %bitcast.320, ...), custom_call_target="tpu_custom_call", output_to_operand_aliasing={{1}: (13, {}), {2}: (14, {}), {3}: (15, {})} | custom-call | flops 8800000000 | tf_op jit(solution)/shard_map/pallas_call | solution.py:560
  143.0 4.2 %collective-permute-start.12 = (f32[4,4,128,128]{3,2,1,0:T(8,128)}, f32[4,4,128,128]{3,2,1,0:T(8,128)S(1)}, u32[]{:S(2)}, u32[]{:S(2)}) collective-permute-start(f32[4,4,128,128]{3,2,1,0:T(8,128)} %get-tuple-element.64), channel_id=1, source_target_pairs={{0,4},{4,0},{8,12},{12,8},{16,20},{20,16},{24,28},{28,24},{1,5},{5... | collective-permute-start | bytes 3145736 | tf_op jit(solution)/shard_map/ppermute | solution.py:625
  147.3 1.3 fusion.4
  148.6 1.2 slice.150
  150.7 1.0 add_add_fusion
  151.9 1.5 bitcast_add_fusion.17
  154.4 1.1 slice.212
  156.3 1.3 bitcast_add_fusion.15
  158.0 1.8 collective-permute-start.26
  159.8 2.5 %collective-permute-start.25 = (f32[576,128]{1,0:T(8,128)S(1)}, f32[576,128]{1,0:T(8,128)S(1)}, u32[]{:S(2)}, u32[]{:S(2)}) collective-permute-start(f32[576,128]{1,0:T(8,128)S(1)} %pad_maximum_fusion.6), channel_id=1, source_target_pairs={{0,8},{4,12},{8,0},{12,4},{16,24},{20,28},{24,16},{28,20},{1,9},{5... | collective-permute-start | bytes 884744 | tf_op jit(solution)/shard_map/ppermute | solution.py:625
  163.8 8.8 %collective-permute-done.17 = f32[736,128]{1,0:T(8,128)S(1)} collective-permute-done((f32[736,128]{1,0:T(8,128)S(1)}, f32[736,128]{1,0:T(8,128)S(1)}, u32[]{:S(2)}, u32[]{:S(2)}) %collective-permute-start.17) | collective-permute-done | bytes 376864 | tf_op jit(solution)/shard_map/ppermute | solution.py:625
  173.3 6.6 %collective-permute-done.13 = f32[1192,128]{1,0:T(8,128)S(1)} collective-permute-done((f32[1192,128]{1,0:T(8,128)S(1)}, f32[1192,128]{1,0:T(8,128)S(1)}, u32[]{:S(2)}, u32[]{:S(2)}) %collective-permute-start.13) | collective-permute-done | bytes 610336 | tf_op jit(solution)/shard_map/ppermute | solution.py:625
  180.1 1.5 collective-permute-start.14
  181.6 1.6 collective-permute-done.18
  184.5 1.3 collective-permute-done.26
  185.8 1.3 fusion
  188.5 1.4 fusion.3
  190.1 1.3 collective-permute-start.21
  191.5 3.0 %collective-permute-start.19 = (f32[352,128]{1,0:T(8,128)S(1)}, f32[352,128]{1,0:T(8,128)S(1)}, u32[]{:S(2)}, u32[]{:S(2)}) collective-permute-start(f32[352,128]{1,0:T(8,128)S(1)} %get-tuple-element.109), channel_id=1, source_target_pairs={{0,8},{4,12},{8,0},{12,4},{16,24},{20,28},{24,16},{28,20},{1,9},{5... | collective-permute-start | bytes 540680 | tf_op jit(solution)/shard_map/ppermute | solution.py:625
  194.6 4.9 %collective-permute-done.21 = f32[352,128]{1,0:T(8,128)S(1)} collective-permute-done((f32[352,128]{1,0:T(8,128)S(1)}, f32[352,128]{1,0:T(8,128)S(1)}, u32[]{:S(2)}, u32[]{:S(2)}) %collective-permute-start.21) | collective-permute-done | bytes 180256 | tf_op jit(solution)/shard_map/ppermute | solution.py:625
  199.5 7.1 %collective-permute-done.20 = f32[352,128]{1,0:T(8,128)S(1)} collective-permute-done((f32[352,128]{1,0:T(8,128)S(1)}, f32[352,128]{1,0:T(8,128)S(1)}, u32[]{:S(2)}, u32[]{:S(2)}) %collective-permute-start.20) | collective-permute-done | bytes 180256 | tf_op jit(solution)/shard_map/ppermute | solution.py:625
  209.8 2.1 %shard_map.275 = (f32[1,512]{1,0:T(1,128)}, f32[1,512]{1,0:T(1,128)}, f32[1,512]{1,0:T(1,128)}, f32[64,128]{1,0:T(8,128)}, f32[128,256]{1,0:T(8,128)}, /*index=5...) custom-call(f32[1360,128]{1,0:T(8,128)} %pad_maximum_fusion.1.packed_ref, f32[8,56,128]{2,1,0:T(8,128)} %bitcast.311), custom_call_target="tpu_custom_call" | custom-call | flops 2200000000 | tf_op jit(solution)/shard_map/pallas_call | solution.py:614
  (99 shorter events, 15.6 us)
Async XLA Ops:
  1.8 3.7 %collective-permute-start = (f32[192,512]{1,0:T(8,128)S(1)}, f32[192,512]{1,0:T(8,128)S(1)}, u32[]{:S(2)}, u32[]{:S(2)}) collective-permute-start(f32[192,512]{1,0:T(8,128)S(1)} %bitcast.310), channel_id=1, source_target_pairs={{0,4},{4,8},{8,12},{12,16},{16,20},{20,24},{24,28},{1,5},{5,9},{9,... | collective-permute-start | bytes 1179656 | tf_op jit(solution)/shard_map/ppermute | solution.py:708
  4.2 5.8 %collective-permute-start.1 = (f32[192,512]{1,0:T(8,128)S(1)}, f32[192,512]{1,0:T(8,128)S(1)}, u32[]{:S(2)}, u32[]{:S(2)}) collective-permute-start(f32[192,512]{1,0:T(8,128)S(1)} %bitcast.309), channel_id=1, source_target_pairs={{4,0},{8,4},{12,8},{16,12},{20,16},{24,20},{28,24},{5,1},{9,5},{13... | collective-permute-start | bytes 1179656 | tf_op jit(solution)/shard_map/ppermute | solution.py:708
  5.5 4.5 %copy-start.6 = (f32[192,512]{1,0:T(8,128)}, f32[192,512]{1,0:T(8,128)S(1)}, u32[]{:S(2)}) copy-start(f32[192,512]{1,0:T(8,128)S(1)} %collective-permute-done.above_ref) | copy-start | bytes 1179652
  10.0 0.8 copy-start.7
  66.9 19.7 %copy-start = (f32[4,4,256,128]{3,2,1,0:T(8,128)S(1)}, f32[4,4,256,128]{3,2,1,0:T(8,128)}, u32[]{:S(2)}) copy-start(f32[4,4,256,128]{3,2,1,0:T(8,128)} %get-tuple-element.50) | copy-start | bytes 6291460
  66.9 19.7 %collective-permute-start.4 = (f32[4,4,256,128]{3,2,1,0:T(8,128)}, f32[4,4,256,128]{3,2,1,0:T(8,128)}, u32[]{:S(2)}, u32[]{:S(2)}) collective-permute-start(f32[4,4,256,128]{3,2,1,0:T(8,128)} %get-tuple-element.51), channel_id=1, source_target_pairs={{0,4},{4,0},{8,12},{12,8},{16,20},{20,16},{24,28},{28,24},{1,5},{5... | collective-permute-start | bytes 6291464 | tf_op jit(solution)/shard_map/ppermute | solution.py:625
  72.9 17.4 %collective-permute-start.5 = (f32[4,4,256,128]{3,2,1,0:T(8,128)}, f32[4,4,256,128]{3,2,1,0:T(8,128)}, u32[]{:S(2)}, u32[]{:S(2)}) collective-permute-start(f32[4,4,256,128]{3,2,1,0:T(8,128)} %get-tuple-element.53), channel_id=1, source_target_pairs={{0,4},{4,0},{8,12},{12,8},{16,20},{20,16},{24,28},{28,24},{1,5},{5... | collective-permute-start | bytes 6291464 | tf_op jit(solution)/shard_map/ppermute | solution.py:625
  73.0 8.7 %collective-permute-start.6 = (f32[4,4,64,128]{3,2,1,0:T(8,128)}, f32[4,4,64,128]{3,2,1,0:T(8,128)S(1)}, u32[]{:S(2)}, u32[]{:S(2)}) collective-permute-start(f32[4,4,64,128]{3,2,1,0:T(8,128)} %get-tuple-element.55), channel_id=1, source_target_pairs={{0,4},{4,0},{8,12},{12,8},{16,20},{20,16},{24,28},{28,24},{1,5},{5... | collective-permute-start | bytes 1572872 | tf_op jit(solution)/shard_map/ppermute | solution.py:625
  73.5 6.0 %collective-permute-start.9 = (f32[680,128]{1,0:T(8,128)}, f32[680,128]{1,0:T(8,128)S(1)}, u32[]{:S(2)}, u32[]{:S(2)}) collective-permute-start(f32[680,128]{1,0:T(8,128)} %get-tuple-element.61), channel_id=1, source_target_pairs={{0,4},{4,0},{8,12},{12,8},{16,20},{20,16},{24,28},{28,24},{1,5},{5... | collective-permute-start | bytes 1044488 | tf_op jit(solution)/shard_map/ppermute | solution.py:625
  73.5 20.9 %collective-permute-start.2 = (f32[8,192,128]{2,1,0:T(8,128)}, f32[8,192,128]{2,1,0:T(8,128)}, u32[]{:S(2)}, u32[]{:S(2)}) collective-permute-start(f32[8,192,128]{2,1,0:T(8,128)} %get-tuple-element.45), channel_id=1, source_target_pairs={{0,4},{4,8},{8,12},{12,16},{16,20},{20,24},{24,28},{1,5},{5,9},{9,... | collective-permute-start | bytes 2359304 | tf_op jit(solution)/shard_map/ppermute | solution.py:708
  79.4 15.0 %collective-permute-start.3 = (f32[8,192,128]{2,1,0:T(8,128)}, f32[8,192,128]{2,1,0:T(8,128)}, u32[]{:S(2)}, u32[]{:S(2)}) collective-permute-start(f32[8,192,128]{2,1,0:T(8,128)} %get-tuple-element.47), channel_id=1, source_target_pairs={{4,0},{8,4},{12,8},{16,12},{20,16},{24,20},{28,24},{5,1},{9,5},{13... | collective-permute-start | bytes 2359304 | tf_op jit(solution)/shard_map/ppermute | solution.py:708
  81.8 7.1 %copy-start.4 = (f32[4,4,64,128]{3,2,1,0:T(8,128)}, f32[4,4,64,128]{3,2,1,0:T(8,128)S(1)}, u32[]{:S(2)}) copy-start(f32[4,4,64,128]{3,2,1,0:T(8,128)S(1)} %collective-permute-done.6) | copy-start | bytes 1572868
  81.8 37.2 %collective-permute-start.10 = (f32[680,128]{1,0:T(8,128)S(1)}, f32[680,128]{1,0:T(8,128)}, u32[]{:S(2)}, u32[]{:S(2)}) collective-permute-start(f32[680,128]{1,0:T(8,128)S(1)} %add.1004), channel_id=1, source_target_pairs={{0,8},{4,12},{8,0},{12,4},{16,24},{20,28},{24,16},{28,20},{1,9},{5... | collective-permute-start | bytes 1044488 | tf_op jit(solution)/shard_map/ppermute | solution.py:625
  84.5 5.9 %copy-start.1 = (f32[4,4,256,128]{3,2,1,0:T(8,128)S(1)}, f32[4,4,256,128]{3,2,1,0:T(8,128)}, u32[]{:S(2)}) copy-start(f32[4,4,256,128]{3,2,1,0:T(8,128)} %get-tuple-element.52) | copy-start | bytes 6291460
  88.9 36.3 %collective-permute-start.7 = (f32[2048,128]{1,0:T(8,128)}, f32[2048,128]{1,0:T(8,128)}, u32[]{:S(2)}, u32[]{:S(2)}) collective-permute-start(f32[2048,128]{1,0:T(8,128)} %bitcast.13.rest_0_), channel_id=1, source_target_pairs={{0,1},{1,0},{2,3},{3,2},{4,5},{5,4},{6,7},{7,6},{8,9},{9,8},{10,11... | collective-permute-start | bytes 3145736 | tf_op jit(solution)/shard_map/ppermute | solution.py:625
  92.8 34.8 %collective-permute-start.8 = (f32[2560,128]{1,0:T(8,128)}, f32[2560,128]{1,0:T(8,128)}, u32[]{:S(2)}, u32[]{:S(2)}) collective-permute-start(f32[2560,128]{1,0:T(8,128)} %pad_maximum_fusion.rest_1_), channel_id=1, source_target_pairs={{0,2},{1,3},{2,0},{3,1},{4,6},{5,7},{6,4},{7,5},{8,10},{9,11},{10,... | collective-permute-start | bytes 3932168 | tf_op jit(solution)/shard_map/ppermute | solution.py:625
  120.0 6.3 %copy-start.2 = (f32[680,128]{1,0:T(8,128)}, f32[680,128]{1,0:T(8,128)S(1)}, u32[]{:S(2)}) copy-start(f32[680,128]{1,0:T(8,128)S(1)} %add_add_fusion.1.rest_5_) | copy-start | bytes 1044484
  120.0 30.6 %collective-permute-start.11 = (f32[680,128]{1,0:T(8,128)S(1)}, f32[680,128]{1,0:T(8,128)}, u32[]{:S(2)}, u32[]{:S(2)}) collective-permute-start(f32[680,128]{1,0:T(8,128)S(1)} %add_add_fusion.1.rest_5_), channel_id=1, source_target_pairs={{0,16},{4,20},{8,24},{12,28},{16,0},{20,4},{24,8},{28,12},{1,17},{... | collective-permute-start | bytes 1044488 | tf_op jit(solution)/shard_map/ppermute | solution.py:625
  127.1 24.8 %collective-permute-start.24 = (f32[1024,128]{1,0:T(8,128)}, f32[1024,128]{1,0:T(8,128)}, u32[]{:S(2)}, u32[]{:S(2)}) collective-permute-start(f32[1024,128]{1,0:T(8,128)} %bitcast_add_fusion.1.rest_3_), channel_id=1, source_target_pairs={{0,2},{1,3},{2,0},{3,1},{4,6},{5,7},{6,4},{7,5},{8,10},{9,11},{10,... | collective-permute-start | bytes 1572872 | tf_op jit(solution)/shard_map/ppermute | solution.py:625
  130.9 22.5 %collective-permute-start.23 = (f32[1280,128]{1,0:T(8,128)}, f32[1280,128]{1,0:T(8,128)}, u32[]{:S(2)}, u32[]{:S(2)}) collective-permute-start(f32[1280,128]{1,0:T(8,128)} %pad_maximum_fusion.2.rest_4_), channel_id=1, source_target_pairs={{0,1},{1,0},{2,3},{3,2},{4,5},{5,4},{6,7},{7,6},{8,9},{9,8},{10,11... | collective-permute-start | bytes 1966088 | tf_op jit(solution)/shard_map/ppermute | solution.py:625
  143.0 5.6 %copy-start.5 = (f32[8,56,128]{2,1,0:T(8,128)S(1)}, f32[8,56,128]{2,1,0:T(8,128)}, u32[]{:S(2)}) copy-start(f32[8,56,128]{2,1,0:T(8,128)} %get-tuple-element.65) | copy-start | bytes 688132
  143.0 7.6 %copy-start.3 = (f32[680,128]{1,0:T(8,128)S(1)}, f32[680,128]{1,0:T(8,128)}, u32[]{:S(2)}) copy-start(f32[680,128]{1,0:T(8,128)} %copy-done.2) | copy-start | bytes 1044484
  143.0 19.2 %collective-permute-start.12 = (f32[4,4,128,128]{3,2,1,0:T(8,128)}, f32[4,4,128,128]{3,2,1,0:T(8,128)S(1)}, u32[]{:S(2)}, u32[]{:S(2)}) collective-permute-start(f32[4,4,128,128]{3,2,1,0:T(8,128)} %get-tuple-element.64), channel_id=1, source_target_pairs={{0,4},{4,0},{8,12},{12,8},{16,20},{20,16},{24,28},{28,24},{1,5},{5... | collective-permute-start | bytes 3145736 | tf_op jit(solution)/shard_map/ppermute | solution.py:625
  150.5 1.4 collective-permute-start.16
  157.7 26.8 %collective-permute-start.27 = (f32[576,128]{1,0:T(8,128)S(1)}, f32[576,128]{1,0:T(8,128)S(1)}, u32[]{:S(2)}, u32[]{:S(2)}) collective-permute-start(f32[576,128]{1,0:T(8,128)S(1)} %pad_maximum_fusion.8), channel_id=1, source_target_pairs={{0,24},{4,28},{8,16},{12,20},{16,8},{20,12},{24,0},{28,4},{1,25},{... | collective-permute-start | bytes 884744 | tf_op jit(solution)/shard_map/ppermute | solution.py:625
  158.0 27.8 %collective-permute-start.26 = (f32[576,128]{1,0:T(8,128)S(1)}, f32[576,128]{1,0:T(8,128)S(1)}, u32[]{:S(2)}, u32[]{:S(2)}) collective-permute-start(f32[576,128]{1,0:T(8,128)S(1)} %pad_maximum_fusion.7), channel_id=1, source_target_pairs={{0,16},{4,20},{8,24},{12,28},{16,0},{20,4},{24,8},{28,12},{1,17},{... | collective-permute-start | bytes 884744 | tf_op jit(solution)/shard_map/ppermute | solution.py:625
  159.8 26.0 %collective-permute-start.25 = (f32[576,128]{1,0:T(8,128)S(1)}, f32[576,128]{1,0:T(8,128)S(1)}, u32[]{:S(2)}, u32[]{:S(2)}) collective-permute-start(f32[576,128]{1,0:T(8,128)S(1)} %pad_maximum_fusion.6), channel_id=1, source_target_pairs={{0,8},{4,12},{8,0},{12,4},{16,24},{20,28},{24,16},{28,20},{1,9},{5... | collective-permute-start | bytes 884744 | tf_op jit(solution)/shard_map/ppermute | solution.py:625
  162.4 10.1 %collective-permute-start.17 = (f32[736,128]{1,0:T(8,128)S(1)}, f32[736,128]{1,0:T(8,128)S(1)}, u32[]{:S(2)}, u32[]{:S(2)}) collective-permute-start(f32[736,128]{1,0:T(8,128)S(1)} %pad_maximum_fusion.5), channel_id=1, source_target_pairs={{0,1},{1,0},{2,3},{3,2},{4,5},{5,4},{6,7},{7,6},{8,9},{9,8},{10,11... | collective-permute-start | bytes 1130504 | tf_op jit(solution)/shard_map/ppermute | solution.py:625
  163.1 16.8 %collective-permute-start.13 = (f32[1192,128]{1,0:T(8,128)S(1)}, f32[1192,128]{1,0:T(8,128)S(1)}, u32[]{:S(2)}, u32[]{:S(2)}) collective-permute-start(f32[1192,128]{1,0:T(8,128)S(1)} %pad_maximum_fusion.3), channel_id=1, source_target_pairs={{0,2},{1,3},{2,0},{3,1},{4,6},{5,7},{6,4},{7,5},{8,10},{9,11},{10,... | collective-permute-start | bytes 1830920 | tf_op jit(solution)/shard_map/ppermute | solution.py:625
  172.7 10.6 %collective-permute-start.18 = (f32[480,128]{1,0:T(8,128)S(1)}, f32[480,128]{1,0:T(8,128)S(1)}, u32[]{:S(2)}, u32[]{:S(2)}) collective-permute-start(f32[480,128]{1,0:T(8,128)S(1)} %pad_maximum_fusion.9), channel_id=1, source_target_pairs={{0,2},{1,3},{2,0},{3,1},{4,6},{5,7},{6,4},{7,5},{8,10},{9,11},{10,... | collective-permute-start | bytes 737288 | tf_op jit(solution)/shard_map/ppermute | solution.py:625
  180.1 9.9 %collective-permute-start.14 = (f32[936,128]{1,0:T(8,128)S(1)}, f32[936,128]{1,0:T(8,128)S(1)}, u32[]{:S(2)}, u32[]{:S(2)}) collective-permute-start(f32[936,128]{1,0:T(8,128)S(1)} %pad_maximum_fusion.4), channel_id=1, source_target_pairs={{0,1},{1,0},{2,3},{3,2},{4,5},{5,4},{6,7},{7,6},{8,9},{9,8},{10,11... | collective-permute-start | bytes 1437704 | tf_op jit(solution)/shard_map/ppermute | solution.py:625
  190.1 9.5 %collective-permute-start.21 = (f32[352,128]{1,0:T(8,128)S(1)}, f32[352,128]{1,0:T(8,128)S(1)}, u32[]{:S(2)}, u32[]{:S(2)}) collective-permute-start(f32[352,128]{1,0:T(8,128)S(1)} %get-tuple-element.111), channel_id=1, source_target_pairs={{0,24},{4,28},{8,16},{12,20},{16,8},{20,12},{24,0},{28,4},{1,25},{... | collective-permute-start | bytes 540680 | tf_op jit(solution)/shard_map/ppermute | solution.py:625
  191.4 15.2 %collective-permute-start.20 = (f32[352,128]{1,0:T(8,128)S(1)}, f32[352,128]{1,0:T(8,128)S(1)}, u32[]{:S(2)}, u32[]{:S(2)}) collective-permute-start(f32[352,128]{1,0:T(8,128)S(1)} %get-tuple-element.110), channel_id=1, source_target_pairs={{0,16},{4,20},{8,24},{12,28},{16,0},{20,4},{24,8},{28,12},{1,17},{... | collective-permute-start | bytes 540680 | tf_op jit(solution)/shard_map/ppermute | solution.py:625
  191.5 15.1 %collective-permute-start.19 = (f32[352,128]{1,0:T(8,128)S(1)}, f32[352,128]{1,0:T(8,128)S(1)}, u32[]{:S(2)}, u32[]{:S(2)}) collective-permute-start(f32[352,128]{1,0:T(8,128)S(1)} %get-tuple-element.109), channel_id=1, source_target_pairs={{0,8},{4,12},{8,0},{12,4},{16,24},{20,28},{24,16},{28,20},{1,9},{5... | collective-permute-start | bytes 540680 | tf_op jit(solution)/shard_map/ppermute | solution.py:625
  194.6 14.2 %collective-permute-start.15 = (f32[680,128]{1,0:T(8,128)S(1)}, f32[680,128]{1,0:T(8,128)S(1)}, u32[]{:S(2)}, u32[]{:S(2)}) collective-permute-start(f32[680,128]{1,0:T(8,128)S(1)} %slice_add_fusion), channel_id=1, source_target_pairs={{0,4},{4,0},{8,12},{12,8},{16,20},{20,16},{24,28},{28,24},{1,5},{5... | collective-permute-start | bytes 1044488 | tf_op jit(solution)/shard_map/ppermute | solution.py:625
  206.6 1.4 collective-permute-start.22

commit v4 on v3

--- a/solution.py
+++ b/solution.py
@@ -15,7 +15,7 @@
 EPSILON = 1e-06
 LANES = 128
 EDGE = 8
-VMEM_BYTES = 62 << 20
+VMEM_BYTES = 64 << 20
 F32 = jnp.float32
 INV_SQRT_2 = 0.7071067811865476
 INV_SQRT_2PI = 0.3989422804014327
@@ -58,8 +58,8 @@
     return pl.BlockSpec(memory_space=pltpu.SMEM)
 
 
-def anywhere():
-    return pl.BlockSpec(memory_space=pl.ANY)
+def in_hbm():
+    return pl.BlockSpec(memory_space=pltpu.HBM)
 
 
 def shape_of(*shape):
@@ -143,9 +143,9 @@
         wide[TAPS + t] = jnp.zeros((8, LANES), F32)
 
 
-def conv_block(row_taps, kern, shifted, wide, out_ref, rows, cols):
+def conv_block(row_taps, kern, shifted, wide, out_ref, rows, cols, turned=False):
     groups = cols // 8
-    spread_taps(kern, wide, False)
+    spread_taps(kern, wide, turned)
 
     def pair(h, _):
         r = 2 * h
@@ -169,24 +169,17 @@
     lax.fori_loop(0, rows // 2, pair, 0)
 
 
-def conv_grad_block(row_taps, kern, shifted, wide, dk, mix_ref, out_ref, dk_ref, rows, cols):
+def kernel_grad_block(row_taps, shifted, dk, mix_ref, dk_ref, rows, cols):
     groups = cols // 8
-    spread_taps(kern, wide, True)
     for t in range(TAPS):
         dk[t] = jnp.zeros((8, LANES), F32)
 
     def one(r, _):
-        start = pl.ds(pl.multiple_of(r * cols, cols), cols)
-        mix = mix_ref[start, :].reshape(groups, 8, LANES)
-        total = jnp.zeros((groups, 8, LANES), F32)
+        mix = mix_ref[pl.ds(pl.multiple_of(r * cols, cols), cols), :].reshape(groups, 8, LANES)
         for i in range(KERN):
-            row = row_taps[r, i + 1]
-            same = jnp.where(row < KERN, 1.0, 0.0).astype(F32)
+            same = jnp.where(row_taps[r, i + 1] < KERN, 1.0, 0.0).astype(F32)
             for b in range(KERN):
-                x = shifted[b, r + i]
-                total = total + wide[row * KERN + b][None] * x
-                dk[i * KERN + b] += jnp.sum(mix * x, axis=0) * same
-        out_ref[start, :] = total.reshape(cols, LANES)
+                dk[i * KERN + b] += jnp.sum(mix * shifted[b, r + i], axis=0) * same
         return 0
 
     lax.fori_loop(0, rows, one, 0)
@@ -485,14 +478,22 @@
     )
 
 
+def lay_flat(above_ref, own_ref, below_ref, flat):
+    reach, cells = above_ref.shape[1], own_ref.shape[1]
+    flat[:EDGE] = jnp.zeros((EDGE, LANES), F32)
+    flat[EDGE : EDGE + reach] = above_ref[0]
+    flat[EDGE + reach : EDGE + reach + cells] = own_ref[0]
+    flat[EDGE + reach + cells : EDGE + 2 * reach + cells] = below_ref[0]
+    flat[EDGE + 2 * reach + cells :] = jnp.zeros((EDGE, LANES), F32)
+
+
 def backward_kernel(
-    place_ref, ids_scalar, ids_ref, above_ref, own_ref, below_ref, mix_ref, kern_ref, canvas_ref, gain_ref,
-    dmiddle_ref, before_ref, in_ref, *rest, rows, cols, first_block, last,
+    place_ref, ids_scalar, ids_ref, above_ref, own_ref, below_ref, kern_ref, canvas_ref, gain_ref,
+    dmiddle_ref, in_ref, *rest, rows, cols,
 ):
-    total_ref, kept_ref, sent_ref, dk_ref = rest[-16:-12]
-    row_taps, padded, valid_ref, col_ref, flat, shifted, laid, wide, dk, djoined, normed, dnorm = rest[-12:]
+    dcanvas_ref, kept_ref, sent_ref, dgain_ref = rest[-15:-11]
+    row_taps, padded, valid_ref, col_ref, flat, shifted, laid, wide, djoined, normed, dnorm = rest[-11:]
     step = pl.program_id(0)
-    block = first_block + step
     cells = rows * cols
     reach = REACH * cols
     core = place_ref[0] % 2
@@ -507,17 +508,11 @@
         conv_masks(ids_scalar, ids_ref, place_ref[0], row_taps, col_ref, rows)
         hat, _ = normalized(canvas_ref[...] * valid_ref[reach : reach + cells, :1])
         normed[...] = hat * gain_ref[...]
-        dnorm[...] = before_ref[...] if first_block else jnp.zeros_like(dnorm)
-
-    flat[:EDGE] = jnp.zeros((EDGE, LANES), F32)
-    flat[EDGE : EDGE + reach] = above_ref[0]
-    flat[EDGE + reach : EDGE + reach + cells] = own_ref[0]
-    flat[EDGE + reach + cells : EDGE + 2 * reach + cells] = below_ref[0]
-    flat[EDGE + 2 * reach + cells :] = jnp.zeros((EDGE, LANES), F32)
+        dnorm[...] = jnp.zeros_like(dnorm)
+
+    lay_flat(above_ref, own_ref, below_ref, flat)
     fill_shifted(flat, col_ref, shifted, rows + 2 * REACH, cols)
-    conv_grad_block(
-        row_taps, laid[block], shifted, wide, dk, mix_ref.at[0], djoined.at[step % 2], dk_ref.at[0], rows, cols
-    )
+    conv_block(row_taps, laid[step], shifted, wide, djoined.at[step % 2], rows, cols, turned=True)
 
     @pl.when(step % 2 == 1)
     def _():
@@ -527,50 +522,42 @@
 
     @pl.when(step == pl.num_programs(0) - 1)
     def _():
-        if not last:
-            total_ref[...] = dnorm[...]
-            return
         hat, scale = normalized(canvas_ref[...] * valid_ref[reach : reach + cells, :1])
         dgain = jnp.sum(dnorm[...] * hat, axis=0, keepdims=True)
+        dgain_ref[...] = jnp.zeros_like(dgain_ref)
         for k in range(dgain.shape[1] // LANES):
-            dk_ref[0, TAPS + k : TAPS + k + 1] = dgain[:, k * LANES : (k + 1) * LANES]
+            dgain_ref[k : k + 1] = dgain[:, k * LANES : (k + 1) * LANES]
         inner = dmiddle_ref[...] + norm_backward(dnorm[...] * gain_ref[...], hat, scale)
-        total_ref[...] = inner * valid_ref[reach : reach + cells, :1]
+        dcanvas_ref[...] = inner * valid_ref[reach : reach + cells, :1]
+
+
+def block_of(size):
+    return pl.BlockSpec((1, size, LANES), lambda i: (i, 0, 0))
 
 
 def backward(
-    place, ids, above, own, below, mix, kern, canvas, gain, dmiddle, before, weight_in,
-    first_block, end_block, written, ties, rows, cols, count_ha, count_ba,
+    place, ids, above, own, below, kern, canvas, gain, dmiddle, weight_in, ties, rows, cols, count_ha, count_ba
 ):
     cells, dim = canvas.shape
     blocks = own.shape[0]
     reach = above.shape[1]
-    steps = end_block - first_block
     own_wide = weight_in.shape[1] // count_ha
     chunk_rows = dim // count_ba * lane_blocks(own_wide)
     groups = 2 * LANES // (2 * own_wide)
-    tall = -(-(TAPS + dim // LANES) // 8) * 8
-
-    def block_of(size):
-        return pl.BlockSpec((1, size, LANES), lambda i: (first_block + i, 0, 0))
-
-    chunk_spec = pl.BlockSpec((groups, count_ba, chunk_rows, LANES), lambda i: (first_block // 2 + i // 2, 0, 0, 0))
+    chunk_spec = pl.BlockSpec((groups, count_ba, chunk_rows, LANES), lambda i: (i // 2, 0, 0, 0))
     chunks = shape_of(count_ha // 2, count_ba, chunk_rows, LANES)
-    fixed = 13
+    gain_shape = (-(-dim // LANES // 8) * 8, LANES)
     return pl.pallas_call(
-        functools.partial(
-            backward_kernel, rows=rows, cols=cols, first_block=first_block, last=end_block == blocks
-        ),
-        grid=(steps,),
+        functools.partial(backward_kernel, rows=rows, cols=cols),
+        grid=(blocks,),
         in_specs=[in_smem(), in_smem(), whole(ids.shape)]
-        + [block_of(size) for size in (reach, cells, reach, cells)]
+        + [block_of(size) for size in (reach, cells, reach)]
         + [whole(kern.shape), whole(canvas.shape)]
-        + [whole((1, dim)), whole((cells, dim)), whole((cells, dim))]
-        + [pl.BlockSpec((dim, 2 * LANES), lambda i: (0, first_block // 2 + i // 2))]
-        + [anywhere()] * (len(written) + len(ties)),
-        out_specs=[whole((cells, dim)), chunk_spec, chunk_spec, block_of(tall)],
-        out_shape=[shape_of(cells, dim), chunks, chunks, shape_of(blocks, tall, LANES)],
-        input_output_aliases={fixed + k: 1 + k for k in range(len(written))},
+        + [whole((1, dim)), whole((cells, dim))]
+        + [pl.BlockSpec((dim, 2 * LANES), lambda i: (0, i // 2))]
+        + [in_hbm()] * len(ties),
+        out_specs=[whole((cells, dim)), chunk_spec, chunk_spec, whole(gain_shape)],
+        out_shape=[shape_of(cells, dim), chunks, chunks, shape_of(*gain_shape)],
         scratch_shapes=mask_scratch(ids, rows)
         + [
             pltpu.VMEM((KERN, cols // 8, 8, LANES), F32),
@@ -578,127 +565,231 @@
             pltpu.VMEM((KERN, rows + 2 * REACH, cols // 8, 8, LANES), F32),
             pltpu.VMEM((blocks, TAPS, LANES), F32),
             pltpu.VMEM((TAPS + KERN, 8, LANES), F32),
-            pltpu.VMEM((TAPS, 8, LANES), F32),
             pltpu.VMEM((2, cells, LANES), F32),
             pltpu.VMEM((cells, dim), F32),
             pltpu.VMEM((cells, dim), F32),
         ],
         compiler_params=params(),
-        cost_estimate=lasting(4 * steps),
-    )(
-        place, ids, ids, above, own, below, mix, kern, canvas, gain, dmiddle, before, weight_in,
-        *written, *ties,
-    )
-
-
-def unpack_kernel(packed_ref, dkern_ref, *outs, dim):
-    row = 0
-    for ref in outs[:3]:
-        for k in range(dim // LANES):
-            ref[:, k * LANES : (k + 1) * LANES] = packed_ref[row : row + 1]
-            row += 1
-    row = packed_ref.shape[0]
-    for ref in reversed(outs[3:6]):
-        tall, width = ref.shape
-        row -= tall * width // LANES
-        for k in range(width // LANES):
-            ref[:, k * LANES : (k + 1) * LANES] = packed_ref[row + k * tall : row + (k + 1) * tall]
-    dk_ref, gain_ref = outs[6:]
-    joined = jnp.concatenate([dkern_ref[k, :TAPS] for k in range(dkern_ref.shape[0])], axis=1)
-    dk_ref[...] = joined[:, joined.shape[1] - dk_ref.shape[1] :]
-    for k in range(dim // LANES):
-        gain_ref[:, k * LANES : (k + 1) * LANES] = dkern_ref[dkern_ref.shape[0] - 1, TAPS + k : TAPS + k + 1]
-
-
-def unpack(packed, dkern, gates, kern, dim):
+        cost_estimate=lasting(20),
+    )(place, ids, ids, above, own, below, kern, canvas, gain, dmiddle, weight_in, *ties)
+
+
+def kernel_grad_kernel(
+    place_ref, ids_scalar, ids_ref, above_ref, own_ref, below_ref, mix_ref, dgain_ref, *rest, rows, cols
+):
+    kept_ref, sent_ref, row_taps, padded, valid_ref, col_ref, flat, shifted, dk, sums = rest[-10:]
+    step = pl.program_id(0)
+
+    @pl.when(step == 0)
+    def _():
+        conv_masks(ids_scalar, ids_ref, place_ref[0], row_taps, col_ref, rows)
+
+    lay_flat(above_ref, own_ref, below_ref, flat)
+    fill_shifted(flat, col_ref, shifted, rows + 2 * REACH, cols)
+    kernel_grad_block(row_taps, shifted, dk, mix_ref.at[0], sums.at[step], rows, cols)
+
+    @pl.when(step == pl.num_programs(0) - 1)
+    def _():
+        count = sums.shape[0]
+        spare = sums.shape[1] - TAPS
+        sums[count - 1, TAPS:] = dgain_ref[:spare]
+        core = place_ref[0] % 2
+        half = count // 2
+        for ref, start in ((kept_ref, core * half), (sent_ref, (1 - core) * half)):
+            ref[...] = sums[pl.ds(start, half)].reshape(ref.shape)
+
+
+def kernel_grad(place, ids, above, own, below, mix, dgain, ties, rows, cols, dim):
+    blocks, cells, _ = own.shape
+    reach = above.shape[1]
+    tall = -(-(TAPS + dim // LANES) // 8) * 8
+    half = (blocks // 2 * tall, LANES)
     return pl.pallas_call(
-        functools.partial(unpack_kernel, dim=dim),
-        out_shape=[shape_of(1, dim)] * 3
-        + [shape_of(*gate.shape) for gate in gates]
-        + [shape_of(*kern.shape), shape_of(1, dim)],
+        functools.partial(kernel_grad_kernel, rows=rows, cols=cols),
+        grid=(blocks,),
+        in_specs=[in_smem(), in_smem(), whole(ids.shape)]
+        + [block_of(size) for size in (reach, cells, reach, cells)]
+        + [whole(dgain.shape)]
+        + [in_hbm()] * len(ties),
+        out_specs=[whole(half), whole(half)],
+        out_shape=[shape_of(*half), shape_of(*half)],
+        scratch_shapes=mask_scratch(ids, rows)
+        + [
+            pltpu.VMEM((KERN, cols // 8, 8, LANES), F32),
+            pltpu.VMEM((cells + 2 * reach + 2 * EDGE, LANES), F32),
+            pltpu.VMEM((KERN, rows + 2 * REACH, cols // 8, 8, LANES), F32),
+            pltpu.VMEM((TAPS, 8, LANES), F32),
+            pltpu.VMEM((blocks, tall, LANES), F32),
+        ],
         compiler_params=params(),
-        cost_estimate=lasting(2),
-    )(packed, dkern)
+        cost_estimate=lasting(11),
+    )(place, ids, ids, above, own, below, mix, dgain, *ties)
 
 
 def exchange(values, axis, bit):
     return lax.ppermute(values, axis, [(i, i ^ bit) for i in range(lax.axis_size(axis))])
 
 
-def picked(parts, index, axis):
-    return [lax.dynamic_index_in_dim(part, index, axis, keepdims=False) for part in parts]
-
-
-def total(parts):
-    result = parts[0]
-    for part in parts[1:]:
-        result = result + part
-    return result
-
-
-def along(way):
-    return lax.axis_index("ha") // 2 if way == "z" else (lax.axis_index("ba") >> way) & 1
+class View:
+    def __init__(self, array, start, ways, fixed, rows):
+        self.array, self.start, self.ways, self.fixed, self.rows = array, start, ways, fixed, rows
+
+    def fix(self, way, step):
+        left = [entry for entry in self.ways if entry[0] != way]
+        (stride,) = [entry[2] for entry in self.ways if entry[0] == way]
+        return View(self.array, self.start, left, self.fixed + [(way, step, stride)], self.rows)
+
+    def size(self):
+        count = self.rows
+        for _, size, _ in self.ways:
+            count *= size
+        return count
+
+    def runs(self, ha, ba):
+        start = self.start
+        for way, step, stride in self.fixed:
+            place = ha // 2 if way == "z" else (ba >> way) & 1
+            start = start + (place ^ step) * stride
+        offsets = [0]
+        for _, size, stride in self.ways:
+            offsets = [offset + k * stride for offset in offsets for k in range(size)]
+        return [pl.multiple_of(start + offset, 8) for offset in offsets]
+
+
+def plain(array):
+    rows = array.reshape(-1, LANES)
+    return [View(rows, 0, [], [], rows.shape[0])]
+
+
+def combine(place, groups, ties=(), epilogue=None, out_shape=None):
+    pieces = [views for group in groups for views in group]
+    arrays = []
+    for views in pieces:
+        for view in views:
+            if not any(view.array is other for other in arrays):
+                arrays.append(view.array)
+    index_of = {id(array): k for k, array in enumerate(arrays)}
+    sizes = [sum(views[0].size() for views in group) for group in groups]
+    copies = sum(view.size() // view.rows for views in pieces for view in views)
+    if epilogue is None:
+        out_shape = [shape_of(size, LANES) for size in sizes]
+
+    def kernel(place_ref, *refs):
+        inputs = refs[: len(arrays)]
+        refs = refs[len(arrays) + len(ties) :]
+        outs, (buffers, sems) = refs[: len(out_shape)], (refs[len(out_shape) : -1], refs[-1])
+        ha, ba = place_ref[0], place_ref[1]
+        moves, count = [], 0
+        for piece, views in enumerate(pieces):
+            moves.append([])
+            for term, view in enumerate(views):
+                source = inputs[index_of[id(view.array)]]
+                for k, start in enumerate(view.runs(ha, ba)):
+                    target = buffers[piece].at[term, pl.ds(k * view.rows, view.rows), :]
+                    moves[-1].append(
+                        pltpu.make_async_copy(source.at[pl.ds(start, view.rows), :], target, sems.at[count])
+                    )
+                    moves[-1][-1].start()
+                    count += 1
+        piece = 0
+        values = []
+        for out, group in enumerate(groups):
+            row = 0
+            for views in group:
+                for move in moves[piece]:
+                    move.wait()
+                value = buffers[piece][0]
+                for term in range(1, len(views)):
+                    value = value + buffers[piece][term]
+                if epilogue is None:
+                    outs[out][row : row + value.shape[0], :] = value
+                values.append(value)
+                row += value.shape[0]
+                piece += 1
+        if epilogue is not None:
+            epilogue(ha, values, outs)
+
+    moved = sum(view.size() for views in pieces for view in views) + sum(sizes)
+    return pl.pallas_call(
+        kernel,
+        in_specs=[in_smem()] + [in_hbm()] * (len(arrays) + len(ties)),
+        out_specs=[pl.BlockSpec(memory_space=pltpu.VMEM)] * len(out_shape),
+        out_shape=out_shape,
+        scratch_shapes=[pltpu.VMEM((len(views), views[0].size(), LANES), F32) for views in pieces]
+        + [pltpu.SemaphoreType.DMA((copies,))],
+        compiler_params=params(),
+        cost_estimate=lasting(1 + moved * LANES * 4 / 3.0e6),
+    )(place, *arrays, *ties)
 
 
 class Sum:
-    def __init__(self, parts):
+    def __init__(self, arrays, first=0, last=None):
+        self.views = []
         bits = lax.axis_size("ba").bit_length() - 1
-        self.parts = [part.reshape(part.shape[:1] + (2,) * bits + part.shape[2:]) for part in parts]
-        self.ways = ["z"] + list(reversed(range(bits)))
+        for array in arrays:
+            groups, parts, rows, _ = array.shape
+            ways = [("z", groups, parts * rows)] + [(bit, 2, rows << bit) for bit in reversed(range(bits))]
+            end = rows if last is None else last
+            self.views.append(View(array.reshape(-1, LANES), first, ways, [], end - first))
 
     def leaving(self, way, step):
-        return total(picked(self.parts, along(way) ^ step, self.ways.index(way)))
-
-    def keep(self, way, got):
-        self.parts = picked(self.parts, along(way), self.ways.index(way)) + got
-        self.ways.remove(way)
-
-    def result(self):
-        return total(self.parts)
+        return [view.fix(way, step) for view in self.views]
+
+    def keep(self, way, arrived):
+        self.views = [view.fix(way, 0) for view in self.views]
+        for array, start in arrived:
+            stride, ways = self.views[0].rows, []
+            for name, size, _ in reversed(self.views[0].ways):
+                ways.insert(0, (name, size, stride))
+                stride *= size
+            self.views.append(View(array, start, ways, [], self.views[0].rows))
+
+
+class Rider:
+    def __init__(self, views):
+        self.views = views
+
+    def leaving(self, way, step):
+        return self.views
+
+    def keep(self, way, arrived):
+        rows = self.views[0].size()
+        self.views = self.views + [View(array, start, [], [], rows) for array, start in arrived]
+
+    def settle(self, array, start=0):
+        self.views = [View(array, start, [], [], self.views[0].size())]
 
 
 class Stage:
-    def __init__(self, sums, way, riders=()):
-        self.sums, self.way, self.riders = sums, way, list(riders)
+    def __init__(self, sums, way):
+        self.sums, self.way = sums, way
         self.steps = range(1, lax.axis_size("ha") // 2) if way == "z" else [1]
-        self.shapes, self.leaving = [], []
-        for step in self.steps:
-            leaving = [one.leaving(way, step) for one in sums]
-            self.shapes = [part.shape for part in leaving]
-            flat = [part.reshape(-1, LANES) for part in leaving] + self.riders
-            self.leaving.append(flat[0] if len(flat) == 1 else jnp.concatenate(flat, axis=0))
-
-    def go(self):
+
+    def groups(self):
+        return [[one.leaving(self.way, step) for one in self.sums] for step in self.steps]
+
+    def go(self, payloads):
         axis, unit = ("ha", 2) if self.way == "z" else ("ba", 1 << self.way)
-        arrived = [exchange(part, axis, unit * step) for step, part in zip(self.steps, self.leaving)]
+        arrived = [exchange(part, axis, unit * step) for step, part in zip(self.steps, payloads)]
         row = 0
-        for one, shape in zip(self.sums, self.shapes):
-            rows = 1
-            for size in shape[:-1]:
-                rows *= size
-            one.keep(self.way, [part[row : row + rows].reshape(shape) for part in arrived])
+        for one in self.sums:
+            rows = sum(view.size() for view in one.leaving(self.way, 1)[:1])
+            if isinstance(one, Rider):
+                one.settle(payloads[0], row)
+            one.keep(self.way, [(part, row) for part in arrived])
             row += rows
-        for k, rider in enumerate(self.riders):
-            self.riders[k] = total([rider] + [part[row : row + rider.shape[0]] for part in arrived])
-            row += rider.shape[0]
-        return self.riders
-
-
-def half_of(rows):
-    core = lax.axis_index("ha") % 2
-    both = rows.reshape(2, rows.shape[0] // 2, rows.shape[1])
-    return total(picked([both], core, 0) + [exchange(picked([both], 1 - core, 0)[0], "ha", 1)])
-
-
-def with_other_half(mine):
-    core = lax.axis_index("ha") % 2
-    other = exchange(mine, "ha", 1)
-    return jnp.concatenate([jnp.where(core == 0, mine, other), jnp.where(core == 0, other, mine)], axis=0)
-
-
-def beside(rows, tall, width):
-    parts = [rows[k * tall : (k + 1) * tall] for k in range(lane_blocks(width))]
-    return jnp.concatenate(parts, axis=1)[:, :width]
+        return arrived
+
+
+def run(place, stages, ties=(), extra=()):
+    groups = [group for stage in stages for group in stage.groups()]
+    made = combine(place, groups + list(extra), ties)
+    rest, arrived = made, []
+    for stage in stages:
+        count = len(stage.steps)
+        arrived += stage.go(rest[:count])
+        rest = rest[count:]
+    return made, rest, arrived
 
 
 def neighbour_rows(top, bottom):
@@ -708,8 +799,35 @@
     return lax.ppermute(bottom, "ha", up), lax.ppermute(top, "ha", down)
 
 
-def after(values, token):
-    return values + 0.0 * token[0, 0]
+def lay_out(ha, values, outs, blocks):
+    first, second, up, down, out, small, small_other, packed, packed_other = values
+    din_ref, dup_ref, ddown_ref, dout_ref, dk_ref, gain_ref = outs[:6]
+    whole_in = jnp.concatenate([first, second], axis=0)
+    for value, ref in ((whole_in, din_ref), (up, dup_ref), (down, ddown_ref), (out, dout_ref)):
+        tall, width = ref.shape
+        for k in range(lane_blocks(width)):
+            columns = slice(k * LANES, min(width, (k + 1) * LANES))
+            ref[:, columns] = value[k * tall : (k + 1) * tall, : columns.stop - columns.start]
+    mine = ha % 2 == 0
+    dkern, packed = (
+        jnp.concatenate([jnp.where(mine, own, other), jnp.where(mine, other, own)], axis=0)
+        for own, other in ((small, small_other), (packed, packed_other))
+    )
+    tall = dkern.shape[0] // blocks
+    joined = jnp.concatenate([dkern[k * tall : k * tall + TAPS] for k in range(blocks)], axis=1)
+    dk_ref[...] = joined[:, joined.shape[1] - dk_ref.shape[1] :]
+    dim = gain_ref.shape[1]
+    vectors = [(gain_ref, dkern, (blocks - 1) * tall + TAPS)]
+    vectors += [(ref, packed, k * dim // LANES) for k, ref in enumerate(outs[6:9])]
+    for ref, rows, start in vectors:
+        for k in range(dim // LANES):
+            ref[:, k * LANES : (k + 1) * LANES] = rows[start + k : start + k + 1]
+    row = packed.shape[0]
+    for ref in reversed(outs[9:]):
+        tall, width = ref.shape
+        row -= tall * width // LANES
+        for k in range(width // LANES):
+            ref[:, k * LANES : (k + 1) * LANES] = packed[row + k * tall : row + (k + 1) * tall]
 
 
 def shards(
@@ -737,7 +855,7 @@
     count_ha, count_ba = lax.axis_size("ha"), lax.axis_size("ba")
     hidden = weight_up.shape[1]
     blocks = weight_in.shape[1] // LANES
-    place = lax.axis_index("ha")[None]
+    place = jnp.stack([lax.axis_index("ha"), lax.axis_index("ba")])
     own = canvas.reshape(cells, dim)
     gates = (gate_first, gate_second, gate_third)
     gain = first_gain[None]
@@ -756,64 +874,77 @@
     )
     above, below = neighbour_rows(dconv_top, dconv_bottom)
 
-    def back(first_block, end_block, before, written, ties):
-        return backward(
-            place, ids, above, dconv, below, joined, depth_kernel, own, gain, dmiddle, before,
-            weight_in, first_block, end_block, written, ties, rows, cols, count_ha, count_ba,
-        )
-
     up = Sum([up_kept, exchange(up_sent, "ha", 1)])
     down = Sum([down_kept, exchange(down_sent, "ha", 1)])
     out = Sum([out_kept, exchange(out_sent, "ha", 1)])
-    packed = packed_kept + exchange(packed_sent, "ha", 1)
-    stages = [Stage([up], order[0]), Stage([down, out], turned[0])]
-    cut = blocks * 3 // 4
-    dnorm, *written = back(0, cut, dmiddle, [], stages[0].leaving + stages[1].leaving)
-    for stage in stages:
-        stage.go()
-    z_steps = [2 << k for k in range((count_ha // 2).bit_length() - 1)]
-    packed = after(packed + exchange(packed, "ha", z_steps[0]), dnorm)
-    stages = [Stage([up], order[1]), Stage([down, out], turned[1])]
-    dcanvas, in_kept, in_sent, dkern = back(
-        cut, blocks, dnorm, written, stages[0].leaving + stages[1].leaving + [packed]
+    packed = plain(packed_kept) + plain(exchange(packed_sent, "ha", 1))
+    made, (packed,), _ = run(place, [Stage([up], order[0]), Stage([down, out], turned[0])], extra=[[packed]])
+    ring = [[2 * z + core for z in range(count_ha // 2)] for core in range(2)]
+    packed = lax.psum(packed, "ha", axis_index_groups=ring)
+    dcanvas, in_kept, in_sent, dgain_one = backward(
+        place, ids, above, dconv, below, depth_kernel, own, gain, dmiddle, weight_in, made,
+        rows, cols, count_ha, count_ba,
     )
-    for stage in stages:
-        stage.go()
-    for step in z_steps[1:]:
-        packed = after(packed + exchange(packed, "ha", step), dcanvas)
+    in_got = exchange(in_sent, "ha", 1)
+    made, _, _ = run(place, [Stage([up], order[1]), Stage([down, out], turned[1])], ties=[dcanvas])
+    small_kept, small_sent = kernel_grad(place, ids, above, dconv, below, joined, dgain_one, made, rows, cols, dim)
+    small = Rider(plain(small_kept) + plain(exchange(small_sent, "ha", 1)))
     for first, second in zip(order[2:], turned[2:]):
-        Stage([up], first).go()
-        Stage([down, out], second).go()
-    Stage([up, down, out], "z").go()
-    parts = [in_kept, exchange(in_sent, "ha", 1)]
+        run(place, [Stage([up], first), Stage([down, out], second)])
+    ahead, _, arrived = run(place, [Stage([up, down, out], "z")], ties=[small_kept])
     middle_row = in_kept.shape[2] // 2
-    in_first = Sum([part[:, :, :middle_row] for part in parts])
-    in_second = Sum([part[:, :, middle_row:] for part in parts])
-    small = half_of(dkern.reshape(-1, LANES))
+    in_first = Sum([in_kept, in_got], 0, middle_row)
+    in_second = Sum([in_kept, in_got], middle_row)
+    packed = Rider(plain(packed))
     for first, second in zip(order, turned):
-        (small,) = Stage([in_first], first, [small]).go()
-        (packed,) = Stage([in_second], second, [packed]).go()
-    sums = [after(one.result(), small) for one in (up, down, out)]
-    (small,) = Stage([in_first, in_second], "z", [small]).go()
-    din = jnp.concatenate([in_first.result(), in_second.result()], axis=0)
-    dup, ddown, dout = sums
-    dscale_one, dgain_two, dscale_two, dfirst, dsecond, dthird, dkern, dgain_one = unpack(
-        with_other_half(packed), with_other_half(small).reshape(dkern.shape), gates, depth_kernel, dim
+        run(place, [Stage([in_first, small], first), Stage([in_second, packed], second)], ties=ahead)
+        ahead = arrived[: len(arrived) * 2 // 3]
+    _, (packed, up, down, out), _ = run(
+        place,
+        [Stage([in_first, in_second, small], "z")],
+        extra=[[packed.views], [up.views], [down.views], [out.views]],
+    )
+    (small,) = combine(place, [[small.views]])
+    din, dup, ddown, dout, dkern, dgain_one, dscale_one, dgain_two, dscale_two, dfirst, dsecond, dthird = combine(
+        place,
+        [
+            [
+                in_first.views,
+                in_second.views,
+                plain(up),
+                plain(down),
+                plain(out),
+                plain(small),
+                plain(exchange(small, "ha", 1)),
+                plain(packed),
+                plain(exchange(packed, "ha", 1)),
+            ]
+        ],
+        epilogue=functools.partial(lay_out, blocks=blocks),
+        out_shape=[
+            shape_of(dim // count_ba, weight_in.shape[1] // count_ha),
+            shape_of(dim // count_ba, hidden // count_ha),
+            shape_of(dim // count_ha, hidden // count_ba),
+            shape_of(dim // count_ha, dim // count_ba),
+            shape_of(*depth_kernel.shape),
+        ]
+        + [shape_of(1, dim)] * 4
+        + [shape_of(*gate.shape) for gate in gates],
     )
     return (
         output.reshape(canvas.shape),
         dcanvas.reshape(canvas.shape),
         dgain_one[0],
-        beside(din, dim // count_ba, weight_in.shape[1] // count_ha),
+        din,
         dkern,
         dfirst,
         dsecond,
         dthird,
-        beside(dout, dim // count_ha, dim // count_ba).T,
+        dout.T,
         dscale_one[0],
         dgain_two[0],
-        beside(dup, dim // count_ba, hidden // count_ha),
-        beside(ddown, dim // count_ha, hidden // count_ba).T,
+        dup,
+        ddown.T,
         dscale_two[0],
     )
 

time: 213 us -> 235 us (1.10)
  Pallas kernels: 92.5 us -> 125 us
  other arithmetic: 25.1 us -> 0.64 us
  waiting for transfers between devices: 38.4 us -> 54.5 us
  between operations: 3.09 us -> 14.2 us
  local copies, waits for them, and re-layouts: 11.8 us -> 1.92 us
  starting transfers between devices: 41.1 us -> 38 us
    pallas_call x3 -> x10, Pallas kernels: 36.4 us -> 68.3 us  [the longest x8 30.4 us: combine(): pl.pallas_call(kernel, in_specs=[in_smem()] + [in_hbm()] * (len(arrays) +...]
    add x31 -> x0, other arithmetic: 17.7 us -> none  [the longest x27 13.3 us: total(): result = result + part]
    psum x0 -> x1, waiting for transfers between devices: none -> 9.53 us  [shards(): packed = lax.psum(packed, 'ha', axis_index_groups=ring)]
    slice x15 -> x0, local copies, waits for them, and re-layouts: 8.61 us -> none  [the longest x8 4.31 us: go(): part[row:row + rows].reshape(shape)]
    ppermute x24 -> x22, waiting for transfers between devices: 33.9 us -> 40.4 us  [exchange(): lax.ppermute(values, axis, [(i, i ^ bit) for i in range(lax.axis_size(axi...]
    concatenate x14 -> x0, other arithmetic: 5.18 us -> none  [the longest x10 2.25 us: __init__(): jnp.concatenate(flat, axis=0)]
    ppermute x24 -> x22, starting transfers between devices: 32.9 us -> 29.7 us  [exchange(): lax.ppermute(values, axis, [(i, i ^ bit) for i in range(lax.axis_size(axi...]
  transfers between devices with their start and end apart: 28 -> 27, of which waited for: 10 -> 11; matrix products, arithmetic and copies ran while one was open for 16% -> 0% of each run, Pallas kernels for 16% -> 23%
where the time goes in v4:
time: 235 us; the launch traced here: 234 us
  Pallas kernels  125 us (53%)
  waiting for transfers between devices  54.5 us (23%)
  starting transfers between devices  38 us (16%)
  between operations  14.2 us (6%)
    pallas_call x1, Pallas kernels, forward(): pl.pallas_call(functools.partial(forward_kernel, rows=rows, cols=cols, co...  56.2 us
    ppermute x22, waiting for transfers between devices, exchange(): lax.ppermute(values, axis, [(i, i ^ bit) for i in range(lax.axis_size(axi...  40.4 us
    pallas_call x8, Pallas kernels, combine(): pl.pallas_call(kernel, in_specs=[in_smem()] + [in_hbm()] * (len(arrays) +...  30.4 us
    ppermute x22, starting transfers between devices, exchange(): lax.ppermute(values, axis, [(i, i ^ bit) for i in range(lax.axis_size(axi...  29.7 us
    pallas_call x1, Pallas kernels, backward(): pl.pallas_call(functools.partial(backward_kernel, rows=rows, cols=cols),...  22.1 us
    pallas_call x1, Pallas kernels, kernel_grad(): pl.pallas_call(functools.partial(kernel_grad_kernel, rows=rows, cols=cols...  15.9 us
    psum x1, waiting for transfers between devices, shards(): packed = lax.psum(packed, 'ha', axis_index_groups=ring)  9.53 us
    ppermute x4, starting transfers between devices, neighbour_rows(): return (lax.ppermute(bottom, 'ha', up), lax.ppermute(top, 'ha', down))  8.19 us
  transfers between devices with their start and end apart: 27, of which 11 were waited for; matrix products, arithmetic and copies ran while one was open for 0% of the time, Pallas kernels for 23%

profile of v4, /device:TPU:0, one launch (start us, length us, event | category | flops | bytes accessed | tf_op | source)
XLA Modules:
  0.0 233.8 jit_solution(15047734182250898471)
XLA Ops:
  7.2 1.2 fusion
  8.3 2.4 %collective-permute-start = (f32[192,512]{1,0:T(8,128)S(1)}, f32[192,512]{1,0:T(8,128)S(1)}, u32[]{:S(2)}, u32[]{:S(2)}) collective-permute-start(f32[192,512]{1,0:T(8,128)S(1)} %bitcast.51), channel_id=1, source_target_pairs={{0,4},{4,8},{8,12},{12,16},{16,20},{20,24},{24,28},{1,5},{5,9},{9,... | collective-permute-start | bytes 1179656 | tf_op jit(solution)/shard_map/ppermute | solution.py:799
  10.7 1.3 collective-permute-start.1
  12.0 0.6 pad_add_fusion.place_ref
  12.7 3.8 %collective-permute-done.1.below_ref = f32[192,512]{1,0:T(8,128)S(1)} collective-permute-done((f32[192,512]{1,0:T(8,128)S(1)}, f32[192,512]{1,0:T(8,128)S(1)}, u32[]{:S(2)}, u32[]{:S(2)}) %collective-permute-start.1) | collective-permute-done | bytes 393248 | tf_op jit(solution)/shard_map/ppermute | solution.py:799
  16.5 0.7 copy-done.1
  17.3 56.2 %shard_map.272 = (f32[8,512,128]{2,1,0:T(8,128)}, f32[512,512]{1,0:T(8,128)}, f32[512,512]{1,0:T(8,128)}, f32[8,512,128]{2,1,0:T(8,128)}, f32[8,192,128]{2,1,0:T...) custom-call(s32[2]{0:T(128)} %pad_add_fusion.place_ref, ...), custom_call_target="tpu_custom_call" | custom-call | flops 60500000768 | tf_op jit(solution)/shard_map/pallas_call | solution.py:407
  73.5 6.1 %collective-permute-start.4 = (f32[4,4,256,128]{3,2,1,0:T(8,128)}, f32[4,4,256,128]{3,2,1,0:T(8,128)}, u32[]{:S(2)}, u32[]{:S(2)}) collective-permute-start(f32[4,4,256,128]{3,2,1,0:T(8,128)} %get-tuple-element.71), channel_id=1, source_target_pairs={{0,4},{4,0},{8,12},{12,8},{16,20},{20,16},{24,28},{28,24},{1,5},{5... | collective-permute-start | bytes 6291464 | tf_op jit(solution)/shard_map/ppermute | solution.py:630
  79.6 0.1 collective-permute-start.5
  79.6 0.4 collective-permute-start.7
  80.2 3.2 %collective-permute-start.2 = (f32[8,192,128]{2,1,0:T(8,128)}, f32[8,192,128]{2,1,0:T(8,128)}, u32[]{:S(2)}, u32[]{:S(2)}) collective-permute-start(f32[8,192,128]{2,1,0:T(8,128)} %get-tuple-element.66), channel_id=1, source_target_pairs={{0,4},{4,8},{8,12},{12,16},{16,20},{20,24},{24,28},{1,5},{5,9},{9,... | collective-permute-start | bytes 2359304 | tf_op jit(solution)/shard_map/ppermute | solution.py:799
  83.4 3.8 %collective-permute-done.7.refs_7_ = f32[680,128]{1,0:T(8,128)} collective-permute-done((f32[680,128]{1,0:T(8,128)}, f32[680,128]{1,0:T(8,128)}, u32[]{:S(2)}, u32[]{:S(2)}) %collective-permute-start.7) | collective-permute-done | bytes 348192 | tf_op jit(solution)/shard_map/ppermute | solution.py:630
  87.2 1.3 collective-permute-start.3
  88.5 5.3 %shard_map.273 = (f32[2048,128]{1,0:T(8,128)}, f32[2560,128]{1,0:T(8,128)}, f32[680,128]{1,0:T(8,128)}) custom-call(s32[2]{0:T(128)} %pad_add_fusion.place_ref, f32[4096,128]{1,0:T(8,128)} %bitcast.27, f32[4096,128]{1,0:T(8,128)} %bitcast.13.refs_1_.refs_11_, f32[4096,128]{1,0:T(8,128)} %bitcast.31, f32[4096,128]{1,0:T(8,128)} %bitcast.15.refs_3_.refs_4_.refs_5_.refs_18_, ...), custom_call_target="tpu_custom_call" | custom-call | flops 4078201600 | tf_op jit(solution)/shard_map/pallas_call | solution.py:713
  93.8 1.5 collective-permute-start.9
  95.3 1.5 collective-permute-start.10
  96.9 22.1 %shard_map.274 = (f32[512,512]{1,0:T(8,128)}, f32[4,4,128,128]{3,2,1,0:T(8,128)}, f32[4,4,128,128]{3,2,1,0:T(8,128)}, f32[8,128]{1,0:T(8,128)}) custom-call(s32[2]{0:T(128)} %pad_add_fusion.place_ref, s32[64,64]{1,0:T(8,128)} %bitcast.55, s32[64,64]{1,0:T(8,128)} %bitcast.56, f32[8,192,128]{2,1,0:T(8,128)} %collective-permute-done.2.above_ref, ...), custom_call_target="tpu_custom_call" | custom-call | flops 22000001024 | tf_op jit(solution)/shard_map/pallas_call | solution.py:550
  119.0 0.7 all-reduce.2.cloned.1.call-update
  119.7 4.7 %collective-permute-start.8 = (f32[4,4,128,128]{3,2,1,0:T(8,128)}, f32[4,4,128,128]{3,2,1,0:T(8,128)}, u32[]{:S(2)}, u32[]{:S(2)}) collective-permute-start(f32[4,4,128,128]{3,2,1,0:T(8,128)} %get-tuple-element.83), channel_id=1, source_target_pairs={{0,4},{4,0},{8,12},{12,8},{16,20},{20,16},{24,28},{28,24},{1,5},{5... | collective-permute-start | bytes 3145736 | tf_op jit(solution)/shard_map/ppermute | solution.py:630
  124.3 2.9 %collective-permute-done.10.refs_5_.refs_6_.refs_19_ = f32[2560,128]{1,0:T(8,128)} collective-permute-done((f32[2560,128]{1,0:T(8,128)}, f32[2560,128]{1,0:T(8,128)}, u32[]{:S(2)}, u32[]{:S(2)}) %collective-permute-start.10) | collective-permute-done | bytes 1310752 | tf_op jit(solution)/shard_map/ppermute | solution.py:630
  127.2 4.0 %shard_map.275 = (f32[1024,128]{1,0:T(8,128)}, f32[1280,128]{1,0:T(8,128)}) custom-call(s32[2]{0:T(128)} %pad_add_fusion.place_ref, f32[4096,128]{1,0:T(8,128)} %bitcast.28, f32[4096,128]{1,0:T(8,128)} %bitcast.13.refs_1_.refs_11_, f32[2048,128]{1,0:T(8,128)} %collective-permute-done.9.refs_2_.refs_12_, f32[4096,128]{1,0:T(8,128)} %bitcast.32, ...), custom_call_target="tpu_custom_call" | custom-call | flops 2830150400 | tf_op jit(solution)/shard_map/pallas_call | solution.py:713
  131.2 1.6 collective-permute-start.12
  132.8 0.6 collective-permute-start.13
  133.4 15.9 %shard_map.276 = (f32[224,128]{1,0:T(8,128)}, f32[224,128]{1,0:T(8,128)}) custom-call(s32[2]{0:T(128)} %pad_add_fusion.place_ref, s32[64,64]{1,0:T(8,128)} %bitcast.57, s32[64,64]{1,0:T(8,128)} %bitcast.58, f32[8,192,128]{2,1,0:T(8,128)} %collective-permute-done.2.above_ref, f32[8,512,128]{2,1,0:T(8,128)} %get-tuple-element.67.own_ref, ...), custom_call_target="tpu_custom_call" | custom-call | flops 12099999744 | tf_op jit(solution)/shard_map/pallas_call | solution.py:607
  149.3 0.2 collective-permute-done.13.refs_7_.refs_20_
  149.5 4.0 %shard_map.277 = (f32[576,128]{1,0:T(8,128)}, f32[576,128]{1,0:T(8,128)}, f32[576,128]{1,0:T(8,128)}) custom-call(s32[2]{0:T(128)} %pad_add_fusion.place_ref, f32[4096,128]{1,0:T(8,128)} %bitcast.29, f32[4096,128]{1,0:T(8,128)} %bitcast.13.refs_1_.refs_11_, f32[2048,128]{1,0:T(8,128)} %collective-permute-done.9.refs_2_.refs_12_, ...), custom_call_target="tpu_custom_call" | custom-call | flops 2722016000 | tf_op jit(solution)/shard_map/pallas_call | solution.py:713
  153.5 9.5 %all-reduce.2.cloned.1.call-done.refs_6_ = f32[680,128]{1,0:T(8,128)} async-done(((f32[680,128]{1,0:T(8,128)}), f32[680,128]{1,0:T(8,128)}) %all-reduce.2.cloned.1.call-update) | async-done | bytes 348176 | tf_op jit(solution)/shard_map/psum | solution.py:883
  163.0 3.4 %shard_map.278 = (f32[736,128]{1,0:T(8,128)}, f32[1192,128]{1,0:T(8,128)}) custom-call(s32[2]{0:T(128)} %pad_add_fusion.place_ref, f32[2048,128]{1,0:T(8,128)} %bitcast.39, f32[2048,128]{1,0:T(8,128)} %bitcast.20.refs_1_.refs_5_.refs_8_, f32[224,128]{1,0:T(8,128)} %get-tuple-element.88.refs_10_.refs_2_, f32[224,128]{1,0:T(8,128)} %collective-permute-done.11.refs_3_, ...), custom_call_target="tpu_custom_call" | custom-call | flops 2058190976 | tf_op jit(solution)/shard_map/pallas_call | solution.py:713
  166.5 1.5 collective-permute-start.15
  168.0 1.5 collective-permute-start.14
  169.5 1.6 collective-permute-start.16
  171.1 1.3 collective-permute-start.17
  172.3 9.3 %collective-permute-done.16.refs_8_.refs_14_ = f32[576,128]{1,0:T(8,128)} collective-permute-done((f32[576,128]{1,0:T(8,128)}, f32[576,128]{1,0:T(8,128)}, u32[]{:S(2)}, u32[]{:S(2)}) %collective-permute-start.16) | collective-permute-done | bytes 294944 | tf_op jit(solution)/shard_map/ppermute | solution.py:630
  181.6 3.4 %collective-permute-done.17.refs_9_.refs_15_ = f32[576,128]{1,0:T(8,128)} collective-permute-done((f32[576,128]{1,0:T(8,128)}, f32[576,128]{1,0:T(8,128)}, u32[]{:S(2)}, u32[]{:S(2)}) %collective-permute-start.17) | collective-permute-done | bytes 294944 | tf_op jit(solution)/shard_map/ppermute | solution.py:630
  185.0 3.4 %shard_map.279 = (f32[480,128]{1,0:T(8,128)}, f32[936,128]{1,0:T(8,128)}) custom-call(s32[2]{0:T(128)} %pad_add_fusion.place_ref, f32[2048,128]{1,0:T(8,128)} %bitcast.41, f32[2048,128]{1,0:T(8,128)} %bitcast.20.refs_1_.refs_5_.refs_8_, f32[736,128]{1,0:T(8,128)} %collective-permute-done.14.refs_2_, f32[736,128]{1,0:T(8,128)} %get-tuple-element.93.refs_3_, ...), custom_call_target="tpu_custom_call" | custom-call | flops 1993610624 | tf_op jit(solution)/shard_map/pallas_call | solution.py:713
  188.4 0.6 collective-permute-start.19
  189.0 1.6 collective-permute-start.20
  190.7 0.5 collective-permute-start.18
  191.2 6.8 %collective-permute-done.20.refs_16_ = f32[576,128]{1,0:T(8,128)} collective-permute-done((f32[576,128]{1,0:T(8,128)}, f32[576,128]{1,0:T(8,128)}, u32[]{:S(2)}, u32[]{:S(2)}) %collective-permute-start.20) | collective-permute-done | bytes 294944 | tf_op jit(solution)/shard_map/ppermute | solution.py:630
  198.0 4.4 %shard_map.280 = (f32[352,128]{1,0:T(8,128)}, f32[352,128]{1,0:T(8,128)}, f32[352,128]{1,0:T(8,128)}, f32[680,128]{1,0:T(8,128)}, f32[256,128]{1,0:T(8,128)}, /*index=5*/f32[256,128]{1,0:T(8,128)}, f32[64,128]{1,0:T(8,128)}) custom-call(s32[2]{0:T(128)} %pad_add_fusion.place_ref, f32[2048,128]{1,0:T(8,128)} %bitcast.43, ...), custom_call_target="tpu_custom_call" | custom-call | flops 3086969600 | tf_op jit(solution)/shard_map/pallas_call | solution.py:713
  202.4 2.1 collective-permute-start.21
  204.4 1.1 collective-permute-start.22
  205.6 1.4 collective-permute-start.23
  206.9 2.8 %collective-permute-done.21.refs_1_.refs_4_ = f32[352,128]{1,0:T(8,128)} collective-permute-done((f32[352,128]{1,0:T(8,128)}, f32[352,128]{1,0:T(8,128)}, u32[]{:S(2)}, u32[]{:S(2)}) %collective-permute-start.21) | collective-permute-done | bytes 180256 | tf_op jit(solution)/shard_map/ppermute | solution.py:630
  209.8 9.5 %collective-permute-done.22.refs_2_.refs_5_ = f32[352,128]{1,0:T(8,128)} collective-permute-done((f32[352,128]{1,0:T(8,128)}, f32[352,128]{1,0:T(8,128)}, u32[]{:S(2)}, u32[]{:S(2)}) %collective-permute-start.22) | collective-permute-done | bytes 180256 | tf_op jit(solution)/shard_map/ppermute | solution.py:630
  219.3 2.4 %shard_map.281.refs_14_ = f32[224,128]{1,0:T(8,128)} custom-call(s32[2]{0:T(128)} %pad_add_fusion.place_ref, f32[352,128]{1,0:T(8,128)} %get-tuple-element.97.refs_0_, f32[352,128]{1,0:T(8,128)} %collective-permute-done.21.refs_1_.refs_4_, f32[352,128]{1,0:T(8,128)} %collective-permute-done.22.refs_2_.refs_5_, f32[352,128]{1,0:T(8,128)} %collective-permute-done.23.refs_3_.refs_6_), custom_call_target="tpu_custom_call" | custom-call | flops 1310261376 | tf_op jit(solution)/shard_map/pallas_call | solution.py:713
  221.8 1.7 collective-permute-done.24.refs_15_
  223.5 3.4 %shard_map.282 = (f32[128,128]{1,0:T(8,128)}, f32[128,256]{1,0:T(8,128)}, f32[64,512]{1,0:T(8,128)}, f32[64,128]{1,0:T(8,128)}, f32[49,960]{1,0:T(8,128)}, /*ind...) custom-call(s32[2]{0:T(128)} %pad_add_fusion.place_ref, ...), custom_call_target="tpu_custom_call" | custom-call | flops 2187351552 | tf_op jit(solution)/shard_map/pallas_call | solution.py:713
  (24 shorter events, 0.2 us)
Async XLA Ops:
  8.3 4.3 %collective-permute-start = (f32[192,512]{1,0:T(8,128)S(1)}, f32[192,512]{1,0:T(8,128)S(1)}, u32[]{:S(2)}, u32[]{:S(2)}) collective-permute-start(f32[192,512]{1,0:T(8,128)S(1)} %bitcast.51), channel_id=1, source_target_pairs={{0,4},{4,8},{8,12},{12,16},{16,20},{20,24},{24,28},{1,5},{5,9},{9,... | collective-permute-start | bytes 1179656 | tf_op jit(solution)/shard_map/ppermute | solution.py:799
  10.7 5.8 %collective-permute-start.1 = (f32[192,512]{1,0:T(8,128)S(1)}, f32[192,512]{1,0:T(8,128)S(1)}, u32[]{:S(2)}, u32[]{:S(2)}) collective-permute-start(f32[192,512]{1,0:T(8,128)S(1)} %bitcast.50), channel_id=1, source_target_pairs={{4,0},{8,4},{12,8},{16,12},{20,16},{24,20},{28,24},{5,1},{9,5},{13... | collective-permute-start | bytes 1179656 | tf_op jit(solution)/shard_map/ppermute | solution.py:799
  12.7 3.8 %copy-start = (f32[192,512]{1,0:T(8,128)}, f32[192,512]{1,0:T(8,128)S(1)}, u32[]{:S(2)}) copy-start(f32[192,512]{1,0:T(8,128)S(1)} %collective-permute-done.above_ref) | copy-start | bytes 1179652
  16.5 0.7 copy-start.1
  73.5 15.0 %collective-permute-start.4 = (f32[4,4,256,128]{3,2,1,0:T(8,128)}, f32[4,4,256,128]{3,2,1,0:T(8,128)}, u32[]{:S(2)}, u32[]{:S(2)}) collective-permute-start(f32[4,4,256,128]{3,2,1,0:T(8,128)} %get-tuple-element.71), channel_id=1, source_target_pairs={{0,4},{4,0},{8,12},{12,8},{16,20},{20,16},{24,28},{28,24},{1,5},{5... | collective-permute-start | bytes 6291464 | tf_op jit(solution)/shard_map/ppermute | solution.py:630
  79.6 8.9 %collective-permute-start.5 = (f32[4,4,256,128]{3,2,1,0:T(8,128)}, f32[4,4,256,128]{3,2,1,0:T(8,128)}, u32[]{:S(2)}, u32[]{:S(2)}) collective-permute-start(f32[4,4,256,128]{3,2,1,0:T(8,128)} %get-tuple-element.73), channel_id=1, source_target_pairs={{0,4},{4,0},{8,12},{12,8},{16,20},{20,16},{24,28},{28,24},{1,5},{5... | collective-permute-start | bytes 6291464 | tf_op jit(solution)/shard_map/ppermute | solution.py:630
  79.6 7.5 %collective-permute-start.7 = (f32[680,128]{1,0:T(8,128)}, f32[680,128]{1,0:T(8,128)}, u32[]{:S(2)}, u32[]{:S(2)}) collective-permute-start(f32[680,128]{1,0:T(8,128)} %get-tuple-element.77), channel_id=1, source_target_pairs={{0,4},{4,0},{8,12},{12,8},{16,20},{20,16},{24,28},{28,24},{1,5},{5... | collective-permute-start | bytes 1044488 | tf_op jit(solution)/shard_map/ppermute | solution.py:630
  80.1 8.4 %collective-permute-start.6 = (f32[4,4,64,128]{3,2,1,0:T(8,128)}, f32[4,4,64,128]{3,2,1,0:T(8,128)}, u32[]{:S(2)}, u32[]{:S(2)}) collective-permute-start(f32[4,4,64,128]{3,2,1,0:T(8,128)} %get-tuple-element.75), channel_id=1, source_target_pairs={{0,4},{4,0},{8,12},{12,8},{16,20},{20,16},{24,28},{28,24},{1,5},{5... | collective-permute-start | bytes 1572872 | tf_op jit(solution)/shard_map/ppermute | solution.py:630
  80.2 16.7 %collective-permute-start.2 = (f32[8,192,128]{2,1,0:T(8,128)}, f32[8,192,128]{2,1,0:T(8,128)}, u32[]{:S(2)}, u32[]{:S(2)}) collective-permute-start(f32[8,192,128]{2,1,0:T(8,128)} %get-tuple-element.66), channel_id=1, source_target_pairs={{0,4},{4,8},{8,12},{12,16},{16,20},{20,24},{24,28},{1,5},{5,9},{9,... | collective-permute-start | bytes 2359304 | tf_op jit(solution)/shard_map/ppermute | solution.py:799
  87.2 9.7 %collective-permute-start.3 = (f32[8,192,128]{2,1,0:T(8,128)}, f32[8,192,128]{2,1,0:T(8,128)}, u32[]{:S(2)}, u32[]{:S(2)}) collective-permute-start(f32[8,192,128]{2,1,0:T(8,128)} %get-tuple-element.68), channel_id=1, source_target_pairs={{4,0},{8,4},{12,8},{16,12},{20,16},{24,20},{28,24},{5,1},{9,5},{13... | collective-permute-start | bytes 2359304 | tf_op jit(solution)/shard_map/ppermute | solution.py:799
  93.8 30.5 %collective-permute-start.9 = (f32[2048,128]{1,0:T(8,128)}, f32[2048,128]{1,0:T(8,128)}, u32[]{:S(2)}, u32[]{:S(2)}) collective-permute-start(f32[2048,128]{1,0:T(8,128)} %get-tuple-element.78.rest_0_), channel_id=1, source_target_pairs={{0,1},{1,0},{2,3},{3,2},{4,5},{5,4},{6,7},{7,6},{8,9},{9,8},{10,11... | collective-permute-start | bytes 3145736 | tf_op jit(solution)/shard_map/ppermute | solution.py:630
  95.3 31.8 %collective-permute-start.10 = (f32[2560,128]{1,0:T(8,128)}, f32[2560,128]{1,0:T(8,128)}, u32[]{:S(2)}, u32[]{:S(2)}) collective-permute-start(f32[2560,128]{1,0:T(8,128)} %get-tuple-element.79.rest_1_), channel_id=1, source_target_pairs={{0,2},{1,3},{2,0},{3,1},{4,6},{5,7},{6,4},{7,5},{8,10},{9,11},{10,... | collective-permute-start | bytes 3932168 | tf_op jit(solution)/shard_map/ppermute | solution.py:630
  118.9 44.1 %all-reduce.2.cloned.1.call-start = ((), (), s32[]{:S(2)}) async-start(), calls=%async_computation | async-start | bytes 696320 | tf_op jit(solution)/shard_map/psum | solution.py:883
  119.7 43.4 %collective-permute-start.8 = (f32[4,4,128,128]{3,2,1,0:T(8,128)}, f32[4,4,128,128]{3,2,1,0:T(8,128)}, u32[]{:S(2)}, u32[]{:S(2)}) collective-permute-start(f32[4,4,128,128]{3,2,1,0:T(8,128)} %get-tuple-element.83), channel_id=1, source_target_pairs={{0,4},{4,0},{8,12},{12,8},{16,20},{20,16},{24,28},{28,24},{1,5},{5... | collective-permute-start | bytes 3145736 | tf_op jit(solution)/shard_map/ppermute | solution.py:630
  131.2 18.0 %collective-permute-start.12 = (f32[1024,128]{1,0:T(8,128)}, f32[1024,128]{1,0:T(8,128)}, u32[]{:S(2)}, u32[]{:S(2)}) collective-permute-start(f32[1024,128]{1,0:T(8,128)} %get-tuple-element.86.rest_0_), channel_id=1, source_target_pairs={{0,2},{1,3},{2,0},{3,1},{4,6},{5,7},{6,4},{7,5},{8,10},{9,11},{10,... | collective-permute-start | bytes 1572872 | tf_op jit(solution)/shard_map/ppermute | solution.py:630
  132.8 16.7 %collective-permute-start.13 = (f32[1280,128]{1,0:T(8,128)}, f32[1280,128]{1,0:T(8,128)}, u32[]{:S(2)}, u32[]{:S(2)}) collective-permute-start(f32[1280,128]{1,0:T(8,128)} %get-tuple-element.87.rest_1_), channel_id=1, source_target_pairs={{0,1},{1,0},{2,3},{3,2},{4,5},{5,4},{6,7},{7,6},{8,9},{9,8},{10,11... | collective-permute-start | bytes 1966088 | tf_op jit(solution)/shard_map/ppermute | solution.py:630
  149.2 13.8 %collective-permute-start.11 = (f32[224,128]{1,0:T(8,128)}, f32[224,128]{1,0:T(8,128)}, u32[]{:S(2)}, u32[]{:S(2)}) collective-permute-start(f32[224,128]{1,0:T(8,128)} %get-tuple-element.89), channel_id=1, source_target_pairs={{0,4},{4,0},{8,12},{12,8},{16,20},{20,16},{24,28},{28,24},{1,5},{5... | collective-permute-start | bytes 344072 | tf_op jit(solution)/shard_map/ppermute | solution.py:630
  166.5 18.5 %collective-permute-start.15 = (f32[1192,128]{1,0:T(8,128)}, f32[1192,128]{1,0:T(8,128)}, u32[]{:S(2)}, u32[]{:S(2)}) collective-permute-start(f32[1192,128]{1,0:T(8,128)} %get-tuple-element.94.refs_7_), channel_id=1, source_target_pairs={{0,2},{1,3},{2,0},{3,1},{4,6},{5,7},{6,4},{7,5},{8,10},{9,11},{10,... | collective-permute-start | bytes 1830920 | tf_op jit(solution)/shard_map/ppermute | solution.py:630
  168.0 17.0 %collective-permute-start.14 = (f32[736,128]{1,0:T(8,128)}, f32[736,128]{1,0:T(8,128)}, u32[]{:S(2)}, u32[]{:S(2)}) collective-permute-start(f32[736,128]{1,0:T(8,128)} %get-tuple-element.93.refs_3_), channel_id=1, source_target_pairs={{0,1},{1,0},{2,3},{3,2},{4,5},{5,4},{6,7},{7,6},{8,9},{9,8},{10,11... | collective-permute-start | bytes 1130504 | tf_op jit(solution)/shard_map/ppermute | solution.py:630
  169.5 12.1 %collective-permute-start.16 = (f32[576,128]{1,0:T(8,128)}, f32[576,128]{1,0:T(8,128)}, u32[]{:S(2)}, u32[]{:S(2)}) collective-permute-start(f32[576,128]{1,0:T(8,128)} %get-tuple-element.90.refs_7_), channel_id=1, source_target_pairs={{0,8},{4,12},{8,0},{12,4},{16,24},{20,28},{24,16},{28,20},{1,9},{5... | collective-permute-start | bytes 884744 | tf_op jit(solution)/shard_map/ppermute | solution.py:630
  171.1 14.0 %collective-permute-start.17 = (f32[576,128]{1,0:T(8,128)}, f32[576,128]{1,0:T(8,128)}, u32[]{:S(2)}, u32[]{:S(2)}) collective-permute-start(f32[576,128]{1,0:T(8,128)} %get-tuple-element.91.refs_8_), channel_id=1, source_target_pairs={{0,16},{4,20},{8,24},{12,28},{16,0},{20,4},{24,8},{28,12},{1,17},{... | collective-permute-start | bytes 884744 | tf_op jit(solution)/shard_map/ppermute | solution.py:630
  188.4 9.6 %collective-permute-start.19 = (f32[936,128]{1,0:T(8,128)}, f32[936,128]{1,0:T(8,128)}, u32[]{:S(2)}, u32[]{:S(2)}) collective-permute-start(f32[936,128]{1,0:T(8,128)} %get-tuple-element.96.refs_9_), channel_id=1, source_target_pairs={{0,1},{1,0},{2,3},{3,2},{4,5},{5,4},{6,7},{7,6},{8,9},{9,8},{10,11... | collective-permute-start | bytes 1437704 | tf_op jit(solution)/shard_map/ppermute | solution.py:630
  189.0 8.9 %collective-permute-start.20 = (f32[576,128]{1,0:T(8,128)}, f32[576,128]{1,0:T(8,128)}, u32[]{:S(2)}, u32[]{:S(2)}) collective-permute-start(f32[576,128]{1,0:T(8,128)} %get-tuple-element.92.refs_9_), channel_id=1, source_target_pairs={{0,24},{4,28},{8,16},{12,20},{16,8},{20,12},{24,0},{28,4},{1,25},{... | collective-permute-start | bytes 884744 | tf_op jit(solution)/shard_map/ppermute | solution.py:630
  190.7 7.3 %collective-permute-start.18 = (f32[480,128]{1,0:T(8,128)}, f32[480,128]{1,0:T(8,128)}, u32[]{:S(2)}, u32[]{:S(2)}) collective-permute-start(f32[480,128]{1,0:T(8,128)} %get-tuple-element.95.refs_8_), channel_id=1, source_target_pairs={{0,2},{1,3},{2,0},{3,1},{4,6},{5,7},{6,4},{7,5},{8,10},{9,11},{10,... | collective-permute-start | bytes 737288 | tf_op jit(solution)/shard_map/ppermute | solution.py:630
  202.4 7.4 %collective-permute-start.21 = (f32[352,128]{1,0:T(8,128)}, f32[352,128]{1,0:T(8,128)}, u32[]{:S(2)}, u32[]{:S(2)}) collective-permute-start(f32[352,128]{1,0:T(8,128)} %get-tuple-element.97.refs_0_), channel_id=1, source_target_pairs={{0,8},{4,12},{8,0},{12,4},{16,24},{20,28},{24,16},{28,20},{1,9},{5... | collective-permute-start | bytes 540680 | tf_op jit(solution)/shard_map/ppermute | solution.py:630
  204.4 14.9 %collective-permute-start.22 = (f32[352,128]{1,0:T(8,128)}, f32[352,128]{1,0:T(8,128)}, u32[]{:S(2)}, u32[]{:S(2)}) collective-permute-start(f32[352,128]{1,0:T(8,128)} %get-tuple-element.98), channel_id=1, source_target_pairs={{0,16},{4,20},{8,24},{12,28},{16,0},{20,4},{24,8},{28,12},{1,17},{... | collective-permute-start | bytes 540680 | tf_op jit(solution)/shard_map/ppermute | solution.py:630
  205.6 13.7 %collective-permute-start.23 = (f32[352,128]{1,0:T(8,128)}, f32[352,128]{1,0:T(8,128)}, u32[]{:S(2)}, u32[]{:S(2)}) collective-permute-start(f32[352,128]{1,0:T(8,128)} %get-tuple-element.99), channel_id=1, source_target_pairs={{0,24},{4,28},{8,16},{12,20},{16,8},{20,12},{24,0},{28,4},{1,25},{... | collective-permute-start | bytes 540680 | tf_op jit(solution)/shard_map/ppermute | solution.py:630
  206.9 16.5 %collective-permute-start.25 = (f32[680,128]{1,0:T(8,128)}, f32[680,128]{1,0:T(8,128)}, u32[]{:S(2)}, u32[]{:S(2)}) collective-permute-start(f32[680,128]{1,0:T(8,128)} %get-tuple-element.103.refs_16_), channel_id=1, source_target_pairs={{0,4},{4,0},{8,12},{12,8},{16,20},{20,16},{24,28},{28,24},{1,5},{5... | collective-permute-start | bytes 1044488 | tf_op jit(solution)/shard_map/ppermute | solution.py:630
  221.8 1.7 collective-permute-start.24
Sparse Core Ops, SparseCore 0:
  122.1 40.8 all-reduce.1

commit v5 on v4

--- a/solution.py
+++ b/solution.py
@@ -143,9 +143,9 @@
         wide[TAPS + t] = jnp.zeros((8, LANES), F32)
 
 
-def conv_block(row_taps, kern, shifted, wide, out_ref, rows, cols, turned=False):
+def conv_block(row_taps, kern, shifted, wide, out_ref, rows, cols):
     groups = cols // 8
-    spread_taps(kern, wide, turned)
+    spread_taps(kern, wide, False)
 
     def pair(h, _):
         r = 2 * h
@@ -169,17 +169,24 @@
     lax.fori_loop(0, rows // 2, pair, 0)
 
 
-def kernel_grad_block(row_taps, shifted, dk, mix_ref, dk_ref, rows, cols):
+def conv_grad_block(row_taps, kern, shifted, wide, dk, mix_ref, out_ref, dk_ref, rows, cols):
     groups = cols // 8
+    spread_taps(kern, wide, True)
     for t in range(TAPS):
         dk[t] = jnp.zeros((8, LANES), F32)
 
     def one(r, _):
-        mix = mix_ref[pl.ds(pl.multiple_of(r * cols, cols), cols), :].reshape(groups, 8, LANES)
+        start = pl.ds(pl.multiple_of(r * cols, cols), cols)
+        mix = mix_ref[start, :].reshape(groups, 8, LANES)
+        total = jnp.zeros((groups, 8, LANES), F32)
         for i in range(KERN):
-            same = jnp.where(row_taps[r, i + 1] < KERN, 1.0, 0.0).astype(F32)
+            row = row_taps[r, i + 1]
+            same = jnp.where(row < KERN, 1.0, 0.0).astype(F32)
             for b in range(KERN):
-                dk[i * KERN + b] += jnp.sum(mix * shifted[b, r + i], axis=0) * same
+                x = shifted[b, r + i]
+                total = total + wide[row * KERN + b][None] * x
+                dk[i * KERN + b] += jnp.sum(mix * x, axis=0) * same
+        out_ref[start, :] = total.reshape(cols, LANES)
         return 0
 
     lax.fori_loop(0, rows, one, 0)
@@ -202,15 +209,15 @@
             ref[z, p, k * tall : (k + 1) * tall, :] = part
 
 
-def share_columns(core, grad, kept_ref, sent_ref, width):
-    groups, parts = kept_ref.shape[:2]
+def share_columns(core, grad, kept_ref, sent_ref, width, plane_first=False):
+    groups, parts = reversed(kept_ref.shape[:2]) if plane_first else kept_ref.shape[:2]
     tall = grad.shape[0] // parts
     for z in range(groups):
         for p in range(parts):
             rows = slice(p * tall, (p + 1) * tall)
             first = grad[rows, 2 * z * width : (2 * z + 1) * width]
             second = grad[rows, (2 * z + 1) * width : (2 * z + 2) * width]
-            share(core, first, second, kept_ref, sent_ref, z, p)
+            share(core, first, second, kept_ref, sent_ref, *((p, z) if plane_first else (z, p)))
 
 
 def share_rows(core, grad, kept_ref, sent_ref, tall):
@@ -229,8 +236,8 @@
     first_gain_ref, first_scale_ref, second_gain_ref, second_scale_ref,
     in_ref, kern_ref, one_ref, two_ref, three_ref, out_ref, up_ref, down_ref,
     joined_ref, output_ref, dmiddle_ref, dconv_ref, dconv_top_ref, dconv_bottom_ref,
-    up_kept_ref, up_sent_ref, down_kept_ref, down_sent_ref, out_kept_ref, out_sent_ref,
-    packed_kept_ref, packed_sent_ref,
+    plane_kept_ref, plane_sent_ref, line_kept_ref, line_sent_ref, packed_kept_ref, packed_sent_ref,
+    up_kept, up_sent, down_kept, down_sent, out_kept, out_sent, sems,
     row_taps, padded, valid_ref, one_keep_ref, two_keep_ref, col_ref, packed_ref, normed, flat, shifted, laid, wide, conv, mixed_ref, mapped_ref, middle_ref, result, dnorm,
     *, rows, cols, count_ha, count_ba,
 ):
@@ -245,6 +252,37 @@
     head_steps = blocks // 2
     ffn_first = head_steps + blocks
     gate_refs = (one_ref, two_ref, three_ref)
+    ffn_steps = up_kept.shape[0]
+
+    def chunk_copies(place):
+        copies = []
+        sides = ((up_kept, down_kept, plane_kept_ref, line_kept_ref), (up_sent, down_sent, plane_sent_ref, line_sent_ref))
+        for up, down, plane, line in sides:
+            cut = plane.shape[2] // 2
+            rest = up.shape[3] - cut
+            zs = pl.ds(place * up.shape[1], up.shape[1])
+            bas = pl.ds(place * down.shape[2], down.shape[2])
+            copies += [
+                (up.at[place, :, ba, pl.ds(0, cut), :], plane.at[ba, zs, pl.ds(0, cut), :])
+                for ba in range(plane.shape[0])
+            ]
+            copies += [
+                (down.at[place, z, :, pl.ds(0, cut), :], plane.at[bas, z, pl.ds(cut, cut), :])
+                for z in range(plane.shape[1])
+            ]
+            copies.append((up.at[place, :, :, pl.ds(cut, rest), :], line.at[zs, :, pl.ds(0, rest), :]))
+            copies.append((down.at[place, :, :, pl.ds(cut, rest), :], line.at[:, bas, pl.ds(rest, rest), :]))
+        return [
+            pltpu.make_async_copy(source, target, sems.at[place, k]) for k, (source, target) in enumerate(copies)
+        ]
+
+    def out_copies():
+        copies = []
+        for k, (source, line) in enumerate(((out_kept, line_kept_ref), (out_sent, line_sent_ref))):
+            rows_out = source.shape[2]
+            target = line.at[:, :, pl.ds(line.shape[2] - rows_out, rows_out), :]
+            copies.append(pltpu.make_async_copy(source, target, sems.at[ffn_steps, k]))
+        return copies
 
     @pl.when(step == 0)
     def _():
@@ -312,9 +350,16 @@
         hidden = pre * cdf
         result[...] += dot(hidden, down_ref[...])
         grad_pre = dot(grad_result, down_ref[...], NT) * slope
-        share_rows(core, dot(grad_result, hidden, TN), down_kept_ref, down_sent_ref, dim // count_ha)
-        width = down_ref.shape[0] // (2 * up_kept_ref.shape[0])
-        share_columns(core, dot(normed[:cells], grad_pre, TN), up_kept_ref, up_sent_ref, width)
+        place = step - ffn_first
+        for ref in (up_kept, up_sent, down_kept, down_sent):
+            assert ref.shape[0] == ffn_steps
+        share_rows(
+            core, dot(grad_result, hidden, TN), down_kept.at[place], down_sent.at[place], dim // count_ha
+        )
+        width = down_ref.shape[0] // (2 * up_kept.shape[1])
+        share_columns(core, dot(normed[:cells], grad_pre, TN), up_kept.at[place], up_sent.at[place], width)
+        for copy in chunk_copies(place):
+            copy.start()
         dnorm[...] += dot(grad_pre, up_ref[...], NT)
 
     @pl.when(step == pl.num_programs(0) - 1)
@@ -330,7 +375,9 @@
         start = mixed_ref.shape[1] - out_ref.shape[0]
         crossed = dot(mixed_ref[:, start:], kept, TN)
         dscale_one = jnp.sum(crossed * out_ref[...], axis=0, keepdims=True)
-        share_rows(core, (crossed * first_scale_ref[...]).T, out_kept_ref, out_sent_ref, dim // count_ha)
+        share_rows(core, (crossed * first_scale_ref[...]).T, out_kept, out_sent, dim // count_ha)
+        for copy in out_copies():
+            copy.start()
         grad = dot(kept * first_scale_ref[...], out_ref[...], NT)
         row = packed_ref.shape[0]
         start = blocks * LANES
@@ -360,6 +407,11 @@
         packed_sent_ref[...] = packed_ref[pl.ds(pl.multiple_of((1 - core) * half, 8), half), :]
         dconv_top_ref[...] = dconv_ref[:, :reach, :]
         dconv_bottom_ref[...] = dconv_ref[:, cells - reach :, :]
+        for copy in out_copies():
+            copy.wait()
+        for place in range(ffn_steps):
+            for copy in chunk_copies(place):
+                copy.wait()
 
 
 def mask_scratch(ids, rows):
@@ -371,9 +423,13 @@
     ]
 
 
-def packed_rows(gates, dim):
+def packed_rows(gates, dim, parts):
     rows = sum(gate.size for gate in gates) // LANES + 3 * dim // LANES
-    return -(-rows // 16) * 16
+    return -(-rows // (8 * parts)) * 8 * parts
+
+
+def plane_share(rows):
+    return max(rows * 13 // 16 // 8 * 8, 8)
 
 
 def forward(
@@ -398,11 +454,14 @@
     down_rows = dim // count_ha * lane_blocks(down_wide)
     out_rows = dim // count_ha * lane_blocks(dim // count_ba)
     half = count_ha // 2
-    up_spec = pl.BlockSpec((chunk // (2 * up_wide), count_ba, up_rows, LANES), lambda i: (ffn_step(i), 0, 0, 0))
-    down_spec = pl.BlockSpec((half, chunk // down_wide, down_rows, LANES), lambda i: (0, ffn_step(i), 0, 0))
-    out_shape = (half, count_ba, out_rows, LANES)
-    packed_shape = (packed_rows(gates, dim), LANES)
+    assert up_rows == down_rows
+    cut = plane_share(up_rows)
+    rest = up_rows - cut
+    plane = (count_ba, half, 2 * cut, LANES)
+    line = (half, count_ba, 2 * rest + out_rows, LANES)
+    packed_shape = (packed_rows(gates, dim, count_ha), LANES)
     half_packed = (packed_shape[0] // 2, LANES)
+    copies = 2 * (count_ba + half + 2)
     cells_ext = cells + 2 * reach
     return pl.pallas_call(
         functools.partial(forward_kernel, rows=rows, cols=cols, count_ha=count_ha, count_ba=count_ba),
@@ -427,12 +486,10 @@
             whole((blocks, cells, LANES)),
             whole((blocks, reach, LANES)),
             whole((blocks, reach, LANES)),
-            up_spec,
-            up_spec,
-            down_spec,
-            down_spec,
-            whole(out_shape),
-            whole(out_shape),
+            in_hbm(),
+            in_hbm(),
+            in_hbm(),
+            in_hbm(),
             whole(half_packed),
             whole(half_packed),
         ],
@@ -443,16 +500,23 @@
             shape_of(blocks, cells, LANES),
             shape_of(blocks, reach, LANES),
             shape_of(blocks, reach, LANES),
-            shape_of(half, count_ba, up_rows, LANES),
-            shape_of(half, count_ba, up_rows, LANES),
-            shape_of(half, count_ba, down_rows, LANES),
-            shape_of(half, count_ba, down_rows, LANES),
-            shape_of(*out_shape),
-            shape_of(*out_shape),
+            shape_of(*plane),
+            shape_of(*plane),
+            shape_of(*line),
+            shape_of(*line),
             shape_of(*half_packed),
             shape_of(*half_packed),
         ],
-        scratch_shapes=mask_scratch(ids, rows)
+        scratch_shapes=[
+            pltpu.VMEM((ffn_steps, chunk // (2 * up_wide), count_ba, up_rows, LANES), F32),
+            pltpu.VMEM((ffn_steps, chunk // (2 * up_wide), count_ba, up_rows, LANES), F32),
+            pltpu.VMEM((ffn_steps, half, chunk // down_wide, down_rows, LANES), F32),
+            pltpu.VMEM((ffn_steps, half, chunk // down_wide, down_rows, LANES), F32),
+            pltpu.VMEM((half, count_ba, out_rows, LANES), F32),
+            pltpu.VMEM((half, count_ba, out_rows, LANES), F32),
+            pltpu.SemaphoreType.DMA((ffn_steps + 1, copies)),
+        ]
+        + mask_scratch(ids, rows)
         + [
             pltpu.VMEM((cells, LANES), F32),
             pltpu.VMEM((cells, LANES), F32),
@@ -488,17 +552,17 @@
 
 
 def backward_kernel(
-    place_ref, ids_scalar, ids_ref, above_ref, own_ref, below_ref, kern_ref, canvas_ref, gain_ref,
+    place_ref, ids_scalar, ids_ref, above_ref, own_ref, below_ref, mix_ref, kern_ref, canvas_ref, gain_ref,
     dmiddle_ref, in_ref, *rest, rows, cols,
 ):
-    dcanvas_ref, kept_ref, sent_ref, dgain_ref = rest[-15:-11]
-    row_taps, padded, valid_ref, col_ref, flat, shifted, laid, wide, djoined, normed, dnorm = rest[-11:]
+    dcanvas_ref, kept_ref, sent_ref, small_kept_ref, small_sent_ref = rest[-18:-13]
+    row_taps, padded, valid_ref, col_ref, flat, shifted, laid, wide, dk, sums, djoined, normed, dnorm = rest[-13:]
     step = pl.program_id(0)
     cells = rows * cols
     reach = REACH * cols
     core = place_ref[0] % 2
     split = laid.shape[0] * LANES - kern_ref.shape[1]
-    width = in_ref.shape[1] // (2 * kept_ref.shape[0])
+    width = in_ref.shape[1] // (2 * kept_ref.shape[1])
 
     @pl.when(step == 0)
     def _():
@@ -512,21 +576,25 @@
 
     lay_flat(above_ref, own_ref, below_ref, flat)
     fill_shifted(flat, col_ref, shifted, rows + 2 * REACH, cols)
-    conv_block(row_taps, laid[step], shifted, wide, djoined.at[step % 2], rows, cols, turned=True)
+    conv_grad_block(
+        row_taps, laid[step], shifted, wide, dk, mix_ref.at[0], djoined.at[step % 2], sums.at[step], rows, cols
+    )
 
     @pl.when(step % 2 == 1)
     def _():
         grad = jnp.concatenate([djoined[0], djoined[1]], axis=1)
-        share_columns(core, dot(normed[...], grad, TN), kept_ref, sent_ref, width)
+        share_columns(core, dot(normed[...], grad, TN), kept_ref, sent_ref, width, plane_first=True)
         dnorm[...] += dot(grad, in_ref[...], NT)
 
     @pl.when(step == pl.num_programs(0) - 1)
     def _():
         hat, scale = normalized(canvas_ref[...] * valid_ref[reach : reach + cells, :1])
         dgain = jnp.sum(dnorm[...] * hat, axis=0, keepdims=True)
-        dgain_ref[...] = jnp.zeros_like(dgain_ref)
+        count = sums.shape[0]
         for k in range(dgain.shape[1] // LANES):
-            dgain_ref[k : k + 1] = dgain[:, k * LANES : (k + 1) * LANES]
+            sums[count - 1, TAPS + k : TAPS + k + 1] = dgain[:, k * LANES : (k + 1) * LANES]
+        for ref, start in ((small_kept_ref, core * (count // 2)), (small_sent_ref, (1 - core) * (count // 2))):
+            ref[...] = sums[pl.ds(start, count // 2)].reshape(ref.shape)
         inner = dmiddle_ref[...] + norm_backward(dnorm[...] * gain_ref[...], hat, scale)
         dcanvas_ref[...] = inner * valid_ref[reach : reach + cells, :1]
 
@@ -536,7 +604,7 @@
 
 
 def backward(
-    place, ids, above, own, below, kern, canvas, gain, dmiddle, weight_in, ties, rows, cols, count_ha, count_ba
+    place, ids, above, own, below, mix, kern, canvas, gain, dmiddle, weight_in, ties, rows, cols, count_ha, count_ba
 ):
     cells, dim = canvas.shape
     blocks = own.shape[0]
@@ -544,20 +612,21 @@
     own_wide = weight_in.shape[1] // count_ha
     chunk_rows = dim // count_ba * lane_blocks(own_wide)
     groups = 2 * LANES // (2 * own_wide)
-    chunk_spec = pl.BlockSpec((groups, count_ba, chunk_rows, LANES), lambda i: (i // 2, 0, 0, 0))
-    chunks = shape_of(count_ha // 2, count_ba, chunk_rows, LANES)
-    gain_shape = (-(-dim // LANES // 8) * 8, LANES)
+    chunk_spec = pl.BlockSpec((count_ba, groups, chunk_rows, LANES), lambda i: (0, i // 2, 0, 0))
+    chunks = shape_of(count_ba, count_ha // 2, chunk_rows, LANES)
+    tall = -(-(TAPS + dim // LANES) // 8) * 8
+    small = (blocks // 2 * tall, LANES)
     return pl.pallas_call(
         functools.partial(backward_kernel, rows=rows, cols=cols),
         grid=(blocks,),
         in_specs=[in_smem(), in_smem(), whole(ids.shape)]
-        + [block_of(size) for size in (reach, cells, reach)]
+        + [block_of(size) for size in (reach, cells, reach, cells)]
         + [whole(kern.shape), whole(canvas.shape)]
         + [whole((1, dim)), whole((cells, dim))]
         + [pl.BlockSpec((dim, 2 * LANES), lambda i: (0, i // 2))]
         + [in_hbm()] * len(ties),
-        out_specs=[whole((cells, dim)), chunk_spec, chunk_spec, whole(gain_shape)],
-        out_shape=[shape_of(cells, dim), chunks, chunks, shape_of(*gain_shape)],
+        out_specs=[whole((cells, dim)), chunk_spec, chunk_spec, whole(small), whole(small)],
+        out_shape=[shape_of(cells, dim), chunks, chunks, shape_of(*small), shape_of(*small)],
         scratch_shapes=mask_scratch(ids, rows)
         + [
             pltpu.VMEM((KERN, cols // 8, 8, LANES), F32),
@@ -565,65 +634,15 @@
             pltpu.VMEM((KERN, rows + 2 * REACH, cols // 8, 8, LANES), F32),
             pltpu.VMEM((blocks, TAPS, LANES), F32),
             pltpu.VMEM((TAPS + KERN, 8, LANES), F32),
+            pltpu.VMEM((TAPS, 8, LANES), F32),
+            pltpu.VMEM((blocks, tall, LANES), F32),
             pltpu.VMEM((2, cells, LANES), F32),
             pltpu.VMEM((cells, dim), F32),
             pltpu.VMEM((cells, dim), F32),
         ],
         compiler_params=params(),
-        cost_estimate=lasting(20),
-    )(place, ids, ids, above, own, below, kern, canvas, gain, dmiddle, weight_in, *ties)
-
-
-def kernel_grad_kernel(
-    place_ref, ids_scalar, ids_ref, above_ref, own_ref, below_ref, mix_ref, dgain_ref, *rest, rows, cols
-):
-    kept_ref, sent_ref, row_taps, padded, valid_ref, col_ref, flat, shifted, dk, sums = rest[-10:]
-    step = pl.program_id(0)
-
-    @pl.when(step == 0)
-    def _():
-        conv_masks(ids_scalar, ids_ref, place_ref[0], row_taps, col_ref, rows)
-
-    lay_flat(above_ref, own_ref, below_ref, flat)
-    fill_shifted(flat, col_ref, shifted, rows + 2 * REACH, cols)
-    kernel_grad_block(row_taps, shifted, dk, mix_ref.at[0], sums.at[step], rows, cols)
-
-    @pl.when(step == pl.num_programs(0) - 1)
-    def _():
-        count = sums.shape[0]
-        spare = sums.shape[1] - TAPS
-        sums[count - 1, TAPS:] = dgain_ref[:spare]
-        core = place_ref[0] % 2
-        half = count // 2
-        for ref, start in ((kept_ref, core * half), (sent_ref, (1 - core) * half)):
-            ref[...] = sums[pl.ds(start, half)].reshape(ref.shape)
-
-
-def kernel_grad(place, ids, above, own, below, mix, dgain, ties, rows, cols, dim):
-    blocks, cells, _ = own.shape
-    reach = above.shape[1]
-    tall = -(-(TAPS + dim // LANES) // 8) * 8
-    half = (blocks // 2 * tall, LANES)
-    return pl.pallas_call(
-        functools.partial(kernel_grad_kernel, rows=rows, cols=cols),
-        grid=(blocks,),
-        in_specs=[in_smem(), in_smem(), whole(ids.shape)]
-        + [block_of(size) for size in (reach, cells, reach, cells)]
-        + [whole(dgain.shape)]
-        + [in_hbm()] * len(ties),
-        out_specs=[whole(half), whole(half)],
-        out_shape=[shape_of(*half), shape_of(*half)],
-        scratch_shapes=mask_scratch(ids, rows)
-        + [
-            pltpu.VMEM((KERN, cols // 8, 8, LANES), F32),
-            pltpu.VMEM((cells + 2 * reach + 2 * EDGE, LANES), F32),
-            pltpu.VMEM((KERN, rows + 2 * REACH, cols // 8, 8, LANES), F32),
-            pltpu.VMEM((TAPS, 8, LANES), F32),
-            pltpu.VMEM((blocks, tall, LANES), F32),
-        ],
-        compiler_params=params(),
-        cost_estimate=lasting(11),
-    )(place, ids, ids, above, own, below, mix, dgain, *ties)
+        cost_estimate=lasting(25),
+    )(place, ids, ids, above, own, below, mix, kern, canvas, gain, dmiddle, weight_in, *ties)
 
 
 def exchange(values, axis, bit):
@@ -648,101 +667,134 @@
     def runs(self, ha, ba):
         start = self.start
         for way, step, stride in self.fixed:
-            place = ha // 2 if way == "z" else (ba >> way) & 1
+            place = ha // 2 if way == "line" else ba
             start = start + (place ^ step) * stride
+        rows, ways = self.rows, list(self.ways)
+        while ways and ways[-1][2] == rows:
+            rows *= ways.pop()[1]
         offsets = [0]
-        for _, size, stride in self.ways:
+        for _, size, stride in ways:
             offsets = [offset + k * stride for offset in offsets for k in range(size)]
-        return [pl.multiple_of(start + offset, 8) for offset in offsets]
-
-
-def plain(array):
-    rows = array.reshape(-1, LANES)
-    return [View(rows, 0, [], [], rows.shape[0])]
+        return [pl.multiple_of(start + offset, 8) for offset in offsets], rows
+
+
+def flat_view(array, start=0, rows=None):
+    flat = array.reshape(-1, LANES)
+    return View(flat, start, [], [], flat.shape[0] if rows is None else rows)
 
 
 def combine(place, groups, ties=(), epilogue=None, out_shape=None):
-    pieces = [views for group in groups for views in group]
-    arrays = []
+    pieces, arrays = [], []
+    for group in groups:
+        for views in group:
+            if not any(views is other for other in pieces):
+                pieces.append(views)
     for views in pieces:
         for view in views:
             if not any(view.array is other for other in arrays):
                 arrays.append(view.array)
     index_of = {id(array): k for k, array in enumerate(arrays)}
+    piece_of = {id(views): k for k, views in enumerate(pieces)}
     sizes = [sum(views[0].size() for views in group) for group in groups]
-    copies = sum(view.size() // view.rows for views in pieces for view in views)
-    if epilogue is None:
+    copies = sum(len(view.runs(0, 0)[0]) for views in pieces for view in views)
+    plain = epilogue is None
+    if plain:
         out_shape = [shape_of(size, LANES) for size in sizes]
 
     def kernel(place_ref, *refs):
         inputs = refs[: len(arrays)]
         refs = refs[len(arrays) + len(ties) :]
-        outs, (buffers, sems) = refs[: len(out_shape)], (refs[len(out_shape) : -1], refs[-1])
+        outs, refs = refs[: len(out_shape)], refs[len(out_shape) :]
+        buffers, refs = refs[: len(pieces)], refs[len(pieces) :]
+        sems, results, out_sems = refs[0], refs[1:-1], refs[-1]
         ha, ba = place_ref[0], place_ref[1]
         moves, count = [], 0
         for piece, views in enumerate(pieces):
             moves.append([])
             for term, view in enumerate(views):
                 source = inputs[index_of[id(view.array)]]
-                for k, start in enumerate(view.runs(ha, ba)):
-                    target = buffers[piece].at[term, pl.ds(k * view.rows, view.rows), :]
-                    moves[-1].append(
-                        pltpu.make_async_copy(source.at[pl.ds(start, view.rows), :], target, sems.at[count])
-                    )
-                    moves[-1][-1].start()
+                starts, rows = view.runs(ha, ba)
+                for k, start in enumerate(starts):
+                    target = buffers[piece].at[term, pl.ds(k * rows, rows), :]
+                    move = pltpu.make_async_copy(source.at[pl.ds(start, rows), :], target, sems.at[count])
+                    move.start()
+                    moves[-1].append(move)
                     count += 1
-        piece = 0
-        values = []
+        values, waited, leaving = [], set(), []
         for out, group in enumerate(groups):
             row = 0
             for views in group:
-                for move in moves[piece]:
-                    move.wait()
+                piece = piece_of[id(views)]
+                if piece not in waited:
+                    waited.add(piece)
+                    for move in moves[piece]:
+                        move.wait()
                 value = buffers[piece][0]
                 for term in range(1, len(views)):
                     value = value + buffers[piece][term]
-                if epilogue is None:
-                    outs[out][row : row + value.shape[0], :] = value
+                if plain:
+                    results[out][row : row + value.shape[0], :] = value
                 values.append(value)
                 row += value.shape[0]
-                piece += 1
-        if epilogue is not None:
+            if plain:
+                leaving.append(pltpu.make_async_copy(results[out], outs[out], out_sems.at[out]))
+                leaving[-1].start()
+        if not plain:
             epilogue(ha, values, outs)
+        for move in leaving:
+            move.wait()
 
     moved = sum(view.size() for views in pieces for view in views) + sum(sizes)
+    scratch = [pltpu.VMEM((len(views), views[0].size(), LANES), F32) for views in pieces]
+    scratch.append(pltpu.SemaphoreType.DMA((copies,)))
+    if plain:
+        scratch += [pltpu.VMEM((size, LANES), F32) for size in sizes]
+    scratch.append(pltpu.SemaphoreType.DMA((len(groups),)))
     return pl.pallas_call(
         kernel,
         in_specs=[in_smem()] + [in_hbm()] * (len(arrays) + len(ties)),
-        out_specs=[pl.BlockSpec(memory_space=pltpu.VMEM)] * len(out_shape),
+        out_specs=[in_hbm() if plain else pl.BlockSpec(memory_space=pltpu.VMEM)] * len(out_shape),
         out_shape=out_shape,
-        scratch_shapes=[pltpu.VMEM((len(views), views[0].size(), LANES), F32) for views in pieces]
-        + [pltpu.SemaphoreType.DMA((copies,))],
+        scratch_shapes=scratch,
         compiler_params=params(),
         cost_estimate=lasting(1 + moved * LANES * 4 / 3.0e6),
     )(place, *arrays, *ties)
 
 
+def tied(arrays, ties):
+    return pl.pallas_call(
+        lambda *refs: None,
+        in_specs=[pl.BlockSpec(memory_space=pl.ANY)] * (len(arrays) + len(ties)),
+        out_specs=[pl.BlockSpec(memory_space=pl.ANY)] * len(arrays),
+        out_shape=[shape_of(*array.shape) for array in arrays],
+        input_output_aliases={k: k for k in range(len(arrays))},
+        compiler_params=params(),
+    )(*arrays, *ties)
+
+
 class Sum:
-    def __init__(self, arrays, first=0, last=None):
+    def __init__(self, arrays, names):
         self.views = []
-        bits = lax.axis_size("ba").bit_length() - 1
+        sizes = {"line": lax.axis_size("ha") // 2, "plane": lax.axis_size("ba")}
         for array in arrays:
-            groups, parts, rows, _ = array.shape
-            ways = [("z", groups, parts * rows)] + [(bit, 2, rows << bit) for bit in reversed(range(bits))]
-            end = rows if last is None else last
-            self.views.append(View(array.reshape(-1, LANES), first, ways, [], end - first))
+            flat = array.reshape(-1, LANES)
+            stride, ways = flat.shape[0], []
+            for name in names:
+                stride //= sizes[name]
+                ways.append((name, sizes[name], stride))
+            self.views.append(View(flat, 0, ways, [], stride))
 
     def leaving(self, way, step):
         return [view.fix(way, step) for view in self.views]
 
-    def keep(self, way, arrived):
+    def keep(self, way, sent, arrived):
         self.views = [view.fix(way, 0) for view in self.views]
-        for array, start in arrived:
-            stride, ways = self.views[0].rows, []
-            for name, size, _ in reversed(self.views[0].ways):
-                ways.insert(0, (name, size, stride))
-                stride *= size
-            self.views.append(View(array, start, ways, [], self.views[0].rows))
+        rows = self.views[0].rows
+        ways = [(name, size, rows) for name, size, _ in self.views[0].ways]
+        self.views += [View(array, start, ways, [], rows) for array, start in arrived]
+
+    def part(self, first, rows):
+        return [View(view.array, view.start + first, view.ways, view.fixed, rows) for view in self.views]
 
 
 class Rider:
@@ -752,44 +804,44 @@
     def leaving(self, way, step):
         return self.views
 
-    def keep(self, way, arrived):
+    def keep(self, way, sent, arrived):
         rows = self.views[0].size()
-        self.views = self.views + [View(array, start, [], [], rows) for array, start in arrived]
-
-    def settle(self, array, start=0):
-        self.views = [View(array, start, [], [], self.views[0].size())]
+        self.views = [View(array, start, [], [], rows) for array, start in [sent] + arrived]
+
+
+class Gather(Rider):
+    def keep(self, way, sent, arrived):
+        rows = self.views[0].size()
+        self.gathered = [[View(array, start, [], [], rows)] for array, start in [sent] + arrived]
 
 
 class Stage:
     def __init__(self, sums, way):
         self.sums, self.way = sums, way
-        self.steps = range(1, lax.axis_size("ha") // 2) if way == "z" else [1]
+        self.steps = range(1, lax.axis_size("ha") // 2 if way == "line" else lax.axis_size("ba"))
 
     def groups(self):
         return [[one.leaving(self.way, step) for one in self.sums] for step in self.steps]
 
     def go(self, payloads):
-        axis, unit = ("ha", 2) if self.way == "z" else ("ba", 1 << self.way)
+        axis, unit = ("ha", 2) if self.way == "line" else ("ba", 1)
         arrived = [exchange(part, axis, unit * step) for step, part in zip(self.steps, payloads)]
         row = 0
         for one in self.sums:
-            rows = sum(view.size() for view in one.leaving(self.way, 1)[:1])
-            if isinstance(one, Rider):
-                one.settle(payloads[0], row)
-            one.keep(self.way, [(part, row) for part in arrived])
+            rows = one.leaving(self.way, 1)[0].size()
+            one.keep(self.way, (payloads[0], row), [(part, row) for part in arrived])
             row += rows
         return arrived
 
 
-def run(place, stages, ties=(), extra=()):
+def run(place, stages):
     groups = [group for stage in stages for group in stage.groups()]
-    made = combine(place, groups + list(extra), ties)
+    made = combine(place, groups)
     rest, arrived = made, []
     for stage in stages:
-        count = len(stage.steps)
-        arrived += stage.go(rest[:count])
-        rest = rest[count:]
-    return made, rest, arrived
+        arrived += stage.go(rest[: len(stage.steps)])
+        rest = rest[len(stage.steps) :]
+    return made, arrived
 
 
 def neighbour_rows(top, bottom):
@@ -799,35 +851,53 @@
     return lax.ppermute(bottom, "ha", up), lax.ppermute(top, "ha", down)
 
 
-def lay_out(ha, values, outs, blocks):
-    first, second, up, down, out, small, small_other, packed, packed_other = values
-    din_ref, dup_ref, ddown_ref, dout_ref, dk_ref, gain_ref = outs[:6]
-    whole_in = jnp.concatenate([first, second], axis=0)
-    for value, ref in ((whole_in, din_ref), (up, dup_ref), (down, ddown_ref), (out, dout_ref)):
-        tall, width = ref.shape
-        for k in range(lane_blocks(width)):
-            columns = slice(k * LANES, min(width, (k + 1) * LANES))
-            ref[:, columns] = value[k * tall : (k + 1) * tall, : columns.stop - columns.start]
+def lay_beside(value, ref):
+    tall, width = ref.shape
+    for k in range(lane_blocks(width)):
+        columns = slice(k * LANES, min(width, (k + 1) * LANES))
+        ref[:, columns] = value[k * tall : (k + 1) * tall, : columns.stop - columns.start]
+
+
+def lay_large(ha, values, outs):
+    up_first, up_second, down_first, down_second, out = values
+    lay_beside(jnp.concatenate([up_first, up_second], axis=0), outs[0])
+    lay_beside(jnp.concatenate([down_first, down_second], axis=0), outs[1])
+    lay_beside(out, outs[2])
+
+
+def lay_small(ha, values, outs, blocks):
+    din_ref, dk_ref, gain_ref = outs[:3]
+    scratch = outs[-1]
+    lay_beside(values[0], din_ref)
+    own, other = values[1], values[2]
+    small_rows = blocks // 2 * (-(-(TAPS + gain_ref.shape[1] // LANES) // 8) * 8)
     mine = ha % 2 == 0
-    dkern, packed = (
-        jnp.concatenate([jnp.where(mine, own, other), jnp.where(mine, other, own)], axis=0)
-        for own, other in ((small, small_other), (packed, packed_other))
-    )
+    first, second = jnp.where(mine, own, other), jnp.where(mine, other, own)
+    dkern = jnp.concatenate([first[:small_rows], second[:small_rows]], axis=0)
     tall = dkern.shape[0] // blocks
     joined = jnp.concatenate([dkern[k * tall : k * tall + TAPS] for k in range(blocks)], axis=1)
     dk_ref[...] = joined[:, joined.shape[1] - dk_ref.shape[1] :]
+    half = own.shape[0] - small_rows
+    count = lax.axis_size("ha") // 2
+    part = half // count
+    for core, rows in ((0, first), (1, second)):
+        for step in range(count):
+            start = core * half + ((ha // 2) ^ step) * part
+            source = small_rows + step * part
+            scratch[pl.ds(pl.multiple_of(start, 8), part), :] = rows[source : source + part]
     dim = gain_ref.shape[1]
-    vectors = [(gain_ref, dkern, (blocks - 1) * tall + TAPS)]
-    vectors += [(ref, packed, k * dim // LANES) for k, ref in enumerate(outs[6:9])]
-    for ref, rows, start in vectors:
-        for k in range(dim // LANES):
-            ref[:, k * LANES : (k + 1) * LANES] = rows[start + k : start + k + 1]
-    row = packed.shape[0]
-    for ref in reversed(outs[9:]):
+    for k in range(dim // LANES):
+        columns = slice(k * LANES, (k + 1) * LANES)
+        row = (blocks - 1) * tall + TAPS + k
+        gain_ref[:, columns] = dkern[row : row + 1]
+        for vector, ref in enumerate(outs[3:6]):
+            ref[:, columns] = scratch[vector * dim // LANES + k : vector * dim // LANES + k + 1, :]
+    row = scratch.shape[0]
+    for ref in reversed(outs[6:-1]):
         tall, width = ref.shape
         row -= tall * width // LANES
         for k in range(width // LANES):
-            ref[:, k * LANES : (k + 1) * LANES] = packed[row + k * tall : row + (k + 1) * tall]
+            ref[:, k * LANES : (k + 1) * LANES] = scratch[row + k * tall : row + (k + 1) * tall, :]
 
 
 def shards(
@@ -860,76 +930,61 @@
     gates = (gate_first, gate_second, gate_third)
     gain = first_gain[None]
     vectors = (gain, scale_first[None], second_gain[None], scale_second[None])
-    order = list(range(count_ba.bit_length() - 1))
-    turned = order[len(order) // 2 :] + order[: len(order) // 2]
-
     ids = image_id[0]
     above, below = neighbour_rows(own[:reach], own[cells - reach :])
     (
-        joined, output, dmiddle, dconv, dconv_top, dconv_bottom, up_kept, up_sent, down_kept, down_sent,
-        out_kept, out_sent, packed_kept, packed_sent,
+        joined, output, dmiddle, dconv, dconv_top, dconv_bottom, plane_kept, plane_sent, line_kept, line_sent,
+        packed_kept, packed_sent,
     ) = forward(
         place, ids, keep_first, keep_second, above, own, below, cotangent.reshape(cells, dim), vectors,
         weight_in, depth_kernel, gates, weight_out, weight_up, weight_down, rows, cols, count_ha, count_ba,
     )
     above, below = neighbour_rows(dconv_top, dconv_bottom)
 
-    up = Sum([up_kept, exchange(up_sent, "ha", 1)])
-    down = Sum([down_kept, exchange(down_sent, "ha", 1)])
-    out = Sum([out_kept, exchange(out_sent, "ha", 1)])
-    packed = plain(packed_kept) + plain(exchange(packed_sent, "ha", 1))
-    made, (packed,), _ = run(place, [Stage([up], order[0]), Stage([down, out], turned[0])], extra=[[packed]])
-    ring = [[2 * z + core for z in range(count_ha // 2)] for core in range(2)]
-    packed = lax.psum(packed, "ha", axis_index_groups=ring)
-    dcanvas, in_kept, in_sent, dgain_one = backward(
-        place, ids, above, dconv, below, depth_kernel, own, gain, dmiddle, weight_in, made,
+    plane_sum = Sum([plane_kept, exchange(plane_sent, "ha", 1)], ["plane", "line"])
+    line_sum = Sum([line_kept, exchange(line_sent, "ha", 1)], ["line", "plane"])
+    packed = Sum([packed_kept, exchange(packed_sent, "ha", 1)], ["line"])
+    made, arrived = run(place, [Stage([line_sum, packed], "line"), Stage([plane_sum], "plane")])
+    dcanvas, in_kept, in_sent, small_kept, small_sent = backward(
+        place, ids, above, dconv, below, joined, depth_kernel, own, gain, dmiddle, weight_in, made,
         rows, cols, count_ha, count_ba,
     )
-    in_got = exchange(in_sent, "ha", 1)
-    made, _, _ = run(place, [Stage([up], order[1]), Stage([down, out], turned[1])], ties=[dcanvas])
-    small_kept, small_sent = kernel_grad(place, ids, above, dconv, below, joined, dgain_one, made, rows, cols, dim)
-    small = Rider(plain(small_kept) + plain(exchange(small_sent, "ha", 1)))
-    for first, second in zip(order[2:], turned[2:]):
-        run(place, [Stage([up], first), Stage([down, out], second)])
-    ahead, _, arrived = run(place, [Stage([up, down, out], "z")], ties=[small_kept])
-    middle_row = in_kept.shape[2] // 2
-    in_first = Sum([in_kept, in_got], 0, middle_row)
-    in_second = Sum([in_kept, in_got], middle_row)
-    packed = Rider(plain(packed))
-    for first, second in zip(order, turned):
-        run(place, [Stage([in_first, small], first), Stage([in_second, packed], second)], ties=ahead)
-        ahead = arrived[: len(arrived) * 2 // 3]
-    _, (packed, up, down, out), _ = run(
-        place,
-        [Stage([in_first, in_second, small], "z")],
-        extra=[[packed.views], [up.views], [down.views], [out.views]],
-    )
-    (small,) = combine(place, [[small.views]])
-    din, dup, ddown, dout, dkern, dgain_one, dscale_one, dgain_two, dscale_two, dfirst, dsecond, dthird = combine(
+    in_sent, small_sent = tied([in_sent, small_sent], arrived[1:])
+    in_sum = Sum([in_kept, exchange(in_sent, "ha", 1)], ["plane", "line"])
+    small = Rider([flat_view(small_kept), flat_view(exchange(small_sent, "ha", 1))])
+    packed = Rider(packed.views)
+    run(place, [Stage([plane_sum, small], "line"), Stage([line_sum, in_sum, packed], "plane")])
+    packed = Gather(packed.views)
+    run(place, [Stage([in_sum, packed], "line"), Stage([small], "plane")])
+    cut = plane_sum.views[0].rows // 2
+    rest = (line_sum.views[0].rows - dim // count_ha * lane_blocks(dim // count_ba)) // 2
+    dup, ddown, dout = combine(
         place,
         [
             [
-                in_first.views,
-                in_second.views,
-                plain(up),
-                plain(down),
-                plain(out),
-                plain(small),
-                plain(exchange(small, "ha", 1)),
-                plain(packed),
-                plain(exchange(packed, "ha", 1)),
+                plane_sum.part(0, cut),
+                line_sum.part(0, rest),
+                plane_sum.part(cut, cut),
+                line_sum.part(rest, rest),
+                line_sum.part(2 * rest, line_sum.views[0].rows - 2 * rest),
             ]
         ],
-        epilogue=functools.partial(lay_out, blocks=blocks),
+        epilogue=lay_large,
         out_shape=[
-            shape_of(dim // count_ba, weight_in.shape[1] // count_ha),
             shape_of(dim // count_ba, hidden // count_ha),
             shape_of(dim // count_ha, hidden // count_ba),
             shape_of(dim // count_ha, dim // count_ba),
-            shape_of(*depth_kernel.shape),
-        ]
+        ],
+    )
+    (halves_of,) = combine(place, [[small.views] + packed.gathered])
+    din, dkern, dgain_one, dscale_one, dgain_two, dscale_two, dfirst, dsecond, dthird, _ = combine(
+        place,
+        [[in_sum.views, [flat_view(halves_of)], [flat_view(exchange(halves_of, "ha", 1))]]],
+        epilogue=functools.partial(lay_small, blocks=blocks),
+        out_shape=[shape_of(dim // count_ba, weight_in.shape[1] // count_ha), shape_of(*depth_kernel.shape)]
         + [shape_of(1, dim)] * 4
-        + [shape_of(*gate.shape) for gate in gates],
+        + [shape_of(*gate.shape) for gate in gates]
+        + [shape_of(packed_rows(gates, dim, count_ha), LANES)],
     )
     return (
         output.reshape(canvas.shape),

time: 235 us -> 212 us (0.902)
  Pallas kernels: 125 us -> 108 us
  between operations: 14.2 us -> 0.97 us
  waiting for transfers between devices: 54.5 us -> 64.1 us
    ppermute x22 -> x24, waiting for transfers between devices: 40.4 us -> 60.2 us  [exchange(): lax.ppermute(values, axis, [(i, i ^ bit) for i in range(lax.axis_size(axi...]
    pallas_call x1, Pallas kernels: 15.9 us -> 0.01 us  [tied(): pl.pallas_call(lambda *refs: None, in_specs=[pl.BlockSpec(memory_space=pl...]
    psum x1 -> x0, waiting for transfers between devices: 9.53 us -> none  [shards(): packed = lax.psum(packed, 'ha', axis_index_groups=ring)]
    pallas_call x1, Pallas kernels: 22.1 us -> 29.1 us  [backward(): pl.pallas_call(functools.partial(backward_kernel, rows=rows, cols=cols),...]
    pallas_call x8 -> x6, Pallas kernels: 30.4 us -> 23.9 us  [combine(): pl.pallas_call(kernel, in_specs=[in_smem()] + [in_hbm()] * (len(arrays) +...]
    ppermute x22 -> x24, starting transfers between devices: 29.7 us -> 27.9 us  [exchange(): lax.ppermute(values, axis, [(i, i ^ bit) for i in range(lax.axis_size(axi...]
  transfers between devices with their start and end apart: 27 -> 28, of which waited for: 11 -> 10; matrix products, arithmetic and copies ran while one was open for 0% -> 0% of each run, Pallas kernels for 23% -> 18%
where the time goes in v5:
time: 212 us; the launch traced here: 211 us
  Pallas kernels  108 us (51%)
  waiting for transfers between devices  64.1 us (30%)
  starting transfers between devices  35.7 us (17%)
    ppermute x24, waiting for transfers between devices, exchange(): lax.ppermute(values, axis, [(i, i ^ bit) for i in range(lax.axis_size(axi...  60.2 us
    pallas_call x1, Pallas kernels, forward(): pl.pallas_call(functools.partial(forward_kernel, rows=rows, cols=cols, co...  55 us
    pallas_call x1, Pallas kernels, backward(): pl.pallas_call(functools.partial(backward_kernel, rows=rows, cols=cols),...  29.1 us
    ppermute x24, starting transfers between devices, exchange(): lax.ppermute(values, axis, [(i, i ^ bit) for i in range(lax.axis_size(axi...  27.9 us
    pallas_call x6, Pallas kernels, combine(): pl.pallas_call(kernel, in_specs=[in_smem()] + [in_hbm()] * (len(arrays) +...  23.9 us
    ppermute x4, starting transfers between devices, neighbour_rows(): return (lax.ppermute(bottom, 'ha', up), lax.ppermute(top, 'ha', down))  7.81 us
  transfers between devices with their start and end apart: 28, of which 10 were waited for; matrix products, arithmetic and copies ran while one was open for 0% of the time, Pallas kernels for 18%

profile of v5, /device:TPU:0, one launch (start us, length us, event | category | flops | bytes accessed | tf_op | source)
XLA Modules:
  0.0 211.4 jit_solution(4111873214935011687)
XLA Ops:
  0.6 1.2 fusion
  1.8 2.4 %collective-permute-start = (f32[192,512]{1,0:T(8,128)S(1)}, f32[192,512]{1,0:T(8,128)S(1)}, u32[]{:S(2)}, u32[]{:S(2)}) collective-permute-start(f32[192,512]{1,0:T(8,128)S(1)} %bitcast.37), channel_id=1, source_target_pairs={{0,4},{4,8},{8,12},{12,16},{16,20},{20,24},{24,28},{1,5},{5,9},{9,... | collective-permute-start | bytes 1179656 | tf_op jit(solution)/shard_map/ppermute | solution.py:851
  4.2 1.3 collective-permute-start.1
  5.5 0.6 pad_add_fusion.place_ref
  6.1 3.9 %collective-permute-done.1.below_ref = f32[192,512]{1,0:T(8,128)S(1)} collective-permute-done((f32[192,512]{1,0:T(8,128)S(1)}, f32[192,512]{1,0:T(8,128)S(1)}, u32[]{:S(2)}, u32[]{:S(2)}) %collective-permute-start.1) | collective-permute-done | bytes 393248 | tf_op jit(solution)/shard_map/ppermute | solution.py:851
  10.0 0.7 copy-done.1
  10.7 55.0 %shard_map.272 = (f32[8,512,128]{2,1,0:T(8,128)}, f32[512,512]{1,0:T(8,128)}, f32[512,512]{1,0:T(8,128)}, f32[8,512,128]{2,1,0:T(8,128)}, f32[8,192,128]{2,1,0:T...) custom-call(s32[2]{0:T(128)} %pad_add_fusion.place_ref, ...), custom_call_target="tpu_custom_call" | custom-call | flops 60500000768 | tf_op jit(solution)/shard_map/pallas_call | solution.py:466
  65.8 6.1 %collective-permute-start.6 = (f32[4,4,416,128]{3,2,1,0:T(8,128)}, f32[4,4,416,128]{3,2,1,0:T(8,128)}, u32[]{:S(2)}, u32[]{:S(2)}) collective-permute-start(f32[4,4,416,128]{3,2,1,0:T(8,128)} %get-tuple-element.74), channel_id=1, source_target_pairs={{0,4},{4,0},{8,12},{12,8},{16,20},{20,16},{24,28},{28,24},{1,5},{5... | collective-permute-start | bytes 10223624 | tf_op jit(solution)/shard_map/ppermute | solution.py:649
  71.9 0.1 collective-permute-start.4
  72.0 0.4 collective-permute-start.5
  72.4 2.9 %collective-permute-start.2 = (f32[8,192,128]{2,1,0:T(8,128)}, f32[8,192,128]{2,1,0:T(8,128)}, u32[]{:S(2)}, u32[]{:S(2)}) collective-permute-start(f32[8,192,128]{2,1,0:T(8,128)} %get-tuple-element.64), channel_id=1, source_target_pairs={{0,4},{4,8},{8,12},{12,16},{16,20},{20,24},{24,28},{1,5},{5,9},{9,... | collective-permute-start | bytes 2359304 | tf_op jit(solution)/shard_map/ppermute | solution.py:851
  75.2 1.3 collective-permute-start.3
  76.5 3.7 %collective-permute-done.5.refs_3_.refs_15_ = f32[704,128]{1,0:T(8,128)} collective-permute-done((f32[704,128]{1,0:T(8,128)}, f32[704,128]{1,0:T(8,128)}, u32[]{:S(2)}, u32[]{:S(2)}) %collective-permute-start.5) | collective-permute-done | bytes 360480 | tf_op jit(solution)/shard_map/ppermute | solution.py:649
  80.3 5.8 %shard_map.273 = (f32[816,128]{1,0:T(8,128)}, f32[816,128]{1,0:T(8,128)}, f32[816,128]{1,0:T(8,128)}, f32[1664,128]{1,0:T(8,128)}, f32[1664,128]{1,0:T(8,128)}, /*index=5*/f32[1664,128]{1,0:T(8,128)}) custom-call(s32[2]{0:T(128)} %pad_add_fusion.place_ref, f32[2560,128]{1,0:T(8,128)} %bitcast.28, f32[2560,128]{1,0:T(8,128)} %bitcast.13.refs_1_.refs_8_.refs_9_, ...), custom_call_target="tpu_custom_call" | custom-call | flops 5290208256 | tf_op jit(solution)/shard_map/pallas_call | solution.py:753
  86.1 2.7 %collective-permute-start.7 = (f32[816,128]{1,0:T(8,128)}, f32[816,128]{1,0:T(8,128)}, u32[]{:S(2)}, u32[]{:S(2)}) collective-permute-start(f32[816,128]{1,0:T(8,128)} %get-tuple-element.76.rest_1_), channel_id=1, source_target_pairs={{0,16},{4,20},{8,24},{12,28},{16,0},{20,4},{24,8},{28,12},{1,17},{... | collective-permute-start | bytes 1253384 | tf_op jit(solution)/shard_map/ppermute | solution.py:649
  88.8 1.3 collective-permute-start.8
  90.1 1.5 collective-permute-start.9
  91.6 0.0 collective-permute-done.2.above_ref
  91.6 1.6 collective-permute-start.10
  93.1 0.5 collective-permute-start.11
  93.6 29.1 %shard_map.274 = (f32[512,512]{1,0:T(8,128)}, f32[4,4,128,128]{3,2,1,0:T(8,128)}, f32[4,4,128,128]{3,2,1,0:T(8,128)}, f32[224,128]{1,0:T(8,128)}, f32[224,128]{1,0:T(8,128)}) custom-call(s32[2]{0:T(128)} %pad_add_fusion.place_ref, s32[64,64]{1,0:T(8,128)} %bitcast.42, s32[64,64]{1,0:T(8,128)} %bitcast.43, f32[8,192,128]{2,1,0:T(8,128)} %collective-permute-done.2.above_ref, ...), custom_call_target="tpu_custom_call" | custom-call | flops 27499999232 | tf_op jit(solution)/shard_map/pallas_call | solution.py:619
  122.8 7.7 %collective-permute-done.10.refs_5_.refs_3_ = f32[1664,128]{1,0:T(8,128)} collective-permute-done((f32[1664,128]{1,0:T(8,128)}, f32[1664,128]{1,0:T(8,128)}, u32[]{:S(2)}, u32[]{:S(2)}) %collective-permute-start.10) | collective-permute-done | bytes 852000 | tf_op jit(solution)/shard_map/ppermute | solution.py:649
  130.5 0.1 collective-permute-start.14
  130.6 0.4 collective-permute-start.13
  131.0 11.9 %collective-permute-done.14.refs_9_.refs_10_ = f32[816,128]{1,0:T(8,128)} collective-permute-done((f32[816,128]{1,0:T(8,128)}, f32[816,128]{1,0:T(8,128)}, u32[]{:S(2)}, u32[]{:S(2)}) %collective-permute-start.14) | collective-permute-done | bytes 417824 | tf_op jit(solution)/shard_map/ppermute | solution.py:649
  142.9 5.3 %shard_map.276 = (f32[640,128]{1,0:T(8,128)}, f32[640,128]{1,0:T(8,128)}, f32[640,128]{1,0:T(8,128)}, f32[848,128]{1,0:T(8,128)}, f32[848,128]{1,0:T(8,128)}, /*index=5*/f32[848,128]{1,0:T(8,128)}) custom-call(s32[2]{0:T(128)} %pad_add_fusion.place_ref, f32[6656,128]{1,0:T(8,128)} %bitcast.26, f32[6656,128]{1,0:T(8,128)} %bitcast.15.refs_5_.refs_1_, ...), custom_call_target="tpu_custom_call" | custom-call | flops 4386084352 | tf_op jit(solution)/shard_map/pallas_call | solution.py:753
  148.2 1.4 collective-permute-start.19
  149.5 1.5 collective-permute-start.16
  151.1 1.2 collective-permute-start.17
  152.3 0.8 collective-permute-start.15
  153.0 1.3 collective-permute-start.20
  154.4 18.4 %collective-permute-done.19.refs_8_.refs_6_ = f32[640,128]{1,0:T(8,128)} collective-permute-done((f32[640,128]{1,0:T(8,128)}, f32[640,128]{1,0:T(8,128)}, u32[]{:S(2)}, u32[]{:S(2)}) %collective-permute-start.19) | collective-permute-done | bytes 327712 | tf_op jit(solution)/shard_map/ppermute | solution.py:649
  172.8 9.8 %collective-permute-done.18.refs_7_.refs_5_ = f32[640,128]{1,0:T(8,128)} collective-permute-done((f32[640,128]{1,0:T(8,128)}, f32[640,128]{1,0:T(8,128)}, u32[]{:S(2)}, u32[]{:S(2)}) %collective-permute-start.18) | collective-permute-done | bytes 327712 | tf_op jit(solution)/shard_map/ppermute | solution.py:649
  182.7 3.2 %shard_map.277 = (f32[304,128]{1,0:T(8,128)}, f32[304,128]{1,0:T(8,128)}, f32[304,128]{1,0:T(8,128)}, f32[224,128]{1,0:T(8,128)}, f32[224,128]{1,0:T(8,128)}, /*index=5*/f32[224,128]{1,0:T(8,128)}) custom-call(s32[2]{0:T(128)} %pad_add_fusion.place_ref, f32[2048,128]{1,0:T(8,128)} %bitcast.32, f32[2048,128]{1,0:T(8,128)} %bitcast.18.refs_13_.refs_1_, ...), custom_call_target="tpu_custom_call" | custom-call | flops 2058190976 | tf_op jit(solution)/shard_map/pallas_call | solution.py:753
  185.9 1.6 collective-permute-start.25
  187.5 1.3 collective-permute-start.22
  188.8 1.4 collective-permute-start.23
  190.2 0.8 collective-permute-start.21
  191.0 1.2 collective-permute-start.26
  192.2 0.7 collective-permute-start.24
  192.9 4.1 %collective-permute-done.26.refs_3_ = f32[224,128]{1,0:T(8,128)} collective-permute-done((f32[224,128]{1,0:T(8,128)}, f32[224,128]{1,0:T(8,128)}, u32[]{:S(2)}, u32[]{:S(2)}) %collective-permute-start.26) | collective-permute-done | bytes 114720 | tf_op jit(solution)/shard_map/ppermute | solution.py:649
  197.0 0.3 collective-permute-done.24.refs_1_
  197.3 3.0 %collective-permute-done.22.refs_6_ = f32[304,128]{1,0:T(8,128)} collective-permute-done((f32[304,128]{1,0:T(8,128)}, f32[304,128]{1,0:T(8,128)}, u32[]{:S(2)}, u32[]{:S(2)}) %collective-permute-start.22) | collective-permute-done | bytes 155680 | tf_op jit(solution)/shard_map/ppermute | solution.py:649
  200.3 1.1 collective-permute-done.21.refs_5_
  201.5 2.7 %shard_map.278.refs_8_ = f32[928,128]{1,0:T(8,128)} custom-call(s32[2]{0:T(128)} %pad_add_fusion.place_ref, f32[224,128]{1,0:T(8,128)} %get-tuple-element.97.refs_0_, f32[224,128]{1,0:T(8,128)} %collective-permute-done.24.refs_1_, f32[224,128]{1,0:T(8,128)} %collective-permute-done.25.refs_2_, f32[224,128]{1,0:T(8,128)} %collective-permute-done.26.refs_3_, ...), custom_call_target="tpu_custom_call" | custom-call | flops 1574589824 | tf_op jit(solution)/shard_map/pallas_call | solution.py:753
  204.2 0.1 collective-permute-start.27
  204.3 3.4 %shard_map.280 = (f32[128,256]{1,0:T(8,128)}, f32[64,512]{1,0:T(8,128)}, f32[64,128]{1,0:T(8,128)}) custom-call(s32[2]{0:T(128)} %pad_add_fusion.place_ref, f32[6656,128]{1,0:T(8,128)} %bitcast.27, f32[6656,128]{1,0:T(8,128)} %bitcast.15.refs_5_.refs_1_, f32[1664,128]{1,0:T(8,128)} %collective-permute-done.9.refs_4_.refs_2_, ...), custom_call_target="tpu_custom_call" | custom-call | flops 2073209600 | tf_op jit(solution)/shard_map/pallas_call | solution.py:753
  207.7 3.5 %shard_map.279 = (f32[128,128]{1,0:T(8,128)}, f32[49,960]{1,0:T(8,128)}, f32[1,512]{1,0:T(1,128)}, f32[1,512]{1,0:T(1,128)}, f32[1,512]{1,0:T(1,128)}, /*index=5...) custom-call(s32[2]{0:T(128)} %pad_add_fusion.place_ref, ...), custom_call_target="tpu_custom_call" | custom-call | flops 2013134976 | tf_op jit(solution)/shard_map/pallas_call | solution.py:753
  (23 shorter events, 0.1 us)
Async XLA Ops:
  1.8 4.3 %collective-permute-start = (f32[192,512]{1,0:T(8,128)S(1)}, f32[192,512]{1,0:T(8,128)S(1)}, u32[]{:S(2)}, u32[]{:S(2)}) collective-permute-start(f32[192,512]{1,0:T(8,128)S(1)} %bitcast.37), channel_id=1, source_target_pairs={{0,4},{4,8},{8,12},{12,16},{16,20},{20,24},{24,28},{1,5},{5,9},{9,... | collective-permute-start | bytes 1179656 | tf_op jit(solution)/shard_map/ppermute | solution.py:851
  4.2 5.8 %collective-permute-start.1 = (f32[192,512]{1,0:T(8,128)S(1)}, f32[192,512]{1,0:T(8,128)S(1)}, u32[]{:S(2)}, u32[]{:S(2)}) collective-permute-start(f32[192,512]{1,0:T(8,128)S(1)} %bitcast.36), channel_id=1, source_target_pairs={{4,0},{8,4},{12,8},{16,12},{20,16},{24,20},{28,24},{5,1},{9,5},{13... | collective-permute-start | bytes 1179656 | tf_op jit(solution)/shard_map/ppermute | solution.py:851
  6.1 3.9 %copy-start = (f32[192,512]{1,0:T(8,128)}, f32[192,512]{1,0:T(8,128)S(1)}, u32[]{:S(2)}) copy-start(f32[192,512]{1,0:T(8,128)S(1)} %collective-permute-done.above_ref) | copy-start | bytes 1179652
  10.0 0.7 copy-start.1
  65.8 14.5 %collective-permute-start.6 = (f32[4,4,416,128]{3,2,1,0:T(8,128)}, f32[4,4,416,128]{3,2,1,0:T(8,128)}, u32[]{:S(2)}, u32[]{:S(2)}) collective-permute-start(f32[4,4,416,128]{3,2,1,0:T(8,128)} %get-tuple-element.74), channel_id=1, source_target_pairs={{0,4},{4,0},{8,12},{12,8},{16,20},{20,16},{24,28},{28,24},{1,5},{5... | collective-permute-start | bytes 10223624 | tf_op jit(solution)/shard_map/ppermute | solution.py:649
  71.9 8.4 %collective-permute-start.4 = (f32[4,4,160,128]{3,2,1,0:T(8,128)}, f32[4,4,160,128]{3,2,1,0:T(8,128)}, u32[]{:S(2)}, u32[]{:S(2)}) collective-permute-start(f32[4,4,160,128]{3,2,1,0:T(8,128)} %get-tuple-element.70), channel_id=1, source_target_pairs={{0,4},{4,0},{8,12},{12,8},{16,20},{20,16},{24,28},{28,24},{1,5},{5... | collective-permute-start | bytes 3932168 | tf_op jit(solution)/shard_map/ppermute | solution.py:649
  72.0 8.3 %collective-permute-start.5 = (f32[704,128]{1,0:T(8,128)}, f32[704,128]{1,0:T(8,128)}, u32[]{:S(2)}, u32[]{:S(2)}) collective-permute-start(f32[704,128]{1,0:T(8,128)} %get-tuple-element.72), channel_id=1, source_target_pairs={{0,4},{4,0},{8,12},{12,8},{16,20},{20,16},{24,28},{28,24},{1,5},{5... | collective-permute-start | bytes 1081352 | tf_op jit(solution)/shard_map/ppermute | solution.py:649
  72.4 19.2 %collective-permute-start.2 = (f32[8,192,128]{2,1,0:T(8,128)}, f32[8,192,128]{2,1,0:T(8,128)}, u32[]{:S(2)}, u32[]{:S(2)}) collective-permute-start(f32[8,192,128]{2,1,0:T(8,128)} %get-tuple-element.64), channel_id=1, source_target_pairs={{0,4},{4,8},{8,12},{12,16},{16,20},{20,24},{24,28},{1,5},{5,9},{9,... | collective-permute-start | bytes 2359304 | tf_op jit(solution)/shard_map/ppermute | solution.py:851
  75.2 17.9 %collective-permute-start.3 = (f32[8,192,128]{2,1,0:T(8,128)}, f32[8,192,128]{2,1,0:T(8,128)}, u32[]{:S(2)}, u32[]{:S(2)}) collective-permute-start(f32[8,192,128]{2,1,0:T(8,128)} %get-tuple-element.66), channel_id=1, source_target_pairs={{4,0},{8,4},{12,8},{16,12},{20,16},{24,20},{28,24},{5,1},{9,5},{13... | collective-permute-start | bytes 2359304 | tf_op jit(solution)/shard_map/ppermute | solution.py:851
  86.1 36.6 %collective-permute-start.7 = (f32[816,128]{1,0:T(8,128)}, f32[816,128]{1,0:T(8,128)}, u32[]{:S(2)}, u32[]{:S(2)}) collective-permute-start(f32[816,128]{1,0:T(8,128)} %get-tuple-element.76.rest_1_), channel_id=1, source_target_pairs={{0,16},{4,20},{8,24},{12,28},{16,0},{20,4},{24,8},{28,12},{1,17},{... | collective-permute-start | bytes 1253384 | tf_op jit(solution)/shard_map/ppermute | solution.py:649
  88.8 34.0 %collective-permute-start.8 = (f32[816,128]{1,0:T(8,128)}, f32[816,128]{1,0:T(8,128)}, u32[]{:S(2)}, u32[]{:S(2)}) collective-permute-start(f32[816,128]{1,0:T(8,128)} %get-tuple-element.77.rest_2_), channel_id=1, source_target_pairs={{0,24},{4,28},{8,16},{12,20},{16,8},{20,12},{24,0},{28,4},{1,25},{... | collective-permute-start | bytes 1253384 | tf_op jit(solution)/shard_map/ppermute | solution.py:649
  90.1 32.7 %collective-permute-start.9 = (f32[1664,128]{1,0:T(8,128)}, f32[1664,128]{1,0:T(8,128)}, u32[]{:S(2)}, u32[]{:S(2)}) collective-permute-start(f32[1664,128]{1,0:T(8,128)} %get-tuple-element.78.rest_3_), channel_id=1, source_target_pairs={{0,1},{1,0},{2,3},{3,2},{4,5},{5,4},{6,7},{7,6},{8,9},{9,8},{10,11... | collective-permute-start | bytes 2555912 | tf_op jit(solution)/shard_map/ppermute | solution.py:649
  91.6 38.9 %collective-permute-start.10 = (f32[1664,128]{1,0:T(8,128)}, f32[1664,128]{1,0:T(8,128)}, u32[]{:S(2)}, u32[]{:S(2)}) collective-permute-start(f32[1664,128]{1,0:T(8,128)} %get-tuple-element.79.rest_4_), channel_id=1, source_target_pairs={{0,2},{1,3},{2,0},{3,1},{4,6},{5,7},{6,4},{7,5},{8,10},{9,11},{10,... | collective-permute-start | bytes 2555912 | tf_op jit(solution)/shard_map/ppermute | solution.py:649
  93.1 37.4 %collective-permute-start.11 = (f32[1664,128]{1,0:T(8,128)}, f32[1664,128]{1,0:T(8,128)}, u32[]{:S(2)}, u32[]{:S(2)}) collective-permute-start(f32[1664,128]{1,0:T(8,128)} %get-tuple-element.80.rest_5_), channel_id=1, source_target_pairs={{0,3},{1,2},{2,1},{3,0},{4,7},{5,6},{6,5},{7,4},{8,11},{9,10},{10,... | collective-permute-start | bytes 2555912 | tf_op jit(solution)/shard_map/ppermute | solution.py:649
  130.5 12.4 %collective-permute-start.12 = (f32[4,4,128,128]{3,2,1,0:T(8,128)}, f32[4,4,128,128]{3,2,1,0:T(8,128)}, u32[]{:S(2)}, u32[]{:S(2)}) collective-permute-start(f32[4,4,128,128]{3,2,1,0:T(8,128)} %get-tuple-element.85), channel_id=1, source_target_pairs={{0,4},{4,0},{8,12},{12,8},{16,20},{20,16},{24,28},{28,24},{1,5},{5... | collective-permute-start | bytes 3145736 | tf_op jit(solution)/shard_map/ppermute | solution.py:649
  130.5 12.4 %collective-permute-start.14 = (f32[816,128]{1,0:T(8,128)}, f32[816,128]{1,0:T(8,128)}, u32[]{:S(2)}, u32[]{:S(2)}) collective-permute-start(f32[816,128]{1,0:T(8,128)} %get-tuple-element.75.rest_0_), channel_id=1, source_target_pairs={{0,8},{4,12},{8,0},{12,4},{16,24},{20,28},{24,16},{28,20},{1,9},{5... | collective-permute-start | bytes 1253384 | tf_op jit(solution)/shard_map/ppermute | solution.py:649
  130.6 12.3 %collective-permute-start.13 = (f32[224,128]{1,0:T(8,128)}, f32[224,128]{1,0:T(8,128)}, u32[]{:S(2)}, u32[]{:S(2)}) collective-permute-start(f32[224,128]{1,0:T(8,128)} %get-tuple-element.87), channel_id=1, source_target_pairs={{0,4},{4,0},{8,12},{12,8},{16,20},{20,16},{24,28},{28,24},{1,5},{5... | collective-permute-start | bytes 344072 | tf_op jit(solution)/shard_map/ppermute | solution.py:649
  148.2 24.6 %collective-permute-start.19 = (f32[640,128]{1,0:T(8,128)}, f32[640,128]{1,0:T(8,128)}, u32[]{:S(2)}, u32[]{:S(2)}) collective-permute-start(f32[640,128]{1,0:T(8,128)} %get-tuple-element.92), channel_id=1, source_target_pairs={{0,16},{4,20},{8,24},{12,28},{16,0},{20,4},{24,8},{28,12},{1,17},{... | collective-permute-start | bytes 983048 | tf_op jit(solution)/shard_map/ppermute | solution.py:649
  149.5 33.1 %collective-permute-start.16 = (f32[848,128]{1,0:T(8,128)}, f32[848,128]{1,0:T(8,128)}, u32[]{:S(2)}, u32[]{:S(2)}) collective-permute-start(f32[848,128]{1,0:T(8,128)} %get-tuple-element.89), channel_id=1, source_target_pairs={{0,2},{1,3},{2,0},{3,1},{4,6},{5,7},{6,4},{7,5},{8,10},{9,11},{10,... | collective-permute-start | bytes 1302536 | tf_op jit(solution)/shard_map/ppermute | solution.py:649
  151.1 31.6 %collective-permute-start.17 = (f32[848,128]{1,0:T(8,128)}, f32[848,128]{1,0:T(8,128)}, u32[]{:S(2)}, u32[]{:S(2)}) collective-permute-start(f32[848,128]{1,0:T(8,128)} %get-tuple-element.90), channel_id=1, source_target_pairs={{0,3},{1,2},{2,1},{3,0},{4,7},{5,6},{6,5},{7,4},{8,11},{9,10},{10,... | collective-permute-start | bytes 1302536 | tf_op jit(solution)/shard_map/ppermute | solution.py:649
  152.3 30.4 %collective-permute-start.15 = (f32[848,128]{1,0:T(8,128)}, f32[848,128]{1,0:T(8,128)}, u32[]{:S(2)}, u32[]{:S(2)}) collective-permute-start(f32[848,128]{1,0:T(8,128)} %get-tuple-element.88.refs_5_), channel_id=1, source_target_pairs={{0,1},{1,0},{2,3},{3,2},{4,5},{5,4},{6,7},{7,6},{8,9},{9,8},{10,11... | collective-permute-start | bytes 1302536 | tf_op jit(solution)/shard_map/ppermute | solution.py:649
  153.0 19.8 %collective-permute-start.20 = (f32[640,128]{1,0:T(8,128)}, f32[640,128]{1,0:T(8,128)}, u32[]{:S(2)}, u32[]{:S(2)}) collective-permute-start(f32[640,128]{1,0:T(8,128)} %get-tuple-element.93), channel_id=1, source_target_pairs={{0,24},{4,28},{8,16},{12,20},{16,8},{20,12},{24,0},{28,4},{1,25},{... | collective-permute-start | bytes 983048 | tf_op jit(solution)/shard_map/ppermute | solution.py:649
  172.8 9.9 %collective-permute-start.18 = (f32[640,128]{1,0:T(8,128)}, f32[640,128]{1,0:T(8,128)}, u32[]{:S(2)}, u32[]{:S(2)}) collective-permute-start(f32[640,128]{1,0:T(8,128)} %get-tuple-element.91.refs_6_), channel_id=1, source_target_pairs={{0,8},{4,12},{8,0},{12,4},{16,24},{20,28},{24,16},{28,20},{1,9},{5... | collective-permute-start | bytes 983048 | tf_op jit(solution)/shard_map/ppermute | solution.py:649
  185.9 6.3 %collective-permute-start.25 = (f32[224,128]{1,0:T(8,128)}, f32[224,128]{1,0:T(8,128)}, u32[]{:S(2)}, u32[]{:S(2)}) collective-permute-start(f32[224,128]{1,0:T(8,128)} %get-tuple-element.98), channel_id=1, source_target_pairs={{0,2},{1,3},{2,0},{3,1},{4,6},{5,7},{6,4},{7,5},{8,10},{9,11},{10,... | collective-permute-start | bytes 344072 | tf_op jit(solution)/shard_map/ppermute | solution.py:649
  187.5 12.8 %collective-permute-start.22 = (f32[304,128]{1,0:T(8,128)}, f32[304,128]{1,0:T(8,128)}, u32[]{:S(2)}, u32[]{:S(2)}) collective-permute-start(f32[304,128]{1,0:T(8,128)} %get-tuple-element.95), channel_id=1, source_target_pairs={{0,16},{4,20},{8,24},{12,28},{16,0},{20,4},{24,8},{28,12},{1,17},{... | collective-permute-start | bytes 466952 | tf_op jit(solution)/shard_map/ppermute | solution.py:649
  188.8 11.5 %collective-permute-start.23 = (f32[304,128]{1,0:T(8,128)}, f32[304,128]{1,0:T(8,128)}, u32[]{:S(2)}, u32[]{:S(2)}) collective-permute-start(f32[304,128]{1,0:T(8,128)} %get-tuple-element.96), channel_id=1, source_target_pairs={{0,24},{4,28},{8,16},{12,20},{16,8},{20,12},{24,0},{28,4},{1,25},{... | collective-permute-start | bytes 466952 | tf_op jit(solution)/shard_map/ppermute | solution.py:649
  190.2 11.3 %collective-permute-start.21 = (f32[304,128]{1,0:T(8,128)}, f32[304,128]{1,0:T(8,128)}, u32[]{:S(2)}, u32[]{:S(2)}) collective-permute-start(f32[304,128]{1,0:T(8,128)} %get-tuple-element.94.refs_4_), channel_id=1, source_target_pairs={{0,8},{4,12},{8,0},{12,4},{16,24},{20,28},{24,16},{28,20},{1,9},{5... | collective-permute-start | bytes 466952 | tf_op jit(solution)/shard_map/ppermute | solution.py:649
  191.0 6.0 %collective-permute-start.26 = (f32[224,128]{1,0:T(8,128)}, f32[224,128]{1,0:T(8,128)}, u32[]{:S(2)}, u32[]{:S(2)}) collective-permute-start(f32[224,128]{1,0:T(8,128)} %get-tuple-element.99), channel_id=1, source_target_pairs={{0,3},{1,2},{2,1},{3,0},{4,7},{5,6},{6,5},{7,4},{8,11},{9,10},{10,... | collective-permute-start | bytes 344072 | tf_op jit(solution)/shard_map/ppermute | solution.py:649
  192.2 5.1 %collective-permute-start.24 = (f32[224,128]{1,0:T(8,128)}, f32[224,128]{1,0:T(8,128)}, u32[]{:S(2)}, u32[]{:S(2)}) collective-permute-start(f32[224,128]{1,0:T(8,128)} %get-tuple-element.97.refs_0_), channel_id=1, source_target_pairs={{0,1},{1,0},{2,3},{3,2},{4,5},{5,4},{6,7},{7,6},{8,9},{9,8},{10,11... | collective-permute-start | bytes 344072 | tf_op jit(solution)/shard_map/ppermute | solution.py:649
  204.2 3.5 %collective-permute-start.27 = (f32[928,128]{1,0:T(8,128)}, f32[928,128]{1,0:T(8,128)}, u32[]{:S(2)}, u32[]{:S(2)}) collective-permute-start(f32[928,128]{1,0:T(8,128)} %shard_map.278.refs_8_), channel_id=1, source_target_pairs={{0,4},{4,0},{8,12},{12,8},{16,20},{20,16},{24,28},{28,24},{1,5},{5... | collective-permute-start | bytes 1425416 | tf_op jit(solution)/shard_map/ppermute | solution.py:649

commit v6 on v5

--- a/solution.py
+++ b/solution.py
@@ -425,11 +425,11 @@
 
 def packed_rows(gates, dim, parts):
     rows = sum(gate.size for gate in gates) // LANES + 3 * dim // LANES
-    return -(-rows // (8 * parts)) * 8 * parts
+    return -(-rows // (16 * parts)) * 16 * parts
 
 
 def plane_share(rows):
-    return max(rows * 13 // 16 // 8 * 8, 8)
+    return max(rows * 3 // 4 // 8 * 8, 8)
 
 
 def forward(
@@ -459,7 +459,7 @@
     rest = up_rows - cut
     plane = (count_ba, half, 2 * cut, LANES)
     line = (half, count_ba, 2 * rest + out_rows, LANES)
-    packed_shape = (packed_rows(gates, dim, count_ha), LANES)
+    packed_shape = (packed_rows(gates, dim, count_ba), LANES)
     half_packed = (packed_shape[0] // 2, LANES)
     copies = 2 * (count_ba + half + 2)
     cells_ext = cells + 2 * reach
@@ -654,6 +654,9 @@
         self.array, self.start, self.ways, self.fixed, self.rows = array, start, ways, fixed, rows
 
     def fix(self, way, step):
+        if way == "line":
+            near = lax.axis_size("ha") // 4
+            return self.fix("far", step // near).fix("near", step % near)
         left = [entry for entry in self.ways if entry[0] != way]
         (stride,) = [entry[2] for entry in self.ways if entry[0] == way]
         return View(self.array, self.start, left, self.fixed + [(way, step, stride)], self.rows)
@@ -666,9 +669,10 @@
 
     def runs(self, ha, ba):
         start = self.start
+        near = lax.axis_size("ha") // 4
+        places = {"plane": ba, "far": ha // 2 // near, "near": ha // 2 % near}
         for way, step, stride in self.fixed:
-            place = ha // 2 if way == "line" else ba
-            start = start + (place ^ step) * stride
+            start = start + (places[way] ^ step) * stride
         rows, ways = self.rows, list(self.ways)
         while ways and ways[-1][2] == rows:
             rows *= ways.pop()[1]
@@ -740,7 +744,7 @@
                 leaving.append(pltpu.make_async_copy(results[out], outs[out], out_sems.at[out]))
                 leaving[-1].start()
         if not plain:
-            epilogue(ha, values, outs)
+            epilogue(ha, ba, values, outs)
         for move in leaving:
             move.wait()
 
@@ -775,7 +779,8 @@
 class Sum:
     def __init__(self, arrays, names):
         self.views = []
-        sizes = {"line": lax.axis_size("ha") // 2, "plane": lax.axis_size("ba")}
+        near = lax.axis_size("ha") // 4
+        sizes = {"plane": lax.axis_size("ba"), "far": 2, "near": near}
         for array in arrays:
             flat = array.reshape(-1, LANES)
             stride, ways = flat.shape[0], []
@@ -790,7 +795,10 @@
     def keep(self, way, sent, arrived):
         self.views = [view.fix(way, 0) for view in self.views]
         rows = self.views[0].rows
-        ways = [(name, size, rows) for name, size, _ in self.views[0].ways]
+        stride, ways = rows, []
+        for name, size, _ in reversed(self.views[0].ways):
+            ways.insert(0, (name, size, stride))
+            stride *= size
         self.views += [View(array, start, ways, [], rows) for array, start in arrived]
 
     def part(self, first, rows):
@@ -816,21 +824,33 @@
 
 
 class Stage:
-    def __init__(self, sums, way):
-        self.sums, self.way = sums, way
-        self.steps = range(1, lax.axis_size("ha") // 2 if way == "line" else lax.axis_size("ba"))
+    def __init__(self, members, way):
+        self.members, self.way = members, way
+        line, near = lax.axis_size("ha") // 2, lax.axis_size("ha") // 4
+        self.steps = {"plane": range(1, lax.axis_size("ba")), "line": range(1, line), "far": [near]}[way]
+        self.near = near
+
+    def taking(self, step):
+        return [(one, way) for one, way in self.members if way != "near" or step < self.near]
 
     def groups(self):
-        return [[one.leaving(self.way, step) for one in self.sums] for step in self.steps]
+        return [
+            [one.leaving(way, step // self.near if way == "far" else step) for one, way in self.taking(step)]
+            for step in self.steps
+        ]
 
     def go(self, payloads):
-        axis, unit = ("ha", 2) if self.way == "line" else ("ba", 1)
+        axis, unit = ("ba", 1) if self.way == "plane" else ("ha", 2)
         arrived = [exchange(part, axis, unit * step) for step, part in zip(self.steps, payloads)]
-        row = 0
-        for one in self.sums:
-            rows = one.leaving(self.way, 1)[0].size()
-            one.keep(self.way, (payloads[0], row), [(part, row) for part in arrived])
-            row += rows
+        places = {}
+        for step, sent, part in zip(self.steps, payloads, arrived):
+            row = 0
+            for one, way in self.taking(step):
+                places.setdefault(id(one), []).append(((sent, row), (part, row)))
+                row += one.leaving(way, 1)[0].size()
+        for one, way in self.members:
+            mine = places.get(id(one), [])
+            one.keep(way, mine[0][0] if mine else None, [part for _, part in mine])
         return arrived
 
 
@@ -858,14 +878,14 @@
         ref[:, columns] = value[k * tall : (k + 1) * tall, : columns.stop - columns.start]
 
 
-def lay_large(ha, values, outs):
+def lay_large(ha, ba, values, outs):
     up_first, up_second, down_first, down_second, out = values
     lay_beside(jnp.concatenate([up_first, up_second], axis=0), outs[0])
     lay_beside(jnp.concatenate([down_first, down_second], axis=0), outs[1])
     lay_beside(out, outs[2])
 
 
-def lay_small(ha, values, outs, blocks):
+def lay_small(ha, ba, values, outs, blocks):
     din_ref, dk_ref, gain_ref = outs[:3]
     scratch = outs[-1]
     lay_beside(values[0], din_ref)
@@ -878,11 +898,11 @@
     joined = jnp.concatenate([dkern[k * tall : k * tall + TAPS] for k in range(blocks)], axis=1)
     dk_ref[...] = joined[:, joined.shape[1] - dk_ref.shape[1] :]
     half = own.shape[0] - small_rows
-    count = lax.axis_size("ha") // 2
+    count = lax.axis_size("ba")
     part = half // count
     for core, rows in ((0, first), (1, second)):
         for step in range(count):
-            start = core * half + ((ha // 2) ^ step) * part
+            start = core * half + (ba ^ step) * part
             source = small_rows + step * part
             scratch[pl.ds(pl.multiple_of(start, 8), part), :] = rows[source : source + part]
     dim = gain_ref.shape[1]
@@ -941,21 +961,35 @@
     )
     above, below = neighbour_rows(dconv_top, dconv_bottom)
 
-    plane_sum = Sum([plane_kept, exchange(plane_sent, "ha", 1)], ["plane", "line"])
-    line_sum = Sum([line_kept, exchange(line_sent, "ha", 1)], ["line", "plane"])
-    packed = Sum([packed_kept, exchange(packed_sent, "ha", 1)], ["line"])
-    made, arrived = run(place, [Stage([line_sum, packed], "line"), Stage([plane_sum], "plane")])
+    plane_sum = Sum([plane_kept, exchange(plane_sent, "ha", 1)], ["plane", "far", "near"])
+    line_sum = Sum([line_kept, exchange(line_sent, "ha", 1)], ["far", "near", "plane"])
+    packed = Sum([packed_kept, exchange(packed_sent, "ha", 1)], ["plane"])
+    made, arrived = run(
+        place, [Stage([(line_sum, "far")], "far"), Stage([(plane_sum, "plane"), (packed, "plane")], "plane")]
+    )
     dcanvas, in_kept, in_sent, small_kept, small_sent = backward(
         place, ids, above, dconv, below, joined, depth_kernel, own, gain, dmiddle, weight_in, made,
         rows, cols, count_ha, count_ba,
     )
-    in_sent, small_sent = tied([in_sent, small_sent], arrived[1:])
-    in_sum = Sum([in_kept, exchange(in_sent, "ha", 1)], ["plane", "line"])
+    in_sent, small_sent = tied([in_sent, small_sent], arrived)
+    in_sum = Sum([in_kept, exchange(in_sent, "ha", 1)], ["plane", "far", "near"])
     small = Rider([flat_view(small_kept), flat_view(exchange(small_sent, "ha", 1))])
     packed = Rider(packed.views)
-    run(place, [Stage([plane_sum, small], "line"), Stage([line_sum, in_sum, packed], "plane")])
+    run(
+        place,
+        [
+            Stage([(plane_sum, "line"), (packed, "line"), (line_sum, "near")], "line"),
+            Stage([(in_sum, "plane"), (small, "plane")], "plane"),
+        ],
+    )
     packed = Gather(packed.views)
-    run(place, [Stage([in_sum, packed], "line"), Stage([small], "plane")])
+    run(
+        place,
+        [
+            Stage([(in_sum, "line"), (small, "line")], "line"),
+            Stage([(line_sum, "plane"), (packed, "plane")], "plane"),
+        ],
+    )
     cut = plane_sum.views[0].rows // 2
     rest = (line_sum.views[0].rows - dim // count_ha * lane_blocks(dim // count_ba)) // 2
     dup, ddown, dout = combine(
@@ -984,7 +1018,7 @@
         out_shape=[shape_of(dim // count_ba, weight_in.shape[1] // count_ha), shape_of(*depth_kernel.shape)]
         + [shape_of(1, dim)] * 4
         + [shape_of(*gate.shape) for gate in gates]
-        + [shape_of(packed_rows(gates, dim, count_ha), LANES)],
+        + [shape_of(packed_rows(gates, dim, count_ba), LANES)],
     )
     return (
         output.reshape(canvas.shape),

time: 212 us -> 217 us (1.024)
  starting transfers between devices: 35.7 us -> 45.4 us
  waiting for transfers between devices: 64.1 us -> 59.7 us
    ppermute x24 -> x22, starting transfers between devices: 27.9 us -> 37.5 us  [exchange(): lax.ppermute(values, axis, [(i, i ^ bit) for i in range(lax.axis_size(axi...]
    ppermute x24 -> x22, waiting for transfers between devices: 60.2 us -> 55.9 us  [exchange(): lax.ppermute(values, axis, [(i, i ^ bit) for i in range(lax.axis_size(axi...]
  transfers between devices with their start and end apart: 28 -> 26, of which waited for: 10 -> 9; matrix products, arithmetic and copies ran while one was open for 0% -> 0% of each run, Pallas kernels for 18% -> 18%
where the time goes in v6:
time: 217 us
  Pallas kernels  108 us (50%)
  waiting for transfers between devices  59.7 us (28%)
  starting transfers between devices  45.4 us (21%)
    ppermute x22, waiting for transfers between devices, exchange(): lax.ppermute(values, axis, [(i, i ^ bit) for i in range(lax.axis_size(axi...  55.9 us
    pallas_call x1, Pallas kernels, forward(): pl.pallas_call(functools.partial(forward_kernel, rows=rows, cols=cols, co...  55.1 us
    ppermute x22, starting transfers between devices, exchange(): lax.ppermute(values, axis, [(i, i ^ bit) for i in range(lax.axis_size(axi...  37.5 us
    pallas_call x1, Pallas kernels, backward(): pl.pallas_call(functools.partial(backward_kernel, rows=rows, cols=cols),...  29.2 us
    pallas_call x6, Pallas kernels, combine(): pl.pallas_call(kernel, in_specs=[in_smem()] + [in_hbm()] * (len(arrays) +...  23.7 us
    ppermute x4, starting transfers between devices, neighbour_rows(): return (lax.ppermute(bottom, 'ha', up), lax.ppermute(top, 'ha', down))  7.81 us
  transfers between devices with their start and end apart: 26, of which 9 were waited for; matrix products, arithmetic and copies ran while one was open for 0% of the time, Pallas kernels for 18%

profile of v6, /device:TPU:0, one launch (start us, length us, event | category | flops | bytes accessed | tf_op | source)
XLA Modules:
  0.0 216.5 jit_solution(9495384411184375184)
XLA Ops:
  0.6 1.2 fusion
  1.8 2.4 %collective-permute-start = (f32[192,512]{1,0:T(8,128)S(1)}, f32[192,512]{1,0:T(8,128)S(1)}, u32[]{:S(2)}, u32[]{:S(2)}) collective-permute-start(f32[192,512]{1,0:T(8,128)S(1)} %bitcast.35), channel_id=1, source_target_pairs={{0,4},{4,8},{8,12},{12,16},{16,20},{20,24},{24,28},{1,5},{5,9},{9,... | collective-permute-start | bytes 1179656 | tf_op jit(solution)/shard_map/ppermute | solution.py:871
  4.2 1.3 collective-permute-start.1
  5.5 0.7 pad_add_fusion.place_ref
  6.2 3.8 %collective-permute-done.1.below_ref = f32[192,512]{1,0:T(8,128)S(1)} collective-permute-done((f32[192,512]{1,0:T(8,128)S(1)}, f32[192,512]{1,0:T(8,128)S(1)}, u32[]{:S(2)}, u32[]{:S(2)}) %collective-permute-start.1) | collective-permute-done | bytes 393248 | tf_op jit(solution)/shard_map/ppermute | solution.py:871
  10.0 0.8 copy-done.1
  10.7 55.1 %shard_map.272 = (f32[8,512,128]{2,1,0:T(8,128)}, f32[512,512]{1,0:T(8,128)}, f32[512,512]{1,0:T(8,128)}, f32[8,512,128]{2,1,0:T(8,128)}, f32[8,192,128]{2,1,0:T...) custom-call(s32[2]{0:T(128)} %pad_add_fusion.place_ref, ...), custom_call_target="tpu_custom_call" | custom-call | flops 60500000768 | tf_op jit(solution)/shard_map/pallas_call | solution.py:466
  65.8 6.1 %collective-permute-start.5 = (f32[4,4,384,128]{3,2,1,0:T(8,128)}, f32[4,4,384,128]{3,2,1,0:T(8,128)}, u32[]{:S(2)}, u32[]{:S(2)}) collective-permute-start(f32[4,4,384,128]{3,2,1,0:T(8,128)} %get-tuple-element.70), channel_id=1, source_target_pairs={{0,4},{4,0},{8,12},{12,8},{16,20},{20,16},{24,28},{28,24},{1,5},{5... | collective-permute-start | bytes 9437192 | tf_op jit(solution)/shard_map/ppermute | solution.py:649
  71.9 0.1 collective-permute-start.4
  72.0 0.4 collective-permute-start.6
  72.4 2.9 %collective-permute-start.2 = (f32[8,192,128]{2,1,0:T(8,128)}, f32[8,192,128]{2,1,0:T(8,128)}, u32[]{:S(2)}, u32[]{:S(2)}) collective-permute-start(f32[8,192,128]{2,1,0:T(8,128)} %get-tuple-element.62), channel_id=1, source_target_pairs={{0,4},{4,8},{8,12},{12,16},{16,20},{20,24},{24,28},{1,5},{5,9},{9,... | collective-permute-start | bytes 2359304 | tf_op jit(solution)/shard_map/ppermute | solution.py:871
  75.3 1.3 collective-permute-start.3
  76.5 3.7 %collective-permute-done.6.refs_5_.refs_6_ = f32[704,128]{1,0:T(8,128)} collective-permute-done((f32[704,128]{1,0:T(8,128)}, f32[704,128]{1,0:T(8,128)}, u32[]{:S(2)}, u32[]{:S(2)}) %collective-permute-start.6) | collective-permute-done | bytes 360480 | tf_op jit(solution)/shard_map/ppermute | solution.py:649
  80.3 0.0 collective-permute-done.4
  80.3 0.0 collective-permute-done.5
  80.3 5.4 %shard_map.273 = (f32[1536,128]{1,0:T(8,128)}, f32[1712,128]{1,0:T(8,128)}, f32[1712,128]{1,0:T(8,128)}, f32[1712,128]{1,0:T(8,128)}) custom-call(s32[2]{0:T(128)} %pad_add_fusion.place_ref, f32[3072,128]{1,0:T(8,128)} %bitcast.28, f32[3072,128]{1,0:T(8,128)} %bitcast.13.refs_1_.refs_8_.refs_7_.refs_9_, f32[6144,128]{1,0:T(8,128)} %bitcast.25, ...), custom_call_target="tpu_custom_call" | custom-call | flops 4857670656 | tf_op jit(solution)/shard_map/pallas_call | solution.py:757
  85.7 2.7 %collective-permute-start.7 = (f32[1536,128]{1,0:T(8,128)}, f32[1536,128]{1,0:T(8,128)}, u32[]{:S(2)}, u32[]{:S(2)}) collective-permute-start(f32[1536,128]{1,0:T(8,128)} %get-tuple-element.73.rest_0_), channel_id=1, source_target_pairs={{0,16},{4,20},{8,24},{12,28},{16,0},{20,4},{24,8},{28,12},{1,17},{... | collective-permute-start | bytes 2359304 | tf_op jit(solution)/shard_map/ppermute | solution.py:649
  88.4 1.5 collective-permute-start.8
  89.9 1.5 collective-permute-start.9
  91.4 0.0 collective-permute-done.2.above_ref
  91.4 0.5 collective-permute-start.10
  91.9 0.0 collective-permute-done.3.below_ref
  91.9 29.2 %shard_map.274 = (f32[512,512]{1,0:T(8,128)}, f32[4,4,128,128]{3,2,1,0:T(8,128)}, f32[4,4,128,128]{3,2,1,0:T(8,128)}, f32[224,128]{1,0:T(8,128)}, f32[224,128]{1,0:T(8,128)}) custom-call(s32[2]{0:T(128)} %pad_add_fusion.place_ref, s32[64,64]{1,0:T(8,128)} %bitcast.40, s32[64,64]{1,0:T(8,128)} %bitcast.41, f32[8,192,128]{2,1,0:T(8,128)} %collective-permute-done.2.above_ref, ...), custom_call_target="tpu_custom_call" | custom-call | flops 27499999232 | tf_op jit(solution)/shard_map/pallas_call | solution.py:619
  121.1 3.5 %collective-permute-done.7.refs_2_.refs_9_.refs_8_.refs_10_ = f32[1536,128]{1,0:T(8,128)} collective-permute-done((f32[1536,128]{1,0:T(8,128)}, f32[1536,128]{1,0:T(8,128)}, u32[]{:S(2)}, u32[]{:S(2)}) %collective-permute-start.7) | collective-permute-done | bytes 786464 | tf_op jit(solution)/shard_map/ppermute | solution.py:649
  124.5 5.6 %collective-permute-done.9.refs_4_.refs_3_ = f32[1712,128]{1,0:T(8,128)} collective-permute-done((f32[1712,128]{1,0:T(8,128)}, f32[1712,128]{1,0:T(8,128)}, u32[]{:S(2)}, u32[]{:S(2)}) %collective-permute-start.9) | collective-permute-done | bytes 876576 | tf_op jit(solution)/shard_map/ppermute | solution.py:649
  130.2 0.5 collective-permute-start.12
  130.7 2.7 %collective-permute-done.12.refs_13_ = f32[224,128]{1,0:T(8,128)} collective-permute-done((f32[224,128]{1,0:T(8,128)}, f32[224,128]{1,0:T(8,128)}, u32[]{:S(2)}, u32[]{:S(2)}) %collective-permute-start.12) | collective-permute-done | bytes 114720 | tf_op jit(solution)/shard_map/ppermute | solution.py:649
  133.3 5.0 %shard_map.276 = (f32[1328,128]{1,0:T(8,128)}, f32[560,128]{1,0:T(8,128)}, f32[560,128]{1,0:T(8,128)}, f32[736,128]{1,0:T(8,128)}, f32[736,128]{1,0:T(8,128)}, /*index=5*/f32[736,128]{1,0:T(8,128)}) custom-call(s32[2]{0:T(128)} %pad_add_fusion.place_ref, f32[6144,128]{1,0:T(8,128)} %bitcast.26, f32[6144,128]{1,0:T(8,128)} %bitcast.15.refs_3_.refs_1_, ...), custom_call_target="tpu_custom_call" | custom-call | flops 4313994752 | tf_op jit(solution)/shard_map/pallas_call | solution.py:757
  138.4 7.9 %collective-permute-start.16 = (f32[1328,128]{1,0:T(8,128)}, f32[1328,128]{1,0:T(8,128)}, u32[]{:S(2)}, u32[]{:S(2)}) collective-permute-start(f32[1328,128]{1,0:T(8,128)} %get-tuple-element.87.refs_10_), channel_id=1, source_target_pairs={{0,8},{4,12},{8,0},{12,4},{16,24},{20,28},{24,16},{28,20},{1,9},{5... | collective-permute-start | bytes 2039816 | tf_op jit(solution)/shard_map/ppermute | solution.py:649
  146.3 1.5 collective-permute-start.14
  147.8 1.5 collective-permute-start.15
  149.3 0.5 collective-permute-start.13
  149.8 18.0 %collective-permute-done.17.refs_11_.refs_6_ = f32[560,128]{1,0:T(8,128)} collective-permute-done((f32[560,128]{1,0:T(8,128)}, f32[560,128]{1,0:T(8,128)}, u32[]{:S(2)}, u32[]{:S(2)}) %collective-permute-start.17) | collective-permute-done | bytes 286752 | tf_op jit(solution)/shard_map/ppermute | solution.py:649
  167.8 0.3 collective-permute-start.18
  168.1 10.2 %collective-permute-done.18.refs_12_.refs_7_ = f32[560,128]{1,0:T(8,128)} collective-permute-done((f32[560,128]{1,0:T(8,128)}, f32[560,128]{1,0:T(8,128)}, u32[]{:S(2)}, u32[]{:S(2)}) %collective-permute-start.18) | collective-permute-done | bytes 286752 | tf_op jit(solution)/shard_map/ppermute | solution.py:649
  178.3 3.7 %shard_map.277 = (f32[352,128]{1,0:T(8,128)}, f32[352,128]{1,0:T(8,128)}, f32[352,128]{1,0:T(8,128)}, f32[368,128]{1,0:T(8,128)}, f32[368,128]{1,0:T(8,128)}, /*index=5*/f32[368,128]{1,0:T(8,128)}) custom-call(s32[2]{0:T(128)} %pad_add_fusion.place_ref, f32[2048,128]{1,0:T(8,128)} %bitcast.51, f32[2048,128]{1,0:T(8,128)} %bitcast.18.refs_11_.refs_1_, ...), custom_call_target="tpu_custom_call" | custom-call | flops 2598862848 | tf_op jit(solution)/shard_map/pallas_call | solution.py:757
  182.0 5.5 %collective-permute-start.20 = (f32[352,128]{1,0:T(8,128)}, f32[352,128]{1,0:T(8,128)}, u32[]{:S(2)}, u32[]{:S(2)}) collective-permute-start(f32[352,128]{1,0:T(8,128)} %get-tuple-element.91), channel_id=1, source_target_pairs={{0,16},{4,20},{8,24},{12,28},{16,0},{20,4},{24,8},{28,12},{1,17},{... | collective-permute-start | bytes 540680 | tf_op jit(solution)/shard_map/ppermute | solution.py:649
  187.5 1.5 collective-permute-start.23
  189.0 1.5 collective-permute-start.24
  190.4 0.5 collective-permute-start.22
  191.0 3.4 %collective-permute-start.21 = (f32[352,128]{1,0:T(8,128)}, f32[352,128]{1,0:T(8,128)}, u32[]{:S(2)}, u32[]{:S(2)}) collective-permute-start(f32[352,128]{1,0:T(8,128)} %get-tuple-element.92), channel_id=1, source_target_pairs={{0,24},{4,28},{8,16},{12,20},{16,8},{20,12},{24,0},{28,4},{1,25},{... | collective-permute-start | bytes 540680 | tf_op jit(solution)/shard_map/ppermute | solution.py:649
  194.3 6.5 %collective-permute-done.20.refs_2_.refs_6_ = f32[352,128]{1,0:T(8,128)} collective-permute-done((f32[352,128]{1,0:T(8,128)}, f32[352,128]{1,0:T(8,128)}, u32[]{:S(2)}, u32[]{:S(2)}) %collective-permute-start.20) | collective-permute-done | bytes 180256 | tf_op jit(solution)/shard_map/ppermute | solution.py:649
  200.9 0.2 collective-permute-start.19
  201.0 5.6 %collective-permute-done.19.refs_1_.refs_5_ = f32[352,128]{1,0:T(8,128)} collective-permute-done((f32[352,128]{1,0:T(8,128)}, f32[352,128]{1,0:T(8,128)}, u32[]{:S(2)}, u32[]{:S(2)}) %collective-permute-start.19) | collective-permute-done | bytes 180256 | tf_op jit(solution)/shard_map/ppermute | solution.py:649
  206.7 2.7 %shard_map.278.refs_8_ = f32[928,128]{1,0:T(8,128)} custom-call(s32[2]{0:T(128)} %pad_add_fusion.place_ref, f32[352,128]{1,0:T(8,128)} %get-tuple-element.90.refs_0_, f32[352,128]{1,0:T(8,128)} %collective-permute-done.19.refs_1_.refs_5_, f32[352,128]{1,0:T(8,128)} %collective-permute-done.20.refs_2_.refs_6_, ...), custom_call_target="tpu_custom_call" | custom-call | flops 1574589824 | tf_op jit(solution)/shard_map/pallas_call | solution.py:757
  209.4 0.1 collective-permute-start.25
  209.5 3.3 %shard_map.280 = (f32[128,256]{1,0:T(8,128)}, f32[64,512]{1,0:T(8,128)}, f32[64,128]{1,0:T(8,128)}) custom-call(s32[2]{0:T(128)} %pad_add_fusion.place_ref, f32[6144,128]{1,0:T(8,128)} %bitcast.27, f32[6144,128]{1,0:T(8,128)} %bitcast.15.refs_3_.refs_1_, f32[1712,128]{1,0:T(8,128)} %collective-permute-done.8.refs_3_.refs_2_, ...), custom_call_target="tpu_custom_call" | custom-call | flops 2037164800 | tf_op jit(solution)/shard_map/pallas_call | solution.py:757
  212.8 3.5 %shard_map.279 = (f32[128,128]{1,0:T(8,128)}, f32[49,960]{1,0:T(8,128)}, f32[1,512]{1,0:T(1,128)}, f32[1,512]{1,0:T(1,128)}, f32[1,512]{1,0:T(1,128)}, /*index=5...) custom-call(s32[2]{0:T(128)} %pad_add_fusion.place_ref, ...), custom_call_target="tpu_custom_call" | custom-call | flops 2013134976 | tf_op jit(solution)/shard_map/pallas_call | solution.py:757
  (19 shorter events, 0.0 us)
Async XLA Ops:
  1.8 4.3 %collective-permute-start = (f32[192,512]{1,0:T(8,128)S(1)}, f32[192,512]{1,0:T(8,128)S(1)}, u32[]{:S(2)}, u32[]{:S(2)}) collective-permute-start(f32[192,512]{1,0:T(8,128)S(1)} %bitcast.35), channel_id=1, source_target_pairs={{0,4},{4,8},{8,12},{12,16},{16,20},{20,24},{24,28},{1,5},{5,9},{9,... | collective-permute-start | bytes 1179656 | tf_op jit(solution)/shard_map/ppermute | solution.py:871
  4.2 5.8 %collective-permute-start.1 = (f32[192,512]{1,0:T(8,128)S(1)}, f32[192,512]{1,0:T(8,128)S(1)}, u32[]{:S(2)}, u32[]{:S(2)}) collective-permute-start(f32[192,512]{1,0:T(8,128)S(1)} %bitcast.34), channel_id=1, source_target_pairs={{4,0},{8,4},{12,8},{16,12},{20,16},{24,20},{28,24},{5,1},{9,5},{13... | collective-permute-start | bytes 1179656 | tf_op jit(solution)/shard_map/ppermute | solution.py:871
  6.2 3.8 %copy-start = (f32[192,512]{1,0:T(8,128)}, f32[192,512]{1,0:T(8,128)S(1)}, u32[]{:S(2)}) copy-start(f32[192,512]{1,0:T(8,128)S(1)} %collective-permute-done.above_ref) | copy-start | bytes 1179652
  10.0 0.8 copy-start.1
  65.8 14.5 %collective-permute-start.5 = (f32[4,4,384,128]{3,2,1,0:T(8,128)}, f32[4,4,384,128]{3,2,1,0:T(8,128)}, u32[]{:S(2)}, u32[]{:S(2)}) collective-permute-start(f32[4,4,384,128]{3,2,1,0:T(8,128)} %get-tuple-element.70), channel_id=1, source_target_pairs={{0,4},{4,0},{8,12},{12,8},{16,20},{20,16},{24,28},{28,24},{1,5},{5... | collective-permute-start | bytes 9437192 | tf_op jit(solution)/shard_map/ppermute | solution.py:649
  71.9 8.4 %collective-permute-start.4 = (f32[4,4,192,128]{3,2,1,0:T(8,128)}, f32[4,4,192,128]{3,2,1,0:T(8,128)}, u32[]{:S(2)}, u32[]{:S(2)}) collective-permute-start(f32[4,4,192,128]{3,2,1,0:T(8,128)} %get-tuple-element.68), channel_id=1, source_target_pairs={{0,4},{4,0},{8,12},{12,8},{16,20},{20,16},{24,28},{28,24},{1,5},{5... | collective-permute-start | bytes 4718600 | tf_op jit(solution)/shard_map/ppermute | solution.py:649
  72.0 8.3 %collective-permute-start.6 = (f32[704,128]{1,0:T(8,128)}, f32[704,128]{1,0:T(8,128)}, u32[]{:S(2)}, u32[]{:S(2)}) collective-permute-start(f32[704,128]{1,0:T(8,128)} %get-tuple-element.72), channel_id=1, source_target_pairs={{0,4},{4,0},{8,12},{12,8},{16,20},{20,16},{24,28},{28,24},{1,5},{5... | collective-permute-start | bytes 1081352 | tf_op jit(solution)/shard_map/ppermute | solution.py:649
  72.4 19.0 %collective-permute-start.2 = (f32[8,192,128]{2,1,0:T(8,128)}, f32[8,192,128]{2,1,0:T(8,128)}, u32[]{:S(2)}, u32[]{:S(2)}) collective-permute-start(f32[8,192,128]{2,1,0:T(8,128)} %get-tuple-element.62), channel_id=1, source_target_pairs={{0,4},{4,8},{8,12},{12,16},{16,20},{20,24},{24,28},{1,5},{5,9},{9,... | collective-permute-start | bytes 2359304 | tf_op jit(solution)/shard_map/ppermute | solution.py:871
  75.3 16.6 %collective-permute-start.3 = (f32[8,192,128]{2,1,0:T(8,128)}, f32[8,192,128]{2,1,0:T(8,128)}, u32[]{:S(2)}, u32[]{:S(2)}) collective-permute-start(f32[8,192,128]{2,1,0:T(8,128)} %get-tuple-element.64), channel_id=1, source_target_pairs={{4,0},{8,4},{12,8},{16,12},{20,16},{24,20},{28,24},{5,1},{9,5},{13... | collective-permute-start | bytes 2359304 | tf_op jit(solution)/shard_map/ppermute | solution.py:871
  85.7 38.8 %collective-permute-start.7 = (f32[1536,128]{1,0:T(8,128)}, f32[1536,128]{1,0:T(8,128)}, u32[]{:S(2)}, u32[]{:S(2)}) collective-permute-start(f32[1536,128]{1,0:T(8,128)} %get-tuple-element.73.rest_0_), channel_id=1, source_target_pairs={{0,16},{4,20},{8,24},{12,28},{16,0},{20,4},{24,8},{28,12},{1,17},{... | collective-permute-start | bytes 2359304 | tf_op jit(solution)/shard_map/ppermute | solution.py:649
  88.4 36.1 %collective-permute-start.8 = (f32[1712,128]{1,0:T(8,128)}, f32[1712,128]{1,0:T(8,128)}, u32[]{:S(2)}, u32[]{:S(2)}) collective-permute-start(f32[1712,128]{1,0:T(8,128)} %get-tuple-element.74.rest_1_), channel_id=1, source_target_pairs={{0,1},{1,0},{2,3},{3,2},{4,5},{5,4},{6,7},{7,6},{8,9},{9,8},{10,11... | collective-permute-start | bytes 2629640 | tf_op jit(solution)/shard_map/ppermute | solution.py:649
  89.9 40.3 %collective-permute-start.9 = (f32[1712,128]{1,0:T(8,128)}, f32[1712,128]{1,0:T(8,128)}, u32[]{:S(2)}, u32[]{:S(2)}) collective-permute-start(f32[1712,128]{1,0:T(8,128)} %get-tuple-element.75.rest_2_), channel_id=1, source_target_pairs={{0,2},{1,3},{2,0},{3,1},{4,6},{5,7},{6,4},{7,5},{8,10},{9,11},{10,... | collective-permute-start | bytes 2629640 | tf_op jit(solution)/shard_map/ppermute | solution.py:649
  91.4 38.7 %collective-permute-start.10 = (f32[1712,128]{1,0:T(8,128)}, f32[1712,128]{1,0:T(8,128)}, u32[]{:S(2)}, u32[]{:S(2)}) collective-permute-start(f32[1712,128]{1,0:T(8,128)} %get-tuple-element.76.rest_3_), channel_id=1, source_target_pairs={{0,3},{1,2},{2,1},{3,0},{4,7},{5,6},{6,5},{7,4},{8,11},{9,10},{10,... | collective-permute-start | bytes 2629640 | tf_op jit(solution)/shard_map/ppermute | solution.py:649
  130.2 3.2 %collective-permute-start.11 = (f32[4,4,128,128]{3,2,1,0:T(8,128)}, f32[4,4,128,128]{3,2,1,0:T(8,128)}, u32[]{:S(2)}, u32[]{:S(2)}) collective-permute-start(f32[4,4,128,128]{3,2,1,0:T(8,128)} %get-tuple-element.81), channel_id=1, source_target_pairs={{0,4},{4,0},{8,12},{12,8},{16,20},{20,16},{24,28},{28,24},{1,5},{5... | collective-permute-start | bytes 3145736 | tf_op jit(solution)/shard_map/ppermute | solution.py:649
  130.2 3.2 %collective-permute-start.12 = (f32[224,128]{1,0:T(8,128)}, f32[224,128]{1,0:T(8,128)}, u32[]{:S(2)}, u32[]{:S(2)}) collective-permute-start(f32[224,128]{1,0:T(8,128)} %get-tuple-element.83), channel_id=1, source_target_pairs={{0,4},{4,0},{8,12},{12,8},{16,20},{20,16},{24,28},{28,24},{1,5},{5... | collective-permute-start | bytes 344072 | tf_op jit(solution)/shard_map/ppermute | solution.py:649
  138.4 39.9 %collective-permute-start.16 = (f32[1328,128]{1,0:T(8,128)}, f32[1328,128]{1,0:T(8,128)}, u32[]{:S(2)}, u32[]{:S(2)}) collective-permute-start(f32[1328,128]{1,0:T(8,128)} %get-tuple-element.87.refs_10_), channel_id=1, source_target_pairs={{0,8},{4,12},{8,0},{12,4},{16,24},{20,28},{24,16},{28,20},{1,9},{5... | collective-permute-start | bytes 2039816 | tf_op jit(solution)/shard_map/ppermute | solution.py:649
  146.3 21.5 %collective-permute-start.17 = (f32[560,128]{1,0:T(8,128)}, f32[560,128]{1,0:T(8,128)}, u32[]{:S(2)}, u32[]{:S(2)}) collective-permute-start(f32[560,128]{1,0:T(8,128)} %get-tuple-element.88), channel_id=1, source_target_pairs={{0,16},{4,20},{8,24},{12,28},{16,0},{20,4},{24,8},{28,12},{1,17},{... | collective-permute-start | bytes 860168 | tf_op jit(solution)/shard_map/ppermute | solution.py:649
  146.3 32.0 %collective-permute-start.14 = (f32[736,128]{1,0:T(8,128)}, f32[736,128]{1,0:T(8,128)}, u32[]{:S(2)}, u32[]{:S(2)}) collective-permute-start(f32[736,128]{1,0:T(8,128)} %get-tuple-element.85), channel_id=1, source_target_pairs={{0,2},{1,3},{2,0},{3,1},{4,6},{5,7},{6,4},{7,5},{8,10},{9,11},{10,... | collective-permute-start | bytes 1130504 | tf_op jit(solution)/shard_map/ppermute | solution.py:649
  147.8 30.5 %collective-permute-start.15 = (f32[736,128]{1,0:T(8,128)}, f32[736,128]{1,0:T(8,128)}, u32[]{:S(2)}, u32[]{:S(2)}) collective-permute-start(f32[736,128]{1,0:T(8,128)} %get-tuple-element.86), channel_id=1, source_target_pairs={{0,3},{1,2},{2,1},{3,0},{4,7},{5,6},{6,5},{7,4},{8,11},{9,10},{10,... | collective-permute-start | bytes 1130504 | tf_op jit(solution)/shard_map/ppermute | solution.py:649
  149.3 29.0 %collective-permute-start.13 = (f32[736,128]{1,0:T(8,128)}, f32[736,128]{1,0:T(8,128)}, u32[]{:S(2)}, u32[]{:S(2)}) collective-permute-start(f32[736,128]{1,0:T(8,128)} %get-tuple-element.84.refs_5_), channel_id=1, source_target_pairs={{0,1},{1,0},{2,3},{3,2},{4,5},{5,4},{6,7},{7,6},{8,9},{9,8},{10,11... | collective-permute-start | bytes 1130504 | tf_op jit(solution)/shard_map/ppermute | solution.py:649
  167.8 10.5 %collective-permute-start.18 = (f32[560,128]{1,0:T(8,128)}, f32[560,128]{1,0:T(8,128)}, u32[]{:S(2)}, u32[]{:S(2)}) collective-permute-start(f32[560,128]{1,0:T(8,128)} %get-tuple-element.89), channel_id=1, source_target_pairs={{0,24},{4,28},{8,16},{12,20},{16,8},{20,12},{24,0},{28,4},{1,25},{... | collective-permute-start | bytes 860168 | tf_op jit(solution)/shard_map/ppermute | solution.py:649
  182.0 18.9 %collective-permute-start.20 = (f32[352,128]{1,0:T(8,128)}, f32[352,128]{1,0:T(8,128)}, u32[]{:S(2)}, u32[]{:S(2)}) collective-permute-start(f32[352,128]{1,0:T(8,128)} %get-tuple-element.91), channel_id=1, source_target_pairs={{0,16},{4,20},{8,24},{12,28},{16,0},{20,4},{24,8},{28,12},{1,17},{... | collective-permute-start | bytes 540680 | tf_op jit(solution)/shard_map/ppermute | solution.py:649
  187.5 19.2 %collective-permute-start.23 = (f32[368,128]{1,0:T(8,128)}, f32[368,128]{1,0:T(8,128)}, u32[]{:S(2)}, u32[]{:S(2)}) collective-permute-start(f32[368,128]{1,0:T(8,128)} %get-tuple-element.94), channel_id=1, source_target_pairs={{0,2},{1,3},{2,0},{3,1},{4,6},{5,7},{6,4},{7,5},{8,10},{9,11},{10,... | collective-permute-start | bytes 565256 | tf_op jit(solution)/shard_map/ppermute | solution.py:649
  189.0 17.7 %collective-permute-start.24 = (f32[368,128]{1,0:T(8,128)}, f32[368,128]{1,0:T(8,128)}, u32[]{:S(2)}, u32[]{:S(2)}) collective-permute-start(f32[368,128]{1,0:T(8,128)} %get-tuple-element.95), channel_id=1, source_target_pairs={{0,3},{1,2},{2,1},{3,0},{4,7},{5,6},{6,5},{7,4},{8,11},{9,10},{10,... | collective-permute-start | bytes 565256 | tf_op jit(solution)/shard_map/ppermute | solution.py:649
  190.4 16.2 %collective-permute-start.22 = (f32[368,128]{1,0:T(8,128)}, f32[368,128]{1,0:T(8,128)}, u32[]{:S(2)}, u32[]{:S(2)}) collective-permute-start(f32[368,128]{1,0:T(8,128)} %get-tuple-element.93.refs_4_), channel_id=1, source_target_pairs={{0,1},{1,0},{2,3},{3,2},{4,5},{5,4},{6,7},{7,6},{8,9},{9,8},{10,11... | collective-permute-start | bytes 565256 | tf_op jit(solution)/shard_map/ppermute | solution.py:649
  191.0 10.1 %collective-permute-start.21 = (f32[352,128]{1,0:T(8,128)}, f32[352,128]{1,0:T(8,128)}, u32[]{:S(2)}, u32[]{:S(2)}) collective-permute-start(f32[352,128]{1,0:T(8,128)} %get-tuple-element.92), channel_id=1, source_target_pairs={{0,24},{4,28},{8,16},{12,20},{16,8},{20,12},{24,0},{28,4},{1,25},{... | collective-permute-start | bytes 540680 | tf_op jit(solution)/shard_map/ppermute | solution.py:649
  200.9 5.8 %collective-permute-start.19 = (f32[352,128]{1,0:T(8,128)}, f32[352,128]{1,0:T(8,128)}, u32[]{:S(2)}, u32[]{:S(2)}) collective-permute-start(f32[352,128]{1,0:T(8,128)} %get-tuple-element.90.refs_0_), channel_id=1, source_target_pairs={{0,8},{4,12},{8,0},{12,4},{16,24},{20,28},{24,16},{28,20},{1,9},{5... | collective-permute-start | bytes 540680 | tf_op jit(solution)/shard_map/ppermute | solution.py:649
  209.4 3.4 %collective-permute-start.25 = (f32[928,128]{1,0:T(8,128)}, f32[928,128]{1,0:T(8,128)}, u32[]{:S(2)}, u32[]{:S(2)}) collective-permute-start(f32[928,128]{1,0:T(8,128)} %shard_map.278.refs_8_), channel_id=1, source_target_pairs={{0,4},{4,0},{8,12},{12,8},{16,20},{20,16},{24,28},{28,24},{1,5},{5... | collective-permute-start | bytes 1425416 | tf_op jit(solution)/shard_map/ppermute | solution.py:649

commit v7 on v6

--- a/solution.py
+++ b/solution.py
@@ -231,187 +231,229 @@
             share(core, first, second, kept_ref, sent_ref, z, p)
 
 
+class Copies:
+    def __init__(self, sems):
+        self.sems, self.count, self.pending = sems, 0, {}
+
+    def start(self, name, source, target):
+        copy = pltpu.make_async_copy(source, target, self.sems.at[self.count])
+        self.count += 1
+        copy.start()
+        self.pending.setdefault(name, []).append(copy)
+
+    def wait(self, *names):
+        for name in names:
+            for copy in self.pending.pop(name):
+                copy.wait()
+
+    def wait_all(self):
+        self.wait(*list(self.pending))
+
+
 def forward_kernel(
-    place_ref, ids_scalar, one_table, two_table, ids_ref, above_ref, own_ref, below_ref, cot_ref,
-    first_gain_ref, first_scale_ref, second_gain_ref, second_scale_ref,
-    in_ref, kern_ref, one_ref, two_ref, three_ref, out_ref, up_ref, down_ref,
-    joined_ref, output_ref, dmiddle_ref, dconv_ref, dconv_top_ref, dconv_bottom_ref,
-    plane_kept_ref, plane_sent_ref, line_kept_ref, line_sent_ref, packed_kept_ref, packed_sent_ref,
-    up_kept, up_sent, down_kept, down_sent, out_kept, out_sent, sems,
-    row_taps, padded, valid_ref, one_keep_ref, two_keep_ref, col_ref, packed_ref, normed, flat, shifted, laid, wide, conv, mixed_ref, mapped_ref, middle_ref, result, dnorm,
+    place_ref, ids_scalar, one_table, two_table, ids_hbm, above_hbm, own_hbm, below_hbm, cot_hbm,
+    first_gain_hbm, first_scale_hbm, second_gain_hbm, second_scale_hbm,
+    in_hbm_ref, kern_hbm, one_hbm, two_hbm, three_hbm, out_hbm, up_hbm, down_hbm,
+    joined_hbm, output_hbm, dmiddle_hbm, dconv_hbm, dconv_top_hbm, dconv_bottom_hbm,
+    plane_kept_ref, plane_sent_ref, line_kept_ref, line_sent_ref, packed_kept_hbm, packed_sent_hbm,
+    ids_ref, rows_ref, cot_ref, first_gain_ref, first_scale_ref, second_gain_ref, second_scale_ref,
+    in_ref, kern_ref, one_ref, two_ref, three_ref, out_ref, up_ref, down_ref, dconv_ref, sems, chunk_sems,
+    up_kept, up_sent, down_kept, down_sent, out_kept, out_sent,
+    row_taps, padded, valid_ref, one_keep_ref, two_keep_ref, col_ref, packed_ref, normed, flat, shifted, laid, wide, conv,
+    mixed_ref, mapped_ref, middle_ref, result, dnorm,
     *, rows, cols, count_ha, count_ba,
 ):
-    step = pl.program_id(0)
     blocks = flat.shape[0]
     cells = rows * cols
     reach = REACH * cols
     cells_ext = cells + 2 * reach
     core = place_ref[0] % 2
     split = one_ref.shape[0]
-    dim = own_ref.shape[1]
+    dim = rows_ref.shape[1]
     head_steps = blocks // 2
-    ffn_first = head_steps + blocks
+    ffn_steps = up_kept.shape[0]
+    chunk = down_ref.shape[1]
     gate_refs = (one_ref, two_ref, three_ref)
-    ffn_steps = up_kept.shape[0]
+
+    copies = Copies(sems)
+    copies.start("ids", ids_hbm, ids_ref)
+    copies.start("above", above_hbm, rows_ref.at[pl.ds(0, reach)])
+    copies.start("own", own_hbm, rows_ref.at[pl.ds(reach, cells)])
+    copies.start("below", below_hbm, rows_ref.at[pl.ds(reach + cells, reach)])
+    copies.start("vectors", first_gain_hbm, first_gain_ref)
+    for k in range(head_steps):
+        copies.start(("in", k), in_hbm_ref.at[:, pl.ds(2 * LANES * k, 2 * LANES)], in_ref.at[k])
+    copies.start("kern", kern_hbm, kern_ref)
+    def weights(k):
+        ends = pl.ds(pl.multiple_of(k * chunk, chunk), chunk)
+        return [
+            pltpu.make_async_copy(up_hbm.at[:, ends], up_ref.at[k], chunk_sems.at[k, 0]),
+            pltpu.make_async_copy(down_hbm.at[ends, :], down_ref.at[k], chunk_sems.at[k, 1]),
+        ]
 
     def chunk_copies(place):
-        copies = []
+        moves = []
         sides = ((up_kept, down_kept, plane_kept_ref, line_kept_ref), (up_sent, down_sent, plane_sent_ref, line_sent_ref))
         for up, down, plane, line in sides:
             cut = plane.shape[2] // 2
             rest = up.shape[3] - cut
             zs = pl.ds(place * up.shape[1], up.shape[1])
             bas = pl.ds(place * down.shape[2], down.shape[2])
-            copies += [
+            moves += [
                 (up.at[place, :, ba, pl.ds(0, cut), :], plane.at[ba, zs, pl.ds(0, cut), :])
                 for ba in range(plane.shape[0])
             ]
-            copies += [
+            moves += [
                 (down.at[place, z, :, pl.ds(0, cut), :], plane.at[bas, z, pl.ds(cut, cut), :])
                 for z in range(plane.shape[1])
             ]
-            copies.append((up.at[place, :, :, pl.ds(cut, rest), :], line.at[zs, :, pl.ds(0, rest), :]))
-            copies.append((down.at[place, :, :, pl.ds(cut, rest), :], line.at[:, bas, pl.ds(rest, rest), :]))
+            moves.append((up.at[place, :, :, pl.ds(cut, rest), :], line.at[zs, :, pl.ds(0, rest), :]))
+            moves.append((down.at[place, :, :, pl.ds(cut, rest), :], line.at[:, bas, pl.ds(rest, rest), :]))
         return [
-            pltpu.make_async_copy(source, target, sems.at[place, k]) for k, (source, target) in enumerate(copies)
+            pltpu.make_async_copy(source, target, chunk_sems.at[place, 2 + k])
+            for k, (source, target) in enumerate(moves)
         ]
 
-    def out_copies():
-        copies = []
-        for k, (source, line) in enumerate(((out_kept, line_kept_ref), (out_sent, line_sent_ref))):
-            rows_out = source.shape[2]
-            target = line.at[:, :, pl.ds(line.shape[2] - rows_out, rows_out), :]
-            copies.append(pltpu.make_async_copy(source, target, sems.at[ffn_steps, k]))
-        return copies
-
-    @pl.when(step == 0)
-    def _():
-        lay_kernel(kern_ref, laid, split)
-        turned = image_ids(ids_ref, padded, place_ref[0], rows)
-        spread_cells((turned >= 0).astype(F32), valid_ref, 0, rows + 2 * REACH)
-        spread_cells(keep_factors(turned, one_table), one_keep_ref, REACH, rows)
-        spread_cells(keep_factors(turned, two_table), two_keep_ref, REACH, rows)
-        conv_masks(ids_scalar, ids_ref, place_ref[0], row_taps, col_ref, rows)
-        start = 0
-        for ref in (above_ref, own_ref, below_ref):
-            size = ref.shape[0]
-            hat, _ = normalized(ref[...] * valid_ref[start : start + size, :1])
-            normed[start : start + size] = hat * first_gain_ref[...]
-            start += size
-
-    @pl.when(step < head_steps)
-    def _():
-        joined = dot(normed[...], in_ref[...])
+    copies.wait("ids")
+    turned = image_ids(ids_ref, padded, place_ref[0], rows)
+    spread_cells((turned >= 0).astype(F32), valid_ref, 0, rows + 2 * REACH)
+    spread_cells(keep_factors(turned, one_table), one_keep_ref, REACH, rows)
+    spread_cells(keep_factors(turned, two_table), two_keep_ref, REACH, rows)
+    conv_masks(ids_scalar, ids_ref, place_ref[0], row_taps, col_ref, rows)
+    copies.wait("vectors")
+    start = 0
+    for name, size in (("above", reach), ("own", cells), ("below", reach)):
+        copies.wait(name)
+        hat, _ = normalized(rows_ref[start : start + size, :] * valid_ref[start : start + size, :1])
+        normed[start : start + size] = hat * first_gain_ref[...]
+        start += size
+
+    for k in range(blocks):
+        flat[k, :EDGE] = jnp.zeros((EDGE, LANES), F32)
+        flat[k, EDGE + cells_ext :] = jnp.zeros((EDGE, LANES), F32)
+    for step in range(head_steps):
+        copies.wait(("in", step))
+        joined = dot(normed[...], in_ref[step])
         for k in range(2):
-            part = joined[:, k * LANES : (k + 1) * LANES]
-            block = 2 * step + k
-            flat[block, :EDGE] = jnp.zeros((EDGE, LANES), F32)
-            flat[block, EDGE : EDGE + cells_ext] = part
-            flat[block, EDGE + cells_ext :] = jnp.zeros((EDGE, LANES), F32)
-            joined_ref[k] = part[reach : reach + cells]
-
-    @pl.when((step >= head_steps) & (step < ffn_first))
-    def _():
-        block = step - head_steps
+            flat[2 * step + k, EDGE : EDGE + cells_ext] = joined[:, k * LANES : (k + 1) * LANES]
+        if step == 0:
+            copies.start("gates", first_scale_hbm, first_scale_ref)
+            copies.start("gates", second_gain_hbm, second_gain_ref)
+            copies.start("gates", second_scale_hbm, second_scale_ref)
+            for source, target in zip((one_hbm, two_hbm, three_hbm, out_hbm, cot_hbm), gate_refs + (out_ref, cot_ref)):
+                copies.start("gates", source, target)
+            for k in range(ffn_steps):
+                for copy in weights(k):
+                    copy.start()
+        pair = pl.ds(2 * step, 2)
+        copies.start("outs", flat.at[pair, pl.ds(EDGE + reach, cells), :], joined_hbm.at[pair])
+
+    copies.wait("kern")
+    lay_kernel(kern_ref, laid, split)
+
+    def conv_step(block, _):
         fill_shifted(flat.at[block], col_ref, shifted, rows + 2 * REACH, cols)
         conv_block(row_taps, laid[block], shifted, wide, conv.at[block], rows, cols)
+        return 0
+
+    lax.fori_loop(0, blocks, conv_step, 0)
 
     def conv_part(start, width):
         return jnp.concatenate([conv[start // LANES + k] for k in range(width // LANES)], axis=1)
 
-    @pl.when(step == ffn_first)
-    def _():
-        mixed = conv[0, :, :split] * conv[0, :, split:]
-        mixed_ref[:, :split] = mixed
-        start = 2 * split
-        for ref in gate_refs:
-            width = ref.shape[1]
-            mapped = dot(mixed, ref[...])
-            mapped_ref[:, start - 2 * split : start - 2 * split + width] = mapped
-            mixed = mapped * conv_part(start, width)
-            mixed_ref[:, start : start + width] = mixed
-            start += width
-        branch = dot(mixed, out_ref[...])
-        masked = own_ref[...] * valid_ref[reach : reach + cells, :1]
-        middle = masked + one_keep_ref[:, :1] * first_scale_ref[...] * branch
-        middle_ref[...] = middle
-        hat, _ = normalized(middle)
-        normed[:cells] = hat * second_gain_ref[...]
-        normed[cells : cells + reach] = jnp.zeros((reach, dim), F32)
-        result[...] = jnp.zeros_like(result)
-        dnorm[...] = jnp.zeros_like(dnorm)
-
-    @pl.when(step >= ffn_first)
-    def _():
+    copies.wait("gates")
+    mixed = conv[0, :, :split] * conv[0, :, split:]
+    mixed_ref[:, :split] = mixed
+    start = 2 * split
+    for ref in gate_refs:
+        width = ref.shape[1]
+        mapped = dot(mixed, ref[...])
+        mapped_ref[:, start - 2 * split : start - 2 * split + width] = mapped
+        mixed = mapped * conv_part(start, width)
+        mixed_ref[:, start : start + width] = mixed
+        start += width
+    branch = dot(mixed, out_ref[...])
+    masked = rows_ref[reach : reach + cells, :] * valid_ref[reach : reach + cells, :1]
+    middle = masked + one_keep_ref[:, :1] * first_scale_ref[...] * branch
+    middle_ref[...] = middle
+    hat, _ = normalized(middle)
+    normed[:cells] = hat * second_gain_ref[...]
+    result[...] = jnp.zeros_like(result)
+    dnorm[...] = jnp.zeros_like(dnorm)
+
+    def ffn_step(place, _):
+        for copy in weights(place):
+            copy.wait()
         grad_result = two_keep_ref[:, :1] * second_scale_ref[...] * cot_ref[...]
-        pre = dot(normed[:cells], up_ref[...])
+        pre = dot(normed[:cells], up_ref[place])
         cdf = 0.5 + 0.5 * lax.erf(pre * INV_SQRT_2)
         slope = cdf + pre * (INV_SQRT_2PI * jnp.exp(-0.5 * pre * pre))
         hidden = pre * cdf
-        result[...] += dot(hidden, down_ref[...])
-        grad_pre = dot(grad_result, down_ref[...], NT) * slope
-        place = step - ffn_first
-        for ref in (up_kept, up_sent, down_kept, down_sent):
-            assert ref.shape[0] == ffn_steps
+        result[...] += dot(hidden, down_ref[place])
+        grad_pre = dot(grad_result, down_ref[place], NT) * slope
         share_rows(
             core, dot(grad_result, hidden, TN), down_kept.at[place], down_sent.at[place], dim // count_ha
         )
-        width = down_ref.shape[0] // (2 * up_kept.shape[1])
+        width = chunk // (2 * up_kept.shape[1])
         share_columns(core, dot(normed[:cells], grad_pre, TN), up_kept.at[place], up_sent.at[place], width)
         for copy in chunk_copies(place):
             copy.start()
-        dnorm[...] += dot(grad_pre, up_ref[...], NT)
-
-    @pl.when(step == pl.num_programs(0) - 1)
-    def _():
-        hat, scale = normalized(middle_ref[...])
-        kept = two_keep_ref[:, :1] * result[...]
-        output_ref[...] = middle_ref[...] + second_scale_ref[...] * kept
-        dscale_two = jnp.sum(cot_ref[...] * kept, axis=0, keepdims=True)
-        dgain_two = jnp.sum(dnorm[...] * hat, axis=0, keepdims=True)
-        dmiddle = cot_ref[...] + norm_backward(dnorm[...] * second_gain_ref[...], hat, scale)
-        dmiddle_ref[...] = dmiddle
-        kept = one_keep_ref[:, :1] * dmiddle
-        start = mixed_ref.shape[1] - out_ref.shape[0]
-        crossed = dot(mixed_ref[:, start:], kept, TN)
-        dscale_one = jnp.sum(crossed * out_ref[...], axis=0, keepdims=True)
-        share_rows(core, (crossed * first_scale_ref[...]).T, out_kept, out_sent, dim // count_ha)
-        for copy in out_copies():
-            copy.start()
-        grad = dot(kept * first_scale_ref[...], out_ref[...], NT)
-        row = packed_ref.shape[0]
-        start = blocks * LANES
-        for ref in reversed(gate_refs):
-            tall, width = ref.shape
-            start -= width
-            source = start - tall if tall > split else 0
-            columns = slice(start - 2 * split, start - 2 * split + width)
-            dconv = grad * mapped_ref[:, columns]
-            for k in range(width // LANES):
-                dconv_ref[start // LANES + k] = dconv[:, k * LANES : (k + 1) * LANES]
-            grad_mapped = grad * conv_part(start, width)
-            part = dot(mixed_ref[:, source : source + tall], grad_mapped, TN)
-            row -= tall * width // LANES
-            for k in range(width // LANES):
-                packed_ref[row + k * tall : row + (k + 1) * tall] = part[:, k * LANES : (k + 1) * LANES]
-            grad = dot(grad_mapped, ref[...], NT)
-        dconv_ref[0] = jnp.concatenate([grad * conv[0, :, split:], grad * conv[0, :, :split]], axis=1)
-        packed_ref[:row] = jnp.zeros((row, LANES), F32)
-        row = 0
-        for vector in (dscale_one, dgain_two, dscale_two):
-            for k in range(dim // LANES):
-                packed_ref[row : row + 1] = vector[:, k * LANES : (k + 1) * LANES]
-                row += 1
-        half = packed_kept_ref.shape[0]
-        packed_kept_ref[...] = packed_ref[pl.ds(pl.multiple_of(core * half, 8), half), :]
-        packed_sent_ref[...] = packed_ref[pl.ds(pl.multiple_of((1 - core) * half, 8), half), :]
-        dconv_top_ref[...] = dconv_ref[:, :reach, :]
-        dconv_bottom_ref[...] = dconv_ref[:, cells - reach :, :]
-        for copy in out_copies():
+        dnorm[...] += dot(grad_pre, up_ref[place], NT)
+        return 0
+
+    lax.fori_loop(0, ffn_steps, ffn_step, 0)
+
+    hat, scale = normalized(middle_ref[...])
+    kept = two_keep_ref[:, :1] * result[...]
+    dscale_two = jnp.sum(cot_ref[...] * kept, axis=0, keepdims=True)
+    result[...] = middle_ref[...] + second_scale_ref[...] * kept
+    copies.start("outs", result, output_hbm)
+    dgain_two = jnp.sum(dnorm[...] * hat, axis=0, keepdims=True)
+    dmiddle = cot_ref[...] + norm_backward(dnorm[...] * second_gain_ref[...], hat, scale)
+    dnorm[...] = dmiddle
+    copies.start("outs", dnorm, dmiddle_hbm)
+    kept = one_keep_ref[:, :1] * dmiddle
+    grad = dot(kept * first_scale_ref[...], out_ref[...], NT)
+    row = packed_ref.shape[0]
+    start = blocks * LANES
+    for ref in reversed(gate_refs):
+        tall, width = ref.shape
+        start -= width
+        source = start - tall if tall > split else 0
+        columns = slice(start - 2 * split, start - 2 * split + width)
+        dconv = grad * mapped_ref[:, columns]
+        for k in range(width // LANES):
+            dconv_ref[start // LANES + k] = dconv[:, k * LANES : (k + 1) * LANES]
+        grad_mapped = grad * conv_part(start, width)
+        part = dot(mixed_ref[:, source : source + tall], grad_mapped, TN)
+        row -= tall * width // LANES
+        for k in range(width // LANES):
+            packed_ref[row + k * tall : row + (k + 1) * tall] = part[:, k * LANES : (k + 1) * LANES]
+        grad = dot(grad_mapped, ref[...], NT)
+    dconv_ref[0] = jnp.concatenate([grad * conv[0, :, split:], grad * conv[0, :, :split]], axis=1)
+    copies.start("outs", dconv_ref.at[:, pl.ds(0, reach), :], dconv_top_hbm)
+    copies.start("outs", dconv_ref.at[:, pl.ds(cells - reach, reach), :], dconv_bottom_hbm)
+    copies.start("outs", dconv_ref, dconv_hbm)
+    start = mixed_ref.shape[1] - out_ref.shape[0]
+    crossed = dot(mixed_ref[:, start:], kept, TN)
+    dscale_one = jnp.sum(crossed * out_ref[...], axis=0, keepdims=True)
+    packed_ref[:row] = jnp.zeros((row, LANES), F32)
+    row = 0
+    for vector in (dscale_one, dgain_two, dscale_two):
+        for k in range(dim // LANES):
+            packed_ref[row : row + 1] = vector[:, k * LANES : (k + 1) * LANES]
+            row += 1
+    half = packed_kept_hbm.shape[0]
+    for place, target in ((core, packed_kept_hbm), (1 - core, packed_sent_hbm)):
+        copies.start("outs", packed_ref.at[pl.ds(pl.multiple_of(place * half, 8), half), :], target)
+    share_rows(core, (crossed * first_scale_ref[...]).T, out_kept, out_sent, dim // count_ha)
+    for source, line in ((out_kept, line_kept_ref), (out_sent, line_sent_ref)):
+        tall = source.shape[2]
+        copies.start("outs", source, line.at[:, :, pl.ds(line.shape[2] - tall, tall), :])
+    for place in range(ffn_steps):
+        for copy in chunk_copies(place):
             copy.wait()
-        for place in range(ffn_steps):
-            for copy in chunk_copies(place):
-                copy.wait()
+    copies.wait_all()
 
 
 def mask_scratch(ids, rows):
@@ -443,11 +485,7 @@
     split = gates[0].shape[0]
     wide = blocks * LANES
     head_steps = blocks // 2
-    ffn_first = head_steps + blocks
     ffn_steps = hidden // chunk
-
-    def ffn_step(i):
-        return jnp.clip(i - ffn_first, 0, ffn_steps - 1)
 
     up_wide, down_wide = hidden // count_ha, hidden // count_ba
     up_rows = dim // count_ba * lane_blocks(up_wide)
@@ -461,85 +499,67 @@
     line = (half, count_ba, 2 * rest + out_rows, LANES)
     packed_shape = (packed_rows(gates, dim, count_ba), LANES)
     half_packed = (packed_shape[0] // 2, LANES)
-    copies = 2 * (count_ba + half + 2)
     cells_ext = cells + 2 * reach
-    return pl.pallas_call(
-        functools.partial(forward_kernel, rows=rows, cols=cols, count_ha=count_ha, count_ba=count_ba),
-        grid=(ffn_first + ffn_steps,),
-        in_specs=[in_smem()] * 4
-        + [whole(x.shape) for x in (ids, above, own, below, cot)]
-        + [whole((1, dim))] * 4
-        + [
-            pl.BlockSpec((dim, 2 * LANES), lambda i: (0, jnp.minimum(i, head_steps - 1))),
-            whole(kern.shape),
-        ]
-        + [whole(gate.shape) for gate in gates]
-        + [
-            whole(weight_out.shape),
-            pl.BlockSpec((dim, chunk), lambda i: (0, ffn_step(i))),
-            pl.BlockSpec((chunk, dim), lambda i: (ffn_step(i), 0)),
-        ],
-        out_specs=[
-            pl.BlockSpec((2, cells, LANES), lambda i: (jnp.minimum(i, head_steps - 1), 0, 0)),
-            whole((cells, dim)),
-            whole((cells, dim)),
-            whole((blocks, cells, LANES)),
-            whole((blocks, reach, LANES)),
-            whole((blocks, reach, LANES)),
-            in_hbm(),
-            in_hbm(),
-            in_hbm(),
-            in_hbm(),
-            whole(half_packed),
-            whole(half_packed),
-        ],
-        out_shape=[
-            shape_of(blocks, cells, LANES),
-            shape_of(cells, dim),
-            shape_of(cells, dim),
-            shape_of(blocks, cells, LANES),
-            shape_of(blocks, reach, LANES),
-            shape_of(blocks, reach, LANES),
-            shape_of(*plane),
-            shape_of(*plane),
-            shape_of(*line),
-            shape_of(*line),
-            shape_of(*half_packed),
-            shape_of(*half_packed),
-        ],
-        scratch_shapes=[
-            pltpu.VMEM((ffn_steps, chunk // (2 * up_wide), count_ba, up_rows, LANES), F32),
-            pltpu.VMEM((ffn_steps, chunk // (2 * up_wide), count_ba, up_rows, LANES), F32),
-            pltpu.VMEM((ffn_steps, half, chunk // down_wide, down_rows, LANES), F32),
-            pltpu.VMEM((ffn_steps, half, chunk // down_wide, down_rows, LANES), F32),
-            pltpu.VMEM((half, count_ba, out_rows, LANES), F32),
-            pltpu.VMEM((half, count_ba, out_rows, LANES), F32),
-            pltpu.SemaphoreType.DMA((ffn_steps + 1, copies)),
-        ]
-        + mask_scratch(ids, rows)
-        + [
-            pltpu.VMEM((cells, LANES), F32),
-            pltpu.VMEM((cells, LANES), F32),
-            pltpu.VMEM((KERN, cols // 8, 8, LANES), F32),
-            pltpu.VMEM(packed_shape, F32),
-            pltpu.VMEM((cells_ext, dim), F32),
-            pltpu.VMEM((blocks, cells_ext + 2 * EDGE, LANES), F32),
-            pltpu.VMEM((KERN, rows + 2 * REACH, cols // 8, 8, LANES), F32),
-            pltpu.VMEM((blocks, TAPS, LANES), F32),
-            pltpu.VMEM((TAPS + KERN, 8, LANES), F32),
-            pltpu.VMEM((blocks, cells, LANES), F32),
-            pltpu.VMEM((cells, wide), F32),
-            pltpu.VMEM((cells, wide - 2 * split), F32),
-            pltpu.VMEM((cells, dim), F32),
-            pltpu.VMEM((cells, dim), F32),
-            pltpu.VMEM((cells, dim), F32),
-        ],
-        compiler_params=params(),
-        cost_estimate=lasting(55),
-    )(
+    vmem = functools.partial(pltpu.VMEM, dtype=F32)
+    operands = (
         place, ids, keep_one, keep_two, ids, above, own, below, cot, *vectors,
         weight_in, kern, *gates, weight_out, weight_up, weight_down,
     )
+    out_shape = [
+        shape_of(blocks, cells, LANES),
+        shape_of(cells, dim),
+        shape_of(cells, dim),
+        shape_of(blocks, cells, LANES),
+        shape_of(blocks, reach, LANES),
+        shape_of(blocks, reach, LANES),
+        shape_of(*plane),
+        shape_of(*plane),
+        shape_of(*line),
+        shape_of(*line),
+        shape_of(*half_packed),
+        shape_of(*half_packed),
+    ]
+    return pl.pallas_call(
+        functools.partial(forward_kernel, rows=rows, cols=cols, count_ha=count_ha, count_ba=count_ba),
+        in_specs=[in_smem()] * 4 + [in_hbm()] * (len(operands) - 4),
+        out_specs=[in_hbm()] * len(out_shape),
+        out_shape=out_shape,
+        scratch_shapes=[pltpu.VMEM(ids.shape, jnp.int32), vmem((cells_ext, dim)), vmem((cells, dim))]
+        + [vmem((1, dim))] * 4
+        + [vmem((head_steps, dim, 2 * LANES)), vmem(kern.shape)]
+        + [vmem(gate.shape) for gate in gates]
+        + [
+            vmem(weight_out.shape),
+            vmem((ffn_steps, dim, chunk)),
+            vmem((ffn_steps, chunk, dim)),
+            vmem((blocks, cells, LANES)),
+            pltpu.SemaphoreType.DMA((40 + head_steps,)),
+            pltpu.SemaphoreType.DMA((ffn_steps, 2 + 2 * (count_ba + half + 2))),
+        ]
+        + [vmem((ffn_steps, chunk // (2 * up_wide), count_ba, up_rows, LANES))] * 2
+        + [vmem((ffn_steps, half, chunk // down_wide, down_rows, LANES))] * 2
+        + [vmem((half, count_ba, out_rows, LANES))] * 2
+        + mask_scratch(ids, rows)
+        + [
+            vmem((cells, LANES)),
+            vmem((cells, LANES)),
+            vmem((KERN, cols // 8, 8, LANES)),
+            vmem(packed_shape),
+            vmem((cells_ext, dim)),
+            vmem((blocks, cells_ext + 2 * EDGE, LANES)),
+            vmem((KERN, rows + 2 * REACH, cols // 8, 8, LANES)),
+            vmem((blocks, TAPS, LANES)),
+            vmem((TAPS + KERN, 8, LANES)),
+            vmem((blocks, cells, LANES)),
+            vmem((cells, wide)),
+            vmem((cells, wide - 2 * split)),
+            vmem((cells, dim)),
+            vmem((cells, dim)),
+            vmem((cells, dim)),
+        ],
+        compiler_params=params(),
+        cost_estimate=lasting(45),
+    )(*operands)
 
 
 def lay_flat(above_ref, own_ref, below_ref, flat):
@@ -839,9 +859,13 @@
             for step in self.steps
         ]
 
-    def go(self, payloads):
+    def go(self, payloads, in_turn=False):
         axis, unit = ("ba", 1) if self.way == "plane" else ("ha", 2)
-        arrived = [exchange(part, axis, unit * step) for step, part in zip(self.steps, payloads)]
+        arrived = []
+        for step, part in zip(self.steps, payloads):
+            if in_turn and step == len(self.steps) and step > 2:
+                (part,) = tied([part], arrived[1:2])
+            arrived.append(exchange(part, axis, unit * step))
         places = {}
         for step, sent, part in zip(self.steps, payloads, arrived):
             row = 0
@@ -854,14 +878,9 @@
         return arrived
 
 
-def run(place, stages):
-    groups = [group for stage in stages for group in stage.groups()]
-    made = combine(place, groups)
-    rest, arrived = made, []
-    for stage in stages:
-        arrived += stage.go(rest[: len(stage.steps)])
-        rest = rest[len(stage.steps) :]
-    return made, arrived
+def run(place, stage, ties=(), in_turn=False):
+    made = list(combine(place, stage.groups(), ties))
+    return made, stage.go(made, in_turn)
 
 
 def neighbour_rows(top, bottom):
@@ -964,9 +983,9 @@
     plane_sum = Sum([plane_kept, exchange(plane_sent, "ha", 1)], ["plane", "far", "near"])
     line_sum = Sum([line_kept, exchange(line_sent, "ha", 1)], ["far", "near", "plane"])
     packed = Sum([packed_kept, exchange(packed_sent, "ha", 1)], ["plane"])
-    made, arrived = run(
-        place, [Stage([(line_sum, "far")], "far"), Stage([(plane_sum, "plane"), (packed, "plane")], "plane")]
-    )
+    made, arrived = run(place, Stage([(plane_sum, "plane"), (packed, "plane")], "plane"))
+    more, far = run(place, Stage([(line_sum, "far")], "far"), ties=made + [above, below])
+    made, arrived = made + more, arrived + far
     dcanvas, in_kept, in_sent, small_kept, small_sent = backward(
         place, ids, above, dconv, below, joined, depth_kernel, own, gain, dmiddle, weight_in, made,
         rows, cols, count_ha, count_ba,
@@ -975,21 +994,13 @@
     in_sum = Sum([in_kept, exchange(in_sent, "ha", 1)], ["plane", "far", "near"])
     small = Rider([flat_view(small_kept), flat_view(exchange(small_sent, "ha", 1))])
     packed = Rider(packed.views)
-    run(
-        place,
-        [
-            Stage([(plane_sum, "line"), (packed, "line"), (line_sum, "near")], "line"),
-            Stage([(in_sum, "plane"), (small, "plane")], "plane"),
-        ],
+    made, arrived = run(
+        place, Stage([(plane_sum, "line"), (packed, "line"), (line_sum, "near")], "line"), in_turn=True
     )
+    run(place, Stage([(in_sum, "plane"), (small, "plane")], "plane"), ties=made)
+    made, _ = run(place, Stage([(in_sum, "line"), (small, "line")], "line"), ties=arrived, in_turn=True)
     packed = Gather(packed.views)
-    run(
-        place,
-        [
-            Stage([(in_sum, "line"), (small, "line")], "line"),
-            Stage([(line_sum, "plane"), (packed, "plane")], "plane"),
-        ],
-    )
+    run(place, Stage([(line_sum, "plane"), (packed, "plane")], "plane"), ties=made)
     cut = plane_sum.views[0].rows // 2
     rest = (line_sum.views[0].rows - dim // count_ha * lane_blocks(dim // count_ba)) // 2
     dup, ddown, dout = combine(

time: 217 us -> 203 us (0.935)
  waiting for transfers between devices: 59.7 us -> 42.6 us
  Pallas kernels: 108 us -> 113 us
  starting transfers between devices: 45.4 us -> 42.6 us
    ppermute x22, waiting for transfers between devices: 55.9 us -> 38.7 us  [exchange(): lax.ppermute(values, axis, [(i, i ^ bit) for i in range(lax.axis_size(axi...]
    pallas_call x6 -> x9, Pallas kernels: 23.7 us -> 30 us  [combine(): pl.pallas_call(kernel, in_specs=[in_smem()] + [in_hbm()] * (len(arrays) +...]
    ppermute x22, starting transfers between devices: 37.5 us -> 34.4 us  [exchange(): lax.ppermute(values, axis, [(i, i ^ bit) for i in range(lax.axis_size(axi...]
  transfers between devices with their start and end apart: 26 -> 26, of which waited for: 9 -> 11; matrix products, arithmetic and copies ran while one was open for 0% -> 0% of each run, Pallas kernels for 18% -> 25%
where the time goes in v7:
time: 203 us; the launch traced here: 202 us
  Pallas kernels  113 us (56%)
  starting transfers between devices  42.6 us (21%)
  waiting for transfers between devices  42.6 us (21%)
    pallas_call x1, Pallas kernels, forward(): pl.pallas_call(functools.partial(forward_kernel, rows=rows, cols=cols, co...  54.1 us
    ppermute x22, waiting for transfers between devices, exchange(): lax.ppermute(values, axis, [(i, i ^ bit) for i in range(lax.axis_size(axi...  38.7 us
    ppermute x22, starting transfers between devices, exchange(): lax.ppermute(values, axis, [(i, i ^ bit) for i in range(lax.axis_size(axi...  34.4 us
    pallas_call x9, Pallas kernels, combine(): pl.pallas_call(kernel, in_specs=[in_smem()] + [in_hbm()] * (len(arrays) +...  30 us
    pallas_call x1, Pallas kernels, backward(): pl.pallas_call(functools.partial(backward_kernel, rows=rows, cols=cols),...  29.4 us
    ppermute x4, starting transfers between devices, neighbour_rows(): return (lax.ppermute(bottom, 'ha', up), lax.ppermute(top, 'ha', down))  8.2 us
  transfers between devices with their start and end apart: 26, of which 11 were waited for; matrix products, arithmetic and copies ran while one was open for 0% of the time, Pallas kernels for 25%

profile of v7, /device:TPU:0, one launch (start us, length us, event | category | flops | bytes accessed | tf_op | source)
XLA Modules:
  0.0 202.1 jit_solution(18056530474441328599)
XLA Ops:
  0.6 1.2 fusion
  1.8 2.4 %collective-permute-start = (f32[192,512]{1,0:T(8,128)S(1)}, f32[192,512]{1,0:T(8,128)S(1)}, u32[]{:S(2)}, u32[]{:S(2)}) collective-permute-start(f32[192,512]{1,0:T(8,128)S(1)} %bitcast.35), channel_id=1, source_target_pairs={{0,4},{4,8},{8,12},{12,16},{16,20},{20,24},{24,28},{1,5},{5,9},{9,... | collective-permute-start | bytes 1179656 | tf_op jit(solution)/shard_map/ppermute | solution.py:890
  4.2 1.3 collective-permute-start.1
  5.5 0.6 pad_add_fusion.place_ref
  6.1 3.9 %collective-permute-done.1.below_hbm = f32[192,512]{1,0:T(8,128)S(1)} collective-permute-done((f32[192,512]{1,0:T(8,128)S(1)}, f32[192,512]{1,0:T(8,128)S(1)}, u32[]{:S(2)}, u32[]{:S(2)}) %collective-permute-start.1) | collective-permute-done | bytes 393248 | tf_op jit(solution)/shard_map/ppermute | solution.py:890
  10.0 0.8 copy-done.1
  10.7 54.1 %shard_map.272 = (f32[8,512,128]{2,1,0:T(8,128)}, f32[512,512]{1,0:T(8,128)}, f32[512,512]{1,0:T(8,128)}, f32[8,512,128]{2,1,0:T(8,128)}, f32[8,192,128]{2,1,0:T...) custom-call(s32[2]{0:T(128)} %pad_add_fusion.place_ref, ...), custom_call_target="tpu_custom_call" | custom-call | flops 49500000256 | tf_op jit(solution)/shard_map/pallas_call | solution.py:522
  64.8 6.0 %collective-permute-start.4 = (f32[4,4,384,128]{3,2,1,0:T(8,128)}, f32[4,4,384,128]{3,2,1,0:T(8,128)}, u32[]{:S(2)}, u32[]{:S(2)}) collective-permute-start(f32[4,4,384,128]{3,2,1,0:T(8,128)} %get-tuple-element.67), channel_id=1, source_target_pairs={{0,4},{4,0},{8,12},{12,8},{16,20},{20,16},{24,28},{28,24},{1,5},{5... | collective-permute-start | bytes 9437192 | tf_op jit(solution)/shard_map/ppermute | solution.py:669
  70.9 0.1 collective-permute-start.6
  71.0 3.2 %collective-permute-start.2 = (f32[8,192,128]{2,1,0:T(8,128)}, f32[8,192,128]{2,1,0:T(8,128)}, u32[]{:S(2)}, u32[]{:S(2)}) collective-permute-start(f32[8,192,128]{2,1,0:T(8,128)} %get-tuple-element.61), channel_id=1, source_target_pairs={{0,4},{4,8},{8,12},{12,16},{16,20},{20,24},{24,28},{1,5},{5,9},{9,... | collective-permute-start | bytes 2359304 | tf_op jit(solution)/shard_map/ppermute | solution.py:890
  74.2 1.3 collective-permute-start.3
  75.5 1.2 collective-permute-start.5
  76.7 3.7 %collective-permute-done.5.refs_3_.refs_6_ = f32[704,128]{1,0:T(8,128)} collective-permute-done((f32[704,128]{1,0:T(8,128)}, f32[704,128]{1,0:T(8,128)}, u32[]{:S(2)}, u32[]{:S(2)}) %collective-permute-start.5) | collective-permute-done | bytes 360480 | tf_op jit(solution)/shard_map/ppermute | solution.py:669
  80.4 4.4 %shard_map.273 = (f32[1712,128]{1,0:T(8,128)}, f32[1712,128]{1,0:T(8,128)}, f32[1712,128]{1,0:T(8,128)}) custom-call(s32[2]{0:T(128)} %pad_add_fusion.place_ref, f32[6144,128]{1,0:T(8,128)} %bitcast.29, f32[6144,128]{1,0:T(8,128)} %bitcast.13.refs_1_, f32[704,128]{1,0:T(8,128)} %get-tuple-element.68.refs_2_.refs_5_, ...), custom_call_target="tpu_custom_call" | custom-call | flops 3992595200 | tf_op jit(solution)/shard_map/pallas_call | solution.py:777
  84.8 1.6 collective-permute-start.7
  86.4 1.5 collective-permute-start.8
  87.9 0.5 collective-permute-start.9
  88.4 3.1 %shard_map.274.rest_3_ = f32[1536,128]{1,0:T(8,128)} custom-call(s32[2]{0:T(128)} %pad_add_fusion.place_ref, f32[3072,128]{1,0:T(8,128)} %bitcast.25, f32[3072,128]{1,0:T(8,128)} %bitcast.15.refs_1_.refs_8_.refs_9_, f32[1712,128]{1,0:T(8,128)} %get-tuple-element.70.refs_2_.rest_0_, f32[1712,128]{1,0:T(8,128)} %get-tuple-element.71.refs_3_.rest_1_, ...), custom_call_target="tpu_custom_call" | custom-call | flops 1965075200 | tf_op jit(solution)/shard_map/pallas_call | solution.py:777
  91.5 2.7 %collective-permute-start.10 = (f32[1536,128]{1,0:T(8,128)}, f32[1536,128]{1,0:T(8,128)}, u32[]{:S(2)}, u32[]{:S(2)}) collective-permute-start(f32[1536,128]{1,0:T(8,128)} %shard_map.274.rest_3_), channel_id=1, source_target_pairs={{0,16},{4,20},{8,24},{12,28},{16,0},{20,4},{24,8},{28,12},{1,17},{... | collective-permute-start | bytes 2359304 | tf_op jit(solution)/shard_map/ppermute | solution.py:669
  94.1 29.4 %shard_map.275 = (f32[512,512]{1,0:T(8,128)}, f32[4,4,128,128]{3,2,1,0:T(8,128)}, f32[4,4,128,128]{3,2,1,0:T(8,128)}, f32[224,128]{1,0:T(8,128)}, f32[224,128]{1,0:T(8,128)}) custom-call(s32[2]{0:T(128)} %pad_add_fusion.place_ref, s32[64,64]{1,0:T(8,128)} %bitcast.40, s32[64,64]{1,0:T(8,128)} %bitcast.41, ...), custom_call_target="tpu_custom_call" | custom-call | flops 27499999232 | tf_op jit(solution)/shard_map/pallas_call | solution.py:639
  123.5 5.3 %collective-permute-done.10.refs_5_.refs_9_.refs_2_.refs_10_ = f32[1536,128]{1,0:T(8,128)} collective-permute-done((f32[1536,128]{1,0:T(8,128)}, f32[1536,128]{1,0:T(8,128)}, u32[]{:S(2)}, u32[]{:S(2)}) %collective-permute-start.10) | collective-permute-done | bytes 786464 | tf_op jit(solution)/shard_map/ppermute | solution.py:669
  128.9 0.1 collective-permute-start.11
  129.0 0.5 collective-permute-start.12
  129.5 4.1 %shard_map.277 = (f32[1328,128]{1,0:T(8,128)}, f32[560,128]{1,0:T(8,128)}, f32[560,128]{1,0:T(8,128)}) custom-call(s32[2]{0:T(128)} %pad_add_fusion.place_ref, f32[6144,128]{1,0:T(8,128)} %bitcast.30, f32[6144,128]{1,0:T(8,128)} %bitcast.13.refs_1_, f32[1712,128]{1,0:T(8,128)} %collective-permute-done.7.refs_2_, f32[1712,128]{1,0:T(8,128)} %collective-permute-done.8.refs_3_, ...), custom_call_target="tpu_custom_call" | custom-call | flops 3238658048 | tf_op jit(solution)/shard_map/pallas_call | solution.py:777
  133.6 2.2 %collective-permute-start.17 = (f32[560,128]{1,0:T(8,128)}, f32[560,128]{1,0:T(8,128)}, u32[]{:S(2)}, u32[]{:S(2)}) collective-permute-start(f32[560,128]{1,0:T(8,128)} %get-tuple-element.83.refs_5_), channel_id=1, source_target_pairs={{0,16},{4,20},{8,24},{12,28},{16,0},{20,4},{24,8},{28,12},{1,17},{... | collective-permute-start | bytes 860168 | tf_op jit(solution)/shard_map/ppermute | solution.py:669
  135.8 2.9 %shard_map.278 = (f32[736,128]{1,0:T(8,128)}, f32[736,128]{1,0:T(8,128)}, f32[736,128]{1,0:T(8,128)}) custom-call(s32[2]{0:T(128)} %pad_add_fusion.place_ref, f32[2048,128]{1,0:T(8,128)} %bitcast.50, f32[2048,128]{1,0:T(8,128)} %bitcast.18.refs_1_, f32[224,128]{1,0:T(8,128)} %get-tuple-element.80.refs_2_, f32[224,128]{1,0:T(8,128)} %collective-permute-done.12.refs_3_, ...), custom_call_target="tpu_custom_call" | custom-call | flops 2175336448 | tf_op jit(solution)/shard_map/pallas_call | solution.py:777
  138.7 1.6 collective-permute-start.14
  140.3 1.4 collective-permute-start.15
  141.7 0.5 collective-permute-start.13
  142.3 12.8 %collective-permute-done.17.refs_1_.refs_7_.refs_5_.refs_6_ = f32[560,128]{1,0:T(8,128)} collective-permute-done((f32[560,128]{1,0:T(8,128)}, f32[560,128]{1,0:T(8,128)}, u32[]{:S(2)}, u32[]{:S(2)}) %collective-permute-start.17) | collective-permute-done | bytes 286752 | tf_op jit(solution)/shard_map/ppermute | solution.py:669
  155.1 1.7 collective-permute-start.18
  156.8 0.4 collective-permute-done.16.refs_6_.refs_3_.refs_5_
  157.3 8.3 %collective-permute-done.18.refs_8_.refs_6_.refs_7_ = f32[560,128]{1,0:T(8,128)} collective-permute-done((f32[560,128]{1,0:T(8,128)}, f32[560,128]{1,0:T(8,128)}, u32[]{:S(2)}, u32[]{:S(2)}) %collective-permute-start.18) | collective-permute-done | bytes 286752 | tf_op jit(solution)/shard_map/ppermute | solution.py:669
  165.6 2.9 %shard_map.280 = (f32[352,128]{1,0:T(8,128)}, f32[352,128]{1,0:T(8,128)}, f32[352,128]{1,0:T(8,128)}) custom-call(s32[2]{0:T(128)} %pad_add_fusion.place_ref, f32[2048,128]{1,0:T(8,128)} %bitcast.51, f32[2048,128]{1,0:T(8,128)} %bitcast.18.refs_1_, f32[736,128]{1,0:T(8,128)} %collective-permute-done.13.refs_2_, f32[736,128]{1,0:T(8,128)} %collective-permute-done.14.refs_3_, ...), custom_call_target="tpu_custom_call" | custom-call | flops 1826903424 | tf_op jit(solution)/shard_map/pallas_call | solution.py:777
  168.6 6.6 %collective-permute-start.20 = (f32[352,128]{1,0:T(8,128)}, f32[352,128]{1,0:T(8,128)}, u32[]{:S(2)}, u32[]{:S(2)}) collective-permute-start(f32[352,128]{1,0:T(8,128)} %get-tuple-element.89.refs_8_), channel_id=1, source_target_pairs={{0,16},{4,20},{8,24},{12,28},{16,0},{20,4},{24,8},{28,12},{1,17},{... | collective-permute-start | bytes 540680 | tf_op jit(solution)/shard_map/ppermute | solution.py:669
  175.2 3.0 %shard_map.282 = (f32[368,128]{1,0:T(8,128)}, f32[368,128]{1,0:T(8,128)}, f32[368,128]{1,0:T(8,128)}) custom-call(s32[2]{0:T(128)} %pad_add_fusion.place_ref, f32[3072,128]{1,0:T(8,128)} %bitcast.27, f32[3072,128]{1,0:T(8,128)} %bitcast.15.refs_1_.refs_8_.refs_9_, f32[1536,128]{1,0:T(8,128)} %collective-permute-done.10.refs_5_.refs_9_.refs_2_.refs_10_, ...), custom_call_target="tpu_custom_call" | custom-call | flops 1871959424 | tf_op jit(solution)/shard_map/pallas_call | solution.py:777
  178.2 1.6 collective-permute-start.23
  179.8 1.4 collective-permute-start.24
  181.2 0.6 collective-permute-start.22
  181.8 2.3 %collective-permute-done.20.refs_1_.refs_2_.refs_6_ = f32[352,128]{1,0:T(8,128)} collective-permute-done((f32[352,128]{1,0:T(8,128)}, f32[352,128]{1,0:T(8,128)}, u32[]{:S(2)}, u32[]{:S(2)}) %collective-permute-start.20) | collective-permute-done | bytes 180256 | tf_op jit(solution)/shard_map/ppermute | solution.py:669
  184.2 2.4 %collective-permute-start.21 = (f32[352,128]{1,0:T(8,128)}, f32[352,128]{1,0:T(8,128)}, u32[]{:S(2)}, u32[]{:S(2)}) collective-permute-start(f32[352,128]{1,0:T(8,128)} %shard_map.281), channel_id=1, source_target_pairs={{0,24},{4,28},{8,16},{12,20},{16,8},{20,12},{24,0},{28,4},{1,25},{... | collective-permute-start | bytes 540680 | tf_op jit(solution)/shard_map/ppermute | solution.py:669
  186.6 1.4 collective-permute-done.19.refs_1_.refs_5_
  188.0 1.0 collective-permute-done.23.refs_6_.refs_12_
  189.0 1.2 collective-permute-done.22.refs_5_.refs_11_
  190.2 2.1 %collective-permute-done.21.refs_3_.refs_7_ = f32[352,128]{1,0:T(8,128)} collective-permute-done((f32[352,128]{1,0:T(8,128)}, f32[352,128]{1,0:T(8,128)}, u32[]{:S(2)}, u32[]{:S(2)}) %collective-permute-start.21) | collective-permute-done | bytes 180256 | tf_op jit(solution)/shard_map/ppermute | solution.py:669
  192.3 2.7 %shard_map.283.refs_8_ = f32[928,128]{1,0:T(8,128)} custom-call(s32[2]{0:T(128)} %pad_add_fusion.place_ref, f32[352,128]{1,0:T(8,128)} %get-tuple-element.88.refs_7_.refs_0_, f32[352,128]{1,0:T(8,128)} %collective-permute-done.19.refs_1_.refs_5_, f32[352,128]{1,0:T(8,128)} %collective-permute-done.20.refs_1_.refs_2_.refs_6_, ...), custom_call_target="tpu_custom_call" | custom-call | flops 1574589824 | tf_op jit(solution)/shard_map/pallas_call | solution.py:777
  195.1 3.3 %shard_map.285 = (f32[128,256]{1,0:T(8,128)}, f32[64,512]{1,0:T(8,128)}, f32[64,128]{1,0:T(8,128)}) custom-call(s32[2]{0:T(128)} %pad_add_fusion.place_ref, f32[6144,128]{1,0:T(8,128)} %bitcast.31, f32[6144,128]{1,0:T(8,128)} %bitcast.13.refs_1_, f32[1712,128]{1,0:T(8,128)} %collective-permute-done.7.refs_2_, f32[1712,128]{1,0:T(8,128)} %collective-permute-done.8.refs_3_, ...), custom_call_target="tpu_custom_call" | custom-call | flops 2037164800 | tf_op jit(solution)/shard_map/pallas_call | solution.py:777
  198.4 3.5 %shard_map.284 = (f32[128,128]{1,0:T(8,128)}, f32[49,960]{1,0:T(8,128)}, f32[1,512]{1,0:T(1,128)}, f32[1,512]{1,0:T(1,128)}, f32[1,512]{1,0:T(1,128)}, /*index=5...) custom-call(s32[2]{0:T(128)} %pad_add_fusion.place_ref, ...), custom_call_target="tpu_custom_call" | custom-call | flops 2013134976 | tf_op jit(solution)/shard_map/pallas_call | solution.py:777
  (24 shorter events, 0.3 us)
Async XLA Ops:
  1.8 4.2 %collective-permute-start = (f32[192,512]{1,0:T(8,128)S(1)}, f32[192,512]{1,0:T(8,128)S(1)}, u32[]{:S(2)}, u32[]{:S(2)}) collective-permute-start(f32[192,512]{1,0:T(8,128)S(1)} %bitcast.35), channel_id=1, source_target_pairs={{0,4},{4,8},{8,12},{12,16},{16,20},{20,24},{24,28},{1,5},{5,9},{9,... | collective-permute-start | bytes 1179656 | tf_op jit(solution)/shard_map/ppermute | solution.py:890
  4.2 5.8 %collective-permute-start.1 = (f32[192,512]{1,0:T(8,128)S(1)}, f32[192,512]{1,0:T(8,128)S(1)}, u32[]{:S(2)}, u32[]{:S(2)}) collective-permute-start(f32[192,512]{1,0:T(8,128)S(1)} %bitcast.34), channel_id=1, source_target_pairs={{4,0},{8,4},{12,8},{16,12},{20,16},{24,20},{28,24},{5,1},{9,5},{13... | collective-permute-start | bytes 1179656 | tf_op jit(solution)/shard_map/ppermute | solution.py:890
  6.1 3.9 %copy-start = (f32[192,512]{1,0:T(8,128)}, f32[192,512]{1,0:T(8,128)S(1)}, u32[]{:S(2)}) copy-start(f32[192,512]{1,0:T(8,128)S(1)} %collective-permute-done.above_hbm) | copy-start | bytes 1179652
  10.0 0.8 copy-start.1
  64.8 15.6 %collective-permute-start.4 = (f32[4,4,384,128]{3,2,1,0:T(8,128)}, f32[4,4,384,128]{3,2,1,0:T(8,128)}, u32[]{:S(2)}, u32[]{:S(2)}) collective-permute-start(f32[4,4,384,128]{3,2,1,0:T(8,128)} %get-tuple-element.67), channel_id=1, source_target_pairs={{0,4},{4,0},{8,12},{12,8},{16,20},{20,16},{24,28},{28,24},{1,5},{5... | collective-permute-start | bytes 9437192 | tf_op jit(solution)/shard_map/ppermute | solution.py:669
  70.9 17.5 %collective-permute-start.6 = (f32[4,4,192,128]{3,2,1,0:T(8,128)}, f32[4,4,192,128]{3,2,1,0:T(8,128)}, u32[]{:S(2)}, u32[]{:S(2)}) collective-permute-start(f32[4,4,192,128]{3,2,1,0:T(8,128)} %get-tuple-element.74), channel_id=1, source_target_pairs={{0,4},{4,0},{8,12},{12,8},{16,20},{20,16},{24,28},{28,24},{1,5},{5... | collective-permute-start | bytes 4718600 | tf_op jit(solution)/shard_map/ppermute | solution.py:669
  71.0 16.9 %collective-permute-start.2 = (f32[8,192,128]{2,1,0:T(8,128)}, f32[8,192,128]{2,1,0:T(8,128)}, u32[]{:S(2)}, u32[]{:S(2)}) collective-permute-start(f32[8,192,128]{2,1,0:T(8,128)} %get-tuple-element.61), channel_id=1, source_target_pairs={{0,4},{4,8},{8,12},{12,16},{16,20},{20,24},{24,28},{1,5},{5,9},{9,... | collective-permute-start | bytes 2359304 | tf_op jit(solution)/shard_map/ppermute | solution.py:890
  74.2 14.2 %collective-permute-start.3 = (f32[8,192,128]{2,1,0:T(8,128)}, f32[8,192,128]{2,1,0:T(8,128)}, u32[]{:S(2)}, u32[]{:S(2)}) collective-permute-start(f32[8,192,128]{2,1,0:T(8,128)} %get-tuple-element.63), channel_id=1, source_target_pairs={{4,0},{8,4},{12,8},{16,12},{20,16},{24,20},{28,24},{5,1},{9,5},{13... | collective-permute-start | bytes 2359304 | tf_op jit(solution)/shard_map/ppermute | solution.py:890
  75.5 4.9 %collective-permute-start.5 = (f32[704,128]{1,0:T(8,128)}, f32[704,128]{1,0:T(8,128)}, u32[]{:S(2)}, u32[]{:S(2)}) collective-permute-start(f32[704,128]{1,0:T(8,128)} %get-tuple-element.69), channel_id=1, source_target_pairs={{0,4},{4,0},{8,12},{12,8},{16,20},{20,16},{24,28},{28,24},{1,5},{5... | collective-permute-start | bytes 1081352 | tf_op jit(solution)/shard_map/ppermute | solution.py:669
  84.8 44.0 %collective-permute-start.7 = (f32[1712,128]{1,0:T(8,128)}, f32[1712,128]{1,0:T(8,128)}, u32[]{:S(2)}, u32[]{:S(2)}) collective-permute-start(f32[1712,128]{1,0:T(8,128)} %get-tuple-element.70.refs_2_.rest_0_), channel_id=1, source_target_pairs={{0,1},{1,0},{2,3},{3,2},{4,5},{5,4},{6,7},{7,6},{8,9},{9,8},{10,11... | collective-permute-start | bytes 2629640 | tf_op jit(solution)/shard_map/ppermute | solution.py:669
  86.4 42.5 %collective-permute-start.8 = (f32[1712,128]{1,0:T(8,128)}, f32[1712,128]{1,0:T(8,128)}, u32[]{:S(2)}, u32[]{:S(2)}) collective-permute-start(f32[1712,128]{1,0:T(8,128)} %get-tuple-element.71.refs_3_.rest_1_), channel_id=1, source_target_pairs={{0,2},{1,3},{2,0},{3,1},{4,6},{5,7},{6,4},{7,5},{8,10},{9,11},{10,... | collective-permute-start | bytes 2629640 | tf_op jit(solution)/shard_map/ppermute | solution.py:669
  87.9 41.0 %collective-permute-start.9 = (f32[1712,128]{1,0:T(8,128)}, f32[1712,128]{1,0:T(8,128)}, u32[]{:S(2)}, u32[]{:S(2)}) collective-permute-start(f32[1712,128]{1,0:T(8,128)} %get-tuple-element.72.refs_4_.rest_2_), channel_id=1, source_target_pairs={{0,3},{1,2},{2,1},{3,0},{4,7},{5,6},{6,5},{7,4},{8,11},{9,10},{10,... | collective-permute-start | bytes 2629640 | tf_op jit(solution)/shard_map/ppermute | solution.py:669
  91.5 37.4 %collective-permute-start.10 = (f32[1536,128]{1,0:T(8,128)}, f32[1536,128]{1,0:T(8,128)}, u32[]{:S(2)}, u32[]{:S(2)}) collective-permute-start(f32[1536,128]{1,0:T(8,128)} %shard_map.274.rest_3_), channel_id=1, source_target_pairs={{0,16},{4,20},{8,24},{12,28},{16,0},{20,4},{24,8},{28,12},{1,17},{... | collective-permute-start | bytes 2359304 | tf_op jit(solution)/shard_map/ppermute | solution.py:669
  128.9 6.9 %collective-permute-start.11 = (f32[4,4,128,128]{3,2,1,0:T(8,128)}, f32[4,4,128,128]{3,2,1,0:T(8,128)}, u32[]{:S(2)}, u32[]{:S(2)}) collective-permute-start(f32[4,4,128,128]{3,2,1,0:T(8,128)} %get-tuple-element.79), channel_id=1, source_target_pairs={{0,4},{4,0},{8,12},{12,8},{16,20},{20,16},{24,28},{28,24},{1,5},{5... | collective-permute-start | bytes 3145736 | tf_op jit(solution)/shard_map/ppermute | solution.py:669
  129.0 6.8 %collective-permute-start.12 = (f32[224,128]{1,0:T(8,128)}, f32[224,128]{1,0:T(8,128)}, u32[]{:S(2)}, u32[]{:S(2)}) collective-permute-start(f32[224,128]{1,0:T(8,128)} %get-tuple-element.81), channel_id=1, source_target_pairs={{0,4},{4,0},{8,12},{12,8},{16,20},{20,16},{24,28},{28,24},{1,5},{5... | collective-permute-start | bytes 344072 | tf_op jit(solution)/shard_map/ppermute | solution.py:669
  133.5 23.8 %collective-permute-start.16 = (f32[1328,128]{1,0:T(8,128)}, f32[1328,128]{1,0:T(8,128)}, u32[]{:S(2)}, u32[]{:S(2)}) collective-permute-start(f32[1328,128]{1,0:T(8,128)} %get-tuple-element.82.refs_4_), channel_id=1, source_target_pairs={{0,8},{4,12},{8,0},{12,4},{16,24},{20,28},{24,16},{28,20},{1,9},{5... | collective-permute-start | bytes 2039816 | tf_op jit(solution)/shard_map/ppermute | solution.py:669
  133.6 21.5 %collective-permute-start.17 = (f32[560,128]{1,0:T(8,128)}, f32[560,128]{1,0:T(8,128)}, u32[]{:S(2)}, u32[]{:S(2)}) collective-permute-start(f32[560,128]{1,0:T(8,128)} %get-tuple-element.83.refs_5_), channel_id=1, source_target_pairs={{0,16},{4,20},{8,24},{12,28},{16,0},{20,4},{24,8},{28,12},{1,17},{... | collective-permute-start | bytes 860168 | tf_op jit(solution)/shard_map/ppermute | solution.py:669
  138.7 26.9 %collective-permute-start.14 = (f32[736,128]{1,0:T(8,128)}, f32[736,128]{1,0:T(8,128)}, u32[]{:S(2)}, u32[]{:S(2)}) collective-permute-start(f32[736,128]{1,0:T(8,128)} %get-tuple-element.86), channel_id=1, source_target_pairs={{0,2},{1,3},{2,0},{3,1},{4,6},{5,7},{6,4},{7,5},{8,10},{9,11},{10,... | collective-permute-start | bytes 1130504 | tf_op jit(solution)/shard_map/ppermute | solution.py:669
  140.3 25.3 %collective-permute-start.15 = (f32[736,128]{1,0:T(8,128)}, f32[736,128]{1,0:T(8,128)}, u32[]{:S(2)}, u32[]{:S(2)}) collective-permute-start(f32[736,128]{1,0:T(8,128)} %get-tuple-element.87), channel_id=1, source_target_pairs={{0,3},{1,2},{2,1},{3,0},{4,7},{5,6},{6,5},{7,4},{8,11},{9,10},{10,... | collective-permute-start | bytes 1130504 | tf_op jit(solution)/shard_map/ppermute | solution.py:669
  141.7 23.9 %collective-permute-start.13 = (f32[736,128]{1,0:T(8,128)}, f32[736,128]{1,0:T(8,128)}, u32[]{:S(2)}, u32[]{:S(2)}) collective-permute-start(f32[736,128]{1,0:T(8,128)} %get-tuple-element.85.refs_5_), channel_id=1, source_target_pairs={{0,1},{1,0},{2,3},{3,2},{4,5},{5,4},{6,7},{7,6},{8,9},{9,8},{10,11... | collective-permute-start | bytes 1130504 | tf_op jit(solution)/shard_map/ppermute | solution.py:669
  155.1 10.5 %collective-permute-start.18 = (f32[560,128]{1,0:T(8,128)}, f32[560,128]{1,0:T(8,128)}, u32[]{:S(2)}, u32[]{:S(2)}) collective-permute-start(f32[560,128]{1,0:T(8,128)} %shard_map.279), channel_id=1, source_target_pairs={{0,24},{4,28},{8,16},{12,20},{16,8},{20,12},{24,0},{28,4},{1,25},{... | collective-permute-start | bytes 860168 | tf_op jit(solution)/shard_map/ppermute | solution.py:669
  168.6 15.6 %collective-permute-start.20 = (f32[352,128]{1,0:T(8,128)}, f32[352,128]{1,0:T(8,128)}, u32[]{:S(2)}, u32[]{:S(2)}) collective-permute-start(f32[352,128]{1,0:T(8,128)} %get-tuple-element.89.refs_8_), channel_id=1, source_target_pairs={{0,16},{4,20},{8,24},{12,28},{16,0},{20,4},{24,8},{28,12},{1,17},{... | collective-permute-start | bytes 540680 | tf_op jit(solution)/shard_map/ppermute | solution.py:669
  178.2 10.8 %collective-permute-start.23 = (f32[368,128]{1,0:T(8,128)}, f32[368,128]{1,0:T(8,128)}, u32[]{:S(2)}, u32[]{:S(2)}) collective-permute-start(f32[368,128]{1,0:T(8,128)} %get-tuple-element.92), channel_id=1, source_target_pairs={{0,2},{1,3},{2,0},{3,1},{4,6},{5,7},{6,4},{7,5},{8,10},{9,11},{10,... | collective-permute-start | bytes 565256 | tf_op jit(solution)/shard_map/ppermute | solution.py:669
  179.8 9.2 %collective-permute-start.24 = (f32[368,128]{1,0:T(8,128)}, f32[368,128]{1,0:T(8,128)}, u32[]{:S(2)}, u32[]{:S(2)}) collective-permute-start(f32[368,128]{1,0:T(8,128)} %get-tuple-element.93), channel_id=1, source_target_pairs={{0,3},{1,2},{2,1},{3,0},{4,7},{5,6},{6,5},{7,4},{8,11},{9,10},{10,... | collective-permute-start | bytes 565256 | tf_op jit(solution)/shard_map/ppermute | solution.py:669
  181.2 9.0 %collective-permute-start.22 = (f32[368,128]{1,0:T(8,128)}, f32[368,128]{1,0:T(8,128)}, u32[]{:S(2)}, u32[]{:S(2)}) collective-permute-start(f32[368,128]{1,0:T(8,128)} %get-tuple-element.91.refs_4_), channel_id=1, source_target_pairs={{0,1},{1,0},{2,3},{3,2},{4,5},{5,4},{6,7},{7,6},{8,9},{9,8},{10,11... | collective-permute-start | bytes 565256 | tf_op jit(solution)/shard_map/ppermute | solution.py:669
  181.8 6.2 %collective-permute-start.19 = (f32[352,128]{1,0:T(8,128)}, f32[352,128]{1,0:T(8,128)}, u32[]{:S(2)}, u32[]{:S(2)}) collective-permute-start(f32[352,128]{1,0:T(8,128)} %get-tuple-element.88.refs_7_.refs_0_), channel_id=1, source_target_pairs={{0,8},{4,12},{8,0},{12,4},{16,24},{20,28},{24,16},{28,20},{1,9},{5... | collective-permute-start | bytes 540680 | tf_op jit(solution)/shard_map/ppermute | solution.py:669
  184.2 8.1 %collective-permute-start.21 = (f32[352,128]{1,0:T(8,128)}, f32[352,128]{1,0:T(8,128)}, u32[]{:S(2)}, u32[]{:S(2)}) collective-permute-start(f32[352,128]{1,0:T(8,128)} %shard_map.281), channel_id=1, source_target_pairs={{0,24},{4,28},{8,16},{12,20},{16,8},{20,12},{24,0},{28,4},{1,25},{... | collective-permute-start | bytes 540680 | tf_op jit(solution)/shard_map/ppermute | solution.py:669
  195.0 3.4 %collective-permute-start.25 = (f32[928,128]{1,0:T(8,128)}, f32[928,128]{1,0:T(8,128)}, u32[]{:S(2)}, u32[]{:S(2)}) collective-permute-start(f32[928,128]{1,0:T(8,128)} %shard_map.283.refs_8_), channel_id=1, source_target_pairs={{0,4},{4,0},{8,12},{12,8},{16,20},{20,16},{24,28},{28,24},{1,5},{5... | collective-permute-start | bytes 1425416 | tf_op jit(solution)/shard_map/ppermute | solution.py:669

commit v8 on v7

--- a/solution.py
+++ b/solution.py
@@ -793,6 +793,7 @@
         out_shape=[shape_of(*array.shape) for array in arrays],
         input_output_aliases={k: k for k in range(len(arrays))},
         compiler_params=params(),
+        cost_estimate=lasting(0.5),
     )(*arrays, *ties)
 
 
@@ -847,11 +848,20 @@
     def __init__(self, members, way):
         self.members, self.way = members, way
         line, near = lax.axis_size("ha") // 2, lax.axis_size("ha") // 4
-        self.steps = {"plane": range(1, lax.axis_size("ba")), "line": range(1, line), "far": [near]}[way]
+        self.steps = {
+            "plane": range(1, lax.axis_size("ba")),
+            "line": range(1, line),
+            "far": [near],
+            "halves": range(1, near + 1),
+        }[way]
         self.near = near
 
     def taking(self, step):
-        return [(one, way) for one, way in self.members if way != "near" or step < self.near]
+        return [
+            (one, way)
+            for one, way in self.members
+            if way not in ("near", "far") or (way == "near") == (step < self.near)
+        ]
 
     def groups(self):
         return [
@@ -878,8 +888,10 @@
         return arrived
 
 
-def run(place, stage, ties=(), in_turn=False):
+def run(place, stage, ties=(), in_turn=False, late_ties=()):
     made = list(combine(place, stage.groups(), ties))
+    if late_ties:
+        made = list(tied(made, late_ties))
     return made, stage.go(made, in_turn)
 
 
@@ -980,11 +992,15 @@
     )
     above, below = neighbour_rows(dconv_top, dconv_bottom)
 
+    packed = Sum([packed_kept, exchange(packed_sent, "ha", 1)], ["plane"])
     plane_sum = Sum([plane_kept, exchange(plane_sent, "ha", 1)], ["plane", "far", "near"])
     line_sum = Sum([line_kept, exchange(line_sent, "ha", 1)], ["far", "near", "plane"])
-    packed = Sum([packed_kept, exchange(packed_sent, "ha", 1)], ["plane"])
-    made, arrived = run(place, Stage([(plane_sum, "plane"), (packed, "plane")], "plane"))
-    more, far = run(place, Stage([(line_sum, "far")], "far"), ties=made + [above, below])
+    first, _ = run(place, Stage([(packed, "plane")], "plane"))
+    packed = Rider(packed.views)
+    made, arrived = run(place, Stage([(plane_sum, "plane")], "plane"), ties=first)
+    more, far = run(
+        place, Stage([(line_sum, "far"), (packed, "far")], "far"), ties=made, late_ties=[above, below]
+    )
     made, arrived = made + more, arrived + far
     dcanvas, in_kept, in_sent, small_kept, small_sent = backward(
         place, ids, above, dconv, below, joined, depth_kernel, own, gain, dmiddle, weight_in, made,
@@ -995,10 +1011,12 @@
     small = Rider([flat_view(small_kept), flat_view(exchange(small_sent, "ha", 1))])
     packed = Rider(packed.views)
     made, arrived = run(
-        place, Stage([(plane_sum, "line"), (packed, "line"), (line_sum, "near")], "line"), in_turn=True
+        place, Stage([(plane_sum, "far"), (line_sum, "near"), (packed, "near")], "halves")
     )
     run(place, Stage([(in_sum, "plane"), (small, "plane")], "plane"), ties=made)
-    made, _ = run(place, Stage([(in_sum, "line"), (small, "line")], "line"), ties=arrived, in_turn=True)
+    made, _ = run(
+        place, Stage([(plane_sum, "near"), (in_sum, "line"), (small, "line")], "line"), ties=arrived, in_turn=True
+    )
     packed = Gather(packed.views)
     run(place, Stage([(line_sum, "plane"), (packed, "plane")], "plane"), ties=made)
     cut = plane_sum.views[0].rows // 2
@@ -1021,7 +1039,7 @@
             shape_of(dim // count_ha, dim // count_ba),
         ],
     )
-    (halves_of,) = combine(place, [[small.views] + packed.gathered])
+    (halves_of,) = combine(place, [[small.views] + packed.gathered], ties=[dup])
     din, dkern, dgain_one, dscale_one, dgain_two, dscale_two, dfirst, dsecond, dthird, _ = combine(
         place,
         [[in_sum.views, [flat_view(halves_of)], [flat_view(exchange(halves_of, "ha", 1))]]],

time: 203 us -> 202 us (level)
  starting transfers between devices: 42.6 us -> 40.2 us
    pallas_call x9 -> x10, Pallas kernels: 30 us -> 32 us  [combine(): pl.pallas_call(kernel, in_specs=[in_smem()] + [in_hbm()] * (len(arrays) +...]
    ppermute x22 -> x24, starting transfers between devices: 34.4 us -> 32.4 us  [exchange(): lax.ppermute(values, axis, [(i, i ^ bit) for i in range(lax.axis_size(axi...]
    ppermute x22 -> x24, waiting for transfers between devices: 38.7 us -> 37.5 us  [exchange(): lax.ppermute(values, axis, [(i, i ^ bit) for i in range(lax.axis_size(axi...]
  transfers between devices with their start and end apart: 26 -> 28, of which waited for: 11 -> 12; matrix products, arithmetic and copies ran while one was open for 0% -> 0% of each run, Pallas kernels for 25% -> 26%
where the time goes in v8:
time: 202 us; the launch traced here: 201 us
  Pallas kernels  115 us (57%)
  waiting for transfers between devices  41.4 us (20%)
  starting transfers between devices  40.2 us (20%)
    pallas_call x1, Pallas kernels, forward(): pl.pallas_call(functools.partial(forward_kernel, rows=rows, cols=cols, co...  54.1 us
    ppermute x24, waiting for transfers between devices, exchange(): lax.ppermute(values, axis, [(i, i ^ bit) for i in range(lax.axis_size(axi...  37.5 us
    ppermute x24, starting transfers between devices, exchange(): lax.ppermute(values, axis, [(i, i ^ bit) for i in range(lax.axis_size(axi...  32.4 us
    pallas_call x10, Pallas kernels, combine(): pl.pallas_call(kernel, in_specs=[in_smem()] + [in_hbm()] * (len(arrays) +...  32 us
    pallas_call x1, Pallas kernels, backward(): pl.pallas_call(functools.partial(backward_kernel, rows=rows, cols=cols),...  29.4 us
    ppermute x4, starting transfers between devices, neighbour_rows(): return (lax.ppermute(bottom, 'ha', up), lax.ppermute(top, 'ha', down))  7.81 us
  transfers between devices with their start and end apart: 28, of which 12 were waited for; matrix products, arithmetic and copies ran while one was open for 0% of the time, Pallas kernels for 26%

profile of v8, /device:TPU:0, one launch (start us, length us, event | category | flops | bytes accessed | tf_op | source)
XLA Modules:
  0.0 200.7 jit_solution(3780274612130513219)
XLA Ops:
  0.6 1.2 fusion
  1.8 2.4 %collective-permute-start = (f32[192,512]{1,0:T(8,128)S(1)}, f32[192,512]{1,0:T(8,128)S(1)}, u32[]{:S(2)}, u32[]{:S(2)}) collective-permute-start(f32[192,512]{1,0:T(8,128)S(1)} %bitcast.39), channel_id=1, source_target_pairs={{0,4},{4,8},{8,12},{12,16},{16,20},{20,24},{24,28},{1,5},{5,9},{9,... | collective-permute-start | bytes 1179656 | tf_op jit(solution)/shard_map/ppermute | solution.py:902
  4.2 1.3 collective-permute-start.1
  5.5 0.6 pad_add_fusion.place_ref
  6.1 3.9 %collective-permute-done.1.below_hbm = f32[192,512]{1,0:T(8,128)S(1)} collective-permute-done((f32[192,512]{1,0:T(8,128)S(1)}, f32[192,512]{1,0:T(8,128)S(1)}, u32[]{:S(2)}, u32[]{:S(2)}) %collective-permute-start.1) | collective-permute-done | bytes 393248 | tf_op jit(solution)/shard_map/ppermute | solution.py:902
  10.0 0.7 copy-done.1
  10.7 54.1 %shard_map.272 = (f32[8,512,128]{2,1,0:T(8,128)}, f32[512,512]{1,0:T(8,128)}, f32[512,512]{1,0:T(8,128)}, f32[8,512,128]{2,1,0:T(8,128)}, f32[8,192,128]{2,1,0:T...) custom-call(s32[2]{0:T(128)} %pad_add_fusion.place_ref, ...), custom_call_target="tpu_custom_call" | custom-call | flops 49500000256 | tf_op jit(solution)/shard_map/pallas_call | solution.py:522
  64.8 6.0 %collective-permute-start.4 = (f32[4,4,384,128]{3,2,1,0:T(8,128)}, f32[4,4,384,128]{3,2,1,0:T(8,128)}, u32[]{:S(2)}, u32[]{:S(2)}) collective-permute-start(f32[4,4,384,128]{3,2,1,0:T(8,128)} %get-tuple-element.69), channel_id=1, source_target_pairs={{0,4},{4,0},{8,12},{12,8},{16,20},{20,16},{24,28},{28,24},{1,5},{5... | collective-permute-start | bytes 9437192 | tf_op jit(solution)/shard_map/ppermute | solution.py:669
  71.4 2.9 %collective-permute-start.2 = (f32[8,192,128]{2,1,0:T(8,128)}, f32[8,192,128]{2,1,0:T(8,128)}, u32[]{:S(2)}, u32[]{:S(2)}) collective-permute-start(f32[8,192,128]{2,1,0:T(8,128)} %get-tuple-element.63), channel_id=1, source_target_pairs={{0,4},{4,8},{8,12},{12,16},{16,20},{20,24},{24,28},{1,5},{5,9},{9,... | collective-permute-start | bytes 2359304 | tf_op jit(solution)/shard_map/ppermute | solution.py:902
  74.2 1.3 collective-permute-start.3
  75.5 3.7 %collective-permute-done.5.refs_1_.refs_3_ = f32[704,128]{1,0:T(8,128)} collective-permute-done((f32[704,128]{1,0:T(8,128)}, f32[704,128]{1,0:T(8,128)}, u32[]{:S(2)}, u32[]{:S(2)}) %collective-permute-start.5) | collective-permute-done | bytes 360480 | tf_op jit(solution)/shard_map/ppermute | solution.py:669
  79.3 2.5 %shard_map.273 = (f32[176,128]{1,0:T(8,128)}, f32[176,128]{1,0:T(8,128)}, f32[176,128]{1,0:T(8,128)}) custom-call(s32[2]{0:T(128)} %pad_add_fusion.place_ref, f32[704,128]{1,0:T(8,128)} %get-tuple-element.70.refs_0_.refs_2_, f32[704,128]{1,0:T(8,128)} %collective-permute-done.5.refs_1_.refs_3_), custom_call_target="tpu_custom_call" | custom-call | flops 1397369600 | tf_op jit(solution)/shard_map/pallas_call | solution.py:777
  81.8 1.6 collective-permute-start.7
  83.3 3.7 %collective-permute-done.7.refs_4_ = f32[176,128]{1,0:T(8,128)} collective-permute-done((f32[176,128]{1,0:T(8,128)}, f32[176,128]{1,0:T(8,128)}, u32[]{:S(2)}, u32[]{:S(2)}) %collective-permute-start.7) | collective-permute-done | bytes 90144 | tf_op jit(solution)/shard_map/ppermute | solution.py:669
  87.0 1.5 collective-permute-start.8
  88.6 1.4 collective-permute-start.9
  90.0 4.0 %shard_map.274 = (f32[1536,128]{1,0:T(8,128)}, f32[1536,128]{1,0:T(8,128)}, f32[1536,128]{1,0:T(8,128)}) custom-call(s32[2]{0:T(128)} %pad_add_fusion.place_ref, f32[6144,128]{1,0:T(8,128)} %bitcast.25, f32[6144,128]{1,0:T(8,128)} %bitcast.13.refs_1_.refs_5_, f32[176,128]{1,0:T(8,128)} %get-tuple-element.72.refs_2_, f32[176,128]{1,0:T(8,128)} %get-tuple-element.73.refs_3_, ...), custom_call_target="tpu_custom_call" | custom-call | flops 3695225600 | tf_op jit(solution)/shard_map/pallas_call | solution.py:777
  94.0 0.6 collective-permute-start.10
  94.7 1.9 collective-permute-start.11
  96.5 1.1 collective-permute-start.12
  97.6 3.2 %shard_map.275.refs_0_ = f32[1712,128]{1,0:T(8,128)} custom-call(s32[2]{0:T(128)} %pad_add_fusion.place_ref, f32[3072,128]{1,0:T(8,128)} %bitcast.29, f32[3072,128]{1,0:T(8,128)} %bitcast.15.refs_1_.refs_8_, f32[704,128]{1,0:T(8,128)} %get-tuple-element.70.refs_0_.refs_2_, f32[704,128]{1,0:T(8,128)} %collective-permute-done.5.refs_1_.refs_3_, ...), custom_call_target="tpu_custom_call" | custom-call | flops 2163321600 | tf_op jit(solution)/shard_map/pallas_call | solution.py:777
  100.8 2.7 %collective-permute-start.13 = (f32[1712,128]{1,0:T(8,128)}, f32[1712,128]{1,0:T(8,128)}, u32[]{:S(2)}, u32[]{:S(2)}) collective-permute-start(f32[1712,128]{1,0:T(8,128)} %shard_map.276.rest_3_.refs_3_), channel_id=1, source_target_pairs={{0,16},{4,20},{8,24},{12,28},{16,0},{20,4},{24,8},{28,12},{1,17},{... | collective-permute-start | bytes 2629640 | tf_op jit(solution)/shard_map/ppermute | solution.py:669
  103.5 29.4 %shard_map.277 = (f32[512,512]{1,0:T(8,128)}, f32[4,4,128,128]{3,2,1,0:T(8,128)}, f32[4,4,128,128]{3,2,1,0:T(8,128)}, f32[224,128]{1,0:T(8,128)}, f32[224,128]{1,0:T(8,128)}) custom-call(s32[2]{0:T(128)} %pad_add_fusion.place_ref, s32[64,64]{1,0:T(8,128)} %bitcast.44, s32[64,64]{1,0:T(8,128)} %bitcast.45, ...), custom_call_target="tpu_custom_call" | custom-call | flops 27499999232 | tf_op jit(solution)/shard_map/pallas_call | solution.py:639
  132.9 7.5 %collective-permute-done.13.refs_5_.refs_2_.refs_9_ = f32[1712,128]{1,0:T(8,128)} collective-permute-done((f32[1712,128]{1,0:T(8,128)}, f32[1712,128]{1,0:T(8,128)}, u32[]{:S(2)}, u32[]{:S(2)}) %collective-permute-start.13) | collective-permute-done | bytes 876576 | tf_op jit(solution)/shard_map/ppermute | solution.py:669
  140.4 0.5 collective-permute-start.15
  140.9 3.5 %shard_map.279 = (f32[944,128]{1,0:T(8,128)}, f32[768,128]{1,0:T(8,128)}) custom-call(s32[2]{0:T(128)} %pad_add_fusion.place_ref, f32[3072,128]{1,0:T(8,128)} %bitcast.30, f32[3072,128]{1,0:T(8,128)} %bitcast.15.refs_1_.refs_8_, f32[1712,128]{1,0:T(8,128)} %collective-permute-done.13.refs_5_.refs_2_.refs_9_, f32[1712,128]{1,0:T(8,128)} %shard_map.276.rest_3_.refs_3_, ...), custom_call_target="tpu_custom_call" | custom-call | flops 2640915200 | tf_op jit(solution)/shard_map/pallas_call | solution.py:777
  144.5 2.2 %collective-permute-start.20 = (f32[944,128]{1,0:T(8,128)}, f32[944,128]{1,0:T(8,128)}, u32[]{:S(2)}, u32[]{:S(2)}) collective-permute-start(f32[944,128]{1,0:T(8,128)} %get-tuple-element.87.refs_4_), channel_id=1, source_target_pairs={{0,8},{4,12},{8,0},{12,4},{16,24},{20,28},{24,16},{28,20},{1,9},{5... | collective-permute-start | bytes 1449992 | tf_op jit(solution)/shard_map/ppermute | solution.py:669
  146.7 3.0 %shard_map.280 = (f32[736,128]{1,0:T(8,128)}, f32[736,128]{1,0:T(8,128)}, f32[736,128]{1,0:T(8,128)}) custom-call(s32[2]{0:T(128)} %pad_add_fusion.place_ref, f32[2048,128]{1,0:T(8,128)} %bitcast.33, f32[2048,128]{1,0:T(8,128)} %bitcast.18.refs_1_.refs_7_, f32[224,128]{1,0:T(8,128)} %get-tuple-element.85.refs_2_, ...), custom_call_target="tpu_custom_call" | custom-call | flops 2175336448 | tf_op jit(solution)/shard_map/pallas_call | solution.py:777
  149.7 1.6 collective-permute-start.17
  151.3 0.5 collective-permute-start.18
  151.8 1.5 collective-permute-start.16
  153.2 11.0 %collective-permute-done.19.refs_5_.refs_13_ = f32[768,128]{1,0:T(8,128)} collective-permute-done((f32[768,128]{1,0:T(8,128)}, f32[768,128]{1,0:T(8,128)}, u32[]{:S(2)}, u32[]{:S(2)}) %collective-permute-start.19) | collective-permute-done | bytes 393248 | tf_op jit(solution)/shard_map/ppermute | solution.py:669
  164.3 2.1 %collective-permute-done.20.refs_12_.refs_3_.refs_10_ = f32[944,128]{1,0:T(8,128)} collective-permute-done((f32[944,128]{1,0:T(8,128)}, f32[944,128]{1,0:T(8,128)}, u32[]{:S(2)}, u32[]{:S(2)}) %collective-permute-start.20) | collective-permute-done | bytes 483360 | tf_op jit(solution)/shard_map/ppermute | solution.py:669
  166.4 1.9 collective-permute-done.17.refs_9_.refs_3_
  168.3 1.2 collective-permute-done.16.refs_8_.refs_2_
  169.5 3.4 %shard_map.281 = (f32[736,128]{1,0:T(8,128)}, f32[352,128]{1,0:T(8,128)}, f32[352,128]{1,0:T(8,128)}) custom-call(s32[2]{0:T(128)} %pad_add_fusion.place_ref, f32[6144,128]{1,0:T(8,128)} %bitcast.27, f32[6144,128]{1,0:T(8,128)} %bitcast.13.refs_1_.refs_5_, f32[1536,128]{1,0:T(8,128)} %collective-permute-done.10.refs_2_.refs_6_, ...), custom_call_target="tpu_custom_call" | custom-call | flops 2331530752 | tf_op jit(solution)/shard_map/pallas_call | solution.py:777
  173.3 2.5 %collective-permute-start.22 = (f32[352,128]{1,0:T(8,128)}, f32[352,128]{1,0:T(8,128)}, u32[]{:S(2)}, u32[]{:S(2)}) collective-permute-start(f32[352,128]{1,0:T(8,128)} %get-tuple-element.93.refs_6_), channel_id=1, source_target_pairs={{0,16},{4,20},{8,24},{12,28},{16,0},{20,4},{24,8},{28,12},{1,17},{... | collective-permute-start | bytes 540680 | tf_op jit(solution)/shard_map/ppermute | solution.py:669
  175.7 2.9 %shard_map.283 = (f32[368,128]{1,0:T(8,128)}, f32[368,128]{1,0:T(8,128)}, f32[368,128]{1,0:T(8,128)}) custom-call(s32[2]{0:T(128)} %pad_add_fusion.place_ref, f32[3072,128]{1,0:T(8,128)} %bitcast.31, f32[3072,128]{1,0:T(8,128)} %bitcast.15.refs_1_.refs_8_, f32[1712,128]{1,0:T(8,128)} %collective-permute-done.13.refs_5_.refs_2_.refs_9_, ...), custom_call_target="tpu_custom_call" | custom-call | flops 1805877376 | tf_op jit(solution)/shard_map/pallas_call | solution.py:777
  178.7 1.6 collective-permute-start.25
  180.8 1.5 collective-permute-start.24
  182.2 2.0 collective-permute-done.22.refs_1_.refs_2_.refs_6_
  184.2 2.4 %collective-permute-start.23 = (f32[352,128]{1,0:T(8,128)}, f32[352,128]{1,0:T(8,128)}, u32[]{:S(2)}, u32[]{:S(2)}) collective-permute-start(f32[352,128]{1,0:T(8,128)} %shard_map.282), channel_id=1, source_target_pairs={{0,24},{4,28},{8,16},{12,20},{16,8},{20,12},{24,0},{28,4},{1,25},{... | collective-permute-start | bytes 540680 | tf_op jit(solution)/shard_map/ppermute | solution.py:669
  186.6 1.0 collective-permute-done.26.refs_13_.refs_7_
  187.6 1.1 collective-permute-done.24.refs_11_.refs_5_
  188.7 3.2 %shard_map.284 = (f32[128,256]{1,0:T(8,128)}, f32[64,512]{1,0:T(8,128)}, f32[64,128]{1,0:T(8,128)}) custom-call(s32[2]{0:T(128)} %pad_add_fusion.place_ref, f32[6144,128]{1,0:T(8,128)} %bitcast.28, f32[6144,128]{1,0:T(8,128)} %bitcast.13.refs_1_.refs_5_, f32[1536,128]{1,0:T(8,128)} %collective-permute-done.10.refs_2_.refs_6_, ...), custom_call_target="tpu_custom_call" | custom-call | flops 1965075200 | tf_op jit(solution)/shard_map/pallas_call | solution.py:777
  192.0 2.8 %shard_map.285.refs_8_ = f32[928,128]{1,0:T(8,128)} custom-call(s32[2]{0:T(128)} %pad_add_fusion.place_ref, f32[736,128]{1,0:T(8,128)} %get-tuple-element.92.refs_5_.refs_0_, f32[736,128]{1,0:T(8,128)} %collective-permute-done.21.refs_6_.refs_1_.refs_5_, f32[352,128]{1,0:T(8,128)} %collective-permute-done.22.refs_1_.refs_2_.refs_6_, ...), custom_call_target="tpu_custom_call" | custom-call | flops 1574589824 | tf_op jit(solution)/shard_map/pallas_call | solution.py:777
  194.8 2.2 %collective-permute-done.27.refs_9_ = f32[928,128]{1,0:T(8,128)} collective-permute-done((f32[928,128]{1,0:T(8,128)}, f32[928,128]{1,0:T(8,128)}, u32[]{:S(2)}, u32[]{:S(2)}) %collective-permute-start.27) | collective-permute-done | bytes 475168 | tf_op jit(solution)/shard_map/ppermute | solution.py:669
  197.0 3.5 %shard_map.286 = (f32[128,128]{1,0:T(8,128)}, f32[49,960]{1,0:T(8,128)}, f32[1,512]{1,0:T(1,128)}, f32[1,512]{1,0:T(1,128)}, f32[1,512]{1,0:T(1,128)}, /*index=5...) custom-call(s32[2]{0:T(128)} %pad_add_fusion.place_ref, ...), custom_call_target="tpu_custom_call" | custom-call | flops 2013134976 | tf_op jit(solution)/shard_map/pallas_call | solution.py:777
  (29 shorter events, 1.5 us)
Async XLA Ops:
  1.8 4.3 %collective-permute-start = (f32[192,512]{1,0:T(8,128)S(1)}, f32[192,512]{1,0:T(8,128)S(1)}, u32[]{:S(2)}, u32[]{:S(2)}) collective-permute-start(f32[192,512]{1,0:T(8,128)S(1)} %bitcast.39), channel_id=1, source_target_pairs={{0,4},{4,8},{8,12},{12,16},{16,20},{20,24},{24,28},{1,5},{5,9},{9,... | collective-permute-start | bytes 1179656 | tf_op jit(solution)/shard_map/ppermute | solution.py:902
  4.2 5.8 %collective-permute-start.1 = (f32[192,512]{1,0:T(8,128)S(1)}, f32[192,512]{1,0:T(8,128)S(1)}, u32[]{:S(2)}, u32[]{:S(2)}) collective-permute-start(f32[192,512]{1,0:T(8,128)S(1)} %bitcast.38), channel_id=1, source_target_pairs={{4,0},{8,4},{12,8},{16,12},{20,16},{24,20},{28,24},{5,1},{9,5},{13... | collective-permute-start | bytes 1179656 | tf_op jit(solution)/shard_map/ppermute | solution.py:902
  6.1 3.9 %copy-start = (f32[192,512]{1,0:T(8,128)}, f32[192,512]{1,0:T(8,128)S(1)}, u32[]{:S(2)}) copy-start(f32[192,512]{1,0:T(8,128)S(1)} %collective-permute-done.above_hbm) | copy-start | bytes 1179652
  10.0 0.8 copy-start.1
  64.8 23.8 %collective-permute-start.4 = (f32[4,4,384,128]{3,2,1,0:T(8,128)}, f32[4,4,384,128]{3,2,1,0:T(8,128)}, u32[]{:S(2)}, u32[]{:S(2)}) collective-permute-start(f32[4,4,384,128]{3,2,1,0:T(8,128)} %get-tuple-element.69), channel_id=1, source_target_pairs={{0,4},{4,0},{8,12},{12,8},{16,20},{20,16},{24,28},{28,24},{1,5},{5... | collective-permute-start | bytes 9437192 | tf_op jit(solution)/shard_map/ppermute | solution.py:669
  70.9 25.7 %collective-permute-start.6 = (f32[4,4,192,128]{3,2,1,0:T(8,128)}, f32[4,4,192,128]{3,2,1,0:T(8,128)}, u32[]{:S(2)}, u32[]{:S(2)}) collective-permute-start(f32[4,4,192,128]{3,2,1,0:T(8,128)} %get-tuple-element.79), channel_id=1, source_target_pairs={{0,4},{4,0},{8,12},{12,8},{16,20},{20,16},{24,28},{28,24},{1,5},{5... | collective-permute-start | bytes 4718600 | tf_op jit(solution)/shard_map/ppermute | solution.py:669
  70.9 8.3 %collective-permute-start.5 = (f32[704,128]{1,0:T(8,128)}, f32[704,128]{1,0:T(8,128)}, u32[]{:S(2)}, u32[]{:S(2)}) collective-permute-start(f32[704,128]{1,0:T(8,128)} %get-tuple-element.71), channel_id=1, source_target_pairs={{0,4},{4,0},{8,12},{12,8},{16,20},{20,16},{24,28},{28,24},{1,5},{5... | collective-permute-start | bytes 1081352 | tf_op jit(solution)/shard_map/ppermute | solution.py:669
  71.4 29.4 %collective-permute-start.2 = (f32[8,192,128]{2,1,0:T(8,128)}, f32[8,192,128]{2,1,0:T(8,128)}, u32[]{:S(2)}, u32[]{:S(2)}) collective-permute-start(f32[8,192,128]{2,1,0:T(8,128)} %get-tuple-element.63), channel_id=1, source_target_pairs={{0,4},{4,8},{8,12},{12,16},{16,20},{20,24},{24,28},{1,5},{5,9},{9,... | collective-permute-start | bytes 2359304 | tf_op jit(solution)/shard_map/ppermute | solution.py:902
  74.2 26.5 %collective-permute-start.3 = (f32[8,192,128]{2,1,0:T(8,128)}, f32[8,192,128]{2,1,0:T(8,128)}, u32[]{:S(2)}, u32[]{:S(2)}) collective-permute-start(f32[8,192,128]{2,1,0:T(8,128)} %get-tuple-element.65), channel_id=1, source_target_pairs={{4,0},{8,4},{12,8},{16,12},{20,16},{24,20},{28,24},{5,1},{9,5},{13... | collective-permute-start | bytes 2359304 | tf_op jit(solution)/shard_map/ppermute | solution.py:902
  81.8 5.3 %collective-permute-start.7 = (f32[176,128]{1,0:T(8,128)}, f32[176,128]{1,0:T(8,128)}, u32[]{:S(2)}, u32[]{:S(2)}) collective-permute-start(f32[176,128]{1,0:T(8,128)} %get-tuple-element.72.refs_2_), channel_id=1, source_target_pairs={{0,1},{1,0},{2,3},{3,2},{4,5},{5,4},{6,7},{7,6},{8,9},{9,8},{10,11... | collective-permute-start | bytes 270344 | tf_op jit(solution)/shard_map/ppermute | solution.py:669
  87.0 7.0 %collective-permute-start.8 = (f32[176,128]{1,0:T(8,128)}, f32[176,128]{1,0:T(8,128)}, u32[]{:S(2)}, u32[]{:S(2)}) collective-permute-start(f32[176,128]{1,0:T(8,128)} %get-tuple-element.73.refs_3_), channel_id=1, source_target_pairs={{0,2},{1,3},{2,0},{3,1},{4,6},{5,7},{6,4},{7,5},{8,10},{9,11},{10,... | collective-permute-start | bytes 270344 | tf_op jit(solution)/shard_map/ppermute | solution.py:669
  88.6 6.1 %collective-permute-start.9 = (f32[176,128]{1,0:T(8,128)}, f32[176,128]{1,0:T(8,128)}, u32[]{:S(2)}, u32[]{:S(2)}) collective-permute-start(f32[176,128]{1,0:T(8,128)} %get-tuple-element.74.refs_4_), channel_id=1, source_target_pairs={{0,3},{1,2},{2,1},{3,0},{4,7},{5,6},{6,5},{7,4},{8,11},{9,10},{10,... | collective-permute-start | bytes 270344 | tf_op jit(solution)/shard_map/ppermute | solution.py:669
  94.0 38.8 %collective-permute-start.10 = (f32[1536,128]{1,0:T(8,128)}, f32[1536,128]{1,0:T(8,128)}, u32[]{:S(2)}, u32[]{:S(2)}) collective-permute-start(f32[1536,128]{1,0:T(8,128)} %get-tuple-element.75.refs_7_.rest_0_), channel_id=1, source_target_pairs={{0,1},{1,0},{2,3},{3,2},{4,5},{5,4},{6,7},{7,6},{8,9},{9,8},{10,11... | collective-permute-start | bytes 2359304 | tf_op jit(solution)/shard_map/ppermute | solution.py:669
  94.7 38.2 %collective-permute-start.11 = (f32[1536,128]{1,0:T(8,128)}, f32[1536,128]{1,0:T(8,128)}, u32[]{:S(2)}, u32[]{:S(2)}) collective-permute-start(f32[1536,128]{1,0:T(8,128)} %get-tuple-element.76.refs_8_.rest_1_), channel_id=1, source_target_pairs={{0,2},{1,3},{2,0},{3,1},{4,6},{5,7},{6,4},{7,5},{8,10},{9,11},{10,... | collective-permute-start | bytes 2359304 | tf_op jit(solution)/shard_map/ppermute | solution.py:669
  96.5 36.3 %collective-permute-start.12 = (f32[1536,128]{1,0:T(8,128)}, f32[1536,128]{1,0:T(8,128)}, u32[]{:S(2)}, u32[]{:S(2)}) collective-permute-start(f32[1536,128]{1,0:T(8,128)} %get-tuple-element.77.refs_9_.rest_2_), channel_id=1, source_target_pairs={{0,3},{1,2},{2,1},{3,0},{4,7},{5,6},{6,5},{7,4},{8,11},{9,10},{10,... | collective-permute-start | bytes 2359304 | tf_op jit(solution)/shard_map/ppermute | solution.py:669
  100.8 39.6 %collective-permute-start.13 = (f32[1712,128]{1,0:T(8,128)}, f32[1712,128]{1,0:T(8,128)}, u32[]{:S(2)}, u32[]{:S(2)}) collective-permute-start(f32[1712,128]{1,0:T(8,128)} %shard_map.276.rest_3_.refs_3_), channel_id=1, source_target_pairs={{0,16},{4,20},{8,24},{12,28},{16,0},{20,4},{24,8},{28,12},{1,17},{... | collective-permute-start | bytes 2629640 | tf_op jit(solution)/shard_map/ppermute | solution.py:669
  140.4 6.3 %collective-permute-start.14 = (f32[4,4,128,128]{3,2,1,0:T(8,128)}, f32[4,4,128,128]{3,2,1,0:T(8,128)}, u32[]{:S(2)}, u32[]{:S(2)}) collective-permute-start(f32[4,4,128,128]{3,2,1,0:T(8,128)} %get-tuple-element.84), channel_id=1, source_target_pairs={{0,4},{4,0},{8,12},{12,8},{16,20},{20,16},{24,28},{28,24},{1,5},{5... | collective-permute-start | bytes 3145736 | tf_op jit(solution)/shard_map/ppermute | solution.py:669
  140.4 6.3 %collective-permute-start.15 = (f32[224,128]{1,0:T(8,128)}, f32[224,128]{1,0:T(8,128)}, u32[]{:S(2)}, u32[]{:S(2)}) collective-permute-start(f32[224,128]{1,0:T(8,128)} %get-tuple-element.86), channel_id=1, source_target_pairs={{0,4},{4,0},{8,12},{12,8},{16,20},{20,16},{24,28},{28,24},{1,5},{5... | collective-permute-start | bytes 344072 | tf_op jit(solution)/shard_map/ppermute | solution.py:669
  144.4 19.8 %collective-permute-start.19 = (f32[768,128]{1,0:T(8,128)}, f32[768,128]{1,0:T(8,128)}, u32[]{:S(2)}, u32[]{:S(2)}) collective-permute-start(f32[768,128]{1,0:T(8,128)} %get-tuple-element.88.refs_5_), channel_id=1, source_target_pairs={{0,16},{4,20},{8,24},{12,28},{16,0},{20,4},{24,8},{28,12},{1,17},{... | collective-permute-start | bytes 1179656 | tf_op jit(solution)/shard_map/ppermute | solution.py:669
  144.5 21.9 %collective-permute-start.20 = (f32[944,128]{1,0:T(8,128)}, f32[944,128]{1,0:T(8,128)}, u32[]{:S(2)}, u32[]{:S(2)}) collective-permute-start(f32[944,128]{1,0:T(8,128)} %get-tuple-element.87.refs_4_), channel_id=1, source_target_pairs={{0,8},{4,12},{8,0},{12,4},{16,24},{20,28},{24,16},{28,20},{1,9},{5... | collective-permute-start | bytes 1449992 | tf_op jit(solution)/shard_map/ppermute | solution.py:669
  149.7 18.6 %collective-permute-start.17 = (f32[736,128]{1,0:T(8,128)}, f32[736,128]{1,0:T(8,128)}, u32[]{:S(2)}, u32[]{:S(2)}) collective-permute-start(f32[736,128]{1,0:T(8,128)} %get-tuple-element.90), channel_id=1, source_target_pairs={{0,2},{1,3},{2,0},{3,1},{4,6},{5,7},{6,4},{7,5},{8,10},{9,11},{10,... | collective-permute-start | bytes 1130504 | tf_op jit(solution)/shard_map/ppermute | solution.py:669
  151.3 17.0 %collective-permute-start.18 = (f32[736,128]{1,0:T(8,128)}, f32[736,128]{1,0:T(8,128)}, u32[]{:S(2)}, u32[]{:S(2)}) collective-permute-start(f32[736,128]{1,0:T(8,128)} %get-tuple-element.91), channel_id=1, source_target_pairs={{0,3},{1,2},{2,1},{3,0},{4,7},{5,6},{6,5},{7,4},{8,11},{9,10},{10,... | collective-permute-start | bytes 1130504 | tf_op jit(solution)/shard_map/ppermute | solution.py:669
  151.8 17.7 %collective-permute-start.16 = (f32[736,128]{1,0:T(8,128)}, f32[736,128]{1,0:T(8,128)}, u32[]{:S(2)}, u32[]{:S(2)}) collective-permute-start(f32[736,128]{1,0:T(8,128)} %get-tuple-element.89.refs_11_), channel_id=1, source_target_pairs={{0,1},{1,0},{2,3},{3,2},{4,5},{5,4},{6,7},{7,6},{8,9},{9,8},{10,11... | collective-permute-start | bytes 1130504 | tf_op jit(solution)/shard_map/ppermute | solution.py:669
  172.9 15.8 %collective-permute-start.21 = (f32[736,128]{1,0:T(8,128)}, f32[736,128]{1,0:T(8,128)}, u32[]{:S(2)}, u32[]{:S(2)}) collective-permute-start(f32[736,128]{1,0:T(8,128)} %get-tuple-element.92.refs_5_.refs_0_), channel_id=1, source_target_pairs={{0,8},{4,12},{8,0},{12,4},{16,24},{20,28},{24,16},{28,20},{1,9},{5... | collective-permute-start | bytes 1130504 | tf_op jit(solution)/shard_map/ppermute | solution.py:669
  173.3 10.9 %collective-permute-start.22 = (f32[352,128]{1,0:T(8,128)}, f32[352,128]{1,0:T(8,128)}, u32[]{:S(2)}, u32[]{:S(2)}) collective-permute-start(f32[352,128]{1,0:T(8,128)} %get-tuple-element.93.refs_6_), channel_id=1, source_target_pairs={{0,16},{4,20},{8,24},{12,28},{16,0},{20,4},{24,8},{28,12},{1,17},{... | collective-permute-start | bytes 540680 | tf_op jit(solution)/shard_map/ppermute | solution.py:669
  178.7 7.9 %collective-permute-start.25 = (f32[368,128]{1,0:T(8,128)}, f32[368,128]{1,0:T(8,128)}, u32[]{:S(2)}, u32[]{:S(2)}) collective-permute-start(f32[368,128]{1,0:T(8,128)} %get-tuple-element.96), channel_id=1, source_target_pairs={{0,2},{1,3},{2,0},{3,1},{4,6},{5,7},{6,4},{7,5},{8,10},{9,11},{10,... | collective-permute-start | bytes 565256 | tf_op jit(solution)/shard_map/ppermute | solution.py:669
  180.3 7.3 %collective-permute-start.26 = (f32[368,128]{1,0:T(8,128)}, f32[368,128]{1,0:T(8,128)}, u32[]{:S(2)}, u32[]{:S(2)}) collective-permute-start(f32[368,128]{1,0:T(8,128)} %get-tuple-element.97), channel_id=1, source_target_pairs={{0,3},{1,2},{2,1},{3,0},{4,7},{5,6},{6,5},{7,4},{8,11},{9,10},{10,... | collective-permute-start | bytes 565256 | tf_op jit(solution)/shard_map/ppermute | solution.py:669
  180.8 8.0 %collective-permute-start.24 = (f32[368,128]{1,0:T(8,128)}, f32[368,128]{1,0:T(8,128)}, u32[]{:S(2)}, u32[]{:S(2)}) collective-permute-start(f32[368,128]{1,0:T(8,128)} %get-tuple-element.95.refs_4_), channel_id=1, source_target_pairs={{0,1},{1,0},{2,3},{3,2},{4,5},{5,4},{6,7},{7,6},{8,9},{9,8},{10,11... | collective-permute-start | bytes 565256 | tf_op jit(solution)/shard_map/ppermute | solution.py:669
  184.2 7.7 %collective-permute-start.23 = (f32[352,128]{1,0:T(8,128)}, f32[352,128]{1,0:T(8,128)}, u32[]{:S(2)}, u32[]{:S(2)}) collective-permute-start(f32[352,128]{1,0:T(8,128)} %shard_map.282), channel_id=1, source_target_pairs={{0,24},{4,28},{8,16},{12,20},{16,8},{20,12},{24,0},{28,4},{1,25},{... | collective-permute-start | bytes 540680 | tf_op jit(solution)/shard_map/ppermute | solution.py:669
  194.8 2.2 %collective-permute-start.27 = (f32[928,128]{1,0:T(8,128)}, f32[928,128]{1,0:T(8,128)}, u32[]{:S(2)}, u32[]{:S(2)}) collective-permute-start(f32[928,128]{1,0:T(8,128)} %shard_map.285.refs_8_), channel_id=1, source_target_pairs={{0,4},{4,0},{8,12},{12,8},{16,20},{20,16},{24,28},{28,24},{1,5},{5... | collective-permute-start | bytes 1425416 | tf_op jit(solution)/shard_map/ppermute | solution.py:669

commit v9 on v8

--- a/solution.py
+++ b/solution.py
@@ -849,19 +849,16 @@
         self.members, self.way = members, way
         line, near = lax.axis_size("ha") // 2, lax.axis_size("ha") // 4
         self.steps = {
-            "plane": range(1, lax.axis_size("ba")),
-            "line": range(1, line),
+            "plane": list(range(1, lax.axis_size("ba"))),
+            "line": list(range(1, line)),
+            "near last": list(range(near, line)) + list(range(1, near)),
             "far": [near],
-            "halves": range(1, near + 1),
         }[way]
         self.near = near
 
     def taking(self, step):
-        return [
-            (one, way)
-            for one, way in self.members
-            if way not in ("near", "far") or (way == "near") == (step < self.near)
-        ]
+        takes = {"plane": True, "line": True, "near": step < self.near, "far": step == self.near}
+        return [(one, way) for one, way in self.members if takes[way]]
 
     def groups(self):
         return [
@@ -873,8 +870,8 @@
         axis, unit = ("ba", 1) if self.way == "plane" else ("ha", 2)
         arrived = []
         for step, part in zip(self.steps, payloads):
-            if in_turn and step == len(self.steps) and step > 2:
-                (part,) = tied([part], arrived[1:2])
+            if in_turn and len(arrived) == 2:
+                (part,) = tied([part], arrived[1:])
             arrived.append(exchange(part, axis, unit * step))
         places = {}
         for step, sent, part in zip(self.steps, payloads, arrived):
@@ -992,15 +989,11 @@
     )
     above, below = neighbour_rows(dconv_top, dconv_bottom)
 
-    packed = Sum([packed_kept, exchange(packed_sent, "ha", 1)], ["plane"])
     plane_sum = Sum([plane_kept, exchange(plane_sent, "ha", 1)], ["plane", "far", "near"])
     line_sum = Sum([line_kept, exchange(line_sent, "ha", 1)], ["far", "near", "plane"])
-    first, _ = run(place, Stage([(packed, "plane")], "plane"))
-    packed = Rider(packed.views)
-    made, arrived = run(place, Stage([(plane_sum, "plane")], "plane"), ties=first)
-    more, far = run(
-        place, Stage([(line_sum, "far"), (packed, "far")], "far"), ties=made, late_ties=[above, below]
-    )
+    packed = Sum([packed_kept, exchange(packed_sent, "ha", 1)], ["plane"])
+    made, arrived = run(place, Stage([(plane_sum, "plane"), (packed, "plane")], "plane"))
+    more, far = run(place, Stage([(line_sum, "far")], "far"), ties=made, late_ties=[above, below])
     made, arrived = made + more, arrived + far
     dcanvas, in_kept, in_sent, small_kept, small_sent = backward(
         place, ids, above, dconv, below, joined, depth_kernel, own, gain, dmiddle, weight_in, made,
@@ -1010,8 +1003,9 @@
     in_sum = Sum([in_kept, exchange(in_sent, "ha", 1)], ["plane", "far", "near"])
     small = Rider([flat_view(small_kept), flat_view(exchange(small_sent, "ha", 1))])
     packed = Rider(packed.views)
+    packed = Rider(packed.views)
     made, arrived = run(
-        place, Stage([(plane_sum, "far"), (line_sum, "near"), (packed, "near")], "halves")
+        place, Stage([(plane_sum, "far"), (line_sum, "near"), (packed, "line")], "near last"), in_turn=True
     )
     run(place, Stage([(in_sum, "plane"), (small, "plane")], "plane"), ties=made)
     made, _ = run(

time: 202 us -> 193 us (0.955)
  starting transfers between devices: 40.2 us -> 34.7 us
    ppermute x24 -> x22, starting transfers between devices: 32.4 us -> 26.9 us  [exchange(): lax.ppermute(values, axis, [(i, i ^ bit) for i in range(lax.axis_size(axi...]
    pallas_call x10 -> x9, Pallas kernels: 32 us -> 30 us  [combine(): pl.pallas_call(kernel, in_specs=[in_smem()] + [in_hbm()] * (len(arrays) +...]
    ppermute x24 -> x22, waiting for transfers between devices: 37.5 us -> 36.5 us  [exchange(): lax.ppermute(values, axis, [(i, i ^ bit) for i in range(lax.axis_size(axi...]
  transfers between devices with their start and end apart: 28 -> 26, of which waited for: 12 -> 11; matrix products, arithmetic and copies ran while one was open for 0% -> 0% of each run, Pallas kernels for 26% -> 26%
where the time goes in v9:
time: 193 us; the launch traced here: 192 us
  Pallas kernels  113 us (59%)
  waiting for transfers between devices  40.4 us (21%)
  starting transfers between devices  34.7 us (18%)
  local copies, waits for them, and re-layouts  1.93 us (1%)
    pallas_call x1, Pallas kernels, forward(): pl.pallas_call(functools.partial(forward_kernel, rows=rows, cols=cols, co...  54 us
    ppermute x22, waiting for transfers between devices, exchange(): lax.ppermute(values, axis, [(i, i ^ bit) for i in range(lax.axis_size(axi...  36.5 us
    pallas_call x9, Pallas kernels, combine(): pl.pallas_call(kernel, in_specs=[in_smem()] + [in_hbm()] * (len(arrays) +...  30 us
    pallas_call x1, Pallas kernels, backward(): pl.pallas_call(functools.partial(backward_kernel, rows=rows, cols=cols),...  29.4 us
    ppermute x22, starting transfers between devices, exchange(): lax.ppermute(values, axis, [(i, i ^ bit) for i in range(lax.axis_size(axi...  26.9 us
    ppermute x4, starting transfers between devices, neighbour_rows(): return (lax.ppermute(bottom, 'ha', up), lax.ppermute(top, 'ha', down))  7.85 us
    ppermute x4, waiting for transfers between devices, neighbour_rows(): return (lax.ppermute(bottom, 'ha', up), lax.ppermute(top, 'ha', down))  3.91 us
  transfers between devices with their start and end apart: 26, of which 11 were waited for; matrix products, arithmetic and copies ran while one was open for 0% of the time, Pallas kernels for 26%

profile of v9, /device:TPU:0, one launch (start us, length us, event | category | flops | bytes accessed | tf_op | source)
XLA Modules:
  0.0 192.0 jit_solution(15015132308516508214)
XLA Ops:
  0.6 1.2 fusion
  1.8 2.4 %collective-permute-start = (f32[192,512]{1,0:T(8,128)S(1)}, f32[192,512]{1,0:T(8,128)S(1)}, u32[]{:S(2)}, u32[]{:S(2)}) collective-permute-start(f32[192,512]{1,0:T(8,128)S(1)} %bitcast.39), channel_id=1, source_target_pairs={{0,4},{4,8},{8,12},{12,16},{16,20},{20,24},{24,28},{1,5},{5,9},{9,... | collective-permute-start | bytes 1179656 | tf_op jit(solution)/shard_map/ppermute | solution.py:899
  4.2 1.3 collective-permute-start.1
  5.5 0.6 pad_add_fusion.place_ref
  6.1 3.9 %collective-permute-done.1.below_hbm = f32[192,512]{1,0:T(8,128)S(1)} collective-permute-done((f32[192,512]{1,0:T(8,128)S(1)}, f32[192,512]{1,0:T(8,128)S(1)}, u32[]{:S(2)}, u32[]{:S(2)}) %collective-permute-start.1) | collective-permute-done | bytes 393248 | tf_op jit(solution)/shard_map/ppermute | solution.py:899
  10.0 0.8 copy-done.1
  10.8 54.0 %shard_map.272 = (f32[8,512,128]{2,1,0:T(8,128)}, f32[512,512]{1,0:T(8,128)}, f32[512,512]{1,0:T(8,128)}, f32[8,512,128]{2,1,0:T(8,128)}, f32[8,192,128]{2,1,0:T...) custom-call(s32[2]{0:T(128)} %pad_add_fusion.place_ref, ...), custom_call_target="tpu_custom_call" | custom-call | flops 49500000256 | tf_op jit(solution)/shard_map/pallas_call | solution.py:522
  64.8 6.0 %collective-permute-start.4 = (f32[4,4,384,128]{3,2,1,0:T(8,128)}, f32[4,4,384,128]{3,2,1,0:T(8,128)}, u32[]{:S(2)}, u32[]{:S(2)}) collective-permute-start(f32[4,4,384,128]{3,2,1,0:T(8,128)} %get-tuple-element.67), channel_id=1, source_target_pairs={{0,4},{4,0},{8,12},{12,8},{16,20},{20,16},{24,28},{28,24},{1,5},{5... | collective-permute-start | bytes 9437192 | tf_op jit(solution)/shard_map/ppermute | solution.py:669
  70.8 0.1 collective-permute-start.6
  70.9 0.4 collective-permute-start.5
  71.3 2.9 %collective-permute-start.2 = (f32[8,192,128]{2,1,0:T(8,128)}, f32[8,192,128]{2,1,0:T(8,128)}, u32[]{:S(2)}, u32[]{:S(2)}) collective-permute-start(f32[8,192,128]{2,1,0:T(8,128)} %get-tuple-element.61), channel_id=1, source_target_pairs={{0,4},{4,8},{8,12},{12,16},{16,20},{20,24},{24,28},{1,5},{5,9},{9,... | collective-permute-start | bytes 2359304 | tf_op jit(solution)/shard_map/ppermute | solution.py:899
  74.2 1.3 collective-permute-start.3
  75.5 3.7 %collective-permute-done.5.refs_3_.refs_6_ = f32[704,128]{1,0:T(8,128)} collective-permute-done((f32[704,128]{1,0:T(8,128)}, f32[704,128]{1,0:T(8,128)}, u32[]{:S(2)}, u32[]{:S(2)}) %collective-permute-start.5) | collective-permute-done | bytes 360480 | tf_op jit(solution)/shard_map/ppermute | solution.py:669
  79.2 4.5 %shard_map.273 = (f32[1712,128]{1,0:T(8,128)}, f32[1712,128]{1,0:T(8,128)}, f32[1712,128]{1,0:T(8,128)}) custom-call(s32[2]{0:T(128)} %pad_add_fusion.place_ref, f32[6144,128]{1,0:T(8,128)} %bitcast.25, f32[6144,128]{1,0:T(8,128)} %bitcast.13.refs_1_, f32[704,128]{1,0:T(8,128)} %get-tuple-element.68.refs_2_.refs_5_, ...), custom_call_target="tpu_custom_call" | custom-call | flops 3992595200 | tf_op jit(solution)/shard_map/pallas_call | solution.py:777
  83.7 1.6 collective-permute-start.7
  85.3 1.5 collective-permute-start.8
  86.8 0.5 collective-permute-start.9
  87.3 3.0 %shard_map.274.refs_0_ = f32[1536,128]{1,0:T(8,128)} custom-call(s32[2]{0:T(128)} %pad_add_fusion.place_ref, f32[3072,128]{1,0:T(8,128)} %bitcast.29, f32[3072,128]{1,0:T(8,128)} %bitcast.15.refs_1_.refs_8_, f32[1712,128]{1,0:T(8,128)} %get-tuple-element.70.refs_2_.rest_0_, f32[1712,128]{1,0:T(8,128)} %get-tuple-element.71.refs_3_.rest_1_, ...), custom_call_target="tpu_custom_call" | custom-call | flops 1965075200 | tf_op jit(solution)/shard_map/pallas_call | solution.py:777
  90.3 2.7 %collective-permute-start.10 = (f32[1536,128]{1,0:T(8,128)}, f32[1536,128]{1,0:T(8,128)}, u32[]{:S(2)}, u32[]{:S(2)}) collective-permute-start(f32[1536,128]{1,0:T(8,128)} %shard_map.275.rest_3_), channel_id=1, source_target_pairs={{0,16},{4,20},{8,24},{12,28},{16,0},{20,4},{24,8},{28,12},{1,17},{... | collective-permute-start | bytes 2359304 | tf_op jit(solution)/shard_map/ppermute | solution.py:669
  93.0 29.4 %shard_map.276 = (f32[512,512]{1,0:T(8,128)}, f32[4,4,128,128]{3,2,1,0:T(8,128)}, f32[4,4,128,128]{3,2,1,0:T(8,128)}, f32[224,128]{1,0:T(8,128)}, f32[224,128]{1,0:T(8,128)}) custom-call(s32[2]{0:T(128)} %pad_add_fusion.place_ref, s32[64,64]{1,0:T(8,128)} %bitcast.44, s32[64,64]{1,0:T(8,128)} %bitcast.45, ...), custom_call_target="tpu_custom_call" | custom-call | flops 27499999232 | tf_op jit(solution)/shard_map/pallas_call | solution.py:639
  122.4 5.1 %collective-permute-done.10.refs_5_.refs_9_.refs_2_ = f32[1536,128]{1,0:T(8,128)} collective-permute-done((f32[1536,128]{1,0:T(8,128)}, f32[1536,128]{1,0:T(8,128)}, u32[]{:S(2)}, u32[]{:S(2)}) %collective-permute-start.10) | collective-permute-done | bytes 786464 | tf_op jit(solution)/shard_map/ppermute | solution.py:669
  127.5 0.1 collective-permute-start.11
  127.6 0.5 collective-permute-start.12
  128.0 3.6 %shard_map.278 = (f32[944,128]{1,0:T(8,128)}, f32[176,128]{1,0:T(8,128)}, f32[944,128]{1,0:T(8,128)}) custom-call(s32[2]{0:T(128)} %pad_add_fusion.place_ref, f32[6144,128]{1,0:T(8,128)} %bitcast.26, f32[6144,128]{1,0:T(8,128)} %bitcast.13.refs_1_, f32[1712,128]{1,0:T(8,128)} %collective-permute-done.7.refs_2_, f32[1712,128]{1,0:T(8,128)} %collective-permute-done.8.refs_3_, ...), custom_call_target="tpu_custom_call" | custom-call | flops 2806120448 | tf_op jit(solution)/shard_map/pallas_call | solution.py:777
  131.7 1.9 %collective-permute-start.17 = (f32[176,128]{1,0:T(8,128)}, f32[176,128]{1,0:T(8,128)}, u32[]{:S(2)}, u32[]{:S(2)}) collective-permute-start(f32[176,128]{1,0:T(8,128)} %get-tuple-element.83.refs_5_), channel_id=1, source_target_pairs={{0,24},{4,28},{8,16},{12,20},{16,8},{20,12},{24,0},{28,4},{1,25},{... | collective-permute-start | bytes 270344 | tf_op jit(solution)/shard_map/ppermute | solution.py:669
  133.7 3.0 %shard_map.279 = (f32[736,128]{1,0:T(8,128)}, f32[736,128]{1,0:T(8,128)}, f32[736,128]{1,0:T(8,128)}) custom-call(s32[2]{0:T(128)} %pad_add_fusion.place_ref, f32[2048,128]{1,0:T(8,128)} %bitcast.33, f32[2048,128]{1,0:T(8,128)} %bitcast.18.refs_1_.refs_7_, f32[224,128]{1,0:T(8,128)} %get-tuple-element.80.refs_2_, ...), custom_call_target="tpu_custom_call" | custom-call | flops 2175336448 | tf_op jit(solution)/shard_map/pallas_call | solution.py:777
  136.6 2.8 %collective-permute-done.17.refs_1_.refs_13_.refs_6_ = f32[176,128]{1,0:T(8,128)} collective-permute-done((f32[176,128]{1,0:T(8,128)}, f32[176,128]{1,0:T(8,128)}, u32[]{:S(2)}, u32[]{:S(2)}) %collective-permute-start.17) | collective-permute-done | bytes 90144 | tf_op jit(solution)/shard_map/ppermute | solution.py:669
  139.5 1.5 collective-permute-start.14
  141.0 1.4 collective-permute-start.15
  142.4 0.5 collective-permute-start.13
  143.0 16.4 %collective-permute-done.16.refs_5_.refs_12_ = f32[944,128]{1,0:T(8,128)} collective-permute-done((f32[944,128]{1,0:T(8,128)}, f32[944,128]{1,0:T(8,128)}, u32[]{:S(2)}, u32[]{:S(2)}) %collective-permute-start.16) | collective-permute-done | bytes 483360 | tf_op jit(solution)/shard_map/ppermute | solution.py:669
  159.3 1.9 %collective-permute-done.18.refs_14_.refs_3_.refs_10_ = f32[944,128]{1,0:T(8,128)} collective-permute-done((f32[944,128]{1,0:T(8,128)}, f32[944,128]{1,0:T(8,128)}, u32[]{:S(2)}, u32[]{:S(2)}) %collective-permute-start.18) | collective-permute-done | bytes 483360 | tf_op jit(solution)/shard_map/ppermute | solution.py:669
  161.3 3.4 %shard_map.281 = (f32[736,128]{1,0:T(8,128)}, f32[352,128]{1,0:T(8,128)}, f32[352,128]{1,0:T(8,128)}) custom-call(s32[2]{0:T(128)} %pad_add_fusion.place_ref, f32[6144,128]{1,0:T(8,128)} %bitcast.27, f32[6144,128]{1,0:T(8,128)} %bitcast.13.refs_1_, f32[1712,128]{1,0:T(8,128)} %collective-permute-done.7.refs_2_, f32[1712,128]{1,0:T(8,128)} %collective-permute-done.8.refs_3_, ...), custom_call_target="tpu_custom_call" | custom-call | flops 2331530752 | tf_op jit(solution)/shard_map/pallas_call | solution.py:777
  164.7 2.4 %collective-permute-start.20 = (f32[352,128]{1,0:T(8,128)}, f32[352,128]{1,0:T(8,128)}, u32[]{:S(2)}, u32[]{:S(2)}) collective-permute-start(f32[352,128]{1,0:T(8,128)} %get-tuple-element.89.refs_8_), channel_id=1, source_target_pairs={{0,16},{4,20},{8,24},{12,28},{16,0},{20,4},{24,8},{28,12},{1,17},{... | collective-permute-start | bytes 540680 | tf_op jit(solution)/shard_map/ppermute | solution.py:669
  167.2 3.0 %shard_map.283 = (f32[368,128]{1,0:T(8,128)}, f32[368,128]{1,0:T(8,128)}, f32[368,128]{1,0:T(8,128)}) custom-call(s32[2]{0:T(128)} %pad_add_fusion.place_ref, f32[3072,128]{1,0:T(8,128)} %bitcast.31, f32[3072,128]{1,0:T(8,128)} %bitcast.15.refs_1_.refs_8_, f32[1536,128]{1,0:T(8,128)} %collective-permute-done.10.refs_5_.refs_9_.refs_2_, ...), custom_call_target="tpu_custom_call" | custom-call | flops 1871959424 | tf_op jit(solution)/shard_map/pallas_call | solution.py:777
  170.2 1.6 collective-permute-start.23
  171.8 1.4 collective-permute-start.24
  173.2 0.6 collective-permute-start.22
  173.7 1.9 collective-permute-done.20.refs_1_.refs_2_.refs_6_
  175.6 1.9 %collective-permute-start.21 = (f32[352,128]{1,0:T(8,128)}, f32[352,128]{1,0:T(8,128)}, u32[]{:S(2)}, u32[]{:S(2)}) collective-permute-start(f32[352,128]{1,0:T(8,128)} %shard_map.282), channel_id=1, source_target_pairs={{0,24},{4,28},{8,16},{12,20},{16,8},{20,12},{24,0},{28,4},{1,25},{... | collective-permute-start | bytes 540680 | tf_op jit(solution)/shard_map/ppermute | solution.py:669
  177.5 0.2 collective-permute-done.23.refs_12_.refs_6_
  177.8 1.1 collective-permute-done.24.refs_13_.refs_7_
  178.9 1.2 collective-permute-done.22.refs_11_.refs_5_
  180.0 3.2 %shard_map.284 = (f32[128,256]{1,0:T(8,128)}, f32[64,512]{1,0:T(8,128)}, f32[64,128]{1,0:T(8,128)}) custom-call(s32[2]{0:T(128)} %pad_add_fusion.place_ref, f32[6144,128]{1,0:T(8,128)} %bitcast.28, f32[6144,128]{1,0:T(8,128)} %bitcast.13.refs_1_, f32[1712,128]{1,0:T(8,128)} %collective-permute-done.7.refs_2_, f32[1712,128]{1,0:T(8,128)} %collective-permute-done.8.refs_3_, ...), custom_call_target="tpu_custom_call" | custom-call | flops 1965075200 | tf_op jit(solution)/shard_map/pallas_call | solution.py:777
  183.3 2.7 %shard_map.285.refs_8_ = f32[928,128]{1,0:T(8,128)} custom-call(s32[2]{0:T(128)} %pad_add_fusion.place_ref, f32[736,128]{1,0:T(8,128)} %get-tuple-element.88.refs_7_.refs_0_, f32[736,128]{1,0:T(8,128)} %collective-permute-done.19.refs_6_.refs_1_.refs_5_, f32[352,128]{1,0:T(8,128)} %collective-permute-done.20.refs_1_.refs_2_.refs_6_, ...), custom_call_target="tpu_custom_call" | custom-call | flops 1574589824 | tf_op jit(solution)/shard_map/pallas_call | solution.py:777
  186.1 0.1 collective-permute-start.25
  186.1 2.2 %collective-permute-done.25.refs_9_ = f32[928,128]{1,0:T(8,128)} collective-permute-done((f32[928,128]{1,0:T(8,128)}, f32[928,128]{1,0:T(8,128)}, u32[]{:S(2)}, u32[]{:S(2)}) %collective-permute-start.25) | collective-permute-done | bytes 475168 | tf_op jit(solution)/shard_map/ppermute | solution.py:669
  188.3 3.5 %shard_map.286 = (f32[128,128]{1,0:T(8,128)}, f32[49,960]{1,0:T(8,128)}, f32[1,512]{1,0:T(1,128)}, f32[1,512]{1,0:T(1,128)}, f32[1,512]{1,0:T(1,128)}, /*index=5...) custom-call(s32[2]{0:T(128)} %pad_add_fusion.place_ref, ...), custom_call_target="tpu_custom_call" | custom-call | flops 2013134976 | tf_op jit(solution)/shard_map/pallas_call | solution.py:777
  (25 shorter events, 0.2 us)
Async XLA Ops:
  1.8 4.3 %collective-permute-start = (f32[192,512]{1,0:T(8,128)S(1)}, f32[192,512]{1,0:T(8,128)S(1)}, u32[]{:S(2)}, u32[]{:S(2)}) collective-permute-start(f32[192,512]{1,0:T(8,128)S(1)} %bitcast.39), channel_id=1, source_target_pairs={{0,4},{4,8},{8,12},{12,16},{16,20},{20,24},{24,28},{1,5},{5,9},{9,... | collective-permute-start | bytes 1179656 | tf_op jit(solution)/shard_map/ppermute | solution.py:899
  4.2 5.8 %collective-permute-start.1 = (f32[192,512]{1,0:T(8,128)S(1)}, f32[192,512]{1,0:T(8,128)S(1)}, u32[]{:S(2)}, u32[]{:S(2)}) collective-permute-start(f32[192,512]{1,0:T(8,128)S(1)} %bitcast.38), channel_id=1, source_target_pairs={{4,0},{8,4},{12,8},{16,12},{20,16},{24,20},{28,24},{5,1},{9,5},{13... | collective-permute-start | bytes 1179656 | tf_op jit(solution)/shard_map/ppermute | solution.py:899
  6.1 3.9 %copy-start = (f32[192,512]{1,0:T(8,128)}, f32[192,512]{1,0:T(8,128)S(1)}, u32[]{:S(2)}) copy-start(f32[192,512]{1,0:T(8,128)S(1)} %collective-permute-done.above_hbm) | copy-start | bytes 1179652
  10.0 0.8 copy-start.1
  64.8 14.4 %collective-permute-start.4 = (f32[4,4,384,128]{3,2,1,0:T(8,128)}, f32[4,4,384,128]{3,2,1,0:T(8,128)}, u32[]{:S(2)}, u32[]{:S(2)}) collective-permute-start(f32[4,4,384,128]{3,2,1,0:T(8,128)} %get-tuple-element.67), channel_id=1, source_target_pairs={{0,4},{4,0},{8,12},{12,8},{16,20},{20,16},{24,28},{28,24},{1,5},{5... | collective-permute-start | bytes 9437192 | tf_op jit(solution)/shard_map/ppermute | solution.py:669
  70.8 16.0 %collective-permute-start.6 = (f32[4,4,192,128]{3,2,1,0:T(8,128)}, f32[4,4,192,128]{3,2,1,0:T(8,128)}, u32[]{:S(2)}, u32[]{:S(2)}) collective-permute-start(f32[4,4,192,128]{3,2,1,0:T(8,128)} %get-tuple-element.74), channel_id=1, source_target_pairs={{0,4},{4,0},{8,12},{12,8},{16,20},{20,16},{24,28},{28,24},{1,5},{5... | collective-permute-start | bytes 4718600 | tf_op jit(solution)/shard_map/ppermute | solution.py:669
  70.9 8.3 %collective-permute-start.5 = (f32[704,128]{1,0:T(8,128)}, f32[704,128]{1,0:T(8,128)}, u32[]{:S(2)}, u32[]{:S(2)}) collective-permute-start(f32[704,128]{1,0:T(8,128)} %get-tuple-element.69), channel_id=1, source_target_pairs={{0,4},{4,0},{8,12},{12,8},{16,20},{20,16},{24,28},{28,24},{1,5},{5... | collective-permute-start | bytes 1081352 | tf_op jit(solution)/shard_map/ppermute | solution.py:669
  71.3 19.0 %collective-permute-start.2 = (f32[8,192,128]{2,1,0:T(8,128)}, f32[8,192,128]{2,1,0:T(8,128)}, u32[]{:S(2)}, u32[]{:S(2)}) collective-permute-start(f32[8,192,128]{2,1,0:T(8,128)} %get-tuple-element.61), channel_id=1, source_target_pairs={{0,4},{4,8},{8,12},{12,16},{16,20},{20,24},{24,28},{1,5},{5,9},{9,... | collective-permute-start | bytes 2359304 | tf_op jit(solution)/shard_map/ppermute | solution.py:899
  74.2 16.1 %collective-permute-start.3 = (f32[8,192,128]{2,1,0:T(8,128)}, f32[8,192,128]{2,1,0:T(8,128)}, u32[]{:S(2)}, u32[]{:S(2)}) collective-permute-start(f32[8,192,128]{2,1,0:T(8,128)} %get-tuple-element.63), channel_id=1, source_target_pairs={{4,0},{8,4},{12,8},{16,12},{20,16},{24,20},{28,24},{5,1},{9,5},{13... | collective-permute-start | bytes 2359304 | tf_op jit(solution)/shard_map/ppermute | solution.py:899
  83.7 43.7 %collective-permute-start.7 = (f32[1712,128]{1,0:T(8,128)}, f32[1712,128]{1,0:T(8,128)}, u32[]{:S(2)}, u32[]{:S(2)}) collective-permute-start(f32[1712,128]{1,0:T(8,128)} %get-tuple-element.70.refs_2_.rest_0_), channel_id=1, source_target_pairs={{0,1},{1,0},{2,3},{3,2},{4,5},{5,4},{6,7},{7,6},{8,9},{9,8},{10,11... | collective-permute-start | bytes 2629640 | tf_op jit(solution)/shard_map/ppermute | solution.py:669
  85.3 42.2 %collective-permute-start.8 = (f32[1712,128]{1,0:T(8,128)}, f32[1712,128]{1,0:T(8,128)}, u32[]{:S(2)}, u32[]{:S(2)}) collective-permute-start(f32[1712,128]{1,0:T(8,128)} %get-tuple-element.71.refs_3_.rest_1_), channel_id=1, source_target_pairs={{0,2},{1,3},{2,0},{3,1},{4,6},{5,7},{6,4},{7,5},{8,10},{9,11},{10,... | collective-permute-start | bytes 2629640 | tf_op jit(solution)/shard_map/ppermute | solution.py:669
  86.8 40.7 %collective-permute-start.9 = (f32[1712,128]{1,0:T(8,128)}, f32[1712,128]{1,0:T(8,128)}, u32[]{:S(2)}, u32[]{:S(2)}) collective-permute-start(f32[1712,128]{1,0:T(8,128)} %get-tuple-element.72.refs_4_.rest_2_), channel_id=1, source_target_pairs={{0,3},{1,2},{2,1},{3,0},{4,7},{5,6},{6,5},{7,4},{8,11},{9,10},{10,... | collective-permute-start | bytes 2629640 | tf_op jit(solution)/shard_map/ppermute | solution.py:669
  90.3 37.1 %collective-permute-start.10 = (f32[1536,128]{1,0:T(8,128)}, f32[1536,128]{1,0:T(8,128)}, u32[]{:S(2)}, u32[]{:S(2)}) collective-permute-start(f32[1536,128]{1,0:T(8,128)} %shard_map.275.rest_3_), channel_id=1, source_target_pairs={{0,16},{4,20},{8,24},{12,28},{16,0},{20,4},{24,8},{28,12},{1,17},{... | collective-permute-start | bytes 2359304 | tf_op jit(solution)/shard_map/ppermute | solution.py:669
  127.5 6.2 %collective-permute-start.11 = (f32[4,4,128,128]{3,2,1,0:T(8,128)}, f32[4,4,128,128]{3,2,1,0:T(8,128)}, u32[]{:S(2)}, u32[]{:S(2)}) collective-permute-start(f32[4,4,128,128]{3,2,1,0:T(8,128)} %get-tuple-element.79), channel_id=1, source_target_pairs={{0,4},{4,0},{8,12},{12,8},{16,20},{20,16},{24,28},{28,24},{1,5},{5... | collective-permute-start | bytes 3145736 | tf_op jit(solution)/shard_map/ppermute | solution.py:669
  127.6 6.1 %collective-permute-start.12 = (f32[224,128]{1,0:T(8,128)}, f32[224,128]{1,0:T(8,128)}, u32[]{:S(2)}, u32[]{:S(2)}) collective-permute-start(f32[224,128]{1,0:T(8,128)} %get-tuple-element.81), channel_id=1, source_target_pairs={{0,4},{4,0},{8,12},{12,8},{16,20},{20,16},{24,28},{28,24},{1,5},{5... | collective-permute-start | bytes 344072 | tf_op jit(solution)/shard_map/ppermute | solution.py:669
  131.7 7.8 %collective-permute-start.17 = (f32[176,128]{1,0:T(8,128)}, f32[176,128]{1,0:T(8,128)}, u32[]{:S(2)}, u32[]{:S(2)}) collective-permute-start(f32[176,128]{1,0:T(8,128)} %get-tuple-element.83.refs_5_), channel_id=1, source_target_pairs={{0,24},{4,28},{8,16},{12,20},{16,8},{20,12},{24,0},{28,4},{1,25},{... | collective-permute-start | bytes 270344 | tf_op jit(solution)/shard_map/ppermute | solution.py:669
  133.7 25.7 %collective-permute-start.16 = (f32[944,128]{1,0:T(8,128)}, f32[944,128]{1,0:T(8,128)}, u32[]{:S(2)}, u32[]{:S(2)}) collective-permute-start(f32[944,128]{1,0:T(8,128)} %get-tuple-element.82.refs_4_), channel_id=1, source_target_pairs={{0,16},{4,20},{8,24},{12,28},{16,0},{20,4},{24,8},{28,12},{1,17},{... | collective-permute-start | bytes 1449992 | tf_op jit(solution)/shard_map/ppermute | solution.py:669
  139.5 21.8 %collective-permute-start.18 = (f32[944,128]{1,0:T(8,128)}, f32[944,128]{1,0:T(8,128)}, u32[]{:S(2)}, u32[]{:S(2)}) collective-permute-start(f32[944,128]{1,0:T(8,128)} %shard_map.280), channel_id=1, source_target_pairs={{0,8},{4,12},{8,0},{12,4},{16,24},{20,28},{24,16},{28,20},{1,9},{5... | collective-permute-start | bytes 1449992 | tf_op jit(solution)/shard_map/ppermute | solution.py:669
  139.5 19.9 %collective-permute-start.14 = (f32[736,128]{1,0:T(8,128)}, f32[736,128]{1,0:T(8,128)}, u32[]{:S(2)}, u32[]{:S(2)}) collective-permute-start(f32[736,128]{1,0:T(8,128)} %get-tuple-element.86), channel_id=1, source_target_pairs={{0,2},{1,3},{2,0},{3,1},{4,6},{5,7},{6,4},{7,5},{8,10},{9,11},{10,... | collective-permute-start | bytes 1130504 | tf_op jit(solution)/shard_map/ppermute | solution.py:669
  141.0 18.3 %collective-permute-start.15 = (f32[736,128]{1,0:T(8,128)}, f32[736,128]{1,0:T(8,128)}, u32[]{:S(2)}, u32[]{:S(2)}) collective-permute-start(f32[736,128]{1,0:T(8,128)} %get-tuple-element.87), channel_id=1, source_target_pairs={{0,3},{1,2},{2,1},{3,0},{4,7},{5,6},{6,5},{7,4},{8,11},{9,10},{10,... | collective-permute-start | bytes 1130504 | tf_op jit(solution)/shard_map/ppermute | solution.py:669
  142.4 16.9 %collective-permute-start.13 = (f32[736,128]{1,0:T(8,128)}, f32[736,128]{1,0:T(8,128)}, u32[]{:S(2)}, u32[]{:S(2)}) collective-permute-start(f32[736,128]{1,0:T(8,128)} %get-tuple-element.85.refs_11_), channel_id=1, source_target_pairs={{0,1},{1,0},{2,3},{3,2},{4,5},{5,4},{6,7},{7,6},{8,9},{9,8},{10,11... | collective-permute-start | bytes 1130504 | tf_op jit(solution)/shard_map/ppermute | solution.py:669
  164.7 15.4 %collective-permute-start.19 = (f32[736,128]{1,0:T(8,128)}, f32[736,128]{1,0:T(8,128)}, u32[]{:S(2)}, u32[]{:S(2)}) collective-permute-start(f32[736,128]{1,0:T(8,128)} %get-tuple-element.88.refs_7_.refs_0_), channel_id=1, source_target_pairs={{0,8},{4,12},{8,0},{12,4},{16,24},{20,28},{24,16},{28,20},{1,9},{5... | collective-permute-start | bytes 1130504 | tf_op jit(solution)/shard_map/ppermute | solution.py:669
  164.7 10.9 %collective-permute-start.20 = (f32[352,128]{1,0:T(8,128)}, f32[352,128]{1,0:T(8,128)}, u32[]{:S(2)}, u32[]{:S(2)}) collective-permute-start(f32[352,128]{1,0:T(8,128)} %get-tuple-element.89.refs_8_), channel_id=1, source_target_pairs={{0,16},{4,20},{8,24},{12,28},{16,0},{20,4},{24,8},{28,12},{1,17},{... | collective-permute-start | bytes 540680 | tf_op jit(solution)/shard_map/ppermute | solution.py:669
  170.2 7.6 %collective-permute-start.23 = (f32[368,128]{1,0:T(8,128)}, f32[368,128]{1,0:T(8,128)}, u32[]{:S(2)}, u32[]{:S(2)}) collective-permute-start(f32[368,128]{1,0:T(8,128)} %get-tuple-element.92), channel_id=1, source_target_pairs={{0,2},{1,3},{2,0},{3,1},{4,6},{5,7},{6,4},{7,5},{8,10},{9,11},{10,... | collective-permute-start | bytes 565256 | tf_op jit(solution)/shard_map/ppermute | solution.py:669
  171.8 7.1 %collective-permute-start.24 = (f32[368,128]{1,0:T(8,128)}, f32[368,128]{1,0:T(8,128)}, u32[]{:S(2)}, u32[]{:S(2)}) collective-permute-start(f32[368,128]{1,0:T(8,128)} %get-tuple-element.93), channel_id=1, source_target_pairs={{0,3},{1,2},{2,1},{3,0},{4,7},{5,6},{6,5},{7,4},{8,11},{9,10},{10,... | collective-permute-start | bytes 565256 | tf_op jit(solution)/shard_map/ppermute | solution.py:669
  173.2 6.8 %collective-permute-start.22 = (f32[368,128]{1,0:T(8,128)}, f32[368,128]{1,0:T(8,128)}, u32[]{:S(2)}, u32[]{:S(2)}) collective-permute-start(f32[368,128]{1,0:T(8,128)} %get-tuple-element.91.refs_4_), channel_id=1, source_target_pairs={{0,1},{1,0},{2,3},{3,2},{4,5},{5,4},{6,7},{7,6},{8,9},{9,8},{10,11... | collective-permute-start | bytes 565256 | tf_op jit(solution)/shard_map/ppermute | solution.py:669
  175.6 7.7 %collective-permute-start.21 = (f32[352,128]{1,0:T(8,128)}, f32[352,128]{1,0:T(8,128)}, u32[]{:S(2)}, u32[]{:S(2)}) collective-permute-start(f32[352,128]{1,0:T(8,128)} %shard_map.282), channel_id=1, source_target_pairs={{0,24},{4,28},{8,16},{12,20},{16,8},{20,12},{24,0},{28,4},{1,25},{... | collective-permute-start | bytes 540680 | tf_op jit(solution)/shard_map/ppermute | solution.py:669
  186.1 2.2 %collective-permute-start.25 = (f32[928,128]{1,0:T(8,128)}, f32[928,128]{1,0:T(8,128)}, u32[]{:S(2)}, u32[]{:S(2)}) collective-permute-start(f32[928,128]{1,0:T(8,128)} %shard_map.285.refs_8_), channel_id=1, source_target_pairs={{0,4},{4,0},{8,12},{12,8},{16,20},{20,16},{24,28},{28,24},{1,5},{5... | collective-permute-start | bytes 1425416 | tf_op jit(solution)/shard_map/ppermute | solution.py:669

commit v10 on v9

--- a/solution.py
+++ b/solution.py
@@ -94,6 +94,12 @@
 
 def conv_masks(ids_scalar, ids_ref, place, row_taps, col_mask, rows):
     height, cols = ids_ref.shape
+    column_masks(ids_ref, col_mask)
+    row_masks(ids_scalar, place, row_taps, rows, height, cols)
+
+
+def column_masks(ids_ref, col_mask):
+    height, cols = ids_ref.shape
     wide_ids = jnp.broadcast_to(ids_ref[...].T[:, height // 2 : height // 2 + 1], (cols, LANES))
     column = lax.broadcasted_iota(jnp.int32, (cols, LANES), 0)
     for b in range(KERN):
@@ -103,6 +109,8 @@
         same = (moved == wide_ids) & inside
         col_mask[b] = same.astype(F32).reshape(cols // 8, 8, LANES)
 
+
+def row_masks(ids_scalar, place, row_taps, rows, height, cols):
     def one(r, _):
         own = ids_scalar[place * rows + r, cols // 2]
         row_taps[r, 0] = KERN
@@ -250,16 +258,81 @@
         self.wait(*list(self.pending))
 
 
+def head_kernel(
+    place_ref, ids_scalar, one_table, two_table, ids_hbm, own_hbm, gain_hbm, in_hbm_ref,
+    joined_hbm, valid_hbm, one_keep_hbm, two_keep_hbm, col_hbm,
+    ids_ref, rows_ref, gain_ref, in_ref, padded, valid_ref, one_keep_ref, two_keep_ref, col_ref, normed, joined, sems,
+    *, rows, cols,
+):
+    cells = rows * cols
+    reach = REACH * cols
+    steps = in_ref.shape[0]
+    copies = Copies(sems)
+    copies.start("ids", ids_hbm, ids_ref)
+    copies.start("own", own_hbm, rows_ref)
+    copies.start("own", gain_hbm, gain_ref)
+    for k in range(steps):
+        copies.start(("in", k), in_hbm_ref.at[:, pl.ds(2 * LANES * k, 2 * LANES)], in_ref.at[k])
+    copies.wait("ids")
+    turned = image_ids(ids_ref, padded, place_ref[0], rows)
+    spread_cells((turned >= 0).astype(F32), valid_ref, 0, rows + 2 * REACH)
+    spread_cells(keep_factors(turned, one_table), one_keep_ref, REACH, rows)
+    spread_cells(keep_factors(turned, two_table), two_keep_ref, REACH, rows)
+    column_masks(ids_ref, col_ref)
+    for source, target in (
+        (valid_ref, valid_hbm), (one_keep_ref, one_keep_hbm), (two_keep_ref, two_keep_hbm), (col_ref, col_hbm)
+    ):
+        copies.start("outs", source, target)
+    copies.wait("own")
+    hat, _ = normalized(rows_ref[...] * valid_ref[reach : reach + cells, :1])
+    normed[...] = hat * gain_ref[...]
+    for step in range(steps):
+        copies.wait(("in", step))
+        part = dot(normed[...], in_ref[step])
+        for k in range(2):
+            joined[2 * step + k] = part[:, k * LANES : (k + 1) * LANES]
+        pair = pl.ds(2 * step, 2)
+        copies.start("outs", joined.at[pair], joined_hbm.at[pair])
+    copies.wait_all()
+
+
+def head(place, ids, keep_one, keep_two, own, gain, weight_in, rows, cols):
+    cells, dim = own.shape
+    cells_ext = cells + 2 * REACH * cols
+    blocks = weight_in.shape[1] // LANES
+    vmem = functools.partial(pltpu.VMEM, dtype=F32)
+    shapes = [
+        (blocks, cells, LANES), (cells_ext, LANES), (cells, LANES), (cells, LANES), (KERN, cols // 8, 8, LANES)
+    ]
+    return pl.pallas_call(
+        functools.partial(head_kernel, rows=rows, cols=cols),
+        in_specs=[in_smem()] * 4 + [in_hbm()] * 4,
+        out_specs=[in_hbm()] * len(shapes),
+        out_shape=[shape_of(*shape) for shape in shapes],
+        scratch_shapes=[
+            pltpu.VMEM(ids.shape, jnp.int32),
+            vmem((cells, dim)),
+            vmem((1, dim)),
+            vmem((blocks // 2, dim, 2 * LANES)),
+            pltpu.VMEM((ids.shape[0] + 2 * EDGE, ids.shape[1]), jnp.int32),
+        ]
+        + [vmem(shape) for shape in shapes[1:]]
+        + [vmem((cells, dim)), vmem(shapes[0]), pltpu.SemaphoreType.DMA((7 + blocks,))],
+        compiler_params=params(),
+        cost_estimate=lasting(7),
+    )(place, ids, keep_one, keep_two, ids, own, gain, weight_in)
+
+
 def forward_kernel(
-    place_ref, ids_scalar, one_table, two_table, ids_hbm, above_hbm, own_hbm, below_hbm, cot_hbm,
+    place_ref, ids_scalar, joined_hbm, valid_hbm, one_keep_hbm, two_keep_hbm, col_hbm, above_hbm, own_hbm, below_hbm, cot_hbm,
     first_gain_hbm, first_scale_hbm, second_gain_hbm, second_scale_hbm,
     in_hbm_ref, kern_hbm, one_hbm, two_hbm, three_hbm, out_hbm, up_hbm, down_hbm,
-    joined_hbm, output_hbm, dmiddle_hbm, dconv_hbm, dconv_top_hbm, dconv_bottom_hbm,
+    output_hbm, dmiddle_hbm, dconv_hbm, dconv_top_hbm, dconv_bottom_hbm,
     plane_kept_ref, plane_sent_ref, line_kept_ref, line_sent_ref, packed_kept_hbm, packed_sent_hbm,
-    ids_ref, rows_ref, cot_ref, first_gain_ref, first_scale_ref, second_gain_ref, second_scale_ref,
+    rows_ref, cot_ref, first_gain_ref, first_scale_ref, second_gain_ref, second_scale_ref,
     in_ref, kern_ref, one_ref, two_ref, three_ref, out_ref, up_ref, down_ref, dconv_ref, sems, chunk_sems,
     up_kept, up_sent, down_kept, down_sent, out_kept, out_sent,
-    row_taps, padded, valid_ref, one_keep_ref, two_keep_ref, col_ref, packed_ref, normed, flat, shifted, laid, wide, conv,
+    row_taps, valid_ref, one_keep_ref, two_keep_ref, col_ref, packed_ref, normed, flat, shifted, laid, wide, conv,
     mixed_ref, mapped_ref, middle_ref, result, dnorm,
     *, rows, cols, count_ha, count_ba,
 ):
@@ -276,13 +349,17 @@
     gate_refs = (one_ref, two_ref, three_ref)
 
     copies = Copies(sems)
-    copies.start("ids", ids_hbm, ids_ref)
+    copies.start("rows", valid_hbm, valid_ref)
+    copies.start("rows", first_gain_hbm, first_gain_ref)
     copies.start("above", above_hbm, rows_ref.at[pl.ds(0, reach)])
-    copies.start("own", own_hbm, rows_ref.at[pl.ds(reach, cells)])
     copies.start("below", below_hbm, rows_ref.at[pl.ds(reach + cells, reach)])
-    copies.start("vectors", first_gain_hbm, first_gain_ref)
     for k in range(head_steps):
         copies.start(("in", k), in_hbm_ref.at[:, pl.ds(2 * LANES * k, 2 * LANES)], in_ref.at[k])
+    copies.start("conv", joined_hbm, flat.at[:, pl.ds(EDGE + reach, cells), :])
+    copies.start("conv", col_hbm, col_ref)
+    copies.start("gates", own_hbm, rows_ref.at[pl.ds(reach, cells)])
+    copies.start("gates", one_keep_hbm, one_keep_ref)
+    copies.start("gates", two_keep_hbm, two_keep_ref)
     copies.start("kern", kern_hbm, kern_ref)
     def weights(k):
         ends = pl.ds(pl.multiple_of(k * chunk, chunk), chunk)
@@ -314,28 +391,23 @@
             for k, (source, target) in enumerate(moves)
         ]
 
-    copies.wait("ids")
-    turned = image_ids(ids_ref, padded, place_ref[0], rows)
-    spread_cells((turned >= 0).astype(F32), valid_ref, 0, rows + 2 * REACH)
-    spread_cells(keep_factors(turned, one_table), one_keep_ref, REACH, rows)
-    spread_cells(keep_factors(turned, two_table), two_keep_ref, REACH, rows)
-    conv_masks(ids_scalar, ids_ref, place_ref[0], row_taps, col_ref, rows)
-    copies.wait("vectors")
-    start = 0
-    for name, size in (("above", reach), ("own", cells), ("below", reach)):
+    row_masks(ids_scalar, place_ref[0], row_taps, rows, ids_scalar.shape[0], cols)
+    copies.wait("rows")
+    for name, start, place in (("above", 0, 0), ("below", reach + cells, reach)):
         copies.wait(name)
-        hat, _ = normalized(rows_ref[start : start + size, :] * valid_ref[start : start + size, :1])
-        normed[start : start + size] = hat * first_gain_ref[...]
-        start += size
+        hat, _ = normalized(rows_ref[start : start + reach, :] * valid_ref[start : start + reach, :1])
+        normed[place : place + reach] = hat * first_gain_ref[...]
 
     for k in range(blocks):
         flat[k, :EDGE] = jnp.zeros((EDGE, LANES), F32)
         flat[k, EDGE + cells_ext :] = jnp.zeros((EDGE, LANES), F32)
     for step in range(head_steps):
         copies.wait(("in", step))
-        joined = dot(normed[...], in_ref[step])
+        joined = dot(normed[: 2 * reach], in_ref[step])
         for k in range(2):
-            flat[2 * step + k, EDGE : EDGE + cells_ext] = joined[:, k * LANES : (k + 1) * LANES]
+            part = joined[:, k * LANES : (k + 1) * LANES]
+            flat[2 * step + k, EDGE : EDGE + reach] = part[:reach]
+            flat[2 * step + k, EDGE + reach + cells : EDGE + cells_ext] = part[reach:]
         if step == 0:
             copies.start("gates", first_scale_hbm, first_scale_ref)
             copies.start("gates", second_gain_hbm, second_gain_ref)
@@ -345,9 +417,8 @@
             for k in range(ffn_steps):
                 for copy in weights(k):
                     copy.start()
-        pair = pl.ds(2 * step, 2)
-        copies.start("outs", flat.at[pair, pl.ds(EDGE + reach, cells), :], joined_hbm.at[pair])
-
+
+    copies.wait("conv")
     copies.wait("kern")
     lay_kernel(kern_ref, laid, split)
 
@@ -475,7 +546,7 @@
 
 
 def forward(
-    place, ids, keep_one, keep_two, above, own, below, cot, vectors, weight_in, kern, gates,
+    place, ids, ahead, above, own, below, cot, vectors, weight_in, kern, gates,
     weight_out, weight_up, weight_down, rows, cols, count_ha, count_ba, chunk=512,
 ):
     cells, dim = own.shape
@@ -502,11 +573,10 @@
     cells_ext = cells + 2 * reach
     vmem = functools.partial(pltpu.VMEM, dtype=F32)
     operands = (
-        place, ids, keep_one, keep_two, ids, above, own, below, cot, *vectors,
+        place, ids, *ahead, above, own, below, cot, *vectors,
         weight_in, kern, *gates, weight_out, weight_up, weight_down,
     )
     out_shape = [
-        shape_of(blocks, cells, LANES),
         shape_of(cells, dim),
         shape_of(cells, dim),
         shape_of(blocks, cells, LANES),
@@ -521,10 +591,10 @@
     ]
     return pl.pallas_call(
         functools.partial(forward_kernel, rows=rows, cols=cols, count_ha=count_ha, count_ba=count_ba),
-        in_specs=[in_smem()] * 4 + [in_hbm()] * (len(operands) - 4),
+        in_specs=[in_smem()] * 2 + [in_hbm()] * (len(operands) - 2),
         out_specs=[in_hbm()] * len(out_shape),
         out_shape=out_shape,
-        scratch_shapes=[pltpu.VMEM(ids.shape, jnp.int32), vmem((cells_ext, dim)), vmem((cells, dim))]
+        scratch_shapes=[vmem((cells_ext, dim)), vmem((cells, dim))]
         + [vmem((1, dim))] * 4
         + [vmem((head_steps, dim, 2 * LANES)), vmem(kern.shape)]
         + [vmem(gate.shape) for gate in gates]
@@ -539,13 +609,14 @@
         + [vmem((ffn_steps, chunk // (2 * up_wide), count_ba, up_rows, LANES))] * 2
         + [vmem((ffn_steps, half, chunk // down_wide, down_rows, LANES))] * 2
         + [vmem((half, count_ba, out_rows, LANES))] * 2
-        + mask_scratch(ids, rows)
         + [
+            pltpu.SMEM((rows, KERN + 2), jnp.int32),
+            vmem((cells_ext, LANES)),
             vmem((cells, LANES)),
             vmem((cells, LANES)),
             vmem((KERN, cols // 8, 8, LANES)),
             vmem(packed_shape),
-            vmem((cells_ext, dim)),
+            vmem((max(cells, 2 * reach), dim)),
             vmem((blocks, cells_ext + 2 * EDGE, LANES)),
             vmem((KERN, rows + 2 * REACH, cols // 8, 8, LANES)),
             vmem((blocks, TAPS, LANES)),
@@ -558,7 +629,7 @@
             vmem((cells, dim)),
         ],
         compiler_params=params(),
-        cost_estimate=lasting(45),
+        cost_estimate=lasting(48),
     )(*operands)
 
 
@@ -575,8 +646,8 @@
     place_ref, ids_scalar, ids_ref, above_ref, own_ref, below_ref, mix_ref, kern_ref, canvas_ref, gain_ref,
     dmiddle_ref, in_ref, *rest, rows, cols,
 ):
-    dcanvas_ref, kept_ref, sent_ref, small_kept_ref, small_sent_ref = rest[-18:-13]
-    row_taps, padded, valid_ref, col_ref, flat, shifted, laid, wide, dk, sums, djoined, normed, dnorm = rest[-13:]
+    dcanvas_ref, kept_ref, sent_ref, small_kept_ref, small_sent_ref = rest[-19:-14]
+    row_taps, padded, valid_ref, col_ref, flat, shifted, laid, wide, dk, sums, small, djoined, normed, dnorm = rest[-14:]
     step = pl.program_id(0)
     cells = rows * cols
     reach = REACH * cols
@@ -610,17 +681,25 @@
     def _():
         hat, scale = normalized(canvas_ref[...] * valid_ref[reach : reach + cells, :1])
         dgain = jnp.sum(dnorm[...] * hat, axis=0, keepdims=True)
-        count = sums.shape[0]
+        row = sums.shape[0] * TAPS
+        for k in range(sums.shape[0]):
+            small[k * TAPS : (k + 1) * TAPS, :] = sums[k, :TAPS]
+        small[row:, :] = jnp.zeros((small.shape[0] - row, LANES), F32)
         for k in range(dgain.shape[1] // LANES):
-            sums[count - 1, TAPS + k : TAPS + k + 1] = dgain[:, k * LANES : (k + 1) * LANES]
-        for ref, start in ((small_kept_ref, core * (count // 2)), (small_sent_ref, (1 - core) * (count // 2))):
-            ref[...] = sums[pl.ds(start, count // 2)].reshape(ref.shape)
+            small[row + k : row + k + 1, :] = dgain[:, k * LANES : (k + 1) * LANES]
+        half = small.shape[0] // 2
+        for ref, start in ((small_kept_ref, core * half), (small_sent_ref, (1 - core) * half)):
+            ref[...] = small[pl.ds(pl.multiple_of(start, 8), half), :]
         inner = dmiddle_ref[...] + norm_backward(dnorm[...] * gain_ref[...], hat, scale)
         dcanvas_ref[...] = inner * valid_ref[reach : reach + cells, :1]
 
 
 def block_of(size):
     return pl.BlockSpec((1, size, LANES), lambda i: (i, 0, 0))
+
+
+def small_rows(blocks, dim):
+    return -(-(blocks * TAPS + dim // LANES) // 16) * 16
 
 
 def backward(
@@ -634,8 +713,8 @@
     groups = 2 * LANES // (2 * own_wide)
     chunk_spec = pl.BlockSpec((count_ba, groups, chunk_rows, LANES), lambda i: (0, i // 2, 0, 0))
     chunks = shape_of(count_ba, count_ha // 2, chunk_rows, LANES)
-    tall = -(-(TAPS + dim // LANES) // 8) * 8
-    small = (blocks // 2 * tall, LANES)
+    tall = -(-TAPS // 8) * 8
+    small = (small_rows(blocks, dim) // 2, LANES)
     return pl.pallas_call(
         functools.partial(backward_kernel, rows=rows, cols=cols),
         grid=(blocks,),
@@ -656,6 +735,7 @@
             pltpu.VMEM((TAPS + KERN, 8, LANES), F32),
             pltpu.VMEM((TAPS, 8, LANES), F32),
             pltpu.VMEM((blocks, tall, LANES), F32),
+            pltpu.VMEM((small_rows(blocks, dim), LANES), F32),
             pltpu.VMEM((2, cells, LANES), F32),
             pltpu.VMEM((cells, dim), F32),
             pltpu.VMEM((cells, dim), F32),
@@ -918,25 +998,24 @@
     scratch = outs[-1]
     lay_beside(values[0], din_ref)
     own, other = values[1], values[2]
-    small_rows = blocks // 2 * (-(-(TAPS + gain_ref.shape[1] // LANES) // 8) * 8)
+    small = small_rows(blocks, gain_ref.shape[1]) // 2
     mine = ha % 2 == 0
     first, second = jnp.where(mine, own, other), jnp.where(mine, other, own)
-    dkern = jnp.concatenate([first[:small_rows], second[:small_rows]], axis=0)
-    tall = dkern.shape[0] // blocks
-    joined = jnp.concatenate([dkern[k * tall : k * tall + TAPS] for k in range(blocks)], axis=1)
+    dkern = jnp.concatenate([first[:small], second[:small]], axis=0)
+    joined = jnp.concatenate([dkern[k * TAPS : (k + 1) * TAPS] for k in range(blocks)], axis=1)
     dk_ref[...] = joined[:, joined.shape[1] - dk_ref.shape[1] :]
-    half = own.shape[0] - small_rows
+    half = own.shape[0] - small
     count = lax.axis_size("ba")
     part = half // count
     for core, rows in ((0, first), (1, second)):
         for step in range(count):
             start = core * half + (ba ^ step) * part
-            source = small_rows + step * part
+            source = small + step * part
             scratch[pl.ds(pl.multiple_of(start, 8), part), :] = rows[source : source + part]
     dim = gain_ref.shape[1]
     for k in range(dim // LANES):
         columns = slice(k * LANES, (k + 1) * LANES)
-        row = (blocks - 1) * tall + TAPS + k
+        row = blocks * TAPS + k
         gain_ref[:, columns] = dkern[row : row + 1]
         for vector, ref in enumerate(outs[3:6]):
             ref[:, columns] = scratch[vector * dim // LANES + k : vector * dim // LANES + k + 1, :]
@@ -980,11 +1059,13 @@
     vectors = (gain, scale_first[None], second_gain[None], scale_second[None])
     ids = image_id[0]
     above, below = neighbour_rows(own[:reach], own[cells - reach :])
+    ahead = head(place, ids, keep_first, keep_second, own, gain, weight_in, rows, cols)
+    joined = ahead[0]
     (
-        joined, output, dmiddle, dconv, dconv_top, dconv_bottom, plane_kept, plane_sent, line_kept, line_sent,
+        output, dmiddle, dconv, dconv_top, dconv_bottom, plane_kept, plane_sent, line_kept, line_sent,
         packed_kept, packed_sent,
     ) = forward(
-        place, ids, keep_first, keep_second, above, own, below, cotangent.reshape(cells, dim), vectors,
+        place, ids, ahead, above, own, below, cotangent.reshape(cells, dim), vectors,
         weight_in, depth_kernel, gates, weight_out, weight_up, weight_down, rows, cols, count_ha, count_ba,
     )
     above, below = neighbour_rows(dconv_top, dconv_bottom)

time: 193 us -> 192 us (level)
  waiting for transfers between devices: 40.4 us -> 27.7 us
  starting transfers between devices: 34.7 us -> 43.2 us
  Pallas kernels: 113 us -> 117 us
    ppermute x22, waiting for transfers between devices: 36.5 us -> 27.7 us  [exchange(): lax.ppermute(values, axis, [(i, i ^ bit) for i in range(lax.axis_size(axi...]
    ppermute x22, starting transfers between devices: 26.9 us -> 34.7 us  [exchange(): lax.ppermute(values, axis, [(i, i ^ bit) for i in range(lax.axis_size(axi...]
    pallas_call x0 -> x1, Pallas kernels: none -> 7.68 us  [head(): pl.pallas_call(functools.partial(head_kernel, rows=rows, cols=cols), in_s...]
    pallas_call x1, Pallas kernels: 54 us -> 49.8 us  [forward(): pl.pallas_call(functools.partial(forward_kernel, rows=rows, cols=cols, co...]
    ppermute x4, waiting for transfers between devices: 3.91 us -> 0.01 us  [neighbour_rows(): return (lax.ppermute(bottom, 'ha', up), lax.ppermute(top, 'ha', down))]
  transfers between devices with their start and end apart: 26 -> 26, of which waited for: 11 -> 12; matrix products, arithmetic and copies ran while one was open for 0% -> 0% of each run, Pallas kernels for 26% -> 30%
where the time goes in v10:
time: 192 us; the launch traced here: 191 us
  Pallas kernels  117 us (61%)
  starting transfers between devices  43.2 us (22%)
  waiting for transfers between devices  27.7 us (14%)
  local copies, waits for them, and re-layouts  2.08 us (1%)
    pallas_call x1, Pallas kernels, forward(): pl.pallas_call(functools.partial(forward_kernel, rows=rows, cols=cols, co...  49.8 us
    ppermute x22, starting transfers between devices, exchange(): lax.ppermute(values, axis, [(i, i ^ bit) for i in range(lax.axis_size(axi...  34.7 us
    pallas_call x9, Pallas kernels, combine(): pl.pallas_call(kernel, in_specs=[in_smem()] + [in_hbm()] * (len(arrays) +...  29.9 us
    pallas_call x1, Pallas kernels, backward(): pl.pallas_call(functools.partial(backward_kernel, rows=rows, cols=cols),...  29.3 us
    ppermute x22, waiting for transfers between devices, exchange(): lax.ppermute(values, axis, [(i, i ^ bit) for i in range(lax.axis_size(axi...  27.7 us
    ppermute x4, starting transfers between devices, neighbour_rows(): return (lax.ppermute(bottom, 'ha', up), lax.ppermute(top, 'ha', down))  8.58 us
    pallas_call x1, Pallas kernels, head(): pl.pallas_call(functools.partial(head_kernel, rows=rows, cols=cols), in_s...  7.68 us
  transfers between devices with their start and end apart: 26, of which 12 were waited for; matrix products, arithmetic and copies ran while one was open for 0% of the time, Pallas kernels for 30%

profile of v10, /device:TPU:0, one launch (start us, length us, event | category | flops | bytes accessed | tf_op | source)
XLA Modules:
  0.0 191.5 jit_solution(15876998229913122293)
XLA Ops:
  0.6 2.1 %fusion = (f32[1,3,64,512]{3,2,1,0:T(8,128)}, f32[1,3,64,512]{3,2,1,0:T(8,128)}) fusion(f32[1,8,64,512]{3,2,1,0:T(8,128)} %param.17), kind=kLoop, calls=%fused_computation.1 | loop fusion | bytes 1572864 | tf_op jit(solution)/shard_map/slice | solution.py:1061
  2.7 3.1 %collective-permute-start = (f32[192,512]{1,0:T(8,128)}, f32[192,512]{1,0:T(8,128)}, u32[]{:S(2)}, u32[]{:S(2)}) collective-permute-start(f32[192,512]{1,0:T(8,128)} %bitcast.5), channel_id=1, source_target_pairs={{0,4},{4,8},{8,12},{12,16},{16,20},{20,24},{24,28},{1,5},{5,9},{9,... | collective-permute-start | bytes 1179656 | tf_op jit(solution)/shard_map/ppermute | solution.py:979
  5.8 1.3 collective-permute-start.1
  7.1 0.7 pad_add_fusion.place_ref
  7.8 7.7 %shard_map.272 = (f32[8,512,128]{2,1,0:T(8,128)}, f32[896,128]{1,0:T(8,128)}, f32[512,128]{1,0:T(8,128)}, f32[512,128]{1,0:T(8,128)}, f32[7,8,8,128]{3,2,1,0:T(8,128)}) custom-call(s32[2]{0:T(128)} %pad_add_fusion.place_ref, s32[64,64]{1,0:T(8,128)} %bitcast.41, s32[1,36]{1,0:T(1,128)} %one_table.1, s32[1,36]{1,0:T(1,128)} %two_table.1, s32[64,64]{1,0:T(8,128)} %bitcast.42, ...), custom_call_target="tpu_custom_call" | custom-call | flops 7699999744 | tf_op jit(solution)/shard_map/pallas_call | solution.py:307
  15.5 49.8 %shard_map.273 = (f32[512,512]{1,0:T(8,128)}, f32[512,512]{1,0:T(8,128)}, f32[8,512,128]{2,1,0:T(8,128)}, f32[8,192,128]{2,1,0:T(8,128)}, f32[8,192,128]{2,1,0:T...) custom-call(s32[2]{0:T(128)} %pad_add_fusion.place_ref, ...), custom_call_target="tpu_custom_call" | custom-call | flops 52800000000 | tf_op jit(solution)/shard_map/pallas_call | solution.py:592
  65.3 2.6 %collective-permute-start.4 = (f32[4,4,384,128]{3,2,1,0:T(8,128)}, f32[4,4,384,128]{3,2,1,0:T(8,128)}, u32[]{:S(2)}, u32[]{:S(2)}) collective-permute-start(f32[4,4,384,128]{3,2,1,0:T(8,128)} %get-tuple-element.75), channel_id=1, source_target_pairs={{0,4},{4,0},{8,12},{12,8},{16,20},{20,16},{24,28},{28,24},{1,5},{5... | collective-permute-start | bytes 9437192 | tf_op jit(solution)/shard_map/ppermute | solution.py:749
  67.9 0.1 collective-permute-start.6
  68.0 0.4 collective-permute-start.5
  68.4 2.9 %collective-permute-start.2 = (f32[8,192,128]{2,1,0:T(8,128)}, f32[8,192,128]{2,1,0:T(8,128)}, u32[]{:S(2)}, u32[]{:S(2)}) collective-permute-start(f32[8,192,128]{2,1,0:T(8,128)} %get-tuple-element.70), channel_id=1, source_target_pairs={{0,4},{4,8},{8,12},{12,16},{16,20},{20,24},{24,28},{1,5},{5,9},{9,... | collective-permute-start | bytes 2359304 | tf_op jit(solution)/shard_map/ppermute | solution.py:979
  71.3 1.3 collective-permute-start.3
  72.6 3.7 %collective-permute-done.5.refs_3_.refs_6_ = f32[704,128]{1,0:T(8,128)} collective-permute-done((f32[704,128]{1,0:T(8,128)}, f32[704,128]{1,0:T(8,128)}, u32[]{:S(2)}, u32[]{:S(2)}) %collective-permute-start.5) | collective-permute-done | bytes 360480 | tf_op jit(solution)/shard_map/ppermute | solution.py:749
  76.3 4.5 %shard_map.274 = (f32[1712,128]{1,0:T(8,128)}, f32[1712,128]{1,0:T(8,128)}, f32[1712,128]{1,0:T(8,128)}) custom-call(s32[2]{0:T(128)} %pad_add_fusion.place_ref, f32[6144,128]{1,0:T(8,128)} %bitcast.25, f32[6144,128]{1,0:T(8,128)} %bitcast.13.refs_1_, f32[704,128]{1,0:T(8,128)} %get-tuple-element.76.refs_2_.refs_5_, ...), custom_call_target="tpu_custom_call" | custom-call | flops 3992595200 | tf_op jit(solution)/shard_map/pallas_call | solution.py:857
  80.8 1.6 collective-permute-start.7
  82.3 1.5 collective-permute-start.8
  83.9 0.5 collective-permute-start.9
  84.4 3.0 %shard_map.275.refs_0_ = f32[1536,128]{1,0:T(8,128)} custom-call(s32[2]{0:T(128)} %pad_add_fusion.place_ref, f32[3072,128]{1,0:T(8,128)} %bitcast.29, f32[3072,128]{1,0:T(8,128)} %bitcast.15.refs_1_.refs_8_, f32[1712,128]{1,0:T(8,128)} %get-tuple-element.78.refs_2_.rest_0_, f32[1712,128]{1,0:T(8,128)} %get-tuple-element.79.refs_3_.rest_1_, ...), custom_call_target="tpu_custom_call" | custom-call | flops 1965075200 | tf_op jit(solution)/shard_map/pallas_call | solution.py:857
  87.4 3.1 %collective-permute-start.10 = (f32[1536,128]{1,0:T(8,128)}, f32[1536,128]{1,0:T(8,128)}, u32[]{:S(2)}, u32[]{:S(2)}) collective-permute-start(f32[1536,128]{1,0:T(8,128)} %shard_map.276.rest_3_), channel_id=1, source_target_pairs={{0,16},{4,20},{8,24},{12,28},{16,0},{20,4},{24,8},{28,12},{1,17},{... | collective-permute-start | bytes 2359304 | tf_op jit(solution)/shard_map/ppermute | solution.py:749
  90.5 29.3 %shard_map.277 = (f32[512,512]{1,0:T(8,128)}, f32[4,4,128,128]{3,2,1,0:T(8,128)}, f32[4,4,128,128]{3,2,1,0:T(8,128)}, f32[200,128]{1,0:T(8,128)}, f32[200,128]{1,0:T(8,128)}) custom-call(s32[2]{0:T(128)} %pad_add_fusion.place_ref, s32[64,64]{1,0:T(8,128)} %bitcast.44, s32[64,64]{1,0:T(8,128)} %bitcast.45, ...), custom_call_target="tpu_custom_call" | custom-call | flops 27499999232 | tf_op jit(solution)/shard_map/pallas_call | solution.py:718
  119.8 4.8 %collective-permute-done.10.refs_5_.refs_9_.refs_2_ = f32[1536,128]{1,0:T(8,128)} collective-permute-done((f32[1536,128]{1,0:T(8,128)}, f32[1536,128]{1,0:T(8,128)}, u32[]{:S(2)}, u32[]{:S(2)}) %collective-permute-start.10) | collective-permute-done | bytes 786464 | tf_op jit(solution)/shard_map/ppermute | solution.py:749
  124.8 0.5 collective-permute-start.12
  125.3 3.6 %shard_map.279 = (f32[944,128]{1,0:T(8,128)}, f32[176,128]{1,0:T(8,128)}, f32[944,128]{1,0:T(8,128)}) custom-call(s32[2]{0:T(128)} %pad_add_fusion.place_ref, f32[6144,128]{1,0:T(8,128)} %bitcast.26, f32[6144,128]{1,0:T(8,128)} %bitcast.13.refs_1_, f32[1712,128]{1,0:T(8,128)} %collective-permute-done.7.refs_2_, f32[1712,128]{1,0:T(8,128)} %collective-permute-done.8.refs_3_, ...), custom_call_target="tpu_custom_call" | custom-call | flops 2806120448 | tf_op jit(solution)/shard_map/pallas_call | solution.py:857
  128.9 3.6 %collective-permute-start.17 = (f32[176,128]{1,0:T(8,128)}, f32[176,128]{1,0:T(8,128)}, u32[]{:S(2)}, u32[]{:S(2)}) collective-permute-start(f32[176,128]{1,0:T(8,128)} %get-tuple-element.91.refs_5_), channel_id=1, source_target_pairs={{0,24},{4,28},{8,16},{12,20},{16,8},{20,12},{24,0},{28,4},{1,25},{... | collective-permute-start | bytes 270344 | tf_op jit(solution)/shard_map/ppermute | solution.py:749
  132.5 3.0 %shard_map.280 = (f32[712,128]{1,0:T(8,128)}, f32[712,128]{1,0:T(8,128)}, f32[712,128]{1,0:T(8,128)}) custom-call(s32[2]{0:T(128)} %pad_add_fusion.place_ref, f32[2048,128]{1,0:T(8,128)} %bitcast.33, f32[2048,128]{1,0:T(8,128)} %bitcast.18.refs_1_.refs_7_, f32[200,128]{1,0:T(8,128)} %get-tuple-element.88.refs_2_, ...), custom_call_target="tpu_custom_call" | custom-call | flops 2152808448 | tf_op jit(solution)/shard_map/pallas_call | solution.py:857
  135.5 1.2 collective-permute-done.17.refs_1_.refs_13_.refs_6_
  136.7 9.8 %collective-permute-start.18 = (f32[944,128]{1,0:T(8,128)}, f32[944,128]{1,0:T(8,128)}, u32[]{:S(2)}, u32[]{:S(2)}) collective-permute-start(f32[944,128]{1,0:T(8,128)} %shard_map.281), channel_id=1, source_target_pairs={{0,8},{4,12},{8,0},{12,4},{16,24},{20,28},{24,16},{28,20},{1,9},{5... | collective-permute-start | bytes 1449992 | tf_op jit(solution)/shard_map/ppermute | solution.py:749
  146.5 1.5 collective-permute-start.14
  148.0 1.4 collective-permute-start.15
  149.5 0.5 collective-permute-start.13
  150.0 6.8 %collective-permute-done.16.refs_5_.refs_12_ = f32[944,128]{1,0:T(8,128)} collective-permute-done((f32[944,128]{1,0:T(8,128)}, f32[944,128]{1,0:T(8,128)}, u32[]{:S(2)}, u32[]{:S(2)}) %collective-permute-start.16) | collective-permute-done | bytes 483360 | tf_op jit(solution)/shard_map/ppermute | solution.py:749
  156.8 1.4 collective-permute-done.14.refs_9_.refs_3_
  158.2 1.5 collective-permute-done.13.refs_8_.refs_2_
  159.7 2.2 %collective-permute-done.18.refs_14_.refs_3_.refs_10_ = f32[944,128]{1,0:T(8,128)} collective-permute-done((f32[944,128]{1,0:T(8,128)}, f32[944,128]{1,0:T(8,128)}, u32[]{:S(2)}, u32[]{:S(2)}) %collective-permute-start.18) | collective-permute-done | bytes 483360 | tf_op jit(solution)/shard_map/ppermute | solution.py:749
  161.9 3.4 %shard_map.282 = (f32[712,128]{1,0:T(8,128)}, f32[328,128]{1,0:T(8,128)}, f32[328,128]{1,0:T(8,128)}) custom-call(s32[2]{0:T(128)} %pad_add_fusion.place_ref, f32[6144,128]{1,0:T(8,128)} %bitcast.27, f32[6144,128]{1,0:T(8,128)} %bitcast.13.refs_1_, f32[1712,128]{1,0:T(8,128)} %collective-permute-done.7.refs_2_, f32[1712,128]{1,0:T(8,128)} %collective-permute-done.8.refs_3_, ...), custom_call_target="tpu_custom_call" | custom-call | flops 2299991552 | tf_op jit(solution)/shard_map/pallas_call | solution.py:857
  165.4 1.7 collective-permute-start.20
  167.1 3.0 %shard_map.284 = (f32[368,128]{1,0:T(8,128)}, f32[368,128]{1,0:T(8,128)}, f32[368,128]{1,0:T(8,128)}) custom-call(s32[2]{0:T(128)} %pad_add_fusion.place_ref, f32[3072,128]{1,0:T(8,128)} %bitcast.31, f32[3072,128]{1,0:T(8,128)} %bitcast.15.refs_1_.refs_8_, f32[1536,128]{1,0:T(8,128)} %collective-permute-done.10.refs_5_.refs_9_.refs_2_, ...), custom_call_target="tpu_custom_call" | custom-call | flops 1871959424 | tf_op jit(solution)/shard_map/pallas_call | solution.py:857
  170.1 1.6 collective-permute-start.23
  171.6 1.4 collective-permute-start.24
  173.1 0.5 collective-permute-start.22
  173.6 0.7 collective-permute-done.20.refs_1_.refs_2_.refs_6_
  174.3 2.0 %collective-permute-start.21 = (f32[328,128]{1,0:T(8,128)}, f32[328,128]{1,0:T(8,128)}, u32[]{:S(2)}, u32[]{:S(2)}) collective-permute-start(f32[328,128]{1,0:T(8,128)} %shard_map.283), channel_id=1, source_target_pairs={{0,24},{4,28},{8,16},{12,20},{16,8},{20,12},{24,0},{28,4},{1,25},{... | collective-permute-start | bytes 503816 | tf_op jit(solution)/shard_map/ppermute | solution.py:749
  176.3 0.8 collective-permute-done.23.refs_12_.refs_6_
  177.1 1.3 collective-permute-done.24.refs_13_.refs_7_
  178.4 1.1 collective-permute-done.22.refs_11_.refs_5_
  179.6 3.2 %shard_map.285 = (f32[128,256]{1,0:T(8,128)}, f32[64,512]{1,0:T(8,128)}, f32[64,128]{1,0:T(8,128)}) custom-call(s32[2]{0:T(128)} %pad_add_fusion.place_ref, f32[6144,128]{1,0:T(8,128)} %bitcast.28, f32[6144,128]{1,0:T(8,128)} %bitcast.13.refs_1_, f32[1712,128]{1,0:T(8,128)} %collective-permute-done.7.refs_2_, f32[1712,128]{1,0:T(8,128)} %collective-permute-done.8.refs_3_, ...), custom_call_target="tpu_custom_call" | custom-call | flops 1965075200 | tf_op jit(solution)/shard_map/pallas_call | solution.py:857
  182.8 2.7 %shard_map.286.refs_8_ = f32[904,128]{1,0:T(8,128)} custom-call(s32[2]{0:T(128)} %pad_add_fusion.place_ref, f32[712,128]{1,0:T(8,128)} %get-tuple-element.96.refs_7_.refs_0_, f32[712,128]{1,0:T(8,128)} %collective-permute-done.19.refs_6_.refs_1_.refs_5_, f32[328,128]{1,0:T(8,128)} %collective-permute-done.20.refs_1_.refs_2_.refs_6_, ...), custom_call_target="tpu_custom_call" | custom-call | flops 1552061824 | tf_op jit(solution)/shard_map/pallas_call | solution.py:857
  185.6 2.1 %collective-permute-done.25.refs_9_ = f32[904,128]{1,0:T(8,128)} collective-permute-done((f32[904,128]{1,0:T(8,128)}, f32[904,128]{1,0:T(8,128)}, u32[]{:S(2)}, u32[]{:S(2)}) %collective-permute-start.25) | collective-permute-done | bytes 462880 | tf_op jit(solution)/shard_map/ppermute | solution.py:749
  187.8 3.5 %shard_map.287 = (f32[128,128]{1,0:T(8,128)}, f32[49,960]{1,0:T(8,128)}, f32[1,512]{1,0:T(1,128)}, f32[1,512]{1,0:T(1,128)}, f32[1,512]{1,0:T(1,128)}, /*index=5...) custom-call(s32[2]{0:T(128)} %pad_add_fusion.place_ref, ...), custom_call_target="tpu_custom_call" | custom-call | flops 1995112576 | tf_op jit(solution)/shard_map/pallas_call | solution.py:857
  (22 shorter events, 0.3 us)
Async XLA Ops:
  2.7 12.8 %collective-permute-start = (f32[192,512]{1,0:T(8,128)}, f32[192,512]{1,0:T(8,128)}, u32[]{:S(2)}, u32[]{:S(2)}) collective-permute-start(f32[192,512]{1,0:T(8,128)} %bitcast.5), channel_id=1, source_target_pairs={{0,4},{4,8},{8,12},{12,16},{16,20},{20,24},{24,28},{1,5},{5,9},{9,... | collective-permute-start | bytes 1179656 | tf_op jit(solution)/shard_map/ppermute | solution.py:979
  5.8 9.6 %collective-permute-start.1 = (f32[192,512]{1,0:T(8,128)}, f32[192,512]{1,0:T(8,128)}, u32[]{:S(2)}, u32[]{:S(2)}) collective-permute-start(f32[192,512]{1,0:T(8,128)} %bitcast.6), channel_id=1, source_target_pairs={{4,0},{8,4},{12,8},{16,12},{20,16},{24,20},{28,24},{5,1},{9,5},{13... | collective-permute-start | bytes 1179656 | tf_op jit(solution)/shard_map/ppermute | solution.py:979
  65.3 11.0 %collective-permute-start.4 = (f32[4,4,384,128]{3,2,1,0:T(8,128)}, f32[4,4,384,128]{3,2,1,0:T(8,128)}, u32[]{:S(2)}, u32[]{:S(2)}) collective-permute-start(f32[4,4,384,128]{3,2,1,0:T(8,128)} %get-tuple-element.75), channel_id=1, source_target_pairs={{0,4},{4,0},{8,12},{12,8},{16,20},{20,16},{24,28},{28,24},{1,5},{5... | collective-permute-start | bytes 9437192 | tf_op jit(solution)/shard_map/ppermute | solution.py:749
  67.9 15.9 %collective-permute-start.6 = (f32[4,4,192,128]{3,2,1,0:T(8,128)}, f32[4,4,192,128]{3,2,1,0:T(8,128)}, u32[]{:S(2)}, u32[]{:S(2)}) collective-permute-start(f32[4,4,192,128]{3,2,1,0:T(8,128)} %get-tuple-element.82), channel_id=1, source_target_pairs={{0,4},{4,0},{8,12},{12,8},{16,20},{20,16},{24,28},{28,24},{1,5},{5... | collective-permute-start | bytes 4718600 | tf_op jit(solution)/shard_map/ppermute | solution.py:749
  68.0 8.3 %collective-permute-start.5 = (f32[704,128]{1,0:T(8,128)}, f32[704,128]{1,0:T(8,128)}, u32[]{:S(2)}, u32[]{:S(2)}) collective-permute-start(f32[704,128]{1,0:T(8,128)} %get-tuple-element.77), channel_id=1, source_target_pairs={{0,4},{4,0},{8,12},{12,8},{16,20},{20,16},{24,28},{28,24},{1,5},{5... | collective-permute-start | bytes 1081352 | tf_op jit(solution)/shard_map/ppermute | solution.py:749
  68.4 19.0 %collective-permute-start.2 = (f32[8,192,128]{2,1,0:T(8,128)}, f32[8,192,128]{2,1,0:T(8,128)}, u32[]{:S(2)}, u32[]{:S(2)}) collective-permute-start(f32[8,192,128]{2,1,0:T(8,128)} %get-tuple-element.70), channel_id=1, source_target_pairs={{0,4},{4,8},{8,12},{12,16},{16,20},{20,24},{24,28},{1,5},{5,9},{9,... | collective-permute-start | bytes 2359304 | tf_op jit(solution)/shard_map/ppermute | solution.py:979
  71.3 16.1 %collective-permute-start.3 = (f32[8,192,128]{2,1,0:T(8,128)}, f32[8,192,128]{2,1,0:T(8,128)}, u32[]{:S(2)}, u32[]{:S(2)}) collective-permute-start(f32[8,192,128]{2,1,0:T(8,128)} %get-tuple-element.72), channel_id=1, source_target_pairs={{4,0},{8,4},{12,8},{16,12},{20,16},{24,20},{28,24},{5,1},{9,5},{13... | collective-permute-start | bytes 2359304 | tf_op jit(solution)/shard_map/ppermute | solution.py:979
  80.8 43.9 %collective-permute-start.7 = (f32[1712,128]{1,0:T(8,128)}, f32[1712,128]{1,0:T(8,128)}, u32[]{:S(2)}, u32[]{:S(2)}) collective-permute-start(f32[1712,128]{1,0:T(8,128)} %get-tuple-element.78.refs_2_.rest_0_), channel_id=1, source_target_pairs={{0,1},{1,0},{2,3},{3,2},{4,5},{5,4},{6,7},{7,6},{8,9},{9,8},{10,11... | collective-permute-start | bytes 2629640 | tf_op jit(solution)/shard_map/ppermute | solution.py:749
  82.3 42.3 %collective-permute-start.8 = (f32[1712,128]{1,0:T(8,128)}, f32[1712,128]{1,0:T(8,128)}, u32[]{:S(2)}, u32[]{:S(2)}) collective-permute-start(f32[1712,128]{1,0:T(8,128)} %get-tuple-element.79.refs_3_.rest_1_), channel_id=1, source_target_pairs={{0,2},{1,3},{2,0},{3,1},{4,6},{5,7},{6,4},{7,5},{8,10},{9,11},{10,... | collective-permute-start | bytes 2629640 | tf_op jit(solution)/shard_map/ppermute | solution.py:749
  83.9 40.8 %collective-permute-start.9 = (f32[1712,128]{1,0:T(8,128)}, f32[1712,128]{1,0:T(8,128)}, u32[]{:S(2)}, u32[]{:S(2)}) collective-permute-start(f32[1712,128]{1,0:T(8,128)} %get-tuple-element.80.refs_4_.rest_2_), channel_id=1, source_target_pairs={{0,3},{1,2},{2,1},{3,0},{4,7},{5,6},{6,5},{7,4},{8,11},{9,10},{10,... | collective-permute-start | bytes 2629640 | tf_op jit(solution)/shard_map/ppermute | solution.py:749
  87.4 37.2 %collective-permute-start.10 = (f32[1536,128]{1,0:T(8,128)}, f32[1536,128]{1,0:T(8,128)}, u32[]{:S(2)}, u32[]{:S(2)}) collective-permute-start(f32[1536,128]{1,0:T(8,128)} %shard_map.276.rest_3_), channel_id=1, source_target_pairs={{0,16},{4,20},{8,24},{12,28},{16,0},{20,4},{24,8},{28,12},{1,17},{... | collective-permute-start | bytes 2359304 | tf_op jit(solution)/shard_map/ppermute | solution.py:749
  124.7 7.8 %collective-permute-start.11 = (f32[4,4,128,128]{3,2,1,0:T(8,128)}, f32[4,4,128,128]{3,2,1,0:T(8,128)}, u32[]{:S(2)}, u32[]{:S(2)}) collective-permute-start(f32[4,4,128,128]{3,2,1,0:T(8,128)} %get-tuple-element.87), channel_id=1, source_target_pairs={{0,4},{4,0},{8,12},{12,8},{16,20},{20,16},{24,28},{28,24},{1,5},{5... | collective-permute-start | bytes 3145736 | tf_op jit(solution)/shard_map/ppermute | solution.py:749
  124.8 7.8 %collective-permute-start.12 = (f32[200,128]{1,0:T(8,128)}, f32[200,128]{1,0:T(8,128)}, u32[]{:S(2)}, u32[]{:S(2)}) collective-permute-start(f32[200,128]{1,0:T(8,128)} %get-tuple-element.89), channel_id=1, source_target_pairs={{0,4},{4,0},{8,12},{12,8},{16,20},{20,16},{24,28},{28,24},{1,5},{5... | collective-permute-start | bytes 307208 | tf_op jit(solution)/shard_map/ppermute | solution.py:749
  128.9 7.8 %collective-permute-start.17 = (f32[176,128]{1,0:T(8,128)}, f32[176,128]{1,0:T(8,128)}, u32[]{:S(2)}, u32[]{:S(2)}) collective-permute-start(f32[176,128]{1,0:T(8,128)} %get-tuple-element.91.refs_5_), channel_id=1, source_target_pairs={{0,24},{4,28},{8,16},{12,20},{16,8},{20,12},{24,0},{28,4},{1,25},{... | collective-permute-start | bytes 270344 | tf_op jit(solution)/shard_map/ppermute | solution.py:749
  132.5 24.3 %collective-permute-start.16 = (f32[944,128]{1,0:T(8,128)}, f32[944,128]{1,0:T(8,128)}, u32[]{:S(2)}, u32[]{:S(2)}) collective-permute-start(f32[944,128]{1,0:T(8,128)} %get-tuple-element.90.refs_4_), channel_id=1, source_target_pairs={{0,16},{4,20},{8,24},{12,28},{16,0},{20,4},{24,8},{28,12},{1,17},{... | collective-permute-start | bytes 1449992 | tf_op jit(solution)/shard_map/ppermute | solution.py:749
  136.7 25.2 %collective-permute-start.18 = (f32[944,128]{1,0:T(8,128)}, f32[944,128]{1,0:T(8,128)}, u32[]{:S(2)}, u32[]{:S(2)}) collective-permute-start(f32[944,128]{1,0:T(8,128)} %shard_map.281), channel_id=1, source_target_pairs={{0,8},{4,12},{8,0},{12,4},{16,24},{20,28},{24,16},{28,20},{1,9},{5... | collective-permute-start | bytes 1449992 | tf_op jit(solution)/shard_map/ppermute | solution.py:749
  146.5 11.7 %collective-permute-start.14 = (f32[712,128]{1,0:T(8,128)}, f32[712,128]{1,0:T(8,128)}, u32[]{:S(2)}, u32[]{:S(2)}) collective-permute-start(f32[712,128]{1,0:T(8,128)} %get-tuple-element.94), channel_id=1, source_target_pairs={{0,2},{1,3},{2,0},{3,1},{4,6},{5,7},{6,4},{7,5},{8,10},{9,11},{10,... | collective-permute-start | bytes 1093640 | tf_op jit(solution)/shard_map/ppermute | solution.py:749
  148.0 10.2 %collective-permute-start.15 = (f32[712,128]{1,0:T(8,128)}, f32[712,128]{1,0:T(8,128)}, u32[]{:S(2)}, u32[]{:S(2)}) collective-permute-start(f32[712,128]{1,0:T(8,128)} %get-tuple-element.95), channel_id=1, source_target_pairs={{0,3},{1,2},{2,1},{3,0},{4,7},{5,6},{6,5},{7,4},{8,11},{9,10},{10,... | collective-permute-start | bytes 1093640 | tf_op jit(solution)/shard_map/ppermute | solution.py:749
  149.5 10.3 %collective-permute-start.13 = (f32[712,128]{1,0:T(8,128)}, f32[712,128]{1,0:T(8,128)}, u32[]{:S(2)}, u32[]{:S(2)}) collective-permute-start(f32[712,128]{1,0:T(8,128)} %get-tuple-element.93.refs_11_), channel_id=1, source_target_pairs={{0,1},{1,0},{2,3},{3,2},{4,5},{5,4},{6,7},{7,6},{8,9},{9,8},{10,11... | collective-permute-start | bytes 1093640 | tf_op jit(solution)/shard_map/ppermute | solution.py:749
  165.3 14.3 %collective-permute-start.19 = (f32[712,128]{1,0:T(8,128)}, f32[712,128]{1,0:T(8,128)}, u32[]{:S(2)}, u32[]{:S(2)}) collective-permute-start(f32[712,128]{1,0:T(8,128)} %get-tuple-element.96.refs_7_.refs_0_), channel_id=1, source_target_pairs={{0,8},{4,12},{8,0},{12,4},{16,24},{20,28},{24,16},{28,20},{1,9},{5... | collective-permute-start | bytes 1093640 | tf_op jit(solution)/shard_map/ppermute | solution.py:749
  165.4 8.9 %collective-permute-start.20 = (f32[328,128]{1,0:T(8,128)}, f32[328,128]{1,0:T(8,128)}, u32[]{:S(2)}, u32[]{:S(2)}) collective-permute-start(f32[328,128]{1,0:T(8,128)} %get-tuple-element.97.refs_8_), channel_id=1, source_target_pairs={{0,16},{4,20},{8,24},{12,28},{16,0},{20,4},{24,8},{28,12},{1,17},{... | collective-permute-start | bytes 503816 | tf_op jit(solution)/shard_map/ppermute | solution.py:749
  170.1 7.1 %collective-permute-start.23 = (f32[368,128]{1,0:T(8,128)}, f32[368,128]{1,0:T(8,128)}, u32[]{:S(2)}, u32[]{:S(2)}) collective-permute-start(f32[368,128]{1,0:T(8,128)} %get-tuple-element.100), channel_id=1, source_target_pairs={{0,2},{1,3},{2,0},{3,1},{4,6},{5,7},{6,4},{7,5},{8,10},{9,11},{10,... | collective-permute-start | bytes 565256 | tf_op jit(solution)/shard_map/ppermute | solution.py:749
  171.6 6.8 %collective-permute-start.24 = (f32[368,128]{1,0:T(8,128)}, f32[368,128]{1,0:T(8,128)}, u32[]{:S(2)}, u32[]{:S(2)}) collective-permute-start(f32[368,128]{1,0:T(8,128)} %get-tuple-element.101), channel_id=1, source_target_pairs={{0,3},{1,2},{2,1},{3,0},{4,7},{5,6},{6,5},{7,4},{8,11},{9,10},{10,... | collective-permute-start | bytes 565256 | tf_op jit(solution)/shard_map/ppermute | solution.py:749
  173.1 6.5 %collective-permute-start.22 = (f32[368,128]{1,0:T(8,128)}, f32[368,128]{1,0:T(8,128)}, u32[]{:S(2)}, u32[]{:S(2)}) collective-permute-start(f32[368,128]{1,0:T(8,128)} %get-tuple-element.99.refs_4_), channel_id=1, source_target_pairs={{0,1},{1,0},{2,3},{3,2},{4,5},{5,4},{6,7},{7,6},{8,9},{9,8},{10,11... | collective-permute-start | bytes 565256 | tf_op jit(solution)/shard_map/ppermute | solution.py:749
  174.3 8.5 %collective-permute-start.21 = (f32[328,128]{1,0:T(8,128)}, f32[328,128]{1,0:T(8,128)}, u32[]{:S(2)}, u32[]{:S(2)}) collective-permute-start(f32[328,128]{1,0:T(8,128)} %shard_map.283), channel_id=1, source_target_pairs={{0,24},{4,28},{8,16},{12,20},{16,8},{20,12},{24,0},{28,4},{1,25},{... | collective-permute-start | bytes 503816 | tf_op jit(solution)/shard_map/ppermute | solution.py:749
  185.5 2.2 %collective-permute-start.25 = (f32[904,128]{1,0:T(8,128)}, f32[904,128]{1,0:T(8,128)}, u32[]{:S(2)}, u32[]{:S(2)}) collective-permute-start(f32[904,128]{1,0:T(8,128)} %shard_map.286.refs_8_), channel_id=1, source_target_pairs={{0,4},{4,0},{8,12},{12,8},{16,20},{20,16},{24,28},{28,24},{1,5},{5... | collective-permute-start | bytes 1388552 | tf_op jit(solution)/shard_map/ppermute | solution.py:749

commit v11 on v10

--- a/solution.py
+++ b/solution.py
@@ -931,7 +931,6 @@
         self.steps = {
             "plane": list(range(1, lax.axis_size("ba"))),
             "line": list(range(1, line)),
-            "near last": list(range(near, line)) + list(range(1, near)),
             "far": [near],
         }[way]
         self.near = near
@@ -946,12 +945,12 @@
             for step in self.steps
         ]
 
-    def go(self, payloads, in_turn=False):
+    def go(self, payloads, in_turn=None):
         axis, unit = ("ba", 1) if self.way == "plane" else ("ha", 2)
         arrived = []
         for step, part in zip(self.steps, payloads):
-            if in_turn and len(arrived) == 2:
-                (part,) = tied([part], arrived[1:])
+            if in_turn is not None and len(arrived) == 2:
+                (part,) = tied([part], [arrived[in_turn]])
             arrived.append(exchange(part, axis, unit * step))
         places = {}
         for step, sent, part in zip(self.steps, payloads, arrived):
@@ -965,7 +964,7 @@
         return arrived
 
 
-def run(place, stage, ties=(), in_turn=False, late_ties=()):
+def run(place, stage, ties=(), in_turn=None, late_ties=()):
     made = list(combine(place, stage.groups(), ties))
     if late_ties:
         made = list(tied(made, late_ties))
@@ -1071,8 +1070,10 @@
     above, below = neighbour_rows(dconv_top, dconv_bottom)
 
     plane_sum = Sum([plane_kept, exchange(plane_sent, "ha", 1)], ["plane", "far", "near"])
+    packed_got = exchange(packed_sent, "ha", 1)
+    packed = Sum([packed_kept, packed_got], ["plane"])
+    (line_sent,) = tied([line_sent], [packed_got])
     line_sum = Sum([line_kept, exchange(line_sent, "ha", 1)], ["far", "near", "plane"])
-    packed = Sum([packed_kept, exchange(packed_sent, "ha", 1)], ["plane"])
     made, arrived = run(place, Stage([(plane_sum, "plane"), (packed, "plane")], "plane"))
     more, far = run(place, Stage([(line_sum, "far")], "far"), ties=made, late_ties=[above, below])
     made, arrived = made + more, arrived + far
@@ -1086,11 +1087,11 @@
     packed = Rider(packed.views)
     packed = Rider(packed.views)
     made, arrived = run(
-        place, Stage([(plane_sum, "far"), (line_sum, "near"), (packed, "line")], "near last"), in_turn=True
+        place, Stage([(plane_sum, "far"), (line_sum, "near"), (packed, "line")], "line"), in_turn=0
     )
     run(place, Stage([(in_sum, "plane"), (small, "plane")], "plane"), ties=made)
     made, _ = run(
-        place, Stage([(plane_sum, "near"), (in_sum, "line"), (small, "line")], "line"), ties=arrived, in_turn=True
+        place, Stage([(plane_sum, "near"), (in_sum, "line"), (small, "line")], "line"), ties=arrived, in_turn=1
     )
     packed = Gather(packed.views)
     run(place, Stage([(line_sum, "plane"), (packed, "plane")], "plane"), ties=made)

time: 192 us -> 195 us (1.016)
  waiting for transfers between devices: 27.7 us -> 38.7 us
  starting transfers between devices: 43.2 us -> 34.9 us
    ppermute x22, waiting for transfers between devices: 27.7 us -> 38.7 us  [exchange(): lax.ppermute(values, axis, [(i, i ^ bit) for i in range(lax.axis_size(axi...]
    ppermute x22, starting transfers between devices: 34.7 us -> 26.2 us  [exchange(): lax.ppermute(values, axis, [(i, i ^ bit) for i in range(lax.axis_size(axi...]
  transfers between devices with their start and end apart: 26 -> 26, of which waited for: 12 -> 9; matrix products, arithmetic and copies ran while one was open for 0% -> 0% of each run, Pallas kernels for 30% -> 30%
where the time goes in v11:
time: 195 us; the launch traced here: 194 us
  Pallas kernels  117 us (60%)
  waiting for transfers between devices  38.7 us (20%)
  starting transfers between devices  34.9 us (18%)
  local copies, waits for them, and re-layouts  2.08 us (1%)
    pallas_call x1, Pallas kernels, forward(): pl.pallas_call(functools.partial(forward_kernel, rows=rows, cols=cols, co...  49.8 us
    ppermute x22, waiting for transfers between devices, exchange(): lax.ppermute(values, axis, [(i, i ^ bit) for i in range(lax.axis_size(axi...  38.7 us
    pallas_call x9, Pallas kernels, combine(): pl.pallas_call(kernel, in_specs=[in_smem()] + [in_hbm()] * (len(arrays) +...  29.9 us
    pallas_call x1, Pallas kernels, backward(): pl.pallas_call(functools.partial(backward_kernel, rows=rows, cols=cols),...  29.3 us
    ppermute x22, starting transfers between devices, exchange(): lax.ppermute(values, axis, [(i, i ^ bit) for i in range(lax.axis_size(axi...  26.2 us
    ppermute x4, starting transfers between devices, neighbour_rows(): return (lax.ppermute(bottom, 'ha', up), lax.ppermute(top, 'ha', down))  8.69 us
    pallas_call x1, Pallas kernels, head(): pl.pallas_call(functools.partial(head_kernel, rows=rows, cols=cols), in_s...  7.68 us
  transfers between devices with their start and end apart: 26, of which 9 were waited for; matrix products, arithmetic and copies ran while one was open for 0% of the time, Pallas kernels for 30%

profile of v11, /device:TPU:0, one launch (start us, length us, event | category | flops | bytes accessed | tf_op | source)
XLA Modules:
  0.0 194.1 jit_solution(903084580588264820)
XLA Ops:
  0.6 2.1 %fusion = (f32[1,3,64,512]{3,2,1,0:T(8,128)}, f32[1,3,64,512]{3,2,1,0:T(8,128)}) fusion(f32[1,8,64,512]{3,2,1,0:T(8,128)} %param.17), kind=kLoop, calls=%fused_computation.1 | loop fusion | bytes 1572864 | tf_op jit(solution)/shard_map/slice | solution.py:1060
  2.7 3.1 %collective-permute-start = (f32[192,512]{1,0:T(8,128)}, f32[192,512]{1,0:T(8,128)}, u32[]{:S(2)}, u32[]{:S(2)}) collective-permute-start(f32[192,512]{1,0:T(8,128)} %bitcast.5), channel_id=1, source_target_pairs={{0,4},{4,8},{8,12},{12,16},{16,20},{20,24},{24,28},{1,5},{5,9},{9,... | collective-permute-start | bytes 1179656 | tf_op jit(solution)/shard_map/ppermute | solution.py:978
  5.9 1.3 collective-permute-start.1
  7.1 0.7 pad_add_fusion.place_ref
  7.8 7.7 %shard_map.272 = (f32[8,512,128]{2,1,0:T(8,128)}, f32[896,128]{1,0:T(8,128)}, f32[512,128]{1,0:T(8,128)}, f32[512,128]{1,0:T(8,128)}, f32[7,8,8,128]{3,2,1,0:T(8,128)}) custom-call(s32[2]{0:T(128)} %pad_add_fusion.place_ref, s32[64,64]{1,0:T(8,128)} %bitcast.41, s32[1,36]{1,0:T(1,128)} %one_table.1, s32[1,36]{1,0:T(1,128)} %two_table.1, s32[64,64]{1,0:T(8,128)} %bitcast.42, ...), custom_call_target="tpu_custom_call" | custom-call | flops 7699999744 | tf_op jit(solution)/shard_map/pallas_call | solution.py:307
  15.5 49.8 %shard_map.273 = (f32[512,512]{1,0:T(8,128)}, f32[512,512]{1,0:T(8,128)}, f32[8,512,128]{2,1,0:T(8,128)}, f32[8,192,128]{2,1,0:T(8,128)}, f32[8,192,128]{2,1,0:T...) custom-call(s32[2]{0:T(128)} %pad_add_fusion.place_ref, ...), custom_call_target="tpu_custom_call" | custom-call | flops 52800000000 | tf_op jit(solution)/shard_map/pallas_call | solution.py:592
  65.3 2.6 %collective-permute-start.4 = (f32[4,4,384,128]{3,2,1,0:T(8,128)}, f32[4,4,384,128]{3,2,1,0:T(8,128)}, u32[]{:S(2)}, u32[]{:S(2)}) collective-permute-start(f32[4,4,384,128]{3,2,1,0:T(8,128)} %get-tuple-element.75), channel_id=1, source_target_pairs={{0,4},{4,0},{8,12},{12,8},{16,20},{20,16},{24,28},{28,24},{1,5},{5... | collective-permute-start | bytes 9437192 | tf_op jit(solution)/shard_map/ppermute | solution.py:749
  67.9 0.1 collective-permute-start.5
  68.0 6.1 %collective-permute-done.5.refs_3_.refs_1_.refs_4_ = f32[704,128]{1,0:T(8,128)} collective-permute-done((f32[704,128]{1,0:T(8,128)}, f32[704,128]{1,0:T(8,128)}, u32[]{:S(2)}, u32[]{:S(2)}) %collective-permute-start.5) | collective-permute-done | bytes 360480 | tf_op jit(solution)/shard_map/ppermute | solution.py:749
  74.1 0.4 collective-permute-start.6
  74.4 3.0 %collective-permute-start.2 = (f32[8,192,128]{2,1,0:T(8,128)}, f32[8,192,128]{2,1,0:T(8,128)}, u32[]{:S(2)}, u32[]{:S(2)}) collective-permute-start(f32[8,192,128]{2,1,0:T(8,128)} %get-tuple-element.70), channel_id=1, source_target_pairs={{0,4},{4,8},{8,12},{12,16},{16,20},{20,24},{24,28},{1,5},{5,9},{9,... | collective-permute-start | bytes 2359304 | tf_op jit(solution)/shard_map/ppermute | solution.py:978
  77.4 1.3 collective-permute-start.3
  78.7 4.4 %shard_map.274 = (f32[1712,128]{1,0:T(8,128)}, f32[1712,128]{1,0:T(8,128)}, f32[1712,128]{1,0:T(8,128)}) custom-call(s32[2]{0:T(128)} %pad_add_fusion.place_ref, f32[6144,128]{1,0:T(8,128)} %bitcast.25, f32[6144,128]{1,0:T(8,128)} %bitcast.13.refs_1_.refs_9_, f32[704,128]{1,0:T(8,128)} %get-tuple-element.76.refs_2_.refs_3_, ...), custom_call_target="tpu_custom_call" | custom-call | flops 3992595200 | tf_op jit(solution)/shard_map/pallas_call | solution.py:857
  83.1 1.5 collective-permute-start.7
  84.7 1.5 collective-permute-start.8
  86.2 0.5 collective-permute-start.9
  86.7 3.0 %shard_map.276.refs_0_ = f32[1536,128]{1,0:T(8,128)} custom-call(s32[2]{0:T(128)} %pad_add_fusion.place_ref, f32[3072,128]{1,0:T(8,128)} %bitcast.29, f32[3072,128]{1,0:T(8,128)} %bitcast.15.refs_1_.refs_8_, f32[1712,128]{1,0:T(8,128)} %get-tuple-element.78.refs_2_.rest_0_, f32[1712,128]{1,0:T(8,128)} %get-tuple-element.79.refs_3_.rest_1_, ...), custom_call_target="tpu_custom_call" | custom-call | flops 1965075200 | tf_op jit(solution)/shard_map/pallas_call | solution.py:857
  89.8 4.1 %collective-permute-start.10 = (f32[1536,128]{1,0:T(8,128)}, f32[1536,128]{1,0:T(8,128)}, u32[]{:S(2)}, u32[]{:S(2)}) collective-permute-start(f32[1536,128]{1,0:T(8,128)} %shard_map.277.rest_3_), channel_id=1, source_target_pairs={{0,16},{4,20},{8,24},{12,28},{16,0},{20,4},{24,8},{28,12},{1,17},{... | collective-permute-start | bytes 2359304 | tf_op jit(solution)/shard_map/ppermute | solution.py:749
  93.9 29.3 %shard_map.278 = (f32[512,512]{1,0:T(8,128)}, f32[4,4,128,128]{3,2,1,0:T(8,128)}, f32[4,4,128,128]{3,2,1,0:T(8,128)}, f32[200,128]{1,0:T(8,128)}, f32[200,128]{1,0:T(8,128)}) custom-call(s32[2]{0:T(128)} %pad_add_fusion.place_ref, s32[64,64]{1,0:T(8,128)} %bitcast.44, s32[64,64]{1,0:T(8,128)} %bitcast.45, ...), custom_call_target="tpu_custom_call" | custom-call | flops 27499999232 | tf_op jit(solution)/shard_map/pallas_call | solution.py:718
  123.2 6.0 %collective-permute-done.10.refs_5_.refs_2_.refs_9_ = f32[1536,128]{1,0:T(8,128)} collective-permute-done((f32[1536,128]{1,0:T(8,128)}, f32[1536,128]{1,0:T(8,128)}, u32[]{:S(2)}, u32[]{:S(2)}) %collective-permute-start.10) | collective-permute-done | bytes 786464 | tf_op jit(solution)/shard_map/ppermute | solution.py:749
  129.3 0.2 collective-permute-start.11
  129.5 0.4 collective-permute-start.12
  129.9 3.7 %shard_map.280 = (f32[944,128]{1,0:T(8,128)}, f32[944,128]{1,0:T(8,128)}, f32[176,128]{1,0:T(8,128)}) custom-call(s32[2]{0:T(128)} %pad_add_fusion.place_ref, f32[3072,128]{1,0:T(8,128)} %bitcast.30, f32[3072,128]{1,0:T(8,128)} %bitcast.15.refs_1_.refs_8_, f32[1536,128]{1,0:T(8,128)} %collective-permute-done.10.refs_5_.refs_2_.refs_9_, ...), custom_call_target="tpu_custom_call" | custom-call | flops 2806120448 | tf_op jit(solution)/shard_map/pallas_call | solution.py:857
  133.6 0.1 collective-permute-start.17
  133.6 2.9 %collective-permute-start.16 = (f32[944,128]{1,0:T(8,128)}, f32[944,128]{1,0:T(8,128)}, u32[]{:S(2)}, u32[]{:S(2)}) collective-permute-start(f32[944,128]{1,0:T(8,128)} %get-tuple-element.91.refs_5_), channel_id=1, source_target_pairs={{0,16},{4,20},{8,24},{12,28},{16,0},{20,4},{24,8},{28,12},{1,17},{... | collective-permute-start | bytes 1449992 | tf_op jit(solution)/shard_map/ppermute | solution.py:749
  136.6 3.0 %shard_map.281 = (f32[712,128]{1,0:T(8,128)}, f32[712,128]{1,0:T(8,128)}, f32[712,128]{1,0:T(8,128)}) custom-call(s32[2]{0:T(128)} %pad_add_fusion.place_ref, f32[2048,128]{1,0:T(8,128)} %bitcast.33, f32[2048,128]{1,0:T(8,128)} %bitcast.18.refs_1_.refs_7_, f32[200,128]{1,0:T(8,128)} %get-tuple-element.88.refs_2_, ...), custom_call_target="tpu_custom_call" | custom-call | flops 2152808448 | tf_op jit(solution)/shard_map/pallas_call | solution.py:857
  139.6 1.6 collective-permute-start.14
  141.1 1.4 collective-permute-start.15
  142.6 0.5 collective-permute-start.13
  143.1 13.9 %collective-permute-done.17.refs_1_.refs_12_.refs_3_.refs_10_ = f32[944,128]{1,0:T(8,128)} collective-permute-done((f32[944,128]{1,0:T(8,128)}, f32[944,128]{1,0:T(8,128)}, u32[]{:S(2)}, u32[]{:S(2)}) %collective-permute-start.17) | collective-permute-done | bytes 483360 | tf_op jit(solution)/shard_map/ppermute | solution.py:749
  157.1 1.5 collective-permute-start.18
  158.5 5.2 %collective-permute-done.18.refs_14_.refs_6_ = f32[176,128]{1,0:T(8,128)} collective-permute-done((f32[176,128]{1,0:T(8,128)}, f32[176,128]{1,0:T(8,128)}, u32[]{:S(2)}, u32[]{:S(2)}) %collective-permute-start.18) | collective-permute-done | bytes 90144 | tf_op jit(solution)/shard_map/ppermute | solution.py:749
  163.7 3.4 %shard_map.283 = (f32[712,128]{1,0:T(8,128)}, f32[328,128]{1,0:T(8,128)}, f32[328,128]{1,0:T(8,128)}) custom-call(s32[2]{0:T(128)} %pad_add_fusion.place_ref, f32[6144,128]{1,0:T(8,128)} %bitcast.27, f32[6144,128]{1,0:T(8,128)} %bitcast.13.refs_1_.refs_9_, f32[1712,128]{1,0:T(8,128)} %collective-permute-done.7.refs_2_.refs_5_, ...), custom_call_target="tpu_custom_call" | custom-call | flops 2299991552 | tf_op jit(solution)/shard_map/pallas_call | solution.py:857
  167.2 2.0 %collective-permute-start.20 = (f32[328,128]{1,0:T(8,128)}, f32[328,128]{1,0:T(8,128)}, u32[]{:S(2)}, u32[]{:S(2)}) collective-permute-start(f32[328,128]{1,0:T(8,128)} %get-tuple-element.97.refs_8_), channel_id=1, source_target_pairs={{0,16},{4,20},{8,24},{12,28},{16,0},{20,4},{24,8},{28,12},{1,17},{... | collective-permute-start | bytes 503816 | tf_op jit(solution)/shard_map/ppermute | solution.py:749
  169.2 3.0 %shard_map.285 = (f32[368,128]{1,0:T(8,128)}, f32[368,128]{1,0:T(8,128)}, f32[368,128]{1,0:T(8,128)}) custom-call(s32[2]{0:T(128)} %pad_add_fusion.place_ref, f32[3072,128]{1,0:T(8,128)} %bitcast.31, f32[3072,128]{1,0:T(8,128)} %bitcast.15.refs_1_.refs_8_, f32[1536,128]{1,0:T(8,128)} %collective-permute-done.10.refs_5_.refs_2_.refs_9_, ...), custom_call_target="tpu_custom_call" | custom-call | flops 1871959424 | tf_op jit(solution)/shard_map/pallas_call | solution.py:857
  172.2 1.6 collective-permute-start.23
  173.8 1.4 collective-permute-start.24
  175.2 0.5 collective-permute-start.22
  175.8 2.1 %collective-permute-done.20.refs_1_.refs_2_.refs_6_ = f32[328,128]{1,0:T(8,128)} collective-permute-done((f32[328,128]{1,0:T(8,128)}, f32[328,128]{1,0:T(8,128)}, u32[]{:S(2)}, u32[]{:S(2)}) %collective-permute-start.20) | collective-permute-done | bytes 167968 | tf_op jit(solution)/shard_map/ppermute | solution.py:749
  177.9 1.1 collective-permute-start.21
  179.0 1.0 collective-permute-done.23.refs_12_.refs_6_
  179.9 1.1 collective-permute-done.24.refs_13_.refs_7_
  181.0 1.2 collective-permute-done.22.refs_11_.refs_5_
  182.2 3.2 %shard_map.286 = (f32[128,256]{1,0:T(8,128)}, f32[64,512]{1,0:T(8,128)}, f32[64,128]{1,0:T(8,128)}) custom-call(s32[2]{0:T(128)} %pad_add_fusion.place_ref, f32[6144,128]{1,0:T(8,128)} %bitcast.28, f32[6144,128]{1,0:T(8,128)} %bitcast.13.refs_1_.refs_9_, f32[1712,128]{1,0:T(8,128)} %collective-permute-done.7.refs_2_.refs_5_, ...), custom_call_target="tpu_custom_call" | custom-call | flops 1965075200 | tf_op jit(solution)/shard_map/pallas_call | solution.py:857
  185.5 2.7 %shard_map.287.refs_8_ = f32[904,128]{1,0:T(8,128)} custom-call(s32[2]{0:T(128)} %pad_add_fusion.place_ref, f32[712,128]{1,0:T(8,128)} %get-tuple-element.96.refs_7_.refs_0_, f32[712,128]{1,0:T(8,128)} %collective-permute-done.19.refs_6_.refs_1_.refs_5_, f32[328,128]{1,0:T(8,128)} %collective-permute-done.20.refs_1_.refs_2_.refs_6_, ...), custom_call_target="tpu_custom_call" | custom-call | flops 1552061824 | tf_op jit(solution)/shard_map/pallas_call | solution.py:857
  188.2 0.1 collective-permute-start.25
  188.3 2.1 %collective-permute-done.25.refs_9_ = f32[904,128]{1,0:T(8,128)} collective-permute-done((f32[904,128]{1,0:T(8,128)}, f32[904,128]{1,0:T(8,128)}, u32[]{:S(2)}, u32[]{:S(2)}) %collective-permute-start.25) | collective-permute-done | bytes 462880 | tf_op jit(solution)/shard_map/ppermute | solution.py:749
  190.4 3.5 %shard_map.288 = (f32[128,128]{1,0:T(8,128)}, f32[49,960]{1,0:T(8,128)}, f32[1,512]{1,0:T(1,128)}, f32[1,512]{1,0:T(1,128)}, f32[1,512]{1,0:T(1,128)}, /*index=5...) custom-call(s32[2]{0:T(128)} %pad_add_fusion.place_ref, ...), custom_call_target="tpu_custom_call" | custom-call | flops 1995112576 | tf_op jit(solution)/shard_map/pallas_call | solution.py:857
  (23 shorter events, 0.1 us)
Async XLA Ops:
  2.7 12.8 %collective-permute-start = (f32[192,512]{1,0:T(8,128)}, f32[192,512]{1,0:T(8,128)}, u32[]{:S(2)}, u32[]{:S(2)}) collective-permute-start(f32[192,512]{1,0:T(8,128)} %bitcast.5), channel_id=1, source_target_pairs={{0,4},{4,8},{8,12},{12,16},{16,20},{20,24},{24,28},{1,5},{5,9},{9,... | collective-permute-start | bytes 1179656 | tf_op jit(solution)/shard_map/ppermute | solution.py:978
  5.9 9.6 %collective-permute-start.1 = (f32[192,512]{1,0:T(8,128)}, f32[192,512]{1,0:T(8,128)}, u32[]{:S(2)}, u32[]{:S(2)}) collective-permute-start(f32[192,512]{1,0:T(8,128)} %bitcast.6), channel_id=1, source_target_pairs={{4,0},{8,4},{12,8},{16,12},{20,16},{24,20},{28,24},{5,1},{9,5},{13... | collective-permute-start | bytes 1179656 | tf_op jit(solution)/shard_map/ppermute | solution.py:978
  65.3 13.4 %collective-permute-start.4 = (f32[4,4,384,128]{3,2,1,0:T(8,128)}, f32[4,4,384,128]{3,2,1,0:T(8,128)}, u32[]{:S(2)}, u32[]{:S(2)}) collective-permute-start(f32[4,4,384,128]{3,2,1,0:T(8,128)} %get-tuple-element.75), channel_id=1, source_target_pairs={{0,4},{4,0},{8,12},{12,8},{16,20},{20,16},{24,28},{28,24},{1,5},{5... | collective-permute-start | bytes 9437192 | tf_op jit(solution)/shard_map/ppermute | solution.py:749
  67.9 6.1 %collective-permute-start.5 = (f32[704,128]{1,0:T(8,128)}, f32[704,128]{1,0:T(8,128)}, u32[]{:S(2)}, u32[]{:S(2)}) collective-permute-start(f32[704,128]{1,0:T(8,128)} %get-tuple-element.77), channel_id=1, source_target_pairs={{0,4},{4,0},{8,12},{12,8},{16,20},{20,16},{24,28},{28,24},{1,5},{5... | collective-permute-start | bytes 1081352 | tf_op jit(solution)/shard_map/ppermute | solution.py:749
  74.1 12.1 %collective-permute-start.6 = (f32[4,4,192,128]{3,2,1,0:T(8,128)}, f32[4,4,192,128]{3,2,1,0:T(8,128)}, u32[]{:S(2)}, u32[]{:S(2)}) collective-permute-start(f32[4,4,192,128]{3,2,1,0:T(8,128)} %shard_map.275), channel_id=1, source_target_pairs={{0,4},{4,0},{8,12},{12,8},{16,20},{20,16},{24,28},{28,24},{1,5},{5... | collective-permute-start | bytes 4718600 | tf_op jit(solution)/shard_map/ppermute | solution.py:749
  74.4 15.3 %collective-permute-start.2 = (f32[8,192,128]{2,1,0:T(8,128)}, f32[8,192,128]{2,1,0:T(8,128)}, u32[]{:S(2)}, u32[]{:S(2)}) collective-permute-start(f32[8,192,128]{2,1,0:T(8,128)} %get-tuple-element.70), channel_id=1, source_target_pairs={{0,4},{4,8},{8,12},{12,16},{16,20},{20,24},{24,28},{1,5},{5,9},{9,... | collective-permute-start | bytes 2359304 | tf_op jit(solution)/shard_map/ppermute | solution.py:978
  77.4 12.3 %collective-permute-start.3 = (f32[8,192,128]{2,1,0:T(8,128)}, f32[8,192,128]{2,1,0:T(8,128)}, u32[]{:S(2)}, u32[]{:S(2)}) collective-permute-start(f32[8,192,128]{2,1,0:T(8,128)} %get-tuple-element.72), channel_id=1, source_target_pairs={{4,0},{8,4},{12,8},{16,12},{20,16},{24,20},{28,24},{5,1},{9,5},{13... | collective-permute-start | bytes 2359304 | tf_op jit(solution)/shard_map/ppermute | solution.py:978
  83.1 46.1 %collective-permute-start.7 = (f32[1712,128]{1,0:T(8,128)}, f32[1712,128]{1,0:T(8,128)}, u32[]{:S(2)}, u32[]{:S(2)}) collective-permute-start(f32[1712,128]{1,0:T(8,128)} %get-tuple-element.78.refs_2_.rest_0_), channel_id=1, source_target_pairs={{0,1},{1,0},{2,3},{3,2},{4,5},{5,4},{6,7},{7,6},{8,9},{9,8},{10,11... | collective-permute-start | bytes 2629640 | tf_op jit(solution)/shard_map/ppermute | solution.py:749
  84.7 44.6 %collective-permute-start.8 = (f32[1712,128]{1,0:T(8,128)}, f32[1712,128]{1,0:T(8,128)}, u32[]{:S(2)}, u32[]{:S(2)}) collective-permute-start(f32[1712,128]{1,0:T(8,128)} %get-tuple-element.79.refs_3_.rest_1_), channel_id=1, source_target_pairs={{0,2},{1,3},{2,0},{3,1},{4,6},{5,7},{6,4},{7,5},{8,10},{9,11},{10,... | collective-permute-start | bytes 2629640 | tf_op jit(solution)/shard_map/ppermute | solution.py:749
  86.2 43.1 %collective-permute-start.9 = (f32[1712,128]{1,0:T(8,128)}, f32[1712,128]{1,0:T(8,128)}, u32[]{:S(2)}, u32[]{:S(2)}) collective-permute-start(f32[1712,128]{1,0:T(8,128)} %get-tuple-element.80.refs_4_.rest_2_), channel_id=1, source_target_pairs={{0,3},{1,2},{2,1},{3,0},{4,7},{5,6},{6,5},{7,4},{8,11},{9,10},{10,... | collective-permute-start | bytes 2629640 | tf_op jit(solution)/shard_map/ppermute | solution.py:749
  89.8 39.5 %collective-permute-start.10 = (f32[1536,128]{1,0:T(8,128)}, f32[1536,128]{1,0:T(8,128)}, u32[]{:S(2)}, u32[]{:S(2)}) collective-permute-start(f32[1536,128]{1,0:T(8,128)} %shard_map.277.rest_3_), channel_id=1, source_target_pairs={{0,16},{4,20},{8,24},{12,28},{16,0},{20,4},{24,8},{28,12},{1,17},{... | collective-permute-start | bytes 2359304 | tf_op jit(solution)/shard_map/ppermute | solution.py:749
  129.3 7.3 %collective-permute-start.11 = (f32[4,4,128,128]{3,2,1,0:T(8,128)}, f32[4,4,128,128]{3,2,1,0:T(8,128)}, u32[]{:S(2)}, u32[]{:S(2)}) collective-permute-start(f32[4,4,128,128]{3,2,1,0:T(8,128)} %get-tuple-element.87), channel_id=1, source_target_pairs={{0,4},{4,0},{8,12},{12,8},{16,20},{20,16},{24,28},{28,24},{1,5},{5... | collective-permute-start | bytes 3145736 | tf_op jit(solution)/shard_map/ppermute | solution.py:749
  129.5 7.1 %collective-permute-start.12 = (f32[200,128]{1,0:T(8,128)}, f32[200,128]{1,0:T(8,128)}, u32[]{:S(2)}, u32[]{:S(2)}) collective-permute-start(f32[200,128]{1,0:T(8,128)} %get-tuple-element.89), channel_id=1, source_target_pairs={{0,4},{4,0},{8,12},{12,8},{16,20},{20,16},{24,28},{28,24},{1,5},{5... | collective-permute-start | bytes 307208 | tf_op jit(solution)/shard_map/ppermute | solution.py:749
  133.6 23.5 %collective-permute-start.17 = (f32[944,128]{1,0:T(8,128)}, f32[944,128]{1,0:T(8,128)}, u32[]{:S(2)}, u32[]{:S(2)}) collective-permute-start(f32[944,128]{1,0:T(8,128)} %get-tuple-element.90.refs_4_), channel_id=1, source_target_pairs={{0,8},{4,12},{8,0},{12,4},{16,24},{20,28},{24,16},{28,20},{1,9},{5... | collective-permute-start | bytes 1449992 | tf_op jit(solution)/shard_map/ppermute | solution.py:749
  133.6 24.9 %collective-permute-start.16 = (f32[944,128]{1,0:T(8,128)}, f32[944,128]{1,0:T(8,128)}, u32[]{:S(2)}, u32[]{:S(2)}) collective-permute-start(f32[944,128]{1,0:T(8,128)} %get-tuple-element.91.refs_5_), channel_id=1, source_target_pairs={{0,16},{4,20},{8,24},{12,28},{16,0},{20,4},{24,8},{28,12},{1,17},{... | collective-permute-start | bytes 1449992 | tf_op jit(solution)/shard_map/ppermute | solution.py:749
  139.6 24.2 %collective-permute-start.14 = (f32[712,128]{1,0:T(8,128)}, f32[712,128]{1,0:T(8,128)}, u32[]{:S(2)}, u32[]{:S(2)}) collective-permute-start(f32[712,128]{1,0:T(8,128)} %get-tuple-element.94), channel_id=1, source_target_pairs={{0,2},{1,3},{2,0},{3,1},{4,6},{5,7},{6,4},{7,5},{8,10},{9,11},{10,... | collective-permute-start | bytes 1093640 | tf_op jit(solution)/shard_map/ppermute | solution.py:749
  141.1 22.6 %collective-permute-start.15 = (f32[712,128]{1,0:T(8,128)}, f32[712,128]{1,0:T(8,128)}, u32[]{:S(2)}, u32[]{:S(2)}) collective-permute-start(f32[712,128]{1,0:T(8,128)} %get-tuple-element.95), channel_id=1, source_target_pairs={{0,3},{1,2},{2,1},{3,0},{4,7},{5,6},{6,5},{7,4},{8,11},{9,10},{10,... | collective-permute-start | bytes 1093640 | tf_op jit(solution)/shard_map/ppermute | solution.py:749
  142.6 21.2 %collective-permute-start.13 = (f32[712,128]{1,0:T(8,128)}, f32[712,128]{1,0:T(8,128)}, u32[]{:S(2)}, u32[]{:S(2)}) collective-permute-start(f32[712,128]{1,0:T(8,128)} %get-tuple-element.93.refs_11_), channel_id=1, source_target_pairs={{0,1},{1,0},{2,3},{3,2},{4,5},{5,4},{6,7},{7,6},{8,9},{9,8},{10,11... | collective-permute-start | bytes 1093640 | tf_op jit(solution)/shard_map/ppermute | solution.py:749
  157.1 6.6 %collective-permute-start.18 = (f32[176,128]{1,0:T(8,128)}, f32[176,128]{1,0:T(8,128)}, u32[]{:S(2)}, u32[]{:S(2)}) collective-permute-start(f32[176,128]{1,0:T(8,128)} %shard_map.282), channel_id=1, source_target_pairs={{0,24},{4,28},{8,16},{12,20},{16,8},{20,12},{24,0},{28,4},{1,25},{... | collective-permute-start | bytes 270344 | tf_op jit(solution)/shard_map/ppermute | solution.py:749
  167.1 15.1 %collective-permute-start.19 = (f32[712,128]{1,0:T(8,128)}, f32[712,128]{1,0:T(8,128)}, u32[]{:S(2)}, u32[]{:S(2)}) collective-permute-start(f32[712,128]{1,0:T(8,128)} %get-tuple-element.96.refs_7_.refs_0_), channel_id=1, source_target_pairs={{0,8},{4,12},{8,0},{12,4},{16,24},{20,28},{24,16},{28,20},{1,9},{5... | collective-permute-start | bytes 1093640 | tf_op jit(solution)/shard_map/ppermute | solution.py:749
  167.2 10.7 %collective-permute-start.20 = (f32[328,128]{1,0:T(8,128)}, f32[328,128]{1,0:T(8,128)}, u32[]{:S(2)}, u32[]{:S(2)}) collective-permute-start(f32[328,128]{1,0:T(8,128)} %get-tuple-element.97.refs_8_), channel_id=1, source_target_pairs={{0,16},{4,20},{8,24},{12,28},{16,0},{20,4},{24,8},{28,12},{1,17},{... | collective-permute-start | bytes 503816 | tf_op jit(solution)/shard_map/ppermute | solution.py:749
  172.2 7.7 %collective-permute-start.23 = (f32[368,128]{1,0:T(8,128)}, f32[368,128]{1,0:T(8,128)}, u32[]{:S(2)}, u32[]{:S(2)}) collective-permute-start(f32[368,128]{1,0:T(8,128)} %get-tuple-element.100), channel_id=1, source_target_pairs={{0,2},{1,3},{2,0},{3,1},{4,6},{5,7},{6,4},{7,5},{8,10},{9,11},{10,... | collective-permute-start | bytes 565256 | tf_op jit(solution)/shard_map/ppermute | solution.py:749
  173.8 7.2 %collective-permute-start.24 = (f32[368,128]{1,0:T(8,128)}, f32[368,128]{1,0:T(8,128)}, u32[]{:S(2)}, u32[]{:S(2)}) collective-permute-start(f32[368,128]{1,0:T(8,128)} %get-tuple-element.101), channel_id=1, source_target_pairs={{0,3},{1,2},{2,1},{3,0},{4,7},{5,6},{6,5},{7,4},{8,11},{9,10},{10,... | collective-permute-start | bytes 565256 | tf_op jit(solution)/shard_map/ppermute | solution.py:749
  175.2 6.9 %collective-permute-start.22 = (f32[368,128]{1,0:T(8,128)}, f32[368,128]{1,0:T(8,128)}, u32[]{:S(2)}, u32[]{:S(2)}) collective-permute-start(f32[368,128]{1,0:T(8,128)} %get-tuple-element.99.refs_4_), channel_id=1, source_target_pairs={{0,1},{1,0},{2,3},{3,2},{4,5},{5,4},{6,7},{7,6},{8,9},{9,8},{10,11... | collective-permute-start | bytes 565256 | tf_op jit(solution)/shard_map/ppermute | solution.py:749
  177.9 7.6 %collective-permute-start.21 = (f32[328,128]{1,0:T(8,128)}, f32[328,128]{1,0:T(8,128)}, u32[]{:S(2)}, u32[]{:S(2)}) collective-permute-start(f32[328,128]{1,0:T(8,128)} %shard_map.284), channel_id=1, source_target_pairs={{0,24},{4,28},{8,16},{12,20},{16,8},{20,12},{24,0},{28,4},{1,25},{... | collective-permute-start | bytes 503816 | tf_op jit(solution)/shard_map/ppermute | solution.py:749
  188.2 2.2 %collective-permute-start.25 = (f32[904,128]{1,0:T(8,128)}, f32[904,128]{1,0:T(8,128)}, u32[]{:S(2)}, u32[]{:S(2)}) collective-permute-start(f32[904,128]{1,0:T(8,128)} %shard_map.287.refs_8_), channel_id=1, source_target_pairs={{0,4},{4,0},{8,12},{12,8},{16,20},{20,16},{24,28},{28,24},{1,5},{5... | collective-permute-start | bytes 1388552 | tf_op jit(solution)/shard_map/ppermute | solution.py:749

commit v12 on v11

--- a/solution.py
+++ b/solution.py
@@ -960,15 +960,17 @@
                 row += one.leaving(way, 1)[0].size()
         for one, way in self.members:
             mine = places.get(id(one), [])
-            one.keep(way, mine[0][0] if mine else None, [part for _, part in mine])
+            one.keep(way, mine[:2][-1][0] if mine else None, [part for _, part in mine])
         return arrived
 
 
-def run(place, stage, ties=(), in_turn=None, late_ties=()):
-    made = list(combine(place, stage.groups(), ties))
+def run(place, stage, ties=(), in_turn=None, late_ties=(), extra=()):
+    groups = stage.groups()
+    made = list(combine(place, groups + list(extra), ties))
+    made, more = made[: len(groups)], made[len(groups) :]
     if late_ties:
         made = list(tied(made, late_ties))
-    return made, stage.go(made, in_turn)
+    return made, stage.go(made, in_turn), more
 
 
 def neighbour_rows(top, bottom):
@@ -996,21 +998,17 @@
     din_ref, dk_ref, gain_ref = outs[:3]
     scratch = outs[-1]
     lay_beside(values[0], din_ref)
-    own, other = values[1], values[2]
-    small = small_rows(blocks, gain_ref.shape[1]) // 2
+    count = lax.axis_size("ba")
+    own, other = values[1 : 2 + count], values[2 + count :]
     mine = ha % 2 == 0
-    first, second = jnp.where(mine, own, other), jnp.where(mine, other, own)
-    dkern = jnp.concatenate([first[:small], second[:small]], axis=0)
+    dkern = jnp.concatenate([jnp.where(mine, own[0], other[0]), jnp.where(mine, other[0], own[0])], axis=0)
     joined = jnp.concatenate([dkern[k * TAPS : (k + 1) * TAPS] for k in range(blocks)], axis=1)
     dk_ref[...] = joined[:, joined.shape[1] - dk_ref.shape[1] :]
-    half = own.shape[0] - small
-    count = lax.axis_size("ba")
-    part = half // count
-    for core, rows in ((0, first), (1, second)):
-        for step in range(count):
-            start = core * half + (ba ^ step) * part
-            source = small + step * part
-            scratch[pl.ds(pl.multiple_of(start, 8), part), :] = rows[source : source + part]
+    part = own[1].shape[0]
+    for side, parts in ((ha % 2, own[1:]), (1 - ha % 2, other[1:])):
+        for step, rows in enumerate(parts):
+            start = (side * count + (ba ^ step)) * part
+            scratch[pl.ds(pl.multiple_of(start, 8), part), :] = rows
     dim = gain_ref.shape[1]
     for k in range(dim // LANES):
         columns = slice(k * LANES, (k + 1) * LANES)
@@ -1070,12 +1068,10 @@
     above, below = neighbour_rows(dconv_top, dconv_bottom)
 
     plane_sum = Sum([plane_kept, exchange(plane_sent, "ha", 1)], ["plane", "far", "near"])
-    packed_got = exchange(packed_sent, "ha", 1)
-    packed = Sum([packed_kept, packed_got], ["plane"])
-    (line_sent,) = tied([line_sent], [packed_got])
     line_sum = Sum([line_kept, exchange(line_sent, "ha", 1)], ["far", "near", "plane"])
-    made, arrived = run(place, Stage([(plane_sum, "plane"), (packed, "plane")], "plane"))
-    more, far = run(place, Stage([(line_sum, "far")], "far"), ties=made, late_ties=[above, below])
+    packed = Sum([packed_kept, exchange(packed_sent, "ha", 1)], ["plane"])
+    made, arrived, _ = run(place, Stage([(plane_sum, "plane"), (packed, "plane")], "plane"))
+    more, far, _ = run(place, Stage([(line_sum, "far")], "far"), ties=made, late_ties=[above, below])
     made, arrived = made + more, arrived + far
     dcanvas, in_kept, in_sent, small_kept, small_sent = backward(
         place, ids, above, dconv, below, joined, depth_kernel, own, gain, dmiddle, weight_in, made,
@@ -1086,15 +1082,15 @@
     small = Rider([flat_view(small_kept), flat_view(exchange(small_sent, "ha", 1))])
     packed = Rider(packed.views)
     packed = Rider(packed.views)
-    made, arrived = run(
+    made, arrived, _ = run(
         place, Stage([(plane_sum, "far"), (line_sum, "near"), (packed, "line")], "line"), in_turn=0
     )
     run(place, Stage([(in_sum, "plane"), (small, "plane")], "plane"), ties=made)
-    made, _ = run(
-        place, Stage([(plane_sum, "near"), (in_sum, "line"), (small, "line")], "line"), ties=arrived, in_turn=1
-    )
+    along = Stage([(plane_sum, "near"), (in_sum, "line"), (small, "line")], "line")
+    made, arrived, (own_small,) = run(place, along, ties=arrived, in_turn=1, extra=[[small.views]])
     packed = Gather(packed.views)
-    run(place, Stage([(line_sum, "plane"), (packed, "plane")], "plane"), ties=made)
+    across = Stage([(line_sum, "plane"), (packed, "plane")], "plane")
+    _, crossed, (own_packed,) = run(place, across, ties=made, extra=[[packed.views]])
     cut = plane_sum.views[0].rows // 2
     rest = (line_sum.views[0].rows - dim // count_ha * lane_blocks(dim // count_ba)) // 2
     dup, ddown, dout = combine(
@@ -1115,10 +1111,20 @@
             shape_of(dim // count_ha, dim // count_ba),
         ],
     )
-    (halves_of,) = combine(place, [[small.views] + packed.gathered], ties=[dup])
+    sent = list(tied([own_small, own_packed], arrived[1:2]))
+    others = [exchange(part, "ha", 1) for part in sent + arrived + crossed]
+    other_of = {id(part): other for part, other in zip(arrived + crossed, others[2:])}
+
+    def from_other(view):
+        return View(other_of[id(view.array)], view.start, view.ways, view.fixed, view.rows)
+
+    own_parts = [small.views] + packed.gathered
+    other_parts = [[flat_view(others[0])] + [from_other(view) for view in small.views[1:]], [flat_view(others[1])]]
+    other_parts += [[from_other(view) for view in views] for views in packed.gathered[1:]]
     din, dkern, dgain_one, dscale_one, dgain_two, dscale_two, dfirst, dsecond, dthird, _ = combine(
         place,
-        [[in_sum.views, [flat_view(halves_of)], [flat_view(exchange(halves_of, "ha", 1))]]],
+        [[in_sum.views] + own_parts + other_parts],
+        ties=[dup],
         epilogue=functools.partial(lay_small, blocks=blocks),
         out_shape=[shape_of(dim // count_ba, weight_in.shape[1] // count_ha), shape_of(*depth_kernel.shape)]
         + [shape_of(1, dim)] * 4

time: 195 us -> 193 us (0.990)
  Pallas kernels: 117 us -> 114 us
  starting transfers between devices: 34.9 us -> 37.6 us
  waiting for transfers between devices: 38.7 us -> 36 us
    ppermute x22 -> x29, starting transfers between devices: 26.2 us -> 29.1 us  [exchange(): lax.ppermute(values, axis, [(i, i ^ bit) for i in range(lax.axis_size(axi...]
    ppermute x22 -> x29, waiting for transfers between devices: 38.7 us -> 36 us  [exchange(): lax.ppermute(values, axis, [(i, i ^ bit) for i in range(lax.axis_size(axi...]
    pallas_call x9 -> x8, Pallas kernels: 29.9 us -> 27.7 us  [combine(): pl.pallas_call(kernel, in_specs=[in_smem()] + [in_hbm()] * (len(arrays) +...]
  transfers between devices with their start and end apart: 26 -> 33, of which waited for: 9 -> 10; matrix products, arithmetic and copies ran while one was open for 0% -> 0% of each run, Pallas kernels for 30% -> 30%
where the time goes in v12:
time: 193 us; the launch traced here: 192 us
  Pallas kernels  114 us (59%)
  starting transfers between devices  37.6 us (19%)
  waiting for transfers between devices  36 us (19%)
  local copies, waits for them, and re-layouts  2.08 us (1%)
    pallas_call x1, Pallas kernels, forward(): pl.pallas_call(functools.partial(forward_kernel, rows=rows, cols=cols, co...  49.7 us
    ppermute x29, waiting for transfers between devices, exchange(): lax.ppermute(values, axis, [(i, i ^ bit) for i in range(lax.axis_size(axi...  36 us
    pallas_call x1, Pallas kernels, backward(): pl.pallas_call(functools.partial(backward_kernel, rows=rows, cols=cols),...  29.3 us
    ppermute x29, starting transfers between devices, exchange(): lax.ppermute(values, axis, [(i, i ^ bit) for i in range(lax.axis_size(axi...  29.1 us
    pallas_call x8, Pallas kernels, combine(): pl.pallas_call(kernel, in_specs=[in_smem()] + [in_hbm()] * (len(arrays) +...  27.7 us
    ppermute x4, starting transfers between devices, neighbour_rows(): return (lax.ppermute(bottom, 'ha', up), lax.ppermute(top, 'ha', down))  8.59 us
    pallas_call x1, Pallas kernels, head(): pl.pallas_call(functools.partial(head_kernel, rows=rows, cols=cols), in_s...  7.67 us
  transfers between devices with their start and end apart: 33, of which 10 were waited for; matrix products, arithmetic and copies ran while one was open for 0% of the time, Pallas kernels for 30%

profile of v12, /device:TPU:0, one launch (start us, length us, event | category | flops | bytes accessed | tf_op | source)
XLA Modules:
  0.0 191.9 jit_solution(14011926735680514650)
XLA Ops:
  0.6 2.1 %fusion = (f32[1,3,64,512]{3,2,1,0:T(8,128)}, f32[1,3,64,512]{3,2,1,0:T(8,128)}) fusion(f32[1,8,64,512]{3,2,1,0:T(8,128)} %param.17), kind=kLoop, calls=%fused_computation.1 | loop fusion | bytes 1572864 | tf_op jit(solution)/shard_map/slice | solution.py:1058
  2.7 3.1 %collective-permute-start = (f32[192,512]{1,0:T(8,128)}, f32[192,512]{1,0:T(8,128)}, u32[]{:S(2)}, u32[]{:S(2)}) collective-permute-start(f32[192,512]{1,0:T(8,128)} %bitcast.5), channel_id=1, source_target_pairs={{0,4},{4,8},{8,12},{12,16},{16,20},{20,24},{24,28},{1,5},{5,9},{9,... | collective-permute-start | bytes 1179656 | tf_op jit(solution)/shard_map/ppermute | solution.py:980
  5.8 1.3 collective-permute-start.1
  7.1 0.6 pad_add_fusion.place_ref
  7.8 7.7 %shard_map.272 = (f32[8,512,128]{2,1,0:T(8,128)}, f32[896,128]{1,0:T(8,128)}, f32[512,128]{1,0:T(8,128)}, f32[512,128]{1,0:T(8,128)}, f32[7,8,8,128]{3,2,1,0:T(8,128)}) custom-call(s32[2]{0:T(128)} %pad_add_fusion.place_ref, s32[64,64]{1,0:T(8,128)} %bitcast.41, s32[1,36]{1,0:T(1,128)} %one_table.1, s32[1,36]{1,0:T(1,128)} %two_table.1, s32[64,64]{1,0:T(8,128)} %bitcast.42, ...), custom_call_target="tpu_custom_call" | custom-call | flops 7699999744 | tf_op jit(solution)/shard_map/pallas_call | solution.py:307
  15.5 49.7 %shard_map.273 = (f32[512,512]{1,0:T(8,128)}, f32[512,512]{1,0:T(8,128)}, f32[8,512,128]{2,1,0:T(8,128)}, f32[8,192,128]{2,1,0:T(8,128)}, f32[8,192,128]{2,1,0:T...) custom-call(s32[2]{0:T(128)} %pad_add_fusion.place_ref, ...), custom_call_target="tpu_custom_call" | custom-call | flops 52800000000 | tf_op jit(solution)/shard_map/pallas_call | solution.py:592
  65.2 2.6 %collective-permute-start.4 = (f32[4,4,384,128]{3,2,1,0:T(8,128)}, f32[4,4,384,128]{3,2,1,0:T(8,128)}, u32[]{:S(2)}, u32[]{:S(2)}) collective-permute-start(f32[4,4,384,128]{3,2,1,0:T(8,128)} %get-tuple-element.79), channel_id=1, source_target_pairs={{0,4},{4,0},{8,12},{12,8},{16,20},{20,16},{24,28},{28,24},{1,5},{5... | collective-permute-start | bytes 9437192 | tf_op jit(solution)/shard_map/ppermute | solution.py:749
  67.9 0.4 collective-permute-start.5
  68.4 2.9 %collective-permute-start.2 = (f32[8,192,128]{2,1,0:T(8,128)}, f32[8,192,128]{2,1,0:T(8,128)}, u32[]{:S(2)}, u32[]{:S(2)}) collective-permute-start(f32[8,192,128]{2,1,0:T(8,128)} %get-tuple-element.74), channel_id=1, source_target_pairs={{0,4},{4,8},{8,12},{12,16},{16,20},{20,24},{24,28},{1,5},{5,9},{9,... | collective-permute-start | bytes 2359304 | tf_op jit(solution)/shard_map/ppermute | solution.py:980
  71.3 1.3 collective-permute-start.3
  72.6 3.7 %collective-permute-done.5.refs_3_.refs_4_ = f32[704,128]{1,0:T(8,128)} collective-permute-done((f32[704,128]{1,0:T(8,128)}, f32[704,128]{1,0:T(8,128)}, u32[]{:S(2)}, u32[]{:S(2)}) %collective-permute-start.5) | collective-permute-done | bytes 360480 | tf_op jit(solution)/shard_map/ppermute | solution.py:749
  76.3 4.5 %shard_map.274 = (f32[1712,128]{1,0:T(8,128)}, f32[1712,128]{1,0:T(8,128)}, f32[1712,128]{1,0:T(8,128)}) custom-call(s32[2]{0:T(128)} %pad_add_fusion.place_ref, f32[6144,128]{1,0:T(8,128)} %bitcast.25, f32[6144,128]{1,0:T(8,128)} %bitcast.13.refs_1_.refs_9_, f32[704,128]{1,0:T(8,128)} %get-tuple-element.80.refs_2_.refs_3_, ...), custom_call_target="tpu_custom_call" | custom-call | flops 3992595200 | tf_op jit(solution)/shard_map/pallas_call | solution.py:857
  80.8 1.6 collective-permute-start.7
  82.3 1.5 collective-permute-start.8
  83.9 0.5 collective-permute-start.9
  84.3 3.0 %shard_map.275.refs_0_ = f32[1536,128]{1,0:T(8,128)} custom-call(s32[2]{0:T(128)} %pad_add_fusion.place_ref, f32[3072,128]{1,0:T(8,128)} %bitcast.29, f32[3072,128]{1,0:T(8,128)} %bitcast.15.refs_1_.refs_8_, f32[1712,128]{1,0:T(8,128)} %get-tuple-element.82.refs_2_.rest_0_, f32[1712,128]{1,0:T(8,128)} %get-tuple-element.83.refs_3_.rest_1_, ...), custom_call_target="tpu_custom_call" | custom-call | flops 1965075200 | tf_op jit(solution)/shard_map/pallas_call | solution.py:857
  87.4 3.1 %collective-permute-start.10 = (f32[1536,128]{1,0:T(8,128)}, f32[1536,128]{1,0:T(8,128)}, u32[]{:S(2)}, u32[]{:S(2)}) collective-permute-start(f32[1536,128]{1,0:T(8,128)} %shard_map.276.rest_3_), channel_id=1, source_target_pairs={{0,16},{4,20},{8,24},{12,28},{16,0},{20,4},{24,8},{28,12},{1,17},{... | collective-permute-start | bytes 2359304 | tf_op jit(solution)/shard_map/ppermute | solution.py:749
  90.5 29.3 %shard_map.277 = (f32[512,512]{1,0:T(8,128)}, f32[4,4,128,128]{3,2,1,0:T(8,128)}, f32[4,4,128,128]{3,2,1,0:T(8,128)}, f32[200,128]{1,0:T(8,128)}, f32[200,128]{1,0:T(8,128)}) custom-call(s32[2]{0:T(128)} %pad_add_fusion.place_ref, s32[64,64]{1,0:T(8,128)} %bitcast.44, s32[64,64]{1,0:T(8,128)} %bitcast.45, ...), custom_call_target="tpu_custom_call" | custom-call | flops 27499999232 | tf_op jit(solution)/shard_map/pallas_call | solution.py:718
  119.8 4.8 %collective-permute-done.10.refs_5_.refs_2_.refs_9_ = f32[1536,128]{1,0:T(8,128)} collective-permute-done((f32[1536,128]{1,0:T(8,128)}, f32[1536,128]{1,0:T(8,128)}, u32[]{:S(2)}, u32[]{:S(2)}) %collective-permute-start.10) | collective-permute-done | bytes 786464 | tf_op jit(solution)/shard_map/ppermute | solution.py:749
  124.8 0.5 collective-permute-start.12
  125.3 3.7 %shard_map.279 = (f32[944,128]{1,0:T(8,128)}, f32[944,128]{1,0:T(8,128)}, f32[176,128]{1,0:T(8,128)}) custom-call(s32[2]{0:T(128)} %pad_add_fusion.place_ref, f32[3072,128]{1,0:T(8,128)} %bitcast.30, f32[3072,128]{1,0:T(8,128)} %bitcast.15.refs_1_.refs_8_, f32[1536,128]{1,0:T(8,128)} %collective-permute-done.10.refs_5_.refs_2_.refs_9_, ...), custom_call_target="tpu_custom_call" | custom-call | flops 2806120448 | tf_op jit(solution)/shard_map/pallas_call | solution.py:857
  129.0 0.8 collective-permute-start.17
  129.7 3.4 %collective-permute-start.16 = (f32[944,128]{1,0:T(8,128)}, f32[944,128]{1,0:T(8,128)}, u32[]{:S(2)}, u32[]{:S(2)}) collective-permute-start(f32[944,128]{1,0:T(8,128)} %get-tuple-element.95.refs_5_.refs_4_), channel_id=1, source_target_pairs={{0,16},{4,20},{8,24},{12,28},{16,0},{20,4},{24,8},{28,12},{1,17},{... | collective-permute-start | bytes 1449992 | tf_op jit(solution)/shard_map/ppermute | solution.py:749
  133.1 3.0 %shard_map.280 = (f32[712,128]{1,0:T(8,128)}, f32[712,128]{1,0:T(8,128)}, f32[712,128]{1,0:T(8,128)}) custom-call(s32[2]{0:T(128)} %pad_add_fusion.place_ref, f32[2048,128]{1,0:T(8,128)} %bitcast.33, f32[2048,128]{1,0:T(8,128)} %bitcast.18.refs_1_.refs_7_, f32[200,128]{1,0:T(8,128)} %get-tuple-element.92.refs_2_, ...), custom_call_target="tpu_custom_call" | custom-call | flops 2152808448 | tf_op jit(solution)/shard_map/pallas_call | solution.py:857
  136.1 1.5 collective-permute-start.13
  137.6 1.5 collective-permute-start.15
  139.1 0.5 collective-permute-start.14
  139.7 12.8 %collective-permute-done.17.refs_1_.refs_12_.refs_3_.refs_10_ = f32[944,128]{1,0:T(8,128)} collective-permute-done((f32[944,128]{1,0:T(8,128)}, f32[944,128]{1,0:T(8,128)}, u32[]{:S(2)}, u32[]{:S(2)}) %collective-permute-start.17) | collective-permute-done | bytes 483360 | tf_op jit(solution)/shard_map/ppermute | solution.py:749
  152.5 1.8 collective-permute-start.18
  154.3 0.7 collective-permute-done.16.refs_5_.refs_13_
  155.0 4.1 %collective-permute-done.18.refs_14_.refs_6_ = f32[176,128]{1,0:T(8,128)} collective-permute-done((f32[176,128]{1,0:T(8,128)}, f32[176,128]{1,0:T(8,128)}, u32[]{:S(2)}, u32[]{:S(2)}) %collective-permute-start.18) | collective-permute-done | bytes 90144 | tf_op jit(solution)/shard_map/ppermute | solution.py:749
  159.2 3.4 %shard_map.282 = (f32[712,128]{1,0:T(8,128)}, f32[328,128]{1,0:T(8,128)}, f32[328,128]{1,0:T(8,128)}, f32[200,128]{1,0:T(8,128)}) custom-call(s32[2]{0:T(128)} %pad_add_fusion.place_ref, f32[6144,128]{1,0:T(8,128)} %bitcast.27, f32[6144,128]{1,0:T(8,128)} %bitcast.13.refs_1_.refs_9_, f32[1712,128]{1,0:T(8,128)} %collective-permute-done.7.refs_2_.refs_5_, ...), custom_call_target="tpu_custom_call" | custom-call | flops 2337538048 | tf_op jit(solution)/shard_map/pallas_call | solution.py:857
  162.7 2.5 %collective-permute-start.20 = (f32[328,128]{1,0:T(8,128)}, f32[328,128]{1,0:T(8,128)}, u32[]{:S(2)}, u32[]{:S(2)}) collective-permute-start(f32[328,128]{1,0:T(8,128)} %get-tuple-element.101.refs_8_), channel_id=1, source_target_pairs={{0,16},{4,20},{8,24},{12,28},{16,0},{20,4},{24,8},{28,12},{1,17},{... | collective-permute-start | bytes 503816 | tf_op jit(solution)/shard_map/ppermute | solution.py:749
  165.1 3.0 %shard_map.284 = (f32[368,128]{1,0:T(8,128)}, f32[368,128]{1,0:T(8,128)}, f32[368,128]{1,0:T(8,128)}, f32[176,128]{1,0:T(8,128)}) custom-call(s32[2]{0:T(128)} %pad_add_fusion.place_ref, f32[3072,128]{1,0:T(8,128)} %bitcast.31, f32[3072,128]{1,0:T(8,128)} %bitcast.15.refs_1_.refs_8_, f32[1536,128]{1,0:T(8,128)} %collective-permute-done.10.refs_5_.refs_2_.refs_9_, ...), custom_call_target="tpu_custom_call" | custom-call | flops 1905000576 | tf_op jit(solution)/shard_map/pallas_call | solution.py:857
  168.2 1.5 collective-permute-start.22
  169.7 1.5 collective-permute-start.24
  171.2 0.5 collective-permute-start.23
  171.7 3.4 %collective-permute-done.19.refs_6_.refs_5_ = f32[712,128]{1,0:T(8,128)} collective-permute-done((f32[712,128]{1,0:T(8,128)}, f32[712,128]{1,0:T(8,128)}, u32[]{:S(2)}, u32[]{:S(2)}) %collective-permute-start.19) | collective-permute-done | bytes 364576 | tf_op jit(solution)/shard_map/ppermute | solution.py:749
  175.2 1.9 collective-permute-start.21
  177.0 0.2 collective-permute-start.27
  177.2 0.6 collective-permute-done.24.refs_13_.refs_12_
  177.8 1.3 collective-permute-done.23.refs_12_.refs_11_
  179.2 1.6 collective-permute-done.29.refs_17_
  180.9 0.4 collective-permute-start.32
  181.3 2.8 %collective-permute-done.21.refs_7_ = f32[328,128]{1,0:T(8,128)} collective-permute-done((f32[328,128]{1,0:T(8,128)}, f32[328,128]{1,0:T(8,128)}, u32[]{:S(2)}, u32[]{:S(2)}) %collective-permute-start.21) | collective-permute-done | bytes 167968 | tf_op jit(solution)/shard_map/ppermute | solution.py:749
  184.1 0.5 collective-permute-start.28
  184.6 3.2 %shard_map.286 = (f32[128,256]{1,0:T(8,128)}, f32[64,512]{1,0:T(8,128)}, f32[64,128]{1,0:T(8,128)}) custom-call(s32[2]{0:T(128)} %pad_add_fusion.place_ref, f32[6144,128]{1,0:T(8,128)} %bitcast.28, f32[6144,128]{1,0:T(8,128)} %bitcast.13.refs_1_.refs_9_, f32[1712,128]{1,0:T(8,128)} %collective-permute-done.7.refs_2_.refs_5_, ...), custom_call_target="tpu_custom_call" | custom-call | flops 1965075200 | tf_op jit(solution)/shard_map/pallas_call | solution.py:857
  187.9 3.8 %shard_map.287 = (f32[128,128]{1,0:T(8,128)}, f32[49,960]{1,0:T(8,128)}, f32[1,512]{1,0:T(1,128)}, f32[1,512]{1,0:T(1,128)}, f32[1,512]{1,0:T(1,128)}, /*index=5...) custom-call(s32[2]{0:T(128)} %pad_add_fusion.place_ref, ...), custom_call_target="tpu_custom_call" | custom-call | flops 2220392448 | tf_op jit(solution)/shard_map/pallas_call | solution.py:857
  (36 shorter events, 0.5 us)
Async XLA Ops:
  2.7 12.7 %collective-permute-start = (f32[192,512]{1,0:T(8,128)}, f32[192,512]{1,0:T(8,128)}, u32[]{:S(2)}, u32[]{:S(2)}) collective-permute-start(f32[192,512]{1,0:T(8,128)} %bitcast.5), channel_id=1, source_target_pairs={{0,4},{4,8},{8,12},{12,16},{16,20},{20,24},{24,28},{1,5},{5,9},{9,... | collective-permute-start | bytes 1179656 | tf_op jit(solution)/shard_map/ppermute | solution.py:980
  5.8 9.6 %collective-permute-start.1 = (f32[192,512]{1,0:T(8,128)}, f32[192,512]{1,0:T(8,128)}, u32[]{:S(2)}, u32[]{:S(2)}) collective-permute-start(f32[192,512]{1,0:T(8,128)} %bitcast.6), channel_id=1, source_target_pairs={{4,0},{8,4},{12,8},{16,12},{20,16},{24,20},{28,24},{5,1},{9,5},{13... | collective-permute-start | bytes 1179656 | tf_op jit(solution)/shard_map/ppermute | solution.py:980
  65.2 11.0 %collective-permute-start.4 = (f32[4,4,384,128]{3,2,1,0:T(8,128)}, f32[4,4,384,128]{3,2,1,0:T(8,128)}, u32[]{:S(2)}, u32[]{:S(2)}) collective-permute-start(f32[4,4,384,128]{3,2,1,0:T(8,128)} %get-tuple-element.79), channel_id=1, source_target_pairs={{0,4},{4,0},{8,12},{12,8},{16,20},{20,16},{24,28},{28,24},{1,5},{5... | collective-permute-start | bytes 9437192 | tf_op jit(solution)/shard_map/ppermute | solution.py:749
  67.9 16.0 %collective-permute-start.6 = (f32[4,4,192,128]{3,2,1,0:T(8,128)}, f32[4,4,192,128]{3,2,1,0:T(8,128)}, u32[]{:S(2)}, u32[]{:S(2)}) collective-permute-start(f32[4,4,192,128]{3,2,1,0:T(8,128)} %get-tuple-element.86), channel_id=1, source_target_pairs={{0,4},{4,0},{8,12},{12,8},{16,20},{20,16},{24,28},{28,24},{1,5},{5... | collective-permute-start | bytes 4718600 | tf_op jit(solution)/shard_map/ppermute | solution.py:749
  67.9 8.3 %collective-permute-start.5 = (f32[704,128]{1,0:T(8,128)}, f32[704,128]{1,0:T(8,128)}, u32[]{:S(2)}, u32[]{:S(2)}) collective-permute-start(f32[704,128]{1,0:T(8,128)} %get-tuple-element.81), channel_id=1, source_target_pairs={{0,4},{4,0},{8,12},{12,8},{16,20},{20,16},{24,28},{28,24},{1,5},{5... | collective-permute-start | bytes 1081352 | tf_op jit(solution)/shard_map/ppermute | solution.py:749
  68.4 19.0 %collective-permute-start.2 = (f32[8,192,128]{2,1,0:T(8,128)}, f32[8,192,128]{2,1,0:T(8,128)}, u32[]{:S(2)}, u32[]{:S(2)}) collective-permute-start(f32[8,192,128]{2,1,0:T(8,128)} %get-tuple-element.74), channel_id=1, source_target_pairs={{0,4},{4,8},{8,12},{12,16},{16,20},{20,24},{24,28},{1,5},{5,9},{9,... | collective-permute-start | bytes 2359304 | tf_op jit(solution)/shard_map/ppermute | solution.py:980
  71.3 16.1 %collective-permute-start.3 = (f32[8,192,128]{2,1,0:T(8,128)}, f32[8,192,128]{2,1,0:T(8,128)}, u32[]{:S(2)}, u32[]{:S(2)}) collective-permute-start(f32[8,192,128]{2,1,0:T(8,128)} %get-tuple-element.76), channel_id=1, source_target_pairs={{4,0},{8,4},{12,8},{16,12},{20,16},{24,20},{28,24},{5,1},{9,5},{13... | collective-permute-start | bytes 2359304 | tf_op jit(solution)/shard_map/ppermute | solution.py:980
  80.8 43.9 %collective-permute-start.7 = (f32[1712,128]{1,0:T(8,128)}, f32[1712,128]{1,0:T(8,128)}, u32[]{:S(2)}, u32[]{:S(2)}) collective-permute-start(f32[1712,128]{1,0:T(8,128)} %get-tuple-element.82.refs_2_.rest_0_), channel_id=1, source_target_pairs={{0,1},{1,0},{2,3},{3,2},{4,5},{5,4},{6,7},{7,6},{8,9},{9,8},{10,11... | collective-permute-start | bytes 2629640 | tf_op jit(solution)/shard_map/ppermute | solution.py:749
  82.3 42.3 %collective-permute-start.8 = (f32[1712,128]{1,0:T(8,128)}, f32[1712,128]{1,0:T(8,128)}, u32[]{:S(2)}, u32[]{:S(2)}) collective-permute-start(f32[1712,128]{1,0:T(8,128)} %get-tuple-element.83.refs_3_.rest_1_), channel_id=1, source_target_pairs={{0,2},{1,3},{2,0},{3,1},{4,6},{5,7},{6,4},{7,5},{8,10},{9,11},{10,... | collective-permute-start | bytes 2629640 | tf_op jit(solution)/shard_map/ppermute | solution.py:749
  83.9 40.8 %collective-permute-start.9 = (f32[1712,128]{1,0:T(8,128)}, f32[1712,128]{1,0:T(8,128)}, u32[]{:S(2)}, u32[]{:S(2)}) collective-permute-start(f32[1712,128]{1,0:T(8,128)} %get-tuple-element.84.refs_4_.rest_2_), channel_id=1, source_target_pairs={{0,3},{1,2},{2,1},{3,0},{4,7},{5,6},{6,5},{7,4},{8,11},{9,10},{10,... | collective-permute-start | bytes 2629640 | tf_op jit(solution)/shard_map/ppermute | solution.py:749
  87.4 37.2 %collective-permute-start.10 = (f32[1536,128]{1,0:T(8,128)}, f32[1536,128]{1,0:T(8,128)}, u32[]{:S(2)}, u32[]{:S(2)}) collective-permute-start(f32[1536,128]{1,0:T(8,128)} %shard_map.276.rest_3_), channel_id=1, source_target_pairs={{0,16},{4,20},{8,24},{12,28},{16,0},{20,4},{24,8},{28,12},{1,17},{... | collective-permute-start | bytes 2359304 | tf_op jit(solution)/shard_map/ppermute | solution.py:749
  124.7 8.4 %collective-permute-start.11 = (f32[4,4,128,128]{3,2,1,0:T(8,128)}, f32[4,4,128,128]{3,2,1,0:T(8,128)}, u32[]{:S(2)}, u32[]{:S(2)}) collective-permute-start(f32[4,4,128,128]{3,2,1,0:T(8,128)} %get-tuple-element.91), channel_id=1, source_target_pairs={{0,4},{4,0},{8,12},{12,8},{16,20},{20,16},{24,28},{28,24},{1,5},{5... | collective-permute-start | bytes 3145736 | tf_op jit(solution)/shard_map/ppermute | solution.py:749
  124.8 8.4 %collective-permute-start.12 = (f32[200,128]{1,0:T(8,128)}, f32[200,128]{1,0:T(8,128)}, u32[]{:S(2)}, u32[]{:S(2)}) collective-permute-start(f32[200,128]{1,0:T(8,128)} %get-tuple-element.93), channel_id=1, source_target_pairs={{0,4},{4,0},{8,12},{12,8},{16,20},{20,16},{24,28},{28,24},{1,5},{5... | collective-permute-start | bytes 307208 | tf_op jit(solution)/shard_map/ppermute | solution.py:749
  129.0 23.5 %collective-permute-start.17 = (f32[944,128]{1,0:T(8,128)}, f32[944,128]{1,0:T(8,128)}, u32[]{:S(2)}, u32[]{:S(2)}) collective-permute-start(f32[944,128]{1,0:T(8,128)} %get-tuple-element.94.refs_4_), channel_id=1, source_target_pairs={{0,8},{4,12},{8,0},{12,4},{16,24},{20,28},{24,16},{28,20},{1,9},{5... | collective-permute-start | bytes 1449992 | tf_op jit(solution)/shard_map/ppermute | solution.py:749
  129.7 25.3 %collective-permute-start.16 = (f32[944,128]{1,0:T(8,128)}, f32[944,128]{1,0:T(8,128)}, u32[]{:S(2)}, u32[]{:S(2)}) collective-permute-start(f32[944,128]{1,0:T(8,128)} %get-tuple-element.95.refs_5_.refs_4_), channel_id=1, source_target_pairs={{0,16},{4,20},{8,24},{12,28},{16,0},{20,4},{24,8},{28,12},{1,17},{... | collective-permute-start | bytes 1449992 | tf_op jit(solution)/shard_map/ppermute | solution.py:749
  136.1 23.1 %collective-permute-start.13 = (f32[712,128]{1,0:T(8,128)}, f32[712,128]{1,0:T(8,128)}, u32[]{:S(2)}, u32[]{:S(2)}) collective-permute-start(f32[712,128]{1,0:T(8,128)} %get-tuple-element.97), channel_id=1, source_target_pairs={{0,1},{1,0},{2,3},{3,2},{4,5},{5,4},{6,7},{7,6},{8,9},{9,8},{10,11... | collective-permute-start | bytes 1093640 | tf_op jit(solution)/shard_map/ppermute | solution.py:749
  137.6 21.5 %collective-permute-start.15 = (f32[712,128]{1,0:T(8,128)}, f32[712,128]{1,0:T(8,128)}, u32[]{:S(2)}, u32[]{:S(2)}) collective-permute-start(f32[712,128]{1,0:T(8,128)} %get-tuple-element.99), channel_id=1, source_target_pairs={{0,3},{1,2},{2,1},{3,0},{4,7},{5,6},{6,5},{7,4},{8,11},{9,10},{10,... | collective-permute-start | bytes 1093640 | tf_op jit(solution)/shard_map/ppermute | solution.py:749
  139.1 20.0 %collective-permute-start.14 = (f32[712,128]{1,0:T(8,128)}, f32[712,128]{1,0:T(8,128)}, u32[]{:S(2)}, u32[]{:S(2)}) collective-permute-start(f32[712,128]{1,0:T(8,128)} %get-tuple-element.98.refs_11_), channel_id=1, source_target_pairs={{0,2},{1,3},{2,0},{3,1},{4,6},{5,7},{6,4},{7,5},{8,10},{9,11},{10,... | collective-permute-start | bytes 1093640 | tf_op jit(solution)/shard_map/ppermute | solution.py:749
  152.5 6.6 %collective-permute-start.18 = (f32[176,128]{1,0:T(8,128)}, f32[176,128]{1,0:T(8,128)}, u32[]{:S(2)}, u32[]{:S(2)}) collective-permute-start(f32[176,128]{1,0:T(8,128)} %shard_map.281), channel_id=1, source_target_pairs={{0,24},{4,28},{8,16},{12,20},{16,8},{20,12},{24,0},{28,4},{1,25},{... | collective-permute-start | bytes 270344 | tf_op jit(solution)/shard_map/ppermute | solution.py:749
  162.6 12.6 %collective-permute-start.19 = (f32[712,128]{1,0:T(8,128)}, f32[712,128]{1,0:T(8,128)}, u32[]{:S(2)}, u32[]{:S(2)}) collective-permute-start(f32[712,128]{1,0:T(8,128)} %get-tuple-element.100.refs_7_), channel_id=1, source_target_pairs={{0,8},{4,12},{8,0},{12,4},{16,24},{20,28},{24,16},{28,20},{1,9},{5... | collective-permute-start | bytes 1093640 | tf_op jit(solution)/shard_map/ppermute | solution.py:749
  162.7 12.5 %collective-permute-start.20 = (f32[328,128]{1,0:T(8,128)}, f32[328,128]{1,0:T(8,128)}, u32[]{:S(2)}, u32[]{:S(2)}) collective-permute-start(f32[328,128]{1,0:T(8,128)} %get-tuple-element.101.refs_8_), channel_id=1, source_target_pairs={{0,16},{4,20},{8,24},{12,28},{16,0},{20,4},{24,8},{28,12},{1,17},{... | collective-permute-start | bytes 503816 | tf_op jit(solution)/shard_map/ppermute | solution.py:749
  168.2 8.9 %collective-permute-start.22 = (f32[368,128]{1,0:T(8,128)}, f32[368,128]{1,0:T(8,128)}, u32[]{:S(2)}, u32[]{:S(2)}) collective-permute-start(f32[368,128]{1,0:T(8,128)} %get-tuple-element.104), channel_id=1, source_target_pairs={{0,1},{1,0},{2,3},{3,2},{4,5},{5,4},{6,7},{7,6},{8,9},{9,8},{10,11... | collective-permute-start | bytes 565256 | tf_op jit(solution)/shard_map/ppermute | solution.py:749
  169.7 8.1 %collective-permute-start.24 = (f32[368,128]{1,0:T(8,128)}, f32[368,128]{1,0:T(8,128)}, u32[]{:S(2)}, u32[]{:S(2)}) collective-permute-start(f32[368,128]{1,0:T(8,128)} %get-tuple-element.105), channel_id=1, source_target_pairs={{0,3},{1,2},{2,1},{3,0},{4,7},{5,6},{6,5},{7,4},{8,11},{9,10},{10,... | collective-permute-start | bytes 565256 | tf_op jit(solution)/shard_map/ppermute | solution.py:749
  171.2 8.0 %collective-permute-start.23 = (f32[368,128]{1,0:T(8,128)}, f32[368,128]{1,0:T(8,128)}, u32[]{:S(2)}, u32[]{:S(2)}) collective-permute-start(f32[368,128]{1,0:T(8,128)} %get-tuple-element.103.refs_9_), channel_id=1, source_target_pairs={{0,2},{1,3},{2,0},{3,1},{4,6},{5,7},{6,4},{7,5},{8,10},{9,11},{10,... | collective-permute-start | bytes 565256 | tf_op jit(solution)/shard_map/ppermute | solution.py:749
  175.2 12.7 %collective-permute-start.26 = (f32[712,128]{1,0:T(8,128)}, f32[712,128]{1,0:T(8,128)}, u32[]{:S(2)}, u32[]{:S(2)}) collective-permute-start(f32[712,128]{1,0:T(8,128)} %collective-permute-done.19.refs_6_.refs_5_), channel_id=1, source_target_pairs={{0,4},{4,0},{8,12},{12,8},{16,20},{20,16},{24,28},{28,24},{1,5},{5... | collective-permute-start | bytes 1093640 | tf_op jit(solution)/shard_map/ppermute | solution.py:749
  175.2 8.9 %collective-permute-start.21 = (f32[328,128]{1,0:T(8,128)}, f32[328,128]{1,0:T(8,128)}, u32[]{:S(2)}, u32[]{:S(2)}) collective-permute-start(f32[328,128]{1,0:T(8,128)} %shard_map.283), channel_id=1, source_target_pairs={{0,24},{4,28},{8,16},{12,20},{16,8},{20,12},{24,0},{28,4},{1,25},{... | collective-permute-start | bytes 503816 | tf_op jit(solution)/shard_map/ppermute | solution.py:749
  177.0 7.0 %collective-permute-start.27 = (f32[328,128]{1,0:T(8,128)}, f32[328,128]{1,0:T(8,128)}, u32[]{:S(2)}, u32[]{:S(2)}) collective-permute-start(f32[328,128]{1,0:T(8,128)} %collective-permute-done.20.refs_1_.refs_2_.refs_6_), channel_id=1, source_target_pairs={{0,4},{4,0},{8,12},{12,8},{16,20},{20,16},{24,28},{28,24},{1,5},{5... | collective-permute-start | bytes 503816 | tf_op jit(solution)/shard_map/ppermute | solution.py:749
  177.8 3.1 %collective-permute-start.25 = (f32[200,128]{1,0:T(8,128)}, f32[200,128]{1,0:T(8,128)}, u32[]{:S(2)}, u32[]{:S(2)}) collective-permute-start(f32[200,128]{1,0:T(8,128)} %get-tuple-element.108), channel_id=1, source_target_pairs={{0,4},{4,0},{8,12},{12,8},{16,20},{20,16},{24,28},{28,24},{1,5},{5... | collective-permute-start | bytes 307208 | tf_op jit(solution)/shard_map/ppermute | solution.py:749
  179.2 1.6 collective-permute-start.29
  180.8 7.1 %collective-permute-start.30 = (f32[368,128]{1,0:T(8,128)}, f32[368,128]{1,0:T(8,128)}, u32[]{:S(2)}, u32[]{:S(2)}) collective-permute-start(f32[368,128]{1,0:T(8,128)} %collective-permute-done.22.refs_11_.refs_10_), channel_id=1, source_target_pairs={{0,4},{4,0},{8,12},{12,8},{16,20},{20,16},{24,28},{28,24},{1,5},{5... | collective-permute-start | bytes 565256 | tf_op jit(solution)/shard_map/ppermute | solution.py:749
  180.9 6.9 %collective-permute-start.32 = (f32[368,128]{1,0:T(8,128)}, f32[368,128]{1,0:T(8,128)}, u32[]{:S(2)}, u32[]{:S(2)}) collective-permute-start(f32[368,128]{1,0:T(8,128)} %collective-permute-done.24.refs_13_.refs_12_), channel_id=1, source_target_pairs={{0,4},{4,0},{8,12},{12,8},{16,20},{20,16},{24,28},{28,24},{1,5},{5... | collective-permute-start | bytes 565256 | tf_op jit(solution)/shard_map/ppermute | solution.py:749
  184.1 3.8 %collective-permute-start.31 = (f32[368,128]{1,0:T(8,128)}, f32[368,128]{1,0:T(8,128)}, u32[]{:S(2)}, u32[]{:S(2)}) collective-permute-start(f32[368,128]{1,0:T(8,128)} %collective-permute-done.23.refs_12_.refs_11_), channel_id=1, source_target_pairs={{0,4},{4,0},{8,12},{12,8},{16,20},{20,16},{24,28},{28,24},{1,5},{5... | collective-permute-start | bytes 565256 | tf_op jit(solution)/shard_map/ppermute | solution.py:749
  184.1 3.8 %collective-permute-start.28 = (f32[328,128]{1,0:T(8,128)}, f32[328,128]{1,0:T(8,128)}, u32[]{:S(2)}, u32[]{:S(2)}) collective-permute-start(f32[328,128]{1,0:T(8,128)} %collective-permute-done.21.refs_7_), channel_id=1, source_target_pairs={{0,4},{4,0},{8,12},{12,8},{16,20},{20,16},{24,28},{28,24},{1,5},{5... | collective-permute-start | bytes 503816 | tf_op jit(solution)/shard_map/ppermute | solution.py:749

commit v13 on v12

--- a/solution.py
+++ b/solution.py
@@ -964,12 +964,10 @@
         return arrived
 
 
-def run(place, stage, ties=(), in_turn=None, late_ties=(), extra=()):
+def run(place, stage, ties=(), in_turn=None, extra=()):
     groups = stage.groups()
     made = list(combine(place, groups + list(extra), ties))
     made, more = made[: len(groups)], made[len(groups) :]
-    if late_ties:
-        made = list(tied(made, late_ties))
     return made, stage.go(made, in_turn), more
 
 
@@ -1070,9 +1068,12 @@
     plane_sum = Sum([plane_kept, exchange(plane_sent, "ha", 1)], ["plane", "far", "near"])
     line_sum = Sum([line_kept, exchange(line_sent, "ha", 1)], ["far", "near", "plane"])
     packed = Sum([packed_kept, exchange(packed_sent, "ha", 1)], ["plane"])
-    made, arrived, _ = run(place, Stage([(plane_sum, "plane"), (packed, "plane")], "plane"))
-    more, far, _ = run(place, Stage([(line_sum, "far")], "far"), ties=made, late_ties=[above, below])
-    made, arrived = made + more, arrived + far
+    across = Stage([(plane_sum, "plane"), (packed, "plane")], "plane")
+    apart = Stage([(line_sum, "far")], "far")
+    made = list(combine(place, across.groups() + apart.groups()))
+    arrived = across.go(made[: len(across.steps)])
+    made[len(across.steps) :] = tied(made[len(across.steps) :], [above, below])
+    arrived += apart.go(made[len(across.steps) :])
     dcanvas, in_kept, in_sent, small_kept, small_sent = backward(
         place, ids, above, dconv, below, joined, depth_kernel, own, gain, dmiddle, weight_in, made,
         rows, cols, count_ha, count_ba,
@@ -1087,7 +1088,7 @@
     )
     run(place, Stage([(in_sum, "plane"), (small, "plane")], "plane"), ties=made)
     along = Stage([(plane_sum, "near"), (in_sum, "line"), (small, "line")], "line")
-    made, arrived, (own_small,) = run(place, along, ties=arrived, in_turn=1, extra=[[small.views]])
+    made, arrived, (own_small,) = run(place, along, ties=arrived[:2], in_turn=1, extra=[[small.views]])
     packed = Gather(packed.views)
     across = Stage([(line_sum, "plane"), (packed, "plane")], "plane")
     _, crossed, (own_packed,) = run(place, across, ties=made, extra=[[packed.views]])

time: 193 us -> 193 us (level)
  waiting for transfers between devices: 36 us -> 38.5 us
  Pallas kernels: 114 us -> 112 us
    ppermute x29, waiting for transfers between devices: 36 us -> 38.5 us  [exchange(): lax.ppermute(values, axis, [(i, i ^ bit) for i in range(lax.axis_size(axi...]
    pallas_call x8 -> x7, Pallas kernels: 27.7 us -> 25.5 us  [combine(): pl.pallas_call(kernel, in_specs=[in_smem()] + [in_hbm()] * (len(arrays) +...]
  transfers between devices with their start and end apart: 33 -> 33, of which waited for: 10 -> 10; matrix products, arithmetic and copies ran while one was open for 0% -> 0% of each run, Pallas kernels for 30% -> 31%
where the time goes in v13:
time: 193 us; the launch traced here: 192 us
  Pallas kernels  112 us (58%)
  waiting for transfers between devices  38.5 us (20%)
  starting transfers between devices  37.4 us (19%)
  local copies, waits for them, and re-layouts  2.08 us (1%)
    pallas_call x1, Pallas kernels, forward(): pl.pallas_call(functools.partial(forward_kernel, rows=rows, cols=cols, co...  49.7 us
    ppermute x29, waiting for transfers between devices, exchange(): lax.ppermute(values, axis, [(i, i ^ bit) for i in range(lax.axis_size(axi...  38.5 us
    pallas_call x1, Pallas kernels, backward(): pl.pallas_call(functools.partial(backward_kernel, rows=rows, cols=cols),...  29.3 us
    ppermute x29, starting transfers between devices, exchange(): lax.ppermute(values, axis, [(i, i ^ bit) for i in range(lax.axis_size(axi...  28.9 us
    pallas_call x7, Pallas kernels, combine(): pl.pallas_call(kernel, in_specs=[in_smem()] + [in_hbm()] * (len(arrays) +...  25.5 us
    ppermute x4, starting transfers between devices, neighbour_rows(): return (lax.ppermute(bottom, 'ha', up), lax.ppermute(top, 'ha', down))  8.51 us
    pallas_call x1, Pallas kernels, head(): pl.pallas_call(functools.partial(head_kernel, rows=rows, cols=cols), in_s...  7.67 us
  transfers between devices with their start and end apart: 33, of which 10 were waited for; matrix products, arithmetic and copies ran while one was open for 0% of the time, Pallas kernels for 31%

profile of v13, /device:TPU:0, one launch (start us, length us, event | category | flops | bytes accessed | tf_op | source)
XLA Modules:
  0.0 192.0 jit_solution(7413261947193885096)
XLA Ops:
  0.6 2.1 %fusion = (f32[1,3,64,512]{3,2,1,0:T(8,128)}, f32[1,3,64,512]{3,2,1,0:T(8,128)}) fusion(f32[1,8,64,512]{3,2,1,0:T(8,128)} %param.17), kind=kLoop, calls=%fused_computation.1 | loop fusion | bytes 1572864 | tf_op jit(solution)/shard_map/slice | solution.py:1056
  2.7 3.1 %collective-permute-start = (f32[192,512]{1,0:T(8,128)}, f32[192,512]{1,0:T(8,128)}, u32[]{:S(2)}, u32[]{:S(2)}) collective-permute-start(f32[192,512]{1,0:T(8,128)} %bitcast.5), channel_id=1, source_target_pairs={{0,4},{4,8},{8,12},{12,16},{16,20},{20,24},{24,28},{1,5},{5,9},{9,... | collective-permute-start | bytes 1179656 | tf_op jit(solution)/shard_map/ppermute | solution.py:978
  5.8 1.3 collective-permute-start.1
  7.1 0.6 pad_add_fusion.place_ref
  7.8 7.7 %shard_map.272 = (f32[8,512,128]{2,1,0:T(8,128)}, f32[896,128]{1,0:T(8,128)}, f32[512,128]{1,0:T(8,128)}, f32[512,128]{1,0:T(8,128)}, f32[7,8,8,128]{3,2,1,0:T(8,128)}) custom-call(s32[2]{0:T(128)} %pad_add_fusion.place_ref, s32[64,64]{1,0:T(8,128)} %bitcast.41, s32[1,36]{1,0:T(1,128)} %one_table.1, s32[1,36]{1,0:T(1,128)} %two_table.1, s32[64,64]{1,0:T(8,128)} %bitcast.42, ...), custom_call_target="tpu_custom_call" | custom-call | flops 7699999744 | tf_op jit(solution)/shard_map/pallas_call | solution.py:307
  15.5 49.7 %shard_map.273 = (f32[512,512]{1,0:T(8,128)}, f32[512,512]{1,0:T(8,128)}, f32[8,512,128]{2,1,0:T(8,128)}, f32[8,192,128]{2,1,0:T(8,128)}, f32[8,192,128]{2,1,0:T...) custom-call(s32[2]{0:T(128)} %pad_add_fusion.place_ref, ...), custom_call_target="tpu_custom_call" | custom-call | flops 52800000000 | tf_op jit(solution)/shard_map/pallas_call | solution.py:592
  65.2 2.7 %collective-permute-start.4 = (f32[4,4,384,128]{3,2,1,0:T(8,128)}, f32[4,4,384,128]{3,2,1,0:T(8,128)}, u32[]{:S(2)}, u32[]{:S(2)}) collective-permute-start(f32[4,4,384,128]{3,2,1,0:T(8,128)} %get-tuple-element.80), channel_id=1, source_target_pairs={{0,4},{4,0},{8,12},{12,8},{16,20},{20,16},{24,28},{28,24},{1,5},{5... | collective-permute-start | bytes 9437192 | tf_op jit(solution)/shard_map/ppermute | solution.py:749
  67.9 0.4 collective-permute-start.5
  68.4 2.8 %collective-permute-start.2 = (f32[8,192,128]{2,1,0:T(8,128)}, f32[8,192,128]{2,1,0:T(8,128)}, u32[]{:S(2)}, u32[]{:S(2)}) collective-permute-start(f32[8,192,128]{2,1,0:T(8,128)} %get-tuple-element.75), channel_id=1, source_target_pairs={{0,4},{4,8},{8,12},{12,16},{16,20},{20,24},{24,28},{1,5},{5,9},{9,... | collective-permute-start | bytes 2359304 | tf_op jit(solution)/shard_map/ppermute | solution.py:978
  71.2 1.3 collective-permute-start.3
  72.5 3.7 %collective-permute-done.5.refs_3_.refs_4_ = f32[704,128]{1,0:T(8,128)} collective-permute-done((f32[704,128]{1,0:T(8,128)}, f32[704,128]{1,0:T(8,128)}, u32[]{:S(2)}, u32[]{:S(2)}) %collective-permute-start.5) | collective-permute-done | bytes 360480 | tf_op jit(solution)/shard_map/ppermute | solution.py:749
  76.3 5.4 %shard_map.274 = (f32[1712,128]{1,0:T(8,128)}, f32[1712,128]{1,0:T(8,128)}, f32[1712,128]{1,0:T(8,128)}, f32[1536,128]{1,0:T(8,128)}) custom-call(s32[2]{0:T(128)} %pad_add_fusion.place_ref, f32[6144,128]{1,0:T(8,128)} %bitcast.25, f32[6144,128]{1,0:T(8,128)} %bitcast.13.refs_1_.refs_9_, f32[704,128]{1,0:T(8,128)} %get-tuple-element.81.refs_2_.refs_3_, ...), custom_call_target="tpu_custom_call" | custom-call | flops 4857670656 | tf_op jit(solution)/shard_map/pallas_call | solution.py:857
  81.7 4.8 %collective-permute-start.10 = (f32[1536,128]{1,0:T(8,128)}, f32[1536,128]{1,0:T(8,128)}, u32[]{:S(2)}, u32[]{:S(2)}) collective-permute-start(f32[1536,128]{1,0:T(8,128)} %shard_map.275.rest_3_), channel_id=1, source_target_pairs={{0,16},{4,20},{8,24},{12,28},{16,0},{20,4},{24,8},{28,12},{1,17},{... | collective-permute-start | bytes 2359304 | tf_op jit(solution)/shard_map/ppermute | solution.py:749
  86.5 1.5 collective-permute-start.7
  87.9 1.5 collective-permute-start.8
  89.5 0.5 collective-permute-start.9
  90.0 29.3 %shard_map.276 = (f32[512,512]{1,0:T(8,128)}, f32[4,4,128,128]{3,2,1,0:T(8,128)}, f32[4,4,128,128]{3,2,1,0:T(8,128)}, f32[200,128]{1,0:T(8,128)}, f32[200,128]{1,0:T(8,128)}) custom-call(s32[2]{0:T(128)} %pad_add_fusion.place_ref, s32[64,64]{1,0:T(8,128)} %bitcast.44, s32[64,64]{1,0:T(8,128)} %bitcast.45, ...), custom_call_target="tpu_custom_call" | custom-call | flops 27499999232 | tf_op jit(solution)/shard_map/pallas_call | solution.py:718
  119.3 1.5 collective-permute-done.10.refs_5_.refs_2_.refs_9_
  120.8 8.3 %collective-permute-done.8.refs_3_.refs_6_ = f32[1712,128]{1,0:T(8,128)} collective-permute-done((f32[1712,128]{1,0:T(8,128)}, f32[1712,128]{1,0:T(8,128)}, u32[]{:S(2)}, u32[]{:S(2)}) %collective-permute-start.8) | collective-permute-done | bytes 876576 | tf_op jit(solution)/shard_map/ppermute | solution.py:749
  129.2 0.4 collective-permute-start.12
  129.6 3.7 %shard_map.278 = (f32[944,128]{1,0:T(8,128)}, f32[944,128]{1,0:T(8,128)}, f32[176,128]{1,0:T(8,128)}) custom-call(s32[2]{0:T(128)} %pad_add_fusion.place_ref, f32[3072,128]{1,0:T(8,128)} %bitcast.30, f32[3072,128]{1,0:T(8,128)} %bitcast.15.refs_5_.refs_1_.refs_8_, f32[1536,128]{1,0:T(8,128)} %collective-permute-done.10.refs_5_.refs_2_.refs_9_, ...), custom_call_target="tpu_custom_call" | custom-call | flops 2806120448 | tf_op jit(solution)/shard_map/pallas_call | solution.py:857
  133.3 1.9 collective-permute-start.16
  135.2 3.0 %shard_map.279 = (f32[712,128]{1,0:T(8,128)}, f32[712,128]{1,0:T(8,128)}, f32[712,128]{1,0:T(8,128)}) custom-call(s32[2]{0:T(128)} %pad_add_fusion.place_ref, f32[2048,128]{1,0:T(8,128)} %bitcast.33, f32[2048,128]{1,0:T(8,128)} %bitcast.18.refs_1_.refs_7_, f32[200,128]{1,0:T(8,128)} %get-tuple-element.94.refs_2_, ...), custom_call_target="tpu_custom_call" | custom-call | flops 2152808448 | tf_op jit(solution)/shard_map/pallas_call | solution.py:857
  138.2 0.8 collective-permute-start.13
  139.0 2.2 %collective-permute-start.15 = (f32[712,128]{1,0:T(8,128)}, f32[712,128]{1,0:T(8,128)}, u32[]{:S(2)}, u32[]{:S(2)}) collective-permute-start(f32[712,128]{1,0:T(8,128)} %get-tuple-element.101), channel_id=1, source_target_pairs={{0,3},{1,2},{2,1},{3,0},{4,7},{5,6},{6,5},{7,4},{8,11},{9,10},{10,... | collective-permute-start | bytes 1093640 | tf_op jit(solution)/shard_map/ppermute | solution.py:749
  141.3 0.5 collective-permute-start.14
  141.8 14.0 %collective-permute-done.17.refs_12_.refs_1_.refs_3_.refs_10_ = f32[944,128]{1,0:T(8,128)} collective-permute-done((f32[944,128]{1,0:T(8,128)}, f32[944,128]{1,0:T(8,128)}, u32[]{:S(2)}, u32[]{:S(2)}) %collective-permute-start.17) | collective-permute-done | bytes 483360 | tf_op jit(solution)/shard_map/ppermute | solution.py:749
  155.8 2.4 %collective-permute-start.21 = (f32[176,128]{1,0:T(8,128)}, f32[176,128]{1,0:T(8,128)}, u32[]{:S(2)}, u32[]{:S(2)}) collective-permute-start(f32[176,128]{1,0:T(8,128)} %shard_map.282), channel_id=1, source_target_pairs={{0,24},{4,28},{8,16},{12,20},{16,8},{20,12},{24,0},{28,4},{1,25},{... | collective-permute-start | bytes 270344 | tf_op jit(solution)/shard_map/ppermute | solution.py:749
  158.2 0.7 collective-permute-done.16.refs_5_.refs_13_
  158.9 3.4 %shard_map.280 = (f32[712,128]{1,0:T(8,128)}, f32[328,128]{1,0:T(8,128)}, f32[328,128]{1,0:T(8,128)}, f32[200,128]{1,0:T(8,128)}) custom-call(s32[2]{0:T(128)} %pad_add_fusion.place_ref, f32[6144,128]{1,0:T(8,128)} %bitcast.27, f32[6144,128]{1,0:T(8,128)} %bitcast.13.refs_1_.refs_9_, f32[1712,128]{1,0:T(8,128)} %collective-permute-done.7.refs_2_.refs_5_, ...), custom_call_target="tpu_custom_call" | custom-call | flops 2337538048 | tf_op jit(solution)/shard_map/pallas_call | solution.py:857
  162.3 0.4 collective-permute-start.18
  162.7 2.6 %collective-permute-start.19 = (f32[328,128]{1,0:T(8,128)}, f32[328,128]{1,0:T(8,128)}, u32[]{:S(2)}, u32[]{:S(2)}) collective-permute-start(f32[328,128]{1,0:T(8,128)} %get-tuple-element.103.refs_8_), channel_id=1, source_target_pairs={{0,16},{4,20},{8,24},{12,28},{16,0},{20,4},{24,8},{28,12},{1,17},{... | collective-permute-start | bytes 503816 | tf_op jit(solution)/shard_map/ppermute | solution.py:749
  165.3 3.0 %shard_map.283 = (f32[368,128]{1,0:T(8,128)}, f32[368,128]{1,0:T(8,128)}, f32[368,128]{1,0:T(8,128)}, f32[176,128]{1,0:T(8,128)}) custom-call(s32[2]{0:T(128)} %pad_add_fusion.place_ref, f32[3072,128]{1,0:T(8,128)} %bitcast.31, f32[3072,128]{1,0:T(8,128)} %bitcast.15.refs_5_.refs_1_.refs_8_, f32[1536,128]{1,0:T(8,128)} %collective-permute-done.10.refs_5_.refs_2_.refs_9_, ...), custom_call_target="tpu_custom_call" | custom-call | flops 1905000576 | tf_op jit(solution)/shard_map/pallas_call | solution.py:857
  168.4 0.6 collective-permute-start.22
  169.0 1.4 collective-permute-start.24
  170.4 1.5 collective-permute-start.23
  171.9 3.3 %collective-permute-done.18.refs_6_.refs_5_ = f32[712,128]{1,0:T(8,128)} collective-permute-done((f32[712,128]{1,0:T(8,128)}, f32[712,128]{1,0:T(8,128)}, u32[]{:S(2)}, u32[]{:S(2)}) %collective-permute-start.18) | collective-permute-done | bytes 364576 | tf_op jit(solution)/shard_map/ppermute | solution.py:749
  175.3 1.3 collective-permute-start.20
  176.5 0.2 collective-permute-start.27
  176.7 0.7 collective-permute-done.24.refs_13_.refs_12_
  177.4 1.3 collective-permute-done.23.refs_12_.refs_11_
  178.7 1.6 collective-permute-done.29.refs_17_
  180.3 0.2 collective-permute-start.30
  180.5 0.4 collective-permute-start.32
  180.8 3.4 %collective-permute-done.20.refs_7_ = f32[328,128]{1,0:T(8,128)} collective-permute-done((f32[328,128]{1,0:T(8,128)}, f32[328,128]{1,0:T(8,128)}, u32[]{:S(2)}, u32[]{:S(2)}) %collective-permute-start.20) | collective-permute-done | bytes 167968 | tf_op jit(solution)/shard_map/ppermute | solution.py:749
  184.2 0.5 collective-permute-start.28
  184.7 3.2 %shard_map.285 = (f32[128,256]{1,0:T(8,128)}, f32[64,512]{1,0:T(8,128)}, f32[64,128]{1,0:T(8,128)}) custom-call(s32[2]{0:T(128)} %pad_add_fusion.place_ref, f32[6144,128]{1,0:T(8,128)} %bitcast.28, f32[6144,128]{1,0:T(8,128)} %bitcast.13.refs_1_.refs_9_, f32[1712,128]{1,0:T(8,128)} %collective-permute-done.7.refs_2_.refs_5_, ...), custom_call_target="tpu_custom_call" | custom-call | flops 1965075200 | tf_op jit(solution)/shard_map/pallas_call | solution.py:857
  188.0 3.8 %shard_map.286 = (f32[128,128]{1,0:T(8,128)}, f32[49,960]{1,0:T(8,128)}, f32[1,512]{1,0:T(1,128)}, f32[1,512]{1,0:T(1,128)}, f32[1,512]{1,0:T(1,128)}, /*index=5...) custom-call(s32[2]{0:T(128)} %pad_add_fusion.place_ref, ...), custom_call_target="tpu_custom_call" | custom-call | flops 2220392448 | tf_op jit(solution)/shard_map/pallas_call | solution.py:857
  (35 shorter events, 0.4 us)
Async XLA Ops:
  2.7 12.7 %collective-permute-start = (f32[192,512]{1,0:T(8,128)}, f32[192,512]{1,0:T(8,128)}, u32[]{:S(2)}, u32[]{:S(2)}) collective-permute-start(f32[192,512]{1,0:T(8,128)} %bitcast.5), channel_id=1, source_target_pairs={{0,4},{4,8},{8,12},{12,16},{16,20},{20,24},{24,28},{1,5},{5,9},{9,... | collective-permute-start | bytes 1179656 | tf_op jit(solution)/shard_map/ppermute | solution.py:978
  5.8 9.6 %collective-permute-start.1 = (f32[192,512]{1,0:T(8,128)}, f32[192,512]{1,0:T(8,128)}, u32[]{:S(2)}, u32[]{:S(2)}) collective-permute-start(f32[192,512]{1,0:T(8,128)} %bitcast.6), channel_id=1, source_target_pairs={{4,0},{8,4},{12,8},{16,12},{20,16},{24,20},{28,24},{5,1},{9,5},{13... | collective-permute-start | bytes 1179656 | tf_op jit(solution)/shard_map/ppermute | solution.py:978
  65.2 11.1 %collective-permute-start.4 = (f32[4,4,384,128]{3,2,1,0:T(8,128)}, f32[4,4,384,128]{3,2,1,0:T(8,128)}, u32[]{:S(2)}, u32[]{:S(2)}) collective-permute-start(f32[4,4,384,128]{3,2,1,0:T(8,128)} %get-tuple-element.80), channel_id=1, source_target_pairs={{0,4},{4,0},{8,12},{12,8},{16,20},{20,16},{24,28},{28,24},{1,5},{5... | collective-permute-start | bytes 9437192 | tf_op jit(solution)/shard_map/ppermute | solution.py:749
  67.9 8.4 %collective-permute-start.6 = (f32[4,4,192,128]{3,2,1,0:T(8,128)}, f32[4,4,192,128]{3,2,1,0:T(8,128)}, u32[]{:S(2)}, u32[]{:S(2)}) collective-permute-start(f32[4,4,192,128]{3,2,1,0:T(8,128)} %get-tuple-element.84), channel_id=1, source_target_pairs={{0,4},{4,0},{8,12},{12,8},{16,20},{20,16},{24,28},{28,24},{1,5},{5... | collective-permute-start | bytes 4718600 | tf_op jit(solution)/shard_map/ppermute | solution.py:749
  67.9 8.3 %collective-permute-start.5 = (f32[704,128]{1,0:T(8,128)}, f32[704,128]{1,0:T(8,128)}, u32[]{:S(2)}, u32[]{:S(2)}) collective-permute-start(f32[704,128]{1,0:T(8,128)} %get-tuple-element.82), channel_id=1, source_target_pairs={{0,4},{4,0},{8,12},{12,8},{16,20},{20,16},{24,28},{28,24},{1,5},{5... | collective-permute-start | bytes 1081352 | tf_op jit(solution)/shard_map/ppermute | solution.py:749
  68.4 13.3 %collective-permute-start.2 = (f32[8,192,128]{2,1,0:T(8,128)}, f32[8,192,128]{2,1,0:T(8,128)}, u32[]{:S(2)}, u32[]{:S(2)}) collective-permute-start(f32[8,192,128]{2,1,0:T(8,128)} %get-tuple-element.75), channel_id=1, source_target_pairs={{0,4},{4,8},{8,12},{12,16},{16,20},{20,24},{24,28},{1,5},{5,9},{9,... | collective-permute-start | bytes 2359304 | tf_op jit(solution)/shard_map/ppermute | solution.py:978
  71.2 10.5 %collective-permute-start.3 = (f32[8,192,128]{2,1,0:T(8,128)}, f32[8,192,128]{2,1,0:T(8,128)}, u32[]{:S(2)}, u32[]{:S(2)}) collective-permute-start(f32[8,192,128]{2,1,0:T(8,128)} %get-tuple-element.77), channel_id=1, source_target_pairs={{4,0},{8,4},{12,8},{16,12},{20,16},{24,20},{28,24},{5,1},{9,5},{13... | collective-permute-start | bytes 2359304 | tf_op jit(solution)/shard_map/ppermute | solution.py:978
  81.7 39.1 %collective-permute-start.10 = (f32[1536,128]{1,0:T(8,128)}, f32[1536,128]{1,0:T(8,128)}, u32[]{:S(2)}, u32[]{:S(2)}) collective-permute-start(f32[1536,128]{1,0:T(8,128)} %shard_map.275.rest_3_), channel_id=1, source_target_pairs={{0,16},{4,20},{8,24},{12,28},{16,0},{20,4},{24,8},{28,12},{1,17},{... | collective-permute-start | bytes 2359304 | tf_op jit(solution)/shard_map/ppermute | solution.py:749
  86.5 34.3 %collective-permute-start.7 = (f32[1712,128]{1,0:T(8,128)}, f32[1712,128]{1,0:T(8,128)}, u32[]{:S(2)}, u32[]{:S(2)}) collective-permute-start(f32[1712,128]{1,0:T(8,128)} %get-tuple-element.85.rest_0_), channel_id=1, source_target_pairs={{0,1},{1,0},{2,3},{3,2},{4,5},{5,4},{6,7},{7,6},{8,9},{9,8},{10,11... | collective-permute-start | bytes 2629640 | tf_op jit(solution)/shard_map/ppermute | solution.py:749
  87.9 41.1 %collective-permute-start.8 = (f32[1712,128]{1,0:T(8,128)}, f32[1712,128]{1,0:T(8,128)}, u32[]{:S(2)}, u32[]{:S(2)}) collective-permute-start(f32[1712,128]{1,0:T(8,128)} %get-tuple-element.86.rest_1_), channel_id=1, source_target_pairs={{0,2},{1,3},{2,0},{3,1},{4,6},{5,7},{6,4},{7,5},{8,10},{9,11},{10,... | collective-permute-start | bytes 2629640 | tf_op jit(solution)/shard_map/ppermute | solution.py:749
  89.5 39.6 %collective-permute-start.9 = (f32[1712,128]{1,0:T(8,128)}, f32[1712,128]{1,0:T(8,128)}, u32[]{:S(2)}, u32[]{:S(2)}) collective-permute-start(f32[1712,128]{1,0:T(8,128)} %get-tuple-element.87.rest_2_), channel_id=1, source_target_pairs={{0,3},{1,2},{2,1},{3,0},{4,7},{5,6},{6,5},{7,4},{8,11},{9,10},{10,... | collective-permute-start | bytes 2629640 | tf_op jit(solution)/shard_map/ppermute | solution.py:749
  129.1 6.2 %collective-permute-start.11 = (f32[4,4,128,128]{3,2,1,0:T(8,128)}, f32[4,4,128,128]{3,2,1,0:T(8,128)}, u32[]{:S(2)}, u32[]{:S(2)}) collective-permute-start(f32[4,4,128,128]{3,2,1,0:T(8,128)} %get-tuple-element.93), channel_id=1, source_target_pairs={{0,4},{4,0},{8,12},{12,8},{16,20},{20,16},{24,28},{28,24},{1,5},{5... | collective-permute-start | bytes 3145736 | tf_op jit(solution)/shard_map/ppermute | solution.py:749
  129.2 6.0 %collective-permute-start.12 = (f32[200,128]{1,0:T(8,128)}, f32[200,128]{1,0:T(8,128)}, u32[]{:S(2)}, u32[]{:S(2)}) collective-permute-start(f32[200,128]{1,0:T(8,128)} %get-tuple-element.95), channel_id=1, source_target_pairs={{0,4},{4,0},{8,12},{12,8},{16,20},{20,16},{24,28},{28,24},{1,5},{5... | collective-permute-start | bytes 307208 | tf_op jit(solution)/shard_map/ppermute | solution.py:749
  133.3 22.5 %collective-permute-start.17 = (f32[944,128]{1,0:T(8,128)}, f32[944,128]{1,0:T(8,128)}, u32[]{:S(2)}, u32[]{:S(2)}) collective-permute-start(f32[944,128]{1,0:T(8,128)} %get-tuple-element.96.refs_4_), channel_id=1, source_target_pairs={{0,8},{4,12},{8,0},{12,4},{16,24},{20,28},{24,16},{28,20},{1,9},{5... | collective-permute-start | bytes 1449992 | tf_op jit(solution)/shard_map/ppermute | solution.py:749
  133.3 25.6 %collective-permute-start.16 = (f32[944,128]{1,0:T(8,128)}, f32[944,128]{1,0:T(8,128)}, u32[]{:S(2)}, u32[]{:S(2)}) collective-permute-start(f32[944,128]{1,0:T(8,128)} %get-tuple-element.97.refs_5_.refs_4_), channel_id=1, source_target_pairs={{0,16},{4,20},{8,24},{12,28},{16,0},{20,4},{24,8},{28,12},{1,17},{... | collective-permute-start | bytes 1449992 | tf_op jit(solution)/shard_map/ppermute | solution.py:749
  138.2 20.7 %collective-permute-start.13 = (f32[712,128]{1,0:T(8,128)}, f32[712,128]{1,0:T(8,128)}, u32[]{:S(2)}, u32[]{:S(2)}) collective-permute-start(f32[712,128]{1,0:T(8,128)} %get-tuple-element.99), channel_id=1, source_target_pairs={{0,1},{1,0},{2,3},{3,2},{4,5},{5,4},{6,7},{7,6},{8,9},{9,8},{10,11... | collective-permute-start | bytes 1093640 | tf_op jit(solution)/shard_map/ppermute | solution.py:749
  139.0 19.9 %collective-permute-start.15 = (f32[712,128]{1,0:T(8,128)}, f32[712,128]{1,0:T(8,128)}, u32[]{:S(2)}, u32[]{:S(2)}) collective-permute-start(f32[712,128]{1,0:T(8,128)} %get-tuple-element.101), channel_id=1, source_target_pairs={{0,3},{1,2},{2,1},{3,0},{4,7},{5,6},{6,5},{7,4},{8,11},{9,10},{10,... | collective-permute-start | bytes 1093640 | tf_op jit(solution)/shard_map/ppermute | solution.py:749
  141.3 17.6 %collective-permute-start.14 = (f32[712,128]{1,0:T(8,128)}, f32[712,128]{1,0:T(8,128)}, u32[]{:S(2)}, u32[]{:S(2)}) collective-permute-start(f32[712,128]{1,0:T(8,128)} %get-tuple-element.100.refs_11_), channel_id=1, source_target_pairs={{0,2},{1,3},{2,0},{3,1},{4,6},{5,7},{6,4},{7,5},{8,10},{9,11},{10,... | collective-permute-start | bytes 1093640 | tf_op jit(solution)/shard_map/ppermute | solution.py:749
  155.8 9.6 %collective-permute-start.21 = (f32[176,128]{1,0:T(8,128)}, f32[176,128]{1,0:T(8,128)}, u32[]{:S(2)}, u32[]{:S(2)}) collective-permute-start(f32[176,128]{1,0:T(8,128)} %shard_map.282), channel_id=1, source_target_pairs={{0,24},{4,28},{8,16},{12,20},{16,8},{20,12},{24,0},{28,4},{1,25},{... | collective-permute-start | bytes 270344 | tf_op jit(solution)/shard_map/ppermute | solution.py:749
  162.3 12.9 %collective-permute-start.18 = (f32[712,128]{1,0:T(8,128)}, f32[712,128]{1,0:T(8,128)}, u32[]{:S(2)}, u32[]{:S(2)}) collective-permute-start(f32[712,128]{1,0:T(8,128)} %get-tuple-element.102.refs_7_), channel_id=1, source_target_pairs={{0,8},{4,12},{8,0},{12,4},{16,24},{20,28},{24,16},{28,20},{1,9},{5... | collective-permute-start | bytes 1093640 | tf_op jit(solution)/shard_map/ppermute | solution.py:749
  162.7 12.6 %collective-permute-start.19 = (f32[328,128]{1,0:T(8,128)}, f32[328,128]{1,0:T(8,128)}, u32[]{:S(2)}, u32[]{:S(2)}) collective-permute-start(f32[328,128]{1,0:T(8,128)} %get-tuple-element.103.refs_8_), channel_id=1, source_target_pairs={{0,16},{4,20},{8,24},{12,28},{16,0},{20,4},{24,8},{28,12},{1,17},{... | collective-permute-start | bytes 503816 | tf_op jit(solution)/shard_map/ppermute | solution.py:749
  168.4 8.2 %collective-permute-start.22 = (f32[368,128]{1,0:T(8,128)}, f32[368,128]{1,0:T(8,128)}, u32[]{:S(2)}, u32[]{:S(2)}) collective-permute-start(f32[368,128]{1,0:T(8,128)} %get-tuple-element.106), channel_id=1, source_target_pairs={{0,1},{1,0},{2,3},{3,2},{4,5},{5,4},{6,7},{7,6},{8,9},{9,8},{10,11... | collective-permute-start | bytes 565256 | tf_op jit(solution)/shard_map/ppermute | solution.py:749
  169.0 8.4 %collective-permute-start.24 = (f32[368,128]{1,0:T(8,128)}, f32[368,128]{1,0:T(8,128)}, u32[]{:S(2)}, u32[]{:S(2)}) collective-permute-start(f32[368,128]{1,0:T(8,128)} %get-tuple-element.107), channel_id=1, source_target_pairs={{0,3},{1,2},{2,1},{3,0},{4,7},{5,6},{6,5},{7,4},{8,11},{9,10},{10,... | collective-permute-start | bytes 565256 | tf_op jit(solution)/shard_map/ppermute | solution.py:749
  170.4 8.3 %collective-permute-start.23 = (f32[368,128]{1,0:T(8,128)}, f32[368,128]{1,0:T(8,128)}, u32[]{:S(2)}, u32[]{:S(2)}) collective-permute-start(f32[368,128]{1,0:T(8,128)} %get-tuple-element.105.refs_9_), channel_id=1, source_target_pairs={{0,2},{1,3},{2,0},{3,1},{4,6},{5,7},{6,4},{7,5},{8,10},{9,11},{10,... | collective-permute-start | bytes 565256 | tf_op jit(solution)/shard_map/ppermute | solution.py:749
  175.2 12.7 %collective-permute-start.26 = (f32[712,128]{1,0:T(8,128)}, f32[712,128]{1,0:T(8,128)}, u32[]{:S(2)}, u32[]{:S(2)}) collective-permute-start(f32[712,128]{1,0:T(8,128)} %collective-permute-done.18.refs_6_.refs_5_), channel_id=1, source_target_pairs={{0,4},{4,0},{8,12},{12,8},{16,20},{20,16},{24,28},{28,24},{1,5},{5... | collective-permute-start | bytes 1093640 | tf_op jit(solution)/shard_map/ppermute | solution.py:749
  175.3 8.9 %collective-permute-start.20 = (f32[328,128]{1,0:T(8,128)}, f32[328,128]{1,0:T(8,128)}, u32[]{:S(2)}, u32[]{:S(2)}) collective-permute-start(f32[328,128]{1,0:T(8,128)} %shard_map.281), channel_id=1, source_target_pairs={{0,24},{4,28},{8,16},{12,20},{16,8},{20,12},{24,0},{28,4},{1,25},{... | collective-permute-start | bytes 503816 | tf_op jit(solution)/shard_map/ppermute | solution.py:749
  176.5 7.6 %collective-permute-start.27 = (f32[328,128]{1,0:T(8,128)}, f32[328,128]{1,0:T(8,128)}, u32[]{:S(2)}, u32[]{:S(2)}) collective-permute-start(f32[328,128]{1,0:T(8,128)} %collective-permute-done.19.refs_1_.refs_2_.refs_6_), channel_id=1, source_target_pairs={{0,4},{4,0},{8,12},{12,8},{16,20},{20,16},{24,28},{28,24},{1,5},{5... | collective-permute-start | bytes 503816 | tf_op jit(solution)/shard_map/ppermute | solution.py:749
  177.4 3.1 %collective-permute-start.25 = (f32[200,128]{1,0:T(8,128)}, f32[200,128]{1,0:T(8,128)}, u32[]{:S(2)}, u32[]{:S(2)}) collective-permute-start(f32[200,128]{1,0:T(8,128)} %get-tuple-element.110), channel_id=1, source_target_pairs={{0,4},{4,0},{8,12},{12,8},{16,20},{20,16},{24,28},{28,24},{1,5},{5... | collective-permute-start | bytes 307208 | tf_op jit(solution)/shard_map/ppermute | solution.py:749
  178.7 1.6 collective-permute-start.29
  180.3 7.6 %collective-permute-start.30 = (f32[368,128]{1,0:T(8,128)}, f32[368,128]{1,0:T(8,128)}, u32[]{:S(2)}, u32[]{:S(2)}) collective-permute-start(f32[368,128]{1,0:T(8,128)} %collective-permute-done.22.refs_11_.refs_10_), channel_id=1, source_target_pairs={{0,4},{4,0},{8,12},{12,8},{16,20},{20,16},{24,28},{28,24},{1,5},{5... | collective-permute-start | bytes 565256 | tf_op jit(solution)/shard_map/ppermute | solution.py:749
  180.5 7.5 %collective-permute-start.32 = (f32[368,128]{1,0:T(8,128)}, f32[368,128]{1,0:T(8,128)}, u32[]{:S(2)}, u32[]{:S(2)}) collective-permute-start(f32[368,128]{1,0:T(8,128)} %collective-permute-done.24.refs_13_.refs_12_), channel_id=1, source_target_pairs={{0,4},{4,0},{8,12},{12,8},{16,20},{20,16},{24,28},{28,24},{1,5},{5... | collective-permute-start | bytes 565256 | tf_op jit(solution)/shard_map/ppermute | solution.py:749
  184.2 3.8 %collective-permute-start.31 = (f32[368,128]{1,0:T(8,128)}, f32[368,128]{1,0:T(8,128)}, u32[]{:S(2)}, u32[]{:S(2)}) collective-permute-start(f32[368,128]{1,0:T(8,128)} %collective-permute-done.23.refs_12_.refs_11_), channel_id=1, source_target_pairs={{0,4},{4,0},{8,12},{12,8},{16,20},{20,16},{24,28},{28,24},{1,5},{5... | collective-permute-start | bytes 565256 | tf_op jit(solution)/shard_map/ppermute | solution.py:749
  184.2 3.8 %collective-permute-start.28 = (f32[328,128]{1,0:T(8,128)}, f32[328,128]{1,0:T(8,128)}, u32[]{:S(2)}, u32[]{:S(2)}) collective-permute-start(f32[328,128]{1,0:T(8,128)} %collective-permute-done.20.refs_7_), channel_id=1, source_target_pairs={{0,4},{4,0},{8,12},{12,8},{16,20},{20,16},{24,28},{28,24},{1,5},{5... | collective-permute-start | bytes 503816 | tf_op jit(solution)/shard_map/ppermute | solution.py:749

commit v14 on v13

--- a/solution.py
+++ b/solution.py
@@ -276,13 +276,7 @@
     copies.wait("ids")
     turned = image_ids(ids_ref, padded, place_ref[0], rows)
     spread_cells((turned >= 0).astype(F32), valid_ref, 0, rows + 2 * REACH)
-    spread_cells(keep_factors(turned, one_table), one_keep_ref, REACH, rows)
-    spread_cells(keep_factors(turned, two_table), two_keep_ref, REACH, rows)
-    column_masks(ids_ref, col_ref)
-    for source, target in (
-        (valid_ref, valid_hbm), (one_keep_ref, one_keep_hbm), (two_keep_ref, two_keep_hbm), (col_ref, col_hbm)
-    ):
-        copies.start("outs", source, target)
+    copies.start("outs", valid_ref, valid_hbm)
     copies.wait("own")
     hat, _ = normalized(rows_ref[...] * valid_ref[reach : reach + cells, :1])
     normed[...] = hat * gain_ref[...]
@@ -293,6 +287,11 @@
             joined[2 * step + k] = part[:, k * LANES : (k + 1) * LANES]
         pair = pl.ds(2 * step, 2)
         copies.start("outs", joined.at[pair], joined_hbm.at[pair])
+    spread_cells(keep_factors(turned, one_table), one_keep_ref, REACH, rows)
+    spread_cells(keep_factors(turned, two_table), two_keep_ref, REACH, rows)
+    column_masks(ids_ref, col_ref)
+    for source, target in ((one_keep_ref, one_keep_hbm), (two_keep_ref, two_keep_hbm), (col_ref, col_hbm)):
+        copies.start("outs", source, target)
     copies.wait_all()
 
 
@@ -1068,12 +1067,10 @@
     plane_sum = Sum([plane_kept, exchange(plane_sent, "ha", 1)], ["plane", "far", "near"])
     line_sum = Sum([line_kept, exchange(line_sent, "ha", 1)], ["far", "near", "plane"])
     packed = Sum([packed_kept, exchange(packed_sent, "ha", 1)], ["plane"])
-    across = Stage([(plane_sum, "plane"), (packed, "plane")], "plane")
+    made, arrived, _ = run(place, Stage([(plane_sum, "plane"), (packed, "plane")], "plane"))
     apart = Stage([(line_sum, "far")], "far")
-    made = list(combine(place, across.groups() + apart.groups()))
-    arrived = across.go(made[: len(across.steps)])
-    made[len(across.steps) :] = tied(made[len(across.steps) :], [above, below])
-    arrived += apart.go(made[len(across.steps) :])
+    more = list(tied(combine(place, apart.groups(), made), [above, below]))
+    made, arrived = made + more, arrived + apart.go(more)
     dcanvas, in_kept, in_sent, small_kept, small_sent = backward(
         place, ids, above, dconv, below, joined, depth_kernel, own, gain, dmiddle, weight_in, made,
         rows, cols, count_ha, count_ba,

time: 193 us -> 189 us (0.979)
  waiting for transfers between devices: 38.5 us -> 31.9 us
  Pallas kernels: 112 us -> 115 us
    ppermute x29, waiting for transfers between devices: 38.5 us -> 31.9 us  [exchange(): lax.ppermute(values, axis, [(i, i ^ bit) for i in range(lax.axis_size(axi...]
    pallas_call x7 -> x8, Pallas kernels: 25.5 us -> 27.7 us  [combine(): pl.pallas_call(kernel, in_specs=[in_smem()] + [in_hbm()] * (len(arrays) +...]
  transfers between devices with their start and end apart: 33 -> 33, of which waited for: 10 -> 11; matrix products, arithmetic and copies ran while one was open for 0% -> 0% of each run, Pallas kernels for 31% -> 32%
where the time goes in v14:
time: 189 us
  Pallas kernels  115 us (61%)
  starting transfers between devices  38.2 us (20%)
  waiting for transfers between devices  31.9 us (17%)
  local copies, waits for them, and re-layouts  2.08 us (1%)
    pallas_call x1, Pallas kernels, forward(): pl.pallas_call(functools.partial(forward_kernel, rows=rows, cols=cols, co...  49.7 us
    ppermute x29, waiting for transfers between devices, exchange(): lax.ppermute(values, axis, [(i, i ^ bit) for i in range(lax.axis_size(axi...  31.9 us
    ppermute x29, starting transfers between devices, exchange(): lax.ppermute(values, axis, [(i, i ^ bit) for i in range(lax.axis_size(axi...  29.6 us
    pallas_call x1, Pallas kernels, backward(): pl.pallas_call(functools.partial(backward_kernel, rows=rows, cols=cols),...  29.3 us
    pallas_call x8, Pallas kernels, combine(): pl.pallas_call(kernel, in_specs=[in_smem()] + [in_hbm()] * (len(arrays) +...  27.7 us
    ppermute x4, starting transfers between devices, neighbour_rows(): return (lax.ppermute(bottom, 'ha', up), lax.ppermute(top, 'ha', down))  8.59 us
    pallas_call x1, Pallas kernels, head(): pl.pallas_call(functools.partial(head_kernel, rows=rows, cols=cols), in_s...  7.88 us
  transfers between devices with their start and end apart: 33, of which 11 were waited for; matrix products, arithmetic and copies ran while one was open for 0% of the time, Pallas kernels for 32%

profile of v14, /device:TPU:0, one launch (start us, length us, event | category | flops | bytes accessed | tf_op | source)
XLA Modules:
  0.0 188.6 jit_solution(10146749446539114168)
XLA Ops:
  0.6 2.1 %fusion = (f32[1,3,64,512]{3,2,1,0:T(8,128)}, f32[1,3,64,512]{3,2,1,0:T(8,128)}) fusion(f32[1,8,64,512]{3,2,1,0:T(8,128)} %param.17), kind=kLoop, calls=%fused_computation.1 | loop fusion | bytes 1572864 | tf_op jit(solution)/shard_map/slice | solution.py:1055
  2.7 3.1 %collective-permute-start = (f32[192,512]{1,0:T(8,128)}, f32[192,512]{1,0:T(8,128)}, u32[]{:S(2)}, u32[]{:S(2)}) collective-permute-start(f32[192,512]{1,0:T(8,128)} %bitcast.5), channel_id=1, source_target_pairs={{0,4},{4,8},{8,12},{12,16},{16,20},{20,24},{24,28},{1,5},{5,9},{9,... | collective-permute-start | bytes 1179656 | tf_op jit(solution)/shard_map/ppermute | solution.py:977
  5.8 1.3 collective-permute-start.1
  7.1 0.6 pad_add_fusion.place_ref
  7.8 7.9 %shard_map.272 = (f32[8,512,128]{2,1,0:T(8,128)}, f32[896,128]{1,0:T(8,128)}, f32[512,128]{1,0:T(8,128)}, f32[512,128]{1,0:T(8,128)}, f32[7,8,8,128]{3,2,1,0:T(8,128)}) custom-call(s32[2]{0:T(128)} %pad_add_fusion.place_ref, s32[64,64]{1,0:T(8,128)} %bitcast.41, s32[1,36]{1,0:T(1,128)} %one_table.1, s32[1,36]{1,0:T(1,128)} %two_table.1, s32[64,64]{1,0:T(8,128)} %bitcast.42, ...), custom_call_target="tpu_custom_call" | custom-call | flops 7699999744 | tf_op jit(solution)/shard_map/pallas_call | solution.py:306
  15.7 49.7 %shard_map.273 = (f32[512,512]{1,0:T(8,128)}, f32[512,512]{1,0:T(8,128)}, f32[8,512,128]{2,1,0:T(8,128)}, f32[8,192,128]{2,1,0:T(8,128)}, f32[8,192,128]{2,1,0:T...) custom-call(s32[2]{0:T(128)} %pad_add_fusion.place_ref, ...), custom_call_target="tpu_custom_call" | custom-call | flops 52800000000 | tf_op jit(solution)/shard_map/pallas_call | solution.py:591
  65.4 2.6 %collective-permute-start.4 = (f32[4,4,384,128]{3,2,1,0:T(8,128)}, f32[4,4,384,128]{3,2,1,0:T(8,128)}, u32[]{:S(2)}, u32[]{:S(2)}) collective-permute-start(f32[4,4,384,128]{3,2,1,0:T(8,128)} %get-tuple-element.79), channel_id=1, source_target_pairs={{0,4},{4,0},{8,12},{12,8},{16,20},{20,16},{24,28},{28,24},{1,5},{5... | collective-permute-start | bytes 9437192 | tf_op jit(solution)/shard_map/ppermute | solution.py:748
  68.2 0.4 collective-permute-start.5
  68.6 2.9 %collective-permute-start.2 = (f32[8,192,128]{2,1,0:T(8,128)}, f32[8,192,128]{2,1,0:T(8,128)}, u32[]{:S(2)}, u32[]{:S(2)}) collective-permute-start(f32[8,192,128]{2,1,0:T(8,128)} %get-tuple-element.74), channel_id=1, source_target_pairs={{0,4},{4,8},{8,12},{12,16},{16,20},{20,24},{24,28},{1,5},{5,9},{9,... | collective-permute-start | bytes 2359304 | tf_op jit(solution)/shard_map/ppermute | solution.py:977
  71.5 1.3 collective-permute-start.3
  72.8 3.7 %collective-permute-done.5.refs_3_.refs_4_ = f32[704,128]{1,0:T(8,128)} collective-permute-done((f32[704,128]{1,0:T(8,128)}, f32[704,128]{1,0:T(8,128)}, u32[]{:S(2)}, u32[]{:S(2)}) %collective-permute-start.5) | collective-permute-done | bytes 360480 | tf_op jit(solution)/shard_map/ppermute | solution.py:748
  76.5 4.5 %shard_map.274 = (f32[1712,128]{1,0:T(8,128)}, f32[1712,128]{1,0:T(8,128)}, f32[1712,128]{1,0:T(8,128)}) custom-call(s32[2]{0:T(128)} %pad_add_fusion.place_ref, f32[6144,128]{1,0:T(8,128)} %bitcast.25, f32[6144,128]{1,0:T(8,128)} %bitcast.13.refs_1_.refs_9_, f32[704,128]{1,0:T(8,128)} %get-tuple-element.80.refs_2_.refs_3_, ...), custom_call_target="tpu_custom_call" | custom-call | flops 3992595200 | tf_op jit(solution)/shard_map/pallas_call | solution.py:856
  81.0 1.6 collective-permute-start.7
  82.5 1.5 collective-permute-start.8
  84.1 0.5 collective-permute-start.9
  84.6 3.0 %shard_map.275.refs_0_ = f32[1536,128]{1,0:T(8,128)} custom-call(s32[2]{0:T(128)} %pad_add_fusion.place_ref, f32[3072,128]{1,0:T(8,128)} %bitcast.29, f32[3072,128]{1,0:T(8,128)} %bitcast.15.refs_1_.refs_8_, f32[1712,128]{1,0:T(8,128)} %get-tuple-element.82.refs_2_.rest_0_, f32[1712,128]{1,0:T(8,128)} %get-tuple-element.83.refs_3_.rest_1_, ...), custom_call_target="tpu_custom_call" | custom-call | flops 1965075200 | tf_op jit(solution)/shard_map/pallas_call | solution.py:856
  87.6 3.1 %collective-permute-start.10 = (f32[1536,128]{1,0:T(8,128)}, f32[1536,128]{1,0:T(8,128)}, u32[]{:S(2)}, u32[]{:S(2)}) collective-permute-start(f32[1536,128]{1,0:T(8,128)} %shard_map.276.rest_3_), channel_id=1, source_target_pairs={{0,16},{4,20},{8,24},{12,28},{16,0},{20,4},{24,8},{28,12},{1,17},{... | collective-permute-start | bytes 2359304 | tf_op jit(solution)/shard_map/ppermute | solution.py:748
  90.7 29.3 %shard_map.277 = (f32[512,512]{1,0:T(8,128)}, f32[4,4,128,128]{3,2,1,0:T(8,128)}, f32[4,4,128,128]{3,2,1,0:T(8,128)}, f32[200,128]{1,0:T(8,128)}, f32[200,128]{1,0:T(8,128)}) custom-call(s32[2]{0:T(128)} %pad_add_fusion.place_ref, s32[64,64]{1,0:T(8,128)} %bitcast.44, s32[64,64]{1,0:T(8,128)} %bitcast.45, ...), custom_call_target="tpu_custom_call" | custom-call | flops 27499999232 | tf_op jit(solution)/shard_map/pallas_call | solution.py:717
  120.0 4.8 %collective-permute-done.10.refs_5_.refs_2_.refs_9_ = f32[1536,128]{1,0:T(8,128)} collective-permute-done((f32[1536,128]{1,0:T(8,128)}, f32[1536,128]{1,0:T(8,128)}, u32[]{:S(2)}, u32[]{:S(2)}) %collective-permute-start.10) | collective-permute-done | bytes 786464 | tf_op jit(solution)/shard_map/ppermute | solution.py:748
  125.0 0.5 collective-permute-start.12
  125.5 3.7 %shard_map.279 = (f32[944,128]{1,0:T(8,128)}, f32[944,128]{1,0:T(8,128)}, f32[176,128]{1,0:T(8,128)}) custom-call(s32[2]{0:T(128)} %pad_add_fusion.place_ref, f32[3072,128]{1,0:T(8,128)} %bitcast.30, f32[3072,128]{1,0:T(8,128)} %bitcast.15.refs_1_.refs_8_, f32[1536,128]{1,0:T(8,128)} %collective-permute-done.10.refs_5_.refs_2_.refs_9_, ...), custom_call_target="tpu_custom_call" | custom-call | flops 2806120448 | tf_op jit(solution)/shard_map/pallas_call | solution.py:856
  129.2 0.8 collective-permute-start.17
  130.0 3.4 %collective-permute-start.16 = (f32[944,128]{1,0:T(8,128)}, f32[944,128]{1,0:T(8,128)}, u32[]{:S(2)}, u32[]{:S(2)}) collective-permute-start(f32[944,128]{1,0:T(8,128)} %get-tuple-element.95.refs_5_.refs_4_), channel_id=1, source_target_pairs={{0,16},{4,20},{8,24},{12,28},{16,0},{20,4},{24,8},{28,12},{1,17},{... | collective-permute-start | bytes 1449992 | tf_op jit(solution)/shard_map/ppermute | solution.py:748
  133.3 3.0 %shard_map.280 = (f32[712,128]{1,0:T(8,128)}, f32[712,128]{1,0:T(8,128)}, f32[712,128]{1,0:T(8,128)}) custom-call(s32[2]{0:T(128)} %pad_add_fusion.place_ref, f32[2048,128]{1,0:T(8,128)} %bitcast.33, f32[2048,128]{1,0:T(8,128)} %bitcast.18.refs_1_.refs_7_, f32[200,128]{1,0:T(8,128)} %get-tuple-element.92.refs_2_, ...), custom_call_target="tpu_custom_call" | custom-call | flops 2152808448 | tf_op jit(solution)/shard_map/pallas_call | solution.py:856
  136.3 1.5 collective-permute-start.13
  137.9 1.5 collective-permute-start.15
  139.3 0.5 collective-permute-start.14
  139.9 12.8 %collective-permute-done.17.refs_12_.refs_1_.refs_3_.refs_10_ = f32[944,128]{1,0:T(8,128)} collective-permute-done((f32[944,128]{1,0:T(8,128)}, f32[944,128]{1,0:T(8,128)}, u32[]{:S(2)}, u32[]{:S(2)}) %collective-permute-start.17) | collective-permute-done | bytes 483360 | tf_op jit(solution)/shard_map/ppermute | solution.py:748
  152.7 1.8 collective-permute-start.21
  154.5 0.7 collective-permute-done.16.refs_5_.refs_13_
  155.5 1.4 collective-permute-done.14.refs_9_.refs_3_
  156.8 3.4 %shard_map.281 = (f32[712,128]{1,0:T(8,128)}, f32[328,128]{1,0:T(8,128)}, f32[328,128]{1,0:T(8,128)}, f32[200,128]{1,0:T(8,128)}) custom-call(s32[2]{0:T(128)} %pad_add_fusion.place_ref, f32[6144,128]{1,0:T(8,128)} %bitcast.27, f32[6144,128]{1,0:T(8,128)} %bitcast.13.refs_1_.refs_9_, f32[1712,128]{1,0:T(8,128)} %collective-permute-done.7.refs_2_.refs_5_, ...), custom_call_target="tpu_custom_call" | custom-call | flops 2337538048 | tf_op jit(solution)/shard_map/pallas_call | solution.py:856
  160.2 0.4 collective-permute-start.18
  160.7 1.8 collective-permute-start.19
  162.4 3.0 %shard_map.284 = (f32[368,128]{1,0:T(8,128)}, f32[368,128]{1,0:T(8,128)}, f32[368,128]{1,0:T(8,128)}, f32[176,128]{1,0:T(8,128)}) custom-call(s32[2]{0:T(128)} %pad_add_fusion.place_ref, f32[3072,128]{1,0:T(8,128)} %bitcast.31, f32[3072,128]{1,0:T(8,128)} %bitcast.15.refs_1_.refs_8_, f32[1536,128]{1,0:T(8,128)} %collective-permute-done.10.refs_5_.refs_2_.refs_9_, ...), custom_call_target="tpu_custom_call" | custom-call | flops 1905000576 | tf_op jit(solution)/shard_map/pallas_call | solution.py:856
  165.5 1.5 collective-permute-start.22
  167.0 1.5 collective-permute-start.24
  168.5 0.5 collective-permute-start.23
  169.0 2.8 %collective-permute-done.18.refs_6_.refs_5_ = f32[712,128]{1,0:T(8,128)} collective-permute-done((f32[712,128]{1,0:T(8,128)}, f32[712,128]{1,0:T(8,128)}, u32[]{:S(2)}, u32[]{:S(2)}) %collective-permute-start.18) | collective-permute-done | bytes 364576 | tf_op jit(solution)/shard_map/ppermute | solution.py:748
  171.8 2.8 %collective-permute-start.20 = (f32[328,128]{1,0:T(8,128)}, f32[328,128]{1,0:T(8,128)}, u32[]{:S(2)}, u32[]{:S(2)}) collective-permute-start(f32[328,128]{1,0:T(8,128)} %shard_map.282), channel_id=1, source_target_pairs={{0,24},{4,28},{8,16},{12,20},{16,8},{20,12},{24,0},{28,4},{1,25},{... | collective-permute-start | bytes 503816 | tf_op jit(solution)/shard_map/ppermute | solution.py:748
  174.8 0.6 collective-permute-done.24.refs_13_.refs_12_
  175.4 1.3 collective-permute-done.23.refs_12_.refs_11_
  176.7 1.6 collective-permute-done.29.refs_17_
  178.5 0.4 collective-permute-start.32
  178.9 1.9 collective-permute-done.20.refs_7_
  180.7 0.5 collective-permute-start.28
  181.3 3.2 %shard_map.286 = (f32[128,256]{1,0:T(8,128)}, f32[64,512]{1,0:T(8,128)}, f32[64,128]{1,0:T(8,128)}) custom-call(s32[2]{0:T(128)} %pad_add_fusion.place_ref, f32[6144,128]{1,0:T(8,128)} %bitcast.28, f32[6144,128]{1,0:T(8,128)} %bitcast.13.refs_1_.refs_9_, f32[1712,128]{1,0:T(8,128)} %collective-permute-done.7.refs_2_.refs_5_, ...), custom_call_target="tpu_custom_call" | custom-call | flops 1965075200 | tf_op jit(solution)/shard_map/pallas_call | solution.py:856
  184.6 3.8 %shard_map.287 = (f32[128,128]{1,0:T(8,128)}, f32[49,960]{1,0:T(8,128)}, f32[1,512]{1,0:T(1,128)}, f32[1,512]{1,0:T(1,128)}, f32[1,512]{1,0:T(1,128)}, /*index=5...) custom-call(s32[2]{0:T(128)} %pad_add_fusion.place_ref, ...), custom_call_target="tpu_custom_call" | custom-call | flops 2220392448 | tf_op jit(solution)/shard_map/pallas_call | solution.py:856
  (36 shorter events, 0.8 us)
Async XLA Ops:
  2.7 12.9 %collective-permute-start = (f32[192,512]{1,0:T(8,128)}, f32[192,512]{1,0:T(8,128)}, u32[]{:S(2)}, u32[]{:S(2)}) collective-permute-start(f32[192,512]{1,0:T(8,128)} %bitcast.5), channel_id=1, source_target_pairs={{0,4},{4,8},{8,12},{12,16},{16,20},{20,24},{24,28},{1,5},{5,9},{9,... | collective-permute-start | bytes 1179656 | tf_op jit(solution)/shard_map/ppermute | solution.py:977
  5.8 9.8 %collective-permute-start.1 = (f32[192,512]{1,0:T(8,128)}, f32[192,512]{1,0:T(8,128)}, u32[]{:S(2)}, u32[]{:S(2)}) collective-permute-start(f32[192,512]{1,0:T(8,128)} %bitcast.6), channel_id=1, source_target_pairs={{4,0},{8,4},{12,8},{16,12},{20,16},{24,20},{28,24},{5,1},{9,5},{13... | collective-permute-start | bytes 1179656 | tf_op jit(solution)/shard_map/ppermute | solution.py:977
  65.4 11.0 %collective-permute-start.4 = (f32[4,4,384,128]{3,2,1,0:T(8,128)}, f32[4,4,384,128]{3,2,1,0:T(8,128)}, u32[]{:S(2)}, u32[]{:S(2)}) collective-permute-start(f32[4,4,384,128]{3,2,1,0:T(8,128)} %get-tuple-element.79), channel_id=1, source_target_pairs={{0,4},{4,0},{8,12},{12,8},{16,20},{20,16},{24,28},{28,24},{1,5},{5... | collective-permute-start | bytes 9437192 | tf_op jit(solution)/shard_map/ppermute | solution.py:748
  68.1 16.0 %collective-permute-start.6 = (f32[4,4,192,128]{3,2,1,0:T(8,128)}, f32[4,4,192,128]{3,2,1,0:T(8,128)}, u32[]{:S(2)}, u32[]{:S(2)}) collective-permute-start(f32[4,4,192,128]{3,2,1,0:T(8,128)} %get-tuple-element.86), channel_id=1, source_target_pairs={{0,4},{4,0},{8,12},{12,8},{16,20},{20,16},{24,28},{28,24},{1,5},{5... | collective-permute-start | bytes 4718600 | tf_op jit(solution)/shard_map/ppermute | solution.py:748
  68.2 8.3 %collective-permute-start.5 = (f32[704,128]{1,0:T(8,128)}, f32[704,128]{1,0:T(8,128)}, u32[]{:S(2)}, u32[]{:S(2)}) collective-permute-start(f32[704,128]{1,0:T(8,128)} %get-tuple-element.81), channel_id=1, source_target_pairs={{0,4},{4,0},{8,12},{12,8},{16,20},{20,16},{24,28},{28,24},{1,5},{5... | collective-permute-start | bytes 1081352 | tf_op jit(solution)/shard_map/ppermute | solution.py:748
  68.6 19.0 %collective-permute-start.2 = (f32[8,192,128]{2,1,0:T(8,128)}, f32[8,192,128]{2,1,0:T(8,128)}, u32[]{:S(2)}, u32[]{:S(2)}) collective-permute-start(f32[8,192,128]{2,1,0:T(8,128)} %get-tuple-element.74), channel_id=1, source_target_pairs={{0,4},{4,8},{8,12},{12,16},{16,20},{20,24},{24,28},{1,5},{5,9},{9,... | collective-permute-start | bytes 2359304 | tf_op jit(solution)/shard_map/ppermute | solution.py:977
  71.5 16.1 %collective-permute-start.3 = (f32[8,192,128]{2,1,0:T(8,128)}, f32[8,192,128]{2,1,0:T(8,128)}, u32[]{:S(2)}, u32[]{:S(2)}) collective-permute-start(f32[8,192,128]{2,1,0:T(8,128)} %get-tuple-element.76), channel_id=1, source_target_pairs={{4,0},{8,4},{12,8},{16,12},{20,16},{24,20},{28,24},{5,1},{9,5},{13... | collective-permute-start | bytes 2359304 | tf_op jit(solution)/shard_map/ppermute | solution.py:977
  81.0 43.9 %collective-permute-start.7 = (f32[1712,128]{1,0:T(8,128)}, f32[1712,128]{1,0:T(8,128)}, u32[]{:S(2)}, u32[]{:S(2)}) collective-permute-start(f32[1712,128]{1,0:T(8,128)} %get-tuple-element.82.refs_2_.rest_0_), channel_id=1, source_target_pairs={{0,1},{1,0},{2,3},{3,2},{4,5},{5,4},{6,7},{7,6},{8,9},{9,8},{10,11... | collective-permute-start | bytes 2629640 | tf_op jit(solution)/shard_map/ppermute | solution.py:748
  82.5 42.3 %collective-permute-start.8 = (f32[1712,128]{1,0:T(8,128)}, f32[1712,128]{1,0:T(8,128)}, u32[]{:S(2)}, u32[]{:S(2)}) collective-permute-start(f32[1712,128]{1,0:T(8,128)} %get-tuple-element.83.refs_3_.rest_1_), channel_id=1, source_target_pairs={{0,2},{1,3},{2,0},{3,1},{4,6},{5,7},{6,4},{7,5},{8,10},{9,11},{10,... | collective-permute-start | bytes 2629640 | tf_op jit(solution)/shard_map/ppermute | solution.py:748
  84.1 40.8 %collective-permute-start.9 = (f32[1712,128]{1,0:T(8,128)}, f32[1712,128]{1,0:T(8,128)}, u32[]{:S(2)}, u32[]{:S(2)}) collective-permute-start(f32[1712,128]{1,0:T(8,128)} %get-tuple-element.84.refs_4_.rest_2_), channel_id=1, source_target_pairs={{0,3},{1,2},{2,1},{3,0},{4,7},{5,6},{6,5},{7,4},{8,11},{9,10},{10,... | collective-permute-start | bytes 2629640 | tf_op jit(solution)/shard_map/ppermute | solution.py:748
  87.6 37.2 %collective-permute-start.10 = (f32[1536,128]{1,0:T(8,128)}, f32[1536,128]{1,0:T(8,128)}, u32[]{:S(2)}, u32[]{:S(2)}) collective-permute-start(f32[1536,128]{1,0:T(8,128)} %shard_map.276.rest_3_), channel_id=1, source_target_pairs={{0,16},{4,20},{8,24},{12,28},{16,0},{20,4},{24,8},{28,12},{1,17},{... | collective-permute-start | bytes 2359304 | tf_op jit(solution)/shard_map/ppermute | solution.py:748
  124.9 8.4 %collective-permute-start.11 = (f32[4,4,128,128]{3,2,1,0:T(8,128)}, f32[4,4,128,128]{3,2,1,0:T(8,128)}, u32[]{:S(2)}, u32[]{:S(2)}) collective-permute-start(f32[4,4,128,128]{3,2,1,0:T(8,128)} %get-tuple-element.91), channel_id=1, source_target_pairs={{0,4},{4,0},{8,12},{12,8},{16,20},{20,16},{24,28},{28,24},{1,5},{5... | collective-permute-start | bytes 3145736 | tf_op jit(solution)/shard_map/ppermute | solution.py:748
  125.0 8.4 %collective-permute-start.12 = (f32[200,128]{1,0:T(8,128)}, f32[200,128]{1,0:T(8,128)}, u32[]{:S(2)}, u32[]{:S(2)}) collective-permute-start(f32[200,128]{1,0:T(8,128)} %get-tuple-element.93), channel_id=1, source_target_pairs={{0,4},{4,0},{8,12},{12,8},{16,20},{20,16},{24,28},{28,24},{1,5},{5... | collective-permute-start | bytes 307208 | tf_op jit(solution)/shard_map/ppermute | solution.py:748
  129.2 23.5 %collective-permute-start.17 = (f32[944,128]{1,0:T(8,128)}, f32[944,128]{1,0:T(8,128)}, u32[]{:S(2)}, u32[]{:S(2)}) collective-permute-start(f32[944,128]{1,0:T(8,128)} %get-tuple-element.94.refs_4_), channel_id=1, source_target_pairs={{0,8},{4,12},{8,0},{12,4},{16,24},{20,28},{24,16},{28,20},{1,9},{5... | collective-permute-start | bytes 1449992 | tf_op jit(solution)/shard_map/ppermute | solution.py:748
  130.0 25.3 %collective-permute-start.16 = (f32[944,128]{1,0:T(8,128)}, f32[944,128]{1,0:T(8,128)}, u32[]{:S(2)}, u32[]{:S(2)}) collective-permute-start(f32[944,128]{1,0:T(8,128)} %get-tuple-element.95.refs_5_.refs_4_), channel_id=1, source_target_pairs={{0,16},{4,20},{8,24},{12,28},{16,0},{20,4},{24,8},{28,12},{1,17},{... | collective-permute-start | bytes 1449992 | tf_op jit(solution)/shard_map/ppermute | solution.py:748
  136.3 18.9 %collective-permute-start.13 = (f32[712,128]{1,0:T(8,128)}, f32[712,128]{1,0:T(8,128)}, u32[]{:S(2)}, u32[]{:S(2)}) collective-permute-start(f32[712,128]{1,0:T(8,128)} %get-tuple-element.97), channel_id=1, source_target_pairs={{0,1},{1,0},{2,3},{3,2},{4,5},{5,4},{6,7},{7,6},{8,9},{9,8},{10,11... | collective-permute-start | bytes 1093640 | tf_op jit(solution)/shard_map/ppermute | solution.py:748
  137.9 17.6 %collective-permute-start.15 = (f32[712,128]{1,0:T(8,128)}, f32[712,128]{1,0:T(8,128)}, u32[]{:S(2)}, u32[]{:S(2)}) collective-permute-start(f32[712,128]{1,0:T(8,128)} %get-tuple-element.99), channel_id=1, source_target_pairs={{0,3},{1,2},{2,1},{3,0},{4,7},{5,6},{6,5},{7,4},{8,11},{9,10},{10,... | collective-permute-start | bytes 1093640 | tf_op jit(solution)/shard_map/ppermute | solution.py:748
  139.3 17.5 %collective-permute-start.14 = (f32[712,128]{1,0:T(8,128)}, f32[712,128]{1,0:T(8,128)}, u32[]{:S(2)}, u32[]{:S(2)}) collective-permute-start(f32[712,128]{1,0:T(8,128)} %get-tuple-element.98.refs_11_), channel_id=1, source_target_pairs={{0,2},{1,3},{2,0},{3,1},{4,6},{5,7},{6,4},{7,5},{8,10},{9,11},{10,... | collective-permute-start | bytes 1093640 | tf_op jit(solution)/shard_map/ppermute | solution.py:748
  152.7 9.7 %collective-permute-start.21 = (f32[176,128]{1,0:T(8,128)}, f32[176,128]{1,0:T(8,128)}, u32[]{:S(2)}, u32[]{:S(2)}) collective-permute-start(f32[176,128]{1,0:T(8,128)} %shard_map.283), channel_id=1, source_target_pairs={{0,24},{4,28},{8,16},{12,20},{16,8},{20,12},{24,0},{28,4},{1,25},{... | collective-permute-start | bytes 270344 | tf_op jit(solution)/shard_map/ppermute | solution.py:748
  160.2 11.6 %collective-permute-start.18 = (f32[712,128]{1,0:T(8,128)}, f32[712,128]{1,0:T(8,128)}, u32[]{:S(2)}, u32[]{:S(2)}) collective-permute-start(f32[712,128]{1,0:T(8,128)} %get-tuple-element.100.refs_7_), channel_id=1, source_target_pairs={{0,8},{4,12},{8,0},{12,4},{16,24},{20,28},{24,16},{28,20},{1,9},{5... | collective-permute-start | bytes 1093640 | tf_op jit(solution)/shard_map/ppermute | solution.py:748
  160.7 11.2 %collective-permute-start.19 = (f32[328,128]{1,0:T(8,128)}, f32[328,128]{1,0:T(8,128)}, u32[]{:S(2)}, u32[]{:S(2)}) collective-permute-start(f32[328,128]{1,0:T(8,128)} %get-tuple-element.101.refs_8_), channel_id=1, source_target_pairs={{0,16},{4,20},{8,24},{12,28},{16,0},{20,4},{24,8},{28,12},{1,17},{... | collective-permute-start | bytes 503816 | tf_op jit(solution)/shard_map/ppermute | solution.py:748
  165.5 9.2 %collective-permute-start.22 = (f32[368,128]{1,0:T(8,128)}, f32[368,128]{1,0:T(8,128)}, u32[]{:S(2)}, u32[]{:S(2)}) collective-permute-start(f32[368,128]{1,0:T(8,128)} %get-tuple-element.104), channel_id=1, source_target_pairs={{0,1},{1,0},{2,3},{3,2},{4,5},{5,4},{6,7},{7,6},{8,9},{9,8},{10,11... | collective-permute-start | bytes 565256 | tf_op jit(solution)/shard_map/ppermute | solution.py:748
  167.0 8.4 %collective-permute-start.24 = (f32[368,128]{1,0:T(8,128)}, f32[368,128]{1,0:T(8,128)}, u32[]{:S(2)}, u32[]{:S(2)}) collective-permute-start(f32[368,128]{1,0:T(8,128)} %get-tuple-element.105), channel_id=1, source_target_pairs={{0,3},{1,2},{2,1},{3,0},{4,7},{5,6},{6,5},{7,4},{8,11},{9,10},{10,... | collective-permute-start | bytes 565256 | tf_op jit(solution)/shard_map/ppermute | solution.py:748
  168.5 8.2 %collective-permute-start.23 = (f32[368,128]{1,0:T(8,128)}, f32[368,128]{1,0:T(8,128)}, u32[]{:S(2)}, u32[]{:S(2)}) collective-permute-start(f32[368,128]{1,0:T(8,128)} %get-tuple-element.103.refs_9_), channel_id=1, source_target_pairs={{0,2},{1,3},{2,0},{3,1},{4,6},{5,7},{6,4},{7,5},{8,10},{9,11},{10,... | collective-permute-start | bytes 565256 | tf_op jit(solution)/shard_map/ppermute | solution.py:748
  171.8 12.7 %collective-permute-start.26 = (f32[712,128]{1,0:T(8,128)}, f32[712,128]{1,0:T(8,128)}, u32[]{:S(2)}, u32[]{:S(2)}) collective-permute-start(f32[712,128]{1,0:T(8,128)} %collective-permute-done.18.refs_6_.refs_5_), channel_id=1, source_target_pairs={{0,4},{4,0},{8,12},{12,8},{16,20},{20,16},{24,28},{28,24},{1,5},{5... | collective-permute-start | bytes 1093640 | tf_op jit(solution)/shard_map/ppermute | solution.py:748
  171.8 8.9 %collective-permute-start.20 = (f32[328,128]{1,0:T(8,128)}, f32[328,128]{1,0:T(8,128)}, u32[]{:S(2)}, u32[]{:S(2)}) collective-permute-start(f32[328,128]{1,0:T(8,128)} %shard_map.282), channel_id=1, source_target_pairs={{0,24},{4,28},{8,16},{12,20},{16,8},{20,12},{24,0},{28,4},{1,25},{... | collective-permute-start | bytes 503816 | tf_op jit(solution)/shard_map/ppermute | solution.py:748
  174.6 6.1 %collective-permute-start.27 = (f32[328,128]{1,0:T(8,128)}, f32[328,128]{1,0:T(8,128)}, u32[]{:S(2)}, u32[]{:S(2)}) collective-permute-start(f32[328,128]{1,0:T(8,128)} %collective-permute-done.19.refs_1_.refs_2_.refs_6_), channel_id=1, source_target_pairs={{0,4},{4,0},{8,12},{12,8},{16,20},{20,16},{24,28},{28,24},{1,5},{5... | collective-permute-start | bytes 503816 | tf_op jit(solution)/shard_map/ppermute | solution.py:748
  175.4 3.1 %collective-permute-start.25 = (f32[200,128]{1,0:T(8,128)}, f32[200,128]{1,0:T(8,128)}, u32[]{:S(2)}, u32[]{:S(2)}) collective-permute-start(f32[200,128]{1,0:T(8,128)} %get-tuple-element.108), channel_id=1, source_target_pairs={{0,4},{4,0},{8,12},{12,8},{16,20},{20,16},{24,28},{28,24},{1,5},{5... | collective-permute-start | bytes 307208 | tf_op jit(solution)/shard_map/ppermute | solution.py:748
  176.7 1.6 collective-permute-start.29
  178.4 6.1 %collective-permute-start.30 = (f32[368,128]{1,0:T(8,128)}, f32[368,128]{1,0:T(8,128)}, u32[]{:S(2)}, u32[]{:S(2)}) collective-permute-start(f32[368,128]{1,0:T(8,128)} %collective-permute-done.22.refs_11_.refs_10_), channel_id=1, source_target_pairs={{0,4},{4,0},{8,12},{12,8},{16,20},{20,16},{24,28},{28,24},{1,5},{5... | collective-permute-start | bytes 565256 | tf_op jit(solution)/shard_map/ppermute | solution.py:748
  178.5 6.0 %collective-permute-start.32 = (f32[368,128]{1,0:T(8,128)}, f32[368,128]{1,0:T(8,128)}, u32[]{:S(2)}, u32[]{:S(2)}) collective-permute-start(f32[368,128]{1,0:T(8,128)} %collective-permute-done.24.refs_13_.refs_12_), channel_id=1, source_target_pairs={{0,4},{4,0},{8,12},{12,8},{16,20},{20,16},{24,28},{28,24},{1,5},{5... | collective-permute-start | bytes 565256 | tf_op jit(solution)/shard_map/ppermute | solution.py:748
  180.7 3.8 %collective-permute-start.31 = (f32[368,128]{1,0:T(8,128)}, f32[368,128]{1,0:T(8,128)}, u32[]{:S(2)}, u32[]{:S(2)}) collective-permute-start(f32[368,128]{1,0:T(8,128)} %collective-permute-done.23.refs_12_.refs_11_), channel_id=1, source_target_pairs={{0,4},{4,0},{8,12},{12,8},{16,20},{20,16},{24,28},{28,24},{1,5},{5... | collective-permute-start | bytes 565256 | tf_op jit(solution)/shard_map/ppermute | solution.py:748
  180.7 3.8 %collective-permute-start.28 = (f32[328,128]{1,0:T(8,128)}, f32[328,128]{1,0:T(8,128)}, u32[]{:S(2)}, u32[]{:S(2)}) collective-permute-start(f32[328,128]{1,0:T(8,128)} %collective-permute-done.20.refs_7_), channel_id=1, source_target_pairs={{0,4},{4,0},{8,12},{12,8},{16,20},{20,16},{24,28},{28,24},{1,5},{5... | collective-permute-start | bytes 503816 | tf_op jit(solution)/shard_map/ppermute | solution.py:748

commit v15 on v14

--- a/solution.py
+++ b/solution.py
@@ -259,7 +259,7 @@
 
 
 def head_kernel(
-    place_ref, ids_scalar, one_table, two_table, ids_hbm, own_hbm, gain_hbm, in_hbm_ref,
+    ids_scalar, one_table, two_table, ids_hbm, own_hbm, gain_hbm, in_hbm_ref,
     joined_hbm, valid_hbm, one_keep_hbm, two_keep_hbm, col_hbm,
     ids_ref, rows_ref, gain_ref, in_ref, padded, valid_ref, one_keep_ref, two_keep_ref, col_ref, normed, joined, sems,
     *, rows, cols,
@@ -274,7 +274,7 @@
     for k in range(steps):
         copies.start(("in", k), in_hbm_ref.at[:, pl.ds(2 * LANES * k, 2 * LANES)], in_ref.at[k])
     copies.wait("ids")
-    turned = image_ids(ids_ref, padded, place_ref[0], rows)
+    turned = image_ids(ids_ref, padded, lax.axis_index("ha"), rows)
     spread_cells((turned >= 0).astype(F32), valid_ref, 0, rows + 2 * REACH)
     copies.start("outs", valid_ref, valid_hbm)
     copies.wait("own")
@@ -295,7 +295,7 @@
     copies.wait_all()
 
 
-def head(place, ids, keep_one, keep_two, own, gain, weight_in, rows, cols):
+def head(ids, keep_one, keep_two, own, gain, weight_in, rows, cols):
     cells, dim = own.shape
     cells_ext = cells + 2 * REACH * cols
     blocks = weight_in.shape[1] // LANES
@@ -305,7 +305,7 @@
     ]
     return pl.pallas_call(
         functools.partial(head_kernel, rows=rows, cols=cols),
-        in_specs=[in_smem()] * 4 + [in_hbm()] * 4,
+        in_specs=[in_smem()] * 3 + [in_hbm()] * 4,
         out_specs=[in_hbm()] * len(shapes),
         out_shape=[shape_of(*shape) for shape in shapes],
         scratch_shapes=[
@@ -319,11 +319,11 @@
         + [vmem((cells, dim)), vmem(shapes[0]), pltpu.SemaphoreType.DMA((7 + blocks,))],
         compiler_params=params(),
         cost_estimate=lasting(7),
-    )(place, ids, keep_one, keep_two, ids, own, gain, weight_in)
+    )(ids, keep_one, keep_two, ids, own, gain, weight_in)
 
 
 def forward_kernel(
-    place_ref, ids_scalar, joined_hbm, valid_hbm, one_keep_hbm, two_keep_hbm, col_hbm, above_hbm, own_hbm, below_hbm, cot_hbm,
+    ids_scalar, joined_hbm, valid_hbm, one_keep_hbm, two_keep_hbm, col_hbm, above_hbm, own_hbm, below_hbm, cot_hbm,
     first_gain_hbm, first_scale_hbm, second_gain_hbm, second_scale_hbm,
     in_hbm_ref, kern_hbm, one_hbm, two_hbm, three_hbm, out_hbm, up_hbm, down_hbm,
     output_hbm, dmiddle_hbm, dconv_hbm, dconv_top_hbm, dconv_bottom_hbm,
@@ -332,14 +332,14 @@
     in_ref, kern_ref, one_ref, two_ref, three_ref, out_ref, up_ref, down_ref, dconv_ref, sems, chunk_sems,
     up_kept, up_sent, down_kept, down_sent, out_kept, out_sent,
     row_taps, valid_ref, one_keep_ref, two_keep_ref, col_ref, packed_ref, normed, flat, shifted, laid, wide, conv,
-    mixed_ref, mapped_ref, middle_ref, result, dnorm,
+    mixed_ref, mapped_ref, branch_ref, middle_ref, result, dnorm,
     *, rows, cols, count_ha, count_ba,
 ):
     blocks = flat.shape[0]
     cells = rows * cols
     reach = REACH * cols
     cells_ext = cells + 2 * reach
-    core = place_ref[0] % 2
+    core = lax.axis_index("ha") % 2
     split = one_ref.shape[0]
     dim = rows_ref.shape[1]
     head_steps = blocks // 2
@@ -390,7 +390,7 @@
             for k, (source, target) in enumerate(moves)
         ]
 
-    row_masks(ids_scalar, place_ref[0], row_taps, rows, ids_scalar.shape[0], cols)
+    row_masks(ids_scalar, lax.axis_index("ha"), row_taps, rows, ids_scalar.shape[0], cols)
     copies.wait("rows")
     for name, start, place in (("above", 0, 0), ("below", reach + cells, reach)):
         copies.wait(name)
@@ -443,6 +443,7 @@
         mixed_ref[:, start : start + width] = mixed
         start += width
     branch = dot(mixed, out_ref[...])
+    branch_ref[...] = branch
     masked = rows_ref[reach : reach + cells, :] * valid_ref[reach : reach + cells, :1]
     middle = masked + one_keep_ref[:, :1] * first_scale_ref[...] * branch
     middle_ref[...] = middle
@@ -505,8 +506,8 @@
     copies.start("outs", dconv_ref.at[:, pl.ds(cells - reach, reach), :], dconv_bottom_hbm)
     copies.start("outs", dconv_ref, dconv_hbm)
     start = mixed_ref.shape[1] - out_ref.shape[0]
-    crossed = dot(mixed_ref[:, start:], kept, TN)
-    dscale_one = jnp.sum(crossed * out_ref[...], axis=0, keepdims=True)
+    turned = dot(kept * first_scale_ref[...], mixed_ref[:, start:], TN)
+    dscale_one = jnp.sum(kept * branch_ref[...], axis=0, keepdims=True)
     packed_ref[:row] = jnp.zeros((row, LANES), F32)
     row = 0
     for vector in (dscale_one, dgain_two, dscale_two):
@@ -516,7 +517,7 @@
     half = packed_kept_hbm.shape[0]
     for place, target in ((core, packed_kept_hbm), (1 - core, packed_sent_hbm)):
         copies.start("outs", packed_ref.at[pl.ds(pl.multiple_of(place * half, 8), half), :], target)
-    share_rows(core, (crossed * first_scale_ref[...]).T, out_kept, out_sent, dim // count_ha)
+    share_rows(core, turned, out_kept, out_sent, dim // count_ha)
     for source, line in ((out_kept, line_kept_ref), (out_sent, line_sent_ref)):
         tall = source.shape[2]
         copies.start("outs", source, line.at[:, :, pl.ds(line.shape[2] - tall, tall), :])
@@ -545,7 +546,7 @@
 
 
 def forward(
-    place, ids, ahead, above, own, below, cot, vectors, weight_in, kern, gates,
+    ids, ahead, above, own, below, cot, vectors, weight_in, kern, gates,
     weight_out, weight_up, weight_down, rows, cols, count_ha, count_ba, chunk=512,
 ):
     cells, dim = own.shape
@@ -572,7 +573,7 @@
     cells_ext = cells + 2 * reach
     vmem = functools.partial(pltpu.VMEM, dtype=F32)
     operands = (
-        place, ids, *ahead, above, own, below, cot, *vectors,
+        ids, *ahead, above, own, below, cot, *vectors,
         weight_in, kern, *gates, weight_out, weight_up, weight_down,
     )
     out_shape = [
@@ -590,7 +591,7 @@
     ]
     return pl.pallas_call(
         functools.partial(forward_kernel, rows=rows, cols=cols, count_ha=count_ha, count_ba=count_ba),
-        in_specs=[in_smem()] * 2 + [in_hbm()] * (len(operands) - 2),
+        in_specs=[in_smem()] + [in_hbm()] * (len(operands) - 1),
         out_specs=[in_hbm()] * len(out_shape),
         out_shape=out_shape,
         scratch_shapes=[vmem((cells_ext, dim)), vmem((cells, dim))]
@@ -623,6 +624,7 @@
             vmem((blocks, cells, LANES)),
             vmem((cells, wide)),
             vmem((cells, wide - 2 * split)),
+            vmem((cells, dim)),
             vmem((cells, dim)),
             vmem((cells, dim)),
             vmem((cells, dim)),
@@ -1053,13 +1055,13 @@
     vectors = (gain, scale_first[None], second_gain[None], scale_second[None])
     ids = image_id[0]
     above, below = neighbour_rows(own[:reach], own[cells - reach :])
-    ahead = head(place, ids, keep_first, keep_second, own, gain, weight_in, rows, cols)
+    ahead = head(ids, keep_first, keep_second, own, gain, weight_in, rows, cols)
     joined = ahead[0]
     (
         output, dmiddle, dconv, dconv_top, dconv_bottom, plane_kept, plane_sent, line_kept, line_sent,
         packed_kept, packed_sent,
     ) = forward(
-        place, ids, ahead, above, own, below, cotangent.reshape(cells, dim), vectors,
+        ids, ahead, above, own, below, cotangent.reshape(cells, dim), vectors,
         weight_in, depth_kernel, gates, weight_out, weight_up, weight_down, rows, cols, count_ha, count_ba,
     )
     above, below = neighbour_rows(dconv_top, dconv_bottom)

time: 189 us -> 189 us (level)
  transfers between devices with their start and end apart: 33 -> 33, of which waited for: 11 -> 11; matrix products, arithmetic and copies ran while one was open for 0% -> 0% of each run, Pallas kernels for 32% -> 33%
where the time goes in v15:
time: 189 us; the launch traced here: 188 us
  Pallas kernels  115 us (61%)
  starting transfers between devices  38.2 us (20%)
  waiting for transfers between devices  31.3 us (17%)
  local copies, waits for them, and re-layouts  2.08 us (1%)
    pallas_call x1, Pallas kernels, forward(): pl.pallas_call(functools.partial(forward_kernel, rows=rows, cols=cols, co...  49.7 us
    ppermute x29, waiting for transfers between devices, exchange(): lax.ppermute(values, axis, [(i, i ^ bit) for i in range(lax.axis_size(axi...  31.3 us
    ppermute x29, starting transfers between devices, exchange(): lax.ppermute(values, axis, [(i, i ^ bit) for i in range(lax.axis_size(axi...  29.6 us
    pallas_call x1, Pallas kernels, backward(): pl.pallas_call(functools.partial(backward_kernel, rows=rows, cols=cols),...  29.3 us
    pallas_call x8, Pallas kernels, combine(): pl.pallas_call(kernel, in_specs=[in_smem()] + [in_hbm()] * (len(arrays) +...  27.7 us
    ppermute x4, starting transfers between devices, neighbour_rows(): return (lax.ppermute(bottom, 'ha', up), lax.ppermute(top, 'ha', down))  8.59 us
    pallas_call x1, Pallas kernels, head(): pl.pallas_call(functools.partial(head_kernel, rows=rows, cols=cols), in_s...  7.88 us
  transfers between devices with their start and end apart: 33, of which 11 were waited for; matrix products, arithmetic and copies ran while one was open for 0% of the time, Pallas kernels for 33%

profile of v15, /device:TPU:0, one launch (start us, length us, event | category | flops | bytes accessed | tf_op | source)
XLA Modules:
  0.0 187.9 jit_solution(9010649085544237528)
XLA Ops:
  0.6 2.1 %fusion = (f32[1,3,64,512]{3,2,1,0:T(8,128)}, f32[1,3,64,512]{3,2,1,0:T(8,128)}) fusion(f32[1,8,64,512]{3,2,1,0:T(8,128)} %param.17), kind=kLoop, calls=%fused_computation.1 | loop fusion | bytes 1572864 | tf_op jit(solution)/shard_map/slice | solution.py:1057
  2.7 3.1 %collective-permute-start = (f32[192,512]{1,0:T(8,128)}, f32[192,512]{1,0:T(8,128)}, u32[]{:S(2)}, u32[]{:S(2)}) collective-permute-start(f32[192,512]{1,0:T(8,128)} %bitcast.3), channel_id=1, source_target_pairs={{0,4},{4,8},{8,12},{12,16},{16,20},{20,24},{24,28},{1,5},{5,9},{9,... | collective-permute-start | bytes 1179656 | tf_op jit(solution)/shard_map/ppermute | solution.py:979
  5.8 1.3 collective-permute-start.1
  7.1 7.9 %shard_map.272 = (f32[8,512,128]{2,1,0:T(8,128)}, f32[896,128]{1,0:T(8,128)}, f32[512,128]{1,0:T(8,128)}, f32[512,128]{1,0:T(8,128)}, f32[7,8,8,128]{3,2,1,0:T(8,128)}) custom-call(s32[64,64]{1,0:T(8,128)} %bitcast.41, s32[1,36]{1,0:T(1,128)} %one_table.1, s32[1,36]{1,0:T(1,128)} %two_table.1, s32[64,64]{1,0:T(8,128)} %bitcast.42, f32[512,512]{1,0:T(8,128)} %bitcast.36, ...), custom_call_target="tpu_custom_call" | custom-call | flops 7699999744 | tf_op jit(solution)/shard_map/pallas_call | solution.py:306
  15.0 49.7 %shard_map.273 = (f32[512,512]{1,0:T(8,128)}, f32[512,512]{1,0:T(8,128)}, f32[8,512,128]{2,1,0:T(8,128)}, f32[8,192,128]{2,1,0:T(8,128)}, f32[8,192,128]{2,1,0:T...) custom-call(s32[64,64]{1,0:T(8,128)} %bitcast.43, ...), custom_call_target="tpu_custom_call" | custom-call | flops 52800000000 | tf_op jit(solution)/shard_map/pallas_call | solution.py:592
  64.8 2.6 %collective-permute-start.4 = (f32[4,4,384,128]{3,2,1,0:T(8,128)}, f32[4,4,384,128]{3,2,1,0:T(8,128)}, u32[]{:S(2)}, u32[]{:S(2)}) collective-permute-start(f32[4,4,384,128]{3,2,1,0:T(8,128)} %get-tuple-element.79), channel_id=1, source_target_pairs={{0,4},{4,0},{8,12},{12,8},{16,20},{20,16},{24,28},{28,24},{1,5},{5... | collective-permute-start | bytes 9437192 | tf_op jit(solution)/shard_map/ppermute | solution.py:750
  67.5 0.4 collective-permute-start.5
  67.9 2.9 %collective-permute-start.2 = (f32[8,192,128]{2,1,0:T(8,128)}, f32[8,192,128]{2,1,0:T(8,128)}, u32[]{:S(2)}, u32[]{:S(2)}) collective-permute-start(f32[8,192,128]{2,1,0:T(8,128)} %get-tuple-element.74), channel_id=1, source_target_pairs={{0,4},{4,8},{8,12},{12,16},{16,20},{20,24},{24,28},{1,5},{5,9},{9,... | collective-permute-start | bytes 2359304 | tf_op jit(solution)/shard_map/ppermute | solution.py:979
  70.8 1.3 collective-permute-start.3
  72.1 0.6 pad_add_fusion.place_ref
  72.7 3.1 %collective-permute-done.5.refs_3_.refs_4_ = f32[704,128]{1,0:T(8,128)} collective-permute-done((f32[704,128]{1,0:T(8,128)}, f32[704,128]{1,0:T(8,128)}, u32[]{:S(2)}, u32[]{:S(2)}) %collective-permute-start.5) | collective-permute-done | bytes 360480 | tf_op jit(solution)/shard_map/ppermute | solution.py:750
  75.8 4.5 %shard_map.274 = (f32[1712,128]{1,0:T(8,128)}, f32[1712,128]{1,0:T(8,128)}, f32[1712,128]{1,0:T(8,128)}) custom-call(s32[2]{0:T(128)} %pad_add_fusion.place_ref, f32[6144,128]{1,0:T(8,128)} %bitcast.25, f32[6144,128]{1,0:T(8,128)} %bitcast.13.refs_1_.refs_9_, f32[704,128]{1,0:T(8,128)} %get-tuple-element.80.refs_2_.refs_3_, ...), custom_call_target="tpu_custom_call" | custom-call | flops 3992595200 | tf_op jit(solution)/shard_map/pallas_call | solution.py:858
  80.3 1.6 collective-permute-start.7
  81.9 1.5 collective-permute-start.8
  83.4 0.5 collective-permute-start.9
  83.9 3.0 %shard_map.275.refs_0_ = f32[1536,128]{1,0:T(8,128)} custom-call(s32[2]{0:T(128)} %pad_add_fusion.place_ref, f32[3072,128]{1,0:T(8,128)} %bitcast.29, f32[3072,128]{1,0:T(8,128)} %bitcast.15.refs_1_.refs_8_, f32[1712,128]{1,0:T(8,128)} %get-tuple-element.82.refs_2_.rest_0_, f32[1712,128]{1,0:T(8,128)} %get-tuple-element.83.refs_3_.rest_1_, ...), custom_call_target="tpu_custom_call" | custom-call | flops 1965075200 | tf_op jit(solution)/shard_map/pallas_call | solution.py:858
  87.0 3.1 %collective-permute-start.10 = (f32[1536,128]{1,0:T(8,128)}, f32[1536,128]{1,0:T(8,128)}, u32[]{:S(2)}, u32[]{:S(2)}) collective-permute-start(f32[1536,128]{1,0:T(8,128)} %shard_map.276.rest_3_), channel_id=1, source_target_pairs={{0,16},{4,20},{8,24},{12,28},{16,0},{20,4},{24,8},{28,12},{1,17},{... | collective-permute-start | bytes 2359304 | tf_op jit(solution)/shard_map/ppermute | solution.py:750
  90.0 29.3 %shard_map.277 = (f32[512,512]{1,0:T(8,128)}, f32[4,4,128,128]{3,2,1,0:T(8,128)}, f32[4,4,128,128]{3,2,1,0:T(8,128)}, f32[200,128]{1,0:T(8,128)}, f32[200,128]{1,0:T(8,128)}) custom-call(s32[2]{0:T(128)} %pad_add_fusion.place_ref, s32[64,64]{1,0:T(8,128)} %bitcast.44, s32[64,64]{1,0:T(8,128)} %bitcast.45, ...), custom_call_target="tpu_custom_call" | custom-call | flops 27499999232 | tf_op jit(solution)/shard_map/pallas_call | solution.py:719
  119.4 4.8 %collective-permute-done.10.refs_5_.refs_2_.refs_9_ = f32[1536,128]{1,0:T(8,128)} collective-permute-done((f32[1536,128]{1,0:T(8,128)}, f32[1536,128]{1,0:T(8,128)}, u32[]{:S(2)}, u32[]{:S(2)}) %collective-permute-start.10) | collective-permute-done | bytes 786464 | tf_op jit(solution)/shard_map/ppermute | solution.py:750
  124.3 0.5 collective-permute-start.12
  124.8 3.7 %shard_map.279 = (f32[944,128]{1,0:T(8,128)}, f32[944,128]{1,0:T(8,128)}, f32[176,128]{1,0:T(8,128)}) custom-call(s32[2]{0:T(128)} %pad_add_fusion.place_ref, f32[3072,128]{1,0:T(8,128)} %bitcast.30, f32[3072,128]{1,0:T(8,128)} %bitcast.15.refs_1_.refs_8_, f32[1536,128]{1,0:T(8,128)} %collective-permute-done.10.refs_5_.refs_2_.refs_9_, ...), custom_call_target="tpu_custom_call" | custom-call | flops 2806120448 | tf_op jit(solution)/shard_map/pallas_call | solution.py:858
  128.5 0.8 collective-permute-start.17
  129.3 3.4 %collective-permute-start.16 = (f32[944,128]{1,0:T(8,128)}, f32[944,128]{1,0:T(8,128)}, u32[]{:S(2)}, u32[]{:S(2)}) collective-permute-start(f32[944,128]{1,0:T(8,128)} %get-tuple-element.95.refs_5_.refs_4_), channel_id=1, source_target_pairs={{0,16},{4,20},{8,24},{12,28},{16,0},{20,4},{24,8},{28,12},{1,17},{... | collective-permute-start | bytes 1449992 | tf_op jit(solution)/shard_map/ppermute | solution.py:750
  132.7 3.0 %shard_map.280 = (f32[712,128]{1,0:T(8,128)}, f32[712,128]{1,0:T(8,128)}, f32[712,128]{1,0:T(8,128)}) custom-call(s32[2]{0:T(128)} %pad_add_fusion.place_ref, f32[2048,128]{1,0:T(8,128)} %bitcast.33, f32[2048,128]{1,0:T(8,128)} %bitcast.18.refs_1_.refs_7_, f32[200,128]{1,0:T(8,128)} %get-tuple-element.92.refs_2_, ...), custom_call_target="tpu_custom_call" | custom-call | flops 2152808448 | tf_op jit(solution)/shard_map/pallas_call | solution.py:858
  135.6 1.5 collective-permute-start.13
  137.2 1.5 collective-permute-start.15
  138.7 0.5 collective-permute-start.14
  139.2 12.8 %collective-permute-done.17.refs_12_.refs_1_.refs_3_.refs_10_ = f32[944,128]{1,0:T(8,128)} collective-permute-done((f32[944,128]{1,0:T(8,128)}, f32[944,128]{1,0:T(8,128)}, u32[]{:S(2)}, u32[]{:S(2)}) %collective-permute-start.17) | collective-permute-done | bytes 483360 | tf_op jit(solution)/shard_map/ppermute | solution.py:750
  152.1 1.8 collective-permute-start.21
  153.9 0.7 collective-permute-done.16.refs_5_.refs_13_
  154.8 1.4 collective-permute-done.14.refs_9_.refs_3_
  156.2 3.4 %shard_map.281 = (f32[712,128]{1,0:T(8,128)}, f32[328,128]{1,0:T(8,128)}, f32[328,128]{1,0:T(8,128)}, f32[200,128]{1,0:T(8,128)}) custom-call(s32[2]{0:T(128)} %pad_add_fusion.place_ref, f32[6144,128]{1,0:T(8,128)} %bitcast.27, f32[6144,128]{1,0:T(8,128)} %bitcast.13.refs_1_.refs_9_, f32[1712,128]{1,0:T(8,128)} %collective-permute-done.7.refs_2_.refs_5_, ...), custom_call_target="tpu_custom_call" | custom-call | flops 2337538048 | tf_op jit(solution)/shard_map/pallas_call | solution.py:858
  159.6 0.4 collective-permute-start.18
  160.0 1.8 collective-permute-start.19
  161.8 3.0 %shard_map.284 = (f32[368,128]{1,0:T(8,128)}, f32[368,128]{1,0:T(8,128)}, f32[368,128]{1,0:T(8,128)}, f32[176,128]{1,0:T(8,128)}) custom-call(s32[2]{0:T(128)} %pad_add_fusion.place_ref, f32[3072,128]{1,0:T(8,128)} %bitcast.31, f32[3072,128]{1,0:T(8,128)} %bitcast.15.refs_1_.refs_8_, f32[1536,128]{1,0:T(8,128)} %collective-permute-done.10.refs_5_.refs_2_.refs_9_, ...), custom_call_target="tpu_custom_call" | custom-call | flops 1905000576 | tf_op jit(solution)/shard_map/pallas_call | solution.py:858
  164.8 1.5 collective-permute-start.22
  166.3 1.5 collective-permute-start.24
  167.8 0.5 collective-permute-start.23
  168.4 2.8 %collective-permute-done.18.refs_6_.refs_5_ = f32[712,128]{1,0:T(8,128)} collective-permute-done((f32[712,128]{1,0:T(8,128)}, f32[712,128]{1,0:T(8,128)}, u32[]{:S(2)}, u32[]{:S(2)}) %collective-permute-start.18) | collective-permute-done | bytes 364576 | tf_op jit(solution)/shard_map/ppermute | solution.py:750
  171.2 2.8 %collective-permute-start.20 = (f32[328,128]{1,0:T(8,128)}, f32[328,128]{1,0:T(8,128)}, u32[]{:S(2)}, u32[]{:S(2)}) collective-permute-start(f32[328,128]{1,0:T(8,128)} %shard_map.282), channel_id=1, source_target_pairs={{0,24},{4,28},{8,16},{12,20},{16,8},{20,12},{24,0},{28,4},{1,25},{... | collective-permute-start | bytes 503816 | tf_op jit(solution)/shard_map/ppermute | solution.py:750
  174.1 0.6 collective-permute-done.24.refs_13_.refs_12_
  174.8 1.3 collective-permute-done.23.refs_12_.refs_11_
  176.1 1.6 collective-permute-done.29.refs_17_
  177.9 0.4 collective-permute-start.32
  178.2 1.9 collective-permute-done.20.refs_7_
  180.1 0.5 collective-permute-start.28
  180.6 3.2 %shard_map.286 = (f32[128,256]{1,0:T(8,128)}, f32[64,512]{1,0:T(8,128)}, f32[64,128]{1,0:T(8,128)}) custom-call(s32[2]{0:T(128)} %pad_add_fusion.place_ref, f32[6144,128]{1,0:T(8,128)} %bitcast.28, f32[6144,128]{1,0:T(8,128)} %bitcast.13.refs_1_.refs_9_, f32[1712,128]{1,0:T(8,128)} %collective-permute-done.7.refs_2_.refs_5_, ...), custom_call_target="tpu_custom_call" | custom-call | flops 1965075200 | tf_op jit(solution)/shard_map/pallas_call | solution.py:858
  183.9 3.8 %shard_map.287 = (f32[128,128]{1,0:T(8,128)}, f32[49,960]{1,0:T(8,128)}, f32[1,512]{1,0:T(1,128)}, f32[1,512]{1,0:T(1,128)}, f32[1,512]{1,0:T(1,128)}, /*index=5...) custom-call(s32[2]{0:T(128)} %pad_add_fusion.place_ref, ...), custom_call_target="tpu_custom_call" | custom-call | flops 2220392448 | tf_op jit(solution)/shard_map/pallas_call | solution.py:858
  (36 shorter events, 0.8 us)
Async XLA Ops:
  2.7 12.3 %collective-permute-start = (f32[192,512]{1,0:T(8,128)}, f32[192,512]{1,0:T(8,128)}, u32[]{:S(2)}, u32[]{:S(2)}) collective-permute-start(f32[192,512]{1,0:T(8,128)} %bitcast.3), channel_id=1, source_target_pairs={{0,4},{4,8},{8,12},{12,16},{16,20},{20,24},{24,28},{1,5},{5,9},{9,... | collective-permute-start | bytes 1179656 | tf_op jit(solution)/shard_map/ppermute | solution.py:979
  5.8 9.2 %collective-permute-start.1 = (f32[192,512]{1,0:T(8,128)}, f32[192,512]{1,0:T(8,128)}, u32[]{:S(2)}, u32[]{:S(2)}) collective-permute-start(f32[192,512]{1,0:T(8,128)} %bitcast.4), channel_id=1, source_target_pairs={{4,0},{8,4},{12,8},{16,12},{20,16},{24,20},{28,24},{5,1},{9,5},{13... | collective-permute-start | bytes 1179656 | tf_op jit(solution)/shard_map/ppermute | solution.py:979
  64.8 11.0 %collective-permute-start.4 = (f32[4,4,384,128]{3,2,1,0:T(8,128)}, f32[4,4,384,128]{3,2,1,0:T(8,128)}, u32[]{:S(2)}, u32[]{:S(2)}) collective-permute-start(f32[4,4,384,128]{3,2,1,0:T(8,128)} %get-tuple-element.79), channel_id=1, source_target_pairs={{0,4},{4,0},{8,12},{12,8},{16,20},{20,16},{24,28},{28,24},{1,5},{5... | collective-permute-start | bytes 9437192 | tf_op jit(solution)/shard_map/ppermute | solution.py:750
  67.4 16.0 %collective-permute-start.6 = (f32[4,4,192,128]{3,2,1,0:T(8,128)}, f32[4,4,192,128]{3,2,1,0:T(8,128)}, u32[]{:S(2)}, u32[]{:S(2)}) collective-permute-start(f32[4,4,192,128]{3,2,1,0:T(8,128)} %get-tuple-element.86), channel_id=1, source_target_pairs={{0,4},{4,0},{8,12},{12,8},{16,20},{20,16},{24,28},{28,24},{1,5},{5... | collective-permute-start | bytes 4718600 | tf_op jit(solution)/shard_map/ppermute | solution.py:750
  67.5 8.3 %collective-permute-start.5 = (f32[704,128]{1,0:T(8,128)}, f32[704,128]{1,0:T(8,128)}, u32[]{:S(2)}, u32[]{:S(2)}) collective-permute-start(f32[704,128]{1,0:T(8,128)} %get-tuple-element.81), channel_id=1, source_target_pairs={{0,4},{4,0},{8,12},{12,8},{16,20},{20,16},{24,28},{28,24},{1,5},{5... | collective-permute-start | bytes 1081352 | tf_op jit(solution)/shard_map/ppermute | solution.py:750
  67.9 19.0 %collective-permute-start.2 = (f32[8,192,128]{2,1,0:T(8,128)}, f32[8,192,128]{2,1,0:T(8,128)}, u32[]{:S(2)}, u32[]{:S(2)}) collective-permute-start(f32[8,192,128]{2,1,0:T(8,128)} %get-tuple-element.74), channel_id=1, source_target_pairs={{0,4},{4,8},{8,12},{12,16},{16,20},{20,24},{24,28},{1,5},{5,9},{9,... | collective-permute-start | bytes 2359304 | tf_op jit(solution)/shard_map/ppermute | solution.py:979
  70.8 16.1 %collective-permute-start.3 = (f32[8,192,128]{2,1,0:T(8,128)}, f32[8,192,128]{2,1,0:T(8,128)}, u32[]{:S(2)}, u32[]{:S(2)}) collective-permute-start(f32[8,192,128]{2,1,0:T(8,128)} %get-tuple-element.76), channel_id=1, source_target_pairs={{4,0},{8,4},{12,8},{16,12},{20,16},{24,20},{28,24},{5,1},{9,5},{13... | collective-permute-start | bytes 2359304 | tf_op jit(solution)/shard_map/ppermute | solution.py:979
  80.3 43.9 %collective-permute-start.7 = (f32[1712,128]{1,0:T(8,128)}, f32[1712,128]{1,0:T(8,128)}, u32[]{:S(2)}, u32[]{:S(2)}) collective-permute-start(f32[1712,128]{1,0:T(8,128)} %get-tuple-element.82.refs_2_.rest_0_), channel_id=1, source_target_pairs={{0,1},{1,0},{2,3},{3,2},{4,5},{5,4},{6,7},{7,6},{8,9},{9,8},{10,11... | collective-permute-start | bytes 2629640 | tf_op jit(solution)/shard_map/ppermute | solution.py:750
  81.9 42.3 %collective-permute-start.8 = (f32[1712,128]{1,0:T(8,128)}, f32[1712,128]{1,0:T(8,128)}, u32[]{:S(2)}, u32[]{:S(2)}) collective-permute-start(f32[1712,128]{1,0:T(8,128)} %get-tuple-element.83.refs_3_.rest_1_), channel_id=1, source_target_pairs={{0,2},{1,3},{2,0},{3,1},{4,6},{5,7},{6,4},{7,5},{8,10},{9,11},{10,... | collective-permute-start | bytes 2629640 | tf_op jit(solution)/shard_map/ppermute | solution.py:750
  83.4 40.8 %collective-permute-start.9 = (f32[1712,128]{1,0:T(8,128)}, f32[1712,128]{1,0:T(8,128)}, u32[]{:S(2)}, u32[]{:S(2)}) collective-permute-start(f32[1712,128]{1,0:T(8,128)} %get-tuple-element.84.refs_4_.rest_2_), channel_id=1, source_target_pairs={{0,3},{1,2},{2,1},{3,0},{4,7},{5,6},{6,5},{7,4},{8,11},{9,10},{10,... | collective-permute-start | bytes 2629640 | tf_op jit(solution)/shard_map/ppermute | solution.py:750
  87.0 37.2 %collective-permute-start.10 = (f32[1536,128]{1,0:T(8,128)}, f32[1536,128]{1,0:T(8,128)}, u32[]{:S(2)}, u32[]{:S(2)}) collective-permute-start(f32[1536,128]{1,0:T(8,128)} %shard_map.276.rest_3_), channel_id=1, source_target_pairs={{0,16},{4,20},{8,24},{12,28},{16,0},{20,4},{24,8},{28,12},{1,17},{... | collective-permute-start | bytes 2359304 | tf_op jit(solution)/shard_map/ppermute | solution.py:750
  124.2 8.4 %collective-permute-start.11 = (f32[4,4,128,128]{3,2,1,0:T(8,128)}, f32[4,4,128,128]{3,2,1,0:T(8,128)}, u32[]{:S(2)}, u32[]{:S(2)}) collective-permute-start(f32[4,4,128,128]{3,2,1,0:T(8,128)} %get-tuple-element.91), channel_id=1, source_target_pairs={{0,4},{4,0},{8,12},{12,8},{16,20},{20,16},{24,28},{28,24},{1,5},{5... | collective-permute-start | bytes 3145736 | tf_op jit(solution)/shard_map/ppermute | solution.py:750
  124.3 8.4 %collective-permute-start.12 = (f32[200,128]{1,0:T(8,128)}, f32[200,128]{1,0:T(8,128)}, u32[]{:S(2)}, u32[]{:S(2)}) collective-permute-start(f32[200,128]{1,0:T(8,128)} %get-tuple-element.93), channel_id=1, source_target_pairs={{0,4},{4,0},{8,12},{12,8},{16,20},{20,16},{24,28},{28,24},{1,5},{5... | collective-permute-start | bytes 307208 | tf_op jit(solution)/shard_map/ppermute | solution.py:750
  128.5 23.5 %collective-permute-start.17 = (f32[944,128]{1,0:T(8,128)}, f32[944,128]{1,0:T(8,128)}, u32[]{:S(2)}, u32[]{:S(2)}) collective-permute-start(f32[944,128]{1,0:T(8,128)} %get-tuple-element.94.refs_4_), channel_id=1, source_target_pairs={{0,8},{4,12},{8,0},{12,4},{16,24},{20,28},{24,16},{28,20},{1,9},{5... | collective-permute-start | bytes 1449992 | tf_op jit(solution)/shard_map/ppermute | solution.py:750
  129.3 25.3 %collective-permute-start.16 = (f32[944,128]{1,0:T(8,128)}, f32[944,128]{1,0:T(8,128)}, u32[]{:S(2)}, u32[]{:S(2)}) collective-permute-start(f32[944,128]{1,0:T(8,128)} %get-tuple-element.95.refs_5_.refs_4_), channel_id=1, source_target_pairs={{0,16},{4,20},{8,24},{12,28},{16,0},{20,4},{24,8},{28,12},{1,17},{... | collective-permute-start | bytes 1449992 | tf_op jit(solution)/shard_map/ppermute | solution.py:750
  135.6 18.9 %collective-permute-start.13 = (f32[712,128]{1,0:T(8,128)}, f32[712,128]{1,0:T(8,128)}, u32[]{:S(2)}, u32[]{:S(2)}) collective-permute-start(f32[712,128]{1,0:T(8,128)} %get-tuple-element.97), channel_id=1, source_target_pairs={{0,1},{1,0},{2,3},{3,2},{4,5},{5,4},{6,7},{7,6},{8,9},{9,8},{10,11... | collective-permute-start | bytes 1093640 | tf_op jit(solution)/shard_map/ppermute | solution.py:750
  137.2 17.6 %collective-permute-start.15 = (f32[712,128]{1,0:T(8,128)}, f32[712,128]{1,0:T(8,128)}, u32[]{:S(2)}, u32[]{:S(2)}) collective-permute-start(f32[712,128]{1,0:T(8,128)} %get-tuple-element.99), channel_id=1, source_target_pairs={{0,3},{1,2},{2,1},{3,0},{4,7},{5,6},{6,5},{7,4},{8,11},{9,10},{10,... | collective-permute-start | bytes 1093640 | tf_op jit(solution)/shard_map/ppermute | solution.py:750
  138.7 17.5 %collective-permute-start.14 = (f32[712,128]{1,0:T(8,128)}, f32[712,128]{1,0:T(8,128)}, u32[]{:S(2)}, u32[]{:S(2)}) collective-permute-start(f32[712,128]{1,0:T(8,128)} %get-tuple-element.98.refs_11_), channel_id=1, source_target_pairs={{0,2},{1,3},{2,0},{3,1},{4,6},{5,7},{6,4},{7,5},{8,10},{9,11},{10,... | collective-permute-start | bytes 1093640 | tf_op jit(solution)/shard_map/ppermute | solution.py:750
  152.1 9.7 %collective-permute-start.21 = (f32[176,128]{1,0:T(8,128)}, f32[176,128]{1,0:T(8,128)}, u32[]{:S(2)}, u32[]{:S(2)}) collective-permute-start(f32[176,128]{1,0:T(8,128)} %shard_map.283), channel_id=1, source_target_pairs={{0,24},{4,28},{8,16},{12,20},{16,8},{20,12},{24,0},{28,4},{1,25},{... | collective-permute-start | bytes 270344 | tf_op jit(solution)/shard_map/ppermute | solution.py:750
  159.6 11.6 %collective-permute-start.18 = (f32[712,128]{1,0:T(8,128)}, f32[712,128]{1,0:T(8,128)}, u32[]{:S(2)}, u32[]{:S(2)}) collective-permute-start(f32[712,128]{1,0:T(8,128)} %get-tuple-element.100.refs_7_), channel_id=1, source_target_pairs={{0,8},{4,12},{8,0},{12,4},{16,24},{20,28},{24,16},{28,20},{1,9},{5... | collective-permute-start | bytes 1093640 | tf_op jit(solution)/shard_map/ppermute | solution.py:750
  160.0 11.2 %collective-permute-start.19 = (f32[328,128]{1,0:T(8,128)}, f32[328,128]{1,0:T(8,128)}, u32[]{:S(2)}, u32[]{:S(2)}) collective-permute-start(f32[328,128]{1,0:T(8,128)} %get-tuple-element.101.refs_8_), channel_id=1, source_target_pairs={{0,16},{4,20},{8,24},{12,28},{16,0},{20,4},{24,8},{28,12},{1,17},{... | collective-permute-start | bytes 503816 | tf_op jit(solution)/shard_map/ppermute | solution.py:750
  164.8 9.2 %collective-permute-start.22 = (f32[368,128]{1,0:T(8,128)}, f32[368,128]{1,0:T(8,128)}, u32[]{:S(2)}, u32[]{:S(2)}) collective-permute-start(f32[368,128]{1,0:T(8,128)} %get-tuple-element.104), channel_id=1, source_target_pairs={{0,1},{1,0},{2,3},{3,2},{4,5},{5,4},{6,7},{7,6},{8,9},{9,8},{10,11... | collective-permute-start | bytes 565256 | tf_op jit(solution)/shard_map/ppermute | solution.py:750
  166.3 8.4 %collective-permute-start.24 = (f32[368,128]{1,0:T(8,128)}, f32[368,128]{1,0:T(8,128)}, u32[]{:S(2)}, u32[]{:S(2)}) collective-permute-start(f32[368,128]{1,0:T(8,128)} %get-tuple-element.105), channel_id=1, source_target_pairs={{0,3},{1,2},{2,1},{3,0},{4,7},{5,6},{6,5},{7,4},{8,11},{9,10},{10,... | collective-permute-start | bytes 565256 | tf_op jit(solution)/shard_map/ppermute | solution.py:750
  167.8 8.2 %collective-permute-start.23 = (f32[368,128]{1,0:T(8,128)}, f32[368,128]{1,0:T(8,128)}, u32[]{:S(2)}, u32[]{:S(2)}) collective-permute-start(f32[368,128]{1,0:T(8,128)} %get-tuple-element.103.refs_9_), channel_id=1, source_target_pairs={{0,2},{1,3},{2,0},{3,1},{4,6},{5,7},{6,4},{7,5},{8,10},{9,11},{10,... | collective-permute-start | bytes 565256 | tf_op jit(solution)/shard_map/ppermute | solution.py:750
  171.1 12.7 %collective-permute-start.26 = (f32[712,128]{1,0:T(8,128)}, f32[712,128]{1,0:T(8,128)}, u32[]{:S(2)}, u32[]{:S(2)}) collective-permute-start(f32[712,128]{1,0:T(8,128)} %collective-permute-done.18.refs_6_.refs_5_), channel_id=1, source_target_pairs={{0,4},{4,0},{8,12},{12,8},{16,20},{20,16},{24,28},{28,24},{1,5},{5... | collective-permute-start | bytes 1093640 | tf_op jit(solution)/shard_map/ppermute | solution.py:750
  171.2 8.9 %collective-permute-start.20 = (f32[328,128]{1,0:T(8,128)}, f32[328,128]{1,0:T(8,128)}, u32[]{:S(2)}, u32[]{:S(2)}) collective-permute-start(f32[328,128]{1,0:T(8,128)} %shard_map.282), channel_id=1, source_target_pairs={{0,24},{4,28},{8,16},{12,20},{16,8},{20,12},{24,0},{28,4},{1,25},{... | collective-permute-start | bytes 503816 | tf_op jit(solution)/shard_map/ppermute | solution.py:750
  174.0 6.1 %collective-permute-start.27 = (f32[328,128]{1,0:T(8,128)}, f32[328,128]{1,0:T(8,128)}, u32[]{:S(2)}, u32[]{:S(2)}) collective-permute-start(f32[328,128]{1,0:T(8,128)} %collective-permute-done.19.refs_1_.refs_2_.refs_6_), channel_id=1, source_target_pairs={{0,4},{4,0},{8,12},{12,8},{16,20},{20,16},{24,28},{28,24},{1,5},{5... | collective-permute-start | bytes 503816 | tf_op jit(solution)/shard_map/ppermute | solution.py:750
  174.8 3.1 %collective-permute-start.25 = (f32[200,128]{1,0:T(8,128)}, f32[200,128]{1,0:T(8,128)}, u32[]{:S(2)}, u32[]{:S(2)}) collective-permute-start(f32[200,128]{1,0:T(8,128)} %get-tuple-element.108), channel_id=1, source_target_pairs={{0,4},{4,0},{8,12},{12,8},{16,20},{20,16},{24,28},{28,24},{1,5},{5... | collective-permute-start | bytes 307208 | tf_op jit(solution)/shard_map/ppermute | solution.py:750
  176.1 1.6 collective-permute-start.29
  177.7 6.1 %collective-permute-start.30 = (f32[368,128]{1,0:T(8,128)}, f32[368,128]{1,0:T(8,128)}, u32[]{:S(2)}, u32[]{:S(2)}) collective-permute-start(f32[368,128]{1,0:T(8,128)} %collective-permute-done.22.refs_11_.refs_10_), channel_id=1, source_target_pairs={{0,4},{4,0},{8,12},{12,8},{16,20},{20,16},{24,28},{28,24},{1,5},{5... | collective-permute-start | bytes 565256 | tf_op jit(solution)/shard_map/ppermute | solution.py:750
  177.9 6.0 %collective-permute-start.32 = (f32[368,128]{1,0:T(8,128)}, f32[368,128]{1,0:T(8,128)}, u32[]{:S(2)}, u32[]{:S(2)}) collective-permute-start(f32[368,128]{1,0:T(8,128)} %collective-permute-done.24.refs_13_.refs_12_), channel_id=1, source_target_pairs={{0,4},{4,0},{8,12},{12,8},{16,20},{20,16},{24,28},{28,24},{1,5},{5... | collective-permute-start | bytes 565256 | tf_op jit(solution)/shard_map/ppermute | solution.py:750
  180.1 3.8 %collective-permute-start.31 = (f32[368,128]{1,0:T(8,128)}, f32[368,128]{1,0:T(8,128)}, u32[]{:S(2)}, u32[]{:S(2)}) collective-permute-start(f32[368,128]{1,0:T(8,128)} %collective-permute-done.23.refs_12_.refs_11_), channel_id=1, source_target_pairs={{0,4},{4,0},{8,12},{12,8},{16,20},{20,16},{24,28},{28,24},{1,5},{5... | collective-permute-start | bytes 565256 | tf_op jit(solution)/shard_map/ppermute | solution.py:750
  180.1 3.8 %collective-permute-start.28 = (f32[328,128]{1,0:T(8,128)}, f32[328,128]{1,0:T(8,128)}, u32[]{:S(2)}, u32[]{:S(2)}) collective-permute-start(f32[328,128]{1,0:T(8,128)} %collective-permute-done.20.refs_7_), channel_id=1, source_target_pairs={{0,4},{4,0},{8,12},{12,8},{16,20},{20,16},{24,28},{28,24},{1,5},{5... | collective-permute-start | bytes 503816 | tf_op jit(solution)/shard_map/ppermute | solution.py:750

commit v16 on v15

--- a/solution.py
+++ b/solution.py
@@ -268,18 +268,19 @@
     reach = REACH * cols
     steps = in_ref.shape[0]
     copies = Copies(sems)
-    copies.start("ids", ids_hbm, ids_ref)
     copies.start("own", own_hbm, rows_ref)
     copies.start("own", gain_hbm, gain_ref)
+    copies.start("ids", ids_hbm, ids_ref)
     for k in range(steps):
         copies.start(("in", k), in_hbm_ref.at[:, pl.ds(2 * LANES * k, 2 * LANES)], in_ref.at[k])
+    copies.wait("own")
+    hat, _ = normalized(rows_ref[...])
+    normed[...] = hat * gain_ref[...]
     copies.wait("ids")
     turned = image_ids(ids_ref, padded, lax.axis_index("ha"), rows)
     spread_cells((turned >= 0).astype(F32), valid_ref, 0, rows + 2 * REACH)
     copies.start("outs", valid_ref, valid_hbm)
-    copies.wait("own")
-    hat, _ = normalized(rows_ref[...] * valid_ref[reach : reach + cells, :1])
-    normed[...] = hat * gain_ref[...]
+    normed[...] *= valid_ref[reach : reach + cells, :1]
     for step in range(steps):
         copies.wait(("in", step))
         part = dot(normed[...], in_ref[step])
@@ -332,7 +333,7 @@
     in_ref, kern_ref, one_ref, two_ref, three_ref, out_ref, up_ref, down_ref, dconv_ref, sems, chunk_sems,
     up_kept, up_sent, down_kept, down_sent, out_kept, out_sent,
     row_taps, valid_ref, one_keep_ref, two_keep_ref, col_ref, packed_ref, normed, flat, shifted, laid, wide, conv,
-    mixed_ref, mapped_ref, branch_ref, middle_ref, result, dnorm,
+    mixed_ref, mapped_ref, middle_ref, result, dnorm,
     *, rows, cols, count_ha, count_ba,
 ):
     blocks = flat.shape[0]
@@ -443,7 +444,6 @@
         mixed_ref[:, start : start + width] = mixed
         start += width
     branch = dot(mixed, out_ref[...])
-    branch_ref[...] = branch
     masked = rows_ref[reach : reach + cells, :] * valid_ref[reach : reach + cells, :1]
     middle = masked + one_keep_ref[:, :1] * first_scale_ref[...] * branch
     middle_ref[...] = middle
@@ -506,8 +506,8 @@
     copies.start("outs", dconv_ref.at[:, pl.ds(cells - reach, reach), :], dconv_bottom_hbm)
     copies.start("outs", dconv_ref, dconv_hbm)
     start = mixed_ref.shape[1] - out_ref.shape[0]
-    turned = dot(kept * first_scale_ref[...], mixed_ref[:, start:], TN)
-    dscale_one = jnp.sum(kept * branch_ref[...], axis=0, keepdims=True)
+    crossed = dot(mixed_ref[:, start:], kept, TN)
+    dscale_one = jnp.sum(crossed * out_ref[...], axis=0, keepdims=True)
     packed_ref[:row] = jnp.zeros((row, LANES), F32)
     row = 0
     for vector in (dscale_one, dgain_two, dscale_two):
@@ -517,7 +517,7 @@
     half = packed_kept_hbm.shape[0]
     for place, target in ((core, packed_kept_hbm), (1 - core, packed_sent_hbm)):
         copies.start("outs", packed_ref.at[pl.ds(pl.multiple_of(place * half, 8), half), :], target)
-    share_rows(core, turned, out_kept, out_sent, dim // count_ha)
+    share_rows(core, (crossed * first_scale_ref[...]).T, out_kept, out_sent, dim // count_ha)
     for source, line in ((out_kept, line_kept_ref), (out_sent, line_sent_ref)):
         tall = source.shape[2]
         copies.start("outs", source, line.at[:, :, pl.ds(line.shape[2] - tall, tall), :])
@@ -627,7 +627,6 @@
             vmem((cells, dim)),
             vmem((cells, dim)),
             vmem((cells, dim)),
-            vmem((cells, dim)),
         ],
         compiler_params=params(),
         cost_estimate=lasting(48),

time: 189 us -> 189 us (level)
  no operation moved by 1% of the time
where the time goes in v16:
time: 189 us; the launch traced here: 188 us
  Pallas kernels  115 us (61%)
  starting transfers between devices  38.2 us (20%)
  waiting for transfers between devices  31.3 us (17%)
  local copies, waits for them, and re-layouts  2.08 us (1%)
    pallas_call x1, Pallas kernels, forward(): pl.pallas_call(functools.partial(forward_kernel, rows=rows, cols=cols, co...  49.7 us
    ppermute x29, waiting for transfers between devices, exchange(): lax.ppermute(values, axis, [(i, i ^ bit) for i in range(lax.axis_size(axi...  31.3 us
    ppermute x29, starting transfers between devices, exchange(): lax.ppermute(values, axis, [(i, i ^ bit) for i in range(lax.axis_size(axi...  29.6 us
    pallas_call x1, Pallas kernels, backward(): pl.pallas_call(functools.partial(backward_kernel, rows=rows, cols=cols),...  29.3 us
    pallas_call x8, Pallas kernels, combine(): pl.pallas_call(kernel, in_specs=[in_smem()] + [in_hbm()] * (len(arrays) +...  27.7 us
    ppermute x4, starting transfers between devices, neighbour_rows(): return (lax.ppermute(bottom, 'ha', up), lax.ppermute(top, 'ha', down))  8.59 us
    pallas_call x1, Pallas kernels, head(): pl.pallas_call(functools.partial(head_kernel, rows=rows, cols=cols), in_s...  8.11 us
  transfers between devices with their start and end apart: 33, of which 11 were waited for; matrix products, arithmetic and copies ran while one was open for 0% of the time, Pallas kernels for 33%

profile of v16, /device:TPU:0, one launch (start us, length us, event | category | flops | bytes accessed | tf_op | source)
XLA Modules:
  0.0 188.2 jit_solution(16929730860475552087)
XLA Ops:
  0.6 2.1 %fusion = (f32[1,3,64,512]{3,2,1,0:T(8,128)}, f32[1,3,64,512]{3,2,1,0:T(8,128)}) fusion(f32[1,8,64,512]{3,2,1,0:T(8,128)} %param.17), kind=kLoop, calls=%fused_computation.1 | loop fusion | bytes 1572864 | tf_op jit(solution)/shard_map/slice | solution.py:1056
  2.7 3.1 %collective-permute-start = (f32[192,512]{1,0:T(8,128)}, f32[192,512]{1,0:T(8,128)}, u32[]{:S(2)}, u32[]{:S(2)}) collective-permute-start(f32[192,512]{1,0:T(8,128)} %bitcast.3), channel_id=1, source_target_pairs={{0,4},{4,8},{8,12},{12,16},{16,20},{20,24},{24,28},{1,5},{5,9},{9,... | collective-permute-start | bytes 1179656 | tf_op jit(solution)/shard_map/ppermute | solution.py:978
  5.8 1.3 collective-permute-start.1
  7.1 8.1 %shard_map.272 = (f32[8,512,128]{2,1,0:T(8,128)}, f32[896,128]{1,0:T(8,128)}, f32[512,128]{1,0:T(8,128)}, f32[512,128]{1,0:T(8,128)}, f32[7,8,8,128]{3,2,1,0:T(8,128)}) custom-call(s32[64,64]{1,0:T(8,128)} %bitcast.41, s32[1,36]{1,0:T(1,128)} %one_table.1, s32[1,36]{1,0:T(1,128)} %two_table.1, s32[64,64]{1,0:T(8,128)} %bitcast.42, f32[512,512]{1,0:T(8,128)} %bitcast.36, ...), custom_call_target="tpu_custom_call" | custom-call | flops 7699999744 | tf_op jit(solution)/shard_map/pallas_call | solution.py:307
  15.3 49.7 %shard_map.273 = (f32[512,512]{1,0:T(8,128)}, f32[512,512]{1,0:T(8,128)}, f32[8,512,128]{2,1,0:T(8,128)}, f32[8,192,128]{2,1,0:T(8,128)}, f32[8,192,128]{2,1,0:T...) custom-call(s32[64,64]{1,0:T(8,128)} %bitcast.43, ...), custom_call_target="tpu_custom_call" | custom-call | flops 52800000000 | tf_op jit(solution)/shard_map/pallas_call | solution.py:592
  65.0 2.6 %collective-permute-start.4 = (f32[4,4,384,128]{3,2,1,0:T(8,128)}, f32[4,4,384,128]{3,2,1,0:T(8,128)}, u32[]{:S(2)}, u32[]{:S(2)}) collective-permute-start(f32[4,4,384,128]{3,2,1,0:T(8,128)} %get-tuple-element.79), channel_id=1, source_target_pairs={{0,4},{4,0},{8,12},{12,8},{16,20},{20,16},{24,28},{28,24},{1,5},{5... | collective-permute-start | bytes 9437192 | tf_op jit(solution)/shard_map/ppermute | solution.py:749
  67.7 0.4 collective-permute-start.5
  68.2 2.9 %collective-permute-start.2 = (f32[8,192,128]{2,1,0:T(8,128)}, f32[8,192,128]{2,1,0:T(8,128)}, u32[]{:S(2)}, u32[]{:S(2)}) collective-permute-start(f32[8,192,128]{2,1,0:T(8,128)} %get-tuple-element.74), channel_id=1, source_target_pairs={{0,4},{4,8},{8,12},{12,16},{16,20},{20,24},{24,28},{1,5},{5,9},{9,... | collective-permute-start | bytes 2359304 | tf_op jit(solution)/shard_map/ppermute | solution.py:978
  71.1 1.3 collective-permute-start.3
  72.4 0.6 pad_add_fusion.place_ref
  73.0 3.1 %collective-permute-done.5.refs_3_.refs_4_ = f32[704,128]{1,0:T(8,128)} collective-permute-done((f32[704,128]{1,0:T(8,128)}, f32[704,128]{1,0:T(8,128)}, u32[]{:S(2)}, u32[]{:S(2)}) %collective-permute-start.5) | collective-permute-done | bytes 360480 | tf_op jit(solution)/shard_map/ppermute | solution.py:749
  76.0 4.5 %shard_map.274 = (f32[1712,128]{1,0:T(8,128)}, f32[1712,128]{1,0:T(8,128)}, f32[1712,128]{1,0:T(8,128)}) custom-call(s32[2]{0:T(128)} %pad_add_fusion.place_ref, f32[6144,128]{1,0:T(8,128)} %bitcast.25, f32[6144,128]{1,0:T(8,128)} %bitcast.13.refs_1_.refs_9_, f32[704,128]{1,0:T(8,128)} %get-tuple-element.80.refs_2_.refs_3_, ...), custom_call_target="tpu_custom_call" | custom-call | flops 3992595200 | tf_op jit(solution)/shard_map/pallas_call | solution.py:857
  80.6 1.6 collective-permute-start.7
  82.1 1.5 collective-permute-start.8
  83.6 0.5 collective-permute-start.9
  84.1 3.0 %shard_map.275.refs_0_ = f32[1536,128]{1,0:T(8,128)} custom-call(s32[2]{0:T(128)} %pad_add_fusion.place_ref, f32[3072,128]{1,0:T(8,128)} %bitcast.29, f32[3072,128]{1,0:T(8,128)} %bitcast.15.refs_1_.refs_8_, f32[1712,128]{1,0:T(8,128)} %get-tuple-element.82.refs_2_.rest_0_, f32[1712,128]{1,0:T(8,128)} %get-tuple-element.83.refs_3_.rest_1_, ...), custom_call_target="tpu_custom_call" | custom-call | flops 1965075200 | tf_op jit(solution)/shard_map/pallas_call | solution.py:857
  87.2 3.1 %collective-permute-start.10 = (f32[1536,128]{1,0:T(8,128)}, f32[1536,128]{1,0:T(8,128)}, u32[]{:S(2)}, u32[]{:S(2)}) collective-permute-start(f32[1536,128]{1,0:T(8,128)} %shard_map.276.rest_3_), channel_id=1, source_target_pairs={{0,16},{4,20},{8,24},{12,28},{16,0},{20,4},{24,8},{28,12},{1,17},{... | collective-permute-start | bytes 2359304 | tf_op jit(solution)/shard_map/ppermute | solution.py:749
  90.3 29.3 %shard_map.277 = (f32[512,512]{1,0:T(8,128)}, f32[4,4,128,128]{3,2,1,0:T(8,128)}, f32[4,4,128,128]{3,2,1,0:T(8,128)}, f32[200,128]{1,0:T(8,128)}, f32[200,128]{1,0:T(8,128)}) custom-call(s32[2]{0:T(128)} %pad_add_fusion.place_ref, s32[64,64]{1,0:T(8,128)} %bitcast.44, s32[64,64]{1,0:T(8,128)} %bitcast.45, ...), custom_call_target="tpu_custom_call" | custom-call | flops 27499999232 | tf_op jit(solution)/shard_map/pallas_call | solution.py:718
  119.6 4.8 %collective-permute-done.10.refs_5_.refs_2_.refs_9_ = f32[1536,128]{1,0:T(8,128)} collective-permute-done((f32[1536,128]{1,0:T(8,128)}, f32[1536,128]{1,0:T(8,128)}, u32[]{:S(2)}, u32[]{:S(2)}) %collective-permute-start.10) | collective-permute-done | bytes 786464 | tf_op jit(solution)/shard_map/ppermute | solution.py:749
  124.6 0.5 collective-permute-start.12
  125.0 3.7 %shard_map.279 = (f32[944,128]{1,0:T(8,128)}, f32[944,128]{1,0:T(8,128)}, f32[176,128]{1,0:T(8,128)}) custom-call(s32[2]{0:T(128)} %pad_add_fusion.place_ref, f32[3072,128]{1,0:T(8,128)} %bitcast.30, f32[3072,128]{1,0:T(8,128)} %bitcast.15.refs_1_.refs_8_, f32[1536,128]{1,0:T(8,128)} %collective-permute-done.10.refs_5_.refs_2_.refs_9_, ...), custom_call_target="tpu_custom_call" | custom-call | flops 2806120448 | tf_op jit(solution)/shard_map/pallas_call | solution.py:857
  128.7 0.8 collective-permute-start.17
  129.5 3.4 %collective-permute-start.16 = (f32[944,128]{1,0:T(8,128)}, f32[944,128]{1,0:T(8,128)}, u32[]{:S(2)}, u32[]{:S(2)}) collective-permute-start(f32[944,128]{1,0:T(8,128)} %get-tuple-element.95.refs_5_.refs_4_), channel_id=1, source_target_pairs={{0,16},{4,20},{8,24},{12,28},{16,0},{20,4},{24,8},{28,12},{1,17},{... | collective-permute-start | bytes 1449992 | tf_op jit(solution)/shard_map/ppermute | solution.py:749
  132.9 3.0 %shard_map.280 = (f32[712,128]{1,0:T(8,128)}, f32[712,128]{1,0:T(8,128)}, f32[712,128]{1,0:T(8,128)}) custom-call(s32[2]{0:T(128)} %pad_add_fusion.place_ref, f32[2048,128]{1,0:T(8,128)} %bitcast.33, f32[2048,128]{1,0:T(8,128)} %bitcast.18.refs_1_.refs_7_, f32[200,128]{1,0:T(8,128)} %get-tuple-element.92.refs_2_, ...), custom_call_target="tpu_custom_call" | custom-call | flops 2152808448 | tf_op jit(solution)/shard_map/pallas_call | solution.py:857
  135.9 1.5 collective-permute-start.13
  137.4 1.5 collective-permute-start.15
  138.9 0.5 collective-permute-start.14
  139.4 12.8 %collective-permute-done.17.refs_12_.refs_1_.refs_3_.refs_10_ = f32[944,128]{1,0:T(8,128)} collective-permute-done((f32[944,128]{1,0:T(8,128)}, f32[944,128]{1,0:T(8,128)}, u32[]{:S(2)}, u32[]{:S(2)}) %collective-permute-start.17) | collective-permute-done | bytes 483360 | tf_op jit(solution)/shard_map/ppermute | solution.py:749
  152.3 1.8 collective-permute-start.21
  154.1 0.7 collective-permute-done.16.refs_5_.refs_13_
  155.1 1.4 collective-permute-done.14.refs_9_.refs_3_
  156.4 3.4 %shard_map.281 = (f32[712,128]{1,0:T(8,128)}, f32[328,128]{1,0:T(8,128)}, f32[328,128]{1,0:T(8,128)}, f32[200,128]{1,0:T(8,128)}) custom-call(s32[2]{0:T(128)} %pad_add_fusion.place_ref, f32[6144,128]{1,0:T(8,128)} %bitcast.27, f32[6144,128]{1,0:T(8,128)} %bitcast.13.refs_1_.refs_9_, f32[1712,128]{1,0:T(8,128)} %collective-permute-done.7.refs_2_.refs_5_, ...), custom_call_target="tpu_custom_call" | custom-call | flops 2337538048 | tf_op jit(solution)/shard_map/pallas_call | solution.py:857
  159.8 0.4 collective-permute-start.18
  160.2 1.8 collective-permute-start.19
  162.0 3.0 %shard_map.284 = (f32[368,128]{1,0:T(8,128)}, f32[368,128]{1,0:T(8,128)}, f32[368,128]{1,0:T(8,128)}, f32[176,128]{1,0:T(8,128)}) custom-call(s32[2]{0:T(128)} %pad_add_fusion.place_ref, f32[3072,128]{1,0:T(8,128)} %bitcast.31, f32[3072,128]{1,0:T(8,128)} %bitcast.15.refs_1_.refs_8_, f32[1536,128]{1,0:T(8,128)} %collective-permute-done.10.refs_5_.refs_2_.refs_9_, ...), custom_call_target="tpu_custom_call" | custom-call | flops 1905000576 | tf_op jit(solution)/shard_map/pallas_call | solution.py:857
  165.0 1.5 collective-permute-start.22
  166.6 1.5 collective-permute-start.24
  168.1 0.5 collective-permute-start.23
  168.6 2.8 %collective-permute-done.18.refs_6_.refs_5_ = f32[712,128]{1,0:T(8,128)} collective-permute-done((f32[712,128]{1,0:T(8,128)}, f32[712,128]{1,0:T(8,128)}, u32[]{:S(2)}, u32[]{:S(2)}) %collective-permute-start.18) | collective-permute-done | bytes 364576 | tf_op jit(solution)/shard_map/ppermute | solution.py:749
  171.4 2.8 %collective-permute-start.20 = (f32[328,128]{1,0:T(8,128)}, f32[328,128]{1,0:T(8,128)}, u32[]{:S(2)}, u32[]{:S(2)}) collective-permute-start(f32[328,128]{1,0:T(8,128)} %shard_map.282), channel_id=1, source_target_pairs={{0,24},{4,28},{8,16},{12,20},{16,8},{20,12},{24,0},{28,4},{1,25},{... | collective-permute-start | bytes 503816 | tf_op jit(solution)/shard_map/ppermute | solution.py:749
  174.4 0.6 collective-permute-done.24.refs_13_.refs_12_
  175.0 1.3 collective-permute-done.23.refs_12_.refs_11_
  176.3 1.6 collective-permute-done.29.refs_17_
  178.1 0.4 collective-permute-start.32
  178.5 1.9 collective-permute-done.20.refs_7_
  180.3 0.5 collective-permute-start.28
  180.8 3.2 %shard_map.286 = (f32[128,256]{1,0:T(8,128)}, f32[64,512]{1,0:T(8,128)}, f32[64,128]{1,0:T(8,128)}) custom-call(s32[2]{0:T(128)} %pad_add_fusion.place_ref, f32[6144,128]{1,0:T(8,128)} %bitcast.28, f32[6144,128]{1,0:T(8,128)} %bitcast.13.refs_1_.refs_9_, f32[1712,128]{1,0:T(8,128)} %collective-permute-done.7.refs_2_.refs_5_, ...), custom_call_target="tpu_custom_call" | custom-call | flops 1965075200 | tf_op jit(solution)/shard_map/pallas_call | solution.py:857
  184.1 3.8 %shard_map.287 = (f32[128,128]{1,0:T(8,128)}, f32[49,960]{1,0:T(8,128)}, f32[1,512]{1,0:T(1,128)}, f32[1,512]{1,0:T(1,128)}, f32[1,512]{1,0:T(1,128)}, /*index=5...) custom-call(s32[2]{0:T(128)} %pad_add_fusion.place_ref, ...), custom_call_target="tpu_custom_call" | custom-call | flops 2220392448 | tf_op jit(solution)/shard_map/pallas_call | solution.py:857
  (36 shorter events, 0.8 us)
Async XLA Ops:
  2.7 12.5 %collective-permute-start = (f32[192,512]{1,0:T(8,128)}, f32[192,512]{1,0:T(8,128)}, u32[]{:S(2)}, u32[]{:S(2)}) collective-permute-start(f32[192,512]{1,0:T(8,128)} %bitcast.3), channel_id=1, source_target_pairs={{0,4},{4,8},{8,12},{12,16},{16,20},{20,24},{24,28},{1,5},{5,9},{9,... | collective-permute-start | bytes 1179656 | tf_op jit(solution)/shard_map/ppermute | solution.py:978
  5.8 9.4 %collective-permute-start.1 = (f32[192,512]{1,0:T(8,128)}, f32[192,512]{1,0:T(8,128)}, u32[]{:S(2)}, u32[]{:S(2)}) collective-permute-start(f32[192,512]{1,0:T(8,128)} %bitcast.4), channel_id=1, source_target_pairs={{4,0},{8,4},{12,8},{16,12},{20,16},{24,20},{28,24},{5,1},{9,5},{13... | collective-permute-start | bytes 1179656 | tf_op jit(solution)/shard_map/ppermute | solution.py:978
  65.0 11.0 %collective-permute-start.4 = (f32[4,4,384,128]{3,2,1,0:T(8,128)}, f32[4,4,384,128]{3,2,1,0:T(8,128)}, u32[]{:S(2)}, u32[]{:S(2)}) collective-permute-start(f32[4,4,384,128]{3,2,1,0:T(8,128)} %get-tuple-element.79), channel_id=1, source_target_pairs={{0,4},{4,0},{8,12},{12,8},{16,20},{20,16},{24,28},{28,24},{1,5},{5... | collective-permute-start | bytes 9437192 | tf_op jit(solution)/shard_map/ppermute | solution.py:749
  67.6 16.0 %collective-permute-start.6 = (f32[4,4,192,128]{3,2,1,0:T(8,128)}, f32[4,4,192,128]{3,2,1,0:T(8,128)}, u32[]{:S(2)}, u32[]{:S(2)}) collective-permute-start(f32[4,4,192,128]{3,2,1,0:T(8,128)} %get-tuple-element.86), channel_id=1, source_target_pairs={{0,4},{4,0},{8,12},{12,8},{16,20},{20,16},{24,28},{28,24},{1,5},{5... | collective-permute-start | bytes 4718600 | tf_op jit(solution)/shard_map/ppermute | solution.py:749
  67.7 8.3 %collective-permute-start.5 = (f32[704,128]{1,0:T(8,128)}, f32[704,128]{1,0:T(8,128)}, u32[]{:S(2)}, u32[]{:S(2)}) collective-permute-start(f32[704,128]{1,0:T(8,128)} %get-tuple-element.81), channel_id=1, source_target_pairs={{0,4},{4,0},{8,12},{12,8},{16,20},{20,16},{24,28},{28,24},{1,5},{5... | collective-permute-start | bytes 1081352 | tf_op jit(solution)/shard_map/ppermute | solution.py:749
  68.2 19.0 %collective-permute-start.2 = (f32[8,192,128]{2,1,0:T(8,128)}, f32[8,192,128]{2,1,0:T(8,128)}, u32[]{:S(2)}, u32[]{:S(2)}) collective-permute-start(f32[8,192,128]{2,1,0:T(8,128)} %get-tuple-element.74), channel_id=1, source_target_pairs={{0,4},{4,8},{8,12},{12,16},{16,20},{20,24},{24,28},{1,5},{5,9},{9,... | collective-permute-start | bytes 2359304 | tf_op jit(solution)/shard_map/ppermute | solution.py:978
  71.1 16.1 %collective-permute-start.3 = (f32[8,192,128]{2,1,0:T(8,128)}, f32[8,192,128]{2,1,0:T(8,128)}, u32[]{:S(2)}, u32[]{:S(2)}) collective-permute-start(f32[8,192,128]{2,1,0:T(8,128)} %get-tuple-element.76), channel_id=1, source_target_pairs={{4,0},{8,4},{12,8},{16,12},{20,16},{24,20},{28,24},{5,1},{9,5},{13... | collective-permute-start | bytes 2359304 | tf_op jit(solution)/shard_map/ppermute | solution.py:978
  80.6 43.9 %collective-permute-start.7 = (f32[1712,128]{1,0:T(8,128)}, f32[1712,128]{1,0:T(8,128)}, u32[]{:S(2)}, u32[]{:S(2)}) collective-permute-start(f32[1712,128]{1,0:T(8,128)} %get-tuple-element.82.refs_2_.rest_0_), channel_id=1, source_target_pairs={{0,1},{1,0},{2,3},{3,2},{4,5},{5,4},{6,7},{7,6},{8,9},{9,8},{10,11... | collective-permute-start | bytes 2629640 | tf_op jit(solution)/shard_map/ppermute | solution.py:749
  82.1 42.3 %collective-permute-start.8 = (f32[1712,128]{1,0:T(8,128)}, f32[1712,128]{1,0:T(8,128)}, u32[]{:S(2)}, u32[]{:S(2)}) collective-permute-start(f32[1712,128]{1,0:T(8,128)} %get-tuple-element.83.refs_3_.rest_1_), channel_id=1, source_target_pairs={{0,2},{1,3},{2,0},{3,1},{4,6},{5,7},{6,4},{7,5},{8,10},{9,11},{10,... | collective-permute-start | bytes 2629640 | tf_op jit(solution)/shard_map/ppermute | solution.py:749
  83.6 40.8 %collective-permute-start.9 = (f32[1712,128]{1,0:T(8,128)}, f32[1712,128]{1,0:T(8,128)}, u32[]{:S(2)}, u32[]{:S(2)}) collective-permute-start(f32[1712,128]{1,0:T(8,128)} %get-tuple-element.84.refs_4_.rest_2_), channel_id=1, source_target_pairs={{0,3},{1,2},{2,1},{3,0},{4,7},{5,6},{6,5},{7,4},{8,11},{9,10},{10,... | collective-permute-start | bytes 2629640 | tf_op jit(solution)/shard_map/ppermute | solution.py:749
  87.2 37.2 %collective-permute-start.10 = (f32[1536,128]{1,0:T(8,128)}, f32[1536,128]{1,0:T(8,128)}, u32[]{:S(2)}, u32[]{:S(2)}) collective-permute-start(f32[1536,128]{1,0:T(8,128)} %shard_map.276.rest_3_), channel_id=1, source_target_pairs={{0,16},{4,20},{8,24},{12,28},{16,0},{20,4},{24,8},{28,12},{1,17},{... | collective-permute-start | bytes 2359304 | tf_op jit(solution)/shard_map/ppermute | solution.py:749
  124.5 8.4 %collective-permute-start.11 = (f32[4,4,128,128]{3,2,1,0:T(8,128)}, f32[4,4,128,128]{3,2,1,0:T(8,128)}, u32[]{:S(2)}, u32[]{:S(2)}) collective-permute-start(f32[4,4,128,128]{3,2,1,0:T(8,128)} %get-tuple-element.91), channel_id=1, source_target_pairs={{0,4},{4,0},{8,12},{12,8},{16,20},{20,16},{24,28},{28,24},{1,5},{5... | collective-permute-start | bytes 3145736 | tf_op jit(solution)/shard_map/ppermute | solution.py:749
  124.6 8.4 %collective-permute-start.12 = (f32[200,128]{1,0:T(8,128)}, f32[200,128]{1,0:T(8,128)}, u32[]{:S(2)}, u32[]{:S(2)}) collective-permute-start(f32[200,128]{1,0:T(8,128)} %get-tuple-element.93), channel_id=1, source_target_pairs={{0,4},{4,0},{8,12},{12,8},{16,20},{20,16},{24,28},{28,24},{1,5},{5... | collective-permute-start | bytes 307208 | tf_op jit(solution)/shard_map/ppermute | solution.py:749
  128.7 23.5 %collective-permute-start.17 = (f32[944,128]{1,0:T(8,128)}, f32[944,128]{1,0:T(8,128)}, u32[]{:S(2)}, u32[]{:S(2)}) collective-permute-start(f32[944,128]{1,0:T(8,128)} %get-tuple-element.94.refs_4_), channel_id=1, source_target_pairs={{0,8},{4,12},{8,0},{12,4},{16,24},{20,28},{24,16},{28,20},{1,9},{5... | collective-permute-start | bytes 1449992 | tf_op jit(solution)/shard_map/ppermute | solution.py:749
  129.5 25.3 %collective-permute-start.16 = (f32[944,128]{1,0:T(8,128)}, f32[944,128]{1,0:T(8,128)}, u32[]{:S(2)}, u32[]{:S(2)}) collective-permute-start(f32[944,128]{1,0:T(8,128)} %get-tuple-element.95.refs_5_.refs_4_), channel_id=1, source_target_pairs={{0,16},{4,20},{8,24},{12,28},{16,0},{20,4},{24,8},{28,12},{1,17},{... | collective-permute-start | bytes 1449992 | tf_op jit(solution)/shard_map/ppermute | solution.py:749
  135.9 18.9 %collective-permute-start.13 = (f32[712,128]{1,0:T(8,128)}, f32[712,128]{1,0:T(8,128)}, u32[]{:S(2)}, u32[]{:S(2)}) collective-permute-start(f32[712,128]{1,0:T(8,128)} %get-tuple-element.97), channel_id=1, source_target_pairs={{0,1},{1,0},{2,3},{3,2},{4,5},{5,4},{6,7},{7,6},{8,9},{9,8},{10,11... | collective-permute-start | bytes 1093640 | tf_op jit(solution)/shard_map/ppermute | solution.py:749
  137.4 17.6 %collective-permute-start.15 = (f32[712,128]{1,0:T(8,128)}, f32[712,128]{1,0:T(8,128)}, u32[]{:S(2)}, u32[]{:S(2)}) collective-permute-start(f32[712,128]{1,0:T(8,128)} %get-tuple-element.99), channel_id=1, source_target_pairs={{0,3},{1,2},{2,1},{3,0},{4,7},{5,6},{6,5},{7,4},{8,11},{9,10},{10,... | collective-permute-start | bytes 1093640 | tf_op jit(solution)/shard_map/ppermute | solution.py:749
  138.9 17.5 %collective-permute-start.14 = (f32[712,128]{1,0:T(8,128)}, f32[712,128]{1,0:T(8,128)}, u32[]{:S(2)}, u32[]{:S(2)}) collective-permute-start(f32[712,128]{1,0:T(8,128)} %get-tuple-element.98.refs_11_), channel_id=1, source_target_pairs={{0,2},{1,3},{2,0},{3,1},{4,6},{5,7},{6,4},{7,5},{8,10},{9,11},{10,... | collective-permute-start | bytes 1093640 | tf_op jit(solution)/shard_map/ppermute | solution.py:749
  152.3 9.7 %collective-permute-start.21 = (f32[176,128]{1,0:T(8,128)}, f32[176,128]{1,0:T(8,128)}, u32[]{:S(2)}, u32[]{:S(2)}) collective-permute-start(f32[176,128]{1,0:T(8,128)} %shard_map.283), channel_id=1, source_target_pairs={{0,24},{4,28},{8,16},{12,20},{16,8},{20,12},{24,0},{28,4},{1,25},{... | collective-permute-start | bytes 270344 | tf_op jit(solution)/shard_map/ppermute | solution.py:749
  159.8 11.6 %collective-permute-start.18 = (f32[712,128]{1,0:T(8,128)}, f32[712,128]{1,0:T(8,128)}, u32[]{:S(2)}, u32[]{:S(2)}) collective-permute-start(f32[712,128]{1,0:T(8,128)} %get-tuple-element.100.refs_7_), channel_id=1, source_target_pairs={{0,8},{4,12},{8,0},{12,4},{16,24},{20,28},{24,16},{28,20},{1,9},{5... | collective-permute-start | bytes 1093640 | tf_op jit(solution)/shard_map/ppermute | solution.py:749
  160.2 11.2 %collective-permute-start.19 = (f32[328,128]{1,0:T(8,128)}, f32[328,128]{1,0:T(8,128)}, u32[]{:S(2)}, u32[]{:S(2)}) collective-permute-start(f32[328,128]{1,0:T(8,128)} %get-tuple-element.101.refs_8_), channel_id=1, source_target_pairs={{0,16},{4,20},{8,24},{12,28},{16,0},{20,4},{24,8},{28,12},{1,17},{... | collective-permute-start | bytes 503816 | tf_op jit(solution)/shard_map/ppermute | solution.py:749
  165.0 9.2 %collective-permute-start.22 = (f32[368,128]{1,0:T(8,128)}, f32[368,128]{1,0:T(8,128)}, u32[]{:S(2)}, u32[]{:S(2)}) collective-permute-start(f32[368,128]{1,0:T(8,128)} %get-tuple-element.104), channel_id=1, source_target_pairs={{0,1},{1,0},{2,3},{3,2},{4,5},{5,4},{6,7},{7,6},{8,9},{9,8},{10,11... | collective-permute-start | bytes 565256 | tf_op jit(solution)/shard_map/ppermute | solution.py:749
  166.6 8.4 %collective-permute-start.24 = (f32[368,128]{1,0:T(8,128)}, f32[368,128]{1,0:T(8,128)}, u32[]{:S(2)}, u32[]{:S(2)}) collective-permute-start(f32[368,128]{1,0:T(8,128)} %get-tuple-element.105), channel_id=1, source_target_pairs={{0,3},{1,2},{2,1},{3,0},{4,7},{5,6},{6,5},{7,4},{8,11},{9,10},{10,... | collective-permute-start | bytes 565256 | tf_op jit(solution)/shard_map/ppermute | solution.py:749
  168.1 8.2 %collective-permute-start.23 = (f32[368,128]{1,0:T(8,128)}, f32[368,128]{1,0:T(8,128)}, u32[]{:S(2)}, u32[]{:S(2)}) collective-permute-start(f32[368,128]{1,0:T(8,128)} %get-tuple-element.103.refs_9_), channel_id=1, source_target_pairs={{0,2},{1,3},{2,0},{3,1},{4,6},{5,7},{6,4},{7,5},{8,10},{9,11},{10,... | collective-permute-start | bytes 565256 | tf_op jit(solution)/shard_map/ppermute | solution.py:749
  171.4 12.7 %collective-permute-start.26 = (f32[712,128]{1,0:T(8,128)}, f32[712,128]{1,0:T(8,128)}, u32[]{:S(2)}, u32[]{:S(2)}) collective-permute-start(f32[712,128]{1,0:T(8,128)} %collective-permute-done.18.refs_6_.refs_5_), channel_id=1, source_target_pairs={{0,4},{4,0},{8,12},{12,8},{16,20},{20,16},{24,28},{28,24},{1,5},{5... | collective-permute-start | bytes 1093640 | tf_op jit(solution)/shard_map/ppermute | solution.py:749
  171.4 8.9 %collective-permute-start.20 = (f32[328,128]{1,0:T(8,128)}, f32[328,128]{1,0:T(8,128)}, u32[]{:S(2)}, u32[]{:S(2)}) collective-permute-start(f32[328,128]{1,0:T(8,128)} %shard_map.282), channel_id=1, source_target_pairs={{0,24},{4,28},{8,16},{12,20},{16,8},{20,12},{24,0},{28,4},{1,25},{... | collective-permute-start | bytes 503816 | tf_op jit(solution)/shard_map/ppermute | solution.py:749
  174.2 6.1 %collective-permute-start.27 = (f32[328,128]{1,0:T(8,128)}, f32[328,128]{1,0:T(8,128)}, u32[]{:S(2)}, u32[]{:S(2)}) collective-permute-start(f32[328,128]{1,0:T(8,128)} %collective-permute-done.19.refs_1_.refs_2_.refs_6_), channel_id=1, source_target_pairs={{0,4},{4,0},{8,12},{12,8},{16,20},{20,16},{24,28},{28,24},{1,5},{5... | collective-permute-start | bytes 503816 | tf_op jit(solution)/shard_map/ppermute | solution.py:749
  175.0 3.1 %collective-permute-start.25 = (f32[200,128]{1,0:T(8,128)}, f32[200,128]{1,0:T(8,128)}, u32[]{:S(2)}, u32[]{:S(2)}) collective-permute-start(f32[200,128]{1,0:T(8,128)} %get-tuple-element.108), channel_id=1, source_target_pairs={{0,4},{4,0},{8,12},{12,8},{16,20},{20,16},{24,28},{28,24},{1,5},{5... | collective-permute-start | bytes 307208 | tf_op jit(solution)/shard_map/ppermute | solution.py:749
  176.3 1.6 collective-permute-start.29
  177.9 6.1 %collective-permute-start.30 = (f32[368,128]{1,0:T(8,128)}, f32[368,128]{1,0:T(8,128)}, u32[]{:S(2)}, u32[]{:S(2)}) collective-permute-start(f32[368,128]{1,0:T(8,128)} %collective-permute-done.22.refs_11_.refs_10_), channel_id=1, source_target_pairs={{0,4},{4,0},{8,12},{12,8},{16,20},{20,16},{24,28},{28,24},{1,5},{5... | collective-permute-start | bytes 565256 | tf_op jit(solution)/shard_map/ppermute | solution.py:749
  178.1 6.0 %collective-permute-start.32 = (f32[368,128]{1,0:T(8,128)}, f32[368,128]{1,0:T(8,128)}, u32[]{:S(2)}, u32[]{:S(2)}) collective-permute-start(f32[368,128]{1,0:T(8,128)} %collective-permute-done.24.refs_13_.refs_12_), channel_id=1, source_target_pairs={{0,4},{4,0},{8,12},{12,8},{16,20},{20,16},{24,28},{28,24},{1,5},{5... | collective-permute-start | bytes 565256 | tf_op jit(solution)/shard_map/ppermute | solution.py:749
  180.3 3.8 %collective-permute-start.31 = (f32[368,128]{1,0:T(8,128)}, f32[368,128]{1,0:T(8,128)}, u32[]{:S(2)}, u32[]{:S(2)}) collective-permute-start(f32[368,128]{1,0:T(8,128)} %collective-permute-done.23.refs_12_.refs_11_), channel_id=1, source_target_pairs={{0,4},{4,0},{8,12},{12,8},{16,20},{20,16},{24,28},{28,24},{1,5},{5... | collective-permute-start | bytes 565256 | tf_op jit(solution)/shard_map/ppermute | solution.py:749
  180.3 3.8 %collective-permute-start.28 = (f32[328,128]{1,0:T(8,128)}, f32[328,128]{1,0:T(8,128)}, u32[]{:S(2)}, u32[]{:S(2)}) collective-permute-start(f32[328,128]{1,0:T(8,128)} %collective-permute-done.20.refs_7_), channel_id=1, source_target_pairs={{0,4},{4,0},{8,12},{12,8},{16,20},{20,16},{24,28},{28,24},{1,5},{5... | collective-permute-start | bytes 503816 | tf_op jit(solution)/shard_map/ppermute | solution.py:749
